TPU v7x, 32 devices: a whole 2x2x4 slice. The times are simulated.
32 devices in a mesh: leaf: 4 (over z), front: 8 (over y, x, core).
Axes of the slice: x: 2, y: 2, z: 4, core: 2. Of those that a mesh axis runs over, the one named last changes fastest.
Arguments:
- leaf_lower_inv: float32 [2, 4, 512, 512], P(None, 'leaf', 'front'), may hold values from -0.1875 to 0.1875
- leaf_upper_inv: float32 [2, 4, 512, 512], P(None, 'leaf', 'front'), may hold values from -0.1875 to 0.1875
- leaf_to_mid_lower: float32 [2, 4, 1024, 512], P(None, 'leaf', 'front'), may hold values from -0.125 to 0.125
- leaf_to_root_lower: float32 [2, 4, 2048, 512], P(None, 'leaf', 'front'), may hold values from -0.125 to 0.125
- leaf_to_mid_upper: float32 [2, 4, 512, 1024], P(None, 'leaf', None, 'front'), may hold values from -0.125 to 0.125
- leaf_to_root_upper: float32 [2, 4, 512, 2048], P(None, 'leaf', None, 'front'), may hold values from -0.09375 to 0.09375
- mid_lower_inv: float32 [2, 2, 1024, 1024], P(None, None, 'front'), may hold values from -0.125 to 0.125
- mid_upper_inv: float32 [2, 2, 1024, 1024], P(None, None, 'front'), may hold values from -0.125 to 0.125
- mid_to_root_lower: float32 [2, 2, 2048, 1024], P(None, None, 'front'), may hold values from -0.09375 to 0.09375
- mid_to_root_upper: float32 [2, 2, 1024, 2048], P(None, None, None, 'front'), may hold values from -0.09375 to 0.09375
- root_lower_inv: float32 [2, 2048, 2048], P(None, 'front'), may hold values from -0.09375 to 0.09375
- root_upper_inv: float32 [2, 2048, 2048], P(None, 'front'), may hold values from -0.09375 to 0.09375
- leaf_sources: float32 [2, 2048, 32], P(None, ('leaf', 'front')), may hold values from -6 to 6
- mid_sources: float32 [2, 2, 1024, 32], P(None, None, 'front'), may hold values from -6 to 6
- root_sources: float32 [2, 2048, 32], P(None, 'front'), may hold values from -6 to 6
- receiver_data: float32 [2, 1024, 32], P(None, ('leaf', 'front')), may hold values from -6 to 6
- receiver_block: int32 [1024, 1], P(('leaf', 'front')), may hold values from 0 to 31; in each aligned block of 32 rows (0 to 31, 32 to 63, ...) at most 2 rows name the same one
- receiver_offset: int32 [1024], P(('leaf', 'front')), may hold values from 0 to 63
Outputs:
- leaf_field: float32 [2, 2048, 32], P(None, ('leaf', 'front'))
- mid_field: float32 [2, 2, 1024, 32], P(None, None, 'front')
- root_field: float32 [2, 2048, 32], P(None, 'front')
- leaf_adjoint: float32 [2, 2048, 32], P(None, ('leaf', 'front'))
- mid_adjoint: float32 [2, 2, 1024, 32], P(None, None, 'front')
- root_adjoint: float32 [2, 2048, 32], P(None, 'front')
Inputs may be any that keep to these rules, and one draw needn't show every extreme that they name: `receiver_block`: among the 32 receivers of one device, at most 2 name the same block.
All inputs are finite; a program needn't handle non-finite values.
Results may differ from a plain program's by a relative error of at most 0.00018.
Values sent between devices are 32-bit elements; how exact they have to be, the bound alone decides.
No kernel may reach another device: no remote copies, remote signals or barrier semaphores. Data moves between devices by JAX's collectives and lax.ppermute only.
A program may use at most 64 MiB of HBM per device.

v0:
```python
import jax
import jax.numpy as jnp
from jax import lax
from jax.sharding import PartitionSpec as P

CAP = 2


def product(a, b):
    real_part = jnp.matmul(a[0], b[0], precision=lax.Precision.HIGHEST) - jnp.matmul(
        a[1], b[1], precision=lax.Precision.HIGHEST
    )
    imag_part = jnp.matmul(a[0], b[1], precision=lax.Precision.HIGHEST) + jnp.matmul(
        a[1], b[0], precision=lax.Precision.HIGHEST
    )
    return jnp.stack([real_part, imag_part])


def panel_apply(matrices, shard):
    portion = lax.all_gather(shard, "front", axis=2, tiled=True)
    return tuple((product(matrix, portion) for matrix in matrices))


def panel_sum(partial_value):
    return lax.psum_scatter(partial_value, "front", scatter_dimension=2, tiled=True)


def solve_tree(leaf_rhs, mid_rhs, root_rhs, factors):
    (
        leaf_lower_inv,
        leaf_upper_inv,
        leaf_to_mid_lower,
        leaf_to_root_lower,
        leaf_to_mid_upper,
        leaf_to_root_upper,
        mid_lower_inv,
        mid_upper_inv,
        mid_to_root_lower,
        mid_to_root_upper,
        root_lower_inv,
        root_upper_inv,
    ) = factors
    group_index = lax.axis_index("leaf")
    parent = group_index // 2
    (leaf_pass,) = panel_apply((leaf_lower_inv,), leaf_rhs)
    to_mid, to_root = panel_apply((leaf_to_mid_lower, leaf_to_root_lower), leaf_pass)
    parent_mask = (jnp.arange(2) == parent).astype(jnp.float32).reshape(1, 2, 1, 1)
    mid_terms = parent_mask * to_mid
    mid_total, root_total = lax.psum((mid_terms, to_root), "leaf")
    mid_part, root_part = (mid_rhs, root_rhs)
    (mid_pass,) = panel_apply((mid_lower_inv,), mid_part - mid_total)
    (from_mid,) = panel_apply((mid_to_root_lower,), mid_pass)
    root_cut = root_part - root_total - jnp.sum(from_mid, axis=1, keepdims=True)
    (root_pass,) = panel_apply((root_lower_inv,), root_cut)
    (root_solution,) = panel_apply((root_upper_inv,), root_pass)
    mid_tail = panel_sum(product(mid_to_root_upper, root_solution))
    (mid_solution,) = panel_apply((mid_upper_inv,), mid_pass - mid_tail)
    parent_solution = lax.dynamic_slice_in_dim(mid_solution, parent, 1, 1)
    leaf_tail = panel_sum(
        product(leaf_to_mid_upper, parent_solution) + product(leaf_to_root_upper, root_solution)
    )
    (leaf_solution,) = panel_apply((leaf_upper_inv,), leaf_pass - leaf_tail)
    return (leaf_solution, mid_solution, root_solution)


def body(
    leaf_lower_inv,
    leaf_upper_inv,
    leaf_to_mid_lower,
    leaf_to_root_lower,
    leaf_to_mid_upper,
    leaf_to_root_upper,
    mid_lower_inv,
    mid_upper_inv,
    mid_to_root_lower,
    mid_to_root_upper,
    root_lower_inv,
    root_upper_inv,
    leaf_sources,
    mid_sources,
    root_sources,
    receiver_data,
    receiver_block,
    receiver_offset,
):
    factors = (
        leaf_lower_inv,
        leaf_upper_inv,
        leaf_to_mid_lower,
        leaf_to_root_lower,
        leaf_to_mid_upper,
        leaf_to_root_upper,
        mid_lower_inv,
        mid_upper_inv,
        mid_to_root_lower,
        mid_to_root_upper,
        root_lower_inv[:, None],
        root_upper_inv[:, None],
    )
    leaf_count = lax.axis_size("leaf")
    front_count = lax.axis_size("front")
    device_count = leaf_count * front_count
    columns = receiver_data.shape[2]
    block_rows = leaf_sources.shape[1]
    targets = receiver_block[:, 0]
    dest_hits = (targets[:, None] == jnp.arange(device_count)[None, :]).astype(jnp.int32)
    before = jnp.cumsum(dest_hits, axis=0) - dest_hits
    position = jnp.sum(before * dest_hits, axis=1)
    column = targets * CAP + position
    chosen = column[:, None] == jnp.arange(device_count * CAP)[None, :]
    payload = jnp.einsum(
        "rs,crn->scn", chosen.astype(jnp.float32), receiver_data, precision=lax.Precision.HIGHEST
    )
    payload = payload.reshape(device_count, CAP, 2 * columns)
    offsets = jnp.sum(chosen.astype(jnp.int32) * receiver_offset[:, None], axis=0).reshape(
        device_count, CAP
    )
    arrived_data, arrived_rows = (
        lax.all_to_all(payload, ("leaf", "front"), split_axis=0, concat_axis=0, tiled=True),
        lax.all_to_all(offsets, ("leaf", "front"), split_axis=0, concat_axis=0, tiled=True),
    )
    row_hits = (arrived_rows.reshape(-1)[None, :] == jnp.arange(block_rows)[:, None]).astype(
        jnp.float32
    )
    adjoint_rows = jnp.dot(
        row_hits, arrived_data.reshape(-1, 2 * columns), precision=lax.Precision.HIGHEST
    )
    adjoint_rows = adjoint_rows.reshape(block_rows, 2, columns).transpose(1, 0, 2)
    conjugate_sign = jnp.array([1.0, -1.0], jnp.float32).reshape(2, 1, 1)
    adjoint_leaf = (adjoint_rows * conjugate_sign)[:, None]
    mid_zero = jnp.zeros_like(mid_sources)
    root_zero = jnp.zeros_like(root_sources)[:, None]
    leaf_field, mid_field, root_field = solve_tree(
        leaf_sources[:, None], mid_sources, root_sources[:, None], factors
    )
    leaf_back, mid_back, root_back = solve_tree(adjoint_leaf, mid_zero, root_zero, factors)
    return (
        leaf_field[:, 0],
        mid_field,
        root_field[:, 0],
        leaf_back[:, 0] * conjugate_sign,
        mid_back * conjugate_sign[:, None],
        root_back[:, 0] * conjugate_sign,
    )


def solution(mesh):
    in_specs = (
        P(None, "leaf", "front", None),
        P(None, "leaf", "front", None),
        P(None, "leaf", "front", None),
        P(None, "leaf", "front", None),
        P(None, "leaf", None, "front"),
        P(None, "leaf", None, "front"),
        P(None, None, "front", None),
        P(None, None, "front", None),
        P(None, None, "front", None),
        P(None, None, None, "front"),
        P(None, "front", None),
        P(None, "front", None),
        P(None, ("leaf", "front"), None),
        P(None, None, "front", None),
        P(None, "front", None),
        P(None, ("leaf", "front"), None),
        P(("leaf", "front"), None),
        P(("leaf", "front")),
    )
    out_specs = (
        P(None, ("leaf", "front"), None),
        P(None, None, "front", None),
        P(None, "front", None),
        P(None, ("leaf", "front"), None),
        P(None, None, "front", None),
        P(None, "front", None),
    )
    return jax.shard_map(body, mesh=mesh, in_specs=in_specs, out_specs=out_specs, check_vma=False)
```

profile of v0, /device:TPU:0, one launch (start us, length us, event | category | flops | bytes accessed | tf_op | source)
XLA Modules:
  0.0 476.9 jit_solution(2885307134025810713)
XLA Ops:
  11.0 7.3 %all-to-all-start = ((s32[32,1,2]{2,1,0:T(1,128)}), s32[32,1,2]{2,1,0:T(1,128)S(1)}, u32[]{:S(2)}, u32[]{:S(2)}) async-start(s32[32,1,2]{2,1,0:T(1,128)} %bitcast.98), calls=%async_computation.1 | async-start | bytes 32768 | tf_op jit(solution)/shard_map/all_to_all | solution.py:120
  19.1 10.1 %all-gather = f32[2,512,32]{2,0,1:T(2,128)S(1)} all-gather(f32[2,64,32]{2,0,1:T(2,128)S(1)} %copy.29), channel_id=2, replica_groups=mesh['leaf'=4,'front'=8] {'front'}, dimensions={1}, use_global_device_ids=true | all-gather | bytes 147456 | tf_op jit(solution)/shard_map/all_gather | solution.py:20
  33.4 9.9 %all_gather.49 = f32[2,1,512,32]{3,0,1,2:T(2,128)S(1)} all-gather(f32[2,1,64,32]{3,0,1,2:T(2,128)S(1)} %copy.30), channel_id=1, replica_groups=mesh['leaf'=4,'front'=8] {'front'}, dimensions={2}, use_global_device_ids=true | all-gather | bytes 147456 | tf_op jit(solution)/shard_map/all_gather | solution.py:20
  50.1 4.6 all-to-all-start.1
  56.1 5.7 %all-to-all-done.1 = f32[32,1,128]{2,1,0:T(1,128)S(1)} async-done(((f32[32,1,128]{2,1,0:T(1,128)}), f32[32,1,128]{2,1,0:T(1,128)S(1)}, u32[]{:S(2)}, u32[]{:S(2)}) %all-to-all-start.1) | async-done | bytes 16416 | tf_op jit(solution)/shard_map/all_to_all | solution.py:119
  63.4 8.9 %all-gather.1 = f32[2,512,32]{2,0,1:T(2,128)S(1)} all-gather(f32[2,64,32]{2,0,1:T(2,128)S(1)} %copy.36), channel_id=3, replica_groups=mesh['leaf'=4,'front'=8] {'front'}, dimensions={1}, use_global_device_ids=true | all-gather | bytes 147456 | tf_op jit(solution)/shard_map/all_gather | solution.py:20
  75.7 10.3 %all_gather.57 = f32[2,1,512,32]{3,0,1,2:T(2,128)S(1)} all-gather(f32[2,1,64,32]{3,0,1,2:T(2,128)S(1)} %copy.37), channel_id=1, replica_groups=mesh['leaf'=4,'front'=8] {'front'}, dimensions={2}, use_global_device_ids=true | all-gather | bytes 147456 | tf_op jit(solution)/shard_map/all_gather | solution.py:20
  92.4 33.4 %all-reduce.3.cloned.1.call-done = (f32[2,2,128,32]{2,3,1,0:T(8,128)}, f32[2,1,256,32]{2,3,1,0:T(8,128)}, f32[2,2,128,32]{2,3,1,0:T(8,128)}, f32[2,1,256,32]{2,3,1,0:T(8,128)}) async-done(((f32[2,2,128,32]{2,3,1,0:T(8,128)}, f32[2,1,256,32]{2,3,1,0:T(8,128)}, f32[2,2,128,32]{2,3,1,0:T(8,128)}, f32[2,1,256,32]{2,3,1,0:T(8,128)}), (f32[2,2,128,32]{2,3,1,0:T(8,128)}, f32[2,1,256,32]{2,3,1,0:T(8,128)}, ...) | async-done | bytes 262160 | tf_op jit(solution)/shard_map/psum | solution.py:49
  126.6 10.8 %all_gather.58 = f32[2,2,1024,32]{2,3,1,0:T(8,128)S(1)} all-gather(f32[2,2,128,32]{2,3,1,0:T(8,128)S(1)} %broadcast_subtract_fusion), channel_id=1, replica_groups=mesh['leaf'=4,'front'=8] {'front'}, dimensions={2}, use_global_device_ids=true | all-gather | bytes 589824 | tf_op jit(solution)/shard_map/all_gather | solution.py:20
  141.8 11.7 %all_gather.59 = f32[2,2,1024,32]{2,3,1,0:T(8,128)S(1)} all-gather(f32[2,2,128,32]{2,3,1,0:T(8,128)S(1)} %pad_maximum_fusion.7), channel_id=1, replica_groups=mesh['leaf'=4,'front'=8] {'front'}, dimensions={2}, use_global_device_ids=true | all-gather | bytes 589824 | tf_op jit(solution)/shard_map/all_gather | solution.py:20
  155.6 2.0 fusion.50
  157.6 2.0 fusion.145
  159.6 2.0 fusion.139
  161.7 9.1 %all_gather.60 = f32[2,1,2048,32]{2,3,1,0:T(8,128)S(1)} all-gather(f32[2,1,256,32]{2,3,1,0:T(8,128)S(1)} %bitcast_subtract_fusion), channel_id=1, replica_groups=mesh['leaf'=4,'front'=8] {'front'}, dimensions={2}, use_global_device_ids=true | all-gather | bytes 589824 | tf_op jit(solution)/shard_map/all_gather | solution.py:20
  178.6 10.0 %all_gather.61 = f32[2,1,2048,32]{2,3,1,0:T(8,128)S(1)} all-gather(f32[2,1,256,32]{2,3,1,0:T(8,128)S(1)} %pad_maximum_fusion.9), channel_id=1, replica_groups=mesh['leaf'=4,'front'=8] {'front'}, dimensions={2}, use_global_device_ids=true | all-gather | bytes 589824 | tf_op jit(solution)/shard_map/all_gather | solution.py:20
  201.6 10.6 %all_gather.50 = f32[2,2,1024,32]{2,3,1,0:T(8,128)S(1)} all-gather(f32[2,2,128,32]{2,3,1,0:T(8,128)S(1)} %sub.199), channel_id=1, replica_groups=mesh['leaf'=4,'front'=8] {'front'}, dimensions={2}, use_global_device_ids=true | all-gather | bytes 589824 | tf_op jit(solution)/shard_map/all_gather | solution.py:20
  216.7 11.2 %all_gather.51 = f32[2,2,1024,32]{2,3,1,0:T(8,128)S(1)} all-gather(f32[2,2,128,32]{2,3,1,0:T(8,128)S(1)} %pad_maximum_fusion.4), channel_id=1, replica_groups=mesh['leaf'=4,'front'=8] {'front'}, dimensions={2}, use_global_device_ids=true | all-gather | bytes 589824 | tf_op jit(solution)/shard_map/all_gather | solution.py:20
  231.9 2.0 fusion.133
  234.0 2.0 fusion.127
  236.0 9.4 %all_gather.52 = f32[2,1,2048,32]{2,3,1,0:T(8,128)S(1)} all-gather(f32[2,1,256,32]{2,3,1,0:T(8,128)S(1)} %bitcast_subtract_fusion.1), channel_id=1, replica_groups=mesh['leaf'=4,'front'=8] {'front'}, dimensions={2}, use_global_device_ids=true | all-gather | bytes 589824 | tf_op jit(solution)/shard_map/all_gather | solution.py:20
  253.2 10.0 %all_gather.53 = f32[2,1,2048,32]{2,3,1,0:T(8,128)S(1)} all-gather(f32[2,1,256,32]{2,3,1,0:T(8,128)S(1)} %pad_maximum_fusion.6), channel_id=1, replica_groups=mesh['leaf'=4,'front'=8] {'front'}, dimensions={2}, use_global_device_ids=true | all-gather | bytes 589824 | tf_op jit(solution)/shard_map/all_gather | solution.py:20
  278.5 3.7 fusion.184
  282.2 3.6 fusion.6
  294.4 17.0 %reduce-scatter.11.cloned.1.call-done = f32[2,2,128,32]{2,3,1,0:T(8,128)} async-done(((f32[2,2,1024,32]{2,3,1,0:T(8,128)}), f32[2,2,128,32]{2,3,1,0:T(8,128)}) %reduce-scatter.11.cloned.1.call-update) | async-done | bytes 65552 | tf_op jit(solution)/shard_map/reduce_scatter | solution.py:25
  312.2 10.8 %all_gather.62 = f32[2,2,1024,32]{2,3,1,0:T(8,128)S(1)} all-gather(f32[2,2,128,32]{2,3,1,0:T(8,128)S(1)} %fusion.395), channel_id=1, replica_groups=mesh['leaf'=4,'front'=8] {'front'}, dimensions={2}, use_global_device_ids=true | all-gather | bytes 589824 | tf_op jit(solution)/shard_map/all_gather | solution.py:20
  328.3 20.3 %reduce-scatter.9.cloned.1.call-done = f32[2,2,128,32]{2,3,1,0:T(8,128)} async-done(((f32[2,2,1024,32]{2,3,1,0:T(8,128)}), f32[2,2,128,32]{2,3,1,0:T(8,128)}) %reduce-scatter.9.cloned.1.call-update) | async-done | bytes 65552 | tf_op jit(solution)/shard_map/reduce_scatter | solution.py:25
  349.5 11.3 %all_gather.54 = f32[2,2,1024,32]{2,3,1,0:T(8,128)S(1)} all-gather(f32[2,2,128,32]{2,3,1,0:T(8,128)S(1)} %fusion.396), channel_id=1, replica_groups=mesh['leaf'=4,'front'=8] {'front'}, dimensions={2}, use_global_device_ids=true | all-gather | bytes 589824 | tf_op jit(solution)/shard_map/all_gather | solution.py:20
  368.9 3.4 bitcast_reduce_fusion
  375.1 32.0 %reduce-scatter.15.cloned.1.call-done = f32[64,64]{1,0:T(8,128)} async-done(((f32[512,64]{1,0:T(8,128)}), f32[64,64]{1,0:T(8,128)}) %reduce-scatter.15.cloned.1.call-update) | async-done | bytes 16400
  408.1 35.5 %reduce-scatter.13.cloned.1.call-done = f32[64,64]{1,0:T(8,128)} async-done(((f32[512,64]{1,0:T(8,128)}), f32[64,64]{1,0:T(8,128)}) %reduce-scatter.13.cloned.1.call-update) | async-done | bytes 16400
  444.7 10.0 %all_gather.55 = f32[2,1,512,32]{3,0,1,2:T(2,128)S(1)} all-gather(f32[2,1,64,32]{3,0,1,2:T(2,128)S(1)} %copy.31), channel_id=1, replica_groups=mesh['leaf'=4,'front'=8] {'front'}, dimensions={2}, use_global_device_ids=true | all-gather | bytes 147456 | tf_op jit(solution)/shard_map/all_gather | solution.py:20
  457.3 8.9 %all_gather.63 = f32[2,1,512,32]{3,0,1,2:T(2,128)S(1)} all-gather(f32[2,1,64,32]{3,0,1,2:T(2,128)S(1)} %copy.38), channel_id=1, replica_groups=mesh['leaf'=4,'front'=8] {'front'}, dimensions={2}, use_global_device_ids=true | all-gather | bytes 147456 | tf_op jit(solution)/shard_map/all_gather | solution.py:20
  (233 shorter events, 122.4 us)
Async XLA Ops:
  7.2 24.0 %copy-start.12 = (f32[2,1,64,512]{3,2,1,0:T(8,128)S(1)}, f32[2,1,64,512]{3,2,1,0:T(8,128)}, u32[]{:S(2)}) copy-start(f32[2,1,64,512]{3,2,1,0:T(8,128)} %param.19) | copy-start | bytes 786436
  11.0 39.1 %all-to-all-start = ((s32[32,1,2]{2,1,0:T(1,128)}), s32[32,1,2]{2,1,0:T(1,128)S(1)}, u32[]{:S(2)}, u32[]{:S(2)}) async-start(s32[32,1,2]{2,1,0:T(1,128)} %bitcast.98), calls=%async_computation.1 | async-start | bytes 32768 | tf_op jit(solution)/shard_map/all_to_all | solution.py:120
  29.3 14.5 %copy-start.9 = (f32[2,1,128,512]{3,2,1,0:T(8,128)S(1)}, f32[2,1,128,512]{3,2,1,0:T(8,128)}, u32[]{:S(2)}) copy-start(f32[2,1,128,512]{3,2,1,0:T(8,128)} %param.21) | copy-start | bytes 1572868
  31.1 13.8 %copy-start.8 = (f32[2,1,256,512]{3,2,1,0:T(8,128)S(1)}, f32[2,1,256,512]{3,2,1,0:T(8,128)}, u32[]{:S(2)}) copy-start(f32[2,1,256,512]{3,2,1,0:T(8,128)} %param.22) | copy-start | bytes 3145732
  33.4 12.6 %copy-start.27 = (f32[2,32,32]{2,1,0:T(8,128)S(1)}, f32[2,32,32]{2,1,0:T(8,128)}, u32[]{:S(2)}) copy-start(f32[2,32,32]{2,1,0:T(8,128)} %param.34) | copy-start | bytes 24580
  45.5 17.7 %copy-start.28 = (f32[2]{0:T(128)S(1)}, f32[2]{0:T(128)}, u32[]{:S(2)}) copy-start(f32[2]{0:T(128)} %constant.35.clone) | copy-start | bytes 28
  50.1 11.7 %all-to-all-start.1 = ((f32[32,1,128]{2,1,0:T(1,128)}), f32[32,1,128]{2,1,0:T(1,128)S(1)}, u32[]{:S(2)}, u32[]{:S(2)}) async-start(f32[32,1,128]{2,1,0:T(1,128)} %reshape.298), calls=%async_computation.2 | async-start | bytes 32768 | tf_op jit(solution)/shard_map/all_to_all | solution.py:119
  54.7 71.0 %all-reduce.3.cloned.1.call-start = ((), (), s32[]{:S(2)}) async-start(), calls=%async_computation.10 | async-start | bytes 524288 | tf_op jit(solution)/shard_map/psum | solution.py:49
  74.4 14.2 %copy-start.18 = (f32[1,1,64,32]{2,3,1,0:T(8,128)}, f32[1,1,64,32]{2,3,1,0:T(8,128)S(1)}, u32[]{:S(2)}) copy-start(f32[1,1,64,32]{2,3,1,0:T(8,128)S(1)} %fusion.205) | copy-start | bytes 24580
  75.7 12.9 %copy-start.10 = (f32[2,1,128,512]{3,2,1,0:T(8,128)S(1)}, f32[2,1,128,512]{3,2,1,0:T(8,128)}, u32[]{:S(2)}) copy-start(f32[2,1,128,512]{3,2,1,0:T(8,128)} %param.21) | copy-start | bytes 1572868
  88.6 48.7 %copy-start.5 = (f32[2,2,128,1024]{3,2,1,0:T(8,128)S(1)}, f32[2,2,128,1024]{3,2,1,0:T(8,128)}, u32[]{:S(2)}) copy-start(f32[2,2,128,1024]{3,2,1,0:T(8,128)} %param.25) | copy-start | bytes 6291460
  92.3 219.1 %reduce-scatter.11.cloned.1.call-start = ((), (), s32[]{:S(2)}) async-start(), calls=%async_computation.7 | async-start | bytes 589824 | tf_op jit(solution)/shard_map/reduce_scatter | solution.py:25
  138.4 15.1 %copy-start = (f32[2,2,256,1024]{3,2,1,0:T(8,128)S(1)}, f32[2,2,256,1024]{3,2,1,0:T(8,128)}, u32[]{:S(2)}) copy-start(f32[2,2,256,1024]{3,2,1,0:T(8,128)} %param.27) | copy-start | bytes 12582916
  157.6 4.1 copy-start.24
  157.6 13.2 %copy-start.1 = (f32[2,256,2048]{2,1,0:T(8,128)S(1)}, f32[2,256,2048]{2,1,0:T(8,128)}, u32[]{:S(2)}) copy-start(f32[2,256,2048]{2,1,0:T(8,128)} %param.29) | copy-start | bytes 12582916
  174.7 13.9 %copy-start.2 = (f32[2,256,2048]{2,1,0:T(8,128)S(1)}, f32[2,256,2048]{2,1,0:T(8,128)}, u32[]{:S(2)}) copy-start(f32[2,256,2048]{2,1,0:T(8,128)} %param.30) | copy-start | bytes 12582916
  190.5 5.8 %copy-start.7 = (f32[2,1,512,256]{3,2,1,0:T(8,128)S(1)}, f32[2,1,512,256]{3,2,1,0:T(8,128)}, u32[]{:S(2)}) copy-start(f32[2,1,512,256]{3,2,1,0:T(8,128)} %param.24) | copy-start | bytes 3145732
  192.5 5.0 %copy-start.3 = (f32[2,2,1024,256]{3,2,1,0:T(8,128)S(1)}, f32[2,2,1024,256]{3,2,1,0:T(8,128)}, u32[]{:S(2)}) copy-start(f32[2,2,1024,256]{3,2,1,0:T(8,128)} %param.28) | copy-start | bytes 12582916
  197.5 4.0 copy-start.22
  231.9 4.1 copy-start.25
  231.9 4.1 copy-start.26
  278.2 70.4 %reduce-scatter.9.cloned.1.call-start = ((), (), s32[]{:S(2)}) async-start(), calls=%async_computation.6 | async-start | bytes 589824 | tf_op jit(solution)/shard_map/reduce_scatter | solution.py:25
  278.5 7.3 %copy-start.4 = (f32[2,2,1024,256]{3,2,1,0:T(8,128)S(1)}, f32[2,2,1024,256]{3,2,1,0:T(8,128)}, u32[]{:S(2)}) copy-start(f32[2,2,1024,256]{3,2,1,0:T(8,128)} %param.28) | copy-start | bytes 12582916
  289.8 33.3 %copy-start.6 = (f32[2,2,128,1024]{3,2,1,0:T(8,128)S(1)}, f32[2,2,128,1024]{3,2,1,0:T(8,128)}, u32[]{:S(2)}) copy-start(f32[2,2,128,1024]{3,2,1,0:T(8,128)} %param.26) | copy-start | bytes 6291460
  294.3 112.7 %reduce-scatter.15.cloned.1.call-start = ((), (), s32[]{:S(2)}) async-start(), calls=%async_computation.9 | async-start | bytes 294912
  363.0 4.3 copy-start.14
  368.9 5.5 %copy-start.30 = (f32[2]{0:T(128)S(1)}, f32[2]{0:T(128)}, u32[]{:S(2)}) copy-start(f32[2]{0:T(128)} %constant.35.clone) | copy-start | bytes 28
  368.9 39.1 %copy-start.19 = (f32[1,1,64,32]{2,3,1,0:T(8,128)S(1)}, f32[1,1,64,32]{2,3,1,0:T(8,128)}, u32[]{:S(2)}) copy-start(f32[1,1,64,32]{2,3,1,0:T(8,128)} %copy-done.18) | copy-start | bytes 24580
  368.9 39.1 %copy-start.21 = (f32[1,1,64,32]{2,3,1,0:T(8,128)S(1)}, f32[1,1,64,32]{2,3,1,0:T(8,128)}, u32[]{:S(2)}) copy-start(f32[1,1,64,32]{2,3,1,0:T(8,128)} %copy-done.20) | copy-start | bytes 24580
  368.9 75.6 %copy-start.17 = (f32[1,1,64,32]{2,3,1,0:T(8,128)S(1)}, f32[1,1,64,32]{2,3,1,0:T(8,128)}, u32[]{:S(2)}) copy-start(f32[1,1,64,32]{2,3,1,0:T(8,128)} %copy-done.16) | copy-start | bytes 24580
  373.3 81.7 %copy-start.13 = (f32[2,1,64,512]{3,2,1,0:T(8,128)S(1)}, f32[2,1,64,512]{3,2,1,0:T(8,128)}, u32[]{:S(2)}) copy-start(f32[2,1,64,512]{3,2,1,0:T(8,128)} %param.20) | copy-start | bytes 786436
  373.3 70.3 %reduce-scatter.13.cloned.1.call-start = ((), (), s32[]{:S(2)}) async-start(), calls=%async_computation.8 | async-start | bytes 294912
  (6 other events, 14.8 us)
Sparse Core Ops, SparseCore 0:
  92.4 33.2 all-reduce.2
  278.3 33.0 reduce-scatter.10
  314.5 34.1 reduce-scatter.8
  373.4 33.5 reduce-scatter.14
  409.9 33.6 reduce-scatter.12
where the time goes:
time: 486 us; the launch traced here: 477 us
  blocking collectives  163 us (34%)
  waiting for transfers between devices  144 us (30%)
  matrix products  112 us (23%)
  local copies, waits for them, and re-layouts  15.8 us (3%)
  between operations  15.1 us (3%)
  other arithmetic  14.8 us (3%)
  starting transfers between devices  12.3 us (3%)
    all_gather x16, blocking collectives, panel_apply(): portion = lax.all_gather(shard, 'front', axis=2, tiled=True)  163 us
    unnamed x7, waiting for transfers between devices  67.5 us
    reduce_scatter x2, waiting for transfers between devices, panel_sum(): lax.psum_scatter(partial_value, 'front', scatter_dimension=2, tiled=True)  37.3 us
    psum x1, waiting for transfers between devices, solve_tree(): mid_total, root_total = lax.psum((mid_terms, to_root), 'leaf')  33.4 us
    dot_general x24, matrix products, product(): jnp.matmul(a[0], b[1], precision=lax.Precision.HIGHEST)  29.1 us
    dot_general x24, matrix products, product(): jnp.matmul(a[1], b[1], precision=lax.Precision.HIGHEST)  28.9 us
    dot_general x24, matrix products, product(): jnp.matmul(a[1], b[0], precision=lax.Precision.HIGHEST)  27 us
    dot_general x24, matrix products, product(): jnp.matmul(a[0], b[0], precision=lax.Precision.HIGHEST)  26.5 us
  transfers between devices with their start and end apart: 7, of which 6 were waited for; matrix products, arithmetic and copies ran while one was open for 8% of the time, Pallas kernels for 0%

commit v1 on v0

v1 whole, which is shorter than its diff:
```python
import functools

import jax
import jax.numpy as jnp
from jax import lax
from jax.experimental import pallas as pl
from jax.experimental.pallas import tpu as pltpu
from jax.sharding import PartitionSpec as P

CAP = 2
LANES = 128
F32 = jnp.float32
BF16 = jnp.bfloat16
VM = pl.BlockSpec(memory_space=pltpu.VMEM)
SM = pl.BlockSpec(memory_space=pltpu.SMEM)


def call(kernel, outs, *args, scalars=1, flops=0, nbytes=0, vmem=24):
    return pl.pallas_call(
        kernel,
        out_shape=[jax.ShapeDtypeStruct(shape, F32) for shape in outs],
        in_specs=[SM] * scalars + [VM] * (len(args) - scalars),
        out_specs=[VM] * len(outs),
        compiler_params=pltpu.CompilerParams(vmem_limit_bytes=vmem * 2**20),
        cost_estimate=pl.CostEstimate(flops=flops, bytes_accessed=nbytes, transcendentals=0),
    )(*args)


def split(x):
    high = x.astype(BF16)
    return high, (x - high.astype(F32)).astype(BF16)


def dot(a, b):
    return jnp.dot(a, b, preferred_element_type=F32)


def turned(x):
    half = x.shape[1] // 2
    return jnp.concatenate([-x[:, half:], x[:, :half]], axis=1)


def columns_of(x):
    return jnp.concatenate(split(x), axis=1), jnp.concatenate(split(turned(x)), axis=1)


def complex_dot(real, imag, w, wt):
    n = w.shape[1] // 2
    real_high, real_low = split(real)
    imag_high, imag_low = split(imag)
    wide = dot(real_high, w) + dot(imag_high, wt)
    rest = dot(real_low, w[:, :n]) + dot(imag_low, wt[:, :n])
    return (wide[:, :n] + wide[:, n:]) + rest


def apply_rows(matrix, x, step=512):
    depth = x.shape[0]
    step = min(step, depth)
    total = None
    for at in range(0, depth, step):
        w, wt = columns_of(x[at : at + step])
        part = complex_dot(matrix[0, :, at : at + step], matrix[1, :, at : at + step], w, wt)
        total = part if total is None else total + part
    return total


def assemble(where, parts, here):
    rows = parts[0].shape[0]
    for k, part in enumerate(parts):
        start = pl.multiple_of((here ^ k) * rows, 8)
        where[pl.ds(start, rows), :] = part[...]


def unpacked(x):
    return jnp.concatenate([x[:, 32 * j : 32 * j + 32] for j in range(4)], axis=0)


def packed(x):
    rows = x.shape[0] // 4
    return jnp.concatenate([x[rows * j : rows * j + rows] for j in range(4)], axis=1)


def exchange(axis, blocks):
    size = lax.axis_size(axis)
    return [blocks[0]] + [
        lax.ppermute(blocks[k], axis, [(i, i ^ k) for i in range(size)]) for k in range(1, size)
    ]


def gather(axis, block):
    return exchange(axis, [block] * lax.axis_size(axis))


def pack_receivers(groups, fronts, rows, ids, data, block, offset, *out):
    count = data.shape[1]
    slots = fronts * CAP
    down = lax.broadcasted_iota(jnp.int32, (count, count), 0)
    across = lax.broadcasted_iota(jnp.int32, (count, count), 1)
    eye = down == across
    block_col = block[...]
    block_row = jnp.sum(jnp.where(eye, block_col, 0), axis=0, keepdims=True)
    offset_col = jnp.sum(jnp.where(eye, offset[...], 0), axis=1, keepdims=True)
    same = (block_col == block_row) & (down < across)
    slot_row = block_row * CAP + jnp.sum(same.astype(jnp.int32), axis=0, keepdims=True)
    row_col = (block_col & (fronts - 1)) * rows + offset_col + 1
    width = data.shape[2]
    lane = lax.broadcasted_iota(jnp.int32, (count, width), 1)
    index = jnp.where(lane == 0, row_col, 0).astype(F32)
    lines = jnp.concatenate([index, data[0], jnp.zeros((count, width), F32), -data[1]], axis=1)
    for k in range(groups):
        first = (ids[0] ^ k) * slots
        pick = lax.broadcasted_iota(jnp.int32, (slots, count), 0) + first == slot_row
        out[k][...] = jnp.dot(
            pick.astype(F32), lines, precision=lax.Precision.HIGHEST, preferred_element_type=F32
        )


def message_rows(rows, slots):
    return max(rows, slots), 8 * -(-slots // (8 * LANES))


def pack_leaf(groups, sources, *refs):
    arrived, out = refs[:groups], refs[groups]
    rows, width = sources.shape[1], sources.shape[2]
    lines = jnp.concatenate([ref[...] for ref in arrived], axis=0)
    slots = lines.shape[0]
    body, tail = message_rows(rows, slots)
    zero = jnp.zeros((rows, width), F32)
    own = jnp.concatenate([sources[0], zero, sources[1], zero], axis=1)
    lane = lax.broadcasted_iota(jnp.int32, (slots, LANES), 1)
    data = jnp.where((lane // width) % 2 == 1, lines, 0.0)
    index = lines[:, 0:1]

    def padded(x):
        if x.shape[0] == body:
            return x
        return jnp.concatenate([x, jnp.zeros((body - x.shape[0], LANES), F32)], axis=0)

    out[0:body, :] = padded(own) + padded(data)
    out[body:, :] = jnp.zeros((tail, LANES), F32)
    for at in range(0, slots, LANES):
        size = min(LANES, slots - at)
        eye = lax.broadcasted_iota(jnp.int32, (size, size), 0) == lax.broadcasted_iota(
            jnp.int32, (size, size), 1
        )
        line = jnp.sum(jnp.where(eye, index[at : at + size], 0.0), axis=0, keepdims=True)
        out[body + at // LANES : body + at // LANES + 1, 0:size] = line


def leaf_lower(fronts, slots, ids, matrix, *refs):
    messages, out, rhs = refs[:fronts], refs[fronts], refs[fronts + 1]
    rows = matrix.shape[1]
    total = rows * fronts
    body, _ = message_rows(rows, slots)
    lane = lax.broadcasted_iota(jnp.int32, (slots, LANES), 1)
    taken = (lane // 32) % 2 == 1
    own = lax.broadcasted_iota(jnp.int32, (rows, LANES), 1)
    own = (own // 32) % 2 == 0
    for k in range(fronts):
        start = pl.multiple_of((ids[1] ^ k) * rows, 8)
        rhs[pl.ds(start, rows), :] = jnp.where(own, messages[k][0:rows, :], 0.0)
    group = max(1, 512 // slots)
    for k in range(0, fronts, group):
        chosen = messages[k : k + group]
        lines = jnp.concatenate([jnp.where(taken, ref[0:slots, :], 0.0) for ref in chosen], axis=0)
        index = jnp.concatenate(
            [
                ref[body + at // LANES : body + at // LANES + 1, 0 : min(LANES, slots - at)]
                for ref in chosen
                for at in range(0, slots, LANES)
            ],
            axis=1,
        )
        row = lax.broadcasted_iota(jnp.int32, (total, index.shape[1]), 0)
        pick = (row + 1 == index.astype(jnp.int32)).astype(BF16)
        both = dot(pick, jnp.concatenate(split(lines), axis=1))
        rhs[...] += both[:, :LANES] + both[:, LANES:]
    out[...] = apply_rows(matrix, rhs[...])


def leaf_to_mid(fronts, ids, matrix, sources, *refs):
    parts, out, full, whole = refs[:fronts], refs[fronts], refs[fronts + 1], refs[fronts + 2]
    assemble(whole, parts, ids[1])
    y = whole[...]
    full[...] = y
    zero = jnp.zeros_like(sources[0])
    own = jnp.concatenate([sources[0], zero, sources[1], zero], axis=1)
    first = ((ids[0] & 1) == 0).astype(F32)
    out[...] = own * first - apply_rows(matrix, y)


def leaf_to_root(matrix, full, out):
    out[...] = apply_rows(matrix, full[...])


def mid_lower(fronts, ids, matrix, *refs):
    parts, out, whole = refs[:fronts], refs[fronts], refs[fronts + 1]
    assemble(whole, parts, ids[1])
    out[...] = apply_rows(matrix, whole[...])


def mid_to_root(fronts, groups, ids, matrix, from_leaf, *refs):
    parts, outs = refs[:fronts], refs[fronts : fronts + groups]
    whole, quarters = refs[fronts + groups :]
    assemble(whole, parts, ids[1])
    cut = -(from_leaf[...] + apply_rows(matrix, whole[...]))
    for q in range(groups):
        piece = jnp.concatenate([cut[:, 16 * q : 16 * q + 16], cut[:, 64 + 16 * q : 80 + 16 * q]], axis=1)
        quarters[q] = packed(piece)
    for k in range(groups):
        outs[k][...] = quarters[ids[0] ^ k]


def root_sum(groups, own, *refs):
    total = own[...]
    for ref in refs[:groups]:
        total = total + ref[...]
    refs[groups][...] = total


def root_rows(fronts, ids, matrix, *refs):
    parts, out, whole = refs[:fronts], refs[fronts], refs[fronts + 1]
    rows = matrix.shape[1]
    for k, part in enumerate(parts):
        start = pl.multiple_of((ids[1] ^ k) * rows, 8)
        whole[pl.ds(start, rows), :] = unpacked(part[...])
    out[...] = packed(apply_rows(matrix, whole[...]))


def root_spread(groups, ids, *refs):
    parts, out, forward, adjoint, whole = refs[:groups], *refs[groups:]
    for k, part in enumerate(parts):
        whole[ids[0] ^ k] = unpacked(part[...])
    pieces = [whole[q] for q in range(groups)]
    x = jnp.concatenate([p[:, :16] for p in pieces] + [p[:, 16:] for p in pieces], axis=1)
    out[...] = x
    forward[0] = x[:, 0:32]
    forward[1] = x[:, 64:96]
    adjoint[0] = x[:, 32:64]
    adjoint[1] = -x[:, 96:128]


def send_rows(product, blocks, here, outs):
    rows = outs[0].shape[0]
    blocks[...] = product
    for k, out in enumerate(outs):
        out[...] = blocks[pl.ds(pl.multiple_of((here ^ k) * rows, 8), rows), :]


def apply_columns(matrix, x, out, step=256):
    w, wt = columns_of(x)
    for at in range(0, matrix.shape[1], step):
        out[at : at + step, :] = complex_dot(matrix[0, at : at + step, :], matrix[1, at : at + step, :], w, wt)


def root_to_mid(fronts, ids, matrix, x, *refs):
    outs, blocks = refs[:fronts], refs[fronts]
    apply_columns(matrix, x[...], blocks)
    rows = outs[0].shape[0]
    for k, out in enumerate(outs):
        out[...] = blocks[pl.ds(pl.multiple_of((ids[1] ^ k) * rows, 8), rows), :]


def root_to_leaf(matrix, x, out):
    apply_columns(matrix, x[...], out)


def subtract_sum(fronts, *refs):
    rest, out = refs[fronts:-1], refs[-1]
    tail = refs[0][...]
    for ref in refs[1:fronts]:
        tail = tail + ref[...]
    value = rest[0][...]
    for ref in rest[1:]:
        value = value + ref[...]
    out[...] = value - tail


def mid_upper(fronts, ids, matrix, coupling, from_root, *refs):
    parts, out, outs = refs[:fronts], refs[fronts], refs[fronts + 1 : 2 * fronts + 1]
    whole, blocks = refs[2 * fronts + 1 :]
    assemble(whole, parts, ids[1])
    x = apply_rows(matrix, whole[...])
    out[...] = x
    apply_columns(coupling, x, blocks)
    blocks[...] += from_root[...]
    rows = outs[0].shape[0]
    for k, ref in enumerate(outs):
        ref[...] = blocks[pl.ds(pl.multiple_of((ids[1] ^ k) * rows, 8), rows), :]


def leaf_upper(fronts, ids, matrix, *refs):
    parts, forward, adjoint, whole = refs[:fronts], *refs[fronts:]
    assemble(whole, parts, ids[1])
    x = apply_rows(matrix, whole[...])
    forward[0] = x[:, 0:32]
    forward[1] = x[:, 64:96]
    adjoint[0] = x[:, 32:64]
    adjoint[1] = -x[:, 96:128]


def mid_outputs(ids, mine, other, forward, adjoint):
    parent = ids[0] // 2
    for at, ref in ((parent, mine), (1 - parent, other)):
        x = ref[...]
        forward[0, at] = x[:, 0:32]
        forward[1, at] = x[:, 64:96]
        adjoint[0, at] = x[:, 32:64]
        adjoint[1, at] = -x[:, 96:128]


def body(
    leaf_lower_inv,
    leaf_upper_inv,
    leaf_to_mid_lower,
    leaf_to_root_lower,
    leaf_to_mid_upper,
    leaf_to_root_upper,
    mid_lower_inv,
    mid_upper_inv,
    mid_to_root_lower,
    mid_to_root_upper,
    root_lower_inv,
    root_upper_inv,
    leaf_sources,
    mid_sources,
    root_sources,
    receiver_data,
    receiver_block,
    receiver_offset,
):
    groups, fronts = lax.axis_size("leaf"), lax.axis_size("front")
    group, front = lax.axis_index("leaf"), lax.axis_index("front")
    ids = jnp.stack([group, front]).astype(jnp.int32)
    parent = group // 2
    n0, n1, n2 = leaf_sources.shape[1], mid_sources.shape[2], root_sources.shape[1]
    slots = fronts * CAP

    def own(array):
        return lax.dynamic_index_in_dim(array, parent, 1, keepdims=False)

    def kernel(fn, outs, *args, scratch=(), vmem=24, scalars=1):
        weights = sum(a.size for a in args[scalars : scalars + 1])
        return pl.pallas_call(
            fn,
            out_shape=[jax.ShapeDtypeStruct(shape, F32) for shape in outs],
            in_specs=[SM] * scalars + [VM] * (len(args) - scalars),
            out_specs=[VM] * len(outs),
            scratch_shapes=[pltpu.VMEM(shape, F32) for shape in scratch],
            compiler_params=pltpu.CompilerParams(vmem_limit_bytes=vmem * 2**20),
            cost_estimate=pl.CostEstimate(
                flops=weights * 6 * 128, bytes_accessed=weights * 4, transcendentals=0
            ),
        )(*args)

    with jax.named_scope("right_hand_sides"):
        payload = kernel(
            functools.partial(pack_receivers, groups, fronts, n0),
            [(slots, LANES)] * groups,
            ids,
            receiver_data,
            receiver_block,
            receiver_offset.reshape(1, -1),
        )
        arrived = exchange("leaf", payload)
        (message,) = kernel(
            functools.partial(pack_leaf, groups),
            [(sum(message_rows(n0, groups * slots)), LANES)],
            leaf_sources,
            *arrived,
            scalars=0,
        )
    with jax.named_scope("leaf_lower"):
        messages = gather("front", message)
        (y_leaf,) = kernel(
            functools.partial(leaf_lower, fronts, groups * slots),
            [(n0, LANES)],
            ids,
            leaf_lower_inv[:, 0],
            *messages,
            scratch=[(n0 * fronts, LANES)],
        )
    with jax.named_scope("mid_lower"):
        parts = gather("front", y_leaf)
        cut_mid, y_full = kernel(
            functools.partial(leaf_to_mid, fronts),
            [(n1, LANES), (n0 * fronts, LANES)],
            ids,
            leaf_to_mid_lower[:, 0],
            own(mid_sources),
            *parts,
            scratch=[(n0 * fronts, LANES)],
        )
        parts = gather("front", cut_mid)
        (from_leaf,) = kernel(leaf_to_root, [(n2, LANES)], leaf_to_root_lower[:, 0], y_full, scalars=0)
        (y_mid,) = kernel(
            functools.partial(mid_lower, fronts),
            [(n1, LANES)],
            ids,
            own(mid_lower_inv),
            *parts,
            scratch=[(n1 * fronts, LANES)],
        )
    with jax.named_scope("root_cut"):
        parts = gather("front", y_mid)
        y_sibling = lax.ppermute(y_mid, "leaf", [(i, i ^ 1) for i in range(groups)])
        quarters = kernel(
            functools.partial(mid_to_root, fronts, groups),
            [(n2 // 4, LANES)] * groups,
            ids,
            own(mid_to_root_lower),
            from_leaf,
            *parts,
            scratch=[(n1 * fronts, LANES), (groups, n2 // 4, LANES)],
        )
        both = jnp.concatenate([root_sources, jnp.zeros_like(root_sources)], axis=2)
        quarter = lax.dynamic_slice_in_dim(both, group * 16, 16, 2)
        quarter = jnp.concatenate([quarter[0], quarter[1]], axis=1)
        quarter = quarter.reshape(4, n2 // 4, 32).transpose(1, 0, 2).reshape(n2 // 4, LANES)
        arrived = exchange("leaf", quarters)
        (cut_root,) = kernel(
            functools.partial(root_sum, groups), [(n2 // 4, LANES)], quarter, *arrived, scalars=0
        )
    with jax.named_scope("root_solve"):
        parts = gather("front", cut_root)
        (y_root,) = kernel(
            functools.partial(root_rows, fronts),
            [(n2 // 4, LANES)],
            ids,
            root_lower_inv,
            *parts,
            scratch=[(n2 * fronts, 32)],
        )
        parts = gather("front", y_root)
        (x_quarter,) = kernel(
            functools.partial(root_rows, fronts),
            [(n2 // 4, LANES)],
            ids,
            root_upper_inv,
            *parts,
            scratch=[(n2 * fronts, 32)],
        )
        arrived = gather("leaf", x_quarter)
        x_root, root_field, root_adjoint = kernel(
            functools.partial(root_spread, groups),
            [(n2, LANES), (2, n2, 32), (2, n2, 32)],
            ids,
            *arrived,
            scratch=[(groups, n2, 32)],
        )
    with jax.named_scope("mid_upper"):
        blocks = kernel(
            functools.partial(root_to_mid, fronts),
            [(n1, LANES)] * fronts,
            ids,
            own(mid_to_root_upper),
            x_root,
            scratch=[(n1 * fronts, LANES)],
        )
        parts = exchange("front", blocks)
        (from_root,) = kernel(
            root_to_leaf, [(n0 * fronts, LANES)], leaf_to_root_upper[:, 0], x_root, scalars=0
        )
        (rest,) = kernel(
            functools.partial(subtract_sum, fronts), [(n1, LANES)], *parts, y_mid, y_sibling, scalars=0
        )
        parts = gather("front", rest)
        x_mid, *blocks = kernel(
            functools.partial(mid_upper, fronts),
            [(n1, LANES)] + [(n0, LANES)] * fronts,
            ids,
            own(mid_upper_inv),
            leaf_to_mid_upper[:, 0],
            from_root,
            *parts,
            scratch=[(n1 * fronts, LANES), (n0 * fronts, LANES)],
        )
    with jax.named_scope("leaf_upper"):
        parts = exchange("front", blocks)
        x_other = lax.ppermute(x_mid, "leaf", [(i, i ^ 2) for i in range(groups)])
        (rest,) = kernel(
            functools.partial(subtract_sum, fronts), [(n0, LANES)], *parts, y_leaf, scalars=0
        )
        parts = gather("front", rest)
        mid_field, mid_adjoint = kernel(
            mid_outputs, [(2, 2, n1, 32)] * 2, ids, x_mid, x_other
        )
        leaf_field, leaf_adjoint = kernel(
            functools.partial(leaf_upper, fronts),
            [(2, n0, 32)] * 2,
            ids,
            leaf_upper_inv[:, 0],
            *parts,
            scratch=[(n0 * fronts, LANES)],
        )
    return leaf_field, mid_field, root_field, leaf_adjoint, mid_adjoint, root_adjoint


def solution(mesh):
    in_specs = (
        P(None, "leaf", "front", None),
        P(None, "leaf", "front", None),
        P(None, "leaf", "front", None),
        P(None, "leaf", "front", None),
        P(None, "leaf", None, "front"),
        P(None, "leaf", None, "front"),
        P(None, None, "front", None),
        P(None, None, "front", None),
        P(None, None, "front", None),
        P(None, None, None, "front"),
        P(None, "front", None),
        P(None, "front", None),
        P(None, ("leaf", "front"), None),
        P(None, None, "front", None),
        P(None, "front", None),
        P(None, ("leaf", "front"), None),
        P(("leaf", "front"), None),
        P(("leaf", "front")),
    )
    out_specs = (
        P(None, ("leaf", "front"), None),
        P(None, None, "front", None),
        P(None, "front", None),
        P(None, ("leaf", "front"), None),
        P(None, None, "front", None),
        P(None, "front", None),
    )
    return jax.shard_map(body, mesh=mesh, in_specs=in_specs, out_specs=out_specs, check_vma=False)
```

time: 486 us -> 160 us (0.33); the launches traced: 477 us -> 160 us
  blocking collectives: 163 us -> 0 us
  matrix products: 112 us -> 0 us
  waiting for transfers between devices: 144 us -> 38.7 us
  starting transfers between devices: 12.3 us -> 78 us
  Pallas kernels: 0 us -> 19.7 us
  other arithmetic: 14.8 us -> 0.08 us
  between operations: 15.1 us -> 1.12 us
  local copies, waits for them, and re-layouts: 15.8 us -> 22 us
    all_gather x16 -> x0, blocking collectives: 163 us -> none  [panel_apply(): portion = lax.all_gather(shard, 'front', axis=2, tiled=True)]
    dot_general x97 -> x0, matrix products: 112 us -> none  [the longest x24 29.1 us: product(): jnp.matmul(a[0], b[1], precision=lax.Precision.HIGHEST)]
    ppermute x0 -> x81, starting transfers between devices: none -> 78 us  [the longest x79 77.8 us: exchange(): lax.ppermute(blocks[k], axis, [(i, i ^ k) for i in range(size)])]
    unnamed x7 -> x0, waiting for transfers between devices: 67.5 us -> none
    ppermute x0 -> x81, waiting for transfers between devices: none -> 38.7 us  [the longest x79 38.7 us: exchange(): lax.ppermute(blocks[k], axis, [(i, i ^ k) for i in range(size)])]
    reduce_scatter x2 -> x0, waiting for transfers between devices: 37.3 us -> none  [panel_sum(): lax.psum_scatter(partial_value, 'front', scatter_dimension=2, tiled=True)]
    psum x1 -> x0, waiting for transfers between devices: 33.4 us -> none  [solve_tree(): mid_total, root_total = lax.psum((mid_terms, to_root), 'leaf')]
    pallas_call x0 -> x18, Pallas kernels: none -> 19.7 us  [kernel(): pl.pallas_call(fn, out_shape=[jax.ShapeDtypeStruct(shape, F32) for shape...]
  transfers between devices with their start and end apart: 7 -> 81, of which waited for: 6 -> 28; matrix products, arithmetic and copies ran while one was open for 8% -> 6% of each run, Pallas kernels for 0% -> 3%
where the time goes in v1:
time: 160 us
  starting transfers between devices  78 us (49%)
  waiting for transfers between devices  38.7 us (24%)
  local copies, waits for them, and re-layouts  22 us (14%)
  Pallas kernels  19.7 us (12%)
    ppermute x79, starting transfers between devices, exchange(): lax.ppermute(blocks[k], axis, [(i, i ^ k) for i in range(size)])  77.8 us
    ppermute x79, waiting for transfers between devices, exchange(): lax.ppermute(blocks[k], axis, [(i, i ^ k) for i in range(size)])  38.7 us
    pallas_call x18, Pallas kernels, kernel(): pl.pallas_call(fn, out_shape=[jax.ShapeDtypeStruct(shape, F32) for shape...  19.7 us
    unnamed x48, local copies, waits for them, and re-layouts  15.6 us
  transfers between devices with their start and end apart: 81, of which 28 were waited for; matrix products, arithmetic and copies ran while one was open for 6% of the time, Pallas kernels for 3%

profile of v1, /device:TPU:0, one launch (start us, length us, event | category | flops | bytes accessed | tf_op | source)
XLA Modules:
  0.0 159.6 jit_solution(8577373953589668651)
XLA Ops:
  3.9 3.0 %collective-permute-start = (f32[16,128]{1,0:T(8,128)S(1)}, f32[16,128]{1,0:T(8,128)S(1)}, u32[]{:S(2)}, u32[]{:S(2)}) collective-permute-start(f32[16,128]{1,0:T(8,128)S(1)} %get-tuple-element.41), channel_id=1, source_target_pairs={{0,8},{8,0},{16,24},{24,16},{1,9},{9,1},{17,25},{25,17},{2,10},{10... | collective-permute-start | bytes 24584 | tf_op jit(solution)/shard_map/right_hand_sides/ppermute | solution.py:86
  6.9 2.6 %collective-permute-start.1 = (f32[16,128]{1,0:T(8,128)S(1)}, f32[16,128]{1,0:T(8,128)S(1)}, u32[]{:S(2)}, u32[]{:S(2)}) collective-permute-start(f32[16,128]{1,0:T(8,128)S(1)} %get-tuple-element.42), channel_id=1, source_target_pairs={{0,16},{8,24},{16,0},{24,8},{1,17},{9,25},{17,1},{25,9},{2,18},{10... | collective-permute-start | bytes 24584 | tf_op jit(solution)/shard_map/right_hand_sides/ppermute | solution.py:86
  11.5 3.5 %collective-permute-done.2.refs_3_ = f32[16,128]{1,0:T(8,128)S(1)} collective-permute-done((f32[16,128]{1,0:T(8,128)S(1)}, f32[16,128]{1,0:T(8,128)S(1)}, u32[]{:S(2)}, u32[]{:S(2)}) %collective-permute-start.2) | collective-permute-done | bytes 8224 | tf_op jit(solution)/shard_map/right_hand_sides/ppermute | solution.py:86
  15.2 1.6 collective-permute-start.4
  17.0 1.5 collective-permute-start.6
  18.7 2.4 %collective-permute-start.8 = (f32[72,128]{1,0:T(8,128)S(1)}, f32[72,128]{1,0:T(8,128)S(1)}, u32[]{:S(2)}, u32[]{:S(2)}) collective-permute-start(f32[72,128]{1,0:T(8,128)S(1)} %right_hand_sides.3.refs_0_), channel_id=1, source_target_pairs={{0,6},{1,7},{2,4},{3,5},{4,2},{5,3},{6,0},{7,1},{8,14},{9,15},{10,... | collective-permute-start | bytes 110600 | tf_op jit(solution)/shard_map/leaf_lower/ppermute | solution.py:86
  22.1 1.5 collective-permute-done.8.refs_6_
  23.6 1.9 %collective-permute-done.9.refs_7_ = f32[72,128]{1,0:T(8,128)S(1)} collective-permute-done((f32[72,128]{1,0:T(8,128)S(1)}, f32[72,128]{1,0:T(8,128)S(1)}, u32[]{:S(2)}, u32[]{:S(2)}) %collective-permute-start.9) | collective-permute-done | bytes 36896 | tf_op jit(solution)/shard_map/leaf_lower/ppermute | solution.py:86
  42.8 1.8 %collective-permute-start.22 = (f32[128,128]{1,0:T(8,128)S(1)}, f32[128,128]{1,0:T(8,128)S(1)}, u32[]{:S(2)}, u32[]{:S(2)}) collective-permute-start(f32[128,128]{1,0:T(8,128)S(1)} %get-tuple-element.45.refs_0_), channel_id=1, source_target_pairs={{0,6},{1,7},{2,4},{3,5},{4,2},{5,3},{6,0},{7,1},{8,14},{9,15},{10,... | collective-permute-start | bytes 196616 | tf_op jit(solution)/shard_map/mid_lower/ppermute | solution.py:86
  46.4 1.8 %collective-permute-done.22.refs_6_ = f32[128,128]{1,0:T(8,128)S(1)} collective-permute-done((f32[128,128]{1,0:T(8,128)S(1)}, f32[128,128]{1,0:T(8,128)S(1)}, u32[]{:S(2)}, u32[]{:S(2)}) %collective-permute-start.22) | collective-permute-done | bytes 65568 | tf_op jit(solution)/shard_map/mid_lower/ppermute | solution.py:86
  48.2 1.5 collective-permute-done.23.refs_7_
  51.7 1.6 dynamic-slice_bitcast_fusion.1.matrix
  56.1 1.6 %collective-permute-start.29 = (f32[128,128]{1,0:T(8,128)S(1)}, f32[128,128]{1,0:T(8,128)}, u32[]{:S(2)}, u32[]{:S(2)}) collective-permute-start(f32[128,128]{1,0:T(8,128)S(1)} %mid_lower.5.refs_0_.refs_8_), channel_id=1, source_target_pairs={{0,6},{1,7},{2,4},{3,5},{4,2},{5,3},{6,0},{7,1},{8,14},{9,15},{10,... | collective-permute-start | bytes 196616 | tf_op jit(solution)/shard_map/root_cut/ppermute | solution.py:86
  63.0 1.6 copy-done.1
  64.6 2.2 %root_cut.2 = (f32[64,128]{1,0:T(8,128)S(1)}, f32[64,128]{1,0:T(8,128)S(1)}, f32[64,128]{1,0:T(8,128)S(1)}, f32[64,128]{1,0:T(8,128)S(1)}) custom-call(s32[2]{0:T(128)S(1)} %pad_add_fusion.ids, f32[2,256,1024]{2,1,0:T(8,128)S(1)} %copy-done.1, f32[256,128]{1,0:T(8,128)S(1)} %mid_lower.4.from_leaf, f32[128,128]{1,0:T(8,128)S(1)} %mid_lower.5.refs_0_.refs_8_, ...), custom_call_target="tpu_custom_call" | custom-call | flops 402653184 | bytes 2097152 | tf_op jit(solution)/shard_map/root_cut/pallas_call | solution.py:344
  67.5 3.8 %collective-permute-start.33 = (f32[64,128]{1,0:T(8,128)S(1)}, f32[64,128]{1,0:T(8,128)S(1)}, u32[]{:S(2)}, u32[]{:S(2)}) collective-permute-start(f32[64,128]{1,0:T(8,128)S(1)} %get-tuple-element.49), channel_id=1, source_target_pairs={{0,24},{8,16},{16,8},{24,0},{1,25},{9,17},{17,9},{25,1},{2,26},{10... | collective-permute-start | bytes 98312 | tf_op jit(solution)/shard_map/root_cut/ppermute | solution.py:86
  71.9 1.7 %collective-permute-done.33.refs_3_ = f32[64,128]{1,0:T(8,128)S(1)} collective-permute-done((f32[64,128]{1,0:T(8,128)S(1)}, f32[64,128]{1,0:T(8,128)S(1)}, u32[]{:S(2)}, u32[]{:S(2)}) %collective-permute-start.33) | collective-permute-done | bytes 32800 | tf_op jit(solution)/shard_map/root_cut/ppermute | solution.py:86
  77.3 1.6 %collective-permute-start.39 = (f32[64,128]{1,0:T(8,128)S(1)}, f32[64,128]{1,0:T(8,128)S(1)}, u32[]{:S(2)}, u32[]{:S(2)}) collective-permute-start(f32[64,128]{1,0:T(8,128)S(1)} %root_cut.3.refs_0_), channel_id=1, source_target_pairs={{0,6},{1,7},{2,4},{3,5},{4,2},{5,3},{6,0},{7,1},{8,14},{9,15},{10,... | collective-permute-start | bytes 98312 | tf_op jit(solution)/shard_map/root_solve/ppermute | solution.py:86
  80.0 2.1 %collective-permute-done.39.refs_6_ = f32[64,128]{1,0:T(8,128)S(1)} collective-permute-done((f32[64,128]{1,0:T(8,128)S(1)}, f32[64,128]{1,0:T(8,128)S(1)}, u32[]{:S(2)}, u32[]{:S(2)}) %collective-permute-start.39) | collective-permute-done | bytes 32800 | tf_op jit(solution)/shard_map/root_solve/ppermute | solution.py:86
  83.1 2.2 %copy-done.2 = f32[2,256,2048]{2,1,0:T(8,128)S(1)} copy-done((f32[2,256,2048]{2,1,0:T(8,128)S(1)}, f32[2,256,2048]{2,1,0:T(8,128)}, u32[]{:S(2)}) %copy-start.2) | copy-done | bytes 4194328
  85.3 2.7 %root_solve.3.refs_0_ = f32[64,128]{1,0:T(8,128)S(1)} custom-call(s32[2]{0:T(128)S(1)} %pad_add_fusion.ids, f32[2,256,2048]{2,1,0:T(8,128)S(1)} %copy-done.2, f32[64,128]{1,0:T(8,128)S(1)} %root_cut.3.refs_0_, f32[64,128]{1,0:T(8,128)S(1)} %collective-permute-done.34.refs_1_, f32[64,128]{1,0:T(8,128)S(1)} %collective-permute-done.35.refs_2_, ...), custom_call_target="tpu_custom_call" | custom-call | flops 805306368 | bytes 4194304 | tf_op jit(solution)/shard_map/root_solve/pallas_call | solution.py:344
  94.4 2.2 %collective-permute-done.46.refs_6_ = f32[64,128]{1,0:T(8,128)S(1)} collective-permute-done((f32[64,128]{1,0:T(8,128)S(1)}, f32[64,128]{1,0:T(8,128)S(1)}, u32[]{:S(2)}, u32[]{:S(2)}) %collective-permute-start.46) | collective-permute-done | bytes 32800 | tf_op jit(solution)/shard_map/root_solve/ppermute | solution.py:86
  97.4 2.7 %root_solve.4.refs_0_ = f32[64,128]{1,0:T(8,128)S(1)} custom-call(s32[2]{0:T(128)S(1)} %pad_add_fusion.ids, f32[2,256,2048]{2,1,0:T(8,128)S(1)} %copy-done.3, f32[64,128]{1,0:T(8,128)S(1)} %root_solve.3.refs_0_, f32[64,128]{1,0:T(8,128)S(1)} %collective-permute-done.41.refs_1_, f32[64,128]{1,0:T(8,128)S(1)} %collective-permute-done.42.refs_2_, ...), custom_call_target="tpu_custom_call" | custom-call | flops 805306368 | bytes 4194304 | tf_op jit(solution)/shard_map/root_solve/pallas_call | solution.py:344
  100.9 3.3 %collective-permute-start.49 = (f32[64,128]{1,0:T(8,128)S(1)}, f32[64,128]{1,0:T(8,128)S(1)}, u32[]{:S(2)}, u32[]{:S(2)}) collective-permute-start(f32[64,128]{1,0:T(8,128)S(1)} %root_solve.4.refs_0_), channel_id=1, source_target_pairs={{0,16},{8,24},{16,0},{24,8},{1,17},{9,25},{17,1},{25,9},{2,18},{10... | collective-permute-start | bytes 98312 | tf_op jit(solution)/shard_map/root_solve/ppermute | solution.py:86
  106.1 3.8 %collective-permute-done.50.refs_3_ = f32[64,128]{1,0:T(8,128)S(1)} collective-permute-done((f32[64,128]{1,0:T(8,128)S(1)}, f32[64,128]{1,0:T(8,128)S(1)}, u32[]{:S(2)}, u32[]{:S(2)}) %collective-permute-start.50) | collective-permute-done | bytes 32800 | tf_op jit(solution)/shard_map/root_solve/ppermute | solution.py:86
  116.3 1.6 %collective-permute-start.56 = (f32[128,128]{1,0:T(8,128)S(1)}, f32[128,128]{1,0:T(8,128)S(1)}, u32[]{:S(2)}, u32[]{:S(2)}) collective-permute-start(f32[128,128]{1,0:T(8,128)S(1)} %get-tuple-element.57), channel_id=1, source_target_pairs={{0,6},{1,7},{2,4},{3,5},{4,2},{5,3},{6,0},{7,1},{8,14},{9,15},{10,... | collective-permute-start | bytes 196616 | tf_op jit(solution)/shard_map/mid_upper/ppermute | solution.py:86
  119.7 2.0 %collective-permute-done.56.refs_6_ = f32[128,128]{1,0:T(8,128)S(1)} collective-permute-done((f32[128,128]{1,0:T(8,128)S(1)}, f32[128,128]{1,0:T(8,128)S(1)}, u32[]{:S(2)}, u32[]{:S(2)}) %collective-permute-start.56) | collective-permute-done | bytes 65568 | tf_op jit(solution)/shard_map/mid_upper/ppermute | solution.py:86
  126.6 1.6 %collective-permute-start.64 = (f32[128,128]{1,0:T(8,128)S(1)}, f32[128,128]{1,0:T(8,128)S(1)}, u32[]{:S(2)}, u32[]{:S(2)}) collective-permute-start(f32[128,128]{1,0:T(8,128)S(1)} %mid_upper.6.refs_0_), channel_id=1, source_target_pairs={{0,6},{1,7},{2,4},{3,5},{4,2},{5,3},{6,0},{7,1},{8,14},{9,15},{10,... | collective-permute-start | bytes 196616 | tf_op jit(solution)/shard_map/mid_upper/ppermute | solution.py:86
  130.2 1.8 %collective-permute-done.64.refs_6_ = f32[128,128]{1,0:T(8,128)S(1)} collective-permute-done((f32[128,128]{1,0:T(8,128)S(1)}, f32[128,128]{1,0:T(8,128)S(1)}, u32[]{:S(2)}, u32[]{:S(2)}) %collective-permute-start.64) | collective-permute-done | bytes 65568 | tf_op jit(solution)/shard_map/mid_upper/ppermute | solution.py:86
  133.2 1.6 %mid_upper.7 = (f32[128,128]{1,0:T(8,128)S(1)}, f32[64,128]{1,0:T(8,128)S(1)}, f32[64,128]{1,0:T(8,128)S(1)}, f32[64,128]{1,0:T(8,128)S(1)}, f32[64,128]{1,0:T(8...) custom-call(s32[2]{0:T(128)S(1)} %pad_add_fusion.ids, ...), custom_call_target="tpu_custom_call" | custom-call | flops 201326592 | bytes 1048576 | tf_op jit(solution)/shard_map/mid_upper/pallas_call | solution.py:344
  138.6 1.7 %collective-permute-start.71 = (f32[64,128]{1,0:T(8,128)S(1)}, f32[64,128]{1,0:T(8,128)S(1)}, u32[]{:S(2)}, u32[]{:S(2)}) collective-permute-start(f32[64,128]{1,0:T(8,128)S(1)} %get-tuple-element.65), channel_id=1, source_target_pairs={{0,6},{1,7},{2,4},{3,5},{4,2},{5,3},{6,0},{7,1},{8,14},{9,15},{10,... | collective-permute-start | bytes 98312 | tf_op jit(solution)/shard_map/leaf_upper/ppermute | solution.py:86
  141.2 2.2 %collective-permute-done.71.refs_6_ = f32[64,128]{1,0:T(8,128)S(1)} collective-permute-done((f32[64,128]{1,0:T(8,128)S(1)}, f32[64,128]{1,0:T(8,128)S(1)}, u32[]{:S(2)}, u32[]{:S(2)}) %collective-permute-start.71) | collective-permute-done | bytes 32800 | tf_op jit(solution)/shard_map/leaf_upper/ppermute | solution.py:86
  (210 shorter events, 89.7 us)
Async XLA Ops:
  3.9 6.5 %collective-permute-start = (f32[16,128]{1,0:T(8,128)S(1)}, f32[16,128]{1,0:T(8,128)S(1)}, u32[]{:S(2)}, u32[]{:S(2)}) collective-permute-start(f32[16,128]{1,0:T(8,128)S(1)} %get-tuple-element.41), channel_id=1, source_target_pairs={{0,8},{8,0},{16,24},{24,16},{1,9},{9,1},{17,25},{25,17},{2,10},{10... | collective-permute-start | bytes 24584 | tf_op jit(solution)/shard_map/right_hand_sides/ppermute | solution.py:86
  9.5 5.4 %collective-permute-start.2 = (f32[16,128]{1,0:T(8,128)S(1)}, f32[16,128]{1,0:T(8,128)S(1)}, u32[]{:S(2)}, u32[]{:S(2)}) collective-permute-start(f32[16,128]{1,0:T(8,128)S(1)} %get-tuple-element.43), channel_id=1, source_target_pairs={{0,24},{8,16},{16,8},{24,0},{1,25},{9,17},{17,9},{25,1},{2,26},{10... | collective-permute-start | bytes 24584 | tf_op jit(solution)/shard_map/right_hand_sides/ppermute | solution.py:86
  15.2 6.0 %collective-permute-start.4 = (f32[72,128]{1,0:T(8,128)S(1)}, f32[72,128]{1,0:T(8,128)S(1)}, u32[]{:S(2)}, u32[]{:S(2)}) collective-permute-start(f32[72,128]{1,0:T(8,128)S(1)} %right_hand_sides.3.refs_0_), channel_id=1, source_target_pairs={{0,2},{1,3},{2,0},{3,1},{4,6},{5,7},{6,4},{7,5},{8,10},{9,11},{10,... | collective-permute-start | bytes 110600 | tf_op jit(solution)/shard_map/leaf_lower/ppermute | solution.py:86
  28.6 6.4 %collective-permute-start.12 = (f32[64,128]{1,0:T(8,128)S(1)}, f32[64,128]{1,0:T(8,128)S(1)}, u32[]{:S(2)}, u32[]{:S(2)}) collective-permute-start(f32[64,128]{1,0:T(8,128)S(1)} %leaf_lower.1.refs_0_.refs_8_), channel_id=1, source_target_pairs={{0,3},{1,2},{2,1},{3,0},{4,7},{5,6},{6,5},{7,4},{8,11},{9,10},{10,... | collective-permute-start | bytes 98312 | tf_op jit(solution)/shard_map/mid_lower/ppermute | solution.py:86
  29.7 5.3 %collective-permute-start.13 = (f32[64,128]{1,0:T(8,128)S(1)}, f32[64,128]{1,0:T(8,128)S(1)}, u32[]{:S(2)}, u32[]{:S(2)}) collective-permute-start(f32[64,128]{1,0:T(8,128)S(1)} %leaf_lower.1.refs_0_.refs_8_), channel_id=1, source_target_pairs={{0,4},{1,5},{2,6},{3,7},{4,0},{5,1},{6,2},{7,3},{8,12},{9,13},{10,... | collective-permute-start | bytes 98312 | tf_op jit(solution)/shard_map/mid_lower/ppermute | solution.py:86
  39.3 5.3 %collective-permute-start.18 = (f32[128,128]{1,0:T(8,128)S(1)}, f32[128,128]{1,0:T(8,128)S(1)}, u32[]{:S(2)}, u32[]{:S(2)}) collective-permute-start(f32[128,128]{1,0:T(8,128)S(1)} %get-tuple-element.45.refs_0_), channel_id=1, source_target_pairs={{0,2},{1,3},{2,0},{3,1},{4,6},{5,7},{6,4},{7,5},{8,10},{9,11},{10,... | collective-permute-start | bytes 196616 | tf_op jit(solution)/shard_map/mid_lower/ppermute | solution.py:86
  40.1 5.4 %collective-permute-start.19 = (f32[128,128]{1,0:T(8,128)S(1)}, f32[128,128]{1,0:T(8,128)S(1)}, u32[]{:S(2)}, u32[]{:S(2)}) collective-permute-start(f32[128,128]{1,0:T(8,128)S(1)} %get-tuple-element.45.refs_0_), channel_id=1, source_target_pairs={{0,3},{1,2},{2,1},{3,0},{4,7},{5,6},{6,5},{7,4},{8,11},{9,10},{10,... | collective-permute-start | bytes 196616 | tf_op jit(solution)/shard_map/mid_lower/ppermute | solution.py:86
  42.8 5.4 %collective-permute-start.22 = (f32[128,128]{1,0:T(8,128)S(1)}, f32[128,128]{1,0:T(8,128)S(1)}, u32[]{:S(2)}, u32[]{:S(2)}) collective-permute-start(f32[128,128]{1,0:T(8,128)S(1)} %get-tuple-element.45.refs_0_), channel_id=1, source_target_pairs={{0,6},{1,7},{2,4},{3,5},{4,2},{5,3},{6,0},{7,1},{8,14},{9,15},{10,... | collective-permute-start | bytes 196616 | tf_op jit(solution)/shard_map/mid_lower/ppermute | solution.py:86
  50.8 5.3 %collective-permute-start.24 = (f32[128,128]{1,0:T(8,128)S(1)}, f32[128,128]{1,0:T(8,128)}, u32[]{:S(2)}, u32[]{:S(2)}) collective-permute-start(f32[128,128]{1,0:T(8,128)S(1)} %mid_lower.5.refs_0_.refs_8_), channel_id=1, source_target_pairs={{0,1},{1,0},{2,3},{3,2},{4,5},{5,4},{6,7},{7,6},{8,9},{9,8},{10,11... | collective-permute-start | bytes 196616 | tf_op jit(solution)/shard_map/root_cut/ppermute | solution.py:86
  51.0 6.7 %collective-permute-start.25 = (f32[128,128]{1,0:T(8,128)S(1)}, f32[128,128]{1,0:T(8,128)}, u32[]{:S(2)}, u32[]{:S(2)}) collective-permute-start(f32[128,128]{1,0:T(8,128)S(1)} %mid_lower.5.refs_0_.refs_8_), channel_id=1, source_target_pairs={{0,2},{1,3},{2,0},{3,1},{4,6},{5,7},{6,4},{7,5},{8,10},{9,11},{10,... | collective-permute-start | bytes 196616 | tf_op jit(solution)/shard_map/root_cut/ppermute | solution.py:86
  53.2 9.7 %collective-permute-start.26 = (f32[128,128]{1,0:T(8,128)S(1)}, f32[128,128]{1,0:T(8,128)}, u32[]{:S(2)}, u32[]{:S(2)}) collective-permute-start(f32[128,128]{1,0:T(8,128)S(1)} %mid_lower.5.refs_0_.refs_8_), channel_id=1, source_target_pairs={{0,3},{1,2},{2,1},{3,0},{4,7},{5,6},{6,5},{7,4},{8,11},{9,10},{10,... | collective-permute-start | bytes 196616 | tf_op jit(solution)/shard_map/root_cut/ppermute | solution.py:86
  54.4 8.6 %collective-permute-start.27 = (f32[128,128]{1,0:T(8,128)S(1)}, f32[128,128]{1,0:T(8,128)}, u32[]{:S(2)}, u32[]{:S(2)}) collective-permute-start(f32[128,128]{1,0:T(8,128)S(1)} %mid_lower.5.refs_0_.refs_8_), channel_id=1, source_target_pairs={{0,4},{1,5},{2,6},{3,7},{4,0},{5,1},{6,2},{7,3},{8,12},{9,13},{10,... | collective-permute-start | bytes 196616 | tf_op jit(solution)/shard_map/root_cut/ppermute | solution.py:86
  54.9 8.1 %collective-permute-start.28 = (f32[128,128]{1,0:T(8,128)S(1)}, f32[128,128]{1,0:T(8,128)}, u32[]{:S(2)}, u32[]{:S(2)}) collective-permute-start(f32[128,128]{1,0:T(8,128)S(1)} %mid_lower.5.refs_0_.refs_8_), channel_id=1, source_target_pairs={{0,5},{1,4},{2,7},{3,6},{4,1},{5,0},{6,3},{7,2},{8,13},{9,12},{10,... | collective-permute-start | bytes 196616 | tf_op jit(solution)/shard_map/root_cut/ppermute | solution.py:86
  56.1 6.9 %collective-permute-start.29 = (f32[128,128]{1,0:T(8,128)S(1)}, f32[128,128]{1,0:T(8,128)}, u32[]{:S(2)}, u32[]{:S(2)}) collective-permute-start(f32[128,128]{1,0:T(8,128)S(1)} %mid_lower.5.refs_0_.refs_8_), channel_id=1, source_target_pairs={{0,6},{1,7},{2,4},{3,5},{4,2},{5,3},{6,0},{7,1},{8,14},{9,15},{10,... | collective-permute-start | bytes 196616 | tf_op jit(solution)/shard_map/root_cut/ppermute | solution.py:86
  57.7 5.3 %collective-permute-start.30 = (f32[128,128]{1,0:T(8,128)S(1)}, f32[128,128]{1,0:T(8,128)}, u32[]{:S(2)}, u32[]{:S(2)}) collective-permute-start(f32[128,128]{1,0:T(8,128)S(1)} %mid_lower.5.refs_0_.refs_8_), channel_id=1, source_target_pairs={{0,7},{1,6},{2,5},{3,4},{4,3},{5,2},{6,1},{7,0},{8,15},{9,14},{10,... | collective-permute-start | bytes 196616 | tf_op jit(solution)/shard_map/root_cut/ppermute | solution.py:86
  67.5 6.1 %collective-permute-start.33 = (f32[64,128]{1,0:T(8,128)S(1)}, f32[64,128]{1,0:T(8,128)S(1)}, u32[]{:S(2)}, u32[]{:S(2)}) collective-permute-start(f32[64,128]{1,0:T(8,128)S(1)} %get-tuple-element.49), channel_id=1, source_target_pairs={{0,24},{8,16},{16,8},{24,0},{1,25},{9,17},{17,9},{25,1},{2,26},{10... | collective-permute-start | bytes 98312 | tf_op jit(solution)/shard_map/root_cut/ppermute | solution.py:86
  74.4 5.5 %collective-permute-start.36 = (f32[64,128]{1,0:T(8,128)S(1)}, f32[64,128]{1,0:T(8,128)S(1)}, u32[]{:S(2)}, u32[]{:S(2)}) collective-permute-start(f32[64,128]{1,0:T(8,128)S(1)} %root_cut.3.refs_0_), channel_id=1, source_target_pairs={{0,3},{1,2},{2,1},{3,0},{4,7},{5,6},{6,5},{7,4},{8,11},{9,10},{10,... | collective-permute-start | bytes 98312 | tf_op jit(solution)/shard_map/root_solve/ppermute | solution.py:86
  88.6 5.7 %collective-permute-start.43 = (f32[64,128]{1,0:T(8,128)S(1)}, f32[64,128]{1,0:T(8,128)S(1)}, u32[]{:S(2)}, u32[]{:S(2)}) collective-permute-start(f32[64,128]{1,0:T(8,128)S(1)} %root_solve.3.refs_0_), channel_id=1, source_target_pairs={{0,3},{1,2},{2,1},{3,0},{4,7},{5,6},{6,5},{7,4},{8,11},{9,10},{10,... | collective-permute-start | bytes 98312 | tf_op jit(solution)/shard_map/root_solve/ppermute | solution.py:86
  104.2 5.7 %collective-permute-start.50 = (f32[64,128]{1,0:T(8,128)S(1)}, f32[64,128]{1,0:T(8,128)S(1)}, u32[]{:S(2)}, u32[]{:S(2)}) collective-permute-start(f32[64,128]{1,0:T(8,128)S(1)} %root_solve.4.refs_0_), channel_id=1, source_target_pairs={{0,24},{8,16},{16,8},{24,0},{1,25},{9,17},{17,9},{25,1},{2,26},{10... | collective-permute-start | bytes 98312 | tf_op jit(solution)/shard_map/root_solve/ppermute | solution.py:86
  104.7 10.4 %collective-permute-start.58 = (f32[128,128]{1,0:T(8,128)S(1)}, f32[128,128]{1,0:T(8,128)S(1)}, u32[]{:S(2)}, u32[]{:S(2)}) collective-permute-start(f32[128,128]{1,0:T(8,128)S(1)} %mid_lower.5.refs_0_.refs_8_), channel_id=1, source_target_pairs={{0,8},{8,0},{16,24},{24,16},{1,9},{9,1},{17,25},{25,17},{2,10},{10... | collective-permute-start | bytes 196616 | tf_op jit(solution)/shard_map/root_cut/ppermute | solution.py:406
  113.4 5.6 %collective-permute-start.53 = (f32[128,128]{1,0:T(8,128)S(1)}, f32[128,128]{1,0:T(8,128)S(1)}, u32[]{:S(2)}, u32[]{:S(2)}) collective-permute-start(f32[128,128]{1,0:T(8,128)S(1)} %get-tuple-element.54), channel_id=1, source_target_pairs={{0,3},{1,2},{2,1},{3,0},{4,7},{5,6},{6,5},{7,4},{8,11},{9,10},{10,... | collective-permute-start | bytes 196616 | tf_op jit(solution)/shard_map/mid_upper/ppermute | solution.py:86
  116.3 5.4 %collective-permute-start.56 = (f32[128,128]{1,0:T(8,128)S(1)}, f32[128,128]{1,0:T(8,128)S(1)}, u32[]{:S(2)}, u32[]{:S(2)}) collective-permute-start(f32[128,128]{1,0:T(8,128)S(1)} %get-tuple-element.57), channel_id=1, source_target_pairs={{0,6},{1,7},{2,4},{3,5},{4,2},{5,3},{6,0},{7,1},{8,14},{9,15},{10,... | collective-permute-start | bytes 196616 | tf_op jit(solution)/shard_map/mid_upper/ppermute | solution.py:86
  123.9 6.0 %collective-permute-start.61 = (f32[128,128]{1,0:T(8,128)S(1)}, f32[128,128]{1,0:T(8,128)S(1)}, u32[]{:S(2)}, u32[]{:S(2)}) collective-permute-start(f32[128,128]{1,0:T(8,128)S(1)} %mid_upper.6.refs_0_), channel_id=1, source_target_pairs={{0,3},{1,2},{2,1},{3,0},{4,7},{5,6},{6,5},{7,4},{8,11},{9,10},{10,... | collective-permute-start | bytes 196616 | tf_op jit(solution)/shard_map/mid_upper/ppermute | solution.py:86
  126.6 5.3 %collective-permute-start.64 = (f32[128,128]{1,0:T(8,128)S(1)}, f32[128,128]{1,0:T(8,128)S(1)}, u32[]{:S(2)}, u32[]{:S(2)}) collective-permute-start(f32[128,128]{1,0:T(8,128)S(1)} %mid_upper.6.refs_0_), channel_id=1, source_target_pairs={{0,6},{1,7},{2,4},{3,5},{4,2},{5,3},{6,0},{7,1},{8,14},{9,15},{10,... | collective-permute-start | bytes 196616 | tf_op jit(solution)/shard_map/mid_upper/ppermute | solution.py:86
  135.9 5.3 %collective-permute-start.68 = (f32[64,128]{1,0:T(8,128)S(1)}, f32[64,128]{1,0:T(8,128)S(1)}, u32[]{:S(2)}, u32[]{:S(2)}) collective-permute-start(f32[64,128]{1,0:T(8,128)S(1)} %get-tuple-element.62), channel_id=1, source_target_pairs={{0,3},{1,2},{2,1},{3,0},{4,7},{5,6},{6,5},{7,4},{8,11},{9,10},{10,... | collective-permute-start | bytes 98312 | tf_op jit(solution)/shard_map/leaf_upper/ppermute | solution.py:86
  141.2 6.0 %collective-permute-start.80 = (f32[128,128]{1,0:T(8,128)S(1)}, f32[128,128]{1,0:T(8,128)S(1)}, u32[]{:S(2)}, u32[]{:S(2)}) collective-permute-start(f32[128,128]{1,0:T(8,128)S(1)} %get-tuple-element.68.mine), channel_id=1, source_target_pairs={{0,16},{8,24},{16,0},{24,8},{1,17},{9,25},{17,1},{25,9},{2,18},{10... | collective-permute-start | bytes 196616 | tf_op jit(solution)/shard_map/leaf_upper/ppermute | solution.py:480
  144.8 5.5 %collective-permute-start.74 = (f32[64,128]{1,0:T(8,128)S(1)}, f32[64,128]{1,0:T(8,128)S(1)}, u32[]{:S(2)}, u32[]{:S(2)}) collective-permute-start(f32[64,128]{1,0:T(8,128)S(1)} %leaf_upper.3.refs_0_), channel_id=1, source_target_pairs={{0,2},{1,3},{2,0},{3,1},{4,6},{5,7},{6,4},{7,5},{8,10},{9,11},{10,... | collective-permute-start | bytes 98312 | tf_op jit(solution)/shard_map/leaf_upper/ppermute | solution.py:86
  145.4 11.5 %collective-permute-start.75 = (f32[64,128]{1,0:T(8,128)S(1)}, f32[64,128]{1,0:T(8,128)S(1)}, u32[]{:S(2)}, u32[]{:S(2)}) collective-permute-start(f32[64,128]{1,0:T(8,128)S(1)} %leaf_upper.3.refs_0_), channel_id=1, source_target_pairs={{0,3},{1,2},{2,1},{3,0},{4,7},{5,6},{6,5},{7,4},{8,11},{9,10},{10,... | collective-permute-start | bytes 98312 | tf_op jit(solution)/shard_map/leaf_upper/ppermute | solution.py:86
  146.5 10.4 %collective-permute-start.76 = (f32[64,128]{1,0:T(8,128)S(1)}, f32[64,128]{1,0:T(8,128)}, u32[]{:S(2)}, u32[]{:S(2)}) collective-permute-start(f32[64,128]{1,0:T(8,128)S(1)} %leaf_upper.3.refs_0_), channel_id=1, source_target_pairs={{0,4},{1,5},{2,6},{3,7},{4,0},{5,1},{6,2},{7,3},{8,12},{9,13},{10,... | collective-permute-start | bytes 98312 | tf_op jit(solution)/shard_map/leaf_upper/ppermute | solution.py:86
  147.9 9.0 %collective-permute-start.77 = (f32[64,128]{1,0:T(8,128)S(1)}, f32[64,128]{1,0:T(8,128)}, u32[]{:S(2)}, u32[]{:S(2)}) collective-permute-start(f32[64,128]{1,0:T(8,128)S(1)} %leaf_upper.3.refs_0_), channel_id=1, source_target_pairs={{0,5},{1,4},{2,7},{3,6},{4,1},{5,0},{6,3},{7,2},{8,13},{9,12},{10,... | collective-permute-start | bytes 98312 | tf_op jit(solution)/shard_map/leaf_upper/ppermute | solution.py:86
  148.9 8.0 %collective-permute-start.78 = (f32[64,128]{1,0:T(8,128)S(1)}, f32[64,128]{1,0:T(8,128)}, u32[]{:S(2)}, u32[]{:S(2)}) collective-permute-start(f32[64,128]{1,0:T(8,128)S(1)} %leaf_upper.3.refs_0_), channel_id=1, source_target_pairs={{0,6},{1,7},{2,4},{3,5},{4,2},{5,3},{6,0},{7,1},{8,14},{9,15},{10,... | collective-permute-start | bytes 98312 | tf_op jit(solution)/shard_map/leaf_upper/ppermute | solution.py:86
  150.3 6.6 %collective-permute-start.79 = (f32[64,128]{1,0:T(8,128)S(1)}, f32[64,128]{1,0:T(8,128)}, u32[]{:S(2)}, u32[]{:S(2)}) collective-permute-start(f32[64,128]{1,0:T(8,128)S(1)} %leaf_upper.3.refs_0_), channel_id=1, source_target_pairs={{0,7},{1,6},{2,5},{3,4},{4,3},{5,2},{6,1},{7,0},{8,15},{9,14},{10,... | collective-permute-start | bytes 98312 | tf_op jit(solution)/shard_map/leaf_upper/ppermute | solution.py:86
  (69 other events, 432.2 us)

commit v2 on v1

v2 whole, which is shorter than its diff:
```python
import functools

import jax
import jax.numpy as jnp
from jax import lax
from jax.experimental import pallas as pl
from jax.experimental.pallas import tpu as pltpu
from jax.sharding import PartitionSpec as P

CAP = 2
LANES = 128
F32 = jnp.float32
BF16 = jnp.bfloat16
VM = pl.BlockSpec(memory_space=pltpu.VMEM)
SM = pl.BlockSpec(memory_space=pltpu.SMEM)


def split(x):
    high = x.astype(BF16)
    return high, (x - high.astype(F32)).astype(BF16)


def dot(a, b):
    return jnp.dot(a, b, preferred_element_type=F32)


def turned(x):
    half = x.shape[1] // 2
    return jnp.concatenate([-x[:, half:], x[:, :half]], axis=1)


def columns_of(x):
    return jnp.concatenate(split(x), axis=1), jnp.concatenate(split(turned(x)), axis=1)


def complex_dot(real, imag, w, wt):
    n = w.shape[1] // 2
    real_high, real_low = split(real)
    imag_high, imag_low = split(imag)
    wide = dot(real_high, w) + dot(imag_high, wt)
    rest = dot(real_low, w[:, :n]) + dot(imag_low, wt[:, :n])
    return (wide[:, :n] + wide[:, n:]) + rest


def apply_rows(matrix, x, step=512):
    depth = x.shape[0]
    step = min(step, depth)
    total = None
    for at in range(0, depth, step):
        w, wt = columns_of(x[at : at + step])
        part = complex_dot(matrix[0, :, at : at + step], matrix[1, :, at : at + step], w, wt)
        total = part if total is None else total + part
    return total


def unpacked(x):
    return jnp.concatenate([x[:, 32 * j : 32 * j + 32] for j in range(4)], axis=0)


def packed(x):
    rows = x.shape[0] // 4
    return jnp.concatenate([x[rows * j : rows * j + rows] for j in range(4)], axis=1)


def exchange(axis, blocks):
    return lax.all_to_all(blocks, axis, split_axis=0, concat_axis=0, tiled=True)


def to_all(out, value):
    for k in range(out.shape[0]):
        out[k] = value


def flat(ref):
    return ref[...].reshape(-1, ref.shape[2])


def row_blocks(out, value):
    rows = out.shape[1]
    for k in range(out.shape[0]):
        out[k] = value[rows * k : rows * k + rows]


def lanes_of(sources):
    real, imag = sources[0].T, sources[1].T
    zero = jnp.zeros_like(real)
    return jnp.concatenate([real, zero, imag, zero], axis=1)


def fields_of(x, forward, adjoint, where):
    y = x.T
    forward[(0, *where)] = y[0:32]
    forward[(1, *where)] = y[64:96]
    adjoint[(0, *where)] = y[32:64]
    adjoint[(1, *where)] = -y[96:128]


def pack_receivers(fronts, rows, data, block, offset, out):
    count = data.shape[1]
    groups, slots = out.shape[0], out.shape[1]
    down = lax.broadcasted_iota(jnp.int32, (count, count), 0)
    across = lax.broadcasted_iota(jnp.int32, (count, count), 1)
    eye = down == across
    block_row = block[...]
    block_col = jnp.sum(jnp.where(eye, block_row, 0), axis=1, keepdims=True)
    offset_col = jnp.sum(jnp.where(eye, offset[...], 0), axis=1, keepdims=True)
    same = (block_col == block_row) & (down < across)
    slot_row = block_row * CAP + jnp.sum(same.astype(jnp.int32), axis=0, keepdims=True)
    row_col = (block_col & (fronts - 1)) * rows + offset_col + 1
    width = data.shape[2]
    lane = lax.broadcasted_iota(jnp.int32, (count, width), 1)
    index = jnp.where(lane == 0, row_col, 0).astype(F32)
    lines = jnp.concatenate([index, data[0], jnp.zeros((count, width), F32), -data[1]], axis=1)
    pick = lax.broadcasted_iota(jnp.int32, (groups * slots, count), 0) == slot_row
    out[...] = jnp.dot(
        pick.astype(F32), lines, precision=lax.Precision.HIGHEST, preferred_element_type=F32
    ).reshape(groups, slots, LANES)


def message_rows(rows, slots):
    return max(rows, slots), 8 * -(-slots // (8 * LANES))


def pack_leaf(sources, arrived, out):
    lines = flat(arrived)
    slots = lines.shape[0]
    own = lanes_of(sources)
    body, tail = message_rows(own.shape[0], slots)
    lane = lax.broadcasted_iota(jnp.int32, (slots, LANES), 1)
    data = jnp.where((lane // 32) % 2 == 1, lines, 0.0)
    index = lines[:, 0:1]

    def padded(x):
        if x.shape[0] == body:
            return x
        return jnp.concatenate([x, jnp.zeros((body - x.shape[0], LANES), F32)], axis=0)

    value = padded(own) + padded(data)
    places = []
    for at in range(0, slots, LANES):
        size = min(LANES, slots - at)
        eye = lax.broadcasted_iota(jnp.int32, (size, size), 0) == lax.broadcasted_iota(
            jnp.int32, (size, size), 1
        )
        line = jnp.sum(jnp.where(eye, index[at : at + size], 0.0), axis=0, keepdims=True)
        places.append(jnp.concatenate([line, jnp.zeros((1, LANES - size), F32)], axis=1) if size < LANES else line)
    for k in range(out.shape[0]):
        out[k, 0:body, :] = value
        out[k, body:, :] = jnp.zeros((tail, LANES), F32)
        for r, line in enumerate(places):
            out[k, body + r : body + r + 1, :] = line


def leaf_lower(slots, matrix, messages, out, y_own, rhs):
    fronts, rows = messages.shape[0], matrix.shape[1]
    total = rows * fronts
    body, _ = message_rows(rows, slots)
    lane = lax.broadcasted_iota(jnp.int32, (slots, LANES), 1)
    taken = (lane // 32) % 2 == 1
    own = lax.broadcasted_iota(jnp.int32, (rows, LANES), 1)
    own = (own // 32) % 2 == 0
    for k in range(fronts):
        rhs[rows * k : rows * k + rows, :] = jnp.where(own, messages[k, 0:rows, :], 0.0)
    group = max(1, 512 // slots)
    for k in range(0, fronts, group):
        chosen = range(k, min(k + group, fronts))
        lines = jnp.concatenate([jnp.where(taken, messages[i, 0:slots, :], 0.0) for i in chosen], axis=0)
        index = jnp.concatenate(
            [
                messages[i, body + at // LANES : body + at // LANES + 1, 0 : min(LANES, slots - at)]
                for i in chosen
                for at in range(0, slots, LANES)
            ],
            axis=1,
        )
        row = lax.broadcasted_iota(jnp.int32, (total, index.shape[1]), 0)
        pick = (row + 1 == index.astype(jnp.int32)).astype(BF16)
        both = dot(pick, jnp.concatenate(split(lines), axis=1))
        rhs[...] += both[:, :LANES] + both[:, LANES:]
    y = apply_rows(matrix, rhs[...])
    to_all(out, y)
    y_own[...] = y


def leaf_to_mid(ids, matrix, sources, y, out):
    own = lanes_of(sources)
    first = ((ids[0] & 1) == 0).astype(F32)
    to_all(out, own * first - apply_rows(matrix, flat(y)))


def leaf_to_root(matrix, y, out):
    out[...] = apply_rows(matrix, flat(y))


def mid_lower(matrix, parts, out, y_own):
    y = apply_rows(matrix, flat(parts))
    to_all(out, y)
    y_own[...] = y


def mid_to_root(matrix, from_leaf, parts, out):
    cut = -(from_leaf[...] + apply_rows(matrix, flat(parts)))
    for q in range(out.shape[0]):
        piece = jnp.concatenate([cut[:, 16 * q : 16 * q + 16], cut[:, 64 + 16 * q : 80 + 16 * q]], axis=1)
        out[q] = packed(piece)


def root_quarter(ids, sources, out):
    rows = sources.shape[2]
    q = ids[0]
    start = pl.multiple_of((q & 1) * 16, 16)
    piece = jnp.concatenate([sources[0, pl.ds(start, 16), :], sources[1, pl.ds(start, 16), :]], axis=0)
    piece = piece * (q < 2).astype(F32)
    out[...] = packed(piece.T)


def root_sum(own, parts, out):
    total = own[...]
    for k in range(parts.shape[0]):
        total = total + parts[k]
    to_all(out, total)


def root_rows(matrix, parts, out):
    x = jnp.concatenate([unpacked(parts[k]) for k in range(parts.shape[0])], axis=0)
    to_all(out, packed(apply_rows(matrix, x)))


def apply_columns(matrix, x, out, step=256):
    w, wt = columns_of(x)
    for at in range(0, matrix.shape[1], step):
        out[at : at + step, :] = complex_dot(matrix[0, at : at + step, :], matrix[1, at : at + step, :], w, wt)


def root_to_mid(matrix, quarters, out, x_root, blocks):
    pieces = [unpacked(quarters[q]) for q in range(quarters.shape[0])]
    x = jnp.concatenate([p[:, :16] for p in pieces] + [p[:, 16:] for p in pieces], axis=1)
    x_root[...] = x
    apply_columns(matrix, x, blocks)
    row_blocks(out, blocks[...])


def root_to_leaf(matrix, x, out, forward, adjoint):
    apply_columns(matrix, x[...], out)
    fields_of(x[...], forward, adjoint, ())


def rest_of(parts, *refs):
    value = refs[0][...]
    for ref in refs[1:-1]:
        value = value + ref[...]
    tail = parts[0]
    for k in range(1, parts.shape[0]):
        tail = tail + parts[k]
    to_all(refs[-1], value - tail)


def mid_upper(matrix, coupling, from_root, parts, out, x_own, blocks):
    x = apply_rows(matrix, flat(parts))
    x_own[...] = x
    apply_columns(coupling, x, blocks)
    row_blocks(out, blocks[...] + from_root[...])


def leaf_upper(matrix, parts, forward, adjoint):
    fields_of(apply_rows(matrix, flat(parts)), forward, adjoint, ())


def mid_outputs(ids, mine, other, forward, adjoint):
    parent = ids[0] // 2
    fields_of(mine[...], forward, adjoint, (parent,))
    fields_of(other[...], forward, adjoint, (1 - parent,))


def body(
    leaf_lower_inv,
    leaf_upper_inv,
    leaf_to_mid_lower,
    leaf_to_root_lower,
    leaf_to_mid_upper,
    leaf_to_root_upper,
    mid_lower_inv,
    mid_upper_inv,
    mid_to_root_lower,
    mid_to_root_upper,
    root_lower_inv,
    root_upper_inv,
    leaf_sources,
    mid_sources,
    root_sources,
    receiver_data,
    receiver_block,
    receiver_offset,
):
    groups, fronts = lax.axis_size("leaf"), lax.axis_size("front")
    group, front = lax.axis_index("leaf"), lax.axis_index("front")
    ids = jnp.stack([group, front]).astype(jnp.int32)
    parent = group // 2
    n0, n1, n2 = leaf_sources.shape[1], mid_sources.shape[2], root_sources.shape[1]
    slots = fronts * CAP

    def own(array):
        return lax.dynamic_index_in_dim(array, parent, 1, keepdims=False)

    def kernel(fn, outs, *args, scratch=(), vmem=6, scalars=0):
        weights = max(a.size for a in args)
        return pl.pallas_call(
            fn,
            out_shape=[jax.ShapeDtypeStruct(shape, F32) for shape in outs],
            in_specs=[SM] * scalars + [VM] * (len(args) - scalars),
            out_specs=[VM] * len(outs),
            scratch_shapes=[pltpu.VMEM(shape, F32) for shape in scratch],
            compiler_params=pltpu.CompilerParams(vmem_limit_bytes=vmem * 2**20),
            cost_estimate=pl.CostEstimate(
                flops=weights * 6 * 128, bytes_accessed=weights * 4, transcendentals=0
            ),
        )(*args)

    leaf_sources = leaf_sources.transpose(0, 2, 1)
    mid_sources = mid_sources.transpose(0, 1, 3, 2)
    root_sources = root_sources.transpose(0, 2, 1)
    with jax.named_scope("right_hand_sides"):
        (payload,) = kernel(
            functools.partial(pack_receivers, fronts, n0),
            [(groups, slots, LANES)],
            receiver_data,
            receiver_block.reshape(1, -1),
            receiver_offset.reshape(1, -1),
        )
        arrived = exchange("leaf", payload)
        (message,) = kernel(
            pack_leaf, [(fronts, sum(message_rows(n0, groups * slots)), LANES)], leaf_sources, arrived
        )
    with jax.named_scope("leaf_lower"):
        y, y_leaf = kernel(
            functools.partial(leaf_lower, groups * slots),
            [(fronts, n0, LANES), (n0, LANES)],
            leaf_lower_inv[:, 0],
            exchange("front", message),
            scratch=[(n0 * fronts, LANES)],
        )
    with jax.named_scope("mid_lower"):
        y = exchange("front", y)
        (cut_mid,) = kernel(
            leaf_to_mid,
            [(fronts, n1, LANES)],
            ids,
            leaf_to_mid_lower[:, 0],
            own(mid_sources),
            y,
            scalars=1,
        )
        (from_leaf,) = kernel(leaf_to_root, [(n2, LANES)], leaf_to_root_lower[:, 0], y)
        parts, y_mid = kernel(
            mid_lower,
            [(fronts, n1, LANES), (n1, LANES)],
            own(mid_lower_inv),
            exchange("front", cut_mid),
        )
    with jax.named_scope("root_cut"):
        (quarters,) = kernel(
            mid_to_root,
            [(groups, n2 // 4, LANES)],
            own(mid_to_root_lower),
            from_leaf,
            exchange("front", parts),
        )
        y_sibling = lax.ppermute(y_mid, "leaf", [(i, i ^ 1) for i in range(groups)])
        (quarter,) = kernel(root_quarter, [(n2 // 4, LANES)], ids, root_sources, scalars=1)
        (cut_root,) = kernel(
            root_sum, [(fronts, n2 // 4, LANES)], quarter, exchange("leaf", quarters)
        )
    with jax.named_scope("root_solve"):
        (y_root,) = kernel(
            root_rows, [(fronts, n2 // 4, LANES)], root_lower_inv, exchange("front", cut_root)
        )
        (x_quarter,) = kernel(
            root_rows, [(groups, n2 // 4, LANES)], root_upper_inv, exchange("front", y_root)
        )
    with jax.named_scope("mid_upper"):
        blocks, x_root = kernel(
            root_to_mid,
            [(fronts, n1, LANES), (n2, LANES)],
            own(mid_to_root_upper),
            exchange("leaf", x_quarter),
            scratch=[(n1 * fronts, LANES)],
        )
        from_root, root_field, root_adjoint = kernel(
            root_to_leaf,
            [(n0 * fronts, LANES), (2, 32, n2), (2, 32, n2)],
            leaf_to_root_upper[:, 0],
            x_root,
        )
        (rest,) = kernel(
            rest_of, [(fronts, n1, LANES)], exchange("front", blocks), y_mid, y_sibling
        )
        blocks, x_mid = kernel(
            mid_upper,
            [(fronts, n0, LANES), (n1, LANES)],
            own(mid_upper_inv),
            leaf_to_mid_upper[:, 0],
            from_root,
            exchange("front", rest),
            scratch=[(n0 * fronts, LANES)],
        )
    with jax.named_scope("leaf_upper"):
        x_other = lax.ppermute(x_mid, "leaf", [(i, i ^ 2) for i in range(groups)])
        (rest,) = kernel(rest_of, [(fronts, n0, LANES)], exchange("front", blocks), y_leaf)
        mid_field, mid_adjoint = kernel(
            mid_outputs, [(2, 2, 32, n1)] * 2, ids, x_mid, x_other, scalars=1
        )
        leaf_field, leaf_adjoint = kernel(
            leaf_upper, [(2, 32, n0)] * 2, leaf_upper_inv[:, 0], exchange("front", rest)
        )
    return tuple(
        jnp.swapaxes(x, -1, -2)
        for x in (leaf_field, mid_field, root_field, leaf_adjoint, mid_adjoint, root_adjoint)
    )


def solution(mesh):
    in_specs = (
        P(None, "leaf", "front", None),
        P(None, "leaf", "front", None),
        P(None, "leaf", "front", None),
        P(None, "leaf", "front", None),
        P(None, "leaf", None, "front"),
        P(None, "leaf", None, "front"),
        P(None, None, "front", None),
        P(None, None, "front", None),
        P(None, None, "front", None),
        P(None, None, None, "front"),
        P(None, "front", None),
        P(None, "front", None),
        P(None, ("leaf", "front"), None),
        P(None, None, "front", None),
        P(None, "front", None),
        P(None, ("leaf", "front"), None),
        P(("leaf", "front"), None),
        P(("leaf", "front")),
    )
    out_specs = (
        P(None, ("leaf", "front"), None),
        P(None, None, "front", None),
        P(None, "front", None),
        P(None, ("leaf", "front"), None),
        P(None, None, "front", None),
        P(None, "front", None),
    )
    return jax.shard_map(body, mesh=mesh, in_specs=in_specs, out_specs=out_specs, check_vma=False)
```

time: 160 us -> 180 us (1.12)
  blocking collectives: 0 us -> 50.6 us
  starting transfers between devices: 78 us -> 31 us
  waiting for transfers between devices: 38.7 us -> 51.3 us
  Pallas kernels: 19.7 us -> 22.2 us
    ppermute x79 -> x0, starting transfers between devices: 77.8 us -> none  [exchange(): lax.ppermute(blocks[k], axis, [(i, i ^ k) for i in range(size)])]
    all_to_all x0 -> x5, blocking collectives: none -> 50.6 us  [exchange(): return lax.all_to_all(blocks, axis, split_axis=0, concat_axis=0, tiled=True)]
    all_to_all x0 -> x8, waiting for transfers between devices: none -> 42.5 us  [exchange(): return lax.all_to_all(blocks, axis, split_axis=0, concat_axis=0, tiled=True)]
    ppermute x79 -> x0, waiting for transfers between devices: 38.7 us -> none  [exchange(): lax.ppermute(blocks[k], axis, [(i, i ^ k) for i in range(size)])]
    all_to_all x0 -> x8, starting transfers between devices: none -> 28.7 us  [exchange(): return lax.all_to_all(blocks, axis, split_axis=0, concat_axis=0, tiled=True)]
    squeeze x4 -> x5, local copies, waits for them, and re-layouts: 1.92 us -> 7.87 us  [own(): return lax.dynamic_index_in_dim(array, parent, 1, keepdims=False)]
    ppermute x1, waiting for transfers between devices: 0.01 us -> 5.72 us  [body(): x_other = lax.ppermute(x_mid, 'leaf', [(i, i ^ 2) for i in range(groups)])]
    ppermute x1, waiting for transfers between devices: 0.01 us -> 3.06 us  [body(): y_sibling = lax.ppermute(y_mid, 'leaf', [(i, i ^ 1) for i in range(groups)])]
  transfers between devices with their start and end apart: 81 -> 10, of which waited for: 28 -> 9; matrix products, arithmetic and copies ran while one was open for 6% -> 4% of each run, Pallas kernels for 3% -> 2%
where the time goes in v2:
time: 180 us; the launch traced here: 178 us
  waiting for transfers between devices  51.3 us (28%)
  blocking collectives  50.6 us (28%)
  starting transfers between devices  31 us (17%)
  Pallas kernels  22.2 us (12%)
  local copies, waits for them, and re-layouts  22.1 us (12%)
    all_to_all x5, blocking collectives, exchange(): return lax.all_to_all(blocks, axis, split_axis=0, concat_axis=0, tiled=True)  50.6 us
    all_to_all x8, waiting for transfers between devices, exchange(): return lax.all_to_all(blocks, axis, split_axis=0, concat_axis=0, tiled=True)  42.5 us
    all_to_all x8, starting transfers between devices, exchange(): return lax.all_to_all(blocks, axis, split_axis=0, concat_axis=0, tiled=True)  28.7 us
    pallas_call x18, Pallas kernels, kernel(): pl.pallas_call(fn, out_shape=[jax.ShapeDtypeStruct(shape, F32) for shape...  22.2 us
    unnamed x44, local copies, waits for them, and re-layouts  14.3 us
    squeeze x5, local copies, waits for them, and re-layouts, own(): return lax.dynamic_index_in_dim(array, parent, 1, keepdims=False)  7.87 us
    ppermute x1, waiting for transfers between devices, body(): x_other = lax.ppermute(x_mid, 'leaf', [(i, i ^ 2) for i in range(groups)])  5.72 us
  transfers between devices with their start and end apart: 10, of which 9 were waited for; matrix products, arithmetic and copies ran while one was open for 4% of the time, Pallas kernels for 2%

profile of v2, /device:TPU:0, one launch (start us, length us, event | category | flops | bytes accessed | tf_op | source)
XLA Modules:
  0.0 178.3 jit_solution(620179257125093047)
XLA Ops:
  3.1 11.8 %all_to_all.65.arrived = f32[4,16,128]{2,1,0:T(8,128)S(1)} all-to-all(f32[4,16,128]{2,1,0:T(8,128)S(1)} %right_hand_sides.2), channel_id=1, replica_groups=mesh['leaf'=4,'front'=8] {'leaf'}, dimensions={0} | all-to-all | bytes 65536 | tf_op jit(solution)/shard_map/right_hand_sides/all_to_all | solution.py:66
  15.9 10.8 %all_to_all.66.messages = f32[8,72,128]{2,1,0:T(8,128)S(1)} all-to-all(f32[8,72,128]{2,1,0:T(8,128)S(1)} %right_hand_sides.3), channel_id=1, replica_groups=mesh['leaf'=4,'front'=8] {'front'}, dimensions={0} | all-to-all | bytes 589824 | tf_op jit(solution)/shard_map/leaf_lower/all_to_all | solution.py:66
  29.8 3.4 %all-to-all-start.2 = ((f32[8,64,128]{2,1,0:T(8,128)}), f32[8,64,128]{2,1,0:T(8,128)S(1)}, u32[]{:S(2)}, u32[]{:S(2)}) async-start(f32[8,64,128]{2,1,0:T(8,128)} %get-tuple-element.21), calls=%async_computation.2 | async-start | bytes 524288 | tf_op jit(solution)/shard_map/mid_lower/all_to_all | solution.py:66
  33.3 6.8 %all-to-all-done.2.y = f32[8,64,128]{2,1,0:T(8,128)S(1)} async-done(((f32[8,64,128]{2,1,0:T(8,128)}), f32[8,64,128]{2,1,0:T(8,128)S(1)}, u32[]{:S(2)}, u32[]{:S(2)}) %all-to-all-start.2) | async-done | bytes 262176 | tf_op jit(solution)/shard_map/mid_lower/all_to_all | solution.py:66
  40.1 1.9 %mid_lower.4 = f32[8,128,128]{2,1,0:T(8,128)} custom-call(s32[2]{0:T(128)S(1)} %pad_add_fusion.ids, f32[2,128,512]{2,1,0:T(8,128)S(1)} %bitcast.34, f32[2,32,128]{2,1,0:T(8,128)S(1)} %dynamic-slice_bitcast_fusion.4.sources, f32[8,64,128]{2,1,0:T(8,128)S(1)} %all-to-all-done.2.y), custom_call_target="tpu_custom_call" | custom-call | flops 100663296 | bytes 524288 | tf_op jit(solution)/shard_map/mid_lower/pallas_call | solution.py:307
  41.9 4.1 %all-to-all-start.3 = ((f32[8,128,128]{2,1,0:T(8,128)}), f32[8,128,128]{2,1,0:T(8,128)}, u32[]{:S(2)}, u32[]{:S(2)}) async-start(f32[8,128,128]{2,1,0:T(8,128)} %mid_lower.4), calls=%async_computation.3 | async-start | bytes 1048576 | tf_op jit(solution)/shard_map/mid_lower/all_to_all | solution.py:66
  46.2 9.6 %all-to-all-done.3.parts = f32[8,128,128]{2,1,0:T(8,128)} async-done(((f32[8,128,128]{2,1,0:T(8,128)}), f32[8,128,128]{2,1,0:T(8,128)}, u32[]{:S(2)}, u32[]{:S(2)}) %all-to-all-start.3) | async-done | bytes 524320 | tf_op jit(solution)/shard_map/mid_lower/all_to_all | solution.py:66
  55.8 1.6 mid_lower.5
  58.9 3.5 %all-to-all-start.4 = ((f32[8,128,128]{2,1,0:T(8,128)}), f32[8,128,128]{2,1,0:T(8,128)S(1)}, u32[]{:S(2)}, u32[]{:S(2)}) async-start(f32[8,128,128]{2,1,0:T(8,128)} %copy-done.8), calls=%async_computation.4 | async-start | bytes 1048576 | tf_op jit(solution)/shard_map/root_cut/all_to_all | solution.py:66
  62.4 3.3 %dynamic-slice_bitcast_fusion.matrix = f32[2,256,1024]{2,1,0:T(8,128)} fusion(f32[2,2,256,1024]{3,2,1,0:T(8,128)} %param.26, s32[]{:T(128)S(6)} %select_n.17), kind=kLoop, calls=%fused_computation | loop fusion | bytes 4194308 | tf_op jit(solution)/shard_map/root_cut/jit(dynamic_index_in_dim)/squeeze | solution.py:303
  66.3 5.8 %all-to-all-done.4.parts = f32[8,128,128]{2,1,0:T(8,128)S(1)} async-done(((f32[8,128,128]{2,1,0:T(8,128)}), f32[8,128,128]{2,1,0:T(8,128)S(1)}, u32[]{:S(2)}, u32[]{:S(2)}) %all-to-all-start.4) | async-done | bytes 524320 | tf_op jit(solution)/shard_map/root_cut/all_to_all | solution.py:66
  73.7 1.8 root_cut.4
  75.4 3.3 %all-to-all-start.5 = ((f32[4,64,128]{2,1,0:T(8,128)}), f32[4,64,128]{2,1,0:T(8,128)S(1)}, u32[]{:S(2)}, u32[]{:S(2)}) async-start(f32[4,64,128]{2,1,0:T(8,128)} %root_cut.4), calls=%async_computation.5 | async-start | bytes 262144 | tf_op jit(solution)/shard_map/root_cut/all_to_all | solution.py:66
  79.5 5.2 %all-to-all-done.5.parts = f32[4,64,128]{2,1,0:T(8,128)S(1)} async-done(((f32[4,64,128]{2,1,0:T(8,128)}), f32[4,64,128]{2,1,0:T(8,128)S(1)}, u32[]{:S(2)}, u32[]{:S(2)}) %all-to-all-start.5) | async-done | bytes 131104 | tf_op jit(solution)/shard_map/root_cut/all_to_all | solution.py:66
  84.7 9.3 %all_to_all.67.parts = f32[8,64,128]{2,1,0:T(8,128)S(1)} all-to-all(f32[8,64,128]{2,1,0:T(8,128)S(1)} %root_cut.5), channel_id=1, replica_groups=mesh['leaf'=4,'front'=8] {'front'}, dimensions={0} | all-to-all | bytes 524288 | tf_op jit(solution)/shard_map/root_solve/all_to_all | solution.py:66
  94.0 2.2 %copy-done.3 = f32[2,256,2048]{2,1,0:T(8,128)S(1)} copy-done((f32[2,256,2048]{2,1,0:T(8,128)S(1)}, f32[2,256,2048]{2,1,0:T(8,128)}, u32[]{:S(2)}) %copy-start.3) | copy-done | bytes 4194328
  96.2 1.9 %root_solve.2 = f32[8,64,128]{2,1,0:T(8,128)S(1)} custom-call(f32[2,256,2048]{2,1,0:T(8,128)S(1)} %copy-done.3, f32[8,64,128]{2,1,0:T(8,128)S(1)} %all_to_all.67.parts), custom_call_target="tpu_custom_call" | custom-call | flops 805306368 | bytes 4194304 | tf_op jit(solution)/shard_map/root_solve/pallas_call | solution.py:307
  98.2 9.3 %all_to_all.68.parts = f32[8,64,128]{2,1,0:T(8,128)S(1)} all-to-all(f32[8,64,128]{2,1,0:T(8,128)S(1)} %root_solve.2), channel_id=1, replica_groups=mesh['leaf'=4,'front'=8] {'front'}, dimensions={0} | all-to-all | bytes 524288 | tf_op jit(solution)/shard_map/root_solve/all_to_all | solution.py:66
  107.5 2.6 %root_solve.3 = f32[4,64,128]{2,1,0:T(8,128)} custom-call(f32[2,256,2048]{2,1,0:T(8,128)S(1)} %copy-done.4, f32[8,64,128]{2,1,0:T(8,128)S(1)} %all_to_all.68.parts), custom_call_target="tpu_custom_call" | custom-call | flops 805306368 | bytes 4194304 | tf_op jit(solution)/shard_map/root_solve/pallas_call | solution.py:307
  110.1 3.3 %all-to-all-start.8 = ((f32[4,64,128]{2,1,0:T(8,128)}), f32[4,64,128]{2,1,0:T(8,128)S(1)}, u32[]{:S(2)}, u32[]{:S(2)}) async-start(f32[4,64,128]{2,1,0:T(8,128)} %root_solve.3), calls=%async_computation.8 | async-start | bytes 262144 | tf_op jit(solution)/shard_map/mid_upper/all_to_all | solution.py:66
  113.4 3.1 %dynamic-slice_bitcast_fusion.1.matrix = f32[2,1024,256]{2,1,0:T(8,128)} fusion(f32[2,2,1024,256]{3,2,1,0:T(8,128)} %param.27, s32[]{:T(128)S(6)} %select_n.17), kind=kLoop, calls=%fused_computation.1 | loop fusion | bytes 4194308 | tf_op jit(solution)/shard_map/mid_upper/jit(dynamic_index_in_dim)/squeeze | solution.py:303
  116.5 2.8 %all-to-all-done.8.quarters = f32[4,64,128]{2,1,0:T(8,128)S(1)} async-done(((f32[4,64,128]{2,1,0:T(8,128)}), f32[4,64,128]{2,1,0:T(8,128)S(1)}, u32[]{:S(2)}, u32[]{:S(2)}) %all-to-all-start.8) | async-done | bytes 131104 | tf_op jit(solution)/shard_map/mid_upper/all_to_all | solution.py:66
  120.9 1.9 %mid_upper.4 = (f32[8,128,128]{2,1,0:T(8,128)}, f32[256,128]{1,0:T(8,128)S(1)}) custom-call(f32[2,1024,256]{2,1,0:T(8,128)S(1)} %copy-done.2, f32[4,64,128]{2,1,0:T(8,128)S(1)} %all-to-all-done.8.quarters), custom_call_target="tpu_custom_call" | custom-call | flops 402653184 | bytes 2097152 | tf_op jit(solution)/shard_map/mid_upper/pallas_call | solution.py:307
  122.9 3.5 %all-to-all-start.9 = ((f32[8,128,128]{2,1,0:T(8,128)}), f32[8,128,128]{2,1,0:T(8,128)S(1)}, u32[]{:S(2)}, u32[]{:S(2)}) async-start(f32[8,128,128]{2,1,0:T(8,128)} %get-tuple-element.25), calls=%async_computation.9 | async-start | bytes 1048576 | tf_op jit(solution)/shard_map/mid_upper/all_to_all | solution.py:66
  127.7 3.1 %collective-permute-done.refs_1_ = f32[128,128]{1,0:T(8,128)S(1)} collective-permute-done((f32[128,128]{1,0:T(8,128)S(1)}, f32[128,128]{1,0:T(8,128)S(1)}, u32[]{:S(2)}, u32[]{:S(2)}) %collective-permute-start) | collective-permute-done | bytes 65568 | tf_op jit(solution)/shard_map/root_cut/ppermute | solution.py:368
  130.8 5.3 %all-to-all-done.9.parts = f32[8,128,128]{2,1,0:T(8,128)S(1)} async-done(((f32[8,128,128]{2,1,0:T(8,128)}), f32[8,128,128]{2,1,0:T(8,128)S(1)}, u32[]{:S(2)}, u32[]{:S(2)}) %all-to-all-start.9) | async-done | bytes 524320 | tf_op jit(solution)/shard_map/mid_upper/all_to_all | solution.py:66
  136.9 4.1 %all-to-all-start.10 = ((f32[8,128,128]{2,1,0:T(8,128)}), f32[8,128,128]{2,1,0:T(8,128)}, u32[]{:S(2)}, u32[]{:S(2)}) async-start(f32[8,128,128]{2,1,0:T(8,128)} %mid_upper.6), calls=%async_computation.10 | async-start | bytes 1048576 | tf_op jit(solution)/shard_map/mid_upper/all_to_all | solution.py:66
  143.7 7.1 %all-to-all-done.10.parts = f32[8,128,128]{2,1,0:T(8,128)} async-done(((f32[8,128,128]{2,1,0:T(8,128)}), f32[8,128,128]{2,1,0:T(8,128)}, u32[]{:S(2)}, u32[]{:S(2)}) %all-to-all-start.10) | async-done | bytes 524320 | tf_op jit(solution)/shard_map/mid_upper/all_to_all | solution.py:66
  151.9 2.1 %mid_upper.7 = (f32[8,64,128]{2,1,0:T(8,128)S(1)}, f32[128,128]{1,0:T(8,128)S(1)}) custom-call(f32[2,128,1024]{2,1,0:T(8,128)S(1)} %dynamic-slice_bitcast_fusion.3.matrix, f32[2,512,128]{2,1,0:T(8,128)S(1)} %bitcast.35, f32[512,128]{1,0:T(8,128)S(1)} %get-tuple-element.24.from_root, f32[8,128,128]{2,1,0:T(8,128)} %all-to-all-done.10.parts), custom_call_target="tpu_custom_call" | custom-call | flops 201326592 | bytes 1048576 | tf_op jit(solution)/shard_map/mid_upper/pallas_call | solution.py:307
  153.9 9.3 %all_to_all.69.parts = f32[8,64,128]{2,1,0:T(8,128)S(1)} all-to-all(f32[8,64,128]{2,1,0:T(8,128)S(1)} %get-tuple-element.27), channel_id=1, replica_groups=mesh['leaf'=4,'front'=8] {'front'}, dimensions={0} | all-to-all | bytes 524288 | tf_op jit(solution)/shard_map/leaf_upper/all_to_all | solution.py:66
  164.8 3.4 %all-to-all-start.12 = ((f32[8,64,128]{2,1,0:T(8,128)}), f32[8,64,128]{2,1,0:T(8,128)S(1)}, u32[]{:S(2)}, u32[]{:S(2)}) async-start(f32[8,64,128]{2,1,0:T(8,128)} %leaf_upper.3), calls=%async_computation.12 | async-start | bytes 524288 | tf_op jit(solution)/shard_map/leaf_upper/all_to_all | solution.py:66
  169.2 5.7 %collective-permute-done.1.other = f32[128,128]{1,0:T(8,128)S(1)} collective-permute-done((f32[128,128]{1,0:T(8,128)S(1)}, f32[128,128]{1,0:T(8,128)S(1)}, u32[]{:S(2)}, u32[]{:S(2)}) %collective-permute-start.1) | collective-permute-done | bytes 65568 | tf_op jit(solution)/shard_map/leaf_upper/ppermute | solution.py:407
  (61 shorter events, 24.4 us)
Async XLA Ops:
  0.6 45.4 %copy-start = (f32[2,2,128,1024]{3,2,1,0:T(8,128)S(1)}, f32[2,2,128,1024]{3,2,1,0:T(8,128)}, u32[]{:S(2)}) copy-start(f32[2,2,128,1024]{3,2,1,0:T(8,128)} %param.24) | copy-start | bytes 6291460
  0.6 39.4 %copy-start.7 = (f32[2,1,128,512]{3,2,1,0:T(8,128)S(1)}, f32[2,1,128,512]{3,2,1,0:T(8,128)}, u32[]{:S(2)}) copy-start(f32[2,1,128,512]{3,2,1,0:T(8,128)} %param.20) | copy-start | bytes 1572868
  0.7 0.9 copy-start.17
  1.6 0.7 copy-start.19
  2.2 0.7 copy-start.20
  14.9 0.8 copy-start.18
  15.7 17.6 %copy-start.21 = (f32[2,2,128,32]{2,3,1,0:T(8,128)S(1)}, f32[2,2,128,32]{2,3,1,0:T(8,128)}, u32[]{:S(2)}) copy-start(f32[2,2,128,32]{2,3,1,0:T(8,128)} %param.31) | copy-start | bytes 196612
  26.7 1.0 copy-start.10
  29.2 0.6 copy-start.15
  29.8 10.3 %all-to-all-start.2 = ((f32[8,64,128]{2,1,0:T(8,128)}), f32[8,64,128]{2,1,0:T(8,128)S(1)}, u32[]{:S(2)}, u32[]{:S(2)}) async-start(f32[8,64,128]{2,1,0:T(8,128)} %get-tuple-element.21), calls=%async_computation.2 | async-start | bytes 524288 | tf_op jit(solution)/shard_map/mid_lower/all_to_all | solution.py:66
  41.9 13.9 %all-to-all-start.3 = ((f32[8,128,128]{2,1,0:T(8,128)}), f32[8,128,128]{2,1,0:T(8,128)}, u32[]{:S(2)}, u32[]{:S(2)}) async-start(f32[8,128,128]{2,1,0:T(8,128)} %mid_lower.4), calls=%async_computation.3 | async-start | bytes 1048576 | tf_op jit(solution)/shard_map/mid_lower/all_to_all | solution.py:66
  57.5 0.8 copy-start.8
  58.3 0.6 copy-start.12
  58.9 13.2 %all-to-all-start.4 = ((f32[8,128,128]{2,1,0:T(8,128)}), f32[8,128,128]{2,1,0:T(8,128)S(1)}, u32[]{:S(2)}, u32[]{:S(2)}) async-start(f32[8,128,128]{2,1,0:T(8,128)} %copy-done.8), calls=%async_computation.4 | async-start | bytes 1048576 | tf_op jit(solution)/shard_map/root_cut/all_to_all | solution.py:66
  62.4 3.3 %copy-start.6 = (f32[2,1,256,512]{3,2,1,0:T(8,128)S(1)}, f32[2,1,256,512]{3,2,1,0:T(8,128)}, u32[]{:S(2)}) copy-start(f32[2,1,256,512]{3,2,1,0:T(8,128)} %param.21) | copy-start | bytes 3145732
  65.7 13.1 %copy-start.14 = (f32[2,256,32]{1,2,0:T(8,128)S(1)}, f32[2,256,32]{1,2,0:T(8,128)}, u32[]{:S(2)}) copy-start(f32[2,256,32]{1,2,0:T(8,128)} %param.32) | copy-start | bytes 196612
  72.1 1.6 copy-start.1
  75.4 9.2 %all-to-all-start.5 = ((f32[4,64,128]{2,1,0:T(8,128)}), f32[4,64,128]{2,1,0:T(8,128)S(1)}, u32[]{:S(2)}, u32[]{:S(2)}) async-start(f32[4,64,128]{2,1,0:T(8,128)} %root_cut.4), calls=%async_computation.5 | async-start | bytes 262144 | tf_op jit(solution)/shard_map/root_cut/all_to_all | solution.py:66
  94.0 2.2 %copy-start.3 = (f32[2,256,2048]{2,1,0:T(8,128)S(1)}, f32[2,256,2048]{2,1,0:T(8,128)}, u32[]{:S(2)}) copy-start(f32[2,256,2048]{2,1,0:T(8,128)} %matrix.2) | copy-start | bytes 12582916
  96.2 11.3 %copy-start.4 = (f32[2,256,2048]{2,1,0:T(8,128)S(1)}, f32[2,256,2048]{2,1,0:T(8,128)}, u32[]{:S(2)}) copy-start(f32[2,256,2048]{2,1,0:T(8,128)} %matrix.3) | copy-start | bytes 12582916
  110.1 9.2 %all-to-all-start.8 = ((f32[4,64,128]{2,1,0:T(8,128)}), f32[4,64,128]{2,1,0:T(8,128)S(1)}, u32[]{:S(2)}, u32[]{:S(2)}) async-start(f32[4,64,128]{2,1,0:T(8,128)} %root_solve.3), calls=%async_computation.8 | async-start | bytes 262144 | tf_op jit(solution)/shard_map/mid_upper/all_to_all | solution.py:66
  119.3 1.6 copy-start.2
  120.9 5.5 %copy-start.13 = (f32[128,128]{1,0:T(8,128)S(1)}, f32[128,128]{1,0:T(8,128)}, u32[]{:S(2)}) copy-start(f32[128,128]{1,0:T(8,128)} %copy-done.12) | copy-start | bytes 196612
  122.9 13.2 %all-to-all-start.9 = ((f32[8,128,128]{2,1,0:T(8,128)}), f32[8,128,128]{2,1,0:T(8,128)S(1)}, u32[]{:S(2)}, u32[]{:S(2)}) async-start(f32[8,128,128]{2,1,0:T(8,128)} %get-tuple-element.25), calls=%async_computation.9 | async-start | bytes 1048576 | tf_op jit(solution)/shard_map/mid_upper/all_to_all | solution.py:66
  126.4 4.4 %collective-permute-start = (f32[128,128]{1,0:T(8,128)S(1)}, f32[128,128]{1,0:T(8,128)S(1)}, u32[]{:S(2)}, u32[]{:S(2)}) collective-permute-start(f32[128,128]{1,0:T(8,128)S(1)} %copy-done.13), channel_id=1, source_target_pairs={{0,8},{8,0},{16,24},{24,16},{1,9},{9,1},{17,25},{25,17},{2,10},{10... | collective-permute-start | bytes 196616 | tf_op jit(solution)/shard_map/root_cut/ppermute | solution.py:368
  136.9 13.9 %all-to-all-start.10 = ((f32[8,128,128]{2,1,0:T(8,128)}), f32[8,128,128]{2,1,0:T(8,128)}, u32[]{:S(2)}, u32[]{:S(2)}) async-start(f32[8,128,128]{2,1,0:T(8,128)} %mid_upper.6), calls=%async_computation.10 | async-start | bytes 1048576 | tf_op jit(solution)/shard_map/mid_upper/all_to_all | solution.py:66
  141.1 1.5 copy-start.5
  150.8 1.0 copy-start.9
  163.3 0.8 copy-start.16
  164.8 11.4 %all-to-all-start.12 = ((f32[8,64,128]{2,1,0:T(8,128)}), f32[8,64,128]{2,1,0:T(8,128)S(1)}, u32[]{:S(2)}, u32[]{:S(2)}) async-start(f32[8,64,128]{2,1,0:T(8,128)} %leaf_upper.3), calls=%async_computation.12 | async-start | bytes 524288 | tf_op jit(solution)/shard_map/leaf_upper/all_to_all | solution.py:66
  168.2 6.7 %collective-permute-start.1 = (f32[128,128]{1,0:T(8,128)S(1)}, f32[128,128]{1,0:T(8,128)S(1)}, u32[]{:S(2)}, u32[]{:S(2)}) collective-permute-start(f32[128,128]{1,0:T(8,128)S(1)} %get-tuple-element.30.mine), channel_id=1, source_target_pairs={{0,16},{8,24},{16,0},{24,8},{1,17},{9,25},{17,1},{25,9},{2,18},{10... | collective-permute-start | bytes 196616 | tf_op jit(solution)/shard_map/leaf_upper/ppermute | solution.py:407
  176.2 1.0 copy-start.11

commit v3 on v0

v3 whole, which is shorter than its diff:
```python
import functools

import jax
import jax.numpy as jnp
from jax import lax
from jax.experimental import pallas as pl
from jax.experimental.pallas import tpu as pltpu
from jax.sharding import PartitionSpec as P

CAP = 2
LANES = 128
COLS = 32
F32 = jnp.float32
BF16 = jnp.bfloat16
VM = pl.BlockSpec(memory_space=pltpu.VMEM)
HB = pl.BlockSpec(memory_space=pltpu.HBM)


def split(x):
    high = x.astype(BF16)
    return high, (x - high.astype(F32)).astype(BF16)


def dot(a, b):
    return jnp.dot(a, b, preferred_element_type=F32)


def complex_dot(matrix, x):
    half = x.shape[1] // 2
    turned = jnp.concatenate([-x[:, half:], x[:, :half]], axis=1)
    both = jnp.concatenate([x, turned], axis=0)
    columns = jnp.concatenate(split(both), axis=1)
    product = dot(matrix, columns)
    rows, n = product.shape[0] // 2, x.shape[1]
    return (product[:rows, n:] + product[rows:, :n]) + product[:rows, :n]


def pack(x):
    chunks = LANES // x.shape[1]
    rows = x.shape[0] // chunks
    return jnp.concatenate([x[rows * j : rows * j + rows] for j in range(chunks)], axis=1)


def unpack(x, width):
    return jnp.concatenate([x[:, at : at + width] for at in range(0, LANES, width)], axis=0)


def halves(x):
    c = COLS
    return (
        jnp.concatenate([x[:, :c], x[:, 2 * c : 3 * c]], axis=1),
        jnp.concatenate([x[:, c : 2 * c], x[:, 3 * c :]], axis=1),
    )


def joined(forward, adjoint):
    c = COLS
    return jnp.concatenate([forward[:, :c], adjoint[:, :c], forward[:, c:], adjoint[:, c:]], axis=1)


def own_first(group, forward, adjoint):
    even = (group & 1) == 0
    return jnp.where(even, forward, adjoint), jnp.where(even, adjoint, forward)


def by_solve(group, own, other):
    even = (group & 1) == 0
    return joined(jnp.where(even, own, other), jnp.where(even, other, own))


def assemble(where, parts, here, width=LANES):
    rows = parts[0].shape[0] * (LANES // width)
    for k, part in enumerate(parts):
        start = pl.multiple_of((here ^ k) * rows, 8)
        where[pl.ds(start, rows), :] = part[...] if width == LANES else unpack(part[...], width)


def fields_of(x, forward, adjoint, where):
    y = x.T
    c = COLS
    forward[(0, *where)] = y[0:c]
    forward[(1, *where)] = y[2 * c : 3 * c]
    adjoint[(0, *where)] = y[c : 2 * c]
    adjoint[(1, *where)] = -y[3 * c :]


def swap(axis, x, k):
    size = lax.axis_size(axis)
    return lax.ppermute(x, axis, [(i, i ^ k) for i in range(size)])


def gather_front(x):
    fronts = lax.axis_size("front")
    mine = [x] + [swap("front", x, k) for k in range(2, fronts, 2)]
    other = [swap("front", y, 1) for y in mine]
    return [block for pair in zip(mine, other) for block in pair]


def kernel(fn, outs, *args, scratch=(), vmem=8, work=0, hbm=()):
    outs = [o if isinstance(o[0], tuple) else (o, F32) for o in outs]
    return pl.pallas_call(
        fn,
        out_shape=[jax.ShapeDtypeStruct(*o) for o in outs],
        in_specs=[HB if i in hbm else VM for i in range(len(args))],
        out_specs=[VM] * len(outs),
        scratch_shapes=list(scratch),
        compiler_params=pltpu.CompilerParams(vmem_limit_bytes=vmem * 2**20),
        cost_estimate=pl.CostEstimate(flops=work, bytes_accessed=work // 700, transcendentals=0),
    )(*args)


def load_matrices(picks, *refs):
    count = len(picks)
    sources, outs, buffers, sems = (
        refs[:count],
        refs[count : 2 * count],
        refs[2 * count : 3 * count],
        refs[3 * count],
    )
    parent = lax.axis_index("leaf") // 2
    copies = []
    for i, (src, pick) in enumerate(zip(sources, picks)):
        rows = buffers[i].shape[1]
        step = rows // 2 if rows >= 128 else rows
        for n, at in enumerate(range(0, rows, step)):
            span = pl.ds(at, step)
            view = src.at[:, span, :] if pick is None else src.at[:, parent if pick == "own" else 0, span, :]
            copy = pltpu.make_async_copy(view, buffers[i].at[:, span, :], sems.at[2 * i + n])
            copy.start()
            copies.append((i, at, step, copy))
    for i, at, step, copy in copies:
        copy.wait()
        rows, depth = buffers[i].shape[1:]
        for part in range(2):
            high, low = split(buffers[i][part, at : at + step, :])
            outs[i][at : at + step, part * depth : part * depth + depth] = high
            outs[i][rows + at : rows + at + step, part * depth : part * depth + depth] = low


def load(*matrices):
    shapes = [m.shape[-2:] for m, _ in matrices]
    size = sum(r * d for r, d in shapes)
    return kernel(
        functools.partial(load_matrices, tuple(pick for _, pick in matrices)),
        [((2 * r, 2 * d), BF16) for r, d in shapes],
        *[m for m, _ in matrices],
        scratch=[pltpu.VMEM((2, r, d), F32) for r, d in shapes]
        + [pltpu.SemaphoreType.DMA((2 * len(shapes),))],
        hbm=range(len(shapes)),
        vmem=4 + -(-size * 8 // 2**20),
        work=size * 1000,
    )


def pack_receivers(fronts, rows, data_hbm, block_hbm, offset_hbm, *refs):
    groups = lax.axis_size("leaf")
    outs = refs[:groups]
    data, block, offset, sems = refs[groups:]
    copies = [
        pltpu.make_async_copy(src, dst, sems.at[i])
        for i, (src, dst) in enumerate(((data_hbm, data), (block_hbm, block), (offset_hbm, offset)))
    ]
    for copy in copies:
        copy.start()
    for copy in copies:
        copy.wait()
    group = lax.axis_index("leaf")
    count = data.shape[1]
    slots = fronts * CAP
    down = lax.broadcasted_iota(jnp.int32, (count, count), 0)
    across = lax.broadcasted_iota(jnp.int32, (count, count), 1)
    eye = down == across
    block_row = block[...]
    block_col = jnp.sum(jnp.where(eye, block_row, 0), axis=1, keepdims=True)
    offset_col = jnp.sum(jnp.where(eye, offset[...], 0), axis=1, keepdims=True)
    same = (block_col == block_row) & (down < across)
    slot_row = block_row * CAP + jnp.sum(same.astype(jnp.int32), axis=0, keepdims=True)
    row_col = (block_col & (fronts - 1)) * rows + offset_col + 1
    lane = lax.broadcasted_iota(jnp.int32, (count, COLS), 1)
    index = jnp.where(lane == 0, row_col, 0).astype(F32)
    lines = jnp.concatenate([index, data[0], jnp.zeros((count, COLS), F32), -data[1]], axis=1)
    for k, out in enumerate(outs):
        first = (group ^ k) * slots
        pick = lax.broadcasted_iota(jnp.int32, (slots, count), 0) + first == slot_row
        out[...] = jnp.dot(
            pick.astype(F32), lines, precision=lax.Precision.HIGHEST, preferred_element_type=F32
        )


def load_sources(leaf_hbm, mid_hbm, root_hbm, leaf_out, mid_out, root_out, leaf, mid, root, sems):
    group = lax.axis_index("leaf")
    copies = [
        pltpu.make_async_copy(src, dst, sems.at[i])
        for i, (src, dst) in enumerate(
            ((leaf_hbm, leaf), (mid_hbm.at[:, group // 2], mid), (root_hbm, root))
        )
    ]
    for copy in copies:
        copy.start()
    for copy in copies:
        copy.wait()
    forward = ((group & 1) == 0).astype(F32)
    real, imag = leaf[0].T, leaf[1].T
    zero = jnp.zeros_like(real)
    leaf_out[...] = jnp.concatenate([real, zero, imag, zero], axis=1)
    mid_out[...] = pack(jnp.concatenate([mid[0], mid[1]], axis=0).T) * forward
    width = COLS // 2
    low = jnp.concatenate([root[0, :width], root[1, :width]], axis=0)
    high = jnp.concatenate([root[0, width:], root[1, width:]], axis=0)
    root_out[...] = pack(jnp.where(group < 2, low, high).T) * forward


def message_rows(rows, slots):
    return max(rows, slots), 8 * -(-slots // (8 * LANES))


def pack_leaf(own, *refs):
    arrived, out = refs[:-1], refs[-1]
    lines = jnp.concatenate([ref[...] for ref in arrived], axis=0)
    slots = lines.shape[0]
    body, tail = message_rows(own.shape[0], slots)
    lane = lax.broadcasted_iota(jnp.int32, (slots, LANES), 1)
    data = jnp.where((lane // COLS) % 2 == 1, lines, 0.0)
    index = lines[:, 0:1]

    def padded(x):
        if x.shape[0] == body:
            return x
        return jnp.concatenate([x, jnp.zeros((body - x.shape[0], LANES), F32)], axis=0)

    out[0:body, :] = padded(own[...]) + padded(data)
    out[body:, :] = jnp.zeros((tail, LANES), F32)
    for at in range(0, slots, LANES):
        size = min(LANES, slots - at)
        eye = lax.broadcasted_iota(jnp.int32, (size, size), 0) == lax.broadcasted_iota(
            jnp.int32, (size, size), 1
        )
        line = jnp.sum(jnp.where(eye, index[at : at + size], 0.0), axis=0, keepdims=True)
        out[body + at // LANES : body + at // LANES + 1, 0:size] = line


def leaf_lower(slots, matrix, *refs):
    messages, (out, rhs) = refs[:-2], refs[-2:]
    fronts, rows = len(messages), out.shape[0]
    here = lax.axis_index("front")
    total = rows * fronts
    body, _ = message_rows(rows, slots)
    lane = lax.broadcasted_iota(jnp.int32, (slots, LANES), 1)
    taken = (lane // COLS) % 2 == 1
    own = lax.broadcasted_iota(jnp.int32, (rows, LANES), 1)
    own = (own // COLS) % 2 == 0
    for k in range(fronts):
        start = pl.multiple_of((here ^ k) * rows, 8)
        rhs[pl.ds(start, rows), :] = jnp.where(own, messages[k][0:rows, :], 0.0)
    group = max(1, 512 // slots)
    for k in range(0, fronts, group):
        chosen = messages[k : k + group]
        lines = jnp.concatenate([jnp.where(taken, ref[0:slots, :], 0.0) for ref in chosen], axis=0)
        index = jnp.concatenate(
            [
                ref[body + at // LANES : body + at // LANES + 1, 0 : min(LANES, slots - at)]
                for ref in chosen
                for at in range(0, slots, LANES)
            ],
            axis=1,
        )
        row = lax.broadcasted_iota(jnp.int32, (total, index.shape[1]), 0)
        pick = (row + 1 == index.astype(jnp.int32)).astype(BF16)
        both = dot(pick, jnp.concatenate(split(lines), axis=1))
        rhs[...] += both[:, :LANES] + both[:, LANES:]
    out[...] = complex_dot(matrix[...], rhs[...])


def leaf_to_mid(matrix, sources, *refs):
    parts, (keep, send, full) = refs[:-3], refs[-3:]
    assemble(full, parts, lax.axis_index("front"))
    mine, theirs = own_first(lax.axis_index("leaf"), *halves(complex_dot(matrix[...], full[...])))
    keep[...] = sources[...] - pack(mine)
    send[...] = -pack(theirs)


def leaf_to_root(matrix, full, keep, send):
    keep[...], send[...] = own_first(lax.axis_index("leaf"), *halves(complex_dot(matrix[...], full[...])))


def add(*refs):
    total = refs[0][...]
    for ref in refs[1:-1]:
        total = total + ref[...]
    refs[-1][...] = total


def mid_lower(matrix, *refs):
    parts, (out, whole) = refs[:-2], refs[-2:]
    assemble(whole, parts, lax.axis_index("front"), 2 * COLS)
    out[...] = pack(complex_dot(matrix[...], whole[...]))


def mid_to_root(matrix, kept, came, sources, *refs):
    parts, (keep, send, full) = refs[:-3], refs[-3:]
    assemble(full, parts, lax.axis_index("front"), 2 * COLS)
    cut = -(kept[...] + came[...] + complex_dot(matrix[...], full[...]))
    width = COLS // 2
    low = pack(jnp.concatenate([cut[:, :width], cut[:, COLS : COLS + width]], axis=1))
    high = pack(jnp.concatenate([cut[:, width:COLS], cut[:, COLS + width :]], axis=1))
    first = lax.axis_index("leaf") < 2
    keep[...] = jnp.where(first, low, high) + sources[...]
    send[...] = jnp.where(first, high, low)


def root_rows(matrix, *refs):
    parts, (out, whole) = refs[:-2], refs[-2:]
    assemble(whole, parts, lax.axis_index("front"), COLS)
    out[...] = pack(complex_dot(matrix[...], whole[...]))


def halved(value, keep, send):
    rows = keep.shape[0]
    odd = (lax.axis_index("front") & 1) == 1
    low, high = value[:rows], value[rows:]
    keep[...] = jnp.where(odd, high, low)
    send[...] = jnp.where(odd, low, high)


def root_to_mid(matrix, mine, other, keep, send, x_root):
    first = lax.axis_index("leaf") < 2
    mine, other = unpack(mine[...], COLS), unpack(other[...], COLS)
    low, high = jnp.where(first, mine, other), jnp.where(first, other, mine)
    width = COLS // 2
    x = jnp.concatenate([low[:, :width], high[:, :width], low[:, width:], high[:, width:]], axis=1)
    x_root[...] = pack(x)
    halved(pack(complex_dot(matrix[...], x)), keep, send)


def root_to_leaf(matrix, mine, other, out, forward, adjoint):
    x = by_solve(lax.axis_index("leaf"), unpack(mine[...], 2 * COLS), unpack(other[...], 2 * COLS))
    out[...] = complex_dot(matrix[...], x)
    fields_of(x, forward, adjoint, ())


def add_halves(kept, came, first, second):
    rows = first.shape[0]
    first[...] = kept[0:rows, :] + came[0:rows, :]
    second[...] = kept[rows:, :] + came[rows:, :]


def add_pair(a, b, c, d, first, second):
    first[...] = a[...] + b[...]
    second[...] = c[...] + d[...]


def sum_front(kept, sent):
    fronts = lax.axis_size("front")
    rows = kept.shape[0] // 2
    shapes = [(rows, LANES)] * 2
    a, b = kernel(add_halves, shapes, kept, swap("front", sent, 1))
    hops = [1 << i for i in range(1, fronts.bit_length() - 1)]
    for i, hop in enumerate(hops):
        back = hops[-1 - i]
        a, b = kernel(add_pair, shapes, a, swap("front", a, hop), b, swap("front", b, back))
    return [a, b, swap("front", a, 1), swap("front", b, 1)]


def summed(pieces):
    a, b, c, d = (ref[...] for ref in pieces)
    odd = (lax.axis_index("front") & 1) == 1
    mine, theirs = jnp.concatenate([a, b], axis=0), jnp.concatenate([c, d], axis=0)
    return jnp.concatenate([jnp.where(odd, theirs, mine), jnp.where(odd, mine, theirs)], axis=0)


def mid_upper(matrix, y, *refs):
    tail, out = unpack(summed(refs[:4]), 2 * COLS), refs[4]
    out[...] = pack(complex_dot(matrix[...], y[...] - tail))


def mid_to_leaf(matrix, from_root, mine, other, keep, send, x_mid):
    x = by_solve(lax.axis_index("leaf"), unpack(mine[...], 2 * COLS), unpack(other[...], 2 * COLS))
    x_mid[...] = x
    halved(complex_dot(matrix[...], x) + from_root[...], keep, send)


def leaf_upper(matrix, y, *refs):
    forward, adjoint = refs[4:]
    fields_of(complex_dot(matrix[...], y[...] - summed(refs[:4])), forward, adjoint, ())


def mid_outputs(mine, other, forward, adjoint):
    parent = lax.axis_index("leaf") // 2
    fields_of(mine[...], forward, adjoint, (parent,))
    fields_of(other[...], forward, adjoint, (1 - parent,))


def after(x, *others):
    return lax.optimization_barrier((x, *others))[0]


def body(
    leaf_lower_inv,
    leaf_upper_inv,
    leaf_to_mid_lower,
    leaf_to_root_lower,
    leaf_to_mid_upper,
    leaf_to_root_upper,
    mid_lower_inv,
    mid_upper_inv,
    mid_to_root_lower,
    mid_to_root_upper,
    root_lower_inv,
    root_upper_inv,
    leaf_sources,
    mid_sources,
    root_sources,
    receiver_data,
    receiver_block,
    receiver_offset,
):
    groups, fronts = lax.axis_size("leaf"), lax.axis_size("front")
    n0, n1, n2 = leaf_sources.shape[1], mid_sources.shape[2], root_sources.shape[1]
    s0, s1, s2 = n0 * fronts, n1 * fronts, n2 * fronts
    slots, count = fronts * CAP, receiver_data.shape[1]
    dma = pltpu.SemaphoreType.DMA

    with jax.named_scope("right_hand_sides"):
        payload = kernel(
            functools.partial(pack_receivers, fronts, n0),
            [(slots, LANES)] * groups,
            receiver_data,
            receiver_block.reshape(1, -1),
            receiver_offset.reshape(1, -1),
            scratch=[
                pltpu.VMEM((2, count, COLS), F32),
                pltpu.VMEM((1, count), jnp.int32),
                pltpu.VMEM((1, count), jnp.int32),
                dma((3,)),
            ],
            hbm=range(3),
        )
        arrived = [payload[0]] + [swap("leaf", payload[k], k) for k in range(1, groups)]
        leaf_own, mid_own, root_own = kernel(
            load_sources,
            [(n0, LANES), (n1 // 2, LANES), (n2 // 4, LANES)],
            after(leaf_sources.transpose(0, 2, 1), *payload),
            mid_sources.transpose(0, 1, 3, 2),
            root_sources.transpose(0, 2, 1),
            scratch=[
                pltpu.VMEM((2, COLS, n0), F32),
                pltpu.VMEM((2, COLS, n1), F32),
                pltpu.VMEM((2, COLS, n2), F32),
                dma((3,)),
            ],
            hbm=range(3),
        )
        ll, l2m = load((after(leaf_lower_inv, leaf_own), "leaf"), (leaf_to_mid_lower, "leaf"))
        (message,) = kernel(
            pack_leaf, [(sum(message_rows(n0, groups * slots)), LANES)], after(leaf_own, ll), *arrived
        )
    with jax.named_scope("leaf_lower"):
        messages = gather_front(message)
        ml, m2r = load((after(mid_lower_inv, message), "own"), (mid_to_root_lower, "own"))
        (y_leaf,) = kernel(
            functools.partial(leaf_lower, groups * slots),
            [(n0, LANES)],
            after(ll, ml),
            *messages,
            scratch=[pltpu.VMEM((s0, LANES), F32)],
        )
    with jax.named_scope("mid_lower"):
        parts = gather_front(y_leaf)
        (l2r,) = load((after(leaf_to_root_lower, y_leaf), "leaf"))
        keep, send, y_full = kernel(
            leaf_to_mid,
            [(n1 // 2, LANES), (n1 // 2, LANES), (s0, LANES)],
            after(l2m, l2r),
            mid_own,
            *parts,
        )
        came = swap("leaf", send, 1)
        root_kept, root_sent = kernel(leaf_to_root, [(n2, 2 * COLS)] * 2, l2r, after(y_full, send))
        (cut_mid,) = kernel(add, [(n1 // 2, LANES)], after(keep, root_kept), came)
        parts = gather_front(cut_mid)
        root_came = swap("leaf", root_sent, 1)
        (rl,) = load((after(root_lower_inv, cut_mid), None))
        (y_mid,) = kernel(
            mid_lower,
            [(n1 // 2, LANES)],
            after(ml, rl),
            *parts,
            scratch=[pltpu.VMEM((s1, 2 * COLS), F32)],
        )
    with jax.named_scope("root_cut"):
        parts = gather_front(y_mid)
        (ru,) = load((after(root_upper_inv, y_mid), None))
        keep, send, y_mid_full = kernel(
            mid_to_root,
            [(n2 // 4, LANES), (n2 // 4, LANES), (s1, 2 * COLS)],
            after(m2r, ru),
            root_kept,
            root_came,
            root_own,
            *parts,
        )
        came = swap("leaf", send, 2)
        mu, l2r_up = load((after(mid_upper_inv, send), "own"), (leaf_to_root_upper, "leaf"))
        (cut_root,) = kernel(add, [(n2 // 4, LANES)], after(keep, mu), came)
    with jax.named_scope("root_solve"):
        parts = gather_front(cut_root)
        (m2r_up,) = load((after(mid_to_root_upper, cut_root), "own"))
        (y_root,) = kernel(
            root_rows,
            [(n2 // 4, LANES)],
            after(rl, m2r_up),
            *parts,
            scratch=[pltpu.VMEM((s2, COLS), F32)],
        )
        parts = gather_front(y_root)
        l2m_up, lu = load((after(leaf_to_mid_upper, y_root), "leaf"), (leaf_upper_inv, "leaf"))
        (x_root,) = kernel(
            root_rows,
            [(n2 // 4, LANES)],
            after(ru, lu),
            *parts,
            scratch=[pltpu.VMEM((s2, COLS), F32)],
        )
    with jax.named_scope("mid_upper"):
        keep, send, x_root = kernel(
            root_to_mid,
            [(s1 // 4, LANES)] * 2 + [(n2 // 2, LANES)],
            m2r_up,
            x_root,
            swap("leaf", x_root, 2),
        )
        pieces = sum_front(keep, send)
        (x_mid,) = kernel(mid_upper, [(n1 // 2, LANES)], mu, y_mid_full, *pieces)
        from_root, root_field, root_adjoint = kernel(
            root_to_leaf,
            [(s0, LANES), (2, COLS, n2), (2, COLS, n2)],
            l2r_up,
            x_root,
            swap("leaf", after(x_root, send), 1),
        )
    with jax.named_scope("leaf_upper"):
        keep, send, x_mid = kernel(
            mid_to_leaf,
            [(s0 // 2, LANES)] * 2 + [(n1, LANES)],
            l2m_up,
            from_root,
            x_mid,
            swap("leaf", x_mid, 1),
        )
        pieces = sum_front(keep, send)
        x_other = swap("leaf", after(x_mid, send), 2)
        mid_field, mid_adjoint = kernel(mid_outputs, [(2, 2, COLS, n1)] * 2, x_mid, x_other)
        leaf_field, leaf_adjoint = kernel(leaf_upper, [(2, COLS, n0)] * 2, lu, y_full, *pieces)
    return tuple(
        jnp.swapaxes(x, -1, -2)
        for x in (leaf_field, mid_field, root_field, leaf_adjoint, mid_adjoint, root_adjoint)
    )


def solution(mesh):
    in_specs = (
        P(None, "leaf", "front", None),
        P(None, "leaf", "front", None),
        P(None, "leaf", "front", None),
        P(None, "leaf", "front", None),
        P(None, "leaf", None, "front"),
        P(None, "leaf", None, "front"),
        P(None, None, "front", None),
        P(None, None, "front", None),
        P(None, None, "front", None),
        P(None, None, None, "front"),
        P(None, "front", None),
        P(None, "front", None),
        P(None, ("leaf", "front"), None),
        P(None, None, "front", None),
        P(None, "front", None),
        P(None, ("leaf", "front"), None),
        P(("leaf", "front"), None),
        P(("leaf", "front")),
    )
    out_specs = (
        P(None, ("leaf", "front"), None),
        P(None, None, "front", None),
        P(None, "front", None),
        P(None, ("leaf", "front"), None),
        P(None, None, "front", None),
        P(None, "front", None),
    )
    return jax.shard_map(body, mesh=mesh, in_specs=in_specs, out_specs=out_specs, check_vma=False)
```

time: 486 us -> 124 us (0.26); the launches traced: 477 us -> 123 us
  blocking collectives: 163 us -> 0 us
  matrix products: 112 us -> 0 us
  waiting for transfers between devices: 144 us -> 46.9 us
  starting transfers between devices: 12.3 us -> 46 us
  Pallas kernels: 0 us -> 18.8 us
  other arithmetic: 14.8 us -> 0 us
  between operations: 15.1 us -> 1.08 us
  local copies, waits for them, and re-layouts: 15.8 us -> 10.4 us
    all_gather x16 -> x0, blocking collectives: 163 us -> none  [panel_apply(): portion = lax.all_gather(shard, 'front', axis=2, tiled=True)]
    dot_general x97 -> x0, matrix products: 112 us -> none  [the longest x24 29.1 us: product(): jnp.matmul(a[0], b[1], precision=lax.Precision.HIGHEST)]
    unnamed x7 -> x0, waiting for transfers between devices: 67.5 us -> none
    ppermute x0 -> x66, waiting for transfers between devices: none -> 46.9 us  [swap(): return lax.ppermute(x, axis, [(i, i ^ k) for i in range(size)])]
    ppermute x0 -> x66, starting transfers between devices: none -> 46 us  [swap(): return lax.ppermute(x, axis, [(i, i ^ k) for i in range(size)])]
    reduce_scatter x2 -> x0, waiting for transfers between devices: 37.3 us -> none  [panel_sum(): lax.psum_scatter(partial_value, 'front', scatter_dimension=2, tiled=True)]
    psum x1 -> x0, waiting for transfers between devices: 33.4 us -> none  [solve_tree(): mid_total, root_total = lax.psum((mid_terms, to_root), 'leaf')]
    pallas_call x0 -> x32, Pallas kernels: none -> 18.8 us  [kernel(): pl.pallas_call(fn, out_shape=[jax.ShapeDtypeStruct(*o) for o in outs], in...]
  transfers between devices with their start and end apart: 7 -> 66, of which waited for: 6 -> 44; matrix products, arithmetic and copies ran while one was open for 8% -> 0% of each run, Pallas kernels for 0% -> 7%
where the time goes in v3:
time: 124 us; the launch traced here: 123 us
  waiting for transfers between devices  46.9 us (38%)
  starting transfers between devices  46 us (37%)
  Pallas kernels  18.8 us (15%)
  local copies, waits for them, and re-layouts  10.4 us (8%)
    ppermute x66, waiting for transfers between devices, swap(): return lax.ppermute(x, axis, [(i, i ^ k) for i in range(size)])  46.9 us
    ppermute x66, starting transfers between devices, swap(): return lax.ppermute(x, axis, [(i, i ^ k) for i in range(size)])  46 us
    pallas_call x32, Pallas kernels, kernel(): pl.pallas_call(fn, out_shape=[jax.ShapeDtypeStruct(*o) for o in outs], in...  18.8 us
    unnamed x36, local copies, waits for them, and re-layouts  10.4 us
  transfers between devices with their start and end apart: 66, of which 44 were waited for; matrix products, arithmetic and copies ran while one was open for 0% of the time, Pallas kernels for 7%

profile of v3, /device:TPU:0, one launch (start us, length us, event | category | flops | bytes accessed | tf_op | source)
XLA Modules:
  0.0 123.2 jit_solution(14273559708217707206)
XLA Ops:
  3.1 3.1 %collective-permute-start = (f32[16,128]{1,0:T(8,128)S(1)}, f32[16,128]{1,0:T(8,128)S(1)}, u32[]{:S(2)}, u32[]{:S(2)}) collective-permute-start(f32[16,128]{1,0:T(8,128)S(1)} %get-tuple-element.76), channel_id=1, source_target_pairs={{0,8},{8,0},{16,24},{24,16},{1,9},{9,1},{17,25},{25,17},{2,10},{10... | collective-permute-start | bytes 24584 | tf_op jit(solution)/shard_map/right_hand_sides/ppermute | solution.py:89
  6.2 2.6 %collective-permute-start.1 = (f32[16,128]{1,0:T(8,128)S(1)}, f32[16,128]{1,0:T(8,128)S(1)}, u32[]{:S(2)}, u32[]{:S(2)}) collective-permute-start(f32[16,128]{1,0:T(8,128)S(1)} %get-tuple-element.77), channel_id=1, source_target_pairs={{0,16},{8,24},{16,0},{24,8},{1,17},{9,25},{17,1},{25,9},{2,18},{10... | collective-permute-start | bytes 24584 | tf_op jit(solution)/shard_map/right_hand_sides/ppermute | solution.py:89
  14.4 2.5 %collective-permute-start.8 = (f32[72,128]{1,0:T(8,128)S(1)}, f32[72,128]{1,0:T(8,128)S(1)}, u32[]{:S(2)}, u32[]{:S(2)}) collective-permute-start(f32[72,128]{1,0:T(8,128)S(1)} %right_hand_sides.7.refs_0_), channel_id=1, source_target_pairs={{0,6},{1,7},{2,4},{3,5},{4,2},{5,3},{6,0},{7,1},{8,14},{9,15},{10,... | collective-permute-start | bytes 110600 | tf_op jit(solution)/shard_map/leaf_lower/ppermute | solution.py:89
  17.9 1.5 %collective-permute-done.8.refs_6_ = f32[72,128]{1,0:T(8,128)S(1)} collective-permute-done((f32[72,128]{1,0:T(8,128)S(1)}, f32[72,128]{1,0:T(8,128)S(1)}, u32[]{:S(2)}, u32[]{:S(2)}) %collective-permute-start.8) | collective-permute-done | bytes 36896 | tf_op jit(solution)/shard_map/leaf_lower/ppermute | solution.py:89
  21.3 2.2 %copy-done = f32[2,2,256,1024]{3,2,1,0:T(8,128)S(1)} copy-done((f32[2,2,256,1024]{3,2,1,0:T(8,128)S(1)}, f32[2,2,256,1024]{3,2,1,0:T(8,128)}, u32[]{:S(2)}) %copy-start) | copy-done | bytes 4194328
  23.5 1.6 %copy-done.4 = f32[2,2,128,1024]{3,2,1,0:T(8,128)S(1)} copy-done((f32[2,2,128,1024]{3,2,1,0:T(8,128)S(1)}, f32[2,2,128,1024]{3,2,1,0:T(8,128)}, u32[]{:S(2)}) %copy-start.4) | copy-done | bytes 2097176
  26.6 1.6 %collective-permute-start.15 = (f32[64,128]{1,0:T(8,128)S(1)}, f32[64,128]{1,0:T(8,128)S(1)}, u32[]{:S(2)}, u32[]{:S(2)}) collective-permute-start(f32[64,128]{1,0:T(8,128)S(1)} %leaf_lower.3.refs_0_), channel_id=1, source_target_pairs={{0,6},{1,7},{2,4},{3,5},{4,2},{5,3},{6,0},{7,1},{8,14},{9,15},{10,... | collective-permute-start | bytes 98312 | tf_op jit(solution)/shard_map/mid_lower/ppermute | solution.py:89
  35.5 2.8 %collective-permute-done.17.refs_1_ = f32[64,128]{1,0:T(8,128)S(1)} collective-permute-done((f32[64,128]{1,0:T(8,128)S(1)}, f32[64,128]{1,0:T(8,128)S(1)}, u32[]{:S(2)}, u32[]{:S(2)}) %collective-permute-start.17) | collective-permute-done | bytes 32800 | tf_op jit(solution)/shard_map/mid_lower/ppermute | solution.py:89
  38.4 2.5 %collective-permute-start.23 = (f32[64,128]{1,0:T(8,128)S(1)}, f32[64,128]{1,0:T(8,128)S(1)}, u32[]{:S(2)}, u32[]{:S(2)}) collective-permute-start(f32[64,128]{1,0:T(8,128)S(1)} %mid_lower.9.refs_0_), channel_id=1, source_target_pairs={{0,6},{1,7},{2,4},{3,5},{4,2},{5,3},{6,0},{7,1},{8,14},{9,15},{10,... | collective-permute-start | bytes 98312 | tf_op jit(solution)/shard_map/mid_lower/ppermute | solution.py:89
  43.2 1.5 %collective-permute-done.21.refs_4_ = f32[64,128]{1,0:T(8,128)S(1)} collective-permute-done((f32[64,128]{1,0:T(8,128)S(1)}, f32[64,128]{1,0:T(8,128)S(1)}, u32[]{:S(2)}, u32[]{:S(2)}) %collective-permute-start.21) | collective-permute-done | bytes 32800 | tf_op jit(solution)/shard_map/mid_lower/ppermute | solution.py:89
  47.5 1.6 %collective-permute-start.31 = (f32[64,128]{1,0:T(8,128)S(1)}, f32[64,128]{1,0:T(8,128)S(1)}, u32[]{:S(2)}, u32[]{:S(2)}) collective-permute-start(f32[64,128]{1,0:T(8,128)S(1)} %mid_lower.11.refs_0_), channel_id=1, source_target_pairs={{0,6},{1,7},{2,4},{3,5},{4,2},{5,3},{6,0},{7,1},{8,14},{9,15},{10,... | collective-permute-start | bytes 98312 | tf_op jit(solution)/shard_map/root_cut/ppermute | solution.py:89
  54.4 1.6 %collective-permute-done.25.came = f32[256,64]{1,0:T(8,128)S(1)} collective-permute-done((f32[256,64]{1,0:T(8,128)S(1)}, f32[256,64]{1,0:T(8,128)S(1)}, u32[]{:S(2)}, u32[]{:S(2)}) %collective-permute-start.25) | collective-permute-done | bytes 65568 | tf_op jit(solution)/shard_map/mid_lower/ppermute | solution.py:89
  57.4 2.1 %collective-permute-start.33 = (f32[64,128]{1,0:T(8,128)S(1)}, f32[64,128]{1,0:T(8,128)S(1)}, u32[]{:S(2)}, u32[]{:S(2)}) collective-permute-start(f32[64,128]{1,0:T(8,128)S(1)} %get-tuple-element.105), channel_id=1, source_target_pairs={{0,16},{8,24},{16,0},{24,8},{1,17},{9,25},{17,1},{25,9},{2,18},{10... | collective-permute-start | bytes 98312 | tf_op jit(solution)/shard_map/root_cut/ppermute | solution.py:89
  60.1 2.2 %collective-permute-done.33.refs_1_ = f32[64,128]{1,0:T(8,128)S(1)} collective-permute-done((f32[64,128]{1,0:T(8,128)S(1)}, f32[64,128]{1,0:T(8,128)S(1)}, u32[]{:S(2)}, u32[]{:S(2)}) %collective-permute-start.33) | collective-permute-done | bytes 32800 | tf_op jit(solution)/shard_map/root_cut/ppermute | solution.py:89
  62.3 1.6 %collective-permute-start.39 = (f32[64,128]{1,0:T(8,128)S(1)}, f32[64,128]{1,0:T(8,128)S(1)}, u32[]{:S(2)}, u32[]{:S(2)}) collective-permute-start(f32[64,128]{1,0:T(8,128)S(1)} %root_cut.7.refs_0_), channel_id=1, source_target_pairs={{0,6},{1,7},{2,4},{3,5},{4,2},{5,3},{6,0},{7,1},{8,14},{9,15},{10,... | collective-permute-start | bytes 98312 | tf_op jit(solution)/shard_map/root_solve/ppermute | solution.py:89
  64.4 1.5 %collective-permute-start.35 = (f32[64,128]{1,0:T(8,128)S(1)}, f32[64,128]{1,0:T(8,128)S(1)}, u32[]{:S(2)}, u32[]{:S(2)}) collective-permute-start(f32[64,128]{1,0:T(8,128)S(1)} %root_cut.7.refs_0_), channel_id=1, source_target_pairs={{0,2},{1,3},{2,0},{3,1},{4,6},{5,7},{6,4},{7,5},{8,10},{9,11},{10,... | collective-permute-start | bytes 98312 | tf_op jit(solution)/shard_map/root_solve/ppermute | solution.py:89
  69.5 1.9 %root_solve.5.refs_0_ = f32[64,128]{1,0:T(8,128)S(1)} custom-call(bf16[512,4096]{1,0:T(8,128)(2,1)S(1)} %mid_lower.10.matrix, f32[64,128]{1,0:T(8,128)S(1)} %root_cut.7.refs_0_, f32[64,128]{1,0:T(8,128)S(1)} %collective-permute-done.34.refs_1_, f32[64,128]{1,0:T(8,128)S(1)} %collective-permute-done.35.refs_2_, ...), custom_call_target="tpu_custom_call" | custom-call | tf_op jit(solution)/shard_map/root_solve/pallas_call | solution.py:101
  71.4 2.5 %collective-permute-start.46 = (f32[64,128]{1,0:T(8,128)S(1)}, f32[64,128]{1,0:T(8,128)S(1)}, u32[]{:S(2)}, u32[]{:S(2)}) collective-permute-start(f32[64,128]{1,0:T(8,128)S(1)} %root_solve.5.refs_0_), channel_id=1, source_target_pairs={{0,6},{1,7},{2,4},{3,5},{4,2},{5,3},{6,0},{7,1},{8,14},{9,15},{10,... | collective-permute-start | bytes 98312 | tf_op jit(solution)/shard_map/root_solve/ppermute | solution.py:89
  76.2 1.5 %collective-permute-done.44.refs_4_ = f32[64,128]{1,0:T(8,128)S(1)} collective-permute-done((f32[64,128]{1,0:T(8,128)S(1)}, f32[64,128]{1,0:T(8,128)S(1)}, u32[]{:S(2)}, u32[]{:S(2)}) %collective-permute-start.44) | collective-permute-done | bytes 32800 | tf_op jit(solution)/shard_map/root_solve/ppermute | solution.py:89
  79.5 1.9 %root_solve.7.mine = f32[64,128]{1,0:T(8,128)S(1)} custom-call(bf16[512,4096]{1,0:T(8,128)(2,1)S(1)} %root_cut.4.matrix, f32[64,128]{1,0:T(8,128)S(1)} %root_solve.5.refs_0_, f32[64,128]{1,0:T(8,128)S(1)} %collective-permute-done.41.refs_1_, f32[64,128]{1,0:T(8,128)S(1)} %collective-permute-done.42.refs_2_, f32[64,128]{1,0:T(8,128)S(1)} %collective-permute-done.43.refs_3_, ...), custom_call_target="tpu_custom_call" | custom-call | tf_op jit(solution)/shard_map/root_solve/pallas_call | solution.py:101
  81.3 2.1 %collective-permute-start.48 = (f32[64,128]{1,0:T(8,128)S(1)}, f32[64,128]{1,0:T(8,128)S(1)}, u32[]{:S(2)}, u32[]{:S(2)}) collective-permute-start(f32[64,128]{1,0:T(8,128)S(1)} %root_solve.7.mine), channel_id=1, source_target_pairs={{0,16},{8,24},{16,0},{24,8},{1,17},{9,25},{17,1},{25,9},{2,18},{10... | collective-permute-start | bytes 98312 | tf_op jit(solution)/shard_map/mid_upper/ppermute | solution.py:89
  83.5 3.4 %collective-permute-done.48.other = f32[64,128]{1,0:T(8,128)S(1)} collective-permute-done((f32[64,128]{1,0:T(8,128)S(1)}, f32[64,128]{1,0:T(8,128)S(1)}, u32[]{:S(2)}, u32[]{:S(2)}) %collective-permute-start.48) | collective-permute-done | bytes 32800 | tf_op jit(solution)/shard_map/mid_upper/ppermute | solution.py:89
  90.0 1.5 %collective-permute-start.52 = (f32[128,128]{1,0:T(8,128)S(1)}, f32[128,128]{1,0:T(8,128)S(1)}, u32[]{:S(2)}, u32[]{:S(2)}) collective-permute-start(f32[128,128]{1,0:T(8,128)S(1)} %get-tuple-element.123.c), channel_id=1, source_target_pairs={{0,4},{1,5},{2,6},{3,7},{4,0},{5,1},{6,2},{7,3},{8,12},{9,13},{10,... | collective-permute-start | bytes 196616 | tf_op jit(solution)/shard_map/mid_upper/ppermute | solution.py:89
  91.6 2.2 %collective-permute-done.51.b = f32[128,128]{1,0:T(8,128)S(1)} collective-permute-done((f32[128,128]{1,0:T(8,128)S(1)}, f32[128,128]{1,0:T(8,128)S(1)}, u32[]{:S(2)}, u32[]{:S(2)}) %collective-permute-start.51) | collective-permute-done | bytes 65568 | tf_op jit(solution)/shard_map/mid_upper/ppermute | solution.py:89
  94.3 1.6 %collective-permute-start.53 = (f32[128,128]{1,0:T(8,128)S(1)}, f32[128,128]{1,0:T(8,128)S(1)}, u32[]{:S(2)}, u32[]{:S(2)}) collective-permute-start(f32[128,128]{1,0:T(8,128)S(1)} %get-tuple-element.124.a), channel_id=1, source_target_pairs={{0,4},{1,5},{2,6},{3,7},{4,0},{5,1},{6,2},{7,3},{8,12},{9,13},{10,... | collective-permute-start | bytes 196616 | tf_op jit(solution)/shard_map/mid_upper/ppermute | solution.py:89
  95.9 1.5 %collective-permute-start.54 = (f32[128,128]{1,0:T(8,128)S(1)}, f32[128,128]{1,0:T(8,128)S(1)}, u32[]{:S(2)}, u32[]{:S(2)}) collective-permute-start(f32[128,128]{1,0:T(8,128)S(1)} %get-tuple-element.125.c), channel_id=1, source_target_pairs={{0,2},{1,3},{2,0},{3,1},{4,6},{5,7},{6,4},{7,5},{8,10},{9,11},{10,... | collective-permute-start | bytes 196616 | tf_op jit(solution)/shard_map/mid_upper/ppermute | solution.py:89
  98.7 1.5 %collective-permute-done.54.d = f32[128,128]{1,0:T(8,128)S(1)} collective-permute-done((f32[128,128]{1,0:T(8,128)S(1)}, f32[128,128]{1,0:T(8,128)S(1)}, u32[]{:S(2)}, u32[]{:S(2)}) %collective-permute-start.54) | collective-permute-done | bytes 65568 | tf_op jit(solution)/shard_map/mid_upper/ppermute | solution.py:89
  108.6 1.6 %collective-permute-start.59 = (f32[128,128]{1,0:T(8,128)S(1)}, f32[128,128]{1,0:T(8,128)S(1)}, u32[]{:S(2)}, u32[]{:S(2)}) collective-permute-start(f32[128,128]{1,0:T(8,128)S(1)} %get-tuple-element.130.a), channel_id=1, source_target_pairs={{0,2},{1,3},{2,0},{3,1},{4,6},{5,7},{6,4},{7,5},{8,10},{9,11},{10,... | collective-permute-start | bytes 196616 | tf_op jit(solution)/shard_map/leaf_upper/ppermute | solution.py:89
  110.7 2.2 %collective-permute-done.59.b = f32[128,128]{1,0:T(8,128)S(1)} collective-permute-done((f32[128,128]{1,0:T(8,128)S(1)}, f32[128,128]{1,0:T(8,128)S(1)}, u32[]{:S(2)}, u32[]{:S(2)}) %collective-permute-start.59) | collective-permute-done | bytes 65568 | tf_op jit(solution)/shard_map/leaf_upper/ppermute | solution.py:89
  112.9 1.5 %collective-permute-done.60.d = f32[128,128]{1,0:T(8,128)S(1)} collective-permute-done((f32[128,128]{1,0:T(8,128)S(1)}, f32[128,128]{1,0:T(8,128)S(1)}, u32[]{:S(2)}, u32[]{:S(2)}) %collective-permute-start.60) | collective-permute-done | bytes 65568 | tf_op jit(solution)/shard_map/leaf_upper/ppermute | solution.py:89
  115.5 2.4 %collective-permute-start.65 = (f32[128,128]{1,0:T(8,128)S(1)}, f32[128,128]{1,0:T(8,128)S(1)}, u32[]{:S(2)}, u32[]{:S(2)}) collective-permute-start(f32[128,128]{1,0:T(8,128)S(1)} %get-tuple-element.138.mine), channel_id=1, source_target_pairs={{0,16},{8,24},{16,0},{24,8},{1,17},{9,25},{17,1},{25,9},{2,18},{10... | collective-permute-start | bytes 196616 | tf_op jit(solution)/shard_map/leaf_upper/ppermute | solution.py:89
  119.9 1.5 %collective-permute-done.65.other = f32[128,128]{1,0:T(8,128)S(1)} collective-permute-done((f32[128,128]{1,0:T(8,128)S(1)}, f32[128,128]{1,0:T(8,128)S(1)}, u32[]{:S(2)}, u32[]{:S(2)}) %collective-permute-start.65) | collective-permute-done | bytes 65568 | tf_op jit(solution)/shard_map/leaf_upper/ppermute | solution.py:89
  (168 shorter events, 58.8 us)
Async XLA Ops:
  3.1 10.7 %collective-permute-start = (f32[16,128]{1,0:T(8,128)S(1)}, f32[16,128]{1,0:T(8,128)S(1)}, u32[]{:S(2)}, u32[]{:S(2)}) collective-permute-start(f32[16,128]{1,0:T(8,128)S(1)} %get-tuple-element.76), channel_id=1, source_target_pairs={{0,8},{8,0},{16,24},{24,16},{1,9},{9,1},{17,25},{25,17},{2,10},{10... | collective-permute-start | bytes 24584 | tf_op jit(solution)/shard_map/right_hand_sides/ppermute | solution.py:89
  6.2 7.6 %collective-permute-start.1 = (f32[16,128]{1,0:T(8,128)S(1)}, f32[16,128]{1,0:T(8,128)S(1)}, u32[]{:S(2)}, u32[]{:S(2)}) collective-permute-start(f32[16,128]{1,0:T(8,128)S(1)} %get-tuple-element.77), channel_id=1, source_target_pairs={{0,16},{8,24},{16,0},{24,8},{1,17},{9,25},{17,1},{25,9},{2,18},{10... | collective-permute-start | bytes 24584 | tf_op jit(solution)/shard_map/right_hand_sides/ppermute | solution.py:89
  8.8 5.4 %collective-permute-start.2 = (f32[16,128]{1,0:T(8,128)S(1)}, f32[16,128]{1,0:T(8,128)S(1)}, u32[]{:S(2)}, u32[]{:S(2)}) collective-permute-start(f32[16,128]{1,0:T(8,128)S(1)} %get-tuple-element.78), channel_id=1, source_target_pairs={{0,24},{8,16},{16,8},{24,0},{1,25},{9,17},{17,9},{25,1},{2,26},{10... | collective-permute-start | bytes 24584 | tf_op jit(solution)/shard_map/right_hand_sides/ppermute | solution.py:89
  14.4 5.1 %collective-permute-start.8 = (f32[72,128]{1,0:T(8,128)S(1)}, f32[72,128]{1,0:T(8,128)S(1)}, u32[]{:S(2)}, u32[]{:S(2)}) collective-permute-start(f32[72,128]{1,0:T(8,128)S(1)} %right_hand_sides.7.refs_0_), channel_id=1, source_target_pairs={{0,6},{1,7},{2,4},{3,5},{4,2},{5,3},{6,0},{7,1},{8,14},{9,15},{10,... | collective-permute-start | bytes 110600 | tf_op jit(solution)/shard_map/leaf_lower/ppermute | solution.py:89
  16.9 4.0 %collective-permute-start.6 = (f32[72,128]{1,0:T(8,128)S(1)}, f32[72,128]{1,0:T(8,128)S(1)}, u32[]{:S(2)}, u32[]{:S(2)}) collective-permute-start(f32[72,128]{1,0:T(8,128)S(1)} %right_hand_sides.7.refs_0_), channel_id=1, source_target_pairs={{0,4},{1,5},{2,6},{3,7},{4,0},{5,1},{6,2},{7,3},{8,12},{9,13},{10,... | collective-permute-start | bytes 110600 | tf_op jit(solution)/shard_map/leaf_lower/ppermute | solution.py:89
  17.4 4.0 %collective-permute-start.4 = (f32[72,128]{1,0:T(8,128)S(1)}, f32[72,128]{1,0:T(8,128)S(1)}, u32[]{:S(2)}, u32[]{:S(2)}) collective-permute-start(f32[72,128]{1,0:T(8,128)S(1)} %right_hand_sides.7.refs_0_), channel_id=1, source_target_pairs={{0,2},{1,3},{2,0},{3,1},{4,6},{5,7},{6,4},{7,5},{8,10},{9,11},{10,... | collective-permute-start | bytes 110600 | tf_op jit(solution)/shard_map/leaf_lower/ppermute | solution.py:89
  17.9 8.0 %collective-permute-start.3 = (f32[72,128]{1,0:T(8,128)S(1)}, f32[72,128]{1,0:T(8,128)S(1)}, u32[]{:S(2)}, u32[]{:S(2)}) collective-permute-start(f32[72,128]{1,0:T(8,128)S(1)} %right_hand_sides.7.refs_0_), channel_id=1, source_target_pairs={{0,1},{1,0},{2,3},{3,2},{4,5},{5,4},{6,7},{7,6},{8,9},{9,8},{10,11... | collective-permute-start | bytes 110600 | tf_op jit(solution)/shard_map/leaf_lower/ppermute | solution.py:89
  19.4 6.5 %collective-permute-start.9 = (f32[72,128]{1,0:T(8,128)S(1)}, f32[72,128]{1,0:T(8,128)S(1)}, u32[]{:S(2)}, u32[]{:S(2)}) collective-permute-start(f32[72,128]{1,0:T(8,128)S(1)} %collective-permute-done.8.refs_6_), channel_id=1, source_target_pairs={{0,1},{1,0},{2,3},{3,2},{4,5},{5,4},{6,7},{7,6},{8,9},{9,8},{10,11... | collective-permute-start | bytes 110600 | tf_op jit(solution)/shard_map/leaf_lower/ppermute | solution.py:89
  20.8 5.1 %collective-permute-start.7 = (f32[72,128]{1,0:T(8,128)S(1)}, f32[72,128]{1,0:T(8,128)S(1)}, u32[]{:S(2)}, u32[]{:S(2)}) collective-permute-start(f32[72,128]{1,0:T(8,128)S(1)} %collective-permute-done.6.refs_4_), channel_id=1, source_target_pairs={{0,1},{1,0},{2,3},{3,2},{4,5},{5,4},{6,7},{7,6},{8,9},{9,8},{10,11... | collective-permute-start | bytes 110600 | tf_op jit(solution)/shard_map/leaf_lower/ppermute | solution.py:89
  21.3 4.6 %collective-permute-start.5 = (f32[72,128]{1,0:T(8,128)S(1)}, f32[72,128]{1,0:T(8,128)S(1)}, u32[]{:S(2)}, u32[]{:S(2)}) collective-permute-start(f32[72,128]{1,0:T(8,128)S(1)} %collective-permute-done.4.refs_2_), channel_id=1, source_target_pairs={{0,1},{1,0},{2,3},{3,2},{4,5},{5,4},{6,7},{7,6},{8,9},{9,8},{10,11... | collective-permute-start | bytes 110600 | tf_op jit(solution)/shard_map/leaf_lower/ppermute | solution.py:89
  26.6 4.9 %collective-permute-start.15 = (f32[64,128]{1,0:T(8,128)S(1)}, f32[64,128]{1,0:T(8,128)S(1)}, u32[]{:S(2)}, u32[]{:S(2)}) collective-permute-start(f32[64,128]{1,0:T(8,128)S(1)} %leaf_lower.3.refs_0_), channel_id=1, source_target_pairs={{0,6},{1,7},{2,4},{3,5},{4,2},{5,3},{6,0},{7,1},{8,14},{9,15},{10,... | collective-permute-start | bytes 98312 | tf_op jit(solution)/shard_map/mid_lower/ppermute | solution.py:89
  34.4 4.0 %collective-permute-start.17 = (f32[64,128]{1,0:T(8,128)S(1)}, f32[64,128]{1,0:T(8,128)S(1)}, u32[]{:S(2)}, u32[]{:S(2)}) collective-permute-start(f32[64,128]{1,0:T(8,128)S(1)} %get-tuple-element.93), channel_id=1, source_target_pairs={{0,8},{8,0},{16,24},{24,16},{1,9},{9,1},{17,25},{25,17},{2,10},{10... | collective-permute-start | bytes 98312 | tf_op jit(solution)/shard_map/mid_lower/ppermute | solution.py:89
  38.4 4.9 %collective-permute-start.23 = (f32[64,128]{1,0:T(8,128)S(1)}, f32[64,128]{1,0:T(8,128)S(1)}, u32[]{:S(2)}, u32[]{:S(2)}) collective-permute-start(f32[64,128]{1,0:T(8,128)S(1)} %mid_lower.9.refs_0_), channel_id=1, source_target_pairs={{0,6},{1,7},{2,4},{3,5},{4,2},{5,3},{6,0},{7,1},{8,14},{9,15},{10,... | collective-permute-start | bytes 98312 | tf_op jit(solution)/shard_map/mid_lower/ppermute | solution.py:89
  41.9 4.3 %collective-permute-start.18 = (f32[64,128]{1,0:T(8,128)S(1)}, f32[64,128]{1,0:T(8,128)S(1)}, u32[]{:S(2)}, u32[]{:S(2)}) collective-permute-start(f32[64,128]{1,0:T(8,128)S(1)} %mid_lower.9.refs_0_), channel_id=1, source_target_pairs={{0,1},{1,0},{2,3},{3,2},{4,5},{5,4},{6,7},{7,6},{8,9},{9,8},{10,11... | collective-permute-start | bytes 98312 | tf_op jit(solution)/shard_map/mid_lower/ppermute | solution.py:89
  47.5 4.9 %collective-permute-start.31 = (f32[64,128]{1,0:T(8,128)S(1)}, f32[64,128]{1,0:T(8,128)S(1)}, u32[]{:S(2)}, u32[]{:S(2)}) collective-permute-start(f32[64,128]{1,0:T(8,128)S(1)} %mid_lower.11.refs_0_), channel_id=1, source_target_pairs={{0,6},{1,7},{2,4},{3,5},{4,2},{5,3},{6,0},{7,1},{8,14},{9,15},{10,... | collective-permute-start | bytes 98312 | tf_op jit(solution)/shard_map/root_cut/ppermute | solution.py:89
  51.1 5.0 %collective-permute-start.25 = (f32[256,64]{1,0:T(8,128)S(1)}, f32[256,64]{1,0:T(8,128)S(1)}, u32[]{:S(2)}, u32[]{:S(2)}) collective-permute-start(f32[256,64]{1,0:T(8,128)S(1)} %get-tuple-element.102), channel_id=1, source_target_pairs={{0,8},{8,0},{16,24},{24,16},{1,9},{9,1},{17,25},{25,17},{2,10},{10... | collective-permute-start | bytes 196616 | tf_op jit(solution)/shard_map/mid_lower/ppermute | solution.py:89
  51.6 4.5 %collective-permute-start.26 = (f32[64,128]{1,0:T(8,128)S(1)}, f32[64,128]{1,0:T(8,128)S(1)}, u32[]{:S(2)}, u32[]{:S(2)}) collective-permute-start(f32[64,128]{1,0:T(8,128)S(1)} %mid_lower.11.refs_0_), channel_id=1, source_target_pairs={{0,1},{1,0},{2,3},{3,2},{4,5},{5,4},{6,7},{7,6},{8,9},{9,8},{10,11... | collective-permute-start | bytes 98312 | tf_op jit(solution)/shard_map/root_cut/ppermute | solution.py:89
  57.4 4.9 %collective-permute-start.33 = (f32[64,128]{1,0:T(8,128)S(1)}, f32[64,128]{1,0:T(8,128)S(1)}, u32[]{:S(2)}, u32[]{:S(2)}) collective-permute-start(f32[64,128]{1,0:T(8,128)S(1)} %get-tuple-element.105), channel_id=1, source_target_pairs={{0,16},{8,24},{16,0},{24,8},{1,17},{9,25},{17,1},{25,9},{2,18},{10... | collective-permute-start | bytes 98312 | tf_op jit(solution)/shard_map/root_cut/ppermute | solution.py:89
  62.3 4.9 %collective-permute-start.39 = (f32[64,128]{1,0:T(8,128)S(1)}, f32[64,128]{1,0:T(8,128)S(1)}, u32[]{:S(2)}, u32[]{:S(2)}) collective-permute-start(f32[64,128]{1,0:T(8,128)S(1)} %root_cut.7.refs_0_), channel_id=1, source_target_pairs={{0,6},{1,7},{2,4},{3,5},{4,2},{5,3},{6,0},{7,1},{8,14},{9,15},{10,... | collective-permute-start | bytes 98312 | tf_op jit(solution)/shard_map/root_solve/ppermute | solution.py:89
  71.4 4.9 %collective-permute-start.46 = (f32[64,128]{1,0:T(8,128)S(1)}, f32[64,128]{1,0:T(8,128)S(1)}, u32[]{:S(2)}, u32[]{:S(2)}) collective-permute-start(f32[64,128]{1,0:T(8,128)S(1)} %root_solve.5.refs_0_), channel_id=1, source_target_pairs={{0,6},{1,7},{2,4},{3,5},{4,2},{5,3},{6,0},{7,1},{8,14},{9,15},{10,... | collective-permute-start | bytes 98312 | tf_op jit(solution)/shard_map/root_solve/ppermute | solution.py:89
  81.3 5.5 %collective-permute-start.48 = (f32[64,128]{1,0:T(8,128)S(1)}, f32[64,128]{1,0:T(8,128)S(1)}, u32[]{:S(2)}, u32[]{:S(2)}) collective-permute-start(f32[64,128]{1,0:T(8,128)S(1)} %root_solve.7.mine), channel_id=1, source_target_pairs={{0,16},{8,24},{16,0},{24,8},{1,17},{9,25},{17,1},{25,9},{2,18},{10... | collective-permute-start | bytes 98312 | tf_op jit(solution)/shard_map/mid_upper/ppermute | solution.py:89
  89.4 4.3 %collective-permute-start.51 = (f32[128,128]{1,0:T(8,128)S(1)}, f32[128,128]{1,0:T(8,128)S(1)}, u32[]{:S(2)}, u32[]{:S(2)}) collective-permute-start(f32[128,128]{1,0:T(8,128)S(1)} %get-tuple-element.122.a), channel_id=1, source_target_pairs={{0,2},{1,3},{2,0},{3,1},{4,6},{5,7},{6,4},{7,5},{8,10},{9,11},{10,... | collective-permute-start | bytes 196616 | tf_op jit(solution)/shard_map/mid_upper/ppermute | solution.py:89
  90.0 4.3 %collective-permute-start.52 = (f32[128,128]{1,0:T(8,128)S(1)}, f32[128,128]{1,0:T(8,128)S(1)}, u32[]{:S(2)}, u32[]{:S(2)}) collective-permute-start(f32[128,128]{1,0:T(8,128)S(1)} %get-tuple-element.123.c), channel_id=1, source_target_pairs={{0,4},{1,5},{2,6},{3,7},{4,0},{5,1},{6,2},{7,3},{8,12},{9,13},{10,... | collective-permute-start | bytes 196616 | tf_op jit(solution)/shard_map/mid_upper/ppermute | solution.py:89
  94.3 4.3 %collective-permute-start.53 = (f32[128,128]{1,0:T(8,128)S(1)}, f32[128,128]{1,0:T(8,128)S(1)}, u32[]{:S(2)}, u32[]{:S(2)}) collective-permute-start(f32[128,128]{1,0:T(8,128)S(1)} %get-tuple-element.124.a), channel_id=1, source_target_pairs={{0,4},{1,5},{2,6},{3,7},{4,0},{5,1},{6,2},{7,3},{8,12},{9,13},{10,... | collective-permute-start | bytes 196616 | tf_op jit(solution)/shard_map/mid_upper/ppermute | solution.py:89
  95.9 4.3 %collective-permute-start.54 = (f32[128,128]{1,0:T(8,128)S(1)}, f32[128,128]{1,0:T(8,128)S(1)}, u32[]{:S(2)}, u32[]{:S(2)}) collective-permute-start(f32[128,128]{1,0:T(8,128)S(1)} %get-tuple-element.125.c), channel_id=1, source_target_pairs={{0,2},{1,3},{2,0},{3,1},{4,6},{5,7},{6,4},{7,5},{8,10},{9,11},{10,... | collective-permute-start | bytes 196616 | tf_op jit(solution)/shard_map/mid_upper/ppermute | solution.py:89
  100.8 4.3 %collective-permute-start.49 = (f32[128,128]{1,0:T(8,128)S(1)}, f32[128,128]{1,0:T(8,128)S(1)}, u32[]{:S(2)}, u32[]{:S(2)}) collective-permute-start(f32[128,128]{1,0:T(8,128)S(1)} %get-tuple-element.118.mine), channel_id=1, source_target_pairs={{0,8},{8,0},{16,24},{24,16},{1,9},{9,1},{17,25},{25,17},{2,10},{10... | collective-permute-start | bytes 196616 | tf_op jit(solution)/shard_map/mid_upper/ppermute | solution.py:89
  102.7 4.0 %collective-permute-start.57 = (f32[64,128]{1,0:T(8,128)S(1)}, f32[64,128]{1,0:T(8,128)S(1)}, u32[]{:S(2)}, u32[]{:S(2)}) collective-permute-start(f32[64,128]{1,0:T(8,128)S(1)} %mid_upper.11.mine), channel_id=1, source_target_pairs={{0,8},{8,0},{16,24},{24,16},{1,9},{9,1},{17,25},{25,17},{2,10},{10... | collective-permute-start | bytes 98312 | tf_op jit(solution)/shard_map/leaf_upper/ppermute | solution.py:89
  108.6 4.3 %collective-permute-start.59 = (f32[128,128]{1,0:T(8,128)S(1)}, f32[128,128]{1,0:T(8,128)S(1)}, u32[]{:S(2)}, u32[]{:S(2)}) collective-permute-start(f32[128,128]{1,0:T(8,128)S(1)} %get-tuple-element.130.a), channel_id=1, source_target_pairs={{0,2},{1,3},{2,0},{3,1},{4,6},{5,7},{6,4},{7,5},{8,10},{9,11},{10,... | collective-permute-start | bytes 196616 | tf_op jit(solution)/shard_map/leaf_upper/ppermute | solution.py:89
  110.2 4.3 %collective-permute-start.60 = (f32[128,128]{1,0:T(8,128)S(1)}, f32[128,128]{1,0:T(8,128)S(1)}, u32[]{:S(2)}, u32[]{:S(2)}) collective-permute-start(f32[128,128]{1,0:T(8,128)S(1)} %get-tuple-element.131.c), channel_id=1, source_target_pairs={{0,4},{1,5},{2,6},{3,7},{4,0},{5,1},{6,2},{7,3},{8,12},{9,13},{10,... | collective-permute-start | bytes 196616 | tf_op jit(solution)/shard_map/leaf_upper/ppermute | solution.py:89
  114.5 4.3 %collective-permute-start.61 = (f32[128,128]{1,0:T(8,128)S(1)}, f32[128,128]{1,0:T(8,128)S(1)}, u32[]{:S(2)}, u32[]{:S(2)}) collective-permute-start(f32[128,128]{1,0:T(8,128)S(1)} %get-tuple-element.132.a), channel_id=1, source_target_pairs={{0,4},{1,5},{2,6},{3,7},{4,0},{5,1},{6,2},{7,3},{8,12},{9,13},{10,... | collective-permute-start | bytes 196616 | tf_op jit(solution)/shard_map/leaf_upper/ppermute | solution.py:89
  115.0 4.3 %collective-permute-start.62 = (f32[128,128]{1,0:T(8,128)S(1)}, f32[128,128]{1,0:T(8,128)S(1)}, u32[]{:S(2)}, u32[]{:S(2)}) collective-permute-start(f32[128,128]{1,0:T(8,128)S(1)} %get-tuple-element.133.c), channel_id=1, source_target_pairs={{0,2},{1,3},{2,0},{3,1},{4,6},{5,7},{6,4},{7,5},{8,10},{9,11},{10,... | collective-permute-start | bytes 196616 | tf_op jit(solution)/shard_map/leaf_upper/ppermute | solution.py:89
  115.5 5.9 %collective-permute-start.65 = (f32[128,128]{1,0:T(8,128)S(1)}, f32[128,128]{1,0:T(8,128)S(1)}, u32[]{:S(2)}, u32[]{:S(2)}) collective-permute-start(f32[128,128]{1,0:T(8,128)S(1)} %get-tuple-element.138.mine), channel_id=1, source_target_pairs={{0,16},{8,24},{16,0},{24,8},{1,17},{9,25},{17,1},{25,9},{2,18},{10... | collective-permute-start | bytes 196616 | tf_op jit(solution)/shard_map/leaf_upper/ppermute | solution.py:89
  (52 other events, 227.9 us)

commit v4 on v3

--- a/solution.py
+++ b/solution.py
@@ -45,27 +45,29 @@
     return jnp.concatenate([x[:, at : at + width] for at in range(0, LANES, width)], axis=0)
 
 
-def halves(x):
-    c = COLS
-    return (
-        jnp.concatenate([x[:, :c], x[:, 2 * c : 3 * c]], axis=1),
-        jnp.concatenate([x[:, c : 2 * c], x[:, 3 * c :]], axis=1),
-    )
-
-
-def joined(forward, adjoint):
-    c = COLS
-    return jnp.concatenate([forward[:, :c], adjoint[:, :c], forward[:, c:], adjoint[:, c:]], axis=1)
-
-
-def own_first(group, forward, adjoint):
-    even = (group & 1) == 0
-    return jnp.where(even, forward, adjoint), jnp.where(even, adjoint, forward)
-
-
-def by_solve(group, own, other):
-    even = (group & 1) == 0
-    return joined(jnp.where(even, own, other), jnp.where(even, other, own))
+def quarter_of(x, q):
+    w = COLS // 2
+    return pack(jnp.concatenate([x[:, w * q : w * q + w], x[:, 64 + w * q : 64 + w * q + w]], axis=1))
+
+
+def all_quarters(quarters):
+    w = COLS // 2
+    return jnp.concatenate([x[:, :w] for x in quarters] + [x[:, w:] for x in quarters], axis=1)
+
+
+def send_quarters(x, held, outs):
+    here = lax.axis_index("leaf")
+    for q in range(len(outs)):
+        held[q] = quarter_of(x, q)
+    for k, out in enumerate(outs):
+        out[...] = held[here ^ k]
+
+
+def take_quarters(parts, held):
+    here = lax.axis_index("leaf")
+    for k, part in enumerate(parts):
+        held[here ^ k] = part[...]
+    return all_quarters([unpack(held[q], COLS) for q in range(len(parts))])
 
 
 def assemble(where, parts, here, width=LANES):
@@ -89,11 +91,23 @@
     return lax.ppermute(x, axis, [(i, i ^ k) for i in range(size)])
 
 
-def gather_front(x):
+def gather_front(x, meanwhile=None):
     fronts = lax.axis_size("front")
-    mine = [x] + [swap("front", x, k) for k in range(2, fronts, 2)]
-    other = [swap("front", y, 1) for y in mine]
-    return [block for pair in zip(mine, other) for block in pair]
+    mine = {0: x}
+    for k in range(fronts - 2, 0, -2):
+        mine[k] = swap("front", x, k)
+    extra = tuple(meanwhile(x)) if meanwhile else ()
+    other = {}
+    for k in range(fronts - 2, -1, -2):
+        other[k] = swap("front", after(mine[k], *extra) if k and extra else mine[k], 1)
+    return [held[k] for k in range(0, fronts, 2) for held in (mine, other)], extra
+
+
+def planes(x):
+    groups = lax.axis_size("leaf")
+    blocks = x if isinstance(x, (list, tuple)) else [x] * groups
+    came = {k: swap("leaf", blocks[k], k) for k in range(groups - 1, 0, -1)}
+    return [blocks[0]] + [came[k] for k in range(1, groups)]
 
 
 def kernel(fn, outs, *args, scratch=(), vmem=8, work=0, hbm=()):
@@ -106,7 +120,7 @@
         scratch_shapes=list(scratch),
         compiler_params=pltpu.CompilerParams(vmem_limit_bytes=vmem * 2**20),
         cost_estimate=pl.CostEstimate(flops=work, bytes_accessed=work // 700, transcendentals=0),
-    )(*args)
+    )(*(pltpu.with_memory_space_constraint(a, pltpu.HBM) if i in hbm else a for i, a in enumerate(args)))
 
 
 def load_matrices(picks, *refs):
@@ -117,14 +131,13 @@
         refs[2 * count : 3 * count],
         refs[3 * count],
     )
-    parent = lax.axis_index("leaf") // 2
     copies = []
     for i, (src, pick) in enumerate(zip(sources, picks)):
         rows = buffers[i].shape[1]
         step = rows // 2 if rows >= 128 else rows
         for n, at in enumerate(range(0, rows, step)):
             span = pl.ds(at, step)
-            view = src.at[:, span, :] if pick is None else src.at[:, parent if pick == "own" else 0, span, :]
+            view = src.at[:, span, :] if pick is None else src.at[:, pick, span, :]
             copy = pltpu.make_async_copy(view, buffers[i].at[:, span, :], sems.at[2 * i + n])
             copy.start()
             copies.append((i, at, step, copy))
@@ -191,23 +204,25 @@
     group = lax.axis_index("leaf")
     copies = [
         pltpu.make_async_copy(src, dst, sems.at[i])
-        for i, (src, dst) in enumerate(
-            ((leaf_hbm, leaf), (mid_hbm.at[:, group // 2], mid), (root_hbm, root))
-        )
+        for i, (src, dst) in enumerate(((leaf_hbm, leaf), (mid_hbm, mid), (root_hbm, root)))
     ]
     for copy in copies:
         copy.start()
     for copy in copies:
         copy.wait()
-    forward = ((group & 1) == 0).astype(F32)
+    forward = (group < 2).astype(F32)
     real, imag = leaf[0].T, leaf[1].T
     zero = jnp.zeros_like(real)
     leaf_out[...] = jnp.concatenate([real, zero, imag, zero], axis=1)
-    mid_out[...] = pack(jnp.concatenate([mid[0], mid[1]], axis=0).T) * forward
     width = COLS // 2
-    low = jnp.concatenate([root[0, :width], root[1, :width]], axis=0)
-    high = jnp.concatenate([root[0, width:], root[1, width:]], axis=0)
-    root_out[...] = pack(jnp.where(group < 2, low, high).T) * forward
+
+    def quarter(real, imag):
+        low = jnp.concatenate([real[:width], imag[:width]], axis=0)
+        high = jnp.concatenate([real[width:], imag[width:]], axis=0)
+        return pack(jnp.where(group == 0, low, high).T) * forward
+
+    mid_out[...] = jnp.concatenate([quarter(mid[0, p], mid[1, p]) for p in range(2)], axis=0)
+    root_out[...] = quarter(root[0], root[1])
 
 
 def message_rows(rows, slots):
@@ -271,41 +286,47 @@
     out[...] = complex_dot(matrix[...], rhs[...])
 
 
-def leaf_to_mid(matrix, sources, *refs):
-    parts, (keep, send, full) = refs[:-3], refs[-3:]
+def leaf_to_mid(matrix, *refs):
+    parts, outs, (full, held) = refs[:-6], refs[-6:-2], refs[-2:]
     assemble(full, parts, lax.axis_index("front"))
-    mine, theirs = own_first(lax.axis_index("leaf"), *halves(complex_dot(matrix[...], full[...])))
-    keep[...] = sources[...] - pack(mine)
-    send[...] = -pack(theirs)
-
-
-def leaf_to_root(matrix, full, keep, send):
-    keep[...], send[...] = own_first(lax.axis_index("leaf"), *halves(complex_dot(matrix[...], full[...])))
-
-
-def add(*refs):
-    total = refs[0][...]
-    for ref in refs[1:-1]:
-        total = total + ref[...]
-    refs[-1][...] = total
-
-
-def mid_lower(matrix, *refs):
+    send_quarters(complex_dot(matrix[...], full[...]), held, outs)
+
+
+def leaf_to_root(matrix, full, *refs):
+    send_quarters(complex_dot(matrix[...], full[...]), refs[-1], refs[:-1])
+
+
+def cut_mids(sources, own, sibling, far, other, out):
+    parent = lax.axis_index("leaf") // 2
+    rows = own.shape[0]
+    for at, value in ((parent, own[...] + sibling[...]), (1 - parent, far[...] + other[...])):
+        span = pl.ds(pl.multiple_of(at * rows, 8), rows)
+        out[span, :] = sources[span, :] - value
+
+
+def assemble_mids(where, parts):
+    here = lax.axis_index("front")
+    for k, part in enumerate(parts):
+        half = part.shape[0] // 2
+        rows = half * (LANES // COLS)
+        start = pl.multiple_of((here ^ k) * rows, 8)
+        for p in range(2):
+            where[p, pl.ds(start, rows), :] = unpack(part[half * p : half * p + half, :], COLS)
+
+
+def mid_lower(first, second, *refs):
     parts, (out, whole) = refs[:-2], refs[-2:]
-    assemble(whole, parts, lax.axis_index("front"), 2 * COLS)
-    out[...] = pack(complex_dot(matrix[...], whole[...]))
-
-
-def mid_to_root(matrix, kept, came, sources, *refs):
-    parts, (keep, send, full) = refs[:-3], refs[-3:]
-    assemble(full, parts, lax.axis_index("front"), 2 * COLS)
-    cut = -(kept[...] + came[...] + complex_dot(matrix[...], full[...]))
-    width = COLS // 2
-    low = pack(jnp.concatenate([cut[:, :width], cut[:, COLS : COLS + width]], axis=1))
-    high = pack(jnp.concatenate([cut[:, width:COLS], cut[:, COLS + width :]], axis=1))
-    first = lax.axis_index("leaf") < 2
-    keep[...] = jnp.where(first, low, high) + sources[...]
-    send[...] = jnp.where(first, high, low)
+    assemble_mids(whole, parts)
+    out[...] = jnp.concatenate(
+        [pack(complex_dot(matrix[...], whole[p])) for p, matrix in enumerate((first, second))], axis=0
+    )
+
+
+def mid_to_root(first, second, sources, a, b, c, d, *refs):
+    parts, (out, whole) = refs[:-2], refs[-2:]
+    assemble_mids(whole, parts)
+    known = sources[...] - ((a[...] + b[...]) + (c[...] + d[...]))
+    out[...] = known - pack(complex_dot(first[...], whole[0]) + complex_dot(second[...], whole[1]))
 
 
 def root_rows(matrix, *refs):
@@ -322,20 +343,40 @@
     send[...] = jnp.where(odd, low, high)
 
 
-def root_to_mid(matrix, mine, other, keep, send, x_root):
-    first = lax.axis_index("leaf") < 2
-    mine, other = unpack(mine[...], COLS), unpack(other[...], COLS)
-    low, high = jnp.where(first, mine, other), jnp.where(first, other, mine)
-    width = COLS // 2
-    x = jnp.concatenate([low[:, :width], high[:, :width], low[:, width:], high[:, width:]], axis=1)
-    x_root[...] = pack(x)
-    halved(pack(complex_dot(matrix[...], x)), keep, send)
-
-
-def root_to_leaf(matrix, mine, other, out, forward, adjoint):
-    x = by_solve(lax.axis_index("leaf"), unpack(mine[...], 2 * COLS), unpack(other[...], 2 * COLS))
+def root_to_mid(first, second, quarter, y, keep, send, terms):
+    x = unpack(quarter[...], COLS)
+    rows = keep.shape[0]
+    half = y.shape[0] // 2
+    height = half * (LANES // COLS)
+    start = pl.multiple_of(lax.axis_index("front") * height, 8)
+    for p, matrix in enumerate((first, second)):
+        terms[...] = complex_dot(matrix[...], x)
+        terms[pl.ds(start, height), :] -= unpack(y[half * p : half * p + half, :], COLS)
+        value = pack(terms[...])
+        kept = (lax.axis_index("front") & 1) == p
+
+        @pl.when(kept)
+        def _():
+            keep[...] = value
+
+        @pl.when(jnp.logical_not(kept))
+        def _():
+            send[...] = value
+
+
+def root_to_leaf(matrix, *refs):
+    parts, (out, forward, adjoint, held) = refs[:-4], refs[-4:]
+    x = take_quarters(parts, held)
     out[...] = complex_dot(matrix[...], x)
     fields_of(x, forward, adjoint, ())
+
+
+def halved(value, keep, send):
+    rows = keep.shape[0]
+    odd = (lax.axis_index("front") & 1) == 1
+    low, high = value[:rows], value[rows:]
+    keep[...] = jnp.where(odd, high, low)
+    send[...] = jnp.where(odd, low, high)
 
 
 def add_halves(kept, came, first, second):
@@ -368,14 +409,23 @@
     return jnp.concatenate([jnp.where(odd, theirs, mine), jnp.where(odd, mine, theirs)], axis=0)
 
 
-def mid_upper(matrix, y, *refs):
-    tail, out = unpack(summed(refs[:4]), 2 * COLS), refs[4]
-    out[...] = pack(complex_dot(matrix[...], y[...] - tail))
-
-
-def mid_to_leaf(matrix, from_root, mine, other, keep, send, x_mid):
-    x = by_solve(lax.axis_index("leaf"), unpack(mine[...], 2 * COLS), unpack(other[...], 2 * COLS))
-    x_mid[...] = x
+def mid_upper(first, second, *refs):
+    value, out = summed(refs[:4]), refs[4]
+    rows = value.shape[0] // 2
+    out[...] = -jnp.concatenate(
+        [
+            pack(complex_dot(matrix[...], unpack(value[rows * p : rows * p + rows], COLS)))
+            for p, matrix in enumerate((first, second))
+        ],
+        axis=0,
+    )
+
+
+def mid_to_leaf(matrix, from_root, *refs):
+    parts, (keep, send, held) = refs[:-3], refs[-3:]
+    half = parts[0].shape[0] // 2
+    start = pl.multiple_of(lax.axis_index("leaf") // 2 * half, 8)
+    x = take_quarters([part[pl.ds(start, half), :] for part in parts], held)
     halved(complex_dot(matrix[...], x) + from_root[...], keep, send)
 
 
@@ -384,10 +434,12 @@
     fields_of(complex_dot(matrix[...], y[...] - summed(refs[:4])), forward, adjoint, ())
 
 
-def mid_outputs(mine, other, forward, adjoint):
-    parent = lax.axis_index("leaf") // 2
-    fields_of(mine[...], forward, adjoint, (parent,))
-    fields_of(other[...], forward, adjoint, (1 - parent,))
+def mid_outputs(*refs):
+    parts, (forward, adjoint, held) = refs[:-3], refs[-3:]
+    half = parts[0].shape[0] // 2
+    for p in range(2):
+        x = take_quarters([part[half * p : half * p + half, :] for part in parts], held)
+        fields_of(x, forward, adjoint, (p,))
 
 
 def after(x, *others):
@@ -420,6 +472,8 @@
     slots, count = fronts * CAP, receiver_data.shape[1]
     dma = pltpu.SemaphoreType.DMA
 
+    vmem = pltpu.VMEM
+
     with jax.named_scope("right_hand_sides"):
         payload = kernel(
             functools.partial(pack_receivers, fronts, n0),
@@ -428,14 +482,14 @@
             receiver_block.reshape(1, -1),
             receiver_offset.reshape(1, -1),
             scratch=[
-                pltpu.VMEM((2, count, COLS), F32),
-                pltpu.VMEM((1, count), jnp.int32),
-                pltpu.VMEM((1, count), jnp.int32),
+                vmem((2, count, COLS), F32),
+                vmem((1, count), jnp.int32),
+                vmem((1, count), jnp.int32),
                 dma((3,)),
             ],
             hbm=range(3),
         )
-        arrived = [payload[0]] + [swap("leaf", payload[k], k) for k in range(1, groups)]
+        arrived = planes(payload)
         leaf_own, mid_own, root_own = kernel(
             load_sources,
             [(n0, LANES), (n1 // 2, LANES), (n2 // 4, LANES)],
@@ -443,113 +497,122 @@
             mid_sources.transpose(0, 1, 3, 2),
             root_sources.transpose(0, 2, 1),
             scratch=[
-                pltpu.VMEM((2, COLS, n0), F32),
-                pltpu.VMEM((2, COLS, n1), F32),
-                pltpu.VMEM((2, COLS, n2), F32),
+                vmem((2, COLS, n0), F32),
+                vmem((2, 2, COLS, n1), F32),
+                vmem((2, COLS, n2), F32),
                 dma((3,)),
             ],
             hbm=range(3),
         )
-        ll, l2m = load((after(leaf_lower_inv, leaf_own), "leaf"), (leaf_to_mid_lower, "leaf"))
+        ll, l2m, l2r = load(
+            (after(leaf_lower_inv, leaf_own), 0), (leaf_to_mid_lower, 0), (leaf_to_root_lower, 0)
+        )
         (message,) = kernel(
             pack_leaf, [(sum(message_rows(n0, groups * slots)), LANES)], after(leaf_own, ll), *arrived
         )
     with jax.named_scope("leaf_lower"):
-        messages = gather_front(message)
-        ml, m2r = load((after(mid_lower_inv, message), "own"), (mid_to_root_lower, "own"))
+        messages, ml = gather_front(
+            message, lambda x: load((after(mid_lower_inv, x), 0), (mid_lower_inv, 1))
+        )
         (y_leaf,) = kernel(
             functools.partial(leaf_lower, groups * slots),
             [(n0, LANES)],
-            after(ll, ml),
+            ll,
             *messages,
-            scratch=[pltpu.VMEM((s0, LANES), F32)],
+            scratch=[vmem((s0, LANES), F32)],
         )
     with jax.named_scope("mid_lower"):
-        parts = gather_front(y_leaf)
-        (l2r,) = load((after(leaf_to_root_lower, y_leaf), "leaf"))
-        keep, send, y_full = kernel(
+        parts, m2r = gather_front(
+            y_leaf, lambda x: load((after(mid_to_root_lower, x), 0), (mid_to_root_lower, 1))
+        )
+        *blocks, y_full = kernel(
             leaf_to_mid,
-            [(n1 // 2, LANES), (n1 // 2, LANES), (s0, LANES)],
-            after(l2m, l2r),
-            mid_own,
+            [(n1 // 4, LANES)] * groups + [(s0, LANES)],
+            l2m,
             *parts,
-        )
-        came = swap("leaf", send, 1)
-        root_kept, root_sent = kernel(leaf_to_root, [(n2, 2 * COLS)] * 2, l2r, after(y_full, send))
-        (cut_mid,) = kernel(add, [(n1 // 2, LANES)], after(keep, root_kept), came)
-        parts = gather_front(cut_mid)
-        root_came = swap("leaf", root_sent, 1)
-        (rl,) = load((after(root_lower_inv, cut_mid), None))
+            scratch=[vmem((groups, n1 // 4, LANES), F32)],
+        )
+        came = planes(blocks)
+        to_root = kernel(
+            leaf_to_root,
+            [(n2 // 4, LANES)] * groups,
+            l2r,
+            after(y_full, *blocks),
+            scratch=[vmem((groups, n2 // 4, LANES), F32)],
+        )
+        (cut_mid,) = kernel(cut_mids, [(n1 // 2, LANES)], after(mid_own, *to_root), *came)
+        parts, (rl,) = gather_front(cut_mid, lambda x: load((after(root_lower_inv, x), None)))
         (y_mid,) = kernel(
-            mid_lower,
-            [(n1 // 2, LANES)],
-            after(ml, rl),
+            mid_lower, [(n1 // 2, LANES)], *ml, *parts, scratch=[vmem((2, s1, COLS), F32)]
+        )
+    with jax.named_scope("root_cut"):
+        parts, (ru,) = gather_front(y_mid, lambda x: load((after(root_upper_inv, x), None)))
+        from_leaves = planes([after(block, cut_mid) for block in to_root])
+        (cut_root,) = kernel(
+            mid_to_root,
+            [(n2 // 4, LANES)],
+            *m2r,
+            root_own,
+            *from_leaves,
             *parts,
-            scratch=[pltpu.VMEM((s1, 2 * COLS), F32)],
-        )
-    with jax.named_scope("root_cut"):
-        parts = gather_front(y_mid)
-        (ru,) = load((after(root_upper_inv, y_mid), None))
-        keep, send, y_mid_full = kernel(
-            mid_to_root,
-            [(n2 // 4, LANES), (n2 // 4, LANES), (s1, 2 * COLS)],
-            after(m2r, ru),
-            root_kept,
-            root_came,
-            root_own,
-            *parts,
-        )
-        came = swap("leaf", send, 2)
-        mu, l2r_up = load((after(mid_upper_inv, send), "own"), (leaf_to_root_upper, "leaf"))
-        (cut_root,) = kernel(add, [(n2 // 4, LANES)], after(keep, mu), came)
+            scratch=[vmem((2, s1, COLS), F32)],
+        )
     with jax.named_scope("root_solve"):
-        parts = gather_front(cut_root)
-        (m2r_up,) = load((after(mid_to_root_upper, cut_root), "own"))
+        parts, m2r_up = gather_front(
+            cut_root, lambda x: load((after(mid_to_root_upper, x), 0), (mid_to_root_upper, 1))
+        )
         (y_root,) = kernel(
-            root_rows,
-            [(n2 // 4, LANES)],
-            after(rl, m2r_up),
-            *parts,
-            scratch=[pltpu.VMEM((s2, COLS), F32)],
-        )
-        parts = gather_front(y_root)
-        l2m_up, lu = load((after(leaf_to_mid_upper, y_root), "leaf"), (leaf_upper_inv, "leaf"))
+            root_rows, [(n2 // 4, LANES)], rl, *parts, scratch=[vmem((s2, COLS), F32)]
+        )
+        parts, (*mu, l2r_up, l2m_up, lu) = gather_front(
+            y_root,
+            lambda x: load(
+                (after(mid_upper_inv, x), 0),
+                (mid_upper_inv, 1),
+                (leaf_to_root_upper, 0),
+                (leaf_to_mid_upper, 0),
+                (leaf_upper_inv, 0),
+            ),
+        )
         (x_root,) = kernel(
-            root_rows,
-            [(n2 // 4, LANES)],
-            after(ru, lu),
-            *parts,
-            scratch=[pltpu.VMEM((s2, COLS), F32)],
+            root_rows, [(n2 // 4, LANES)], ru, *parts, scratch=[vmem((s2, COLS), F32)]
         )
     with jax.named_scope("mid_upper"):
-        keep, send, x_root = kernel(
+        keep, send = kernel(
             root_to_mid,
-            [(s1 // 4, LANES)] * 2 + [(n2 // 2, LANES)],
-            m2r_up,
+            [(s1 // 4, LANES)] * 2,
+            *m2r_up,
             x_root,
-            swap("leaf", x_root, 2),
+            y_mid,
+            scratch=[vmem((s1, COLS), F32)],
         )
         pieces = sum_front(keep, send)
-        (x_mid,) = kernel(mid_upper, [(n1 // 2, LANES)], mu, y_mid_full, *pieces)
+        (x_mid,) = kernel(mid_upper, [(n1 // 2, LANES)], *mu, *pieces)
         from_root, root_field, root_adjoint = kernel(
             root_to_leaf,
             [(s0, LANES), (2, COLS, n2), (2, COLS, n2)],
             l2r_up,
-            x_root,
-            swap("leaf", after(x_root, send), 1),
+            *planes(after(x_root, send)),
+            scratch=[vmem((groups, n2 // 4, LANES), F32)],
         )
     with jax.named_scope("leaf_upper"):
-        keep, send, x_mid = kernel(
+        x_mids = planes(x_mid)
+        keep, send = kernel(
             mid_to_leaf,
-            [(s0 // 2, LANES)] * 2 + [(n1, LANES)],
+            [(s0 // 2, LANES)] * 2,
             l2m_up,
             from_root,
-            x_mid,
-            swap("leaf", x_mid, 1),
+            *x_mids,
+            scratch=[vmem((groups, n1 // 4, LANES), F32)],
         )
         pieces = sum_front(keep, send)
-        x_other = swap("leaf", after(x_mid, send), 2)
-        mid_field, mid_adjoint = kernel(mid_outputs, [(2, 2, COLS, n1)] * 2, x_mid, x_other)
+        mid_field, mid_adjoint = kernel(
+            mid_outputs,
+            [(2, 2, COLS, n1)] * 2,
+            after(x_mids[0], send),
+            *x_mids[1:],
+            scratch=[vmem((groups, n1 // 4, LANES), F32)],
+        )
         leaf_field, leaf_adjoint = kernel(leaf_upper, [(2, COLS, n0)] * 2, lu, y_full, *pieces)
     return tuple(
         jnp.swapaxes(x, -1, -2)

time: 124 us -> 129 us (1.040)
  Pallas kernels: 18.8 us -> 36.9 us
  waiting for transfers between devices: 46.9 us -> 32.5 us
  starting transfers between devices: 46 us -> 58.8 us
  local copies, waits for them, and re-layouts: 10.4 us -> 0 us
    pallas_call x32 -> x30, Pallas kernels: 18.8 us -> 36.9 us  [kernel(): pl.pallas_call(fn, out_shape=[jax.ShapeDtypeStruct(*o) for o in outs], in...]
    ppermute x66 -> x71, waiting for transfers between devices: 46.9 us -> 32.5 us  [swap(): return lax.ppermute(x, axis, [(i, i ^ k) for i in range(size)])]
    ppermute x66 -> x71, starting transfers between devices: 46 us -> 58.8 us  [swap(): return lax.ppermute(x, axis, [(i, i ^ k) for i in range(size)])]
    unnamed x36 -> x0, local copies, waits for them, and re-layouts: 10.4 us -> none
  transfers between devices with their start and end apart: 66 -> 71, of which waited for: 44 -> 34; matrix products, arithmetic and copies ran while one was open for 0% -> 0% of each run, Pallas kernels for 7% -> 18%
where the time goes in v4:
time: 129 us
  starting transfers between devices  58.8 us (46%)
  Pallas kernels  36.9 us (29%)
  waiting for transfers between devices  32.5 us (25%)
    ppermute x71, starting transfers between devices, swap(): return lax.ppermute(x, axis, [(i, i ^ k) for i in range(size)])  58.8 us
    pallas_call x30, Pallas kernels, kernel(): pl.pallas_call(fn, out_shape=[jax.ShapeDtypeStruct(*o) for o in outs], in...  36.9 us
    ppermute x71, waiting for transfers between devices, swap(): return lax.ppermute(x, axis, [(i, i ^ k) for i in range(size)])  32.5 us
  transfers between devices with their start and end apart: 71, of which 34 were waited for; matrix products, arithmetic and copies ran while one was open for 0% of the time, Pallas kernels for 18%

profile of v4, /device:TPU:0, one launch (start us, length us, event | category | flops | bytes accessed | tf_op | source)
XLA Modules:
  0.0 129.2 jit_solution(11606950674790925613)
XLA Ops:
  1.7 3.1 %collective-permute-start = (f32[16,128]{1,0:T(8,128)S(1)}, f32[16,128]{1,0:T(8,128)S(1)}, u32[]{:S(2)}, u32[]{:S(2)}) collective-permute-start(f32[16,128]{1,0:T(8,128)S(1)} %get-tuple-element.95), channel_id=1, source_target_pairs={{0,8},{8,0},{16,24},{24,16},{1,9},{9,1},{17,25},{25,17},{2,10},{10... | collective-permute-start | bytes 24584 | tf_op jit(solution)/shard_map/right_hand_sides/ppermute | solution.py:91
  4.8 2.6 %collective-permute-start.1 = (f32[16,128]{1,0:T(8,128)S(1)}, f32[16,128]{1,0:T(8,128)S(1)}, u32[]{:S(2)}, u32[]{:S(2)}) collective-permute-start(f32[16,128]{1,0:T(8,128)S(1)} %get-tuple-element.96), channel_id=1, source_target_pairs={{0,16},{8,24},{16,0},{24,8},{1,17},{9,25},{17,1},{25,9},{2,18},{10... | collective-permute-start | bytes 24584 | tf_op jit(solution)/shard_map/right_hand_sides/ppermute | solution.py:91
  8.6 1.6 %right_hand_sides.6 = (bf16[128,1024]{1,0:T(8,128)(2,1)S(1)}, bf16[256,1024]{1,0:T(8,128)(2,1)S(1)}, bf16[512,1024]{1,0:T(8,128)(2,1)S(1)}) custom-call(f32[2,1,64,512]{3,2,1,0:T(8,128)} %refs_0_, f32[2,1,128,512]{3,2,1,0:T(8,128)} %refs_1_.5, f32[2,1,256,512]{3,2,1,0:T(8,128)} %refs_2_.2), custom_call_target="tpu_custom_call" | custom-call | flops 229376000 | bytes 327680 | tf_op jit(solution)/shard_map/right_hand_sides/pallas_call | solution.py:115
  10.2 2.7 %collective-permute-done.2.refs_3_ = f32[16,128]{1,0:T(8,128)S(1)} collective-permute-done((f32[16,128]{1,0:T(8,128)S(1)}, f32[16,128]{1,0:T(8,128)S(1)}, u32[]{:S(2)}, u32[]{:S(2)}) %collective-permute-start.2) | collective-permute-done | bytes 8224 | tf_op jit(solution)/shard_map/right_hand_sides/ppermute | solution.py:91
  12.9 2.5 %collective-permute-start.8 = (f32[72,128]{1,0:T(8,128)S(1)}, f32[72,128]{1,0:T(8,128)S(1)}, u32[]{:S(2)}, u32[]{:S(2)}) collective-permute-start(f32[72,128]{1,0:T(8,128)S(1)} %right_hand_sides.7.refs_0_), channel_id=1, source_target_pairs={{0,6},{1,7},{2,4},{3,5},{4,2},{5,3},{6,0},{7,1},{8,14},{9,15},{10,... | collective-permute-start | bytes 110600 | tf_op jit(solution)/shard_map/leaf_lower/ppermute | solution.py:91
  16.5 1.6 %leaf_lower.2 = (bf16[256,2048]{1,0:T(8,128)(2,1)S(1)}, bf16[256,2048]{1,0:T(8,128)(2,1)S(1)}) custom-call(f32[2,2,128,1024]{3,2,1,0:T(8,128)} %refs_1_.6, f32[2,2,128,1024]{3,2,1,0:T(8,128)} %refs_1_.6), custom_call_target="tpu_custom_call" | custom-call | flops 262144000 | bytes 374491 | tf_op jit(solution)/shard_map/leaf_lower/pallas_call | solution.py:115
  25.8 2.4 %mid_lower.6 = (bf16[512,2048]{1,0:T(8,128)(2,1)S(1)}, bf16[512,2048]{1,0:T(8,128)(2,1)S(1)}) custom-call(f32[2,2,256,1024]{3,2,1,0:T(8,128)} %refs_1_.7, f32[2,2,256,1024]{3,2,1,0:T(8,128)} %refs_1_.7), custom_call_target="tpu_custom_call" | custom-call | flops 524288000 | bytes 748982 | tf_op jit(solution)/shard_map/mid_lower/pallas_call | solution.py:115
  30.9 1.7 %collective-permute-start.18 = (f32[32,128]{1,0:T(8,128)S(1)}, f32[32,128]{1,0:T(8,128)S(1)}, u32[]{:S(2)}, u32[]{:S(2)}) collective-permute-start(f32[32,128]{1,0:T(8,128)S(1)} %get-tuple-element.121), channel_id=1, source_target_pairs={{0,16},{8,24},{16,0},{24,8},{1,17},{9,25},{17,1},{25,9},{2,18},{10... | collective-permute-start | bytes 49160 | tf_op jit(solution)/shard_map/mid_lower/ppermute | solution.py:91
  32.6 2.7 %collective-permute-start.19 = (f32[32,128]{1,0:T(8,128)S(1)}, f32[32,128]{1,0:T(8,128)S(1)}, u32[]{:S(2)}, u32[]{:S(2)}) collective-permute-start(f32[32,128]{1,0:T(8,128)S(1)} %get-tuple-element.122), channel_id=1, source_target_pairs={{0,24},{8,16},{16,8},{24,0},{1,25},{9,17},{17,9},{25,1},{2,26},{10... | collective-permute-start | bytes 49160 | tf_op jit(solution)/shard_map/mid_lower/ppermute | solution.py:91
  36.2 2.0 %collective-permute-done.19.other = f32[32,128]{1,0:T(8,128)S(1)} collective-permute-done((f32[32,128]{1,0:T(8,128)S(1)}, f32[32,128]{1,0:T(8,128)S(1)}, u32[]{:S(2)}, u32[]{:S(2)}) %collective-permute-start.19) | collective-permute-done | bytes 16416 | tf_op jit(solution)/shard_map/mid_lower/ppermute | solution.py:91
  38.2 2.3 %collective-permute-start.28 = (f32[64,128]{1,0:T(8,128)S(1)}, f32[64,128]{1,0:T(8,128)S(1)}, u32[]{:S(2)}, u32[]{:S(2)}) collective-permute-start(f32[64,128]{1,0:T(8,128)S(1)} %mid_lower.9.refs_0_), channel_id=1, source_target_pairs={{0,6},{1,7},{2,4},{3,5},{4,2},{5,3},{6,0},{7,1},{8,14},{9,15},{10,... | collective-permute-start | bytes 98312 | tf_op jit(solution)/shard_map/mid_lower/ppermute | solution.py:91
  41.8 2.5 %mid_lower.10.matrix = bf16[512,4096]{1,0:T(8,128)(2,1)S(1)} custom-call(f32[2,256,2048]{2,1,0:T(8,128)} %refs_0_.3), custom_call_target="tpu_custom_call" | custom-call | flops 524288000 | bytes 748982 | tf_op jit(solution)/shard_map/mid_lower/pallas_call | solution.py:115
  45.4 3.2 %collective-permute-start.21 = (f32[64,128]{1,0:T(8,128)S(1)}, f32[64,128]{1,0:T(8,128)S(1)}, u32[]{:S(2)}, u32[]{:S(2)}) collective-permute-start(f32[64,128]{1,0:T(8,128)S(1)} %get-tuple-element.133), channel_id=1, source_target_pairs={{0,16},{8,24},{16,0},{24,8},{1,17},{9,25},{17,1},{25,9},{2,18},{10... | collective-permute-start | bytes 98312 | tf_op jit(solution)/shard_map/root_cut/ppermute | solution.py:91
  48.7 2.0 %mid_lower.11.refs_0_.y = f32[64,128]{1,0:T(8,128)S(1)} custom-call(bf16[256,2048]{1,0:T(8,128)(2,1)S(1)} %get-tuple-element.107.first, bf16[256,2048]{1,0:T(8,128)(2,1)S(1)} %get-tuple-element.108.second, f32[64,128]{1,0:T(8,128)S(1)} %mid_lower.9.refs_0_, f32[64,128]{1,0:T(8,128)S(1)} %collective-permute-done.23.refs_1_, ...), custom_call_target="tpu_custom_call" | custom-call | tf_op jit(solution)/shard_map/mid_lower/pallas_call | solution.py:115
  50.7 2.3 %collective-permute-start.35 = (f32[64,128]{1,0:T(8,128)S(1)}, f32[64,128]{1,0:T(8,128)S(1)}, u32[]{:S(2)}, u32[]{:S(2)}) collective-permute-start(f32[64,128]{1,0:T(8,128)S(1)} %mid_lower.11.refs_0_.y), channel_id=1, source_target_pairs={{0,6},{1,7},{2,4},{3,5},{4,2},{5,3},{6,0},{7,1},{8,14},{9,15},{10,... | collective-permute-start | bytes 98312 | tf_op jit(solution)/shard_map/root_cut/ppermute | solution.py:91
  54.2 2.5 %root_cut.2.matrix = bf16[512,4096]{1,0:T(8,128)(2,1)S(1)} custom-call(f32[2,256,2048]{2,1,0:T(8,128)} %refs_0_.4), custom_call_target="tpu_custom_call" | custom-call | flops 524288000 | bytes 748982 | tf_op jit(solution)/shard_map/root_cut/pallas_call | solution.py:115
  59.0 3.5 %collective-permute-done.22.d = f32[64,128]{1,0:T(8,128)S(1)} collective-permute-done((f32[64,128]{1,0:T(8,128)S(1)}, f32[64,128]{1,0:T(8,128)S(1)}, u32[]{:S(2)}, u32[]{:S(2)}) %collective-permute-start.22) | collective-permute-done | bytes 32800 | tf_op jit(solution)/shard_map/root_cut/ppermute | solution.py:91
  62.6 1.7 %root_cut.3.refs_0_ = f32[64,128]{1,0:T(8,128)S(1)} custom-call(bf16[512,2048]{1,0:T(8,128)(2,1)S(1)} %get-tuple-element.113.first, bf16[512,2048]{1,0:T(8,128)(2,1)S(1)} %get-tuple-element.114.second, f32[64,128]{1,0:T(8,128)S(1)} %get-tuple-element.130.sources, f32[64,128]{1,0:T(8,128)S(1)} %get-tuple-element.131.a, ...), custom_call_target="tpu_custom_call" | custom-call | tf_op jit(solution)/shard_map/root_cut/pallas_call | solution.py:115
  64.3 2.3 %collective-permute-start.42 = (f32[64,128]{1,0:T(8,128)S(1)}, f32[64,128]{1,0:T(8,128)S(1)}, u32[]{:S(2)}, u32[]{:S(2)}) collective-permute-start(f32[64,128]{1,0:T(8,128)S(1)} %root_cut.3.refs_0_), channel_id=1, source_target_pairs={{0,6},{1,7},{2,4},{3,5},{4,2},{5,3},{6,0},{7,1},{8,14},{9,15},{10,... | collective-permute-start | bytes 98312 | tf_op jit(solution)/shard_map/root_solve/ppermute | solution.py:91
  67.9 2.4 %root_solve.4 = (bf16[2048,512]{1,0:T(8,128)(2,1)S(1)}, bf16[2048,512]{1,0:T(8,128)(2,1)S(1)}) custom-call(f32[2,2,1024,256]{3,2,1,0:T(8,128)} %refs_1_.8, f32[2,2,1024,256]{3,2,1,0:T(8,128)} %refs_1_.8), custom_call_target="tpu_custom_call" | custom-call | flops 524288000 | bytes 748982 | tf_op jit(solution)/shard_map/root_solve/pallas_call | solution.py:115
  72.7 2.0 %root_solve.5.refs_0_ = f32[64,128]{1,0:T(8,128)S(1)} custom-call(bf16[512,4096]{1,0:T(8,128)(2,1)S(1)} %mid_lower.10.matrix, f32[64,128]{1,0:T(8,128)S(1)} %root_cut.3.refs_0_, f32[64,128]{1,0:T(8,128)S(1)} %collective-permute-done.37.refs_1_, f32[64,128]{1,0:T(8,128)S(1)} %collective-permute-done.38.refs_2_, ...), custom_call_target="tpu_custom_call" | custom-call | tf_op jit(solution)/shard_map/root_solve/pallas_call | solution.py:115
  74.7 1.8 %collective-permute-start.49 = (f32[64,128]{1,0:T(8,128)S(1)}, f32[64,128]{1,0:T(8,128)S(1)}, u32[]{:S(2)}, u32[]{:S(2)}) collective-permute-start(f32[64,128]{1,0:T(8,128)S(1)} %root_solve.5.refs_0_), channel_id=1, source_target_pairs={{0,6},{1,7},{2,4},{3,5},{4,2},{5,3},{6,0},{7,1},{8,14},{9,15},{10,... | collective-permute-start | bytes 98312 | tf_op jit(solution)/shard_map/root_solve/ppermute | solution.py:91
  78.3 2.2 %root_solve.6 = (bf16[256,2048]{1,0:T(8,128)(2,1)S(1)}, bf16[256,2048]{1,0:T(8,128)(2,1)S(1)}, bf16[1024,512]{1,0:T(8,128)(2,1)S(1)}, bf16[1024,256]{1,0:T(8,128)(2,1)S(1)}, bf16[128,1024]{1,0:T(8,128)(2,1)S(1)}) custom-call(f32[2,2,128,1024]{3,2,1,0:T(8,128)} %refs_1_.9, f32[2,2,128,1024]{3,2,1,0:T(8,128)} %refs_1_.9, f32[2,1,512,256]{3,2,1,0:T(8,128)} %refs_2_.3, ...), custom_call_target="tpu_custom_call" | custom-call | flops 491520000 | bytes 702171 | tf_op jit(solution)/shard_map/root_solve/pallas_call | solution.py:115
  82.7 1.9 %root_solve.7.quarter.refs_0_ = f32[64,128]{1,0:T(8,128)S(1)} custom-call(bf16[512,4096]{1,0:T(8,128)(2,1)S(1)} %root_cut.2.matrix, f32[64,128]{1,0:T(8,128)S(1)} %root_solve.5.refs_0_, f32[64,128]{1,0:T(8,128)S(1)} %collective-permute-done.44.refs_1_, f32[64,128]{1,0:T(8,128)S(1)} %collective-permute-done.45.refs_2_, ...), custom_call_target="tpu_custom_call" | custom-call | tf_op jit(solution)/shard_map/root_solve/pallas_call | solution.py:115
  84.5 3.2 %mid_upper.6 = (f32[256,128]{1,0:T(8,128)S(1)}, f32[256,128]{1,0:T(8,128)S(1)}) custom-call(bf16[2048,512]{1,0:T(8,128)(2,1)S(1)} %get-tuple-element.143.first, bf16[2048,512]{1,0:T(8,128)(2,1)S(1)} %get-tuple-element.144.second, f32[64,128]{1,0:T(8,128)S(1)} %root_solve.7.quarter.refs_0_, f32[64,128]{1,0:T(8,128)S(1)} %mid_lower.11.refs_0_.y), custom_call_target="tpu_custom_call" | custom-call | tf_op jit(solution)/shard_map/mid_upper/pallas_call | solution.py:115
  94.8 1.6 %collective-permute-start.57 = (f32[128,128]{1,0:T(8,128)S(1)}, f32[128,128]{1,0:T(8,128)S(1)}, u32[]{:S(2)}, u32[]{:S(2)}) collective-permute-start(f32[128,128]{1,0:T(8,128)S(1)} %get-tuple-element.163.a), channel_id=1, source_target_pairs={{0,4},{1,5},{2,6},{3,7},{4,0},{5,1},{6,2},{7,3},{8,12},{9,13},{10,... | collective-permute-start | bytes 196616 | tf_op jit(solution)/shard_map/mid_upper/ppermute | solution.py:91
  97.2 2.0 %collective-permute-done.57.b = f32[128,128]{1,0:T(8,128)S(1)} collective-permute-done((f32[128,128]{1,0:T(8,128)S(1)}, f32[128,128]{1,0:T(8,128)S(1)}, u32[]{:S(2)}, u32[]{:S(2)}) %collective-permute-start.57) | collective-permute-done | bytes 65568 | tf_op jit(solution)/shard_map/mid_upper/ppermute | solution.py:91
  102.4 3.2 %collective-permute-start.51 = (f32[64,128]{1,0:T(8,128)S(1)}, f32[64,128]{1,0:T(8,128)S(1)}, u32[]{:S(2)}, u32[]{:S(2)}) collective-permute-start(f32[64,128]{1,0:T(8,128)S(1)} %root_solve.7.quarter.refs_0_), channel_id=1, source_target_pairs={{0,8},{8,0},{16,24},{24,16},{1,9},{9,1},{17,25},{25,17},{2,10},{10... | collective-permute-start | bytes 98312 | tf_op jit(solution)/shard_map/mid_upper/ppermute | solution.py:91
  105.7 2.0 %mid_upper.11.refs_0_ = f32[64,128]{1,0:T(8,128)S(1)} custom-call(bf16[256,2048]{1,0:T(8,128)(2,1)S(1)} %get-tuple-element.152.first, bf16[256,2048]{1,0:T(8,128)(2,1)S(1)} %get-tuple-element.153.second, f32[128,128]{1,0:T(8,128)S(1)} %get-tuple-element.165.refs_0_, f32[128,128]{1,0:T(8,128)S(1)} %get-tuple-element.166.refs_1_, ...), custom_call_target="tpu_custom_call" | custom-call | tf_op jit(solution)/shard_map/mid_upper/pallas_call | solution.py:115
  109.2 2.9 %collective-permute-start.61 = (f32[64,128]{1,0:T(8,128)S(1)}, f32[64,128]{1,0:T(8,128)S(1)}, u32[]{:S(2)}, u32[]{:S(2)}) collective-permute-start(f32[64,128]{1,0:T(8,128)S(1)} %mid_upper.11.refs_0_), channel_id=1, source_target_pairs={{0,8},{8,0},{16,24},{24,16},{1,9},{9,1},{17,25},{25,17},{2,10},{10... | collective-permute-start | bytes 98312 | tf_op jit(solution)/shard_map/leaf_upper/ppermute | solution.py:91
  117.7 3.0 %collective-permute-done.65.b = f32[128,128]{1,0:T(8,128)S(1)} collective-permute-done((f32[128,128]{1,0:T(8,128)S(1)}, f32[128,128]{1,0:T(8,128)S(1)}, u32[]{:S(2)}, u32[]{:S(2)}) %collective-permute-start.65) | collective-permute-done | bytes 65568 | tf_op jit(solution)/shard_map/leaf_upper/ppermute | solution.py:91
  123.3 2.5 %collective-permute-done.67.b = f32[128,128]{1,0:T(8,128)S(1)} collective-permute-done((f32[128,128]{1,0:T(8,128)S(1)}, f32[128,128]{1,0:T(8,128)S(1)}, u32[]{:S(2)}, u32[]{:S(2)}) %collective-permute-start.67) | collective-permute-done | bytes 65568 | tf_op jit(solution)/shard_map/leaf_upper/ppermute | solution.py:91
  (140 shorter events, 52.3 us)
Async XLA Ops:
  1.7 8.4 %collective-permute-start = (f32[16,128]{1,0:T(8,128)S(1)}, f32[16,128]{1,0:T(8,128)S(1)}, u32[]{:S(2)}, u32[]{:S(2)}) collective-permute-start(f32[16,128]{1,0:T(8,128)S(1)} %get-tuple-element.95), channel_id=1, source_target_pairs={{0,8},{8,0},{16,24},{24,16},{1,9},{9,1},{17,25},{25,17},{2,10},{10... | collective-permute-start | bytes 24584 | tf_op jit(solution)/shard_map/right_hand_sides/ppermute | solution.py:91
  4.8 5.4 %collective-permute-start.1 = (f32[16,128]{1,0:T(8,128)S(1)}, f32[16,128]{1,0:T(8,128)S(1)}, u32[]{:S(2)}, u32[]{:S(2)}) collective-permute-start(f32[16,128]{1,0:T(8,128)S(1)} %get-tuple-element.96), channel_id=1, source_target_pairs={{0,16},{8,24},{16,0},{24,8},{1,17},{9,25},{17,1},{25,9},{2,18},{10... | collective-permute-start | bytes 24584 | tf_op jit(solution)/shard_map/right_hand_sides/ppermute | solution.py:91
  7.4 5.4 %collective-permute-start.2 = (f32[16,128]{1,0:T(8,128)S(1)}, f32[16,128]{1,0:T(8,128)S(1)}, u32[]{:S(2)}, u32[]{:S(2)}) collective-permute-start(f32[16,128]{1,0:T(8,128)S(1)} %get-tuple-element.97), channel_id=1, source_target_pairs={{0,24},{8,16},{16,8},{24,0},{1,25},{9,17},{17,9},{25,1},{2,26},{10... | collective-permute-start | bytes 24584 | tf_op jit(solution)/shard_map/right_hand_sides/ppermute | solution.py:91
  12.9 5.2 %collective-permute-start.8 = (f32[72,128]{1,0:T(8,128)S(1)}, f32[72,128]{1,0:T(8,128)S(1)}, u32[]{:S(2)}, u32[]{:S(2)}) collective-permute-start(f32[72,128]{1,0:T(8,128)S(1)} %right_hand_sides.7.refs_0_), channel_id=1, source_target_pairs={{0,6},{1,7},{2,4},{3,5},{4,2},{5,3},{6,0},{7,1},{8,14},{9,15},{10,... | collective-permute-start | bytes 110600 | tf_op jit(solution)/shard_map/leaf_lower/ppermute | solution.py:91
  22.3 6.0 %collective-permute-start.15 = (f32[64,128]{1,0:T(8,128)S(1)}, f32[64,128]{1,0:T(8,128)S(1)}, u32[]{:S(2)}, u32[]{:S(2)}) collective-permute-start(f32[64,128]{1,0:T(8,128)S(1)} %leaf_lower.3.refs_0_), channel_id=1, source_target_pairs={{0,6},{1,7},{2,4},{3,5},{4,2},{5,3},{6,0},{7,1},{8,14},{9,15},{10,... | collective-permute-start | bytes 98312 | tf_op jit(solution)/shard_map/mid_lower/ppermute | solution.py:91
  23.8 4.4 %collective-permute-start.13 = (f32[64,128]{1,0:T(8,128)S(1)}, f32[64,128]{1,0:T(8,128)S(1)}, u32[]{:S(2)}, u32[]{:S(2)}) collective-permute-start(f32[64,128]{1,0:T(8,128)S(1)} %leaf_lower.3.refs_0_), channel_id=1, source_target_pairs={{0,4},{1,5},{2,6},{3,7},{4,0},{5,1},{6,2},{7,3},{8,12},{9,13},{10,... | collective-permute-start | bytes 98312 | tf_op jit(solution)/shard_map/mid_lower/ppermute | solution.py:91
  30.9 5.3 %collective-permute-start.17 = (f32[32,128]{1,0:T(8,128)S(1)}, f32[32,128]{1,0:T(8,128)S(1)}, u32[]{:S(2)}, u32[]{:S(2)}) collective-permute-start(f32[32,128]{1,0:T(8,128)S(1)} %get-tuple-element.120), channel_id=1, source_target_pairs={{0,8},{8,0},{16,24},{24,16},{1,9},{9,1},{17,25},{25,17},{2,10},{10... | collective-permute-start | bytes 49160 | tf_op jit(solution)/shard_map/mid_lower/ppermute | solution.py:91
  30.9 5.2 %collective-permute-start.18 = (f32[32,128]{1,0:T(8,128)S(1)}, f32[32,128]{1,0:T(8,128)S(1)}, u32[]{:S(2)}, u32[]{:S(2)}) collective-permute-start(f32[32,128]{1,0:T(8,128)S(1)} %get-tuple-element.121), channel_id=1, source_target_pairs={{0,16},{8,24},{16,0},{24,8},{1,17},{9,25},{17,1},{25,9},{2,18},{10... | collective-permute-start | bytes 49160 | tf_op jit(solution)/shard_map/mid_lower/ppermute | solution.py:91
  32.6 5.5 %collective-permute-start.19 = (f32[32,128]{1,0:T(8,128)S(1)}, f32[32,128]{1,0:T(8,128)S(1)}, u32[]{:S(2)}, u32[]{:S(2)}) collective-permute-start(f32[32,128]{1,0:T(8,128)S(1)} %get-tuple-element.122), channel_id=1, source_target_pairs={{0,24},{8,16},{16,8},{24,0},{1,25},{9,17},{17,9},{25,1},{2,26},{10... | collective-permute-start | bytes 49160 | tf_op jit(solution)/shard_map/mid_lower/ppermute | solution.py:91
  38.2 6.1 %collective-permute-start.28 = (f32[64,128]{1,0:T(8,128)S(1)}, f32[64,128]{1,0:T(8,128)S(1)}, u32[]{:S(2)}, u32[]{:S(2)}) collective-permute-start(f32[64,128]{1,0:T(8,128)S(1)} %mid_lower.9.refs_0_), channel_id=1, source_target_pairs={{0,6},{1,7},{2,4},{3,5},{4,2},{5,3},{6,0},{7,1},{8,14},{9,15},{10,... | collective-permute-start | bytes 98312 | tf_op jit(solution)/shard_map/mid_lower/ppermute | solution.py:91
  45.4 13.1 %collective-permute-start.20 = (f32[64,128]{1,0:T(8,128)S(1)}, f32[64,128]{1,0:T(8,128)S(1)}, u32[]{:S(2)}, u32[]{:S(2)}) collective-permute-start(f32[64,128]{1,0:T(8,128)S(1)} %get-tuple-element.132), channel_id=1, source_target_pairs={{0,8},{8,0},{16,24},{24,16},{1,9},{9,1},{17,25},{25,17},{2,10},{10... | collective-permute-start | bytes 98312 | tf_op jit(solution)/shard_map/root_cut/ppermute | solution.py:91
  45.4 13.2 %collective-permute-start.21 = (f32[64,128]{1,0:T(8,128)S(1)}, f32[64,128]{1,0:T(8,128)S(1)}, u32[]{:S(2)}, u32[]{:S(2)}) collective-permute-start(f32[64,128]{1,0:T(8,128)S(1)} %get-tuple-element.133), channel_id=1, source_target_pairs={{0,16},{8,24},{16,0},{24,8},{1,17},{9,25},{17,1},{25,9},{2,18},{10... | collective-permute-start | bytes 98312 | tf_op jit(solution)/shard_map/root_cut/ppermute | solution.py:91
  50.7 6.1 %collective-permute-start.35 = (f32[64,128]{1,0:T(8,128)S(1)}, f32[64,128]{1,0:T(8,128)S(1)}, u32[]{:S(2)}, u32[]{:S(2)}) collective-permute-start(f32[64,128]{1,0:T(8,128)S(1)} %mid_lower.11.refs_0_.y), channel_id=1, source_target_pairs={{0,6},{1,7},{2,4},{3,5},{4,2},{5,3},{6,0},{7,1},{8,14},{9,15},{10,... | collective-permute-start | bytes 98312 | tf_op jit(solution)/shard_map/root_cut/ppermute | solution.py:91
  52.9 5.1 %collective-permute-start.33 = (f32[64,128]{1,0:T(8,128)S(1)}, f32[64,128]{1,0:T(8,128)S(1)}, u32[]{:S(2)}, u32[]{:S(2)}) collective-permute-start(f32[64,128]{1,0:T(8,128)S(1)} %mid_lower.11.refs_0_.y), channel_id=1, source_target_pairs={{0,4},{1,5},{2,6},{3,7},{4,0},{5,1},{6,2},{7,3},{8,12},{9,13},{10,... | collective-permute-start | bytes 98312 | tf_op jit(solution)/shard_map/root_cut/ppermute | solution.py:91
  53.4 4.6 %collective-permute-start.31 = (f32[64,128]{1,0:T(8,128)S(1)}, f32[64,128]{1,0:T(8,128)S(1)}, u32[]{:S(2)}, u32[]{:S(2)}) collective-permute-start(f32[64,128]{1,0:T(8,128)S(1)} %mid_lower.11.refs_0_.y), channel_id=1, source_target_pairs={{0,2},{1,3},{2,0},{3,1},{4,6},{5,7},{6,4},{7,5},{8,10},{9,11},{10,... | collective-permute-start | bytes 98312 | tf_op jit(solution)/shard_map/root_cut/ppermute | solution.py:91
  56.8 5.8 %collective-permute-start.22 = (f32[64,128]{1,0:T(8,128)S(1)}, f32[64,128]{1,0:T(8,128)S(1)}, u32[]{:S(2)}, u32[]{:S(2)}) collective-permute-start(f32[64,128]{1,0:T(8,128)S(1)} %get-tuple-element.134), channel_id=1, source_target_pairs={{0,24},{8,16},{16,8},{24,0},{1,25},{9,17},{17,9},{25,1},{2,26},{10... | collective-permute-start | bytes 98312 | tf_op jit(solution)/shard_map/root_cut/ppermute | solution.py:91
  58.0 4.6 %collective-permute-start.30 = (f32[64,128]{1,0:T(8,128)S(1)}, f32[64,128]{1,0:T(8,128)S(1)}, u32[]{:S(2)}, u32[]{:S(2)}) collective-permute-start(f32[64,128]{1,0:T(8,128)S(1)} %mid_lower.11.refs_0_.y), channel_id=1, source_target_pairs={{0,1},{1,0},{2,3},{3,2},{4,5},{5,4},{6,7},{7,6},{8,9},{9,8},{10,11... | collective-permute-start | bytes 98312 | tf_op jit(solution)/shard_map/root_cut/ppermute | solution.py:91
  58.0 4.5 %collective-permute-start.32 = (f32[64,128]{1,0:T(8,128)S(1)}, f32[64,128]{1,0:T(8,128)S(1)}, u32[]{:S(2)}, u32[]{:S(2)}) collective-permute-start(f32[64,128]{1,0:T(8,128)S(1)} %collective-permute-done.31.refs_2_), channel_id=1, source_target_pairs={{0,1},{1,0},{2,3},{3,2},{4,5},{5,4},{6,7},{7,6},{8,9},{9,8},{10,11... | collective-permute-start | bytes 98312 | tf_op jit(solution)/shard_map/root_cut/ppermute | solution.py:91
  64.3 6.0 %collective-permute-start.42 = (f32[64,128]{1,0:T(8,128)S(1)}, f32[64,128]{1,0:T(8,128)S(1)}, u32[]{:S(2)}, u32[]{:S(2)}) collective-permute-start(f32[64,128]{1,0:T(8,128)S(1)} %root_cut.3.refs_0_), channel_id=1, source_target_pairs={{0,6},{1,7},{2,4},{3,5},{4,2},{5,3},{6,0},{7,1},{8,14},{9,15},{10,... | collective-permute-start | bytes 98312 | tf_op jit(solution)/shard_map/root_solve/ppermute | solution.py:91
  74.7 5.7 %collective-permute-start.49 = (f32[64,128]{1,0:T(8,128)S(1)}, f32[64,128]{1,0:T(8,128)S(1)}, u32[]{:S(2)}, u32[]{:S(2)}) collective-permute-start(f32[64,128]{1,0:T(8,128)S(1)} %root_solve.5.refs_0_), channel_id=1, source_target_pairs={{0,6},{1,7},{2,4},{3,5},{4,2},{5,3},{6,0},{7,1},{8,14},{9,15},{10,... | collective-permute-start | bytes 98312 | tf_op jit(solution)/shard_map/root_solve/ppermute | solution.py:91
  89.2 4.3 %collective-permute-start.55 = (f32[128,128]{1,0:T(8,128)S(1)}, f32[128,128]{1,0:T(8,128)S(1)}, u32[]{:S(2)}, u32[]{:S(2)}) collective-permute-start(f32[128,128]{1,0:T(8,128)S(1)} %get-tuple-element.161.a), channel_id=1, source_target_pairs={{0,2},{1,3},{2,0},{3,1},{4,6},{5,7},{6,4},{7,5},{8,10},{9,11},{10,... | collective-permute-start | bytes 196616 | tf_op jit(solution)/shard_map/mid_upper/ppermute | solution.py:91
  94.8 4.3 %collective-permute-start.57 = (f32[128,128]{1,0:T(8,128)S(1)}, f32[128,128]{1,0:T(8,128)S(1)}, u32[]{:S(2)}, u32[]{:S(2)}) collective-permute-start(f32[128,128]{1,0:T(8,128)S(1)} %get-tuple-element.163.a), channel_id=1, source_target_pairs={{0,4},{1,5},{2,6},{3,7},{4,0},{5,1},{6,2},{7,3},{8,12},{9,13},{10,... | collective-permute-start | bytes 196616 | tf_op jit(solution)/shard_map/mid_upper/ppermute | solution.py:91
  100.7 5.0 %collective-permute-start.59 = (f32[128,128]{1,0:T(8,128)S(1)}, f32[128,128]{1,0:T(8,128)S(1)}, u32[]{:S(2)}, u32[]{:S(2)}) collective-permute-start(f32[128,128]{1,0:T(8,128)S(1)} %get-tuple-element.165.refs_0_), channel_id=1, source_target_pairs={{0,1},{1,0},{2,3},{3,2},{4,5},{5,4},{6,7},{7,6},{8,9},{9,8},{10,11... | collective-permute-start | bytes 196616 | tf_op jit(solution)/shard_map/mid_upper/ppermute | solution.py:91
  100.8 4.9 %collective-permute-start.60 = (f32[128,128]{1,0:T(8,128)S(1)}, f32[128,128]{1,0:T(8,128)S(1)}, u32[]{:S(2)}, u32[]{:S(2)}) collective-permute-start(f32[128,128]{1,0:T(8,128)S(1)} %get-tuple-element.166.refs_1_), channel_id=1, source_target_pairs={{0,1},{1,0},{2,3},{3,2},{4,5},{5,4},{6,7},{7,6},{8,9},{9,8},{10,11... | collective-permute-start | bytes 196616 | tf_op jit(solution)/shard_map/mid_upper/ppermute | solution.py:91
  101.3 7.9 %collective-permute-start.53 = (f32[64,128]{1,0:T(8,128)S(1)}, f32[64,128]{1,0:T(8,128)S(1)}, u32[]{:S(2)}, u32[]{:S(2)}) collective-permute-start(f32[64,128]{1,0:T(8,128)S(1)} %root_solve.7.quarter.refs_0_), channel_id=1, source_target_pairs={{0,24},{8,16},{16,8},{24,0},{1,25},{9,17},{17,9},{25,1},{2,26},{10... | collective-permute-start | bytes 98312 | tf_op jit(solution)/shard_map/mid_upper/ppermute | solution.py:91
  102.4 9.7 %collective-permute-start.52 = (f32[64,128]{1,0:T(8,128)S(1)}, f32[64,128]{1,0:T(8,128)S(1)}, u32[]{:S(2)}, u32[]{:S(2)}) collective-permute-start(f32[64,128]{1,0:T(8,128)S(1)} %root_solve.7.quarter.refs_0_), channel_id=1, source_target_pairs={{0,16},{8,24},{16,0},{24,8},{1,17},{9,25},{17,1},{25,9},{2,18},{10... | collective-permute-start | bytes 98312 | tf_op jit(solution)/shard_map/mid_upper/ppermute | solution.py:91
  102.4 9.7 %collective-permute-start.51 = (f32[64,128]{1,0:T(8,128)S(1)}, f32[64,128]{1,0:T(8,128)S(1)}, u32[]{:S(2)}, u32[]{:S(2)}) collective-permute-start(f32[64,128]{1,0:T(8,128)S(1)} %root_solve.7.quarter.refs_0_), channel_id=1, source_target_pairs={{0,8},{8,0},{16,24},{24,16},{1,9},{9,1},{17,25},{25,17},{2,10},{10... | collective-permute-start | bytes 98312 | tf_op jit(solution)/shard_map/mid_upper/ppermute | solution.py:91
  107.6 5.9 %collective-permute-start.63 = (f32[64,128]{1,0:T(8,128)S(1)}, f32[64,128]{1,0:T(8,128)S(1)}, u32[]{:S(2)}, u32[]{:S(2)}) collective-permute-start(f32[64,128]{1,0:T(8,128)S(1)} %mid_upper.11.refs_0_), channel_id=1, source_target_pairs={{0,24},{8,16},{16,8},{24,0},{1,25},{9,17},{17,9},{25,1},{2,26},{10... | collective-permute-start | bytes 98312 | tf_op jit(solution)/shard_map/leaf_upper/ppermute | solution.py:91
  108.9 5.4 %collective-permute-start.62 = (f32[64,128]{1,0:T(8,128)S(1)}, f32[64,128]{1,0:T(8,128)S(1)}, u32[]{:S(2)}, u32[]{:S(2)}) collective-permute-start(f32[64,128]{1,0:T(8,128)S(1)} %mid_upper.11.refs_0_), channel_id=1, source_target_pairs={{0,16},{8,24},{16,0},{24,8},{1,17},{9,25},{17,1},{25,9},{2,18},{10... | collective-permute-start | bytes 98312 | tf_op jit(solution)/shard_map/leaf_upper/ppermute | solution.py:91
  109.2 5.1 %collective-permute-start.61 = (f32[64,128]{1,0:T(8,128)S(1)}, f32[64,128]{1,0:T(8,128)S(1)}, u32[]{:S(2)}, u32[]{:S(2)}) collective-permute-start(f32[64,128]{1,0:T(8,128)S(1)} %mid_upper.11.refs_0_), channel_id=1, source_target_pairs={{0,8},{8,0},{16,24},{24,16},{1,9},{9,1},{17,25},{25,17},{2,10},{10... | collective-permute-start | bytes 98312 | tf_op jit(solution)/shard_map/leaf_upper/ppermute | solution.py:91
  116.3 4.3 %collective-permute-start.65 = (f32[128,128]{1,0:T(8,128)S(1)}, f32[128,128]{1,0:T(8,128)S(1)}, u32[]{:S(2)}, u32[]{:S(2)}) collective-permute-start(f32[128,128]{1,0:T(8,128)S(1)} %get-tuple-element.169.a), channel_id=1, source_target_pairs={{0,2},{1,3},{2,0},{3,1},{4,6},{5,7},{6,4},{7,5},{8,10},{9,11},{10,... | collective-permute-start | bytes 196616 | tf_op jit(solution)/shard_map/leaf_upper/ppermute | solution.py:91
  121.5 4.3 %collective-permute-start.67 = (f32[128,128]{1,0:T(8,128)S(1)}, f32[128,128]{1,0:T(8,128)S(1)}, u32[]{:S(2)}, u32[]{:S(2)}) collective-permute-start(f32[128,128]{1,0:T(8,128)S(1)} %get-tuple-element.171.a), channel_id=1, source_target_pairs={{0,4},{1,5},{2,6},{3,7},{4,0},{5,1},{6,2},{7,3},{8,12},{9,13},{10,... | collective-permute-start | bytes 196616 | tf_op jit(solution)/shard_map/leaf_upper/ppermute | solution.py:91
  (39 other events, 110.7 us)

commit v5 on v3

--- a/solution.py
+++ b/solution.py
@@ -8,6 +8,7 @@
 from jax.sharding import PartitionSpec as P
 
 CAP = 2
+CHUNKS = 4
 LANES = 128
 COLS = 32
 F32 = jnp.float32
@@ -70,7 +71,7 @@
 
 def assemble(where, parts, here, width=LANES):
     rows = parts[0].shape[0] * (LANES // width)
-    for k, part in enumerate(parts):
+    for k, part in zip(origins(len(parts)), parts):
         start = pl.multiple_of((here ^ k) * rows, 8)
         where[pl.ds(start, rows), :] = part[...] if width == LANES else unpack(part[...], width)
 
@@ -89,14 +90,21 @@
     return lax.ppermute(x, axis, [(i, i ^ k) for i in range(size)])
 
 
-def gather_front(x):
+def gather_front(x, meanwhile=None):
     fronts = lax.axis_size("front")
     mine = [x] + [swap("front", x, k) for k in range(2, fronts, 2)]
-    other = [swap("front", y, 1) for y in mine]
-    return [block for pair in zip(mine, other) for block in pair]
-
-
-def kernel(fn, outs, *args, scratch=(), vmem=8, work=0, hbm=()):
+    extra = tuple(meanwhile(x)) if meanwhile else ()
+    other = [swap("front", after(y, *extra) if i == 1 and extra else y, 1) for i, y in enumerate(mine)]
+    pairs = list(zip(mine, other))
+    return [block for pair in pairs[:1] + pairs[:0:-1] for block in pair], extra
+
+
+def origins(count):
+    evens = [0, *range(count - 2, 0, -2)]
+    return [e + core for e in evens for core in range(2)]
+
+
+def kernel(fn, outs, *args, scratch=(), vmem=8, work=0, hbm=(), pinned=()):
     outs = [o if isinstance(o[0], tuple) else (o, F32) for o in outs]
     return pl.pallas_call(
         fn,
@@ -106,7 +114,7 @@
         scratch_shapes=list(scratch),
         compiler_params=pltpu.CompilerParams(vmem_limit_bytes=vmem * 2**20),
         cost_estimate=pl.CostEstimate(flops=work, bytes_accessed=work // 700, transcendentals=0),
-    )(*args)
+    )(*(pltpu.with_memory_space_constraint(a, pltpu.HBM) if i in pinned else a for i, a in enumerate(args)))
 
 
 def load_matrices(picks, *refs):
@@ -121,11 +129,11 @@
     copies = []
     for i, (src, pick) in enumerate(zip(sources, picks)):
         rows = buffers[i].shape[1]
-        step = rows // 2 if rows >= 128 else rows
+        step = max(rows // CHUNKS, 16)
         for n, at in enumerate(range(0, rows, step)):
             span = pl.ds(at, step)
             view = src.at[:, span, :] if pick is None else src.at[:, parent if pick == "own" else 0, span, :]
-            copy = pltpu.make_async_copy(view, buffers[i].at[:, span, :], sems.at[2 * i + n])
+            copy = pltpu.make_async_copy(view, buffers[i].at[:, span, :], sems.at[CHUNKS * i + n])
             copy.start()
             copies.append((i, at, step, copy))
     for i, at, step, copy in copies:
@@ -137,7 +145,7 @@
             outs[i][rows + at : rows + at + step, part * depth : part * depth + depth] = low
 
 
-def load(*matrices):
+def load(*matrices, pinned=False):
     shapes = [m.shape[-2:] for m, _ in matrices]
     size = sum(r * d for r, d in shapes)
     return kernel(
@@ -145,8 +153,9 @@
         [((2 * r, 2 * d), BF16) for r, d in shapes],
         *[m for m, _ in matrices],
         scratch=[pltpu.VMEM((2, r, d), F32) for r, d in shapes]
-        + [pltpu.SemaphoreType.DMA((2 * len(shapes),))],
+        + [pltpu.SemaphoreType.DMA((CHUNKS * len(shapes),))],
         hbm=range(len(shapes)),
+        pinned=range(len(shapes)) if pinned else (),
         vmem=4 + -(-size * 8 // 2**20),
         work=size * 1000,
     )
@@ -249,9 +258,9 @@
     taken = (lane // COLS) % 2 == 1
     own = lax.broadcasted_iota(jnp.int32, (rows, LANES), 1)
     own = (own // COLS) % 2 == 0
-    for k in range(fronts):
+    for k, message in zip(origins(fronts), messages):
         start = pl.multiple_of((here ^ k) * rows, 8)
-        rhs[pl.ds(start, rows), :] = jnp.where(own, messages[k][0:rows, :], 0.0)
+        rhs[pl.ds(start, rows), :] = jnp.where(own, message[0:rows, :], 0.0)
     group = max(1, 512 // slots)
     for k in range(0, fronts, group):
         chosen = messages[k : k + group]
@@ -434,6 +443,7 @@
                 dma((3,)),
             ],
             hbm=range(3),
+            pinned=range(3),
         )
         arrived = [payload[0]] + [swap("leaf", payload[k], k) for k in range(1, groups)]
         leaf_own, mid_own, root_own = kernel(
@@ -449,51 +459,55 @@
                 dma((3,)),
             ],
             hbm=range(3),
-        )
-        ll, l2m = load((after(leaf_lower_inv, leaf_own), "leaf"), (leaf_to_mid_lower, "leaf"))
+            pinned=range(3),
+        )
         (message,) = kernel(
-            pack_leaf, [(sum(message_rows(n0, groups * slots)), LANES)], after(leaf_own, ll), *arrived
+            pack_leaf, [(sum(message_rows(n0, groups * slots)), LANES)], leaf_own, *arrived
         )
     with jax.named_scope("leaf_lower"):
-        messages = gather_front(message)
-        ml, m2r = load((after(mid_lower_inv, message), "own"), (mid_to_root_lower, "own"))
+        messages, (ll, l2m) = gather_front(
+            message,
+            lambda x: load((after(leaf_lower_inv, x), "leaf"), (leaf_to_mid_lower, "leaf"), pinned=True),
+        )
         (y_leaf,) = kernel(
             functools.partial(leaf_lower, groups * slots),
             [(n0, LANES)],
-            after(ll, ml),
+            ll,
             *messages,
             scratch=[pltpu.VMEM((s0, LANES), F32)],
         )
     with jax.named_scope("mid_lower"):
-        parts = gather_front(y_leaf)
-        (l2r,) = load((after(leaf_to_root_lower, y_leaf), "leaf"))
+        parts, (l2r, ml) = gather_front(
+            y_leaf,
+            lambda x: load((after(leaf_to_root_lower, x), "leaf"), (mid_lower_inv, "own"), pinned=True),
+        )
         keep, send, y_full = kernel(
             leaf_to_mid,
             [(n1 // 2, LANES), (n1 // 2, LANES), (s0, LANES)],
-            after(l2m, l2r),
+            l2m,
             mid_own,
             *parts,
         )
         came = swap("leaf", send, 1)
         root_kept, root_sent = kernel(leaf_to_root, [(n2, 2 * COLS)] * 2, l2r, after(y_full, send))
         (cut_mid,) = kernel(add, [(n1 // 2, LANES)], after(keep, root_kept), came)
-        parts = gather_front(cut_mid)
+        parts, (m2r,) = gather_front(
+            cut_mid, lambda x: load((after(mid_to_root_lower, x), "own"), pinned=True)
+        )
         root_came = swap("leaf", root_sent, 1)
-        (rl,) = load((after(root_lower_inv, cut_mid), None))
         (y_mid,) = kernel(
             mid_lower,
             [(n1 // 2, LANES)],
-            after(ml, rl),
+            ml,
             *parts,
             scratch=[pltpu.VMEM((s1, 2 * COLS), F32)],
         )
     with jax.named_scope("root_cut"):
-        parts = gather_front(y_mid)
-        (ru,) = load((after(root_upper_inv, y_mid), None))
+        parts, (rl,) = gather_front(y_mid, lambda x: load((after(root_lower_inv, x), None)))
         keep, send, y_mid_full = kernel(
             mid_to_root,
             [(n2 // 4, LANES), (n2 // 4, LANES), (s1, 2 * COLS)],
-            after(m2r, ru),
+            m2r,
             root_kept,
             root_came,
             root_own,
@@ -503,21 +517,24 @@
         mu, l2r_up = load((after(mid_upper_inv, send), "own"), (leaf_to_root_upper, "leaf"))
         (cut_root,) = kernel(add, [(n2 // 4, LANES)], after(keep, mu), came)
     with jax.named_scope("root_solve"):
-        parts = gather_front(cut_root)
-        (m2r_up,) = load((after(mid_to_root_upper, cut_root), "own"))
+        parts, (ru,) = gather_front(cut_root, lambda x: load((after(root_upper_inv, x), None)))
         (y_root,) = kernel(
             root_rows,
             [(n2 // 4, LANES)],
-            after(rl, m2r_up),
+            rl,
             *parts,
             scratch=[pltpu.VMEM((s2, COLS), F32)],
         )
-        parts = gather_front(y_root)
-        l2m_up, lu = load((after(leaf_to_mid_upper, y_root), "leaf"), (leaf_upper_inv, "leaf"))
+        parts, (m2r_up, l2m_up, lu) = gather_front(
+            y_root,
+            lambda x: load(
+                (after(mid_to_root_upper, x), "own"), (leaf_to_mid_upper, "leaf"), (leaf_upper_inv, "leaf")
+            ),
+        )
         (x_root,) = kernel(
             root_rows,
             [(n2 // 4, LANES)],
-            after(ru, lu),
+            ru,
             *parts,
             scratch=[pltpu.VMEM((s2, COLS), F32)],
         )

time: 124 us -> 122 us (0.984)
  local copies, waits for them, and re-layouts: 10.4 us -> 0.04 us
  waiting for transfers between devices: 46.9 us -> 53 us
  Pallas kernels: 18.8 us -> 24.6 us
  starting transfers between devices: 46 us -> 43.2 us
    unnamed x36 -> x14, local copies, waits for them, and re-layouts: 10.4 us -> 0.04 us
    ppermute x66, waiting for transfers between devices: 46.9 us -> 53 us  [swap(): return lax.ppermute(x, axis, [(i, i ^ k) for i in range(size)])]
    pallas_call x32 -> x31, Pallas kernels: 18.8 us -> 24.6 us  [kernel(): pl.pallas_call(fn, out_shape=[jax.ShapeDtypeStruct(*o) for o in outs], in...]
    ppermute x66, starting transfers between devices: 46 us -> 43.2 us  [swap(): return lax.ppermute(x, axis, [(i, i ^ k) for i in range(size)])]
  transfers between devices with their start and end apart: 66 -> 66, of which waited for: 44 -> 44; matrix products, arithmetic and copies ran while one was open for 0% -> 0% of each run, Pallas kernels for 7% -> 12%
where the time goes in v5:
time: 122 us
  waiting for transfers between devices  53 us (43%)
  starting transfers between devices  43.2 us (35%)
  Pallas kernels  24.6 us (20%)
    ppermute x66, waiting for transfers between devices, swap(): return lax.ppermute(x, axis, [(i, i ^ k) for i in range(size)])  53 us
    ppermute x66, starting transfers between devices, swap(): return lax.ppermute(x, axis, [(i, i ^ k) for i in range(size)])  43.2 us
    pallas_call x31, Pallas kernels, kernel(): pl.pallas_call(fn, out_shape=[jax.ShapeDtypeStruct(*o) for o in outs], in...  24.6 us
  transfers between devices with their start and end apart: 66, of which 44 were waited for; matrix products, arithmetic and copies ran while one was open for 0% of the time, Pallas kernels for 12%

profile of v5, /device:TPU:0, one launch (start us, length us, event | category | flops | bytes accessed | tf_op | source)
XLA Modules:
  0.0 121.9 jit_solution(1762119333787117439)
XLA Ops:
  1.7 3.1 %collective-permute-start = (f32[16,128]{1,0:T(8,128)S(1)}, f32[16,128]{1,0:T(8,128)S(1)}, u32[]{:S(2)}, u32[]{:S(2)}) collective-permute-start(f32[16,128]{1,0:T(8,128)S(1)} %get-tuple-element.75), channel_id=1, source_target_pairs={{0,8},{8,0},{16,24},{24,16},{1,9},{9,1},{17,25},{25,17},{2,10},{10... | collective-permute-start | bytes 24584 | tf_op jit(solution)/shard_map/right_hand_sides/ppermute | solution.py:90
  4.8 2.6 %collective-permute-start.1 = (f32[16,128]{1,0:T(8,128)S(1)}, f32[16,128]{1,0:T(8,128)S(1)}, u32[]{:S(2)}, u32[]{:S(2)}) collective-permute-start(f32[16,128]{1,0:T(8,128)S(1)} %get-tuple-element.76), channel_id=1, source_target_pairs={{0,16},{8,24},{16,0},{24,8},{1,17},{9,25},{17,1},{25,9},{2,18},{10... | collective-permute-start | bytes 24584 | tf_op jit(solution)/shard_map/right_hand_sides/ppermute | solution.py:90
  9.4 3.5 %collective-permute-done.2.refs_3_ = f32[16,128]{1,0:T(8,128)S(1)} collective-permute-done((f32[16,128]{1,0:T(8,128)S(1)}, f32[16,128]{1,0:T(8,128)S(1)}, u32[]{:S(2)}, u32[]{:S(2)}) %collective-permute-start.2) | collective-permute-done | bytes 8224 | tf_op jit(solution)/shard_map/right_hand_sides/ppermute | solution.py:90
  12.9 1.6 %collective-permute-start.8 = (f32[72,128]{1,0:T(8,128)S(1)}, f32[72,128]{1,0:T(8,128)S(1)}, u32[]{:S(2)}, u32[]{:S(2)}) collective-permute-start(f32[72,128]{1,0:T(8,128)S(1)} %right_hand_sides.5.refs_0_), channel_id=1, source_target_pairs={{0,2},{1,3},{2,0},{3,1},{4,6},{5,7},{6,4},{7,5},{8,10},{9,11},{10,... | collective-permute-start | bytes 110600 | tf_op jit(solution)/shard_map/leaf_lower/ppermute | solution.py:90
  14.5 1.5 %collective-permute-start.6 = (f32[72,128]{1,0:T(8,128)S(1)}, f32[72,128]{1,0:T(8,128)S(1)}, u32[]{:S(2)}, u32[]{:S(2)}) collective-permute-start(f32[72,128]{1,0:T(8,128)S(1)} %right_hand_sides.5.refs_0_), channel_id=1, source_target_pairs={{0,4},{1,5},{2,6},{3,7},{4,0},{5,1},{6,2},{7,3},{8,12},{9,13},{10,... | collective-permute-start | bytes 110600 | tf_op jit(solution)/shard_map/leaf_lower/ppermute | solution.py:90
  18.5 2.4 %collective-permute-done.4.refs_2_ = f32[72,128]{1,0:T(8,128)S(1)} collective-permute-done((f32[72,128]{1,0:T(8,128)S(1)}, f32[72,128]{1,0:T(8,128)S(1)}, u32[]{:S(2)}, u32[]{:S(2)}) %collective-permute-start.4) | collective-permute-done | bytes 36896 | tf_op jit(solution)/shard_map/leaf_lower/ppermute | solution.py:90
  24.0 2.4 %collective-permute-start.11 = (f32[64,128]{1,0:T(8,128)S(1)}, f32[64,128]{1,0:T(8,128)S(1)}, u32[]{:S(2)}, u32[]{:S(2)}) collective-permute-start(f32[64,128]{1,0:T(8,128)S(1)} %leaf_lower.3.refs_0_), channel_id=1, source_target_pairs={{0,6},{1,7},{2,4},{3,5},{4,2},{5,3},{6,0},{7,1},{8,14},{9,15},{10,... | collective-permute-start | bytes 98312 | tf_op jit(solution)/shard_map/mid_lower/ppermute | solution.py:90
  26.5 1.6 %mid_lower.6 = (bf16[512,1024]{1,0:T(8,128)(2,1)S(1)}, bf16[256,2048]{1,0:T(8,128)(2,1)S(1)}) custom-call(f32[2,1,256,512]{3,2,1,0:T(8,128)} %refs_0_.1, f32[2,2,128,1024]{3,2,1,0:T(8,128)} %refs_1_.5), custom_call_target="tpu_custom_call" | custom-call | flops 262144000 | bytes 374491 | tf_op jit(solution)/shard_map/mid_lower/pallas_call | solution.py:109
  31.5 3.3 %collective-permute-done.17.refs_1_ = f32[64,128]{1,0:T(8,128)S(1)} collective-permute-done((f32[64,128]{1,0:T(8,128)S(1)}, f32[64,128]{1,0:T(8,128)S(1)}, u32[]{:S(2)}, u32[]{:S(2)}) %collective-permute-start.17) | collective-permute-done | bytes 32800 | tf_op jit(solution)/shard_map/mid_lower/ppermute | solution.py:90
  34.7 1.5 %collective-permute-start.23 = (f32[64,128]{1,0:T(8,128)S(1)}, f32[64,128]{1,0:T(8,128)S(1)}, u32[]{:S(2)}, u32[]{:S(2)}) collective-permute-start(f32[64,128]{1,0:T(8,128)S(1)} %mid_lower.9.refs_0_), channel_id=1, source_target_pairs={{0,2},{1,3},{2,0},{3,1},{4,6},{5,7},{6,4},{7,5},{8,10},{9,11},{10,... | collective-permute-start | bytes 98312 | tf_op jit(solution)/shard_map/mid_lower/ppermute | solution.py:90
  36.2 1.5 %collective-permute-start.21 = (f32[64,128]{1,0:T(8,128)S(1)}, f32[64,128]{1,0:T(8,128)S(1)}, u32[]{:S(2)}, u32[]{:S(2)}) collective-permute-start(f32[64,128]{1,0:T(8,128)S(1)} %mid_lower.9.refs_0_), channel_id=1, source_target_pairs={{0,4},{1,5},{2,6},{3,7},{4,0},{5,1},{6,2},{7,3},{8,12},{9,13},{10,... | collective-permute-start | bytes 98312 | tf_op jit(solution)/shard_map/mid_lower/ppermute | solution.py:90
  38.2 1.6 %mid_lower.10.matrix = bf16[512,2048]{1,0:T(8,128)(2,1)S(1)} custom-call(f32[2,2,256,1024]{3,2,1,0:T(8,128)} %refs_0_.2), custom_call_target="tpu_custom_call" | custom-call | flops 262144000 | bytes 374491 | tf_op jit(solution)/shard_map/mid_lower/pallas_call | solution.py:109
  40.5 2.1 %collective-permute-done.19.refs_2_ = f32[64,128]{1,0:T(8,128)S(1)} collective-permute-done((f32[64,128]{1,0:T(8,128)S(1)}, f32[64,128]{1,0:T(8,128)S(1)}, u32[]{:S(2)}, u32[]{:S(2)}) %collective-permute-start.19) | collective-permute-done | bytes 32800 | tf_op jit(solution)/shard_map/mid_lower/ppermute | solution.py:90
  46.1 2.5 %collective-permute-start.27 = (f32[64,128]{1,0:T(8,128)S(1)}, f32[64,128]{1,0:T(8,128)S(1)}, u32[]{:S(2)}, u32[]{:S(2)}) collective-permute-start(f32[64,128]{1,0:T(8,128)S(1)} %mid_lower.11.refs_0_), channel_id=1, source_target_pairs={{0,6},{1,7},{2,4},{3,5},{4,2},{5,3},{6,0},{7,1},{8,14},{9,15},{10,... | collective-permute-start | bytes 98312 | tf_op jit(solution)/shard_map/root_cut/ppermute | solution.py:90
  54.2 5.0 %collective-permute-done.33.refs_1_ = f32[64,128]{1,0:T(8,128)S(1)} collective-permute-done((f32[64,128]{1,0:T(8,128)S(1)}, f32[64,128]{1,0:T(8,128)S(1)}, u32[]{:S(2)}, u32[]{:S(2)}) %collective-permute-start.33) | collective-permute-done | bytes 32800 | tf_op jit(solution)/shard_map/root_cut/ppermute | solution.py:90
  59.2 1.5 %collective-permute-start.39 = (f32[64,128]{1,0:T(8,128)S(1)}, f32[64,128]{1,0:T(8,128)S(1)}, u32[]{:S(2)}, u32[]{:S(2)}) collective-permute-start(f32[64,128]{1,0:T(8,128)S(1)} %root_cut.7.refs_0_), channel_id=1, source_target_pairs={{0,2},{1,3},{2,0},{3,1},{4,6},{5,7},{6,4},{7,5},{8,10},{9,11},{10,... | collective-permute-start | bytes 98312 | tf_op jit(solution)/shard_map/root_solve/ppermute | solution.py:90
  60.7 1.5 %collective-permute-start.37 = (f32[64,128]{1,0:T(8,128)S(1)}, f32[64,128]{1,0:T(8,128)S(1)}, u32[]{:S(2)}, u32[]{:S(2)}) collective-permute-start(f32[64,128]{1,0:T(8,128)S(1)} %root_cut.7.refs_0_), channel_id=1, source_target_pairs={{0,4},{1,5},{2,6},{3,7},{4,0},{5,1},{6,2},{7,3},{8,12},{9,13},{10,... | collective-permute-start | bytes 98312 | tf_op jit(solution)/shard_map/root_solve/ppermute | solution.py:90
  64.6 2.4 %collective-permute-done.35.refs_2_ = f32[64,128]{1,0:T(8,128)S(1)} collective-permute-done((f32[64,128]{1,0:T(8,128)S(1)}, f32[64,128]{1,0:T(8,128)S(1)}, u32[]{:S(2)}, u32[]{:S(2)}) %collective-permute-start.35) | collective-permute-done | bytes 32800 | tf_op jit(solution)/shard_map/root_solve/ppermute | solution.py:90
  68.4 1.9 %root_solve.5.refs_0_ = f32[64,128]{1,0:T(8,128)S(1)} custom-call(bf16[512,4096]{1,0:T(8,128)(2,1)S(1)} %root_cut.4.matrix, f32[64,128]{1,0:T(8,128)S(1)} %root_cut.7.refs_0_, f32[64,128]{1,0:T(8,128)S(1)} %collective-permute-done.34.refs_1_, f32[64,128]{1,0:T(8,128)S(1)} %collective-permute-done.35.refs_2_, f32[64,128]{1,0:T(8,128)S(1)} %collective-permute-done.36.refs_3_, ...), custom_call_target="tpu_custom_call" | custom-call | tf_op jit(solution)/shard_map/root_solve/pallas_call | solution.py:109
  71.3 2.5 %collective-permute-start.42 = (f32[64,128]{1,0:T(8,128)S(1)}, f32[64,128]{1,0:T(8,128)S(1)}, u32[]{:S(2)}, u32[]{:S(2)}) collective-permute-start(f32[64,128]{1,0:T(8,128)S(1)} %root_solve.5.refs_0_), channel_id=1, source_target_pairs={{0,6},{1,7},{2,4},{3,5},{4,2},{5,3},{6,0},{7,1},{8,14},{9,15},{10,... | collective-permute-start | bytes 98312 | tf_op jit(solution)/shard_map/root_solve/ppermute | solution.py:90
  77.5 1.9 %root_solve.7.mine = f32[64,128]{1,0:T(8,128)S(1)} custom-call(bf16[512,4096]{1,0:T(8,128)(2,1)S(1)} %root_solve.4.matrix, f32[64,128]{1,0:T(8,128)S(1)} %root_solve.5.refs_0_, f32[64,128]{1,0:T(8,128)S(1)} %collective-permute-done.41.refs_1_, f32[64,128]{1,0:T(8,128)S(1)} %collective-permute-done.42.refs_2_, f32[64,128]{1,0:T(8,128)S(1)} %collective-permute-done.43.refs_3_, ...), custom_call_target="tpu_custom_call" | custom-call | tf_op jit(solution)/shard_map/root_solve/pallas_call | solution.py:109
  79.5 5.2 %collective-permute-done.48.other = f32[64,128]{1,0:T(8,128)S(1)} collective-permute-done((f32[64,128]{1,0:T(8,128)S(1)}, f32[64,128]{1,0:T(8,128)S(1)}, u32[]{:S(2)}, u32[]{:S(2)}) %collective-permute-start.48) | collective-permute-done | bytes 32800 | tf_op jit(solution)/shard_map/mid_upper/ppermute | solution.py:90
  87.2 1.6 %collective-permute-start.51 = (f32[128,128]{1,0:T(8,128)S(1)}, f32[128,128]{1,0:T(8,128)S(1)}, u32[]{:S(2)}, u32[]{:S(2)}) collective-permute-start(f32[128,128]{1,0:T(8,128)S(1)} %get-tuple-element.120.a), channel_id=1, source_target_pairs={{0,2},{1,3},{2,0},{3,1},{4,6},{5,7},{6,4},{7,5},{8,10},{9,11},{10,... | collective-permute-start | bytes 196616 | tf_op jit(solution)/shard_map/mid_upper/ppermute | solution.py:90
  88.7 1.5 %collective-permute-start.52 = (f32[128,128]{1,0:T(8,128)S(1)}, f32[128,128]{1,0:T(8,128)S(1)}, u32[]{:S(2)}, u32[]{:S(2)}) collective-permute-start(f32[128,128]{1,0:T(8,128)S(1)} %get-tuple-element.121.c), channel_id=1, source_target_pairs={{0,4},{1,5},{2,6},{3,7},{4,0},{5,1},{6,2},{7,3},{8,12},{9,13},{10,... | collective-permute-start | bytes 196616 | tf_op jit(solution)/shard_map/mid_upper/ppermute | solution.py:90
  91.5 1.5 %collective-permute-done.52.d = f32[128,128]{1,0:T(8,128)S(1)} collective-permute-done((f32[128,128]{1,0:T(8,128)S(1)}, f32[128,128]{1,0:T(8,128)S(1)}, u32[]{:S(2)}, u32[]{:S(2)}) %collective-permute-start.52) | collective-permute-done | bytes 65568 | tf_op jit(solution)/shard_map/mid_upper/ppermute | solution.py:90
  93.0 1.6 %collective-permute-start.53 = (f32[128,128]{1,0:T(8,128)S(1)}, f32[128,128]{1,0:T(8,128)S(1)}, u32[]{:S(2)}, u32[]{:S(2)}) collective-permute-start(f32[128,128]{1,0:T(8,128)S(1)} %get-tuple-element.122.a), channel_id=1, source_target_pairs={{0,4},{1,5},{2,6},{3,7},{4,0},{5,1},{6,2},{7,3},{8,12},{9,13},{10,... | collective-permute-start | bytes 196616 | tf_op jit(solution)/shard_map/mid_upper/ppermute | solution.py:90
  95.1 2.2 %collective-permute-done.53.b = f32[128,128]{1,0:T(8,128)S(1)} collective-permute-done((f32[128,128]{1,0:T(8,128)S(1)}, f32[128,128]{1,0:T(8,128)S(1)}, u32[]{:S(2)}, u32[]{:S(2)}) %collective-permute-start.53) | collective-permute-done | bytes 65568 | tf_op jit(solution)/shard_map/mid_upper/ppermute | solution.py:90
  97.3 1.5 %collective-permute-done.54.d = f32[128,128]{1,0:T(8,128)S(1)} collective-permute-done((f32[128,128]{1,0:T(8,128)S(1)}, f32[128,128]{1,0:T(8,128)S(1)}, u32[]{:S(2)}, u32[]{:S(2)}) %collective-permute-start.54) | collective-permute-done | bytes 65568 | tf_op jit(solution)/shard_map/mid_upper/ppermute | solution.py:90
  108.4 3.2 %collective-permute-done.59.b = f32[128,128]{1,0:T(8,128)S(1)} collective-permute-done((f32[128,128]{1,0:T(8,128)S(1)}, f32[128,128]{1,0:T(8,128)S(1)}, u32[]{:S(2)}, u32[]{:S(2)}) %collective-permute-start.59) | collective-permute-done | bytes 65568 | tf_op jit(solution)/shard_map/leaf_upper/ppermute | solution.py:90
  112.8 1.5 %collective-permute-start.62 = (f32[128,128]{1,0:T(8,128)S(1)}, f32[128,128]{1,0:T(8,128)S(1)}, u32[]{:S(2)}, u32[]{:S(2)}) collective-permute-start(f32[128,128]{1,0:T(8,128)S(1)} %get-tuple-element.131.c), channel_id=1, source_target_pairs={{0,2},{1,3},{2,0},{3,1},{4,6},{5,7},{6,4},{7,5},{8,10},{9,11},{10,... | collective-permute-start | bytes 196616 | tf_op jit(solution)/shard_map/leaf_upper/ppermute | solution.py:90
  114.8 1.7 %collective-permute-done.61.b = f32[128,128]{1,0:T(8,128)S(1)} collective-permute-done((f32[128,128]{1,0:T(8,128)S(1)}, f32[128,128]{1,0:T(8,128)S(1)}, u32[]{:S(2)}, u32[]{:S(2)}) %collective-permute-start.61) | collective-permute-done | bytes 65568 | tf_op jit(solution)/shard_map/leaf_upper/ppermute | solution.py:90
  117.6 2.5 %collective-permute-done.65.other = f32[128,128]{1,0:T(8,128)S(1)} collective-permute-done((f32[128,128]{1,0:T(8,128)S(1)}, f32[128,128]{1,0:T(8,128)S(1)}, u32[]{:S(2)}, u32[]{:S(2)}) %collective-permute-start.65) | collective-permute-done | bytes 65568 | tf_op jit(solution)/shard_map/leaf_upper/ppermute | solution.py:90
  (145 shorter events, 49.3 us)
Async XLA Ops:
  1.7 6.8 %collective-permute-start = (f32[16,128]{1,0:T(8,128)S(1)}, f32[16,128]{1,0:T(8,128)S(1)}, u32[]{:S(2)}, u32[]{:S(2)}) collective-permute-start(f32[16,128]{1,0:T(8,128)S(1)} %get-tuple-element.75), channel_id=1, source_target_pairs={{0,8},{8,0},{16,24},{24,16},{1,9},{9,1},{17,25},{25,17},{2,10},{10... | collective-permute-start | bytes 24584 | tf_op jit(solution)/shard_map/right_hand_sides/ppermute | solution.py:90
  4.8 4.5 %collective-permute-start.1 = (f32[16,128]{1,0:T(8,128)S(1)}, f32[16,128]{1,0:T(8,128)S(1)}, u32[]{:S(2)}, u32[]{:S(2)}) collective-permute-start(f32[16,128]{1,0:T(8,128)S(1)} %get-tuple-element.76), channel_id=1, source_target_pairs={{0,16},{8,24},{16,0},{24,8},{1,17},{9,25},{17,1},{25,9},{2,18},{10... | collective-permute-start | bytes 24584 | tf_op jit(solution)/shard_map/right_hand_sides/ppermute | solution.py:90
  7.4 5.4 %collective-permute-start.2 = (f32[16,128]{1,0:T(8,128)S(1)}, f32[16,128]{1,0:T(8,128)S(1)}, u32[]{:S(2)}, u32[]{:S(2)}) collective-permute-start(f32[16,128]{1,0:T(8,128)S(1)} %get-tuple-element.77), channel_id=1, source_target_pairs={{0,24},{8,16},{16,8},{24,0},{1,25},{9,17},{17,9},{25,1},{2,26},{10... | collective-permute-start | bytes 24584 | tf_op jit(solution)/shard_map/right_hand_sides/ppermute | solution.py:90
  12.9 4.9 %collective-permute-start.8 = (f32[72,128]{1,0:T(8,128)S(1)}, f32[72,128]{1,0:T(8,128)S(1)}, u32[]{:S(2)}, u32[]{:S(2)}) collective-permute-start(f32[72,128]{1,0:T(8,128)S(1)} %right_hand_sides.5.refs_0_), channel_id=1, source_target_pairs={{0,2},{1,3},{2,0},{3,1},{4,6},{5,7},{6,4},{7,5},{8,10},{9,11},{10,... | collective-permute-start | bytes 110600 | tf_op jit(solution)/shard_map/leaf_lower/ppermute | solution.py:90
  16.0 4.9 %collective-permute-start.4 = (f32[72,128]{1,0:T(8,128)S(1)}, f32[72,128]{1,0:T(8,128)S(1)}, u32[]{:S(2)}, u32[]{:S(2)}) collective-permute-start(f32[72,128]{1,0:T(8,128)S(1)} %right_hand_sides.5.refs_0_), channel_id=1, source_target_pairs={{0,6},{1,7},{2,4},{3,5},{4,2},{5,3},{6,0},{7,1},{8,14},{9,15},{10,... | collective-permute-start | bytes 110600 | tf_op jit(solution)/shard_map/leaf_lower/ppermute | solution.py:90
  16.5 4.9 %collective-permute-start.3 = (f32[72,128]{1,0:T(8,128)S(1)}, f32[72,128]{1,0:T(8,128)S(1)}, u32[]{:S(2)}, u32[]{:S(2)}) collective-permute-start(f32[72,128]{1,0:T(8,128)S(1)} %right_hand_sides.5.refs_0_), channel_id=1, source_target_pairs={{0,1},{1,0},{2,3},{3,2},{4,5},{5,4},{6,7},{7,6},{8,9},{9,8},{10,11... | collective-permute-start | bytes 110600 | tf_op jit(solution)/shard_map/leaf_lower/ppermute | solution.py:90
  22.9 5.2 %collective-permute-start.15 = (f32[64,128]{1,0:T(8,128)S(1)}, f32[64,128]{1,0:T(8,128)S(1)}, u32[]{:S(2)}, u32[]{:S(2)}) collective-permute-start(f32[64,128]{1,0:T(8,128)S(1)} %leaf_lower.3.refs_0_), channel_id=1, source_target_pairs={{0,2},{1,3},{2,0},{3,1},{4,6},{5,7},{6,4},{7,5},{8,10},{9,11},{10,... | collective-permute-start | bytes 98312 | tf_op jit(solution)/shard_map/mid_lower/ppermute | solution.py:90
  23.5 4.6 %collective-permute-start.13 = (f32[64,128]{1,0:T(8,128)S(1)}, f32[64,128]{1,0:T(8,128)S(1)}, u32[]{:S(2)}, u32[]{:S(2)}) collective-permute-start(f32[64,128]{1,0:T(8,128)S(1)} %leaf_lower.3.refs_0_), channel_id=1, source_target_pairs={{0,4},{1,5},{2,6},{3,7},{4,0},{5,1},{6,2},{7,3},{8,12},{9,13},{10,... | collective-permute-start | bytes 98312 | tf_op jit(solution)/shard_map/mid_lower/ppermute | solution.py:90
  24.0 4.8 %collective-permute-start.11 = (f32[64,128]{1,0:T(8,128)S(1)}, f32[64,128]{1,0:T(8,128)S(1)}, u32[]{:S(2)}, u32[]{:S(2)}) collective-permute-start(f32[64,128]{1,0:T(8,128)S(1)} %leaf_lower.3.refs_0_), channel_id=1, source_target_pairs={{0,6},{1,7},{2,4},{3,5},{4,2},{5,3},{6,0},{7,1},{8,14},{9,15},{10,... | collective-permute-start | bytes 98312 | tf_op jit(solution)/shard_map/mid_lower/ppermute | solution.py:90
  34.7 5.1 %collective-permute-start.23 = (f32[64,128]{1,0:T(8,128)S(1)}, f32[64,128]{1,0:T(8,128)S(1)}, u32[]{:S(2)}, u32[]{:S(2)}) collective-permute-start(f32[64,128]{1,0:T(8,128)S(1)} %mid_lower.9.refs_0_), channel_id=1, source_target_pairs={{0,2},{1,3},{2,0},{3,1},{4,6},{5,7},{6,4},{7,5},{8,10},{9,11},{10,... | collective-permute-start | bytes 98312 | tf_op jit(solution)/shard_map/mid_lower/ppermute | solution.py:90
  36.2 4.3 %collective-permute-start.21 = (f32[64,128]{1,0:T(8,128)S(1)}, f32[64,128]{1,0:T(8,128)S(1)}, u32[]{:S(2)}, u32[]{:S(2)}) collective-permute-start(f32[64,128]{1,0:T(8,128)S(1)} %mid_lower.9.refs_0_), channel_id=1, source_target_pairs={{0,4},{1,5},{2,6},{3,7},{4,0},{5,1},{6,2},{7,3},{8,12},{9,13},{10,... | collective-permute-start | bytes 98312 | tf_op jit(solution)/shard_map/mid_lower/ppermute | solution.py:90
  37.8 4.8 %collective-permute-start.19 = (f32[64,128]{1,0:T(8,128)S(1)}, f32[64,128]{1,0:T(8,128)S(1)}, u32[]{:S(2)}, u32[]{:S(2)}) collective-permute-start(f32[64,128]{1,0:T(8,128)S(1)} %mid_lower.9.refs_0_), channel_id=1, source_target_pairs={{0,6},{1,7},{2,4},{3,5},{4,2},{5,3},{6,0},{7,1},{8,14},{9,15},{10,... | collective-permute-start | bytes 98312 | tf_op jit(solution)/shard_map/mid_lower/ppermute | solution.py:90
  38.2 4.9 %collective-permute-start.18 = (f32[64,128]{1,0:T(8,128)S(1)}, f32[64,128]{1,0:T(8,128)S(1)}, u32[]{:S(2)}, u32[]{:S(2)}) collective-permute-start(f32[64,128]{1,0:T(8,128)S(1)} %mid_lower.9.refs_0_), channel_id=1, source_target_pairs={{0,1},{1,0},{2,3},{3,2},{4,5},{5,4},{6,7},{7,6},{8,9},{9,8},{10,11... | collective-permute-start | bytes 98312 | tf_op jit(solution)/shard_map/mid_lower/ppermute | solution.py:90
  43.1 8.4 %collective-permute-start.25 = (f32[256,64]{1,0:T(8,128)S(1)}, f32[256,64]{1,0:T(8,128)S(1)}, u32[]{:S(2)}, u32[]{:S(2)}) collective-permute-start(f32[256,64]{1,0:T(8,128)S(1)} %get-tuple-element.98), channel_id=1, source_target_pairs={{0,8},{8,0},{16,24},{24,16},{1,9},{9,1},{17,25},{25,17},{2,10},{10... | collective-permute-start | bytes 196616 | tf_op jit(solution)/shard_map/mid_lower/ppermute | solution.py:90
  45.0 4.7 %collective-permute-start.31 = (f32[64,128]{1,0:T(8,128)S(1)}, f32[64,128]{1,0:T(8,128)S(1)}, u32[]{:S(2)}, u32[]{:S(2)}) collective-permute-start(f32[64,128]{1,0:T(8,128)S(1)} %mid_lower.11.refs_0_), channel_id=1, source_target_pairs={{0,2},{1,3},{2,0},{3,1},{4,6},{5,7},{6,4},{7,5},{8,10},{9,11},{10,... | collective-permute-start | bytes 98312 | tf_op jit(solution)/shard_map/root_cut/ppermute | solution.py:90
  46.1 4.8 %collective-permute-start.27 = (f32[64,128]{1,0:T(8,128)S(1)}, f32[64,128]{1,0:T(8,128)S(1)}, u32[]{:S(2)}, u32[]{:S(2)}) collective-permute-start(f32[64,128]{1,0:T(8,128)S(1)} %mid_lower.11.refs_0_), channel_id=1, source_target_pairs={{0,6},{1,7},{2,4},{3,5},{4,2},{5,3},{6,0},{7,1},{8,14},{9,15},{10,... | collective-permute-start | bytes 98312 | tf_op jit(solution)/shard_map/root_cut/ppermute | solution.py:90
  53.6 5.6 %collective-permute-start.33 = (f32[64,128]{1,0:T(8,128)S(1)}, f32[64,128]{1,0:T(8,128)S(1)}, u32[]{:S(2)}, u32[]{:S(2)}) collective-permute-start(f32[64,128]{1,0:T(8,128)S(1)} %get-tuple-element.102), channel_id=1, source_target_pairs={{0,16},{8,24},{16,0},{24,8},{1,17},{9,25},{17,1},{25,9},{2,18},{10... | collective-permute-start | bytes 98312 | tf_op jit(solution)/shard_map/root_cut/ppermute | solution.py:90
  59.2 4.6 %collective-permute-start.39 = (f32[64,128]{1,0:T(8,128)S(1)}, f32[64,128]{1,0:T(8,128)S(1)}, u32[]{:S(2)}, u32[]{:S(2)}) collective-permute-start(f32[64,128]{1,0:T(8,128)S(1)} %root_cut.7.refs_0_), channel_id=1, source_target_pairs={{0,2},{1,3},{2,0},{3,1},{4,6},{5,7},{6,4},{7,5},{8,10},{9,11},{10,... | collective-permute-start | bytes 98312 | tf_op jit(solution)/shard_map/root_solve/ppermute | solution.py:90
  62.2 4.8 %collective-permute-start.35 = (f32[64,128]{1,0:T(8,128)S(1)}, f32[64,128]{1,0:T(8,128)S(1)}, u32[]{:S(2)}, u32[]{:S(2)}) collective-permute-start(f32[64,128]{1,0:T(8,128)S(1)} %root_cut.7.refs_0_), channel_id=1, source_target_pairs={{0,6},{1,7},{2,4},{3,5},{4,2},{5,3},{6,0},{7,1},{8,14},{9,15},{10,... | collective-permute-start | bytes 98312 | tf_op jit(solution)/shard_map/root_solve/ppermute | solution.py:90
  62.7 4.9 %collective-permute-start.34 = (f32[64,128]{1,0:T(8,128)S(1)}, f32[64,128]{1,0:T(8,128)S(1)}, u32[]{:S(2)}, u32[]{:S(2)}) collective-permute-start(f32[64,128]{1,0:T(8,128)S(1)} %root_cut.7.refs_0_), channel_id=1, source_target_pairs={{0,1},{1,0},{2,3},{3,2},{4,5},{5,4},{6,7},{7,6},{8,9},{9,8},{10,11... | collective-permute-start | bytes 98312 | tf_op jit(solution)/shard_map/root_solve/ppermute | solution.py:90
  70.3 5.1 %collective-permute-start.46 = (f32[64,128]{1,0:T(8,128)S(1)}, f32[64,128]{1,0:T(8,128)S(1)}, u32[]{:S(2)}, u32[]{:S(2)}) collective-permute-start(f32[64,128]{1,0:T(8,128)S(1)} %root_solve.5.refs_0_), channel_id=1, source_target_pairs={{0,2},{1,3},{2,0},{3,1},{4,6},{5,7},{6,4},{7,5},{8,10},{9,11},{10,... | collective-permute-start | bytes 98312 | tf_op jit(solution)/shard_map/root_solve/ppermute | solution.py:90
  70.8 4.5 %collective-permute-start.44 = (f32[64,128]{1,0:T(8,128)S(1)}, f32[64,128]{1,0:T(8,128)S(1)}, u32[]{:S(2)}, u32[]{:S(2)}) collective-permute-start(f32[64,128]{1,0:T(8,128)S(1)} %root_solve.5.refs_0_), channel_id=1, source_target_pairs={{0,4},{1,5},{2,6},{3,7},{4,0},{5,1},{6,2},{7,3},{8,12},{9,13},{10,... | collective-permute-start | bytes 98312 | tf_op jit(solution)/shard_map/root_solve/ppermute | solution.py:90
  71.3 4.8 %collective-permute-start.42 = (f32[64,128]{1,0:T(8,128)S(1)}, f32[64,128]{1,0:T(8,128)S(1)}, u32[]{:S(2)}, u32[]{:S(2)}) collective-permute-start(f32[64,128]{1,0:T(8,128)S(1)} %root_solve.5.refs_0_), channel_id=1, source_target_pairs={{0,6},{1,7},{2,4},{3,5},{4,2},{5,3},{6,0},{7,1},{8,14},{9,15},{10,... | collective-permute-start | bytes 98312 | tf_op jit(solution)/shard_map/root_solve/ppermute | solution.py:90
  79.4 5.2 %collective-permute-start.48 = (f32[64,128]{1,0:T(8,128)S(1)}, f32[64,128]{1,0:T(8,128)S(1)}, u32[]{:S(2)}, u32[]{:S(2)}) collective-permute-start(f32[64,128]{1,0:T(8,128)S(1)} %root_solve.7.mine), channel_id=1, source_target_pairs={{0,16},{8,24},{16,0},{24,8},{1,17},{9,25},{17,1},{25,9},{2,18},{10... | collective-permute-start | bytes 98312 | tf_op jit(solution)/shard_map/mid_upper/ppermute | solution.py:90
  87.2 4.3 %collective-permute-start.51 = (f32[128,128]{1,0:T(8,128)S(1)}, f32[128,128]{1,0:T(8,128)S(1)}, u32[]{:S(2)}, u32[]{:S(2)}) collective-permute-start(f32[128,128]{1,0:T(8,128)S(1)} %get-tuple-element.120.a), channel_id=1, source_target_pairs={{0,2},{1,3},{2,0},{3,1},{4,6},{5,7},{6,4},{7,5},{8,10},{9,11},{10,... | collective-permute-start | bytes 196616 | tf_op jit(solution)/shard_map/mid_upper/ppermute | solution.py:90
  93.0 4.3 %collective-permute-start.53 = (f32[128,128]{1,0:T(8,128)S(1)}, f32[128,128]{1,0:T(8,128)S(1)}, u32[]{:S(2)}, u32[]{:S(2)}) collective-permute-start(f32[128,128]{1,0:T(8,128)S(1)} %get-tuple-element.122.a), channel_id=1, source_target_pairs={{0,4},{1,5},{2,6},{3,7},{4,0},{5,1},{6,2},{7,3},{8,12},{9,13},{10,... | collective-permute-start | bytes 196616 | tf_op jit(solution)/shard_map/mid_upper/ppermute | solution.py:90
  94.6 4.3 %collective-permute-start.54 = (f32[128,128]{1,0:T(8,128)S(1)}, f32[128,128]{1,0:T(8,128)S(1)}, u32[]{:S(2)}, u32[]{:S(2)}) collective-permute-start(f32[128,128]{1,0:T(8,128)S(1)} %get-tuple-element.123.c), channel_id=1, source_target_pairs={{0,2},{1,3},{2,0},{3,1},{4,6},{5,7},{6,4},{7,5},{8,10},{9,11},{10,... | collective-permute-start | bytes 196616 | tf_op jit(solution)/shard_map/mid_upper/ppermute | solution.py:90
  99.5 4.3 %collective-permute-start.49 = (f32[128,128]{1,0:T(8,128)S(1)}, f32[128,128]{1,0:T(8,128)S(1)}, u32[]{:S(2)}, u32[]{:S(2)}) collective-permute-start(f32[128,128]{1,0:T(8,128)S(1)} %get-tuple-element.116.mine), channel_id=1, source_target_pairs={{0,8},{8,0},{16,24},{24,16},{1,9},{9,1},{17,25},{25,17},{2,10},{10... | collective-permute-start | bytes 196616 | tf_op jit(solution)/shard_map/mid_upper/ppermute | solution.py:90
  107.3 4.3 %collective-permute-start.59 = (f32[128,128]{1,0:T(8,128)S(1)}, f32[128,128]{1,0:T(8,128)S(1)}, u32[]{:S(2)}, u32[]{:S(2)}) collective-permute-start(f32[128,128]{1,0:T(8,128)S(1)} %get-tuple-element.128.a), channel_id=1, source_target_pairs={{0,2},{1,3},{2,0},{3,1},{4,6},{5,7},{6,4},{7,5},{8,10},{9,11},{10,... | collective-permute-start | bytes 196616 | tf_op jit(solution)/shard_map/leaf_upper/ppermute | solution.py:90
  107.9 4.3 %collective-permute-start.60 = (f32[128,128]{1,0:T(8,128)S(1)}, f32[128,128]{1,0:T(8,128)S(1)}, u32[]{:S(2)}, u32[]{:S(2)}) collective-permute-start(f32[128,128]{1,0:T(8,128)S(1)} %get-tuple-element.129.c), channel_id=1, source_target_pairs={{0,4},{1,5},{2,6},{3,7},{4,0},{5,1},{6,2},{7,3},{8,12},{9,13},{10,... | collective-permute-start | bytes 196616 | tf_op jit(solution)/shard_map/leaf_upper/ppermute | solution.py:90
  112.2 4.3 %collective-permute-start.61 = (f32[128,128]{1,0:T(8,128)S(1)}, f32[128,128]{1,0:T(8,128)S(1)}, u32[]{:S(2)}, u32[]{:S(2)}) collective-permute-start(f32[128,128]{1,0:T(8,128)S(1)} %get-tuple-element.130.a), channel_id=1, source_target_pairs={{0,4},{1,5},{2,6},{3,7},{4,0},{5,1},{6,2},{7,3},{8,12},{9,13},{10,... | collective-permute-start | bytes 196616 | tf_op jit(solution)/shard_map/leaf_upper/ppermute | solution.py:90
  114.2 5.9 %collective-permute-start.65 = (f32[128,128]{1,0:T(8,128)S(1)}, f32[128,128]{1,0:T(8,128)S(1)}, u32[]{:S(2)}, u32[]{:S(2)}) collective-permute-start(f32[128,128]{1,0:T(8,128)S(1)} %get-tuple-element.136.mine), channel_id=1, source_target_pairs={{0,16},{8,24},{16,0},{24,8},{1,17},{9,25},{17,1},{25,9},{2,18},{10... | collective-permute-start | bytes 196616 | tf_op jit(solution)/shard_map/leaf_upper/ppermute | solution.py:90
  (41 other events, 157.5 us)

commit v6 on v5

--- a/solution.py
+++ b/solution.py
@@ -70,10 +70,11 @@
 
 
 def assemble(where, parts, here, width=LANES):
-    rows = parts[0].shape[0] * (LANES // width)
-    for k, part in zip(origins(len(parts)), parts):
-        start = pl.multiple_of((here ^ k) * rows, 8)
-        where[pl.ds(start, rows), :] = part[...] if width == LANES else unpack(part[...], width)
+    rows = parts[0].shape[0]
+    for (k, at), part in zip(origins(parts), parts):
+        for chunk in range(LANES // width):
+            start = pl.multiple_of((here ^ k) * rows * (LANES // width) + chunk * rows + at, 8)
+            where[pl.ds(start, part.shape[0]), :] = part[:, chunk * width : chunk * width + width]
 
 
 def fields_of(x, forward, adjoint, where):
@@ -90,18 +91,35 @@
     return lax.ppermute(x, axis, [(i, i ^ k) for i in range(size)])
 
 
+def rows_of(at, count, src, out):
+    out[...] = src[at : at + count, :]
+
+
 def gather_front(x, meanwhile=None):
     fronts = lax.axis_size("front")
-    mine = [x] + [swap("front", x, k) for k in range(2, fronts, 2)]
+    if fronts != 8:
+        mine = [x] + [swap("front", x, k) for k in range(2, fronts, 2)]
+        return [b for y in mine for b in (y, swap("front", y, 1))], tuple(meanwhile(x)) if meanwhile else ()
+    one, two = 2, 4
+    near, far = swap("front", x, one), swap("front", x, two)
     extra = tuple(meanwhile(x)) if meanwhile else ()
-    other = [swap("front", after(y, *extra) if i == 1 and extra else y, 1) for i, y in enumerate(mine)]
-    pairs = list(zip(mine, other))
-    return [block for pair in pairs[:1] + pairs[:0:-1] for block in pair], extra
-
-
-def origins(count):
-    evens = [0, *range(count - 2, 0, -2)]
-    return [e + core for e in evens for core in range(2)]
+    if extra:
+        near = after(near, *extra)
+    rows = x.shape[0]
+    cut = -(-rows // 16) * 8
+    (top,) = kernel(functools.partial(rows_of, 0, cut), [(cut, LANES)], near)
+    (low,) = kernel(functools.partial(rows_of, cut, rows - cut), [(rows - cut, LANES)], far)
+    top, low = swap("front", top, two), swap("front", low, one)
+    return [b for y in (x, near, far, top, low) for b in (y, swap("front", y, 1))], extra
+
+
+def origins(blocks):
+    if len(blocks) == 10:
+        cut = blocks[6].shape[0]
+        places = [(0, 0), (2, 0), (4, 0), (6, 0), (6, cut)]
+    else:
+        places = [(k, 0) for k in range(0, len(blocks), 2)]
+    return [(k + core, at) for k, at in places for core in range(2)]
 
 
 def kernel(fn, outs, *args, scratch=(), vmem=8, work=0, hbm=(), pinned=()):
@@ -162,9 +180,8 @@
 
 
 def pack_receivers(fronts, rows, data_hbm, block_hbm, offset_hbm, *refs):
-    groups = lax.axis_size("leaf")
-    outs = refs[:groups]
-    data, block, offset, sems = refs[groups:]
+    own, far, near = refs[:3]
+    data, block, offset, sems = refs[3:]
     copies = [
         pltpu.make_async_copy(src, dst, sems.at[i])
         for i, (src, dst) in enumerate(((data_hbm, data), (block_hbm, block), (offset_hbm, offset)))
@@ -188,12 +205,21 @@
     lane = lax.broadcasted_iota(jnp.int32, (count, COLS), 1)
     index = jnp.where(lane == 0, row_col, 0).astype(F32)
     lines = jnp.concatenate([index, data[0], jnp.zeros((count, COLS), F32), -data[1]], axis=1)
-    for k, out in enumerate(outs):
-        first = (group ^ k) * slots
-        pick = lax.broadcasted_iota(jnp.int32, (slots, count), 0) + first == slot_row
-        out[...] = jnp.dot(
-            pick.astype(F32), lines, precision=lax.Precision.HIGHEST, preferred_element_type=F32
-        )
+    targets = [group, group ^ 2, group ^ 1, group ^ 3]
+    place = lax.broadcasted_iota(jnp.int32, (slots, count), 0)
+    pick = jnp.concatenate([place + target * slots == slot_row for target in targets], axis=0)
+    picked = jnp.dot(
+        pick.astype(F32), lines, precision=lax.Precision.HIGHEST, preferred_element_type=F32
+    )
+    own[...] = picked[:slots]
+    far[...] = picked[slots : 2 * slots]
+    near[...] = picked[2 * slots :]
+
+
+def pass_on(far, came, out):
+    rows = far.shape[0]
+    out[0:rows, :] = far[...]
+    out[rows:, :] = came[rows:, :]
 
 
 def load_sources(leaf_hbm, mid_hbm, root_hbm, leaf_out, mid_out, root_out, leaf, mid, root, sems):
@@ -223,9 +249,8 @@
     return max(rows, slots), 8 * -(-slots // (8 * LANES))
 
 
-def pack_leaf(own, *refs):
-    arrived, out = refs[:-1], refs[-1]
-    lines = jnp.concatenate([ref[...] for ref in arrived], axis=0)
+def pack_leaf(own, mine, near, far, out):
+    lines = jnp.concatenate([mine[...], near[0 : mine.shape[0], :], far[...]], axis=0)
     slots = lines.shape[0]
     body, tail = message_rows(own.shape[0], slots)
     lane = lax.broadcasted_iota(jnp.int32, (slots, LANES), 1)
@@ -249,26 +274,28 @@
 
 
 def leaf_lower(slots, matrix, *refs):
-    messages, (out, rhs) = refs[:-2], refs[-2:]
-    fronts, rows = len(messages), out.shape[0]
+    parts, (out, rhs, messages) = refs[:-3], refs[-3:]
+    rows = out.shape[0]
     here = lax.axis_index("front")
+    for (k, at), part in zip(origins(parts), parts):
+        messages[here ^ k, at : at + part.shape[0], :] = part[...]
+    fronts = messages.shape[0]
     total = rows * fronts
     body, _ = message_rows(rows, slots)
     lane = lax.broadcasted_iota(jnp.int32, (slots, LANES), 1)
     taken = (lane // COLS) % 2 == 1
     own = lax.broadcasted_iota(jnp.int32, (rows, LANES), 1)
     own = (own // COLS) % 2 == 0
-    for k, message in zip(origins(fronts), messages):
-        start = pl.multiple_of((here ^ k) * rows, 8)
-        rhs[pl.ds(start, rows), :] = jnp.where(own, message[0:rows, :], 0.0)
+    for k in range(fronts):
+        rhs[rows * k : rows * k + rows, :] = jnp.where(own, messages[k, 0:rows, :], 0.0)
     group = max(1, 512 // slots)
     for k in range(0, fronts, group):
-        chosen = messages[k : k + group]
-        lines = jnp.concatenate([jnp.where(taken, ref[0:slots, :], 0.0) for ref in chosen], axis=0)
+        chosen = range(k, min(k + group, fronts))
+        lines = jnp.concatenate([jnp.where(taken, messages[i, 0:slots, :], 0.0) for i in chosen], axis=0)
         index = jnp.concatenate(
             [
-                ref[body + at // LANES : body + at // LANES + 1, 0 : min(LANES, slots - at)]
-                for ref in chosen
+                messages[i, body + at // LANES : body + at // LANES + 1, 0 : min(LANES, slots - at)]
+                for i in chosen
                 for at in range(0, slots, LANES)
             ],
             axis=1,
@@ -432,7 +459,7 @@
     with jax.named_scope("right_hand_sides"):
         payload = kernel(
             functools.partial(pack_receivers, fronts, n0),
-            [(slots, LANES)] * groups,
+            [(slots, LANES), (slots, LANES), (2 * slots, LANES)],
             receiver_data,
             receiver_block.reshape(1, -1),
             receiver_offset.reshape(1, -1),
@@ -445,7 +472,10 @@
             hbm=range(3),
             pinned=range(3),
         )
-        arrived = [payload[0]] + [swap("leaf", payload[k], k) for k in range(1, groups)]
+        own, far, near = payload
+        came = swap("leaf", near, 1)
+        (both,) = kernel(pass_on, [(2 * slots, LANES)], far, came)
+        arrived = [own, came, swap("leaf", both, 2)]
         leaf_own, mid_own, root_own = kernel(
             load_sources,
             [(n0, LANES), (n1 // 2, LANES), (n2 // 4, LANES)],
@@ -474,7 +504,7 @@
             [(n0, LANES)],
             ll,
             *messages,
-            scratch=[pltpu.VMEM((s0, LANES), F32)],
+            scratch=[pltpu.VMEM((s0, LANES), F32), pltpu.VMEM((fronts, *message.shape), F32)],
         )
     with jax.named_scope("mid_lower"):
         parts, (l2r, ml) = gather_front(

time: 122 us -> 134 us (1.098)
  starting transfers between devices: 43.2 us -> 57.9 us
  waiting for transfers between devices: 53 us -> 50.1 us
    ppermute x66 -> x77, starting transfers between devices: 43.2 us -> 57.9 us  [swap(): return lax.ppermute(x, axis, [(i, i ^ k) for i in range(size)])]
    ppermute x66 -> x77, waiting for transfers between devices: 53 us -> 50.1 us  [swap(): return lax.ppermute(x, axis, [(i, i ^ k) for i in range(size)])]
    pallas_call x31 -> x44, Pallas kernels: 24.6 us -> 24.6 us  [kernel(): pl.pallas_call(fn, out_shape=[jax.ShapeDtypeStruct(*o) for o in outs], in...]
  transfers between devices with their start and end apart: 66 -> 77, of which waited for: 44 -> 43; matrix products, arithmetic and copies ran while one was open for 0% -> 0% of each run, Pallas kernels for 12% -> 11%
where the time goes in v6:
time: 134 us
  starting transfers between devices  57.9 us (43%)
  waiting for transfers between devices  50.1 us (37%)
  Pallas kernels  24.6 us (18%)
    ppermute x77, starting transfers between devices, swap(): return lax.ppermute(x, axis, [(i, i ^ k) for i in range(size)])  57.9 us
    ppermute x77, waiting for transfers between devices, swap(): return lax.ppermute(x, axis, [(i, i ^ k) for i in range(size)])  50.1 us
    pallas_call x44, Pallas kernels, kernel(): pl.pallas_call(fn, out_shape=[jax.ShapeDtypeStruct(*o) for o in outs], in...  24.6 us
  transfers between devices with their start and end apart: 77, of which 43 were waited for; matrix products, arithmetic and copies ran while one was open for 0% of the time, Pallas kernels for 11%

profile of v6, /device:TPU:0, one launch (start us, length us, event | category | flops | bytes accessed | tf_op | source)
XLA Modules:
  0.0 133.6 jit_solution(793724764218740059)
XLA Ops:
  1.7 3.1 %collective-permute-start = (f32[32,128]{1,0:T(8,128)S(1)}, f32[32,128]{1,0:T(8,128)S(1)}, u32[]{:S(2)}, u32[]{:S(2)}) collective-permute-start(f32[32,128]{1,0:T(8,128)S(1)} %get-tuple-element.75), channel_id=1, source_target_pairs={{0,8},{8,0},{16,24},{24,16},{1,9},{9,1},{17,25},{25,17},{2,10},{10... | collective-permute-start | bytes 49160 | tf_op jit(solution)/shard_map/right_hand_sides/ppermute | solution.py:91
  4.8 1.7 %collective-permute-done.came.near = f32[32,128]{1,0:T(8,128)S(1)} collective-permute-done((f32[32,128]{1,0:T(8,128)S(1)}, f32[32,128]{1,0:T(8,128)S(1)}, u32[]{:S(2)}, u32[]{:S(2)}) %collective-permute-start) | collective-permute-done | bytes 16416 | tf_op jit(solution)/shard_map/right_hand_sides/ppermute | solution.py:91
  6.5 3.0 %collective-permute-start.1 = (f32[32,128]{1,0:T(8,128)S(1)}, f32[32,128]{1,0:T(8,128)S(1)}, u32[]{:S(2)}, u32[]{:S(2)}) collective-permute-start(f32[32,128]{1,0:T(8,128)S(1)} %right_hand_sides.6), channel_id=1, source_target_pairs={{0,16},{8,24},{16,0},{24,8},{1,17},{9,25},{17,1},{25,9},{2,18},{10... | collective-permute-start | bytes 49160 | tf_op jit(solution)/shard_map/right_hand_sides/ppermute | solution.py:91
  11.3 1.9 %collective-permute-start.3 = (f32[72,128]{1,0:T(8,128)S(1)}, f32[72,128]{1,0:T(8,128)S(1)}, u32[]{:S(2)}, u32[]{:S(2)}) collective-permute-start(f32[72,128]{1,0:T(8,128)S(1)} %right_hand_sides.7.refs_0_), channel_id=1, source_target_pairs={{0,2},{1,3},{2,0},{3,1},{4,6},{5,7},{6,4},{7,5},{8,10},{9,11},{10,... | collective-permute-start | bytes 110600 | tf_op jit(solution)/shard_map/leaf_lower/ppermute | solution.py:91
  13.2 1.5 %collective-permute-start.5 = (f32[72,128]{1,0:T(8,128)S(1)}, f32[72,128]{1,0:T(8,128)S(1)}, u32[]{:S(2)}, u32[]{:S(2)}) collective-permute-start(f32[72,128]{1,0:T(8,128)S(1)} %right_hand_sides.7.refs_0_), channel_id=1, source_target_pairs={{0,4},{1,5},{2,6},{3,7},{4,0},{5,1},{6,2},{7,3},{8,12},{9,13},{10,... | collective-permute-start | bytes 110600 | tf_op jit(solution)/shard_map/leaf_lower/ppermute | solution.py:91
  19.9 1.6 %collective-permute-done.9.refs_8_ = f32[32,128]{1,0:T(8,128)S(1)} collective-permute-done((f32[32,128]{1,0:T(8,128)S(1)}, f32[32,128]{1,0:T(8,128)S(1)}, u32[]{:S(2)}, u32[]{:S(2)}) %collective-permute-start.9) | collective-permute-done | bytes 16416 | tf_op jit(solution)/shard_map/leaf_lower/ppermute | solution.py:91
  23.4 1.5 %collective-permute-start.14 = (f32[64,128]{1,0:T(8,128)S(1)}, f32[64,128]{1,0:T(8,128)S(1)}, u32[]{:S(2)}, u32[]{:S(2)}) collective-permute-start(f32[64,128]{1,0:T(8,128)S(1)} %leaf_lower.7.refs_0_), channel_id=1, source_target_pairs={{0,4},{1,5},{2,6},{3,7},{4,0},{5,1},{6,2},{7,3},{8,12},{9,13},{10,... | collective-permute-start | bytes 98312 | tf_op jit(solution)/shard_map/mid_lower/ppermute | solution.py:91
  25.5 1.6 %mid_lower.10 = (bf16[512,1024]{1,0:T(8,128)(2,1)S(1)}, bf16[256,2048]{1,0:T(8,128)(2,1)S(1)}) custom-call(f32[2,1,256,512]{3,2,1,0:T(8,128)} %refs_0_.1, f32[2,2,128,1024]{3,2,1,0:T(8,128)} %refs_1_.5), custom_call_target="tpu_custom_call" | custom-call | flops 262144000 | bytes 374491 | tf_op jit(solution)/shard_map/mid_lower/pallas_call | solution.py:127
  31.1 1.5 %collective-permute-done.16.refs_6_ = f32[32,128]{1,0:T(8,128)S(1)} collective-permute-done((f32[32,128]{1,0:T(8,128)S(1)}, f32[32,128]{1,0:T(8,128)S(1)}, u32[]{:S(2)}, u32[]{:S(2)}) %collective-permute-start.16) | collective-permute-done | bytes 16416 | tf_op jit(solution)/shard_map/mid_lower/ppermute | solution.py:91
  34.3 1.6 %collective-permute-start.20 = (f32[64,128]{1,0:T(8,128)S(1)}, f32[64,128]{1,0:T(8,128)S(1)}, u32[]{:S(2)}, u32[]{:S(2)}) collective-permute-start(f32[64,128]{1,0:T(8,128)S(1)} %get-tuple-element.89), channel_id=1, source_target_pairs={{0,8},{8,0},{16,24},{24,16},{1,9},{9,1},{17,25},{25,17},{2,10},{10... | collective-permute-start | bytes 98312 | tf_op jit(solution)/shard_map/mid_lower/ppermute | solution.py:91
  36.6 1.7 %collective-permute-done.20.refs_1_ = f32[64,128]{1,0:T(8,128)S(1)} collective-permute-done((f32[64,128]{1,0:T(8,128)S(1)}, f32[64,128]{1,0:T(8,128)S(1)}, u32[]{:S(2)}, u32[]{:S(2)}) %collective-permute-start.20) | collective-permute-done | bytes 32800 | tf_op jit(solution)/shard_map/mid_lower/ppermute | solution.py:91
  40.4 1.6 %mid_lower.16.matrix = bf16[512,2048]{1,0:T(8,128)(2,1)S(1)} custom-call(f32[2,2,256,1024]{3,2,1,0:T(8,128)} %refs_0_.2), custom_call_target="tpu_custom_call" | custom-call | flops 262144000 | bytes 374491 | tf_op jit(solution)/shard_map/mid_lower/pallas_call | solution.py:127
  47.0 1.6 %collective-permute-start.30 = (f32[256,64]{1,0:T(8,128)S(1)}, f32[256,64]{1,0:T(8,128)S(1)}, u32[]{:S(2)}, u32[]{:S(2)}) collective-permute-start(f32[256,64]{1,0:T(8,128)S(1)} %get-tuple-element.96), channel_id=1, source_target_pairs={{0,8},{8,0},{16,24},{24,16},{1,9},{9,1},{17,25},{25,17},{2,10},{10... | collective-permute-start | bytes 196616 | tf_op jit(solution)/shard_map/mid_lower/ppermute | solution.py:91
  49.7 1.6 %collective-permute-start.34 = (f32[64,128]{1,0:T(8,128)S(1)}, f32[64,128]{1,0:T(8,128)S(1)}, u32[]{:S(2)}, u32[]{:S(2)}) collective-permute-start(f32[64,128]{1,0:T(8,128)S(1)} %mid_lower.19.refs_0_), channel_id=1, source_target_pairs={{0,4},{1,5},{2,6},{3,7},{4,0},{5,1},{6,2},{7,3},{8,12},{9,13},{10,... | collective-permute-start | bytes 98312 | tf_op jit(solution)/shard_map/root_cut/ppermute | solution.py:91
  52.9 2.3 %collective-permute-done.32.src.refs_2_ = f32[64,128]{1,0:T(8,128)S(1)} collective-permute-done((f32[64,128]{1,0:T(8,128)S(1)}, f32[64,128]{1,0:T(8,128)S(1)}, u32[]{:S(2)}, u32[]{:S(2)}) %collective-permute-start.32) | collective-permute-done | bytes 32800 | tf_op jit(solution)/shard_map/root_cut/ppermute | solution.py:91
  56.0 1.5 %collective-permute-start.36 = (f32[32,128]{1,0:T(8,128)S(1)}, f32[32,128]{1,0:T(8,128)S(1)}, u32[]{:S(2)}, u32[]{:S(2)}) collective-permute-start(f32[32,128]{1,0:T(8,128)S(1)} %root_cut.7), channel_id=1, source_target_pairs={{0,4},{1,5},{2,6},{3,7},{4,0},{5,1},{6,2},{7,3},{8,12},{9,13},{10,... | collective-permute-start | bytes 49160 | tf_op jit(solution)/shard_map/root_cut/ppermute | solution.py:91
  57.5 1.5 %collective-permute-done.38.refs_8_ = f32[32,128]{1,0:T(8,128)S(1)} collective-permute-done((f32[32,128]{1,0:T(8,128)S(1)}, f32[32,128]{1,0:T(8,128)S(1)}, u32[]{:S(2)}, u32[]{:S(2)}) %collective-permute-start.38) | collective-permute-done | bytes 16416 | tf_op jit(solution)/shard_map/root_cut/ppermute | solution.py:91
  62.2 2.7 %collective-permute-start.40 = (f32[64,128]{1,0:T(8,128)S(1)}, f32[64,128]{1,0:T(8,128)S(1)}, u32[]{:S(2)}, u32[]{:S(2)}) collective-permute-start(f32[64,128]{1,0:T(8,128)S(1)} %get-tuple-element.100), channel_id=1, source_target_pairs={{0,16},{8,24},{16,0},{24,8},{1,17},{9,25},{17,1},{25,9},{2,18},{10... | collective-permute-start | bytes 98312 | tf_op jit(solution)/shard_map/root_cut/ppermute | solution.py:91
  65.4 1.8 %collective-permute-done.40.refs_1_ = f32[64,128]{1,0:T(8,128)S(1)} collective-permute-done((f32[64,128]{1,0:T(8,128)S(1)}, f32[64,128]{1,0:T(8,128)S(1)}, u32[]{:S(2)}, u32[]{:S(2)}) %collective-permute-start.40) | collective-permute-done | bytes 32800 | tf_op jit(solution)/shard_map/root_cut/ppermute | solution.py:91
  74.9 1.5 %collective-permute-done.46.refs_6_ = f32[32,128]{1,0:T(8,128)S(1)} collective-permute-done((f32[32,128]{1,0:T(8,128)S(1)}, f32[32,128]{1,0:T(8,128)S(1)}, u32[]{:S(2)}, u32[]{:S(2)}) %collective-permute-start.46) | collective-permute-done | bytes 16416 | tf_op jit(solution)/shard_map/root_solve/ppermute | solution.py:91
  77.6 1.9 %root_solve.11.refs_0_ = f32[64,128]{1,0:T(8,128)S(1)} custom-call(bf16[512,4096]{1,0:T(8,128)(2,1)S(1)} %root_cut.6.matrix, f32[64,128]{1,0:T(8,128)S(1)} %root_cut.11.refs_0_, f32[64,128]{1,0:T(8,128)S(1)} %collective-permute-done.41.refs_1_, f32[64,128]{1,0:T(8,128)S(1)} %collective-permute-done.42.src.refs_2_, ...), custom_call_target="tpu_custom_call" | custom-call | tf_op jit(solution)/shard_map/root_solve/pallas_call | solution.py:127
  88.9 1.9 %root_solve.15.mine = f32[64,128]{1,0:T(8,128)S(1)} custom-call(bf16[512,4096]{1,0:T(8,128)(2,1)S(1)} %root_solve.8.matrix, f32[64,128]{1,0:T(8,128)S(1)} %root_solve.11.refs_0_, f32[64,128]{1,0:T(8,128)S(1)} %collective-permute-done.50.refs_1_, f32[64,128]{1,0:T(8,128)S(1)} %collective-permute-done.51.src.refs_2_, ...), custom_call_target="tpu_custom_call" | custom-call | tf_op jit(solution)/shard_map/root_solve/pallas_call | solution.py:127
  90.8 2.6 %collective-permute-start.59 = (f32[64,128]{1,0:T(8,128)S(1)}, f32[64,128]{1,0:T(8,128)S(1)}, u32[]{:S(2)}, u32[]{:S(2)}) collective-permute-start(f32[64,128]{1,0:T(8,128)S(1)} %root_solve.15.mine), channel_id=1, source_target_pairs={{0,16},{8,24},{16,0},{24,8},{1,17},{9,25},{17,1},{25,9},{2,18},{10... | collective-permute-start | bytes 98312 | tf_op jit(solution)/shard_map/mid_upper/ppermute | solution.py:91
  93.3 3.0 %collective-permute-done.59.other = f32[64,128]{1,0:T(8,128)S(1)} collective-permute-done((f32[64,128]{1,0:T(8,128)S(1)}, f32[64,128]{1,0:T(8,128)S(1)}, u32[]{:S(2)}, u32[]{:S(2)}) %collective-permute-start.59) | collective-permute-done | bytes 32800 | tf_op jit(solution)/shard_map/mid_upper/ppermute | solution.py:91
  98.9 1.6 %collective-permute-start.62 = (f32[128,128]{1,0:T(8,128)S(1)}, f32[128,128]{1,0:T(8,128)S(1)}, u32[]{:S(2)}, u32[]{:S(2)}) collective-permute-start(f32[128,128]{1,0:T(8,128)S(1)} %get-tuple-element.118.a), channel_id=1, source_target_pairs={{0,2},{1,3},{2,0},{3,1},{4,6},{5,7},{6,4},{7,5},{8,10},{9,11},{10,... | collective-permute-start | bytes 196616 | tf_op jit(solution)/shard_map/mid_upper/ppermute | solution.py:91
  101.0 2.2 %collective-permute-done.62.b = f32[128,128]{1,0:T(8,128)S(1)} collective-permute-done((f32[128,128]{1,0:T(8,128)S(1)}, f32[128,128]{1,0:T(8,128)S(1)}, u32[]{:S(2)}, u32[]{:S(2)}) %collective-permute-start.62) | collective-permute-done | bytes 65568 | tf_op jit(solution)/shard_map/mid_upper/ppermute | solution.py:91
  106.8 2.2 %collective-permute-done.64.b = f32[128,128]{1,0:T(8,128)S(1)} collective-permute-done((f32[128,128]{1,0:T(8,128)S(1)}, f32[128,128]{1,0:T(8,128)S(1)}, u32[]{:S(2)}, u32[]{:S(2)}) %collective-permute-start.64) | collective-permute-done | bytes 65568 | tf_op jit(solution)/shard_map/mid_upper/ppermute | solution.py:91
  118.0 1.6 %collective-permute-start.70 = (f32[128,128]{1,0:T(8,128)S(1)}, f32[128,128]{1,0:T(8,128)S(1)}, u32[]{:S(2)}, u32[]{:S(2)}) collective-permute-start(f32[128,128]{1,0:T(8,128)S(1)} %get-tuple-element.126.a), channel_id=1, source_target_pairs={{0,2},{1,3},{2,0},{3,1},{4,6},{5,7},{6,4},{7,5},{8,10},{9,11},{10,... | collective-permute-start | bytes 196616 | tf_op jit(solution)/shard_map/leaf_upper/ppermute | solution.py:91
  120.1 2.2 %collective-permute-done.70.b = f32[128,128]{1,0:T(8,128)S(1)} collective-permute-done((f32[128,128]{1,0:T(8,128)S(1)}, f32[128,128]{1,0:T(8,128)S(1)}, u32[]{:S(2)}, u32[]{:S(2)}) %collective-permute-start.70) | collective-permute-done | bytes 65568 | tf_op jit(solution)/shard_map/leaf_upper/ppermute | solution.py:91
  124.5 1.5 %collective-permute-start.73 = (f32[128,128]{1,0:T(8,128)S(1)}, f32[128,128]{1,0:T(8,128)S(1)}, u32[]{:S(2)}, u32[]{:S(2)}) collective-permute-start(f32[128,128]{1,0:T(8,128)S(1)} %get-tuple-element.129.c), channel_id=1, source_target_pairs={{0,2},{1,3},{2,0},{3,1},{4,6},{5,7},{6,4},{7,5},{8,10},{9,11},{10,... | collective-permute-start | bytes 196616 | tf_op jit(solution)/shard_map/leaf_upper/ppermute | solution.py:91
  126.0 2.7 %collective-permute-start.76 = (f32[128,128]{1,0:T(8,128)S(1)}, f32[128,128]{1,0:T(8,128)S(1)}, u32[]{:S(2)}, u32[]{:S(2)}) collective-permute-start(f32[128,128]{1,0:T(8,128)S(1)} %get-tuple-element.134.mine), channel_id=1, source_target_pairs={{0,16},{8,24},{16,0},{24,8},{1,17},{9,25},{17,1},{25,9},{2,18},{10... | collective-permute-start | bytes 196616 | tf_op jit(solution)/shard_map/leaf_upper/ppermute | solution.py:91
  129.3 2.5 %collective-permute-done.76.other = f32[128,128]{1,0:T(8,128)S(1)} collective-permute-done((f32[128,128]{1,0:T(8,128)S(1)}, f32[128,128]{1,0:T(8,128)S(1)}, u32[]{:S(2)}, u32[]{:S(2)}) %collective-permute-start.76) | collective-permute-done | bytes 65568 | tf_op jit(solution)/shard_map/leaf_upper/ppermute | solution.py:91
  (180 shorter events, 69.9 us)
Async XLA Ops:
  1.7 4.8 %collective-permute-start = (f32[32,128]{1,0:T(8,128)S(1)}, f32[32,128]{1,0:T(8,128)S(1)}, u32[]{:S(2)}, u32[]{:S(2)}) collective-permute-start(f32[32,128]{1,0:T(8,128)S(1)} %get-tuple-element.75), channel_id=1, source_target_pairs={{0,8},{8,0},{16,24},{24,16},{1,9},{9,1},{17,25},{25,17},{2,10},{10... | collective-permute-start | bytes 49160 | tf_op jit(solution)/shard_map/right_hand_sides/ppermute | solution.py:91
  6.5 4.7 %collective-permute-start.1 = (f32[32,128]{1,0:T(8,128)S(1)}, f32[32,128]{1,0:T(8,128)S(1)}, u32[]{:S(2)}, u32[]{:S(2)}) collective-permute-start(f32[32,128]{1,0:T(8,128)S(1)} %right_hand_sides.6), channel_id=1, source_target_pairs={{0,16},{8,24},{16,0},{24,8},{1,17},{9,25},{17,1},{25,9},{2,18},{10... | collective-permute-start | bytes 49160 | tf_op jit(solution)/shard_map/right_hand_sides/ppermute | solution.py:91
  11.3 4.7 %collective-permute-start.3 = (f32[72,128]{1,0:T(8,128)S(1)}, f32[72,128]{1,0:T(8,128)S(1)}, u32[]{:S(2)}, u32[]{:S(2)}) collective-permute-start(f32[72,128]{1,0:T(8,128)S(1)} %right_hand_sides.7.refs_0_), channel_id=1, source_target_pairs={{0,2},{1,3},{2,0},{3,1},{4,6},{5,7},{6,4},{7,5},{8,10},{9,11},{10,... | collective-permute-start | bytes 110600 | tf_op jit(solution)/shard_map/leaf_lower/ppermute | solution.py:91
  13.2 4.0 %collective-permute-start.5 = (f32[72,128]{1,0:T(8,128)S(1)}, f32[72,128]{1,0:T(8,128)S(1)}, u32[]{:S(2)}, u32[]{:S(2)}) collective-permute-start(f32[72,128]{1,0:T(8,128)S(1)} %right_hand_sides.7.refs_0_), channel_id=1, source_target_pairs={{0,4},{1,5},{2,6},{3,7},{4,0},{5,1},{6,2},{7,3},{8,12},{9,13},{10,... | collective-permute-start | bytes 110600 | tf_op jit(solution)/shard_map/leaf_lower/ppermute | solution.py:91
  17.2 4.3 %collective-permute-start.2 = (f32[72,128]{1,0:T(8,128)S(1)}, f32[72,128]{1,0:T(8,128)S(1)}, u32[]{:S(2)}, u32[]{:S(2)}) collective-permute-start(f32[72,128]{1,0:T(8,128)S(1)} %right_hand_sides.7.refs_0_), channel_id=1, source_target_pairs={{0,1},{1,0},{2,3},{3,2},{4,5},{5,4},{6,7},{7,6},{8,9},{9,8},{10,11... | collective-permute-start | bytes 110600 | tf_op jit(solution)/shard_map/leaf_lower/ppermute | solution.py:91
  17.2 5.4 %collective-permute-start.6 = (f32[72,128]{1,0:T(8,128)S(1)}, f32[72,128]{1,0:T(8,128)S(1)}, u32[]{:S(2)}, u32[]{:S(2)}) collective-permute-start(f32[72,128]{1,0:T(8,128)S(1)} %collective-permute-done.5.src.refs_4_), channel_id=1, source_target_pairs={{0,1},{1,0},{2,3},{3,2},{4,5},{5,4},{6,7},{7,6},{8,9},{9,8},{10,11... | collective-permute-start | bytes 110600 | tf_op jit(solution)/shard_map/leaf_lower/ppermute | solution.py:91
  17.7 4.9 %collective-permute-start.4 = (f32[72,128]{1,0:T(8,128)S(1)}, f32[72,128]{1,0:T(8,128)S(1)}, u32[]{:S(2)}, u32[]{:S(2)}) collective-permute-start(f32[72,128]{1,0:T(8,128)S(1)} %collective-permute-done.3.src.refs_2_), channel_id=1, source_target_pairs={{0,1},{1,0},{2,3},{3,2},{4,5},{5,4},{6,7},{7,6},{8,9},{9,8},{10,11... | collective-permute-start | bytes 110600 | tf_op jit(solution)/shard_map/leaf_lower/ppermute | solution.py:91
  25.5 7.1 %collective-permute-start.11 = (f32[64,128]{1,0:T(8,128)S(1)}, f32[64,128]{1,0:T(8,128)S(1)}, u32[]{:S(2)}, u32[]{:S(2)}) collective-permute-start(f32[64,128]{1,0:T(8,128)S(1)} %leaf_lower.7.refs_0_), channel_id=1, source_target_pairs={{0,1},{1,0},{2,3},{3,2},{4,5},{5,4},{6,7},{7,6},{8,9},{9,8},{10,11... | collective-permute-start | bytes 98312 | tf_op jit(solution)/shard_map/mid_lower/ppermute | solution.py:91
  29.4 4.4 %collective-permute-start.15 = (f32[64,128]{1,0:T(8,128)S(1)}, f32[64,128]{1,0:T(8,128)S(1)}, u32[]{:S(2)}, u32[]{:S(2)}) collective-permute-start(f32[64,128]{1,0:T(8,128)S(1)} %collective-permute-done.14.src.refs_4_), channel_id=1, source_target_pairs={{0,1},{1,0},{2,3},{3,2},{4,5},{5,4},{6,7},{7,6},{8,9},{9,8},{10,11... | collective-permute-start | bytes 98312 | tf_op jit(solution)/shard_map/mid_lower/ppermute | solution.py:91
  29.4 4.4 %collective-permute-start.13 = (f32[64,128]{1,0:T(8,128)S(1)}, f32[64,128]{1,0:T(8,128)S(1)}, u32[]{:S(2)}, u32[]{:S(2)}) collective-permute-start(f32[64,128]{1,0:T(8,128)S(1)} %collective-permute-done.12.src.refs_2_), channel_id=1, source_target_pairs={{0,1},{1,0},{2,3},{3,2},{4,5},{5,4},{6,7},{7,6},{8,9},{9,8},{10,11... | collective-permute-start | bytes 98312 | tf_op jit(solution)/shard_map/mid_lower/ppermute | solution.py:91
  40.4 6.7 %collective-permute-start.21 = (f32[64,128]{1,0:T(8,128)S(1)}, f32[64,128]{1,0:T(8,128)S(1)}, u32[]{:S(2)}, u32[]{:S(2)}) collective-permute-start(f32[64,128]{1,0:T(8,128)S(1)} %mid_lower.15.refs_0_), channel_id=1, source_target_pairs={{0,1},{1,0},{2,3},{3,2},{4,5},{5,4},{6,7},{7,6},{8,9},{9,8},{10,11... | collective-permute-start | bytes 98312 | tf_op jit(solution)/shard_map/mid_lower/ppermute | solution.py:91
  42.8 5.8 %collective-permute-start.25 = (f32[64,128]{1,0:T(8,128)S(1)}, f32[64,128]{1,0:T(8,128)S(1)}, u32[]{:S(2)}, u32[]{:S(2)}) collective-permute-start(f32[64,128]{1,0:T(8,128)S(1)} %collective-permute-done.24.src.refs_4_), channel_id=1, source_target_pairs={{0,1},{1,0},{2,3},{3,2},{4,5},{5,4},{6,7},{7,6},{8,9},{9,8},{10,11... | collective-permute-start | bytes 98312 | tf_op jit(solution)/shard_map/mid_lower/ppermute | solution.py:91
  42.9 5.8 %collective-permute-start.23 = (f32[64,128]{1,0:T(8,128)S(1)}, f32[64,128]{1,0:T(8,128)S(1)}, u32[]{:S(2)}, u32[]{:S(2)}) collective-permute-start(f32[64,128]{1,0:T(8,128)S(1)} %collective-permute-done.22.src.refs_2_), channel_id=1, source_target_pairs={{0,1},{1,0},{2,3},{3,2},{4,5},{5,4},{6,7},{7,6},{8,9},{9,8},{10,11... | collective-permute-start | bytes 98312 | tf_op jit(solution)/shard_map/mid_lower/ppermute | solution.py:91
  47.0 8.9 %collective-permute-start.30 = (f32[256,64]{1,0:T(8,128)S(1)}, f32[256,64]{1,0:T(8,128)S(1)}, u32[]{:S(2)}, u32[]{:S(2)}) collective-permute-start(f32[256,64]{1,0:T(8,128)S(1)} %get-tuple-element.96), channel_id=1, source_target_pairs={{0,8},{8,0},{16,24},{24,16},{1,9},{9,1},{17,25},{25,17},{2,10},{10... | collective-permute-start | bytes 196616 | tf_op jit(solution)/shard_map/mid_lower/ppermute | solution.py:91
  49.7 5.5 %collective-permute-start.34 = (f32[64,128]{1,0:T(8,128)S(1)}, f32[64,128]{1,0:T(8,128)S(1)}, u32[]{:S(2)}, u32[]{:S(2)}) collective-permute-start(f32[64,128]{1,0:T(8,128)S(1)} %mid_lower.19.refs_0_), channel_id=1, source_target_pairs={{0,4},{1,5},{2,6},{3,7},{4,0},{5,1},{6,2},{7,3},{8,12},{9,13},{10,... | collective-permute-start | bytes 98312 | tf_op jit(solution)/shard_map/root_cut/ppermute | solution.py:91
  51.8 7.9 %collective-permute-start.31 = (f32[64,128]{1,0:T(8,128)S(1)}, f32[64,128]{1,0:T(8,128)S(1)}, u32[]{:S(2)}, u32[]{:S(2)}) collective-permute-start(f32[64,128]{1,0:T(8,128)S(1)} %mid_lower.19.refs_0_), channel_id=1, source_target_pairs={{0,1},{1,0},{2,3},{3,2},{4,5},{5,4},{6,7},{7,6},{8,9},{9,8},{10,11... | collective-permute-start | bytes 98312 | tf_op jit(solution)/shard_map/root_cut/ppermute | solution.py:91
  55.2 4.5 %collective-permute-start.33 = (f32[64,128]{1,0:T(8,128)S(1)}, f32[64,128]{1,0:T(8,128)S(1)}, u32[]{:S(2)}, u32[]{:S(2)}) collective-permute-start(f32[64,128]{1,0:T(8,128)S(1)} %collective-permute-done.32.src.refs_2_), channel_id=1, source_target_pairs={{0,1},{1,0},{2,3},{3,2},{4,5},{5,4},{6,7},{7,6},{8,9},{9,8},{10,11... | collective-permute-start | bytes 98312 | tf_op jit(solution)/shard_map/root_cut/ppermute | solution.py:91
  62.2 5.0 %collective-permute-start.40 = (f32[64,128]{1,0:T(8,128)S(1)}, f32[64,128]{1,0:T(8,128)S(1)}, u32[]{:S(2)}, u32[]{:S(2)}) collective-permute-start(f32[64,128]{1,0:T(8,128)S(1)} %get-tuple-element.100), channel_id=1, source_target_pairs={{0,16},{8,24},{16,0},{24,8},{1,17},{9,25},{17,1},{25,9},{2,18},{10... | collective-permute-start | bytes 98312 | tf_op jit(solution)/shard_map/root_cut/ppermute | solution.py:91
  69.3 7.1 %collective-permute-start.41 = (f32[64,128]{1,0:T(8,128)S(1)}, f32[64,128]{1,0:T(8,128)S(1)}, u32[]{:S(2)}, u32[]{:S(2)}) collective-permute-start(f32[64,128]{1,0:T(8,128)S(1)} %root_cut.11.refs_0_), channel_id=1, source_target_pairs={{0,1},{1,0},{2,3},{3,2},{4,5},{5,4},{6,7},{7,6},{8,9},{9,8},{10,11... | collective-permute-start | bytes 98312 | tf_op jit(solution)/shard_map/root_solve/ppermute | solution.py:91
  73.2 4.4 %collective-permute-start.43 = (f32[64,128]{1,0:T(8,128)S(1)}, f32[64,128]{1,0:T(8,128)S(1)}, u32[]{:S(2)}, u32[]{:S(2)}) collective-permute-start(f32[64,128]{1,0:T(8,128)S(1)} %collective-permute-done.42.src.refs_2_), channel_id=1, source_target_pairs={{0,1},{1,0},{2,3},{3,2},{4,5},{5,4},{6,7},{7,6},{8,9},{9,8},{10,11... | collective-permute-start | bytes 98312 | tf_op jit(solution)/shard_map/root_solve/ppermute | solution.py:91
  81.5 6.2 %collective-permute-start.50 = (f32[64,128]{1,0:T(8,128)S(1)}, f32[64,128]{1,0:T(8,128)S(1)}, u32[]{:S(2)}, u32[]{:S(2)}) collective-permute-start(f32[64,128]{1,0:T(8,128)S(1)} %root_solve.11.refs_0_), channel_id=1, source_target_pairs={{0,1},{1,0},{2,3},{3,2},{4,5},{5,4},{6,7},{7,6},{8,9},{9,8},{10,11... | collective-permute-start | bytes 98312 | tf_op jit(solution)/shard_map/root_solve/ppermute | solution.py:91
  90.8 5.6 %collective-permute-start.59 = (f32[64,128]{1,0:T(8,128)S(1)}, f32[64,128]{1,0:T(8,128)S(1)}, u32[]{:S(2)}, u32[]{:S(2)}) collective-permute-start(f32[64,128]{1,0:T(8,128)S(1)} %root_solve.15.mine), channel_id=1, source_target_pairs={{0,16},{8,24},{16,0},{24,8},{1,17},{9,25},{17,1},{25,9},{2,18},{10... | collective-permute-start | bytes 98312 | tf_op jit(solution)/shard_map/mid_upper/ppermute | solution.py:91
  98.9 4.3 %collective-permute-start.62 = (f32[128,128]{1,0:T(8,128)S(1)}, f32[128,128]{1,0:T(8,128)S(1)}, u32[]{:S(2)}, u32[]{:S(2)}) collective-permute-start(f32[128,128]{1,0:T(8,128)S(1)} %get-tuple-element.118.a), channel_id=1, source_target_pairs={{0,2},{1,3},{2,0},{3,1},{4,6},{5,7},{6,4},{7,5},{8,10},{9,11},{10,... | collective-permute-start | bytes 196616 | tf_op jit(solution)/shard_map/mid_upper/ppermute | solution.py:91
  100.4 4.3 %collective-permute-start.63 = (f32[128,128]{1,0:T(8,128)S(1)}, f32[128,128]{1,0:T(8,128)S(1)}, u32[]{:S(2)}, u32[]{:S(2)}) collective-permute-start(f32[128,128]{1,0:T(8,128)S(1)} %get-tuple-element.119.c), channel_id=1, source_target_pairs={{0,4},{1,5},{2,6},{3,7},{4,0},{5,1},{6,2},{7,3},{8,12},{9,13},{10,... | collective-permute-start | bytes 196616 | tf_op jit(solution)/shard_map/mid_upper/ppermute | solution.py:91
  104.7 4.3 %collective-permute-start.64 = (f32[128,128]{1,0:T(8,128)S(1)}, f32[128,128]{1,0:T(8,128)S(1)}, u32[]{:S(2)}, u32[]{:S(2)}) collective-permute-start(f32[128,128]{1,0:T(8,128)S(1)} %get-tuple-element.120.a), channel_id=1, source_target_pairs={{0,4},{1,5},{2,6},{3,7},{4,0},{5,1},{6,2},{7,3},{8,12},{9,13},{10,... | collective-permute-start | bytes 196616 | tf_op jit(solution)/shard_map/mid_upper/ppermute | solution.py:91
  105.3 4.3 %collective-permute-start.65 = (f32[128,128]{1,0:T(8,128)S(1)}, f32[128,128]{1,0:T(8,128)S(1)}, u32[]{:S(2)}, u32[]{:S(2)}) collective-permute-start(f32[128,128]{1,0:T(8,128)S(1)} %get-tuple-element.121.c), channel_id=1, source_target_pairs={{0,2},{1,3},{2,0},{3,1},{4,6},{5,7},{6,4},{7,5},{8,10},{9,11},{10,... | collective-permute-start | bytes 196616 | tf_op jit(solution)/shard_map/mid_upper/ppermute | solution.py:91
  110.2 4.3 %collective-permute-start.60 = (f32[128,128]{1,0:T(8,128)S(1)}, f32[128,128]{1,0:T(8,128)S(1)}, u32[]{:S(2)}, u32[]{:S(2)}) collective-permute-start(f32[128,128]{1,0:T(8,128)S(1)} %get-tuple-element.114.mine), channel_id=1, source_target_pairs={{0,8},{8,0},{16,24},{24,16},{1,9},{9,1},{17,25},{25,17},{2,10},{10... | collective-permute-start | bytes 196616 | tf_op jit(solution)/shard_map/mid_upper/ppermute | solution.py:91
  118.0 4.3 %collective-permute-start.70 = (f32[128,128]{1,0:T(8,128)S(1)}, f32[128,128]{1,0:T(8,128)S(1)}, u32[]{:S(2)}, u32[]{:S(2)}) collective-permute-start(f32[128,128]{1,0:T(8,128)S(1)} %get-tuple-element.126.a), channel_id=1, source_target_pairs={{0,2},{1,3},{2,0},{3,1},{4,6},{5,7},{6,4},{7,5},{8,10},{9,11},{10,... | collective-permute-start | bytes 196616 | tf_op jit(solution)/shard_map/leaf_upper/ppermute | solution.py:91
  119.6 4.3 %collective-permute-start.71 = (f32[128,128]{1,0:T(8,128)S(1)}, f32[128,128]{1,0:T(8,128)S(1)}, u32[]{:S(2)}, u32[]{:S(2)}) collective-permute-start(f32[128,128]{1,0:T(8,128)S(1)} %get-tuple-element.127.c), channel_id=1, source_target_pairs={{0,4},{1,5},{2,6},{3,7},{4,0},{5,1},{6,2},{7,3},{8,12},{9,13},{10,... | collective-permute-start | bytes 196616 | tf_op jit(solution)/shard_map/leaf_upper/ppermute | solution.py:91
  123.9 4.8 %collective-permute-start.72 = (f32[128,128]{1,0:T(8,128)S(1)}, f32[128,128]{1,0:T(8,128)S(1)}, u32[]{:S(2)}, u32[]{:S(2)}) collective-permute-start(f32[128,128]{1,0:T(8,128)S(1)} %get-tuple-element.128.a), channel_id=1, source_target_pairs={{0,4},{1,5},{2,6},{3,7},{4,0},{5,1},{6,2},{7,3},{8,12},{9,13},{10,... | collective-permute-start | bytes 196616 | tf_op jit(solution)/shard_map/leaf_upper/ppermute | solution.py:91
  124.5 4.3 %collective-permute-start.73 = (f32[128,128]{1,0:T(8,128)S(1)}, f32[128,128]{1,0:T(8,128)S(1)}, u32[]{:S(2)}, u32[]{:S(2)}) collective-permute-start(f32[128,128]{1,0:T(8,128)S(1)} %get-tuple-element.129.c), channel_id=1, source_target_pairs={{0,2},{1,3},{2,0},{3,1},{4,6},{5,7},{6,4},{7,5},{8,10},{9,11},{10,... | collective-permute-start | bytes 196616 | tf_op jit(solution)/shard_map/leaf_upper/ppermute | solution.py:91
  126.0 5.9 %collective-permute-start.76 = (f32[128,128]{1,0:T(8,128)S(1)}, f32[128,128]{1,0:T(8,128)S(1)}, u32[]{:S(2)}, u32[]{:S(2)}) collective-permute-start(f32[128,128]{1,0:T(8,128)S(1)} %get-tuple-element.134.mine), channel_id=1, source_target_pairs={{0,16},{8,24},{16,0},{24,8},{1,17},{9,25},{17,1},{25,9},{2,18},{10... | collective-permute-start | bytes 196616 | tf_op jit(solution)/shard_map/leaf_upper/ppermute | solution.py:91
  (52 other events, 229.9 us)

commit v7 on v6

--- a/solution.py
+++ b/solution.py
@@ -70,11 +70,10 @@
 
 
 def assemble(where, parts, here, width=LANES):
-    rows = parts[0].shape[0]
-    for (k, at), part in zip(origins(parts), parts):
-        for chunk in range(LANES // width):
-            start = pl.multiple_of((here ^ k) * rows * (LANES // width) + chunk * rows + at, 8)
-            where[pl.ds(start, part.shape[0]), :] = part[:, chunk * width : chunk * width + width]
+    rows = parts[0].shape[0] * (LANES // width)
+    for k, part in blocks_of(parts):
+        start = pl.multiple_of((here ^ k) * rows, 8)
+        where[pl.ds(start, rows), :] = part[...] if width == LANES else unpack(part[...], width)
 
 
 def fields_of(x, forward, adjoint, where):
@@ -91,35 +90,34 @@
     return lax.ppermute(x, axis, [(i, i ^ k) for i in range(size)])
 
 
-def rows_of(at, count, src, out):
-    out[...] = src[at : at + count, :]
+def stack(*refs):
+    at = 0
+    for ref in refs[:-1]:
+        refs[-1][at : at + ref.shape[0], :] = ref[...]
+        at += ref.shape[0]
 
 
 def gather_front(x, meanwhile=None):
     fronts = lax.axis_size("front")
-    if fronts != 8:
-        mine = [x] + [swap("front", x, k) for k in range(2, fronts, 2)]
-        return [b for y in mine for b in (y, swap("front", y, 1))], tuple(meanwhile(x)) if meanwhile else ()
-    one, two = 2, 4
-    near, far = swap("front", x, one), swap("front", x, two)
+    mine = [swap("front", x, k) for k in range(2, fronts, 2)]
     extra = tuple(meanwhile(x)) if meanwhile else ()
+    near, last = mine[:-1], mine[-1]
     if extra:
-        near = after(near, *extra)
-    rows = x.shape[0]
-    cut = -(-rows // 16) * 8
-    (top,) = kernel(functools.partial(rows_of, 0, cut), [(cut, LANES)], near)
-    (low,) = kernel(functools.partial(rows_of, cut, rows - cut), [(rows - cut, LANES)], far)
-    top, low = swap("front", top, two), swap("front", low, one)
-    return [b for y in (x, near, far, top, low) for b in (y, swap("front", y, 1))], extra
-
-
-def origins(blocks):
-    if len(blocks) == 10:
-        cut = blocks[6].shape[0]
-        places = [(0, 0), (2, 0), (4, 0), (6, 0), (6, cut)]
-    else:
-        places = [(k, 0) for k in range(0, len(blocks), 2)]
-    return [(k + core, at) for k, at in places for core in range(2)]
+        near = [after(near[0], *extra), *near[1:]]
+    (both,) = kernel(stack, [(len(near) * x.shape[0], LANES)], *near)
+    return [x, swap("front", x, 1), last, *near[::-1], swap("front", last, 1), swap("front", both, 1)], extra
+
+
+def blocks_of(parts):
+    rows, fronts = parts[0].shape[0], 2 * len(parts) - 6
+    evens = list(range(2, fronts, 2))
+    yield 0, parts[0]
+    yield 1, parts[1]
+    for k, part in zip(evens[::-1], parts[2:-2]):
+        yield k, part
+    yield evens[-1] + 1, parts[-2]
+    for i, k in enumerate(evens[:-1]):
+        yield k + 1, parts[-1].at[rows * i : rows * i + rows, :]
 
 
 def kernel(fn, outs, *args, scratch=(), vmem=8, work=0, hbm=(), pinned=()):
@@ -277,8 +275,8 @@
     parts, (out, rhs, messages) = refs[:-3], refs[-3:]
     rows = out.shape[0]
     here = lax.axis_index("front")
-    for (k, at), part in zip(origins(parts), parts):
-        messages[here ^ k, at : at + part.shape[0], :] = part[...]
+    for k, part in blocks_of(parts):
+        messages[here ^ k] = part[...]
     fronts = messages.shape[0]
     total = rows * fronts
     body, _ = message_rows(rows, slots)
@@ -374,38 +372,24 @@
     fields_of(x, forward, adjoint, ())
 
 
-def add_halves(kept, came, first, second):
-    rows = first.shape[0]
-    first[...] = kept[0:rows, :] + came[0:rows, :]
-    second[...] = kept[rows:, :] + came[rows:, :]
-
-
-def add_pair(a, b, c, d, first, second):
-    first[...] = a[...] + b[...]
-    second[...] = c[...] + d[...]
-
-
 def sum_front(kept, sent):
     fronts = lax.axis_size("front")
-    rows = kept.shape[0] // 2
-    shapes = [(rows, LANES)] * 2
-    a, b = kernel(add_halves, shapes, kept, swap("front", sent, 1))
+    (total,) = kernel(add, [kept.shape], kept, swap("front", sent, 1))
     hops = [1 << i for i in range(1, fronts.bit_length() - 1)]
-    for i, hop in enumerate(hops):
-        back = hops[-1 - i]
-        a, b = kernel(add_pair, shapes, a, swap("front", a, hop), b, swap("front", b, back))
-    return [a, b, swap("front", a, 1), swap("front", b, 1)]
+    for hop, back in zip(hops, hops[::-1]):
+        pairs = [(i, i ^ (back if i & 1 else hop)) for i in range(fronts)]
+        (total,) = kernel(add, [kept.shape], total, lax.ppermute(total, "front", pairs))
+    return [total, swap("front", total, 1)]
 
 
 def summed(pieces):
-    a, b, c, d = (ref[...] for ref in pieces)
+    mine, theirs = (ref[...] for ref in pieces)
     odd = (lax.axis_index("front") & 1) == 1
-    mine, theirs = jnp.concatenate([a, b], axis=0), jnp.concatenate([c, d], axis=0)
     return jnp.concatenate([jnp.where(odd, theirs, mine), jnp.where(odd, mine, theirs)], axis=0)
 
 
 def mid_upper(matrix, y, *refs):
-    tail, out = unpack(summed(refs[:4]), 2 * COLS), refs[4]
+    tail, out = unpack(summed(refs[:2]), 2 * COLS), refs[2]
     out[...] = pack(complex_dot(matrix[...], y[...] - tail))
 
 
@@ -416,8 +400,8 @@
 
 
 def leaf_upper(matrix, y, *refs):
-    forward, adjoint = refs[4:]
-    fields_of(complex_dot(matrix[...], y[...] - summed(refs[:4])), forward, adjoint, ())
+    forward, adjoint = refs[2:]
+    fields_of(complex_dot(matrix[...], y[...] - summed(refs[:2])), forward, adjoint, ())
 
 
 def mid_outputs(mine, other, forward, adjoint):

time: 134 us -> 123 us (0.918)
  starting transfers between devices: 57.9 us -> 49.4 us
  waiting for transfers between devices: 50.1 us -> 47.5 us
    ppermute x77 -> x49, waiting for transfers between devices: 50.1 us -> 33.6 us  [swap(): return lax.ppermute(x, axis, [(i, i ^ k) for i in range(size)])]
    ppermute x77 -> x49, starting transfers between devices: 57.9 us -> 43.1 us  [swap(): return lax.ppermute(x, axis, [(i, i ^ k) for i in range(size)])]
    ppermute x0 -> x4, waiting for transfers between devices: none -> 13.8 us  [sum_front(): lax.ppermute(total, 'front', pairs)]
    ppermute x0 -> x4, starting transfers between devices: none -> 6.28 us  [sum_front(): lax.ppermute(total, 'front', pairs)]
    pallas_call x44 -> x38, Pallas kernels: 24.6 us -> 24.6 us  [kernel(): pl.pallas_call(fn, out_shape=[jax.ShapeDtypeStruct(*o) for o in outs], in...]
  transfers between devices with their start and end apart: 77 -> 53, of which waited for: 43 -> 32; matrix products, arithmetic and copies ran while one was open for 0% -> 0% of each run, Pallas kernels for 11% -> 12%
where the time goes in v7:
time: 123 us; the launch traced here: 122 us
  starting transfers between devices  49.4 us (40%)
  waiting for transfers between devices  47.5 us (39%)
  Pallas kernels  24.6 us (20%)
    ppermute x49, starting transfers between devices, swap(): return lax.ppermute(x, axis, [(i, i ^ k) for i in range(size)])  43.1 us
    ppermute x49, waiting for transfers between devices, swap(): return lax.ppermute(x, axis, [(i, i ^ k) for i in range(size)])  33.6 us
    pallas_call x38, Pallas kernels, kernel(): pl.pallas_call(fn, out_shape=[jax.ShapeDtypeStruct(*o) for o in outs], in...  24.6 us
    ppermute x4, waiting for transfers between devices, sum_front(): lax.ppermute(total, 'front', pairs)  13.8 us
    ppermute x4, starting transfers between devices, sum_front(): lax.ppermute(total, 'front', pairs)  6.28 us
  transfers between devices with their start and end apart: 53, of which 32 were waited for; matrix products, arithmetic and copies ran while one was open for 0% of the time, Pallas kernels for 12%

profile of v7, /device:TPU:0, one launch (start us, length us, event | category | flops | bytes accessed | tf_op | source)
XLA Modules:
  0.0 122.5 jit_solution(11382997462479347818)
XLA Ops:
  1.7 3.1 %collective-permute-start = (f32[32,128]{1,0:T(8,128)S(1)}, f32[32,128]{1,0:T(8,128)S(1)}, u32[]{:S(2)}, u32[]{:S(2)}) collective-permute-start(f32[32,128]{1,0:T(8,128)S(1)} %get-tuple-element.63), channel_id=1, source_target_pairs={{0,8},{8,0},{16,24},{24,16},{1,9},{9,1},{17,25},{25,17},{2,10},{10... | collective-permute-start | bytes 49160 | tf_op jit(solution)/shard_map/right_hand_sides/ppermute | solution.py:90
  4.8 1.7 %collective-permute-done.came.near = f32[32,128]{1,0:T(8,128)S(1)} collective-permute-done((f32[32,128]{1,0:T(8,128)S(1)}, f32[32,128]{1,0:T(8,128)S(1)}, u32[]{:S(2)}, u32[]{:S(2)}) %collective-permute-start) | collective-permute-done | bytes 16416 | tf_op jit(solution)/shard_map/right_hand_sides/ppermute | solution.py:90
  6.5 3.0 %collective-permute-start.1 = (f32[32,128]{1,0:T(8,128)S(1)}, f32[32,128]{1,0:T(8,128)S(1)}, u32[]{:S(2)}, u32[]{:S(2)}) collective-permute-start(f32[32,128]{1,0:T(8,128)S(1)} %right_hand_sides.6), channel_id=1, source_target_pairs={{0,16},{8,24},{16,0},{24,8},{1,17},{9,25},{17,1},{25,9},{2,18},{10... | collective-permute-start | bytes 49160 | tf_op jit(solution)/shard_map/right_hand_sides/ppermute | solution.py:90
  11.3 1.9 %collective-permute-start.5 = (f32[72,128]{1,0:T(8,128)S(1)}, f32[72,128]{1,0:T(8,128)S(1)}, u32[]{:S(2)}, u32[]{:S(2)}) collective-permute-start(f32[72,128]{1,0:T(8,128)S(1)} %right_hand_sides.7.refs_0_), channel_id=1, source_target_pairs={{0,2},{1,3},{2,0},{3,1},{4,6},{5,7},{6,4},{7,5},{8,10},{9,11},{10,... | collective-permute-start | bytes 110600 | tf_op jit(solution)/shard_map/leaf_lower/ppermute | solution.py:90
  17.7 1.9 %collective-permute-done.3.refs_2_ = f32[72,128]{1,0:T(8,128)S(1)} collective-permute-done((f32[72,128]{1,0:T(8,128)S(1)}, f32[72,128]{1,0:T(8,128)S(1)}, u32[]{:S(2)}, u32[]{:S(2)}) %collective-permute-start.3) | collective-permute-done | bytes 36896 | tf_op jit(solution)/shard_map/leaf_lower/ppermute | solution.py:90
  22.3 2.8 %collective-permute-start.9 = (f32[64,128]{1,0:T(8,128)S(1)}, f32[64,128]{1,0:T(8,128)S(1)}, u32[]{:S(2)}, u32[]{:S(2)}) collective-permute-start(f32[64,128]{1,0:T(8,128)S(1)} %leaf_lower.5.refs_0_), channel_id=1, source_target_pairs={{0,6},{1,7},{2,4},{3,5},{4,2},{5,3},{6,0},{7,1},{8,14},{9,15},{10,... | collective-permute-start | bytes 98312 | tf_op jit(solution)/shard_map/mid_lower/ppermute | solution.py:90
  25.1 1.6 %mid_lower.8 = (bf16[512,1024]{1,0:T(8,128)(2,1)S(1)}, bf16[256,2048]{1,0:T(8,128)(2,1)S(1)}) custom-call(f32[2,1,256,512]{3,2,1,0:T(8,128)} %refs_0_.1, f32[2,2,128,1024]{3,2,1,0:T(8,128)} %refs_1_.5), custom_call_target="tpu_custom_call" | custom-call | flops 262144000 | bytes 374491 | tf_op jit(solution)/shard_map/mid_lower/pallas_call | solution.py:125
  29.1 1.8 %collective-permute-start.14 = (f32[64,128]{1,0:T(8,128)S(1)}, f32[64,128]{1,0:T(8,128)S(1)}, u32[]{:S(2)}, u32[]{:S(2)}) collective-permute-start(f32[64,128]{1,0:T(8,128)S(1)} %get-tuple-element.77), channel_id=1, source_target_pairs={{0,8},{8,0},{16,24},{24,16},{1,9},{9,1},{17,25},{25,17},{2,10},{10... | collective-permute-start | bytes 98312 | tf_op jit(solution)/shard_map/mid_lower/ppermute | solution.py:90
  31.5 1.6 %collective-permute-done.14.refs_1_ = f32[64,128]{1,0:T(8,128)S(1)} collective-permute-done((f32[64,128]{1,0:T(8,128)S(1)}, f32[64,128]{1,0:T(8,128)S(1)}, u32[]{:S(2)}, u32[]{:S(2)}) %collective-permute-start.14) | collective-permute-done | bytes 32800 | tf_op jit(solution)/shard_map/mid_lower/ppermute | solution.py:90
  33.1 1.6 %collective-permute-start.18 = (f32[64,128]{1,0:T(8,128)S(1)}, f32[64,128]{1,0:T(8,128)S(1)}, u32[]{:S(2)}, u32[]{:S(2)}) collective-permute-start(f32[64,128]{1,0:T(8,128)S(1)} %mid_lower.12.refs_0_), channel_id=1, source_target_pairs={{0,2},{1,3},{2,0},{3,1},{4,6},{5,7},{6,4},{7,5},{8,10},{9,11},{10,... | collective-permute-start | bytes 98312 | tf_op jit(solution)/shard_map/mid_lower/ppermute | solution.py:90
  36.5 1.6 %mid_lower.13.matrix = bf16[512,2048]{1,0:T(8,128)(2,1)S(1)} custom-call(f32[2,2,256,1024]{3,2,1,0:T(8,128)} %refs_0_.2), custom_call_target="tpu_custom_call" | custom-call | flops 262144000 | bytes 374491 | tf_op jit(solution)/shard_map/mid_lower/pallas_call | solution.py:125
  39.4 1.6 %collective-permute-done.16.refs_2_ = f32[64,128]{1,0:T(8,128)S(1)} collective-permute-done((f32[64,128]{1,0:T(8,128)S(1)}, f32[64,128]{1,0:T(8,128)S(1)}, u32[]{:S(2)}, u32[]{:S(2)}) %collective-permute-start.16) | collective-permute-done | bytes 32800 | tf_op jit(solution)/shard_map/mid_lower/ppermute | solution.py:90
  41.0 1.6 %collective-permute-start.21 = (f32[256,64]{1,0:T(8,128)S(1)}, f32[256,64]{1,0:T(8,128)S(1)}, u32[]{:S(2)}, u32[]{:S(2)}) collective-permute-start(f32[256,64]{1,0:T(8,128)S(1)} %get-tuple-element.84), channel_id=1, source_target_pairs={{0,8},{8,0},{16,24},{24,16},{1,9},{9,1},{17,25},{25,17},{2,10},{10... | collective-permute-start | bytes 196616 | tf_op jit(solution)/shard_map/mid_lower/ppermute | solution.py:90
  44.8 2.4 %collective-permute-start.23 = (f32[64,128]{1,0:T(8,128)S(1)}, f32[64,128]{1,0:T(8,128)S(1)}, u32[]{:S(2)}, u32[]{:S(2)}) collective-permute-start(f32[64,128]{1,0:T(8,128)S(1)} %mid_lower.15.refs_0_), channel_id=1, source_target_pairs={{0,6},{1,7},{2,4},{3,5},{4,2},{5,3},{6,0},{7,1},{8,14},{9,15},{10,... | collective-permute-start | bytes 98312 | tf_op jit(solution)/shard_map/root_cut/ppermute | solution.py:90
  52.1 2.7 %collective-permute-start.28 = (f32[64,128]{1,0:T(8,128)S(1)}, f32[64,128]{1,0:T(8,128)S(1)}, u32[]{:S(2)}, u32[]{:S(2)}) collective-permute-start(f32[64,128]{1,0:T(8,128)S(1)} %get-tuple-element.88), channel_id=1, source_target_pairs={{0,16},{8,24},{16,0},{24,8},{1,17},{9,25},{17,1},{25,9},{2,18},{10... | collective-permute-start | bytes 98312 | tf_op jit(solution)/shard_map/root_cut/ppermute | solution.py:90
  55.4 1.8 %collective-permute-done.28.refs_1_ = f32[64,128]{1,0:T(8,128)S(1)} collective-permute-done((f32[64,128]{1,0:T(8,128)S(1)}, f32[64,128]{1,0:T(8,128)S(1)}, u32[]{:S(2)}, u32[]{:S(2)}) %collective-permute-start.28) | collective-permute-done | bytes 32800 | tf_op jit(solution)/shard_map/root_cut/ppermute | solution.py:90
  63.3 1.7 %collective-permute-done.30.refs_2_ = f32[64,128]{1,0:T(8,128)S(1)} collective-permute-done((f32[64,128]{1,0:T(8,128)S(1)}, f32[64,128]{1,0:T(8,128)S(1)}, u32[]{:S(2)}, u32[]{:S(2)}) %collective-permute-start.30) | collective-permute-done | bytes 32800 | tf_op jit(solution)/shard_map/root_solve/ppermute | solution.py:90
  66.2 1.9 %root_solve.8.refs_0_ = f32[64,128]{1,0:T(8,128)S(1)} custom-call(bf16[512,4096]{1,0:T(8,128)(2,1)S(1)} %root_cut.5.matrix, f32[64,128]{1,0:T(8,128)S(1)} %root_cut.9.refs_0_, f32[64,128]{1,0:T(8,128)S(1)} %collective-permute-done.29.refs_1_, f32[64,128]{1,0:T(8,128)S(1)} %collective-permute-done.30.refs_2_, ...), custom_call_target="tpu_custom_call" | custom-call | tf_op jit(solution)/shard_map/root_solve/pallas_call | solution.py:125
  69.2 2.5 %collective-permute-start.36 = (f32[64,128]{1,0:T(8,128)S(1)}, f32[64,128]{1,0:T(8,128)S(1)}, u32[]{:S(2)}, u32[]{:S(2)}) collective-permute-start(f32[64,128]{1,0:T(8,128)S(1)} %root_solve.8.refs_0_), channel_id=1, source_target_pairs={{0,6},{1,7},{2,4},{3,5},{4,2},{5,3},{6,0},{7,1},{8,14},{9,15},{10,... | collective-permute-start | bytes 98312 | tf_op jit(solution)/shard_map/root_solve/ppermute | solution.py:90
  75.2 1.9 %root_solve.11.mine = f32[64,128]{1,0:T(8,128)S(1)} custom-call(bf16[512,4096]{1,0:T(8,128)(2,1)S(1)} %root_solve.6.matrix, f32[64,128]{1,0:T(8,128)S(1)} %root_solve.8.refs_0_, f32[64,128]{1,0:T(8,128)S(1)} %collective-permute-done.35.refs_1_, f32[64,128]{1,0:T(8,128)S(1)} %collective-permute-done.36.refs_2_, ...), custom_call_target="tpu_custom_call" | custom-call | tf_op jit(solution)/shard_map/root_solve/pallas_call | solution.py:125
  77.1 2.5 %collective-permute-start.41 = (f32[64,128]{1,0:T(8,128)S(1)}, f32[64,128]{1,0:T(8,128)S(1)}, u32[]{:S(2)}, u32[]{:S(2)}) collective-permute-start(f32[64,128]{1,0:T(8,128)S(1)} %root_solve.11.mine), channel_id=1, source_target_pairs={{0,16},{8,24},{16,0},{24,8},{1,17},{9,25},{17,1},{25,9},{2,18},{10... | collective-permute-start | bytes 98312 | tf_op jit(solution)/shard_map/mid_upper/ppermute | solution.py:90
  79.6 3.0 %collective-permute-done.41.other = f32[64,128]{1,0:T(8,128)S(1)} collective-permute-done((f32[64,128]{1,0:T(8,128)S(1)}, f32[64,128]{1,0:T(8,128)S(1)}, u32[]{:S(2)}, u32[]{:S(2)}) %collective-permute-start.41) | collective-permute-done | bytes 32800 | tf_op jit(solution)/shard_map/mid_upper/ppermute | solution.py:90
  85.2 1.6 %collective-permute-start.44 = (f32[256,128]{1,0:T(8,128)S(1)}, f32[256,128]{1,0:T(8,128)S(1)}, u32[]{:S(2)}, u32[]{:S(2)}) collective-permute-start(f32[256,128]{1,0:T(8,128)S(1)} %mid_upper.8.refs_0_), channel_id=1, source_target_pairs={{0,2},{1,5},{2,0},{3,7},{4,6},{5,1},{6,4},{7,3},{8,10},{9,13},{10,... | collective-permute-start | bytes 393224 | tf_op jit(solution)/shard_map/mid_upper/ppermute | solution.py:381
  86.8 3.5 %collective-permute-done.44.refs_1_ = f32[256,128]{1,0:T(8,128)S(1)} collective-permute-done((f32[256,128]{1,0:T(8,128)S(1)}, f32[256,128]{1,0:T(8,128)S(1)}, u32[]{:S(2)}, u32[]{:S(2)}) %collective-permute-start.44) | collective-permute-done | bytes 131104 | tf_op jit(solution)/shard_map/mid_upper/ppermute | solution.py:381
  90.3 1.6 %collective-permute-start.45 = (f32[256,128]{1,0:T(8,128)S(1)}, f32[256,128]{1,0:T(8,128)S(1)}, u32[]{:S(2)}, u32[]{:S(2)}) collective-permute-start(f32[256,128]{1,0:T(8,128)S(1)} %mid_upper.9.refs_0_), channel_id=1, source_target_pairs={{0,4},{1,3},{2,6},{3,1},{4,0},{5,7},{6,2},{7,5},{8,12},{9,11},{10,... | collective-permute-start | bytes 393224 | tf_op jit(solution)/shard_map/mid_upper/ppermute | solution.py:381
  91.8 3.4 %collective-permute-done.45.refs_1_ = f32[256,128]{1,0:T(8,128)S(1)} collective-permute-done((f32[256,128]{1,0:T(8,128)S(1)}, f32[256,128]{1,0:T(8,128)S(1)}, u32[]{:S(2)}, u32[]{:S(2)}) %collective-permute-start.45) | collective-permute-done | bytes 131104 | tf_op jit(solution)/shard_map/mid_upper/ppermute | solution.py:381
  103.7 1.6 %collective-permute-start.49 = (f32[256,128]{1,0:T(8,128)S(1)}, f32[256,128]{1,0:T(8,128)S(1)}, u32[]{:S(2)}, u32[]{:S(2)}) collective-permute-start(f32[256,128]{1,0:T(8,128)S(1)} %leaf_upper.7.refs_0_), channel_id=1, source_target_pairs={{0,2},{1,5},{2,0},{3,7},{4,6},{5,1},{6,4},{7,3},{8,10},{9,13},{10,... | collective-permute-start | bytes 393224 | tf_op jit(solution)/shard_map/leaf_upper/ppermute | solution.py:381
  105.2 3.5 %collective-permute-done.49.refs_1_ = f32[256,128]{1,0:T(8,128)S(1)} collective-permute-done((f32[256,128]{1,0:T(8,128)S(1)}, f32[256,128]{1,0:T(8,128)S(1)}, u32[]{:S(2)}, u32[]{:S(2)}) %collective-permute-start.49) | collective-permute-done | bytes 131104 | tf_op jit(solution)/shard_map/leaf_upper/ppermute | solution.py:381
  108.7 1.6 %collective-permute-start.50 = (f32[256,128]{1,0:T(8,128)S(1)}, f32[256,128]{1,0:T(8,128)S(1)}, u32[]{:S(2)}, u32[]{:S(2)}) collective-permute-start(f32[256,128]{1,0:T(8,128)S(1)} %leaf_upper.8.refs_0_), channel_id=1, source_target_pairs={{0,4},{1,3},{2,6},{3,1},{4,0},{5,7},{6,2},{7,5},{8,12},{9,11},{10,... | collective-permute-start | bytes 393224 | tf_op jit(solution)/shard_map/leaf_upper/ppermute | solution.py:381
  110.3 3.5 %collective-permute-done.50.refs_1_ = f32[256,128]{1,0:T(8,128)S(1)} collective-permute-done((f32[256,128]{1,0:T(8,128)S(1)}, f32[256,128]{1,0:T(8,128)S(1)}, u32[]{:S(2)}, u32[]{:S(2)}) %collective-permute-start.50) | collective-permute-done | bytes 131104 | tf_op jit(solution)/shard_map/leaf_upper/ppermute | solution.py:381
  113.8 2.4 %collective-permute-start.52 = (f32[128,128]{1,0:T(8,128)S(1)}, f32[128,128]{1,0:T(8,128)S(1)}, u32[]{:S(2)}, u32[]{:S(2)}) collective-permute-start(f32[128,128]{1,0:T(8,128)S(1)} %get-tuple-element.110.mine), channel_id=1, source_target_pairs={{0,16},{8,24},{16,0},{24,8},{1,17},{9,25},{17,1},{25,9},{2,18},{10... | collective-permute-start | bytes 196616 | tf_op jit(solution)/shard_map/leaf_upper/ppermute | solution.py:90
  116.2 4.4 %collective-permute-done.52.other = f32[128,128]{1,0:T(8,128)S(1)} collective-permute-done((f32[128,128]{1,0:T(8,128)S(1)}, f32[128,128]{1,0:T(8,128)S(1)}, u32[]{:S(2)}, u32[]{:S(2)}) %collective-permute-start.52) | collective-permute-done | bytes 65568 | tf_op jit(solution)/shard_map/leaf_upper/ppermute | solution.py:90
  (126 shorter events, 48.2 us)
Async XLA Ops:
  1.7 4.8 %collective-permute-start = (f32[32,128]{1,0:T(8,128)S(1)}, f32[32,128]{1,0:T(8,128)S(1)}, u32[]{:S(2)}, u32[]{:S(2)}) collective-permute-start(f32[32,128]{1,0:T(8,128)S(1)} %get-tuple-element.63), channel_id=1, source_target_pairs={{0,8},{8,0},{16,24},{24,16},{1,9},{9,1},{17,25},{25,17},{2,10},{10... | collective-permute-start | bytes 49160 | tf_op jit(solution)/shard_map/right_hand_sides/ppermute | solution.py:90
  6.5 4.7 %collective-permute-start.1 = (f32[32,128]{1,0:T(8,128)S(1)}, f32[32,128]{1,0:T(8,128)S(1)}, u32[]{:S(2)}, u32[]{:S(2)}) collective-permute-start(f32[32,128]{1,0:T(8,128)S(1)} %right_hand_sides.6), channel_id=1, source_target_pairs={{0,16},{8,24},{16,0},{24,8},{1,17},{9,25},{17,1},{25,9},{2,18},{10... | collective-permute-start | bytes 49160 | tf_op jit(solution)/shard_map/right_hand_sides/ppermute | solution.py:90
  11.3 4.9 %collective-permute-start.5 = (f32[72,128]{1,0:T(8,128)S(1)}, f32[72,128]{1,0:T(8,128)S(1)}, u32[]{:S(2)}, u32[]{:S(2)}) collective-permute-start(f32[72,128]{1,0:T(8,128)S(1)} %right_hand_sides.7.refs_0_), channel_id=1, source_target_pairs={{0,2},{1,3},{2,0},{3,1},{4,6},{5,7},{6,4},{7,5},{8,10},{9,11},{10,... | collective-permute-start | bytes 110600 | tf_op jit(solution)/shard_map/leaf_lower/ppermute | solution.py:90
  13.2 4.0 %collective-permute-start.4 = (f32[72,128]{1,0:T(8,128)S(1)}, f32[72,128]{1,0:T(8,128)S(1)}, u32[]{:S(2)}, u32[]{:S(2)}) collective-permute-start(f32[72,128]{1,0:T(8,128)S(1)} %right_hand_sides.7.refs_0_), channel_id=1, source_target_pairs={{0,4},{1,5},{2,6},{3,7},{4,0},{5,1},{6,2},{7,3},{8,12},{9,13},{10,... | collective-permute-start | bytes 110600 | tf_op jit(solution)/shard_map/leaf_lower/ppermute | solution.py:90
  14.7 4.9 %collective-permute-start.3 = (f32[72,128]{1,0:T(8,128)S(1)}, f32[72,128]{1,0:T(8,128)S(1)}, u32[]{:S(2)}, u32[]{:S(2)}) collective-permute-start(f32[72,128]{1,0:T(8,128)S(1)} %right_hand_sides.7.refs_0_), channel_id=1, source_target_pairs={{0,6},{1,7},{2,4},{3,5},{4,2},{5,3},{6,0},{7,1},{8,14},{9,15},{10,... | collective-permute-start | bytes 110600 | tf_op jit(solution)/shard_map/leaf_lower/ppermute | solution.py:90
  21.5 5.2 %collective-permute-start.11 = (f32[64,128]{1,0:T(8,128)S(1)}, f32[64,128]{1,0:T(8,128)S(1)}, u32[]{:S(2)}, u32[]{:S(2)}) collective-permute-start(f32[64,128]{1,0:T(8,128)S(1)} %leaf_lower.5.refs_0_), channel_id=1, source_target_pairs={{0,2},{1,3},{2,0},{3,1},{4,6},{5,7},{6,4},{7,5},{8,10},{9,11},{10,... | collective-permute-start | bytes 98312 | tf_op jit(solution)/shard_map/mid_lower/ppermute | solution.py:90
  22.1 4.6 %collective-permute-start.10 = (f32[64,128]{1,0:T(8,128)S(1)}, f32[64,128]{1,0:T(8,128)S(1)}, u32[]{:S(2)}, u32[]{:S(2)}) collective-permute-start(f32[64,128]{1,0:T(8,128)S(1)} %leaf_lower.5.refs_0_), channel_id=1, source_target_pairs={{0,4},{1,5},{2,6},{3,7},{4,0},{5,1},{6,2},{7,3},{8,12},{9,13},{10,... | collective-permute-start | bytes 98312 | tf_op jit(solution)/shard_map/mid_lower/ppermute | solution.py:90
  22.3 5.0 %collective-permute-start.9 = (f32[64,128]{1,0:T(8,128)S(1)}, f32[64,128]{1,0:T(8,128)S(1)}, u32[]{:S(2)}, u32[]{:S(2)}) collective-permute-start(f32[64,128]{1,0:T(8,128)S(1)} %leaf_lower.5.refs_0_), channel_id=1, source_target_pairs={{0,6},{1,7},{2,4},{3,5},{4,2},{5,3},{6,0},{7,1},{8,14},{9,15},{10,... | collective-permute-start | bytes 98312 | tf_op jit(solution)/shard_map/mid_lower/ppermute | solution.py:90
  29.1 4.0 %collective-permute-start.14 = (f32[64,128]{1,0:T(8,128)S(1)}, f32[64,128]{1,0:T(8,128)S(1)}, u32[]{:S(2)}, u32[]{:S(2)}) collective-permute-start(f32[64,128]{1,0:T(8,128)S(1)} %get-tuple-element.77), channel_id=1, source_target_pairs={{0,8},{8,0},{16,24},{24,16},{1,9},{9,1},{17,25},{25,17},{2,10},{10... | collective-permute-start | bytes 98312 | tf_op jit(solution)/shard_map/mid_lower/ppermute | solution.py:90
  33.1 5.1 %collective-permute-start.18 = (f32[64,128]{1,0:T(8,128)S(1)}, f32[64,128]{1,0:T(8,128)S(1)}, u32[]{:S(2)}, u32[]{:S(2)}) collective-permute-start(f32[64,128]{1,0:T(8,128)S(1)} %mid_lower.12.refs_0_), channel_id=1, source_target_pairs={{0,2},{1,3},{2,0},{3,1},{4,6},{5,7},{6,4},{7,5},{8,10},{9,11},{10,... | collective-permute-start | bytes 98312 | tf_op jit(solution)/shard_map/mid_lower/ppermute | solution.py:90
  34.7 4.2 %collective-permute-start.17 = (f32[64,128]{1,0:T(8,128)S(1)}, f32[64,128]{1,0:T(8,128)S(1)}, u32[]{:S(2)}, u32[]{:S(2)}) collective-permute-start(f32[64,128]{1,0:T(8,128)S(1)} %mid_lower.12.refs_0_), channel_id=1, source_target_pairs={{0,4},{1,5},{2,6},{3,7},{4,0},{5,1},{6,2},{7,3},{8,12},{9,13},{10,... | collective-permute-start | bytes 98312 | tf_op jit(solution)/shard_map/mid_lower/ppermute | solution.py:90
  36.2 4.8 %collective-permute-start.16 = (f32[64,128]{1,0:T(8,128)S(1)}, f32[64,128]{1,0:T(8,128)S(1)}, u32[]{:S(2)}, u32[]{:S(2)}) collective-permute-start(f32[64,128]{1,0:T(8,128)S(1)} %mid_lower.12.refs_0_), channel_id=1, source_target_pairs={{0,6},{1,7},{2,4},{3,5},{4,2},{5,3},{6,0},{7,1},{8,14},{9,15},{10,... | collective-permute-start | bytes 98312 | tf_op jit(solution)/shard_map/mid_lower/ppermute | solution.py:90
  41.0 8.6 %collective-permute-start.21 = (f32[256,64]{1,0:T(8,128)S(1)}, f32[256,64]{1,0:T(8,128)S(1)}, u32[]{:S(2)}, u32[]{:S(2)}) collective-permute-start(f32[256,64]{1,0:T(8,128)S(1)} %get-tuple-element.84), channel_id=1, source_target_pairs={{0,8},{8,0},{16,24},{24,16},{1,9},{9,1},{17,25},{25,17},{2,10},{10... | collective-permute-start | bytes 196616 | tf_op jit(solution)/shard_map/mid_lower/ppermute | solution.py:90
  43.7 4.7 %collective-permute-start.25 = (f32[64,128]{1,0:T(8,128)S(1)}, f32[64,128]{1,0:T(8,128)S(1)}, u32[]{:S(2)}, u32[]{:S(2)}) collective-permute-start(f32[64,128]{1,0:T(8,128)S(1)} %mid_lower.15.refs_0_), channel_id=1, source_target_pairs={{0,2},{1,3},{2,0},{3,1},{4,6},{5,7},{6,4},{7,5},{8,10},{9,11},{10,... | collective-permute-start | bytes 98312 | tf_op jit(solution)/shard_map/root_cut/ppermute | solution.py:90
  44.3 4.3 %collective-permute-start.24 = (f32[64,128]{1,0:T(8,128)S(1)}, f32[64,128]{1,0:T(8,128)S(1)}, u32[]{:S(2)}, u32[]{:S(2)}) collective-permute-start(f32[64,128]{1,0:T(8,128)S(1)} %mid_lower.15.refs_0_), channel_id=1, source_target_pairs={{0,4},{1,5},{2,6},{3,7},{4,0},{5,1},{6,2},{7,3},{8,12},{9,13},{10,... | collective-permute-start | bytes 98312 | tf_op jit(solution)/shard_map/root_cut/ppermute | solution.py:90
  44.8 4.8 %collective-permute-start.23 = (f32[64,128]{1,0:T(8,128)S(1)}, f32[64,128]{1,0:T(8,128)S(1)}, u32[]{:S(2)}, u32[]{:S(2)}) collective-permute-start(f32[64,128]{1,0:T(8,128)S(1)} %mid_lower.15.refs_0_), channel_id=1, source_target_pairs={{0,6},{1,7},{2,4},{3,5},{4,2},{5,3},{6,0},{7,1},{8,14},{9,15},{10,... | collective-permute-start | bytes 98312 | tf_op jit(solution)/shard_map/root_cut/ppermute | solution.py:90
  52.1 5.1 %collective-permute-start.28 = (f32[64,128]{1,0:T(8,128)S(1)}, f32[64,128]{1,0:T(8,128)S(1)}, u32[]{:S(2)}, u32[]{:S(2)}) collective-permute-start(f32[64,128]{1,0:T(8,128)S(1)} %get-tuple-element.88), channel_id=1, source_target_pairs={{0,16},{8,24},{16,0},{24,8},{1,17},{9,25},{17,1},{25,9},{2,18},{10... | collective-permute-start | bytes 98312 | tf_op jit(solution)/shard_map/root_cut/ppermute | solution.py:90
  57.2 4.6 %collective-permute-start.32 = (f32[64,128]{1,0:T(8,128)S(1)}, f32[64,128]{1,0:T(8,128)S(1)}, u32[]{:S(2)}, u32[]{:S(2)}) collective-permute-start(f32[64,128]{1,0:T(8,128)S(1)} %root_cut.9.refs_0_), channel_id=1, source_target_pairs={{0,2},{1,3},{2,0},{3,1},{4,6},{5,7},{6,4},{7,5},{8,10},{9,11},{10,... | collective-permute-start | bytes 98312 | tf_op jit(solution)/shard_map/root_solve/ppermute | solution.py:90
  58.7 4.1 %collective-permute-start.31 = (f32[64,128]{1,0:T(8,128)S(1)}, f32[64,128]{1,0:T(8,128)S(1)}, u32[]{:S(2)}, u32[]{:S(2)}) collective-permute-start(f32[64,128]{1,0:T(8,128)S(1)} %root_cut.9.refs_0_), channel_id=1, source_target_pairs={{0,4},{1,5},{2,6},{3,7},{4,0},{5,1},{6,2},{7,3},{8,12},{9,13},{10,... | collective-permute-start | bytes 98312 | tf_op jit(solution)/shard_map/root_solve/ppermute | solution.py:90
  60.2 4.8 %collective-permute-start.30 = (f32[64,128]{1,0:T(8,128)S(1)}, f32[64,128]{1,0:T(8,128)S(1)}, u32[]{:S(2)}, u32[]{:S(2)}) collective-permute-start(f32[64,128]{1,0:T(8,128)S(1)} %root_cut.9.refs_0_), channel_id=1, source_target_pairs={{0,6},{1,7},{2,4},{3,5},{4,2},{5,3},{6,0},{7,1},{8,14},{9,15},{10,... | collective-permute-start | bytes 98312 | tf_op jit(solution)/shard_map/root_solve/ppermute | solution.py:90
  68.1 5.0 %collective-permute-start.38 = (f32[64,128]{1,0:T(8,128)S(1)}, f32[64,128]{1,0:T(8,128)S(1)}, u32[]{:S(2)}, u32[]{:S(2)}) collective-permute-start(f32[64,128]{1,0:T(8,128)S(1)} %root_solve.8.refs_0_), channel_id=1, source_target_pairs={{0,2},{1,3},{2,0},{3,1},{4,6},{5,7},{6,4},{7,5},{8,10},{9,11},{10,... | collective-permute-start | bytes 98312 | tf_op jit(solution)/shard_map/root_solve/ppermute | solution.py:90
  68.7 4.4 %collective-permute-start.37 = (f32[64,128]{1,0:T(8,128)S(1)}, f32[64,128]{1,0:T(8,128)S(1)}, u32[]{:S(2)}, u32[]{:S(2)}) collective-permute-start(f32[64,128]{1,0:T(8,128)S(1)} %root_solve.8.refs_0_), channel_id=1, source_target_pairs={{0,4},{1,5},{2,6},{3,7},{4,0},{5,1},{6,2},{7,3},{8,12},{9,13},{10,... | collective-permute-start | bytes 98312 | tf_op jit(solution)/shard_map/root_solve/ppermute | solution.py:90
  69.2 4.8 %collective-permute-start.36 = (f32[64,128]{1,0:T(8,128)S(1)}, f32[64,128]{1,0:T(8,128)S(1)}, u32[]{:S(2)}, u32[]{:S(2)}) collective-permute-start(f32[64,128]{1,0:T(8,128)S(1)} %root_solve.8.refs_0_), channel_id=1, source_target_pairs={{0,6},{1,7},{2,4},{3,5},{4,2},{5,3},{6,0},{7,1},{8,14},{9,15},{10,... | collective-permute-start | bytes 98312 | tf_op jit(solution)/shard_map/root_solve/ppermute | solution.py:90
  77.1 5.6 %collective-permute-start.41 = (f32[64,128]{1,0:T(8,128)S(1)}, f32[64,128]{1,0:T(8,128)S(1)}, u32[]{:S(2)}, u32[]{:S(2)}) collective-permute-start(f32[64,128]{1,0:T(8,128)S(1)} %root_solve.11.mine), channel_id=1, source_target_pairs={{0,16},{8,24},{16,0},{24,8},{1,17},{9,25},{17,1},{25,9},{2,18},{10... | collective-permute-start | bytes 98312 | tf_op jit(solution)/shard_map/mid_upper/ppermute | solution.py:90
  85.2 5.0 %collective-permute-start.44 = (f32[256,128]{1,0:T(8,128)S(1)}, f32[256,128]{1,0:T(8,128)S(1)}, u32[]{:S(2)}, u32[]{:S(2)}) collective-permute-start(f32[256,128]{1,0:T(8,128)S(1)} %mid_upper.8.refs_0_), channel_id=1, source_target_pairs={{0,2},{1,5},{2,0},{3,7},{4,6},{5,1},{6,4},{7,3},{8,10},{9,13},{10,... | collective-permute-start | bytes 393224 | tf_op jit(solution)/shard_map/mid_upper/ppermute | solution.py:381
  90.3 5.0 %collective-permute-start.45 = (f32[256,128]{1,0:T(8,128)S(1)}, f32[256,128]{1,0:T(8,128)S(1)}, u32[]{:S(2)}, u32[]{:S(2)}) collective-permute-start(f32[256,128]{1,0:T(8,128)S(1)} %mid_upper.9.refs_0_), channel_id=1, source_target_pairs={{0,4},{1,3},{2,6},{3,1},{4,0},{5,7},{6,2},{7,5},{8,12},{9,11},{10,... | collective-permute-start | bytes 393224 | tf_op jit(solution)/shard_map/mid_upper/ppermute | solution.py:381
  95.4 4.5 %collective-permute-start.42 = (f32[128,128]{1,0:T(8,128)S(1)}, f32[128,128]{1,0:T(8,128)S(1)}, u32[]{:S(2)}, u32[]{:S(2)}) collective-permute-start(f32[128,128]{1,0:T(8,128)S(1)} %get-tuple-element.102.mine), channel_id=1, source_target_pairs={{0,8},{8,0},{16,24},{24,16},{1,9},{9,1},{17,25},{25,17},{2,10},{10... | collective-permute-start | bytes 196616 | tf_op jit(solution)/shard_map/mid_upper/ppermute | solution.py:90
  97.7 4.0 %collective-permute-start.47 = (f32[64,128]{1,0:T(8,128)S(1)}, f32[64,128]{1,0:T(8,128)S(1)}, u32[]{:S(2)}, u32[]{:S(2)}) collective-permute-start(f32[64,128]{1,0:T(8,128)S(1)} %mid_upper.11.mine), channel_id=1, source_target_pairs={{0,8},{8,0},{16,24},{24,16},{1,9},{9,1},{17,25},{25,17},{2,10},{10... | collective-permute-start | bytes 98312 | tf_op jit(solution)/shard_map/leaf_upper/ppermute | solution.py:90
  103.7 5.0 %collective-permute-start.49 = (f32[256,128]{1,0:T(8,128)S(1)}, f32[256,128]{1,0:T(8,128)S(1)}, u32[]{:S(2)}, u32[]{:S(2)}) collective-permute-start(f32[256,128]{1,0:T(8,128)S(1)} %leaf_upper.7.refs_0_), channel_id=1, source_target_pairs={{0,2},{1,5},{2,0},{3,7},{4,6},{5,1},{6,4},{7,3},{8,10},{9,13},{10,... | collective-permute-start | bytes 393224 | tf_op jit(solution)/shard_map/leaf_upper/ppermute | solution.py:381
  108.7 5.0 %collective-permute-start.50 = (f32[256,128]{1,0:T(8,128)S(1)}, f32[256,128]{1,0:T(8,128)S(1)}, u32[]{:S(2)}, u32[]{:S(2)}) collective-permute-start(f32[256,128]{1,0:T(8,128)S(1)} %leaf_upper.8.refs_0_), channel_id=1, source_target_pairs={{0,4},{1,3},{2,6},{3,1},{4,0},{5,7},{6,2},{7,5},{8,12},{9,11},{10,... | collective-permute-start | bytes 393224 | tf_op jit(solution)/shard_map/leaf_upper/ppermute | solution.py:381
  113.8 7.6 %collective-permute-start.51 = (f32[256,128]{1,0:T(8,128)S(1)}, f32[256,128]{1,0:T(8,128)S(1)}, u32[]{:S(2)}, u32[]{:S(2)}) collective-permute-start(f32[256,128]{1,0:T(8,128)S(1)} %leaf_upper.9.refs_0_), channel_id=1, source_target_pairs={{0,1},{1,0},{2,3},{3,2},{4,5},{5,4},{6,7},{7,6},{8,9},{9,8},{10,11... | collective-permute-start | bytes 393224 | tf_op jit(solution)/shard_map/leaf_upper/ppermute | solution.py:90
  113.8 6.8 %collective-permute-start.52 = (f32[128,128]{1,0:T(8,128)S(1)}, f32[128,128]{1,0:T(8,128)S(1)}, u32[]{:S(2)}, u32[]{:S(2)}) collective-permute-start(f32[128,128]{1,0:T(8,128)S(1)} %get-tuple-element.110.mine), channel_id=1, source_target_pairs={{0,16},{8,24},{16,0},{24,8},{1,17},{9,25},{17,1},{25,9},{2,18},{10... | collective-permute-start | bytes 196616 | tf_op jit(solution)/shard_map/leaf_upper/ppermute | solution.py:90
  (28 other events, 122.5 us)

commit v8 on v7

--- a/solution.py
+++ b/solution.py
@@ -100,12 +100,13 @@
 def gather_front(x, meanwhile=None):
     fronts = lax.axis_size("front")
     mine = [swap("front", x, k) for k in range(2, fronts, 2)]
-    extra = tuple(meanwhile(x)) if meanwhile else ()
+    own = swap("front", x, 1)
+    extra = tuple(meanwhile(own)) if meanwhile else ()
     near, last = mine[:-1], mine[-1]
     if extra:
         near = [after(near[0], *extra), *near[1:]]
     (both,) = kernel(stack, [(len(near) * x.shape[0], LANES)], *near)
-    return [x, swap("front", x, 1), last, *near[::-1], swap("front", last, 1), swap("front", both, 1)], extra
+    return [x, own, last, *near[::-1], swap("front", last, 1), swap("front", both, 1)], extra
 
 
 def blocks_of(parts):
@@ -372,14 +373,14 @@
     fields_of(x, forward, adjoint, ())
 
 
-def sum_front(kept, sent):
+def sum_front(kept, sent, *others):
     fronts = lax.axis_size("front")
     (total,) = kernel(add, [kept.shape], kept, swap("front", sent, 1))
     hops = [1 << i for i in range(1, fronts.bit_length() - 1)]
     for hop, back in zip(hops, hops[::-1]):
         pairs = [(i, i ^ (back if i & 1 else hop)) for i in range(fronts)]
         (total,) = kernel(add, [kept.shape], total, lax.ppermute(total, "front", pairs))
-    return [total, swap("front", total, 1)]
+    return [total, swap("front", after(total, *others), 1)]
 
 
 def summed(pieces):
@@ -578,9 +579,9 @@
             x_mid,
             swap("leaf", x_mid, 1),
         )
-        pieces = sum_front(keep, send)
-        x_other = swap("leaf", after(x_mid, send), 2)
+        x_other = swap("leaf", x_mid, 2)
         mid_field, mid_adjoint = kernel(mid_outputs, [(2, 2, COLS, n1)] * 2, x_mid, x_other)
+        pieces = sum_front(keep, send, mid_field)
         leaf_field, leaf_adjoint = kernel(leaf_upper, [(2, COLS, n0)] * 2, lu, y_full, *pieces)
     return tuple(
         jnp.swapaxes(x, -1, -2)

time: 123 us -> 121 us (0.984)
  starting transfers between devices: 49.4 us -> 47.9 us
    ppermute x4, waiting for transfers between devices: 13.8 us -> 9.94 us  [sum_front(): lax.ppermute(total, 'front', pairs)]
    ppermute x49, waiting for transfers between devices: 33.6 us -> 37.2 us  [swap(): return lax.ppermute(x, axis, [(i, i ^ k) for i in range(size)])]
    ppermute x49, starting transfers between devices: 43.1 us -> 40.9 us  [swap(): return lax.ppermute(x, axis, [(i, i ^ k) for i in range(size)])]
  transfers between devices with their start and end apart: 53 -> 53, of which waited for: 32 -> 31; matrix products, arithmetic and copies ran while one was open for 0% -> 0% of each run, Pallas kernels for 12% -> 11%
where the time goes in v8:
time: 121 us
  starting transfers between devices  47.9 us (40%)
  waiting for transfers between devices  47.1 us (39%)
  Pallas kernels  24.6 us (20%)
    ppermute x49, starting transfers between devices, swap(): return lax.ppermute(x, axis, [(i, i ^ k) for i in range(size)])  40.9 us
    ppermute x49, waiting for transfers between devices, swap(): return lax.ppermute(x, axis, [(i, i ^ k) for i in range(size)])  37.2 us
    pallas_call x38, Pallas kernels, kernel(): pl.pallas_call(fn, out_shape=[jax.ShapeDtypeStruct(*o) for o in outs], in...  24.6 us
    ppermute x4, waiting for transfers between devices, sum_front(): lax.ppermute(total, 'front', pairs)  9.94 us
    ppermute x4, starting transfers between devices, sum_front(): lax.ppermute(total, 'front', pairs)  6.92 us
  transfers between devices with their start and end apart: 53, of which 31 were waited for; matrix products, arithmetic and copies ran while one was open for 0% of the time, Pallas kernels for 11%

profile of v8, /device:TPU:0, one launch (start us, length us, event | category | flops | bytes accessed | tf_op | source)
XLA Modules:
  0.0 120.7 jit_solution(11351194317511033253)
XLA Ops:
  1.7 3.1 %collective-permute-start = (f32[32,128]{1,0:T(8,128)S(1)}, f32[32,128]{1,0:T(8,128)S(1)}, u32[]{:S(2)}, u32[]{:S(2)}) collective-permute-start(f32[32,128]{1,0:T(8,128)S(1)} %get-tuple-element.63), channel_id=1, source_target_pairs={{0,8},{8,0},{16,24},{24,16},{1,9},{9,1},{17,25},{25,17},{2,10},{10... | collective-permute-start | bytes 49160 | tf_op jit(solution)/shard_map/right_hand_sides/ppermute | solution.py:90
  4.8 1.7 %collective-permute-done.came.near = f32[32,128]{1,0:T(8,128)S(1)} collective-permute-done((f32[32,128]{1,0:T(8,128)S(1)}, f32[32,128]{1,0:T(8,128)S(1)}, u32[]{:S(2)}, u32[]{:S(2)}) %collective-permute-start) | collective-permute-done | bytes 16416 | tf_op jit(solution)/shard_map/right_hand_sides/ppermute | solution.py:90
  6.5 3.0 %collective-permute-start.1 = (f32[32,128]{1,0:T(8,128)S(1)}, f32[32,128]{1,0:T(8,128)S(1)}, u32[]{:S(2)}, u32[]{:S(2)}) collective-permute-start(f32[32,128]{1,0:T(8,128)S(1)} %right_hand_sides.6), channel_id=1, source_target_pairs={{0,16},{8,24},{16,0},{24,8},{1,17},{9,25},{17,1},{25,9},{2,18},{10... | collective-permute-start | bytes 49160 | tf_op jit(solution)/shard_map/right_hand_sides/ppermute | solution.py:90
  11.4 1.9 %collective-permute-start.5 = (f32[72,128]{1,0:T(8,128)S(1)}, f32[72,128]{1,0:T(8,128)S(1)}, u32[]{:S(2)}, u32[]{:S(2)}) collective-permute-start(f32[72,128]{1,0:T(8,128)S(1)} %right_hand_sides.7.refs_0_), channel_id=1, source_target_pairs={{0,2},{1,3},{2,0},{3,1},{4,6},{5,7},{6,4},{7,5},{8,10},{9,11},{10,... | collective-permute-start | bytes 110600 | tf_op jit(solution)/shard_map/leaf_lower/ppermute | solution.py:90
  13.3 1.5 %collective-permute-start.4 = (f32[72,128]{1,0:T(8,128)S(1)}, f32[72,128]{1,0:T(8,128)S(1)}, u32[]{:S(2)}, u32[]{:S(2)}) collective-permute-start(f32[72,128]{1,0:T(8,128)S(1)} %right_hand_sides.7.refs_0_), channel_id=1, source_target_pairs={{0,4},{1,5},{2,6},{3,7},{4,0},{5,1},{6,2},{7,3},{8,12},{9,13},{10,... | collective-permute-start | bytes 110600 | tf_op jit(solution)/shard_map/leaf_lower/ppermute | solution.py:90
  17.3 2.4 %collective-permute-done.3.refs_2_ = f32[72,128]{1,0:T(8,128)S(1)} collective-permute-done((f32[72,128]{1,0:T(8,128)S(1)}, f32[72,128]{1,0:T(8,128)S(1)}, u32[]{:S(2)}, u32[]{:S(2)}) %collective-permute-start.3) | collective-permute-done | bytes 36896 | tf_op jit(solution)/shard_map/leaf_lower/ppermute | solution.py:90
  22.5 2.8 %collective-permute-start.9 = (f32[64,128]{1,0:T(8,128)S(1)}, f32[64,128]{1,0:T(8,128)S(1)}, u32[]{:S(2)}, u32[]{:S(2)}) collective-permute-start(f32[64,128]{1,0:T(8,128)S(1)} %leaf_lower.5.refs_0_), channel_id=1, source_target_pairs={{0,6},{1,7},{2,4},{3,5},{4,2},{5,3},{6,0},{7,1},{8,14},{9,15},{10,... | collective-permute-start | bytes 98312 | tf_op jit(solution)/shard_map/mid_lower/ppermute | solution.py:90
  25.3 1.6 %mid_lower.8 = (bf16[512,1024]{1,0:T(8,128)(2,1)S(1)}, bf16[256,2048]{1,0:T(8,128)(2,1)S(1)}) custom-call(f32[2,1,256,512]{3,2,1,0:T(8,128)} %refs_0_.1, f32[2,2,128,1024]{3,2,1,0:T(8,128)} %refs_1_.5), custom_call_target="tpu_custom_call" | custom-call | flops 262144000 | bytes 374491 | tf_op jit(solution)/shard_map/mid_lower/pallas_call | solution.py:126
  29.1 2.0 %collective-permute-start.14 = (f32[64,128]{1,0:T(8,128)S(1)}, f32[64,128]{1,0:T(8,128)S(1)}, u32[]{:S(2)}, u32[]{:S(2)}) collective-permute-start(f32[64,128]{1,0:T(8,128)S(1)} %get-tuple-element.77), channel_id=1, source_target_pairs={{0,8},{8,0},{16,24},{24,16},{1,9},{9,1},{17,25},{25,17},{2,10},{10... | collective-permute-start | bytes 98312 | tf_op jit(solution)/shard_map/mid_lower/ppermute | solution.py:90
  33.1 1.9 %collective-permute-start.18 = (f32[64,128]{1,0:T(8,128)S(1)}, f32[64,128]{1,0:T(8,128)S(1)}, u32[]{:S(2)}, u32[]{:S(2)}) collective-permute-start(f32[64,128]{1,0:T(8,128)S(1)} %mid_lower.12.refs_0_), channel_id=1, source_target_pairs={{0,2},{1,3},{2,0},{3,1},{4,6},{5,7},{6,4},{7,5},{8,10},{9,11},{10,... | collective-permute-start | bytes 98312 | tf_op jit(solution)/shard_map/mid_lower/ppermute | solution.py:90
  36.7 1.6 %mid_lower.13.matrix = bf16[512,2048]{1,0:T(8,128)(2,1)S(1)} custom-call(f32[2,2,256,1024]{3,2,1,0:T(8,128)} %refs_0_.2), custom_call_target="tpu_custom_call" | custom-call | flops 262144000 | bytes 374491 | tf_op jit(solution)/shard_map/mid_lower/pallas_call | solution.py:126
  38.9 2.4 %collective-permute-done.16.refs_2_ = f32[64,128]{1,0:T(8,128)S(1)} collective-permute-done((f32[64,128]{1,0:T(8,128)S(1)}, f32[64,128]{1,0:T(8,128)S(1)}, u32[]{:S(2)}, u32[]{:S(2)}) %collective-permute-start.16) | collective-permute-done | bytes 32800 | tf_op jit(solution)/shard_map/mid_lower/ppermute | solution.py:90
  43.8 1.6 %collective-permute-start.22 = (f32[256,64]{1,0:T(8,128)S(1)}, f32[256,64]{1,0:T(8,128)S(1)}, u32[]{:S(2)}, u32[]{:S(2)}) collective-permute-start(f32[256,64]{1,0:T(8,128)S(1)} %get-tuple-element.84), channel_id=1, source_target_pairs={{0,8},{8,0},{16,24},{24,16},{1,9},{9,1},{17,25},{25,17},{2,10},{10... | collective-permute-start | bytes 196616 | tf_op jit(solution)/shard_map/mid_lower/ppermute | solution.py:90
  46.4 2.4 %collective-permute-start.23 = (f32[64,128]{1,0:T(8,128)S(1)}, f32[64,128]{1,0:T(8,128)S(1)}, u32[]{:S(2)}, u32[]{:S(2)}) collective-permute-start(f32[64,128]{1,0:T(8,128)S(1)} %mid_lower.15.refs_0_), channel_id=1, source_target_pairs={{0,6},{1,7},{2,4},{3,5},{4,2},{5,3},{6,0},{7,1},{8,14},{9,15},{10,... | collective-permute-start | bytes 98312 | tf_op jit(solution)/shard_map/root_cut/ppermute | solution.py:90
  53.8 2.7 %collective-permute-start.28 = (f32[64,128]{1,0:T(8,128)S(1)}, f32[64,128]{1,0:T(8,128)S(1)}, u32[]{:S(2)}, u32[]{:S(2)}) collective-permute-start(f32[64,128]{1,0:T(8,128)S(1)} %get-tuple-element.88), channel_id=1, source_target_pairs={{0,16},{8,24},{16,0},{24,8},{1,17},{9,25},{17,1},{25,9},{2,18},{10... | collective-permute-start | bytes 98312 | tf_op jit(solution)/shard_map/root_cut/ppermute | solution.py:90
  57.0 1.7 %collective-permute-done.28.refs_1_ = f32[64,128]{1,0:T(8,128)S(1)} collective-permute-done((f32[64,128]{1,0:T(8,128)S(1)}, f32[64,128]{1,0:T(8,128)S(1)}, u32[]{:S(2)}, u32[]{:S(2)}) %collective-permute-start.28) | collective-permute-done | bytes 32800 | tf_op jit(solution)/shard_map/root_cut/ppermute | solution.py:90
  58.8 1.7 %collective-permute-start.32 = (f32[64,128]{1,0:T(8,128)S(1)}, f32[64,128]{1,0:T(8,128)S(1)}, u32[]{:S(2)}, u32[]{:S(2)}) collective-permute-start(f32[64,128]{1,0:T(8,128)S(1)} %root_cut.9.refs_0_), channel_id=1, source_target_pairs={{0,2},{1,3},{2,0},{3,1},{4,6},{5,7},{6,4},{7,5},{8,10},{9,11},{10,... | collective-permute-start | bytes 98312 | tf_op jit(solution)/shard_map/root_solve/ppermute | solution.py:90
  64.4 2.4 %collective-permute-done.30.refs_2_ = f32[64,128]{1,0:T(8,128)S(1)} collective-permute-done((f32[64,128]{1,0:T(8,128)S(1)}, f32[64,128]{1,0:T(8,128)S(1)}, u32[]{:S(2)}, u32[]{:S(2)}) %collective-permute-start.30) | collective-permute-done | bytes 32800 | tf_op jit(solution)/shard_map/root_solve/ppermute | solution.py:90
  68.0 1.9 %root_solve.8.refs_0_ = f32[64,128]{1,0:T(8,128)S(1)} custom-call(bf16[512,4096]{1,0:T(8,128)(2,1)S(1)} %root_cut.5.matrix, f32[64,128]{1,0:T(8,128)S(1)} %root_cut.9.refs_0_, f32[64,128]{1,0:T(8,128)S(1)} %collective-permute-done.29.refs_1_, f32[64,128]{1,0:T(8,128)S(1)} %collective-permute-done.30.refs_2_, ...), custom_call_target="tpu_custom_call" | custom-call | tf_op jit(solution)/shard_map/root_solve/pallas_call | solution.py:126
  71.0 2.6 %collective-permute-start.36 = (f32[64,128]{1,0:T(8,128)S(1)}, f32[64,128]{1,0:T(8,128)S(1)}, u32[]{:S(2)}, u32[]{:S(2)}) collective-permute-start(f32[64,128]{1,0:T(8,128)S(1)} %root_solve.8.refs_0_), channel_id=1, source_target_pairs={{0,6},{1,7},{2,4},{3,5},{4,2},{5,3},{6,0},{7,1},{8,14},{9,15},{10,... | collective-permute-start | bytes 98312 | tf_op jit(solution)/shard_map/root_solve/ppermute | solution.py:90
  77.0 1.9 %root_solve.11.mine = f32[64,128]{1,0:T(8,128)S(1)} custom-call(bf16[512,4096]{1,0:T(8,128)(2,1)S(1)} %root_solve.6.matrix, f32[64,128]{1,0:T(8,128)S(1)} %root_solve.8.refs_0_, f32[64,128]{1,0:T(8,128)S(1)} %collective-permute-done.35.refs_1_, f32[64,128]{1,0:T(8,128)S(1)} %collective-permute-done.36.refs_2_, ...), custom_call_target="tpu_custom_call" | custom-call | tf_op jit(solution)/shard_map/root_solve/pallas_call | solution.py:126
  78.9 2.6 %collective-permute-start.41 = (f32[64,128]{1,0:T(8,128)S(1)}, f32[64,128]{1,0:T(8,128)S(1)}, u32[]{:S(2)}, u32[]{:S(2)}) collective-permute-start(f32[64,128]{1,0:T(8,128)S(1)} %root_solve.11.mine), channel_id=1, source_target_pairs={{0,16},{8,24},{16,0},{24,8},{1,17},{9,25},{17,1},{25,9},{2,18},{10... | collective-permute-start | bytes 98312 | tf_op jit(solution)/shard_map/mid_upper/ppermute | solution.py:90
  81.5 2.3 %collective-permute-done.41.other = f32[64,128]{1,0:T(8,128)S(1)} collective-permute-done((f32[64,128]{1,0:T(8,128)S(1)}, f32[64,128]{1,0:T(8,128)S(1)}, u32[]{:S(2)}, u32[]{:S(2)}) %collective-permute-start.41) | collective-permute-done | bytes 32800 | tf_op jit(solution)/shard_map/mid_upper/ppermute | solution.py:90
  86.3 1.7 %collective-permute-start.44 = (f32[256,128]{1,0:T(8,128)S(1)}, f32[256,128]{1,0:T(8,128)S(1)}, u32[]{:S(2)}, u32[]{:S(2)}) collective-permute-start(f32[256,128]{1,0:T(8,128)S(1)} %mid_upper.8.refs_0_), channel_id=1, source_target_pairs={{0,2},{1,5},{2,0},{3,7},{4,6},{5,1},{6,4},{7,3},{8,10},{9,13},{10,... | collective-permute-start | bytes 393224 | tf_op jit(solution)/shard_map/mid_upper/ppermute | solution.py:382
  88.0 3.3 %collective-permute-done.44.refs_1_ = f32[256,128]{1,0:T(8,128)S(1)} collective-permute-done((f32[256,128]{1,0:T(8,128)S(1)}, f32[256,128]{1,0:T(8,128)S(1)}, u32[]{:S(2)}, u32[]{:S(2)}) %collective-permute-start.44) | collective-permute-done | bytes 131104 | tf_op jit(solution)/shard_map/mid_upper/ppermute | solution.py:382
  91.3 1.7 %collective-permute-start.45 = (f32[256,128]{1,0:T(8,128)S(1)}, f32[256,128]{1,0:T(8,128)S(1)}, u32[]{:S(2)}, u32[]{:S(2)}) collective-permute-start(f32[256,128]{1,0:T(8,128)S(1)} %mid_upper.9.refs_0_), channel_id=1, source_target_pairs={{0,4},{1,3},{2,6},{3,1},{4,0},{5,7},{6,2},{7,5},{8,12},{9,11},{10,... | collective-permute-start | bytes 393224 | tf_op jit(solution)/shard_map/mid_upper/ppermute | solution.py:382
  93.1 3.3 %collective-permute-done.45.refs_1_ = f32[256,128]{1,0:T(8,128)S(1)} collective-permute-done((f32[256,128]{1,0:T(8,128)S(1)}, f32[256,128]{1,0:T(8,128)S(1)}, u32[]{:S(2)}, u32[]{:S(2)}) %collective-permute-start.45) | collective-permute-done | bytes 131104 | tf_op jit(solution)/shard_map/mid_upper/ppermute | solution.py:382
  104.7 1.7 %collective-permute-start.49 = (f32[256,128]{1,0:T(8,128)S(1)}, f32[256,128]{1,0:T(8,128)S(1)}, u32[]{:S(2)}, u32[]{:S(2)}) collective-permute-start(f32[256,128]{1,0:T(8,128)S(1)} %leaf_upper.7.refs_0_), channel_id=1, source_target_pairs={{0,2},{1,5},{2,0},{3,7},{4,6},{5,1},{6,4},{7,3},{8,10},{9,13},{10,... | collective-permute-start | bytes 393224 | tf_op jit(solution)/shard_map/leaf_upper/ppermute | solution.py:382
  106.5 3.3 %collective-permute-done.49.refs_1_ = f32[256,128]{1,0:T(8,128)S(1)} collective-permute-done((f32[256,128]{1,0:T(8,128)S(1)}, f32[256,128]{1,0:T(8,128)S(1)}, u32[]{:S(2)}, u32[]{:S(2)}) %collective-permute-start.49) | collective-permute-done | bytes 131104 | tf_op jit(solution)/shard_map/leaf_upper/ppermute | solution.py:382
  109.8 1.8 %collective-permute-start.50 = (f32[256,128]{1,0:T(8,128)S(1)}, f32[256,128]{1,0:T(8,128)S(1)}, u32[]{:S(2)}, u32[]{:S(2)}) collective-permute-start(f32[256,128]{1,0:T(8,128)S(1)} %leaf_upper.8.refs_0_), channel_id=1, source_target_pairs={{0,4},{1,3},{2,6},{3,1},{4,0},{5,7},{6,2},{7,5},{8,12},{9,11},{10,... | collective-permute-start | bytes 393224 | tf_op jit(solution)/shard_map/leaf_upper/ppermute | solution.py:382
  111.5 2.4 %collective-permute-start.51 = (f32[128,128]{1,0:T(8,128)S(1)}, f32[128,128]{1,0:T(8,128)S(1)}, u32[]{:S(2)}, u32[]{:S(2)}) collective-permute-start(f32[128,128]{1,0:T(8,128)S(1)} %get-tuple-element.108.mine), channel_id=1, source_target_pairs={{0,16},{8,24},{16,0},{24,8},{1,17},{9,25},{17,1},{25,9},{2,18},{10... | collective-permute-start | bytes 196616 | tf_op jit(solution)/shard_map/leaf_upper/ppermute | solution.py:90
  113.9 3.5 %collective-permute-done.51.other = f32[128,128]{1,0:T(8,128)S(1)} collective-permute-done((f32[128,128]{1,0:T(8,128)S(1)}, f32[128,128]{1,0:T(8,128)S(1)}, u32[]{:S(2)}, u32[]{:S(2)}) %collective-permute-start.51) | collective-permute-done | bytes 65568 | tf_op jit(solution)/shard_map/leaf_upper/ppermute | solution.py:90
  (126 shorter events, 47.2 us)
Async XLA Ops:
  1.7 4.8 %collective-permute-start = (f32[32,128]{1,0:T(8,128)S(1)}, f32[32,128]{1,0:T(8,128)S(1)}, u32[]{:S(2)}, u32[]{:S(2)}) collective-permute-start(f32[32,128]{1,0:T(8,128)S(1)} %get-tuple-element.63), channel_id=1, source_target_pairs={{0,8},{8,0},{16,24},{24,16},{1,9},{9,1},{17,25},{25,17},{2,10},{10... | collective-permute-start | bytes 49160 | tf_op jit(solution)/shard_map/right_hand_sides/ppermute | solution.py:90
  6.5 4.7 %collective-permute-start.1 = (f32[32,128]{1,0:T(8,128)S(1)}, f32[32,128]{1,0:T(8,128)S(1)}, u32[]{:S(2)}, u32[]{:S(2)}) collective-permute-start(f32[32,128]{1,0:T(8,128)S(1)} %right_hand_sides.6), channel_id=1, source_target_pairs={{0,16},{8,24},{16,0},{24,8},{1,17},{9,25},{17,1},{25,9},{2,18},{10... | collective-permute-start | bytes 49160 | tf_op jit(solution)/shard_map/right_hand_sides/ppermute | solution.py:90
  11.4 4.9 %collective-permute-start.5 = (f32[72,128]{1,0:T(8,128)S(1)}, f32[72,128]{1,0:T(8,128)S(1)}, u32[]{:S(2)}, u32[]{:S(2)}) collective-permute-start(f32[72,128]{1,0:T(8,128)S(1)} %right_hand_sides.7.refs_0_), channel_id=1, source_target_pairs={{0,2},{1,3},{2,0},{3,1},{4,6},{5,7},{6,4},{7,5},{8,10},{9,11},{10,... | collective-permute-start | bytes 110600 | tf_op jit(solution)/shard_map/leaf_lower/ppermute | solution.py:90
  13.3 4.0 %collective-permute-start.4 = (f32[72,128]{1,0:T(8,128)S(1)}, f32[72,128]{1,0:T(8,128)S(1)}, u32[]{:S(2)}, u32[]{:S(2)}) collective-permute-start(f32[72,128]{1,0:T(8,128)S(1)} %right_hand_sides.7.refs_0_), channel_id=1, source_target_pairs={{0,4},{1,5},{2,6},{3,7},{4,0},{5,1},{6,2},{7,3},{8,12},{9,13},{10,... | collective-permute-start | bytes 110600 | tf_op jit(solution)/shard_map/leaf_lower/ppermute | solution.py:90
  14.8 4.9 %collective-permute-start.3 = (f32[72,128]{1,0:T(8,128)S(1)}, f32[72,128]{1,0:T(8,128)S(1)}, u32[]{:S(2)}, u32[]{:S(2)}) collective-permute-start(f32[72,128]{1,0:T(8,128)S(1)} %right_hand_sides.7.refs_0_), channel_id=1, source_target_pairs={{0,6},{1,7},{2,4},{3,5},{4,2},{5,3},{6,0},{7,1},{8,14},{9,15},{10,... | collective-permute-start | bytes 110600 | tf_op jit(solution)/shard_map/leaf_lower/ppermute | solution.py:90
  21.8 5.1 %collective-permute-start.11 = (f32[64,128]{1,0:T(8,128)S(1)}, f32[64,128]{1,0:T(8,128)S(1)}, u32[]{:S(2)}, u32[]{:S(2)}) collective-permute-start(f32[64,128]{1,0:T(8,128)S(1)} %leaf_lower.5.refs_0_), channel_id=1, source_target_pairs={{0,2},{1,3},{2,0},{3,1},{4,6},{5,7},{6,4},{7,5},{8,10},{9,11},{10,... | collective-permute-start | bytes 98312 | tf_op jit(solution)/shard_map/mid_lower/ppermute | solution.py:90
  22.4 4.6 %collective-permute-start.10 = (f32[64,128]{1,0:T(8,128)S(1)}, f32[64,128]{1,0:T(8,128)S(1)}, u32[]{:S(2)}, u32[]{:S(2)}) collective-permute-start(f32[64,128]{1,0:T(8,128)S(1)} %leaf_lower.5.refs_0_), channel_id=1, source_target_pairs={{0,4},{1,5},{2,6},{3,7},{4,0},{5,1},{6,2},{7,3},{8,12},{9,13},{10,... | collective-permute-start | bytes 98312 | tf_op jit(solution)/shard_map/mid_lower/ppermute | solution.py:90
  22.5 4.8 %collective-permute-start.9 = (f32[64,128]{1,0:T(8,128)S(1)}, f32[64,128]{1,0:T(8,128)S(1)}, u32[]{:S(2)}, u32[]{:S(2)}) collective-permute-start(f32[64,128]{1,0:T(8,128)S(1)} %leaf_lower.5.refs_0_), channel_id=1, source_target_pairs={{0,6},{1,7},{2,4},{3,5},{4,2},{5,3},{6,0},{7,1},{8,14},{9,15},{10,... | collective-permute-start | bytes 98312 | tf_op jit(solution)/shard_map/mid_lower/ppermute | solution.py:90
  29.1 4.0 %collective-permute-start.14 = (f32[64,128]{1,0:T(8,128)S(1)}, f32[64,128]{1,0:T(8,128)S(1)}, u32[]{:S(2)}, u32[]{:S(2)}) collective-permute-start(f32[64,128]{1,0:T(8,128)S(1)} %get-tuple-element.77), channel_id=1, source_target_pairs={{0,8},{8,0},{16,24},{24,16},{1,9},{9,1},{17,25},{25,17},{2,10},{10... | collective-permute-start | bytes 98312 | tf_op jit(solution)/shard_map/mid_lower/ppermute | solution.py:90
  33.1 5.2 %collective-permute-start.18 = (f32[64,128]{1,0:T(8,128)S(1)}, f32[64,128]{1,0:T(8,128)S(1)}, u32[]{:S(2)}, u32[]{:S(2)}) collective-permute-start(f32[64,128]{1,0:T(8,128)S(1)} %mid_lower.12.refs_0_), channel_id=1, source_target_pairs={{0,2},{1,3},{2,0},{3,1},{4,6},{5,7},{6,4},{7,5},{8,10},{9,11},{10,... | collective-permute-start | bytes 98312 | tf_op jit(solution)/shard_map/mid_lower/ppermute | solution.py:90
  35.0 3.9 %collective-permute-start.17 = (f32[64,128]{1,0:T(8,128)S(1)}, f32[64,128]{1,0:T(8,128)S(1)}, u32[]{:S(2)}, u32[]{:S(2)}) collective-permute-start(f32[64,128]{1,0:T(8,128)S(1)} %mid_lower.12.refs_0_), channel_id=1, source_target_pairs={{0,4},{1,5},{2,6},{3,7},{4,0},{5,1},{6,2},{7,3},{8,12},{9,13},{10,... | collective-permute-start | bytes 98312 | tf_op jit(solution)/shard_map/mid_lower/ppermute | solution.py:90
  36.5 4.8 %collective-permute-start.16 = (f32[64,128]{1,0:T(8,128)S(1)}, f32[64,128]{1,0:T(8,128)S(1)}, u32[]{:S(2)}, u32[]{:S(2)}) collective-permute-start(f32[64,128]{1,0:T(8,128)S(1)} %mid_lower.12.refs_0_), channel_id=1, source_target_pairs={{0,6},{1,7},{2,4},{3,5},{4,2},{5,3},{6,0},{7,1},{8,14},{9,15},{10,... | collective-permute-start | bytes 98312 | tf_op jit(solution)/shard_map/mid_lower/ppermute | solution.py:90
  43.6 5.3 %collective-permute-start.21 = (f32[64,128]{1,0:T(8,128)S(1)}, f32[64,128]{1,0:T(8,128)S(1)}, u32[]{:S(2)}, u32[]{:S(2)}) collective-permute-start(f32[64,128]{1,0:T(8,128)S(1)} %mid_lower.15.refs_0_), channel_id=1, source_target_pairs={{0,1},{1,0},{2,3},{3,2},{4,5},{5,4},{6,7},{7,6},{8,9},{9,8},{10,11... | collective-permute-start | bytes 98312 | tf_op jit(solution)/shard_map/root_cut/ppermute | solution.py:90
  43.8 7.4 %collective-permute-start.22 = (f32[256,64]{1,0:T(8,128)S(1)}, f32[256,64]{1,0:T(8,128)S(1)}, u32[]{:S(2)}, u32[]{:S(2)}) collective-permute-start(f32[256,64]{1,0:T(8,128)S(1)} %get-tuple-element.84), channel_id=1, source_target_pairs={{0,8},{8,0},{16,24},{24,16},{1,9},{9,1},{17,25},{25,17},{2,10},{10... | collective-permute-start | bytes 196616 | tf_op jit(solution)/shard_map/mid_lower/ppermute | solution.py:90
  45.4 4.6 %collective-permute-start.25 = (f32[64,128]{1,0:T(8,128)S(1)}, f32[64,128]{1,0:T(8,128)S(1)}, u32[]{:S(2)}, u32[]{:S(2)}) collective-permute-start(f32[64,128]{1,0:T(8,128)S(1)} %mid_lower.15.refs_0_), channel_id=1, source_target_pairs={{0,2},{1,3},{2,0},{3,1},{4,6},{5,7},{6,4},{7,5},{8,10},{9,11},{10,... | collective-permute-start | bytes 98312 | tf_op jit(solution)/shard_map/root_cut/ppermute | solution.py:90
  45.9 4.2 %collective-permute-start.24 = (f32[64,128]{1,0:T(8,128)S(1)}, f32[64,128]{1,0:T(8,128)S(1)}, u32[]{:S(2)}, u32[]{:S(2)}) collective-permute-start(f32[64,128]{1,0:T(8,128)S(1)} %mid_lower.15.refs_0_), channel_id=1, source_target_pairs={{0,4},{1,5},{2,6},{3,7},{4,0},{5,1},{6,2},{7,3},{8,12},{9,13},{10,... | collective-permute-start | bytes 98312 | tf_op jit(solution)/shard_map/root_cut/ppermute | solution.py:90
  46.4 4.8 %collective-permute-start.23 = (f32[64,128]{1,0:T(8,128)S(1)}, f32[64,128]{1,0:T(8,128)S(1)}, u32[]{:S(2)}, u32[]{:S(2)}) collective-permute-start(f32[64,128]{1,0:T(8,128)S(1)} %mid_lower.15.refs_0_), channel_id=1, source_target_pairs={{0,6},{1,7},{2,4},{3,5},{4,2},{5,3},{6,0},{7,1},{8,14},{9,15},{10,... | collective-permute-start | bytes 98312 | tf_op jit(solution)/shard_map/root_cut/ppermute | solution.py:90
  53.8 5.0 %collective-permute-start.28 = (f32[64,128]{1,0:T(8,128)S(1)}, f32[64,128]{1,0:T(8,128)S(1)}, u32[]{:S(2)}, u32[]{:S(2)}) collective-permute-start(f32[64,128]{1,0:T(8,128)S(1)} %get-tuple-element.88), channel_id=1, source_target_pairs={{0,16},{8,24},{16,0},{24,8},{1,17},{9,25},{17,1},{25,9},{2,18},{10... | collective-permute-start | bytes 98312 | tf_op jit(solution)/shard_map/root_cut/ppermute | solution.py:90
  58.8 4.7 %collective-permute-start.32 = (f32[64,128]{1,0:T(8,128)S(1)}, f32[64,128]{1,0:T(8,128)S(1)}, u32[]{:S(2)}, u32[]{:S(2)}) collective-permute-start(f32[64,128]{1,0:T(8,128)S(1)} %root_cut.9.refs_0_), channel_id=1, source_target_pairs={{0,2},{1,3},{2,0},{3,1},{4,6},{5,7},{6,4},{7,5},{8,10},{9,11},{10,... | collective-permute-start | bytes 98312 | tf_op jit(solution)/shard_map/root_solve/ppermute | solution.py:90
  60.5 3.9 %collective-permute-start.31 = (f32[64,128]{1,0:T(8,128)S(1)}, f32[64,128]{1,0:T(8,128)S(1)}, u32[]{:S(2)}, u32[]{:S(2)}) collective-permute-start(f32[64,128]{1,0:T(8,128)S(1)} %root_cut.9.refs_0_), channel_id=1, source_target_pairs={{0,4},{1,5},{2,6},{3,7},{4,0},{5,1},{6,2},{7,3},{8,12},{9,13},{10,... | collective-permute-start | bytes 98312 | tf_op jit(solution)/shard_map/root_solve/ppermute | solution.py:90
  62.0 4.8 %collective-permute-start.30 = (f32[64,128]{1,0:T(8,128)S(1)}, f32[64,128]{1,0:T(8,128)S(1)}, u32[]{:S(2)}, u32[]{:S(2)}) collective-permute-start(f32[64,128]{1,0:T(8,128)S(1)} %root_cut.9.refs_0_), channel_id=1, source_target_pairs={{0,6},{1,7},{2,4},{3,5},{4,2},{5,3},{6,0},{7,1},{8,14},{9,15},{10,... | collective-permute-start | bytes 98312 | tf_op jit(solution)/shard_map/root_solve/ppermute | solution.py:90
  70.1 4.9 %collective-permute-start.38 = (f32[64,128]{1,0:T(8,128)S(1)}, f32[64,128]{1,0:T(8,128)S(1)}, u32[]{:S(2)}, u32[]{:S(2)}) collective-permute-start(f32[64,128]{1,0:T(8,128)S(1)} %root_solve.8.refs_0_), channel_id=1, source_target_pairs={{0,2},{1,3},{2,0},{3,1},{4,6},{5,7},{6,4},{7,5},{8,10},{9,11},{10,... | collective-permute-start | bytes 98312 | tf_op jit(solution)/shard_map/root_solve/ppermute | solution.py:90
  70.6 4.4 %collective-permute-start.37 = (f32[64,128]{1,0:T(8,128)S(1)}, f32[64,128]{1,0:T(8,128)S(1)}, u32[]{:S(2)}, u32[]{:S(2)}) collective-permute-start(f32[64,128]{1,0:T(8,128)S(1)} %root_solve.8.refs_0_), channel_id=1, source_target_pairs={{0,4},{1,5},{2,6},{3,7},{4,0},{5,1},{6,2},{7,3},{8,12},{9,13},{10,... | collective-permute-start | bytes 98312 | tf_op jit(solution)/shard_map/root_solve/ppermute | solution.py:90
  71.0 4.8 %collective-permute-start.36 = (f32[64,128]{1,0:T(8,128)S(1)}, f32[64,128]{1,0:T(8,128)S(1)}, u32[]{:S(2)}, u32[]{:S(2)}) collective-permute-start(f32[64,128]{1,0:T(8,128)S(1)} %root_solve.8.refs_0_), channel_id=1, source_target_pairs={{0,6},{1,7},{2,4},{3,5},{4,2},{5,3},{6,0},{7,1},{8,14},{9,15},{10,... | collective-permute-start | bytes 98312 | tf_op jit(solution)/shard_map/root_solve/ppermute | solution.py:90
  78.9 4.9 %collective-permute-start.41 = (f32[64,128]{1,0:T(8,128)S(1)}, f32[64,128]{1,0:T(8,128)S(1)}, u32[]{:S(2)}, u32[]{:S(2)}) collective-permute-start(f32[64,128]{1,0:T(8,128)S(1)} %root_solve.11.mine), channel_id=1, source_target_pairs={{0,16},{8,24},{16,0},{24,8},{1,17},{9,25},{17,1},{25,9},{2,18},{10... | collective-permute-start | bytes 98312 | tf_op jit(solution)/shard_map/mid_upper/ppermute | solution.py:90
  86.3 5.0 %collective-permute-start.44 = (f32[256,128]{1,0:T(8,128)S(1)}, f32[256,128]{1,0:T(8,128)S(1)}, u32[]{:S(2)}, u32[]{:S(2)}) collective-permute-start(f32[256,128]{1,0:T(8,128)S(1)} %mid_upper.8.refs_0_), channel_id=1, source_target_pairs={{0,2},{1,5},{2,0},{3,7},{4,6},{5,1},{6,4},{7,3},{8,10},{9,13},{10,... | collective-permute-start | bytes 393224 | tf_op jit(solution)/shard_map/mid_upper/ppermute | solution.py:382
  91.3 5.0 %collective-permute-start.45 = (f32[256,128]{1,0:T(8,128)S(1)}, f32[256,128]{1,0:T(8,128)S(1)}, u32[]{:S(2)}, u32[]{:S(2)}) collective-permute-start(f32[256,128]{1,0:T(8,128)S(1)} %mid_upper.9.refs_0_), channel_id=1, source_target_pairs={{0,4},{1,3},{2,6},{3,1},{4,0},{5,7},{6,2},{7,5},{8,12},{9,11},{10,... | collective-permute-start | bytes 393224 | tf_op jit(solution)/shard_map/mid_upper/ppermute | solution.py:382
  96.5 4.5 %collective-permute-start.42 = (f32[128,128]{1,0:T(8,128)S(1)}, f32[128,128]{1,0:T(8,128)S(1)}, u32[]{:S(2)}, u32[]{:S(2)}) collective-permute-start(f32[128,128]{1,0:T(8,128)S(1)} %get-tuple-element.102.mine), channel_id=1, source_target_pairs={{0,8},{8,0},{16,24},{24,16},{1,9},{9,1},{17,25},{25,17},{2,10},{10... | collective-permute-start | bytes 196616 | tf_op jit(solution)/shard_map/mid_upper/ppermute | solution.py:90
  98.8 4.0 %collective-permute-start.47 = (f32[64,128]{1,0:T(8,128)S(1)}, f32[64,128]{1,0:T(8,128)S(1)}, u32[]{:S(2)}, u32[]{:S(2)}) collective-permute-start(f32[64,128]{1,0:T(8,128)S(1)} %mid_upper.11.mine), channel_id=1, source_target_pairs={{0,8},{8,0},{16,24},{24,16},{1,9},{9,1},{17,25},{25,17},{2,10},{10... | collective-permute-start | bytes 98312 | tf_op jit(solution)/shard_map/leaf_upper/ppermute | solution.py:90
  104.7 5.0 %collective-permute-start.49 = (f32[256,128]{1,0:T(8,128)S(1)}, f32[256,128]{1,0:T(8,128)S(1)}, u32[]{:S(2)}, u32[]{:S(2)}) collective-permute-start(f32[256,128]{1,0:T(8,128)S(1)} %leaf_upper.7.refs_0_), channel_id=1, source_target_pairs={{0,2},{1,5},{2,0},{3,7},{4,6},{5,1},{6,4},{7,3},{8,10},{9,13},{10,... | collective-permute-start | bytes 393224 | tf_op jit(solution)/shard_map/leaf_upper/ppermute | solution.py:382
  109.8 8.4 %collective-permute-start.50 = (f32[256,128]{1,0:T(8,128)S(1)}, f32[256,128]{1,0:T(8,128)S(1)}, u32[]{:S(2)}, u32[]{:S(2)}) collective-permute-start(f32[256,128]{1,0:T(8,128)S(1)} %leaf_upper.8.refs_0_), channel_id=1, source_target_pairs={{0,4},{1,3},{2,6},{3,1},{4,0},{5,7},{6,2},{7,5},{8,12},{9,11},{10,... | collective-permute-start | bytes 393224 | tf_op jit(solution)/shard_map/leaf_upper/ppermute | solution.py:382
  111.5 5.9 %collective-permute-start.51 = (f32[128,128]{1,0:T(8,128)S(1)}, f32[128,128]{1,0:T(8,128)S(1)}, u32[]{:S(2)}, u32[]{:S(2)}) collective-permute-start(f32[128,128]{1,0:T(8,128)S(1)} %get-tuple-element.108.mine), channel_id=1, source_target_pairs={{0,16},{8,24},{16,0},{24,8},{1,17},{9,25},{17,1},{25,9},{2,18},{10... | collective-permute-start | bytes 196616 | tf_op jit(solution)/shard_map/leaf_upper/ppermute | solution.py:90
  (28 other events, 134.3 us)

commit v9 on v8

--- a/solution.py
+++ b/solution.py
@@ -97,15 +97,14 @@
         at += ref.shape[0]
 
 
-def gather_front(x, meanwhile=None):
+def gather_front(x, meanwhile=None, others=()):
     fronts = lax.axis_size("front")
     mine = [swap("front", x, k) for k in range(2, fronts, 2)]
+    near, last = mine[:-1], mine[-1]
     own = swap("front", x, 1)
-    extra = tuple(meanwhile(own)) if meanwhile else ()
-    near, last = mine[:-1], mine[-1]
-    if extra:
-        near = [after(near[0], *extra), *near[1:]]
     (both,) = kernel(stack, [(len(near) * x.shape[0], LANES)], *near)
+    extra = tuple(meanwhile((both, own))) if meanwhile else ()
+    last = after(last, *extra, *others)
     return [x, own, last, *near[::-1], swap("front", last, 1), swap("front", both, 1)], extra
 
 
@@ -315,7 +314,8 @@
 
 
 def leaf_to_root(matrix, full, keep, send):
-    keep[...], send[...] = own_first(lax.axis_index("leaf"), *halves(complex_dot(matrix[...], full[...])))
+    mine, theirs = own_first(lax.axis_index("leaf"), *halves(complex_dot(matrix[...], full[...])))
+    keep[...], send[...] = pack(mine), pack(theirs)
 
 
 def add(*refs):
@@ -334,7 +334,7 @@
 def mid_to_root(matrix, kept, came, sources, *refs):
     parts, (keep, send, full) = refs[:-3], refs[-3:]
     assemble(full, parts, lax.axis_index("front"), 2 * COLS)
-    cut = -(kept[...] + came[...] + complex_dot(matrix[...], full[...]))
+    cut = -(unpack(kept[...] + came[...], 2 * COLS) + complex_dot(matrix[...], full[...]))
     width = COLS // 2
     low = pack(jnp.concatenate([cut[:, :width], cut[:, COLS : COLS + width]], axis=1))
     high = pack(jnp.concatenate([cut[:, width:COLS], cut[:, COLS + width :]], axis=1))
@@ -482,7 +482,7 @@
     with jax.named_scope("leaf_lower"):
         messages, (ll, l2m) = gather_front(
             message,
-            lambda x: load((after(leaf_lower_inv, x), "leaf"), (leaf_to_mid_lower, "leaf"), pinned=True),
+            lambda x: load((after(leaf_lower_inv, *x), "leaf"), (leaf_to_mid_lower, "leaf"), pinned=True),
         )
         (y_leaf,) = kernel(
             functools.partial(leaf_lower, groups * slots),
@@ -494,7 +494,7 @@
     with jax.named_scope("mid_lower"):
         parts, (l2r, ml) = gather_front(
             y_leaf,
-            lambda x: load((after(leaf_to_root_lower, x), "leaf"), (mid_lower_inv, "own"), pinned=True),
+            lambda x: load((after(leaf_to_root_lower, *x), "leaf"), (mid_lower_inv, "own"), pinned=True),
         )
         keep, send, y_full = kernel(
             leaf_to_mid,
@@ -504,12 +504,12 @@
             *parts,
         )
         came = swap("leaf", send, 1)
-        root_kept, root_sent = kernel(leaf_to_root, [(n2, 2 * COLS)] * 2, l2r, after(y_full, send))
+        root_kept, root_sent = kernel(leaf_to_root, [(n2 // 2, LANES)] * 2, l2r, after(y_full, send))
         (cut_mid,) = kernel(add, [(n1 // 2, LANES)], after(keep, root_kept), came)
+        root_came = swap("leaf", root_sent, 1)
         parts, (m2r,) = gather_front(
-            cut_mid, lambda x: load((after(mid_to_root_lower, x), "own"), pinned=True)
-        )
-        root_came = swap("leaf", root_sent, 1)
+            cut_mid, lambda x: load((after(mid_to_root_lower, *x), "own"), pinned=True), (root_came,)
+        )
         (y_mid,) = kernel(
             mid_lower,
             [(n1 // 2, LANES)],
@@ -518,7 +518,7 @@
             scratch=[pltpu.VMEM((s1, 2 * COLS), F32)],
         )
     with jax.named_scope("root_cut"):
-        parts, (rl,) = gather_front(y_mid, lambda x: load((after(root_lower_inv, x), None)))
+        parts, (rl,) = gather_front(y_mid, lambda x: load((after(root_lower_inv, *x), None)))
         keep, send, y_mid_full = kernel(
             mid_to_root,
             [(n2 // 4, LANES), (n2 // 4, LANES), (s1, 2 * COLS)],
@@ -532,7 +532,7 @@
         mu, l2r_up = load((after(mid_upper_inv, send), "own"), (leaf_to_root_upper, "leaf"))
         (cut_root,) = kernel(add, [(n2 // 4, LANES)], after(keep, mu), came)
     with jax.named_scope("root_solve"):
-        parts, (ru,) = gather_front(cut_root, lambda x: load((after(root_upper_inv, x), None)))
+        parts, (ru,) = gather_front(cut_root, lambda x: load((after(root_upper_inv, *x), None)))
         (y_root,) = kernel(
             root_rows,
             [(n2 // 4, LANES)],
@@ -543,7 +543,7 @@
         parts, (m2r_up, l2m_up, lu) = gather_front(
             y_root,
             lambda x: load(
-                (after(mid_to_root_upper, x), "own"), (leaf_to_mid_upper, "leaf"), (leaf_upper_inv, "leaf")
+                (after(mid_to_root_upper, *x), "own"), (leaf_to_mid_upper, "leaf"), (leaf_upper_inv, "leaf")
             ),
         )
         (x_root,) = kernel(

time: 121 us -> 119 us (0.983)
  waiting for transfers between devices: 47.1 us -> 45 us
    ppermute x49, waiting for transfers between devices: 37.2 us -> 33.9 us  [swap(): return lax.ppermute(x, axis, [(i, i ^ k) for i in range(size)])]
    ppermute x4, starting transfers between devices: 6.92 us -> 5.6 us  [sum_front(): lax.ppermute(total, 'front', pairs)]
    ppermute x4, waiting for transfers between devices: 9.94 us -> 11.2 us  [sum_front(): lax.ppermute(total, 'front', pairs)]
  transfers between devices with their start and end apart: 53 -> 53, of which waited for: 31 -> 37; matrix products, arithmetic and copies ran while one was open for 0% -> 0% of each run, Pallas kernels for 11% -> 11%
where the time goes in v9:
time: 119 us
  starting transfers between devices  47.7 us (40%)
  waiting for transfers between devices  45 us (38%)
  Pallas kernels  24.7 us (21%)
    ppermute x49, starting transfers between devices, swap(): return lax.ppermute(x, axis, [(i, i ^ k) for i in range(size)])  42.1 us
    ppermute x49, waiting for transfers between devices, swap(): return lax.ppermute(x, axis, [(i, i ^ k) for i in range(size)])  33.9 us
    pallas_call x38, Pallas kernels, kernel(): pl.pallas_call(fn, out_shape=[jax.ShapeDtypeStruct(*o) for o in outs], in...  24.7 us
    ppermute x4, waiting for transfers between devices, sum_front(): lax.ppermute(total, 'front', pairs)  11.2 us
    ppermute x4, starting transfers between devices, sum_front(): lax.ppermute(total, 'front', pairs)  5.6 us
  transfers between devices with their start and end apart: 53, of which 37 were waited for; matrix products, arithmetic and copies ran while one was open for 0% of the time, Pallas kernels for 11%

profile of v9, /device:TPU:0, one launch (start us, length us, event | category | flops | bytes accessed | tf_op | source)
XLA Modules:
  0.0 118.5 jit_solution(13266316053643035784)
XLA Ops:
  1.7 3.1 %collective-permute-start = (f32[32,128]{1,0:T(8,128)S(1)}, f32[32,128]{1,0:T(8,128)S(1)}, u32[]{:S(2)}, u32[]{:S(2)}) collective-permute-start(f32[32,128]{1,0:T(8,128)S(1)} %get-tuple-element.63), channel_id=1, source_target_pairs={{0,8},{8,0},{16,24},{24,16},{1,9},{9,1},{17,25},{25,17},{2,10},{10... | collective-permute-start | bytes 49160 | tf_op jit(solution)/shard_map/right_hand_sides/ppermute | solution.py:90
  4.8 1.7 %collective-permute-done.came.near = f32[32,128]{1,0:T(8,128)S(1)} collective-permute-done((f32[32,128]{1,0:T(8,128)S(1)}, f32[32,128]{1,0:T(8,128)S(1)}, u32[]{:S(2)}, u32[]{:S(2)}) %collective-permute-start) | collective-permute-done | bytes 16416 | tf_op jit(solution)/shard_map/right_hand_sides/ppermute | solution.py:90
  6.5 3.0 %collective-permute-start.1 = (f32[32,128]{1,0:T(8,128)S(1)}, f32[32,128]{1,0:T(8,128)S(1)}, u32[]{:S(2)}, u32[]{:S(2)}) collective-permute-start(f32[32,128]{1,0:T(8,128)S(1)} %right_hand_sides.6), channel_id=1, source_target_pairs={{0,16},{8,24},{16,0},{24,8},{1,17},{9,25},{17,1},{25,9},{2,18},{10... | collective-permute-start | bytes 49160 | tf_op jit(solution)/shard_map/right_hand_sides/ppermute | solution.py:90
  11.3 1.9 %collective-permute-start.3 = (f32[72,128]{1,0:T(8,128)S(1)}, f32[72,128]{1,0:T(8,128)S(1)}, u32[]{:S(2)}, u32[]{:S(2)}) collective-permute-start(f32[72,128]{1,0:T(8,128)S(1)} %right_hand_sides.7.refs_0_), channel_id=1, source_target_pairs={{0,4},{1,5},{2,6},{3,7},{4,0},{5,1},{6,2},{7,3},{8,12},{9,13},{10,... | collective-permute-start | bytes 110600 | tf_op jit(solution)/shard_map/leaf_lower/ppermute | solution.py:90
  13.3 1.5 %collective-permute-start.2 = (f32[72,128]{1,0:T(8,128)S(1)}, f32[72,128]{1,0:T(8,128)S(1)}, u32[]{:S(2)}, u32[]{:S(2)}) collective-permute-start(f32[72,128]{1,0:T(8,128)S(1)} %right_hand_sides.7.refs_0_), channel_id=1, source_target_pairs={{0,2},{1,3},{2,0},{3,1},{4,6},{5,7},{6,4},{7,5},{8,10},{9,11},{10,... | collective-permute-start | bytes 110600 | tf_op jit(solution)/shard_map/leaf_lower/ppermute | solution.py:90
  15.4 1.9 %collective-permute-done.2.refs_0_.refs_4_ = f32[72,128]{1,0:T(8,128)S(1)} collective-permute-done((f32[72,128]{1,0:T(8,128)S(1)}, f32[72,128]{1,0:T(8,128)S(1)}, u32[]{:S(2)}, u32[]{:S(2)}) %collective-permute-start.2) | collective-permute-done | bytes 36896 | tf_op jit(solution)/shard_map/leaf_lower/ppermute | solution.py:90
  22.8 2.3 %collective-permute-start.11 = (f32[64,128]{1,0:T(8,128)S(1)}, f32[64,128]{1,0:T(8,128)S(1)}, u32[]{:S(2)}, u32[]{:S(2)}) collective-permute-start(f32[64,128]{1,0:T(8,128)S(1)} %leaf_lower.5.refs_0_), channel_id=1, source_target_pairs={{0,6},{1,7},{2,4},{3,5},{4,2},{5,3},{6,0},{7,1},{8,14},{9,15},{10,... | collective-permute-start | bytes 98312 | tf_op jit(solution)/shard_map/mid_lower/ppermute | solution.py:90
  26.0 1.6 %mid_lower.9 = (bf16[512,1024]{1,0:T(8,128)(2,1)S(1)}, bf16[256,2048]{1,0:T(8,128)(2,1)S(1)}) custom-call(f32[2,1,256,512]{3,2,1,0:T(8,128)} %refs_0_.1, f32[2,2,128,1024]{3,2,1,0:T(8,128)} %refs_1_.5), custom_call_target="tpu_custom_call" | custom-call | flops 262144000 | bytes 374491 | tf_op jit(solution)/shard_map/mid_lower/pallas_call | solution.py:125
  29.6 1.6 %collective-permute-start.14 = (f32[64,128]{1,0:T(8,128)S(1)}, f32[64,128]{1,0:T(8,128)S(1)}, u32[]{:S(2)}, u32[]{:S(2)}) collective-permute-start(f32[64,128]{1,0:T(8,128)S(1)} %get-tuple-element.77), channel_id=1, source_target_pairs={{0,8},{8,0},{16,24},{24,16},{1,9},{9,1},{17,25},{25,17},{2,10},{10... | collective-permute-start | bytes 98312 | tf_op jit(solution)/shard_map/mid_lower/ppermute | solution.py:90
  33.6 1.7 %collective-permute-start.18 = (f32[64,128]{1,0:T(8,128)S(1)}, f32[64,128]{1,0:T(8,128)S(1)}, u32[]{:S(2)}, u32[]{:S(2)}) collective-permute-start(f32[64,128]{1,0:T(8,128)S(1)} %mid_lower.12.refs_0_), channel_id=1, source_target_pairs={{0,4},{1,5},{2,6},{3,7},{4,0},{5,1},{6,2},{7,3},{8,12},{9,13},{10,... | collective-permute-start | bytes 98312 | tf_op jit(solution)/shard_map/mid_lower/ppermute | solution.py:90
  37.5 1.7 %collective-permute-done.17.refs_0_.refs_4_ = f32[64,128]{1,0:T(8,128)S(1)} collective-permute-done((f32[64,128]{1,0:T(8,128)S(1)}, f32[64,128]{1,0:T(8,128)S(1)}, u32[]{:S(2)}, u32[]{:S(2)}) %collective-permute-start.17) | collective-permute-done | bytes 32800 | tf_op jit(solution)/shard_map/mid_lower/ppermute | solution.py:90
  39.3 1.6 %mid_lower.14.matrix = bf16[512,2048]{1,0:T(8,128)(2,1)S(1)} custom-call(f32[2,2,256,1024]{3,2,1,0:T(8,128)} %refs_0_.2), custom_call_target="tpu_custom_call" | custom-call | flops 262144000 | bytes 374491 | tf_op jit(solution)/shard_map/mid_lower/pallas_call | solution.py:125
  44.9 2.1 %collective-permute-start.25 = (f32[64,128]{1,0:T(8,128)S(1)}, f32[64,128]{1,0:T(8,128)S(1)}, u32[]{:S(2)}, u32[]{:S(2)}) collective-permute-start(f32[64,128]{1,0:T(8,128)S(1)} %mid_lower.15.refs_0_), channel_id=1, source_target_pairs={{0,6},{1,7},{2,4},{3,5},{4,2},{5,3},{6,0},{7,1},{8,14},{9,15},{10,... | collective-permute-start | bytes 98312 | tf_op jit(solution)/shard_map/root_cut/ppermute | solution.py:90
  52.2 2.7 %collective-permute-start.28 = (f32[64,128]{1,0:T(8,128)S(1)}, f32[64,128]{1,0:T(8,128)S(1)}, u32[]{:S(2)}, u32[]{:S(2)}) collective-permute-start(f32[64,128]{1,0:T(8,128)S(1)} %get-tuple-element.88), channel_id=1, source_target_pairs={{0,16},{8,24},{16,0},{24,8},{1,17},{9,25},{17,1},{25,9},{2,18},{10... | collective-permute-start | bytes 98312 | tf_op jit(solution)/shard_map/root_cut/ppermute | solution.py:90
  55.4 1.7 %collective-permute-done.28.refs_1_ = f32[64,128]{1,0:T(8,128)S(1)} collective-permute-done((f32[64,128]{1,0:T(8,128)S(1)}, f32[64,128]{1,0:T(8,128)S(1)}, u32[]{:S(2)}, u32[]{:S(2)}) %collective-permute-start.28) | collective-permute-done | bytes 32800 | tf_op jit(solution)/shard_map/root_cut/ppermute | solution.py:90
  57.1 1.7 %collective-permute-start.32 = (f32[64,128]{1,0:T(8,128)S(1)}, f32[64,128]{1,0:T(8,128)S(1)}, u32[]{:S(2)}, u32[]{:S(2)}) collective-permute-start(f32[64,128]{1,0:T(8,128)S(1)} %root_cut.9.refs_0_), channel_id=1, source_target_pairs={{0,4},{1,5},{2,6},{3,7},{4,0},{5,1},{6,2},{7,3},{8,12},{9,13},{10,... | collective-permute-start | bytes 98312 | tf_op jit(solution)/shard_map/root_solve/ppermute | solution.py:90
  61.0 1.7 %collective-permute-done.31.refs_0_.refs_4_ = f32[64,128]{1,0:T(8,128)S(1)} collective-permute-done((f32[64,128]{1,0:T(8,128)S(1)}, f32[64,128]{1,0:T(8,128)S(1)}, u32[]{:S(2)}, u32[]{:S(2)}) %collective-permute-start.31) | collective-permute-done | bytes 32800 | tf_op jit(solution)/shard_map/root_solve/ppermute | solution.py:90
  65.8 1.9 %root_solve.8.refs_0_ = f32[64,128]{1,0:T(8,128)S(1)} custom-call(bf16[512,4096]{1,0:T(8,128)(2,1)S(1)} %root_cut.6.matrix, f32[64,128]{1,0:T(8,128)S(1)} %root_cut.9.refs_0_, f32[64,128]{1,0:T(8,128)S(1)} %collective-permute-done.29.refs_1_, f32[64,128]{1,0:T(8,128)S(1)} %collective-permute-done.30.refs_2_, ...), custom_call_target="tpu_custom_call" | custom-call | tf_op jit(solution)/shard_map/root_solve/pallas_call | solution.py:125
  69.1 2.1 %collective-permute-start.38 = (f32[64,128]{1,0:T(8,128)S(1)}, f32[64,128]{1,0:T(8,128)S(1)}, u32[]{:S(2)}, u32[]{:S(2)}) collective-permute-start(f32[64,128]{1,0:T(8,128)S(1)} %root_solve.8.refs_0_), channel_id=1, source_target_pairs={{0,6},{1,7},{2,4},{3,5},{4,2},{5,3},{6,0},{7,1},{8,14},{9,15},{10,... | collective-permute-start | bytes 98312 | tf_op jit(solution)/shard_map/root_solve/ppermute | solution.py:90
  72.1 1.4 %root_solve.10 = (bf16[2048,512]{1,0:T(8,128)(2,1)S(1)}, bf16[1024,256]{1,0:T(8,128)(2,1)S(1)}, bf16[128,1024]{1,0:T(8,128)(2,1)S(1)}) custom-call(f32[2,2,1024,256]{3,2,1,0:T(8,128)S(1)} %copy-done, f32[2,1,512,128]{3,2,1,0:T(8,128)S(1)} %copy-done.5, f32[2,1,64,512]{3,2,1,0:T(8,128)S(1)} %copy-done.6), custom_call_target="tpu_custom_call" | custom-call | flops 360448000 | bytes 514925 | tf_op jit(solution)/shard_map/root_solve/pallas_call | solution.py:125
  75.1 1.9 %root_solve.11.mine = f32[64,128]{1,0:T(8,128)S(1)} custom-call(bf16[512,4096]{1,0:T(8,128)(2,1)S(1)} %root_solve.7.matrix, f32[64,128]{1,0:T(8,128)S(1)} %root_solve.8.refs_0_, f32[64,128]{1,0:T(8,128)S(1)} %collective-permute-done.37.refs_1_, f32[64,128]{1,0:T(8,128)S(1)} %collective-permute-done.38.refs_2_, ...), custom_call_target="tpu_custom_call" | custom-call | tf_op jit(solution)/shard_map/root_solve/pallas_call | solution.py:125
  77.0 2.7 %collective-permute-start.41 = (f32[64,128]{1,0:T(8,128)S(1)}, f32[64,128]{1,0:T(8,128)S(1)}, u32[]{:S(2)}, u32[]{:S(2)}) collective-permute-start(f32[64,128]{1,0:T(8,128)S(1)} %root_solve.11.mine), channel_id=1, source_target_pairs={{0,16},{8,24},{16,0},{24,8},{1,17},{9,25},{17,1},{25,9},{2,18},{10... | collective-permute-start | bytes 98312 | tf_op jit(solution)/shard_map/mid_upper/ppermute | solution.py:90
  79.6 2.2 %collective-permute-done.41.other = f32[64,128]{1,0:T(8,128)S(1)} collective-permute-done((f32[64,128]{1,0:T(8,128)S(1)}, f32[64,128]{1,0:T(8,128)S(1)}, u32[]{:S(2)}, u32[]{:S(2)}) %collective-permute-start.41) | collective-permute-done | bytes 32800 | tf_op jit(solution)/shard_map/mid_upper/ppermute | solution.py:90
  83.0 1.3 %collective-permute-done.43.refs_1_ = f32[256,128]{1,0:T(8,128)S(1)} collective-permute-done((f32[256,128]{1,0:T(8,128)S(1)}, f32[256,128]{1,0:T(8,128)S(1)}, u32[]{:S(2)}, u32[]{:S(2)}) %collective-permute-start.43) | collective-permute-done | bytes 131104 | tf_op jit(solution)/shard_map/mid_upper/ppermute | solution.py:90
  85.5 3.9 %collective-permute-done.44.refs_1_ = f32[256,128]{1,0:T(8,128)S(1)} collective-permute-done((f32[256,128]{1,0:T(8,128)S(1)}, f32[256,128]{1,0:T(8,128)S(1)}, u32[]{:S(2)}, u32[]{:S(2)}) %collective-permute-start.44) | collective-permute-done | bytes 131104 | tf_op jit(solution)/shard_map/mid_upper/ppermute | solution.py:382
  89.4 1.7 %collective-permute-start.45 = (f32[256,128]{1,0:T(8,128)S(1)}, f32[256,128]{1,0:T(8,128)S(1)}, u32[]{:S(2)}, u32[]{:S(2)}) collective-permute-start(f32[256,128]{1,0:T(8,128)S(1)} %mid_upper.9.refs_0_), channel_id=1, source_target_pairs={{0,4},{1,3},{2,6},{3,1},{4,0},{5,7},{6,2},{7,5},{8,12},{9,11},{10,... | collective-permute-start | bytes 393224 | tf_op jit(solution)/shard_map/mid_upper/ppermute | solution.py:382
  91.2 3.3 %collective-permute-done.45.refs_1_ = f32[256,128]{1,0:T(8,128)S(1)} collective-permute-done((f32[256,128]{1,0:T(8,128)S(1)}, f32[256,128]{1,0:T(8,128)S(1)}, u32[]{:S(2)}, u32[]{:S(2)}) %collective-permute-start.45) | collective-permute-done | bytes 131104 | tf_op jit(solution)/shard_map/mid_upper/ppermute | solution.py:382
  94.6 1.9 %collective-permute-start.42 = (f32[128,128]{1,0:T(8,128)S(1)}, f32[128,128]{1,0:T(8,128)S(1)}, u32[]{:S(2)}, u32[]{:S(2)}) collective-permute-start(f32[128,128]{1,0:T(8,128)S(1)} %get-tuple-element.102.mine), channel_id=1, source_target_pairs={{0,8},{8,0},{16,24},{24,16},{1,9},{9,1},{17,25},{25,17},{2,10},{10... | collective-permute-start | bytes 196616 | tf_op jit(solution)/shard_map/mid_upper/ppermute | solution.py:90
  104.5 3.9 %collective-permute-done.49.refs_1_ = f32[256,128]{1,0:T(8,128)S(1)} collective-permute-done((f32[256,128]{1,0:T(8,128)S(1)}, f32[256,128]{1,0:T(8,128)S(1)}, u32[]{:S(2)}, u32[]{:S(2)}) %collective-permute-start.49) | collective-permute-done | bytes 131104 | tf_op jit(solution)/shard_map/leaf_upper/ppermute | solution.py:382
  108.4 1.7 %collective-permute-start.50 = (f32[256,128]{1,0:T(8,128)S(1)}, f32[256,128]{1,0:T(8,128)S(1)}, u32[]{:S(2)}, u32[]{:S(2)}) collective-permute-start(f32[256,128]{1,0:T(8,128)S(1)} %leaf_upper.8.refs_0_), channel_id=1, source_target_pairs={{0,4},{1,3},{2,6},{3,1},{4,0},{5,7},{6,2},{7,5},{8,12},{9,11},{10,... | collective-permute-start | bytes 393224 | tf_op jit(solution)/shard_map/leaf_upper/ppermute | solution.py:382
  110.1 2.6 %collective-permute-start.51 = (f32[128,128]{1,0:T(8,128)S(1)}, f32[128,128]{1,0:T(8,128)S(1)}, u32[]{:S(2)}, u32[]{:S(2)}) collective-permute-start(f32[128,128]{1,0:T(8,128)S(1)} %get-tuple-element.108.mine), channel_id=1, source_target_pairs={{0,16},{8,24},{16,0},{24,8},{1,17},{9,25},{17,1},{25,9},{2,18},{10... | collective-permute-start | bytes 196616 | tf_op jit(solution)/shard_map/leaf_upper/ppermute | solution.py:90
  112.7 2.6 %collective-permute-done.51.other = f32[128,128]{1,0:T(8,128)S(1)} collective-permute-done((f32[128,128]{1,0:T(8,128)S(1)}, f32[128,128]{1,0:T(8,128)S(1)}, u32[]{:S(2)}, u32[]{:S(2)}) %collective-permute-start.51) | collective-permute-done | bytes 65568 | tf_op jit(solution)/shard_map/leaf_upper/ppermute | solution.py:90
  (126 shorter events, 48.9 us)
Async XLA Ops:
  1.7 4.8 %collective-permute-start = (f32[32,128]{1,0:T(8,128)S(1)}, f32[32,128]{1,0:T(8,128)S(1)}, u32[]{:S(2)}, u32[]{:S(2)}) collective-permute-start(f32[32,128]{1,0:T(8,128)S(1)} %get-tuple-element.63), channel_id=1, source_target_pairs={{0,8},{8,0},{16,24},{24,16},{1,9},{9,1},{17,25},{25,17},{2,10},{10... | collective-permute-start | bytes 49160 | tf_op jit(solution)/shard_map/right_hand_sides/ppermute | solution.py:90
  6.5 4.7 %collective-permute-start.1 = (f32[32,128]{1,0:T(8,128)S(1)}, f32[32,128]{1,0:T(8,128)S(1)}, u32[]{:S(2)}, u32[]{:S(2)}) collective-permute-start(f32[32,128]{1,0:T(8,128)S(1)} %right_hand_sides.6), channel_id=1, source_target_pairs={{0,16},{8,24},{16,0},{24,8},{1,17},{9,25},{17,1},{25,9},{2,18},{10... | collective-permute-start | bytes 49160 | tf_op jit(solution)/shard_map/right_hand_sides/ppermute | solution.py:90
  11.3 4.0 %collective-permute-start.3 = (f32[72,128]{1,0:T(8,128)S(1)}, f32[72,128]{1,0:T(8,128)S(1)}, u32[]{:S(2)}, u32[]{:S(2)}) collective-permute-start(f32[72,128]{1,0:T(8,128)S(1)} %right_hand_sides.7.refs_0_), channel_id=1, source_target_pairs={{0,4},{1,5},{2,6},{3,7},{4,0},{5,1},{6,2},{7,3},{8,12},{9,13},{10,... | collective-permute-start | bytes 110600 | tf_op jit(solution)/shard_map/leaf_lower/ppermute | solution.py:90
  13.3 4.0 %collective-permute-start.2 = (f32[72,128]{1,0:T(8,128)S(1)}, f32[72,128]{1,0:T(8,128)S(1)}, u32[]{:S(2)}, u32[]{:S(2)}) collective-permute-start(f32[72,128]{1,0:T(8,128)S(1)} %right_hand_sides.7.refs_0_), channel_id=1, source_target_pairs={{0,2},{1,3},{2,0},{3,1},{4,6},{5,7},{6,4},{7,5},{8,10},{9,11},{10,... | collective-permute-start | bytes 110600 | tf_op jit(solution)/shard_map/leaf_lower/ppermute | solution.py:90
  14.7 4.9 %collective-permute-start.5 = (f32[72,128]{1,0:T(8,128)S(1)}, f32[72,128]{1,0:T(8,128)S(1)}, u32[]{:S(2)}, u32[]{:S(2)}) collective-permute-start(f32[72,128]{1,0:T(8,128)S(1)} %right_hand_sides.7.refs_0_), channel_id=1, source_target_pairs={{0,6},{1,7},{2,4},{3,5},{4,2},{5,3},{6,0},{7,1},{8,14},{9,15},{10,... | collective-permute-start | bytes 110600 | tf_op jit(solution)/shard_map/leaf_lower/ppermute | solution.py:90
  17.2 3.6 %collective-permute-start.7 = (f32[144,128]{1,0:T(8,128)S(1)}, f32[144,128]{1,0:T(8,128)S(1)}, u32[]{:S(2)}, u32[]{:S(2)}) collective-permute-start(f32[144,128]{1,0:T(8,128)S(1)} %leaf_lower.3), channel_id=1, source_target_pairs={{0,1},{1,0},{2,3},{3,2},{4,5},{5,4},{6,7},{7,6},{8,9},{9,8},{10,11... | collective-permute-start | bytes 221192 | tf_op jit(solution)/shard_map/leaf_lower/ppermute | solution.py:90
  21.5 4.0 %collective-permute-start.9 = (f32[64,128]{1,0:T(8,128)S(1)}, f32[64,128]{1,0:T(8,128)S(1)}, u32[]{:S(2)}, u32[]{:S(2)}) collective-permute-start(f32[64,128]{1,0:T(8,128)S(1)} %leaf_lower.5.refs_0_), channel_id=1, source_target_pairs={{0,4},{1,5},{2,6},{3,7},{4,0},{5,1},{6,2},{7,3},{8,12},{9,13},{10,... | collective-permute-start | bytes 98312 | tf_op jit(solution)/shard_map/mid_lower/ppermute | solution.py:90
  22.1 3.9 %collective-permute-start.8 = (f32[64,128]{1,0:T(8,128)S(1)}, f32[64,128]{1,0:T(8,128)S(1)}, u32[]{:S(2)}, u32[]{:S(2)}) collective-permute-start(f32[64,128]{1,0:T(8,128)S(1)} %leaf_lower.5.refs_0_), channel_id=1, source_target_pairs={{0,2},{1,3},{2,0},{3,1},{4,6},{5,7},{6,4},{7,5},{8,10},{9,11},{10,... | collective-permute-start | bytes 98312 | tf_op jit(solution)/shard_map/mid_lower/ppermute | solution.py:90
  22.8 4.9 %collective-permute-start.11 = (f32[64,128]{1,0:T(8,128)S(1)}, f32[64,128]{1,0:T(8,128)S(1)}, u32[]{:S(2)}, u32[]{:S(2)}) collective-permute-start(f32[64,128]{1,0:T(8,128)S(1)} %leaf_lower.5.refs_0_), channel_id=1, source_target_pairs={{0,6},{1,7},{2,4},{3,5},{4,2},{5,3},{6,0},{7,1},{8,14},{9,15},{10,... | collective-permute-start | bytes 98312 | tf_op jit(solution)/shard_map/mid_lower/ppermute | solution.py:90
  29.6 4.0 %collective-permute-start.14 = (f32[64,128]{1,0:T(8,128)S(1)}, f32[64,128]{1,0:T(8,128)S(1)}, u32[]{:S(2)}, u32[]{:S(2)}) collective-permute-start(f32[64,128]{1,0:T(8,128)S(1)} %get-tuple-element.77), channel_id=1, source_target_pairs={{0,8},{8,0},{16,24},{24,16},{1,9},{9,1},{17,25},{25,17},{2,10},{10... | collective-permute-start | bytes 98312 | tf_op jit(solution)/shard_map/mid_lower/ppermute | solution.py:90
  32.0 9.1 %collective-permute-start.19 = (f32[128,128]{1,0:T(8,128)S(1)}, f32[128,128]{1,0:T(8,128)S(1)}, u32[]{:S(2)}, u32[]{:S(2)}) collective-permute-start(f32[128,128]{1,0:T(8,128)S(1)} %get-tuple-element.82), channel_id=1, source_target_pairs={{0,8},{8,0},{16,24},{24,16},{1,9},{9,1},{17,25},{25,17},{2,10},{10... | collective-permute-start | bytes 196616 | tf_op jit(solution)/shard_map/mid_lower/ppermute | solution.py:90
  33.6 3.9 %collective-permute-start.18 = (f32[64,128]{1,0:T(8,128)S(1)}, f32[64,128]{1,0:T(8,128)S(1)}, u32[]{:S(2)}, u32[]{:S(2)}) collective-permute-start(f32[64,128]{1,0:T(8,128)S(1)} %mid_lower.12.refs_0_), channel_id=1, source_target_pairs={{0,4},{1,5},{2,6},{3,7},{4,0},{5,1},{6,2},{7,3},{8,12},{9,13},{10,... | collective-permute-start | bytes 98312 | tf_op jit(solution)/shard_map/mid_lower/ppermute | solution.py:90
  35.3 3.9 %collective-permute-start.17 = (f32[64,128]{1,0:T(8,128)S(1)}, f32[64,128]{1,0:T(8,128)S(1)}, u32[]{:S(2)}, u32[]{:S(2)}) collective-permute-start(f32[64,128]{1,0:T(8,128)S(1)} %mid_lower.12.refs_0_), channel_id=1, source_target_pairs={{0,2},{1,3},{2,0},{3,1},{4,6},{5,7},{6,4},{7,5},{8,10},{9,11},{10,... | collective-permute-start | bytes 98312 | tf_op jit(solution)/shard_map/mid_lower/ppermute | solution.py:90
  36.2 4.8 %collective-permute-start.16 = (f32[64,128]{1,0:T(8,128)S(1)}, f32[64,128]{1,0:T(8,128)S(1)}, u32[]{:S(2)}, u32[]{:S(2)}) collective-permute-start(f32[64,128]{1,0:T(8,128)S(1)} %mid_lower.12.refs_0_), channel_id=1, source_target_pairs={{0,6},{1,7},{2,4},{3,5},{4,2},{5,3},{6,0},{7,1},{8,14},{9,15},{10,... | collective-permute-start | bytes 98312 | tf_op jit(solution)/shard_map/mid_lower/ppermute | solution.py:90
  43.4 4.0 %collective-permute-start.23 = (f32[64,128]{1,0:T(8,128)S(1)}, f32[64,128]{1,0:T(8,128)S(1)}, u32[]{:S(2)}, u32[]{:S(2)}) collective-permute-start(f32[64,128]{1,0:T(8,128)S(1)} %mid_lower.15.refs_0_), channel_id=1, source_target_pairs={{0,4},{1,5},{2,6},{3,7},{4,0},{5,1},{6,2},{7,3},{8,12},{9,13},{10,... | collective-permute-start | bytes 98312 | tf_op jit(solution)/shard_map/root_cut/ppermute | solution.py:90
  43.9 3.9 %collective-permute-start.22 = (f32[64,128]{1,0:T(8,128)S(1)}, f32[64,128]{1,0:T(8,128)S(1)}, u32[]{:S(2)}, u32[]{:S(2)}) collective-permute-start(f32[64,128]{1,0:T(8,128)S(1)} %mid_lower.15.refs_0_), channel_id=1, source_target_pairs={{0,2},{1,3},{2,0},{3,1},{4,6},{5,7},{6,4},{7,5},{8,10},{9,11},{10,... | collective-permute-start | bytes 98312 | tf_op jit(solution)/shard_map/root_cut/ppermute | solution.py:90
  44.9 4.8 %collective-permute-start.25 = (f32[64,128]{1,0:T(8,128)S(1)}, f32[64,128]{1,0:T(8,128)S(1)}, u32[]{:S(2)}, u32[]{:S(2)}) collective-permute-start(f32[64,128]{1,0:T(8,128)S(1)} %mid_lower.15.refs_0_), channel_id=1, source_target_pairs={{0,6},{1,7},{2,4},{3,5},{4,2},{5,3},{6,0},{7,1},{8,14},{9,15},{10,... | collective-permute-start | bytes 98312 | tf_op jit(solution)/shard_map/root_cut/ppermute | solution.py:90
  52.2 4.9 %collective-permute-start.28 = (f32[64,128]{1,0:T(8,128)S(1)}, f32[64,128]{1,0:T(8,128)S(1)}, u32[]{:S(2)}, u32[]{:S(2)}) collective-permute-start(f32[64,128]{1,0:T(8,128)S(1)} %get-tuple-element.88), channel_id=1, source_target_pairs={{0,16},{8,24},{16,0},{24,8},{1,17},{9,25},{17,1},{25,9},{2,18},{10... | collective-permute-start | bytes 98312 | tf_op jit(solution)/shard_map/root_cut/ppermute | solution.py:90
  57.1 3.9 %collective-permute-start.32 = (f32[64,128]{1,0:T(8,128)S(1)}, f32[64,128]{1,0:T(8,128)S(1)}, u32[]{:S(2)}, u32[]{:S(2)}) collective-permute-start(f32[64,128]{1,0:T(8,128)S(1)} %root_cut.9.refs_0_), channel_id=1, source_target_pairs={{0,4},{1,5},{2,6},{3,7},{4,0},{5,1},{6,2},{7,3},{8,12},{9,13},{10,... | collective-permute-start | bytes 98312 | tf_op jit(solution)/shard_map/root_solve/ppermute | solution.py:90
  58.8 3.9 %collective-permute-start.31 = (f32[64,128]{1,0:T(8,128)S(1)}, f32[64,128]{1,0:T(8,128)S(1)}, u32[]{:S(2)}, u32[]{:S(2)}) collective-permute-start(f32[64,128]{1,0:T(8,128)S(1)} %root_cut.9.refs_0_), channel_id=1, source_target_pairs={{0,2},{1,3},{2,0},{3,1},{4,6},{5,7},{6,4},{7,5},{8,10},{9,11},{10,... | collective-permute-start | bytes 98312 | tf_op jit(solution)/shard_map/root_solve/ppermute | solution.py:90
  59.8 4.8 %collective-permute-start.30 = (f32[64,128]{1,0:T(8,128)S(1)}, f32[64,128]{1,0:T(8,128)S(1)}, u32[]{:S(2)}, u32[]{:S(2)}) collective-permute-start(f32[64,128]{1,0:T(8,128)S(1)} %root_cut.9.refs_0_), channel_id=1, source_target_pairs={{0,6},{1,7},{2,4},{3,5},{4,2},{5,3},{6,0},{7,1},{8,14},{9,15},{10,... | collective-permute-start | bytes 98312 | tf_op jit(solution)/shard_map/root_solve/ppermute | solution.py:90
  67.6 4.0 %collective-permute-start.36 = (f32[64,128]{1,0:T(8,128)S(1)}, f32[64,128]{1,0:T(8,128)S(1)}, u32[]{:S(2)}, u32[]{:S(2)}) collective-permute-start(f32[64,128]{1,0:T(8,128)S(1)} %root_solve.8.refs_0_), channel_id=1, source_target_pairs={{0,4},{1,5},{2,6},{3,7},{4,0},{5,1},{6,2},{7,3},{8,12},{9,13},{10,... | collective-permute-start | bytes 98312 | tf_op jit(solution)/shard_map/root_solve/ppermute | solution.py:90
  68.1 3.9 %collective-permute-start.35 = (f32[64,128]{1,0:T(8,128)S(1)}, f32[64,128]{1,0:T(8,128)S(1)}, u32[]{:S(2)}, u32[]{:S(2)}) collective-permute-start(f32[64,128]{1,0:T(8,128)S(1)} %root_solve.8.refs_0_), channel_id=1, source_target_pairs={{0,2},{1,3},{2,0},{3,1},{4,6},{5,7},{6,4},{7,5},{8,10},{9,11},{10,... | collective-permute-start | bytes 98312 | tf_op jit(solution)/shard_map/root_solve/ppermute | solution.py:90
  69.1 4.8 %collective-permute-start.38 = (f32[64,128]{1,0:T(8,128)S(1)}, f32[64,128]{1,0:T(8,128)S(1)}, u32[]{:S(2)}, u32[]{:S(2)}) collective-permute-start(f32[64,128]{1,0:T(8,128)S(1)} %root_solve.8.refs_0_), channel_id=1, source_target_pairs={{0,6},{1,7},{2,4},{3,5},{4,2},{5,3},{6,0},{7,1},{8,14},{9,15},{10,... | collective-permute-start | bytes 98312 | tf_op jit(solution)/shard_map/root_solve/ppermute | solution.py:90
  77.0 4.9 %collective-permute-start.41 = (f32[64,128]{1,0:T(8,128)S(1)}, f32[64,128]{1,0:T(8,128)S(1)}, u32[]{:S(2)}, u32[]{:S(2)}) collective-permute-start(f32[64,128]{1,0:T(8,128)S(1)} %root_solve.11.mine), channel_id=1, source_target_pairs={{0,16},{8,24},{16,0},{24,8},{1,17},{9,25},{17,1},{25,9},{2,18},{10... | collective-permute-start | bytes 98312 | tf_op jit(solution)/shard_map/mid_upper/ppermute | solution.py:90
  84.4 5.0 %collective-permute-start.44 = (f32[256,128]{1,0:T(8,128)S(1)}, f32[256,128]{1,0:T(8,128)S(1)}, u32[]{:S(2)}, u32[]{:S(2)}) collective-permute-start(f32[256,128]{1,0:T(8,128)S(1)} %mid_upper.8.refs_0_), channel_id=1, source_target_pairs={{0,2},{1,5},{2,0},{3,7},{4,6},{5,1},{6,4},{7,3},{8,10},{9,13},{10,... | collective-permute-start | bytes 393224 | tf_op jit(solution)/shard_map/mid_upper/ppermute | solution.py:382
  89.4 5.0 %collective-permute-start.45 = (f32[256,128]{1,0:T(8,128)S(1)}, f32[256,128]{1,0:T(8,128)S(1)}, u32[]{:S(2)}, u32[]{:S(2)}) collective-permute-start(f32[256,128]{1,0:T(8,128)S(1)} %mid_upper.9.refs_0_), channel_id=1, source_target_pairs={{0,4},{1,3},{2,6},{3,1},{4,0},{5,7},{6,2},{7,5},{8,12},{9,11},{10,... | collective-permute-start | bytes 393224 | tf_op jit(solution)/shard_map/mid_upper/ppermute | solution.py:382
  94.6 4.6 %collective-permute-start.42 = (f32[128,128]{1,0:T(8,128)S(1)}, f32[128,128]{1,0:T(8,128)S(1)}, u32[]{:S(2)}, u32[]{:S(2)}) collective-permute-start(f32[128,128]{1,0:T(8,128)S(1)} %get-tuple-element.102.mine), channel_id=1, source_target_pairs={{0,8},{8,0},{16,24},{24,16},{1,9},{9,1},{17,25},{25,17},{2,10},{10... | collective-permute-start | bytes 196616 | tf_op jit(solution)/shard_map/mid_upper/ppermute | solution.py:90
  97.5 4.0 %collective-permute-start.47 = (f32[64,128]{1,0:T(8,128)S(1)}, f32[64,128]{1,0:T(8,128)S(1)}, u32[]{:S(2)}, u32[]{:S(2)}) collective-permute-start(f32[64,128]{1,0:T(8,128)S(1)} %mid_upper.11.mine), channel_id=1, source_target_pairs={{0,8},{8,0},{16,24},{24,16},{1,9},{9,1},{17,25},{25,17},{2,10},{10... | collective-permute-start | bytes 98312 | tf_op jit(solution)/shard_map/leaf_upper/ppermute | solution.py:90
  103.4 5.0 %collective-permute-start.49 = (f32[256,128]{1,0:T(8,128)S(1)}, f32[256,128]{1,0:T(8,128)S(1)}, u32[]{:S(2)}, u32[]{:S(2)}) collective-permute-start(f32[256,128]{1,0:T(8,128)S(1)} %leaf_upper.7.refs_0_), channel_id=1, source_target_pairs={{0,2},{1,5},{2,0},{3,7},{4,6},{5,1},{6,4},{7,3},{8,10},{9,13},{10,... | collective-permute-start | bytes 393224 | tf_op jit(solution)/shard_map/leaf_upper/ppermute | solution.py:382
  108.4 7.6 %collective-permute-start.50 = (f32[256,128]{1,0:T(8,128)S(1)}, f32[256,128]{1,0:T(8,128)S(1)}, u32[]{:S(2)}, u32[]{:S(2)}) collective-permute-start(f32[256,128]{1,0:T(8,128)S(1)} %leaf_upper.8.refs_0_), channel_id=1, source_target_pairs={{0,4},{1,3},{2,6},{3,1},{4,0},{5,7},{6,2},{7,5},{8,12},{9,11},{10,... | collective-permute-start | bytes 393224 | tf_op jit(solution)/shard_map/leaf_upper/ppermute | solution.py:382
  110.1 5.2 %collective-permute-start.51 = (f32[128,128]{1,0:T(8,128)S(1)}, f32[128,128]{1,0:T(8,128)S(1)}, u32[]{:S(2)}, u32[]{:S(2)}) collective-permute-start(f32[128,128]{1,0:T(8,128)S(1)} %get-tuple-element.108.mine), channel_id=1, source_target_pairs={{0,16},{8,24},{16,0},{24,8},{1,17},{9,25},{17,1},{25,9},{2,18},{10... | collective-permute-start | bytes 196616 | tf_op jit(solution)/shard_map/leaf_upper/ppermute | solution.py:90
  (28 other events, 116.5 us)

commit v10 on v9

--- a/solution.py
+++ b/solution.py
@@ -32,6 +32,16 @@
     both = jnp.concatenate([x, turned], axis=0)
     columns = jnp.concatenate(split(both), axis=1)
     product = dot(matrix, columns)
+    rows, n = product.shape[0] // 2, x.shape[1]
+    return (product[:rows, n:] + product[rows:, :n]) + product[:rows, :n]
+
+
+def part_dot(matrix, at, x):
+    depth, count, half = matrix.shape[1] // 2, x.shape[0], x.shape[1] // 2
+    at = pl.multiple_of(at, LANES)
+    turned = jnp.concatenate([-x[:, half:], x[:, :half]], axis=1)
+    product = dot(matrix[:, pl.ds(at, count)], jnp.concatenate(split(x), axis=1))
+    product += dot(matrix[:, pl.ds(depth + at, count)], jnp.concatenate(split(turned), axis=1))
     rows, n = product.shape[0] // 2, x.shape[1]
     return (product[:rows, n:] + product[rows:, :n]) + product[:rows, :n]
 
@@ -131,6 +141,77 @@
         compiler_params=pltpu.CompilerParams(vmem_limit_bytes=vmem * 2**20),
         cost_estimate=pl.CostEstimate(flops=work, bytes_accessed=work // 700, transcendentals=0),
     )(*(pltpu.with_memory_space_constraint(a, pltpu.HBM) if i in pinned else a for i, a in enumerate(args)))
+
+
+def chip_product(matrix, k, mine, other, width):
+    here = lax.axis_index("front")
+    odd = (here & 1) == 1
+    if width < LANES:
+        mine, other = unpack(mine, width), unpack(other, width)
+    x = jnp.concatenate([jnp.where(odd, other, mine), jnp.where(odd, mine, other)], axis=0)
+    return part_dot(matrix, ((here ^ k) // 2) * x.shape[0], x)
+
+
+def first_products(width, matrix, mine, other, *refs):
+    near, both, out = refs[:-2], refs[-2], refs[-1]
+    rows = mine.shape[0]
+    total = chip_product(matrix, 0, mine[...], other[...], width)
+    for i, block in enumerate(near):
+        second = both[rows * i : rows * i + rows, :]
+        total += chip_product(matrix, 2 * i + 2, block[...], second, width)
+    out[...] = total
+
+
+def last_product(finish, width, count, matrix, *refs):
+    parts, rest = refs[:count], refs[count:]
+    if count == 3:
+        known, mine, other = parts
+        k = lax.axis_size("front") - 2
+        finish(known[...] + chip_product(matrix, k, mine[...], other[...], width), *rest)
+    else:
+        assemble(rest[-1], parts, lax.axis_index("front"), width)
+        finish(complex_dot(matrix[...], rest[-1][...]), *rest[:-1])
+
+
+def gathered(finish, width, outs, matrix, parts, *args):
+    rows = parts[0].shape[0] * (LANES // width)
+    scratch = []
+    if 2 * rows % LANES == 0:
+        mine, other, last, *near, last_other, both = parts
+        shape = (matrix.shape[0] // 2, width)
+        (known,) = kernel(
+            functools.partial(first_products, width), [shape], matrix, mine, other, *near[::-1], both
+        )
+        parts = [known, last, last_other]
+    else:
+        scratch = [pltpu.VMEM((rows * lax.axis_size("front"), width), F32)]
+    return kernel(
+        functools.partial(last_product, finish, width, len(parts)),
+        outs,
+        matrix,
+        *parts,
+        *args,
+        scratch=scratch,
+    )
+
+
+def whole_of(width, *refs):
+    assemble(refs[-1], refs[:-1], lax.axis_index("front"), width)
+
+
+def half_product(theirs, width, matrix, y, piece):
+    odd = (lax.axis_index("front") & 1) ^ theirs
+    rows, total = piece.shape[0], None
+    for chunk in range(LANES // width):
+        at = chunk * 2 * rows + odd * rows
+        x = y[pl.ds(pl.multiple_of(at, 8), rows), :] - piece[:, chunk * width : chunk * width + width]
+        part = part_dot(matrix, at, x)
+        total = part if total is None else total + part
+    return total
+
+
+def own_half(width, matrix, y, piece, out):
+    out[...] = half_product(0, width, matrix, y, piece)
 
 
 def load_matrices(picks, *refs):
@@ -305,15 +386,15 @@
     out[...] = complex_dot(matrix[...], rhs[...])
 
 
-def leaf_to_mid(matrix, sources, *refs):
+def leaf_to_mid(value, sources, keep, send):
+    mine, theirs = own_first(lax.axis_index("leaf"), *halves(value))
+    keep[...] = sources[...] - pack(mine)
+    send[...] = -pack(theirs)
+
+
+def leaf_to_root(matrix, *refs):
     parts, (keep, send, full) = refs[:-3], refs[-3:]
     assemble(full, parts, lax.axis_index("front"))
-    mine, theirs = own_first(lax.axis_index("leaf"), *halves(complex_dot(matrix[...], full[...])))
-    keep[...] = sources[...] - pack(mine)
-    send[...] = -pack(theirs)
-
-
-def leaf_to_root(matrix, full, keep, send):
     mine, theirs = own_first(lax.axis_index("leaf"), *halves(complex_dot(matrix[...], full[...])))
     keep[...], send[...] = pack(mine), pack(theirs)
 
@@ -325,28 +406,18 @@
     refs[-1][...] = total
 
 
-def mid_lower(matrix, *refs):
-    parts, (out, whole) = refs[:-2], refs[-2:]
-    assemble(whole, parts, lax.axis_index("front"), 2 * COLS)
-    out[...] = pack(complex_dot(matrix[...], whole[...]))
-
-
-def mid_to_root(matrix, kept, came, sources, *refs):
-    parts, (keep, send, full) = refs[:-3], refs[-3:]
-    assemble(full, parts, lax.axis_index("front"), 2 * COLS)
-    cut = -(unpack(kept[...] + came[...], 2 * COLS) + complex_dot(matrix[...], full[...]))
+def packed_to(value, out):
+    out[...] = pack(value)
+
+
+def mid_to_root(value, kept, came, sources, keep, send):
+    cut = -(unpack(kept[...] + came[...], 2 * COLS) + value)
     width = COLS // 2
     low = pack(jnp.concatenate([cut[:, :width], cut[:, COLS : COLS + width]], axis=1))
     high = pack(jnp.concatenate([cut[:, width:COLS], cut[:, COLS + width :]], axis=1))
     first = lax.axis_index("leaf") < 2
     keep[...] = jnp.where(first, low, high) + sources[...]
     send[...] = jnp.where(first, high, low)
-
-
-def root_rows(matrix, *refs):
-    parts, (out, whole) = refs[:-2], refs[-2:]
-    assemble(whole, parts, lax.axis_index("front"), COLS)
-    out[...] = pack(complex_dot(matrix[...], whole[...]))
 
 
 def halved(value, keep, send):
@@ -383,15 +454,8 @@
     return [total, swap("front", after(total, *others), 1)]
 
 
-def summed(pieces):
-    mine, theirs = (ref[...] for ref in pieces)
-    odd = (lax.axis_index("front") & 1) == 1
-    return jnp.concatenate([jnp.where(odd, theirs, mine), jnp.where(odd, mine, theirs)], axis=0)
-
-
-def mid_upper(matrix, y, *refs):
-    tail, out = unpack(summed(refs[:2]), 2 * COLS), refs[2]
-    out[...] = pack(complex_dot(matrix[...], y[...] - tail))
+def mid_upper(matrix, y, piece, known, out):
+    out[...] = pack(known[...] + half_product(1, 2 * COLS, matrix, y, piece))
 
 
 def mid_to_leaf(matrix, from_root, mine, other, keep, send, x_mid):
@@ -400,9 +464,8 @@
     halved(complex_dot(matrix[...], x) + from_root[...], keep, send)
 
 
-def leaf_upper(matrix, y, *refs):
-    forward, adjoint = refs[2:]
-    fields_of(complex_dot(matrix[...], y[...] - summed(refs[:2])), forward, adjoint, ())
+def leaf_upper(matrix, y, piece, known, forward, adjoint):
+    fields_of(known[...] + half_product(1, LANES, matrix, y, piece), forward, adjoint, ())
 
 
 def mid_outputs(mine, other, forward, adjoint):
@@ -496,63 +559,38 @@
             y_leaf,
             lambda x: load((after(leaf_to_root_lower, *x), "leaf"), (mid_lower_inv, "own"), pinned=True),
         )
-        keep, send, y_full = kernel(
-            leaf_to_mid,
-            [(n1 // 2, LANES), (n1 // 2, LANES), (s0, LANES)],
-            l2m,
-            mid_own,
-            *parts,
-        )
+        keep, send = gathered(leaf_to_mid, LANES, [(n1 // 2, LANES)] * 2, l2m, parts, mid_own)
         came = swap("leaf", send, 1)
-        root_kept, root_sent = kernel(leaf_to_root, [(n2 // 2, LANES)] * 2, l2r, after(y_full, send))
+        root_kept, root_sent, y_full = kernel(
+            leaf_to_root, [(n2 // 2, LANES)] * 2 + [(s0, LANES)], l2r, after(parts[0], send), *parts[1:]
+        )
         (cut_mid,) = kernel(add, [(n1 // 2, LANES)], after(keep, root_kept), came)
         root_came = swap("leaf", root_sent, 1)
         parts, (m2r,) = gather_front(
             cut_mid, lambda x: load((after(mid_to_root_lower, *x), "own"), pinned=True), (root_came,)
         )
-        (y_mid,) = kernel(
-            mid_lower,
-            [(n1 // 2, LANES)],
-            ml,
-            *parts,
-            scratch=[pltpu.VMEM((s1, 2 * COLS), F32)],
-        )
+        (y_mid,) = gathered(packed_to, 2 * COLS, [(n1 // 2, LANES)], ml, parts)
     with jax.named_scope("root_cut"):
         parts, (rl,) = gather_front(y_mid, lambda x: load((after(root_lower_inv, *x), None)))
-        keep, send, y_mid_full = kernel(
-            mid_to_root,
-            [(n2 // 4, LANES), (n2 // 4, LANES), (s1, 2 * COLS)],
-            m2r,
-            root_kept,
-            root_came,
-            root_own,
-            *parts,
+        keep, send = gathered(
+            mid_to_root, 2 * COLS, [(n2 // 4, LANES)] * 2, m2r, parts, root_kept, root_came, root_own
         )
         came = swap("leaf", send, 2)
         mu, l2r_up = load((after(mid_upper_inv, send), "own"), (leaf_to_root_upper, "leaf"))
-        (cut_root,) = kernel(add, [(n2 // 4, LANES)], after(keep, mu), came)
+        (y_mid_full,) = kernel(
+            functools.partial(whole_of, 2 * COLS), [(s1, 2 * COLS)], after(parts[0], send), *parts[1:]
+        )
+        (cut_root,) = kernel(add, [(n2 // 4, LANES)], after(keep, mu, y_mid_full), came)
     with jax.named_scope("root_solve"):
         parts, (ru,) = gather_front(cut_root, lambda x: load((after(root_upper_inv, *x), None)))
-        (y_root,) = kernel(
-            root_rows,
-            [(n2 // 4, LANES)],
-            rl,
-            *parts,
-            scratch=[pltpu.VMEM((s2, COLS), F32)],
-        )
+        (y_root,) = gathered(packed_to, COLS, [(n2 // 4, LANES)], rl, parts)
         parts, (m2r_up, l2m_up, lu) = gather_front(
             y_root,
             lambda x: load(
                 (after(mid_to_root_upper, *x), "own"), (leaf_to_mid_upper, "leaf"), (leaf_upper_inv, "leaf")
             ),
         )
-        (x_root,) = kernel(
-            root_rows,
-            [(n2 // 4, LANES)],
-            ru,
-            *parts,
-            scratch=[pltpu.VMEM((s2, COLS), F32)],
-        )
+        (x_root,) = gathered(packed_to, COLS, [(n2 // 4, LANES)], ru, parts)
     with jax.named_scope("mid_upper"):
         keep, send, x_root = kernel(
             root_to_mid,
@@ -561,8 +599,9 @@
             x_root,
             swap("leaf", x_root, 2),
         )
-        pieces = sum_front(keep, send)
-        (x_mid,) = kernel(mid_upper, [(n1 // 2, LANES)], mu, y_mid_full, *pieces)
+        mine, theirs = sum_front(keep, send)
+        (known,) = kernel(functools.partial(own_half, 2 * COLS), [(n1, 2 * COLS)], mu, y_mid_full, mine)
+        (x_mid,) = kernel(mid_upper, [(n1 // 2, LANES)], mu, y_mid_full, theirs, known)
         from_root, root_field, root_adjoint = kernel(
             root_to_leaf,
             [(s0, LANES), (2, COLS, n2), (2, COLS, n2)],
@@ -581,8 +620,11 @@
         )
         x_other = swap("leaf", x_mid, 2)
         mid_field, mid_adjoint = kernel(mid_outputs, [(2, 2, COLS, n1)] * 2, x_mid, x_other)
-        pieces = sum_front(keep, send, mid_field)
-        leaf_field, leaf_adjoint = kernel(leaf_upper, [(2, COLS, n0)] * 2, lu, y_full, *pieces)
+        mine, theirs = sum_front(keep, send, x_other)
+        (known,) = kernel(functools.partial(own_half, LANES), [(n0, LANES)], lu, y_full, mine)
+        leaf_field, leaf_adjoint = kernel(
+            leaf_upper, [(2, COLS, n0)] * 2, lu, y_full, theirs, after(known, mid_field)
+        )
     return tuple(
         jnp.swapaxes(x, -1, -2)
         for x in (leaf_field, mid_field, root_field, leaf_adjoint, mid_adjoint, root_adjoint)

time: 119 us -> 117 us (0.983)
  waiting for transfers between devices: 45 us -> 40.3 us
  Pallas kernels: 24.7 us -> 28.7 us
    ppermute x49, waiting for transfers between devices: 33.9 us -> 28.3 us  [swap(): return lax.ppermute(x, axis, [(i, i ^ k) for i in range(size)])]
    pallas_call x38 -> x46, Pallas kernels: 24.7 us -> 28.7 us  [kernel(): pl.pallas_call(fn, out_shape=[jax.ShapeDtypeStruct(*o) for o in outs], in...]
  transfers between devices with their start and end apart: 53 -> 53, of which waited for: 37 -> 34; matrix products, arithmetic and copies ran while one was open for 0% -> 0% of each run, Pallas kernels for 11% -> 18%
where the time goes in v10:
time: 117 us
  starting transfers between devices  46.8 us (40%)
  waiting for transfers between devices  40.3 us (34%)
  Pallas kernels  28.7 us (25%)
    ppermute x49, starting transfers between devices, swap(): return lax.ppermute(x, axis, [(i, i ^ k) for i in range(size)])  41.5 us
    pallas_call x46, Pallas kernels, kernel(): pl.pallas_call(fn, out_shape=[jax.ShapeDtypeStruct(*o) for o in outs], in...  28.7 us
    ppermute x49, waiting for transfers between devices, swap(): return lax.ppermute(x, axis, [(i, i ^ k) for i in range(size)])  28.3 us
    ppermute x4, waiting for transfers between devices, sum_front(): lax.ppermute(total, 'front', pairs)  12.1 us
    ppermute x4, starting transfers between devices, sum_front(): lax.ppermute(total, 'front', pairs)  5.24 us
  transfers between devices with their start and end apart: 53, of which 34 were waited for; matrix products, arithmetic and copies ran while one was open for 0% of the time, Pallas kernels for 18%

profile of v10, /device:TPU:0, one launch (start us, length us, event | category | flops | bytes accessed | tf_op | source)
XLA Modules:
  0.0 116.9 jit_solution(18446448578071521018)
XLA Ops:
  1.7 3.1 %collective-permute-start = (f32[32,128]{1,0:T(8,128)S(1)}, f32[32,128]{1,0:T(8,128)S(1)}, u32[]{:S(2)}, u32[]{:S(2)}) collective-permute-start(f32[32,128]{1,0:T(8,128)S(1)} %get-tuple-element.64), channel_id=1, source_target_pairs={{0,8},{8,0},{16,24},{24,16},{1,9},{9,1},{17,25},{25,17},{2,10},{10... | collective-permute-start | bytes 49160 | tf_op jit(solution)/shard_map/right_hand_sides/ppermute | solution.py:100
  4.8 1.7 %collective-permute-done.came.near = f32[32,128]{1,0:T(8,128)S(1)} collective-permute-done((f32[32,128]{1,0:T(8,128)S(1)}, f32[32,128]{1,0:T(8,128)S(1)}, u32[]{:S(2)}, u32[]{:S(2)}) %collective-permute-start) | collective-permute-done | bytes 16416 | tf_op jit(solution)/shard_map/right_hand_sides/ppermute | solution.py:100
  6.5 3.0 %collective-permute-start.1 = (f32[32,128]{1,0:T(8,128)S(1)}, f32[32,128]{1,0:T(8,128)S(1)}, u32[]{:S(2)}, u32[]{:S(2)}) collective-permute-start(f32[32,128]{1,0:T(8,128)S(1)} %right_hand_sides.6), channel_id=1, source_target_pairs={{0,16},{8,24},{16,0},{24,8},{1,17},{9,25},{17,1},{25,9},{2,18},{10... | collective-permute-start | bytes 49160 | tf_op jit(solution)/shard_map/right_hand_sides/ppermute | solution.py:100
  11.3 1.9 %collective-permute-start.3 = (f32[72,128]{1,0:T(8,128)S(1)}, f32[72,128]{1,0:T(8,128)S(1)}, u32[]{:S(2)}, u32[]{:S(2)}) collective-permute-start(f32[72,128]{1,0:T(8,128)S(1)} %right_hand_sides.7.refs_0_), channel_id=1, source_target_pairs={{0,4},{1,5},{2,6},{3,7},{4,0},{5,1},{6,2},{7,3},{8,12},{9,13},{10,... | collective-permute-start | bytes 110600 | tf_op jit(solution)/shard_map/leaf_lower/ppermute | solution.py:100
  13.3 1.5 %collective-permute-start.2 = (f32[72,128]{1,0:T(8,128)S(1)}, f32[72,128]{1,0:T(8,128)S(1)}, u32[]{:S(2)}, u32[]{:S(2)}) collective-permute-start(f32[72,128]{1,0:T(8,128)S(1)} %right_hand_sides.7.refs_0_), channel_id=1, source_target_pairs={{0,2},{1,3},{2,0},{3,1},{4,6},{5,7},{6,4},{7,5},{8,10},{9,11},{10,... | collective-permute-start | bytes 110600 | tf_op jit(solution)/shard_map/leaf_lower/ppermute | solution.py:100
  15.4 1.9 %collective-permute-done.2.refs_0_.refs_4_ = f32[72,128]{1,0:T(8,128)S(1)} collective-permute-done((f32[72,128]{1,0:T(8,128)S(1)}, f32[72,128]{1,0:T(8,128)S(1)}, u32[]{:S(2)}, u32[]{:S(2)}) %collective-permute-start.2) | collective-permute-done | bytes 36896 | tf_op jit(solution)/shard_map/leaf_lower/ppermute | solution.py:100
  22.8 2.3 %collective-permute-start.12 = (f32[64,128]{1,0:T(8,128)S(1)}, f32[64,128]{1,0:T(8,128)S(1)}, u32[]{:S(2)}, u32[]{:S(2)}) collective-permute-start(f32[64,128]{1,0:T(8,128)S(1)} %leaf_lower.5.mine.refs_0_), channel_id=1, source_target_pairs={{0,6},{1,7},{2,4},{3,5},{4,2},{5,3},{6,0},{7,1},{8,14},{9,15},{10,... | collective-permute-start | bytes 98312 | tf_op jit(solution)/shard_map/mid_lower/ppermute | solution.py:100
  26.0 1.6 %mid_lower.11 = (bf16[512,1024]{1,0:T(8,128)(2,1)S(1)}, bf16[256,2048]{1,0:T(8,128)(2,1)S(1)}) custom-call(f32[2,1,256,512]{3,2,1,0:T(8,128)} %refs_0_.1, f32[2,2,128,1024]{3,2,1,0:T(8,128)} %refs_1_.5), custom_call_target="tpu_custom_call" | custom-call | flops 262144000 | bytes 374491 | tf_op jit(solution)/shard_map/mid_lower/pallas_call | solution.py:135
  29.5 1.6 %collective-permute-start.14 = (f32[64,128]{1,0:T(8,128)S(1)}, f32[64,128]{1,0:T(8,128)S(1)}, u32[]{:S(2)}, u32[]{:S(2)}) collective-permute-start(f32[64,128]{1,0:T(8,128)S(1)} %get-tuple-element.77), channel_id=1, source_target_pairs={{0,8},{8,0},{16,24},{24,16},{1,9},{9,1},{17,25},{25,17},{2,10},{10... | collective-permute-start | bytes 98312 | tf_op jit(solution)/shard_map/mid_lower/ppermute | solution.py:100
  33.5 1.7 %collective-permute-start.17 = (f32[64,128]{1,0:T(8,128)S(1)}, f32[64,128]{1,0:T(8,128)S(1)}, u32[]{:S(2)}, u32[]{:S(2)}) collective-permute-start(f32[64,128]{1,0:T(8,128)S(1)} %mid_lower.15.mine), channel_id=1, source_target_pairs={{0,4},{1,5},{2,6},{3,7},{4,0},{5,1},{6,2},{7,3},{8,12},{9,13},{10,... | collective-permute-start | bytes 98312 | tf_op jit(solution)/shard_map/mid_lower/ppermute | solution.py:100
  37.4 1.7 %collective-permute-done.16.refs_0_ = f32[64,128]{1,0:T(8,128)S(1)} collective-permute-done((f32[64,128]{1,0:T(8,128)S(1)}, f32[64,128]{1,0:T(8,128)S(1)}, u32[]{:S(2)}, u32[]{:S(2)}) %collective-permute-start.16) | collective-permute-done | bytes 32800 | tf_op jit(solution)/shard_map/mid_lower/ppermute | solution.py:100
  39.2 1.8 %mid_lower.18.matrix = bf16[512,2048]{1,0:T(8,128)(2,1)S(1)} custom-call(f32[2,2,256,1024]{3,2,1,0:T(8,128)} %refs_0_.2), custom_call_target="tpu_custom_call" | custom-call | flops 262144000 | bytes 374491 | tf_op jit(solution)/shard_map/mid_lower/pallas_call | solution.py:135
  44.4 2.1 %collective-permute-start.26 = (f32[64,128]{1,0:T(8,128)S(1)}, f32[64,128]{1,0:T(8,128)S(1)}, u32[]{:S(2)}, u32[]{:S(2)}) collective-permute-start(f32[64,128]{1,0:T(8,128)S(1)} %mid_lower.19.mine.refs_0_), channel_id=1, source_target_pairs={{0,6},{1,7},{2,4},{3,5},{4,2},{5,3},{6,0},{7,1},{8,14},{9,15},{10,... | collective-permute-start | bytes 98312 | tf_op jit(solution)/shard_map/root_cut/ppermute | solution.py:100
  51.2 2.7 %collective-permute-start.28 = (f32[64,128]{1,0:T(8,128)S(1)}, f32[64,128]{1,0:T(8,128)S(1)}, u32[]{:S(2)}, u32[]{:S(2)}) collective-permute-start(f32[64,128]{1,0:T(8,128)S(1)} %get-tuple-element.88), channel_id=1, source_target_pairs={{0,16},{8,24},{16,0},{24,8},{1,17},{9,25},{17,1},{25,9},{2,18},{10... | collective-permute-start | bytes 98312 | tf_op jit(solution)/shard_map/root_cut/ppermute | solution.py:100
  54.6 1.5 %collective-permute-done.28.refs_1_ = f32[64,128]{1,0:T(8,128)S(1)} collective-permute-done((f32[64,128]{1,0:T(8,128)S(1)}, f32[64,128]{1,0:T(8,128)S(1)}, u32[]{:S(2)}, u32[]{:S(2)}) %collective-permute-start.28) | collective-permute-done | bytes 32800 | tf_op jit(solution)/shard_map/root_cut/ppermute | solution.py:100
  56.2 1.6 %collective-permute-start.31 = (f32[64,128]{1,0:T(8,128)S(1)}, f32[64,128]{1,0:T(8,128)S(1)}, u32[]{:S(2)}, u32[]{:S(2)}) collective-permute-start(f32[64,128]{1,0:T(8,128)S(1)} %root_cut.13.mine), channel_id=1, source_target_pairs={{0,4},{1,5},{2,6},{3,7},{4,0},{5,1},{6,2},{7,3},{8,12},{9,13},{10,... | collective-permute-start | bytes 98312 | tf_op jit(solution)/shard_map/root_solve/ppermute | solution.py:100
  60.1 1.6 %collective-permute-done.30.refs_0_ = f32[64,128]{1,0:T(8,128)S(1)} collective-permute-done((f32[64,128]{1,0:T(8,128)S(1)}, f32[64,128]{1,0:T(8,128)S(1)}, u32[]{:S(2)}, u32[]{:S(2)}) %collective-permute-start.30) | collective-permute-done | bytes 32800 | tf_op jit(solution)/shard_map/root_solve/ppermute | solution.py:100
  63.6 1.7 %root_solve.9.refs_0_ = f32[256,32]{1,0:T(8,128)S(1)} custom-call(bf16[512,4096]{1,0:T(8,128)(2,1)S(1)} %root_cut.8.matrix, f32[64,128]{1,0:T(8,128)S(1)} %root_cut.13.mine, f32[64,128]{1,0:T(8,128)S(1)} %collective-permute-done.29.other, f32[64,128]{1,0:T(8,128)S(1)} %collective-permute-done.30.refs_0_, f32[64,128]{1,0:T(8,128)S(1)} %collective-permute-done.31.refs_1_, ...), custom_call_target="tpu_custom_call" | custom-call | tf_op jit(solution)/shard_map/root_solve/pallas_call | solution.py:135
  67.7 2.1 %collective-permute-start.39 = (f32[64,128]{1,0:T(8,128)S(1)}, f32[64,128]{1,0:T(8,128)S(1)}, u32[]{:S(2)}, u32[]{:S(2)}) collective-permute-start(f32[64,128]{1,0:T(8,128)S(1)} %root_solve.11.mine), channel_id=1, source_target_pairs={{0,6},{1,7},{2,4},{3,5},{4,2},{5,3},{6,0},{7,1},{8,14},{9,15},{10,... | collective-permute-start | bytes 98312 | tf_op jit(solution)/shard_map/root_solve/ppermute | solution.py:100
  70.7 1.5 %root_solve.13 = (bf16[2048,512]{1,0:T(8,128)(2,1)S(1)}, bf16[1024,256]{1,0:T(8,128)(2,1)S(1)}, bf16[128,1024]{1,0:T(8,128)(2,1)S(1)}) custom-call(f32[2,2,1024,256]{3,2,1,0:T(8,128)S(1)} %copy-done, f32[2,1,512,128]{3,2,1,0:T(8,128)S(1)} %copy-done.5, f32[2,1,64,512]{3,2,1,0:T(8,128)S(1)} %copy-done.6), custom_call_target="tpu_custom_call" | custom-call | flops 360448000 | bytes 514925 | tf_op jit(solution)/shard_map/root_solve/pallas_call | solution.py:135
  72.8 1.7 %root_solve.14.refs_0_ = f32[256,32]{1,0:T(8,128)S(1)} custom-call(bf16[512,4096]{1,0:T(8,128)(2,1)S(1)} %root_solve.10.matrix, f32[64,128]{1,0:T(8,128)S(1)} %root_solve.11.mine, f32[64,128]{1,0:T(8,128)S(1)} %collective-permute-done.37.other, f32[64,128]{1,0:T(8,128)S(1)} %collective-permute-done.35.refs_0_, ...), custom_call_target="tpu_custom_call" | custom-call | tf_op jit(solution)/shard_map/root_solve/pallas_call | solution.py:135
  75.4 2.6 %collective-permute-start.41 = (f32[64,128]{1,0:T(8,128)S(1)}, f32[64,128]{1,0:T(8,128)S(1)}, u32[]{:S(2)}, u32[]{:S(2)}) collective-permute-start(f32[64,128]{1,0:T(8,128)S(1)} %root_solve.15.mine), channel_id=1, source_target_pairs={{0,16},{8,24},{16,0},{24,8},{1,17},{9,25},{17,1},{25,9},{2,18},{10... | collective-permute-start | bytes 98312 | tf_op jit(solution)/shard_map/mid_upper/ppermute | solution.py:100
  78.0 2.2 %collective-permute-done.41.other = f32[64,128]{1,0:T(8,128)S(1)} collective-permute-done((f32[64,128]{1,0:T(8,128)S(1)}, f32[64,128]{1,0:T(8,128)S(1)}, u32[]{:S(2)}, u32[]{:S(2)}) %collective-permute-start.41) | collective-permute-done | bytes 32800 | tf_op jit(solution)/shard_map/mid_upper/ppermute | solution.py:100
  83.7 4.1 %collective-permute-done.44.refs_1_ = f32[256,128]{1,0:T(8,128)S(1)} collective-permute-done((f32[256,128]{1,0:T(8,128)S(1)}, f32[256,128]{1,0:T(8,128)S(1)}, u32[]{:S(2)}, u32[]{:S(2)}) %collective-permute-start.44) | collective-permute-done | bytes 131104 | tf_op jit(solution)/shard_map/mid_upper/ppermute | solution.py:453
  87.8 1.6 %collective-permute-start.45 = (f32[256,128]{1,0:T(8,128)S(1)}, f32[256,128]{1,0:T(8,128)S(1)}, u32[]{:S(2)}, u32[]{:S(2)}) collective-permute-start(f32[256,128]{1,0:T(8,128)S(1)} %mid_upper.10.refs_0_), channel_id=1, source_target_pairs={{0,4},{1,3},{2,6},{3,1},{4,0},{5,7},{6,2},{7,5},{8,12},{9,11},{10,... | collective-permute-start | bytes 393224 | tf_op jit(solution)/shard_map/mid_upper/ppermute | solution.py:453
  89.4 3.5 %collective-permute-done.45.refs_1_ = f32[256,128]{1,0:T(8,128)S(1)} collective-permute-done((f32[256,128]{1,0:T(8,128)S(1)}, f32[256,128]{1,0:T(8,128)S(1)}, u32[]{:S(2)}, u32[]{:S(2)}) %collective-permute-start.45) | collective-permute-done | bytes 131104 | tf_op jit(solution)/shard_map/mid_upper/ppermute | solution.py:453
  93.0 1.7 %collective-permute-start.42 = (f32[128,128]{1,0:T(8,128)S(1)}, f32[128,128]{1,0:T(8,128)S(1)}, u32[]{:S(2)}, u32[]{:S(2)}) collective-permute-start(f32[128,128]{1,0:T(8,128)S(1)} %get-tuple-element.104.mine), channel_id=1, source_target_pairs={{0,8},{8,0},{16,24},{24,16},{1,9},{9,1},{17,25},{25,17},{2,10},{10... | collective-permute-start | bytes 196616 | tf_op jit(solution)/shard_map/mid_upper/ppermute | solution.py:100
  98.7 1.4 %collective-permute-done.47.other = f32[64,128]{1,0:T(8,128)S(1)} collective-permute-done((f32[64,128]{1,0:T(8,128)S(1)}, f32[64,128]{1,0:T(8,128)S(1)}, u32[]{:S(2)}, u32[]{:S(2)}) %collective-permute-start.47) | collective-permute-done | bytes 32800 | tf_op jit(solution)/shard_map/leaf_upper/ppermute | solution.py:100
  103.2 3.9 %collective-permute-done.49.refs_1_ = f32[256,128]{1,0:T(8,128)S(1)} collective-permute-done((f32[256,128]{1,0:T(8,128)S(1)}, f32[256,128]{1,0:T(8,128)S(1)}, u32[]{:S(2)}, u32[]{:S(2)}) %collective-permute-start.49) | collective-permute-done | bytes 131104 | tf_op jit(solution)/shard_map/leaf_upper/ppermute | solution.py:453
  107.1 1.6 %collective-permute-start.50 = (f32[256,128]{1,0:T(8,128)S(1)}, f32[256,128]{1,0:T(8,128)S(1)}, u32[]{:S(2)}, u32[]{:S(2)}) collective-permute-start(f32[256,128]{1,0:T(8,128)S(1)} %leaf_upper.9.refs_0_), channel_id=1, source_target_pairs={{0,4},{1,3},{2,6},{3,1},{4,0},{5,7},{6,2},{7,5},{8,12},{9,11},{10,... | collective-permute-start | bytes 393224 | tf_op jit(solution)/shard_map/leaf_upper/ppermute | solution.py:453
  108.7 2.8 %collective-permute-start.51 = (f32[128,128]{1,0:T(8,128)S(1)}, f32[128,128]{1,0:T(8,128)S(1)}, u32[]{:S(2)}, u32[]{:S(2)}) collective-permute-start(f32[128,128]{1,0:T(8,128)S(1)} %get-tuple-element.109.mine), channel_id=1, source_target_pairs={{0,16},{8,24},{16,0},{24,8},{1,17},{9,25},{17,1},{25,9},{2,18},{10... | collective-permute-start | bytes 196616 | tf_op jit(solution)/shard_map/leaf_upper/ppermute | solution.py:100
  112.2 2.4 %collective-permute-done.51.other = f32[128,128]{1,0:T(8,128)S(1)} collective-permute-done((f32[128,128]{1,0:T(8,128)S(1)}, f32[128,128]{1,0:T(8,128)S(1)}, u32[]{:S(2)}, u32[]{:S(2)}) %collective-permute-start.51) | collective-permute-done | bytes 65568 | tf_op jit(solution)/shard_map/leaf_upper/ppermute | solution.py:100
  (134 shorter events, 47.7 us)
Async XLA Ops:
  1.7 4.8 %collective-permute-start = (f32[32,128]{1,0:T(8,128)S(1)}, f32[32,128]{1,0:T(8,128)S(1)}, u32[]{:S(2)}, u32[]{:S(2)}) collective-permute-start(f32[32,128]{1,0:T(8,128)S(1)} %get-tuple-element.64), channel_id=1, source_target_pairs={{0,8},{8,0},{16,24},{24,16},{1,9},{9,1},{17,25},{25,17},{2,10},{10... | collective-permute-start | bytes 49160 | tf_op jit(solution)/shard_map/right_hand_sides/ppermute | solution.py:100
  6.5 4.7 %collective-permute-start.1 = (f32[32,128]{1,0:T(8,128)S(1)}, f32[32,128]{1,0:T(8,128)S(1)}, u32[]{:S(2)}, u32[]{:S(2)}) collective-permute-start(f32[32,128]{1,0:T(8,128)S(1)} %right_hand_sides.6), channel_id=1, source_target_pairs={{0,16},{8,24},{16,0},{24,8},{1,17},{9,25},{17,1},{25,9},{2,18},{10... | collective-permute-start | bytes 49160 | tf_op jit(solution)/shard_map/right_hand_sides/ppermute | solution.py:100
  11.3 4.0 %collective-permute-start.3 = (f32[72,128]{1,0:T(8,128)S(1)}, f32[72,128]{1,0:T(8,128)S(1)}, u32[]{:S(2)}, u32[]{:S(2)}) collective-permute-start(f32[72,128]{1,0:T(8,128)S(1)} %right_hand_sides.7.refs_0_), channel_id=1, source_target_pairs={{0,4},{1,5},{2,6},{3,7},{4,0},{5,1},{6,2},{7,3},{8,12},{9,13},{10,... | collective-permute-start | bytes 110600 | tf_op jit(solution)/shard_map/leaf_lower/ppermute | solution.py:100
  13.3 4.0 %collective-permute-start.2 = (f32[72,128]{1,0:T(8,128)S(1)}, f32[72,128]{1,0:T(8,128)S(1)}, u32[]{:S(2)}, u32[]{:S(2)}) collective-permute-start(f32[72,128]{1,0:T(8,128)S(1)} %right_hand_sides.7.refs_0_), channel_id=1, source_target_pairs={{0,2},{1,3},{2,0},{3,1},{4,6},{5,7},{6,4},{7,5},{8,10},{9,11},{10,... | collective-permute-start | bytes 110600 | tf_op jit(solution)/shard_map/leaf_lower/ppermute | solution.py:100
  14.7 4.9 %collective-permute-start.5 = (f32[72,128]{1,0:T(8,128)S(1)}, f32[72,128]{1,0:T(8,128)S(1)}, u32[]{:S(2)}, u32[]{:S(2)}) collective-permute-start(f32[72,128]{1,0:T(8,128)S(1)} %right_hand_sides.7.refs_0_), channel_id=1, source_target_pairs={{0,6},{1,7},{2,4},{3,5},{4,2},{5,3},{6,0},{7,1},{8,14},{9,15},{10,... | collective-permute-start | bytes 110600 | tf_op jit(solution)/shard_map/leaf_lower/ppermute | solution.py:100
  17.2 3.6 %collective-permute-start.7 = (f32[144,128]{1,0:T(8,128)S(1)}, f32[144,128]{1,0:T(8,128)S(1)}, u32[]{:S(2)}, u32[]{:S(2)}) collective-permute-start(f32[144,128]{1,0:T(8,128)S(1)} %leaf_lower.3), channel_id=1, source_target_pairs={{0,1},{1,0},{2,3},{3,2},{4,5},{5,4},{6,7},{7,6},{8,9},{9,8},{10,11... | collective-permute-start | bytes 221192 | tf_op jit(solution)/shard_map/leaf_lower/ppermute | solution.py:100
  21.5 4.0 %collective-permute-start.9 = (f32[64,128]{1,0:T(8,128)S(1)}, f32[64,128]{1,0:T(8,128)S(1)}, u32[]{:S(2)}, u32[]{:S(2)}) collective-permute-start(f32[64,128]{1,0:T(8,128)S(1)} %leaf_lower.5.mine.refs_0_), channel_id=1, source_target_pairs={{0,4},{1,5},{2,6},{3,7},{4,0},{5,1},{6,2},{7,3},{8,12},{9,13},{10,... | collective-permute-start | bytes 98312 | tf_op jit(solution)/shard_map/mid_lower/ppermute | solution.py:100
  22.1 3.9 %collective-permute-start.8 = (f32[64,128]{1,0:T(8,128)S(1)}, f32[64,128]{1,0:T(8,128)S(1)}, u32[]{:S(2)}, u32[]{:S(2)}) collective-permute-start(f32[64,128]{1,0:T(8,128)S(1)} %leaf_lower.5.mine.refs_0_), channel_id=1, source_target_pairs={{0,2},{1,3},{2,0},{3,1},{4,6},{5,7},{6,4},{7,5},{8,10},{9,11},{10,... | collective-permute-start | bytes 98312 | tf_op jit(solution)/shard_map/mid_lower/ppermute | solution.py:100
  22.8 4.9 %collective-permute-start.12 = (f32[64,128]{1,0:T(8,128)S(1)}, f32[64,128]{1,0:T(8,128)S(1)}, u32[]{:S(2)}, u32[]{:S(2)}) collective-permute-start(f32[64,128]{1,0:T(8,128)S(1)} %leaf_lower.5.mine.refs_0_), channel_id=1, source_target_pairs={{0,6},{1,7},{2,4},{3,5},{4,2},{5,3},{6,0},{7,1},{8,14},{9,15},{10,... | collective-permute-start | bytes 98312 | tf_op jit(solution)/shard_map/mid_lower/ppermute | solution.py:100
  29.5 4.0 %collective-permute-start.14 = (f32[64,128]{1,0:T(8,128)S(1)}, f32[64,128]{1,0:T(8,128)S(1)}, u32[]{:S(2)}, u32[]{:S(2)}) collective-permute-start(f32[64,128]{1,0:T(8,128)S(1)} %get-tuple-element.77), channel_id=1, source_target_pairs={{0,8},{8,0},{16,24},{24,16},{1,9},{9,1},{17,25},{25,17},{2,10},{10... | collective-permute-start | bytes 98312 | tf_op jit(solution)/shard_map/mid_lower/ppermute | solution.py:100
  31.9 9.2 %collective-permute-start.20 = (f32[128,128]{1,0:T(8,128)S(1)}, f32[128,128]{1,0:T(8,128)S(1)}, u32[]{:S(2)}, u32[]{:S(2)}) collective-permute-start(f32[128,128]{1,0:T(8,128)S(1)} %get-tuple-element.82), channel_id=1, source_target_pairs={{0,8},{8,0},{16,24},{24,16},{1,9},{9,1},{17,25},{25,17},{2,10},{10... | collective-permute-start | bytes 196616 | tf_op jit(solution)/shard_map/mid_lower/ppermute | solution.py:100
  33.5 3.9 %collective-permute-start.17 = (f32[64,128]{1,0:T(8,128)S(1)}, f32[64,128]{1,0:T(8,128)S(1)}, u32[]{:S(2)}, u32[]{:S(2)}) collective-permute-start(f32[64,128]{1,0:T(8,128)S(1)} %mid_lower.15.mine), channel_id=1, source_target_pairs={{0,4},{1,5},{2,6},{3,7},{4,0},{5,1},{6,2},{7,3},{8,12},{9,13},{10,... | collective-permute-start | bytes 98312 | tf_op jit(solution)/shard_map/mid_lower/ppermute | solution.py:100
  35.2 3.9 %collective-permute-start.16 = (f32[64,128]{1,0:T(8,128)S(1)}, f32[64,128]{1,0:T(8,128)S(1)}, u32[]{:S(2)}, u32[]{:S(2)}) collective-permute-start(f32[64,128]{1,0:T(8,128)S(1)} %mid_lower.15.mine), channel_id=1, source_target_pairs={{0,2},{1,3},{2,0},{3,1},{4,6},{5,7},{6,4},{7,5},{8,10},{9,11},{10,... | collective-permute-start | bytes 98312 | tf_op jit(solution)/shard_map/mid_lower/ppermute | solution.py:100
  36.1 4.9 %collective-permute-start.19 = (f32[64,128]{1,0:T(8,128)S(1)}, f32[64,128]{1,0:T(8,128)S(1)}, u32[]{:S(2)}, u32[]{:S(2)}) collective-permute-start(f32[64,128]{1,0:T(8,128)S(1)} %mid_lower.15.mine), channel_id=1, source_target_pairs={{0,6},{1,7},{2,4},{3,5},{4,2},{5,3},{6,0},{7,1},{8,14},{9,15},{10,... | collective-permute-start | bytes 98312 | tf_op jit(solution)/shard_map/mid_lower/ppermute | solution.py:100
  43.0 4.0 %collective-permute-start.23 = (f32[64,128]{1,0:T(8,128)S(1)}, f32[64,128]{1,0:T(8,128)S(1)}, u32[]{:S(2)}, u32[]{:S(2)}) collective-permute-start(f32[64,128]{1,0:T(8,128)S(1)} %mid_lower.19.mine.refs_0_), channel_id=1, source_target_pairs={{0,4},{1,5},{2,6},{3,7},{4,0},{5,1},{6,2},{7,3},{8,12},{9,13},{10,... | collective-permute-start | bytes 98312 | tf_op jit(solution)/shard_map/root_cut/ppermute | solution.py:100
  43.5 3.9 %collective-permute-start.22 = (f32[64,128]{1,0:T(8,128)S(1)}, f32[64,128]{1,0:T(8,128)S(1)}, u32[]{:S(2)}, u32[]{:S(2)}) collective-permute-start(f32[64,128]{1,0:T(8,128)S(1)} %mid_lower.19.mine.refs_0_), channel_id=1, source_target_pairs={{0,2},{1,3},{2,0},{3,1},{4,6},{5,7},{6,4},{7,5},{8,10},{9,11},{10,... | collective-permute-start | bytes 98312 | tf_op jit(solution)/shard_map/root_cut/ppermute | solution.py:100
  44.4 4.8 %collective-permute-start.26 = (f32[64,128]{1,0:T(8,128)S(1)}, f32[64,128]{1,0:T(8,128)S(1)}, u32[]{:S(2)}, u32[]{:S(2)}) collective-permute-start(f32[64,128]{1,0:T(8,128)S(1)} %mid_lower.19.mine.refs_0_), channel_id=1, source_target_pairs={{0,6},{1,7},{2,4},{3,5},{4,2},{5,3},{6,0},{7,1},{8,14},{9,15},{10,... | collective-permute-start | bytes 98312 | tf_op jit(solution)/shard_map/root_cut/ppermute | solution.py:100
  51.2 4.9 %collective-permute-start.28 = (f32[64,128]{1,0:T(8,128)S(1)}, f32[64,128]{1,0:T(8,128)S(1)}, u32[]{:S(2)}, u32[]{:S(2)}) collective-permute-start(f32[64,128]{1,0:T(8,128)S(1)} %get-tuple-element.88), channel_id=1, source_target_pairs={{0,16},{8,24},{16,0},{24,8},{1,17},{9,25},{17,1},{25,9},{2,18},{10... | collective-permute-start | bytes 98312 | tf_op jit(solution)/shard_map/root_cut/ppermute | solution.py:100
  56.2 3.9 %collective-permute-start.31 = (f32[64,128]{1,0:T(8,128)S(1)}, f32[64,128]{1,0:T(8,128)S(1)}, u32[]{:S(2)}, u32[]{:S(2)}) collective-permute-start(f32[64,128]{1,0:T(8,128)S(1)} %root_cut.13.mine), channel_id=1, source_target_pairs={{0,4},{1,5},{2,6},{3,7},{4,0},{5,1},{6,2},{7,3},{8,12},{9,13},{10,... | collective-permute-start | bytes 98312 | tf_op jit(solution)/shard_map/root_solve/ppermute | solution.py:100
  57.7 3.9 %collective-permute-start.30 = (f32[64,128]{1,0:T(8,128)S(1)}, f32[64,128]{1,0:T(8,128)S(1)}, u32[]{:S(2)}, u32[]{:S(2)}) collective-permute-start(f32[64,128]{1,0:T(8,128)S(1)} %root_cut.13.mine), channel_id=1, source_target_pairs={{0,2},{1,3},{2,0},{3,1},{4,6},{5,7},{6,4},{7,5},{8,10},{9,11},{10,... | collective-permute-start | bytes 98312 | tf_op jit(solution)/shard_map/root_solve/ppermute | solution.py:100
  58.8 4.8 %collective-permute-start.33 = (f32[64,128]{1,0:T(8,128)S(1)}, f32[64,128]{1,0:T(8,128)S(1)}, u32[]{:S(2)}, u32[]{:S(2)}) collective-permute-start(f32[64,128]{1,0:T(8,128)S(1)} %root_cut.13.mine), channel_id=1, source_target_pairs={{0,6},{1,7},{2,4},{3,5},{4,2},{5,3},{6,0},{7,1},{8,14},{9,15},{10,... | collective-permute-start | bytes 98312 | tf_op jit(solution)/shard_map/root_solve/ppermute | solution.py:100
  66.2 4.0 %collective-permute-start.36 = (f32[64,128]{1,0:T(8,128)S(1)}, f32[64,128]{1,0:T(8,128)S(1)}, u32[]{:S(2)}, u32[]{:S(2)}) collective-permute-start(f32[64,128]{1,0:T(8,128)S(1)} %root_solve.11.mine), channel_id=1, source_target_pairs={{0,4},{1,5},{2,6},{3,7},{4,0},{5,1},{6,2},{7,3},{8,12},{9,13},{10,... | collective-permute-start | bytes 98312 | tf_op jit(solution)/shard_map/root_solve/ppermute | solution.py:100
  66.8 3.9 %collective-permute-start.35 = (f32[64,128]{1,0:T(8,128)S(1)}, f32[64,128]{1,0:T(8,128)S(1)}, u32[]{:S(2)}, u32[]{:S(2)}) collective-permute-start(f32[64,128]{1,0:T(8,128)S(1)} %root_solve.11.mine), channel_id=1, source_target_pairs={{0,2},{1,3},{2,0},{3,1},{4,6},{5,7},{6,4},{7,5},{8,10},{9,11},{10,... | collective-permute-start | bytes 98312 | tf_op jit(solution)/shard_map/root_solve/ppermute | solution.py:100
  67.7 4.8 %collective-permute-start.39 = (f32[64,128]{1,0:T(8,128)S(1)}, f32[64,128]{1,0:T(8,128)S(1)}, u32[]{:S(2)}, u32[]{:S(2)}) collective-permute-start(f32[64,128]{1,0:T(8,128)S(1)} %root_solve.11.mine), channel_id=1, source_target_pairs={{0,6},{1,7},{2,4},{3,5},{4,2},{5,3},{6,0},{7,1},{8,14},{9,15},{10,... | collective-permute-start | bytes 98312 | tf_op jit(solution)/shard_map/root_solve/ppermute | solution.py:100
  75.4 4.9 %collective-permute-start.41 = (f32[64,128]{1,0:T(8,128)S(1)}, f32[64,128]{1,0:T(8,128)S(1)}, u32[]{:S(2)}, u32[]{:S(2)}) collective-permute-start(f32[64,128]{1,0:T(8,128)S(1)} %root_solve.15.mine), channel_id=1, source_target_pairs={{0,16},{8,24},{16,0},{24,8},{1,17},{9,25},{17,1},{25,9},{2,18},{10... | collective-permute-start | bytes 98312 | tf_op jit(solution)/shard_map/mid_upper/ppermute | solution.py:100
  82.8 5.0 %collective-permute-start.44 = (f32[256,128]{1,0:T(8,128)S(1)}, f32[256,128]{1,0:T(8,128)S(1)}, u32[]{:S(2)}, u32[]{:S(2)}) collective-permute-start(f32[256,128]{1,0:T(8,128)S(1)} %mid_upper.9.refs_0_), channel_id=1, source_target_pairs={{0,2},{1,5},{2,0},{3,7},{4,6},{5,1},{6,4},{7,3},{8,10},{9,13},{10,... | collective-permute-start | bytes 393224 | tf_op jit(solution)/shard_map/mid_upper/ppermute | solution.py:453
  87.8 5.0 %collective-permute-start.45 = (f32[256,128]{1,0:T(8,128)S(1)}, f32[256,128]{1,0:T(8,128)S(1)}, u32[]{:S(2)}, u32[]{:S(2)}) collective-permute-start(f32[256,128]{1,0:T(8,128)S(1)} %mid_upper.10.refs_0_), channel_id=1, source_target_pairs={{0,4},{1,3},{2,6},{3,1},{4,0},{5,7},{6,2},{7,5},{8,12},{9,11},{10,... | collective-permute-start | bytes 393224 | tf_op jit(solution)/shard_map/mid_upper/ppermute | solution.py:453
  93.0 4.5 %collective-permute-start.42 = (f32[128,128]{1,0:T(8,128)S(1)}, f32[128,128]{1,0:T(8,128)S(1)}, u32[]{:S(2)}, u32[]{:S(2)}) collective-permute-start(f32[128,128]{1,0:T(8,128)S(1)} %get-tuple-element.104.mine), channel_id=1, source_target_pairs={{0,8},{8,0},{16,24},{24,16},{1,9},{9,1},{17,25},{25,17},{2,10},{10... | collective-permute-start | bytes 196616 | tf_op jit(solution)/shard_map/mid_upper/ppermute | solution.py:100
  96.2 4.0 %collective-permute-start.47 = (f32[64,128]{1,0:T(8,128)S(1)}, f32[64,128]{1,0:T(8,128)S(1)}, u32[]{:S(2)}, u32[]{:S(2)}) collective-permute-start(f32[64,128]{1,0:T(8,128)S(1)} %mid_upper.13.mine), channel_id=1, source_target_pairs={{0,8},{8,0},{16,24},{24,16},{1,9},{9,1},{17,25},{25,17},{2,10},{10... | collective-permute-start | bytes 98312 | tf_op jit(solution)/shard_map/leaf_upper/ppermute | solution.py:100
  102.1 5.0 %collective-permute-start.49 = (f32[256,128]{1,0:T(8,128)S(1)}, f32[256,128]{1,0:T(8,128)S(1)}, u32[]{:S(2)}, u32[]{:S(2)}) collective-permute-start(f32[256,128]{1,0:T(8,128)S(1)} %leaf_upper.8.refs_0_), channel_id=1, source_target_pairs={{0,2},{1,5},{2,0},{3,7},{4,6},{5,1},{6,4},{7,3},{8,10},{9,13},{10,... | collective-permute-start | bytes 393224 | tf_op jit(solution)/shard_map/leaf_upper/ppermute | solution.py:453
  107.1 5.0 %collective-permute-start.50 = (f32[256,128]{1,0:T(8,128)S(1)}, f32[256,128]{1,0:T(8,128)S(1)}, u32[]{:S(2)}, u32[]{:S(2)}) collective-permute-start(f32[256,128]{1,0:T(8,128)S(1)} %leaf_upper.9.refs_0_), channel_id=1, source_target_pairs={{0,4},{1,3},{2,6},{3,1},{4,0},{5,7},{6,2},{7,5},{8,12},{9,11},{10,... | collective-permute-start | bytes 393224 | tf_op jit(solution)/shard_map/leaf_upper/ppermute | solution.py:453
  108.7 5.9 %collective-permute-start.51 = (f32[128,128]{1,0:T(8,128)S(1)}, f32[128,128]{1,0:T(8,128)S(1)}, u32[]{:S(2)}, u32[]{:S(2)}) collective-permute-start(f32[128,128]{1,0:T(8,128)S(1)} %get-tuple-element.109.mine), channel_id=1, source_target_pairs={{0,16},{8,24},{16,0},{24,8},{1,17},{9,25},{17,1},{25,9},{2,18},{10... | collective-permute-start | bytes 196616 | tf_op jit(solution)/shard_map/leaf_upper/ppermute | solution.py:100
  (28 other events, 100.7 us)

commit v11 on v10

--- a/solution.py
+++ b/solution.py
@@ -36,14 +36,34 @@
     return (product[:rows, n:] + product[rows:, :n]) + product[:rows, :n]
 
 
-def part_dot(matrix, at, x):
-    depth, count, half = matrix.shape[1] // 2, x.shape[0], x.shape[1] // 2
-    at = pl.multiple_of(at, LANES)
-    turned = jnp.concatenate([-x[:, half:], x[:, :half]], axis=1)
-    product = dot(matrix[:, pl.ds(at, count)], jnp.concatenate(split(x), axis=1))
-    product += dot(matrix[:, pl.ds(depth + at, count)], jnp.concatenate(split(turned), axis=1))
-    rows, n = product.shape[0] // 2, x.shape[1]
+def combined(product):
+    rows, n = product.shape[0] // 2, product.shape[1] // 2
     return (product[:rows, n:] + product[rows:, :n]) + product[:rows, :n]
+
+
+def turn(x, width):
+    half = width // 2
+    lane = lax.broadcasted_iota(jnp.int32, x.shape, 1) % width
+    return jnp.where(lane < half, -pltpu.roll(x, LANES - half, 1), pltpu.roll(x, half, 1))
+
+
+def spread(x, width):
+    high, low = split(x)
+    return jnp.concatenate(
+        [
+            jnp.concatenate([high[:, at : at + width], low[:, at : at + width]], axis=1)
+            for at in range(0, LANES, width)
+        ],
+        axis=0,
+    )
+
+
+def part_dot(matrix, at, blocks, width):
+    depth = matrix.shape[1] // 2
+    columns = jnp.concatenate([spread(x, width) for x in blocks], axis=0)
+    turned = jnp.concatenate([spread(turn(x, width), width) for x in blocks], axis=0)
+    count, at = columns.shape[0], pl.multiple_of(at, LANES)
+    return dot(matrix[:, pl.ds(at, count)], columns) + dot(matrix[:, pl.ds(depth + at, count)], turned)
 
 
 def pack(x):
@@ -146,10 +166,8 @@
 def chip_product(matrix, k, mine, other, width):
     here = lax.axis_index("front")
     odd = (here & 1) == 1
-    if width < LANES:
-        mine, other = unpack(mine, width), unpack(other, width)
-    x = jnp.concatenate([jnp.where(odd, other, mine), jnp.where(odd, mine, other)], axis=0)
-    return part_dot(matrix, ((here ^ k) // 2) * x.shape[0], x)
+    blocks = [jnp.where(odd, other, mine), jnp.where(odd, mine, other)]
+    return part_dot(matrix, ((here ^ k) // 2) * (2 * mine.shape[0] * (LANES // width)), blocks, width)
 
 
 def first_products(width, matrix, mine, other, *refs):
@@ -167,7 +185,7 @@
     if count == 3:
         known, mine, other = parts
         k = lax.axis_size("front") - 2
-        finish(known[...] + chip_product(matrix, k, mine[...], other[...], width), *rest)
+        finish(combined(known[...] + chip_product(matrix, k, mine[...], other[...], width)), *rest)
     else:
         assemble(rest[-1], parts, lax.axis_index("front"), width)
         finish(complex_dot(matrix[...], rest[-1][...]), *rest[:-1])
@@ -178,7 +196,7 @@
     scratch = []
     if 2 * rows % LANES == 0:
         mine, other, last, *near, last_other, both = parts
-        shape = (matrix.shape[0] // 2, width)
+        shape = (matrix.shape[0], 2 * width)
         (known,) = kernel(
             functools.partial(first_products, width), [shape], matrix, mine, other, *near[::-1], both
         )
@@ -201,11 +219,18 @@
 
 def half_product(theirs, width, matrix, y, piece):
     odd = (lax.axis_index("front") & 1) ^ theirs
-    rows, total = piece.shape[0], None
-    for chunk in range(LANES // width):
-        at = chunk * 2 * rows + odd * rows
-        x = y[pl.ds(pl.multiple_of(at, 8), rows), :] - piece[:, chunk * width : chunk * width + width]
-        part = part_dot(matrix, at, x)
+    rows, chunks = piece.shape[0], LANES // width
+    starts = [chunk * 2 * rows + odd * rows for chunk in range(chunks)]
+    own = [y[pl.ds(pl.multiple_of(at, 8), rows), :] for at in starts]
+    x = jnp.concatenate(own, axis=1) - piece[...]
+    if chunks == 1:
+        return part_dot(matrix, starts[0], [x], width)
+    total, depth = None, matrix.shape[1] // 2
+    columns, turned = spread(x, width), spread(turn(x, width), width)
+    for chunk, at in enumerate(starts):
+        at, span = pl.multiple_of(at, LANES), slice(rows * chunk, rows * chunk + rows)
+        part = dot(matrix[:, pl.ds(at, rows)], columns[span])
+        part += dot(matrix[:, pl.ds(depth + at, rows)], turned[span])
         total = part if total is None else total + part
     return total
 
@@ -455,7 +480,7 @@
 
 
 def mid_upper(matrix, y, piece, known, out):
-    out[...] = pack(known[...] + half_product(1, 2 * COLS, matrix, y, piece))
+    out[...] = pack(combined(known[...] + half_product(1, 2 * COLS, matrix, y, piece)))
 
 
 def mid_to_leaf(matrix, from_root, mine, other, keep, send, x_mid):
@@ -465,7 +490,7 @@
 
 
 def leaf_upper(matrix, y, piece, known, forward, adjoint):
-    fields_of(known[...] + half_product(1, LANES, matrix, y, piece), forward, adjoint, ())
+    fields_of(combined(known[...] + half_product(1, LANES, matrix, y, piece)), forward, adjoint, ())
 
 
 def mid_outputs(mine, other, forward, adjoint):
@@ -600,7 +625,7 @@
             swap("leaf", x_root, 2),
         )
         mine, theirs = sum_front(keep, send)
-        (known,) = kernel(functools.partial(own_half, 2 * COLS), [(n1, 2 * COLS)], mu, y_mid_full, mine)
+        (known,) = kernel(functools.partial(own_half, 2 * COLS), [(2 * n1, 4 * COLS)], mu, y_mid_full, mine)
         (x_mid,) = kernel(mid_upper, [(n1 // 2, LANES)], mu, y_mid_full, theirs, known)
         from_root, root_field, root_adjoint = kernel(
             root_to_leaf,
@@ -621,7 +646,7 @@
         x_other = swap("leaf", x_mid, 2)
         mid_field, mid_adjoint = kernel(mid_outputs, [(2, 2, COLS, n1)] * 2, x_mid, x_other)
         mine, theirs = sum_front(keep, send, x_other)
-        (known,) = kernel(functools.partial(own_half, LANES), [(n0, LANES)], lu, y_full, mine)
+        (known,) = kernel(functools.partial(own_half, LANES), [(2 * n0, 2 * LANES)], lu, y_full, mine)
         leaf_field, leaf_adjoint = kernel(
             leaf_upper, [(2, COLS, n0)] * 2, lu, y_full, theirs, after(known, mid_field)
         )

time: 117 us -> 115 us (0.983)
  Pallas kernels: 28.7 us -> 26.2 us
    pallas_call x46, Pallas kernels: 28.7 us -> 26.2 us  [kernel(): pl.pallas_call(fn, out_shape=[jax.ShapeDtypeStruct(*o) for o in outs], in...]
    ppermute x4, starting transfers between devices: 5.24 us -> 6.98 us  [sum_front(): lax.ppermute(total, 'front', pairs)]
  transfers between devices with their start and end apart: 53 -> 53, of which waited for: 34 -> 36; matrix products, arithmetic and copies ran while one was open for 0% -> 0% of each run, Pallas kernels for 18% -> 16%
where the time goes in v11:
time: 115 us
  starting transfers between devices  47.6 us (41%)
  waiting for transfers between devices  39.7 us (35%)
  Pallas kernels  26.2 us (23%)
    ppermute x49, starting transfers between devices, swap(): return lax.ppermute(x, axis, [(i, i ^ k) for i in range(size)])  40.7 us
    ppermute x49, waiting for transfers between devices, swap(): return lax.ppermute(x, axis, [(i, i ^ k) for i in range(size)])  28.3 us
    pallas_call x46, Pallas kernels, kernel(): pl.pallas_call(fn, out_shape=[jax.ShapeDtypeStruct(*o) for o in outs], in...  26.2 us
    ppermute x4, waiting for transfers between devices, sum_front(): lax.ppermute(total, 'front', pairs)  11.4 us
    ppermute x4, starting transfers between devices, sum_front(): lax.ppermute(total, 'front', pairs)  6.98 us
  transfers between devices with their start and end apart: 53, of which 36 were waited for; matrix products, arithmetic and copies ran while one was open for 0% of the time, Pallas kernels for 16%

profile of v11, /device:TPU:0, one launch (start us, length us, event | category | flops | bytes accessed | tf_op | source)
XLA Modules:
  0.0 114.7 jit_solution(10324501565174929411)
XLA Ops:
  1.7 3.1 %collective-permute-start = (f32[32,128]{1,0:T(8,128)S(1)}, f32[32,128]{1,0:T(8,128)S(1)}, u32[]{:S(2)}, u32[]{:S(2)}) collective-permute-start(f32[32,128]{1,0:T(8,128)S(1)} %get-tuple-element.64), channel_id=1, source_target_pairs={{0,8},{8,0},{16,24},{24,16},{1,9},{9,1},{17,25},{25,17},{2,10},{10... | collective-permute-start | bytes 49160 | tf_op jit(solution)/shard_map/right_hand_sides/ppermute | solution.py:120
  4.8 1.7 %collective-permute-done.came.near = f32[32,128]{1,0:T(8,128)S(1)} collective-permute-done((f32[32,128]{1,0:T(8,128)S(1)}, f32[32,128]{1,0:T(8,128)S(1)}, u32[]{:S(2)}, u32[]{:S(2)}) %collective-permute-start) | collective-permute-done | bytes 16416 | tf_op jit(solution)/shard_map/right_hand_sides/ppermute | solution.py:120
  6.5 3.0 %collective-permute-start.1 = (f32[32,128]{1,0:T(8,128)S(1)}, f32[32,128]{1,0:T(8,128)S(1)}, u32[]{:S(2)}, u32[]{:S(2)}) collective-permute-start(f32[32,128]{1,0:T(8,128)S(1)} %right_hand_sides.6), channel_id=1, source_target_pairs={{0,16},{8,24},{16,0},{24,8},{1,17},{9,25},{17,1},{25,9},{2,18},{10... | collective-permute-start | bytes 49160 | tf_op jit(solution)/shard_map/right_hand_sides/ppermute | solution.py:120
  11.3 1.9 %collective-permute-start.3 = (f32[72,128]{1,0:T(8,128)S(1)}, f32[72,128]{1,0:T(8,128)S(1)}, u32[]{:S(2)}, u32[]{:S(2)}) collective-permute-start(f32[72,128]{1,0:T(8,128)S(1)} %right_hand_sides.7.refs_0_), channel_id=1, source_target_pairs={{0,4},{1,5},{2,6},{3,7},{4,0},{5,1},{6,2},{7,3},{8,12},{9,13},{10,... | collective-permute-start | bytes 110600 | tf_op jit(solution)/shard_map/leaf_lower/ppermute | solution.py:120
  13.3 1.5 %collective-permute-start.2 = (f32[72,128]{1,0:T(8,128)S(1)}, f32[72,128]{1,0:T(8,128)S(1)}, u32[]{:S(2)}, u32[]{:S(2)}) collective-permute-start(f32[72,128]{1,0:T(8,128)S(1)} %right_hand_sides.7.refs_0_), channel_id=1, source_target_pairs={{0,2},{1,3},{2,0},{3,1},{4,6},{5,7},{6,4},{7,5},{8,10},{9,11},{10,... | collective-permute-start | bytes 110600 | tf_op jit(solution)/shard_map/leaf_lower/ppermute | solution.py:120
  15.4 1.9 %collective-permute-done.2.refs_0_.refs_4_ = f32[72,128]{1,0:T(8,128)S(1)} collective-permute-done((f32[72,128]{1,0:T(8,128)S(1)}, f32[72,128]{1,0:T(8,128)S(1)}, u32[]{:S(2)}, u32[]{:S(2)}) %collective-permute-start.2) | collective-permute-done | bytes 36896 | tf_op jit(solution)/shard_map/leaf_lower/ppermute | solution.py:120
  17.2 1.3 %leaf_lower.4 = (bf16[128,1024]{1,0:T(8,128)(2,1)S(1)}, bf16[256,1024]{1,0:T(8,128)(2,1)S(1)}) custom-call(f32[2,1,64,512]{3,2,1,0:T(8,128)} %refs_0_, f32[2,1,128,512]{3,2,1,0:T(8,128)} %refs_1_.4), custom_call_target="tpu_custom_call" | custom-call | flops 98304000 | bytes 140434 | tf_op jit(solution)/shard_map/leaf_lower/pallas_call | solution.py:155
  22.8 2.3 %collective-permute-start.12 = (f32[64,128]{1,0:T(8,128)S(1)}, f32[64,128]{1,0:T(8,128)S(1)}, u32[]{:S(2)}, u32[]{:S(2)}) collective-permute-start(f32[64,128]{1,0:T(8,128)S(1)} %leaf_lower.5.mine.refs_0_), channel_id=1, source_target_pairs={{0,6},{1,7},{2,4},{3,5},{4,2},{5,3},{6,0},{7,1},{8,14},{9,15},{10,... | collective-permute-start | bytes 98312 | tf_op jit(solution)/shard_map/mid_lower/ppermute | solution.py:120
  26.0 1.6 %mid_lower.11 = (bf16[512,1024]{1,0:T(8,128)(2,1)S(1)}, bf16[256,2048]{1,0:T(8,128)(2,1)S(1)}) custom-call(f32[2,1,256,512]{3,2,1,0:T(8,128)} %refs_0_.1, f32[2,2,128,1024]{3,2,1,0:T(8,128)} %refs_1_.5), custom_call_target="tpu_custom_call" | custom-call | flops 262144000 | bytes 374491 | tf_op jit(solution)/shard_map/mid_lower/pallas_call | solution.py:155
  29.5 1.6 %collective-permute-start.14 = (f32[64,128]{1,0:T(8,128)S(1)}, f32[64,128]{1,0:T(8,128)S(1)}, u32[]{:S(2)}, u32[]{:S(2)}) collective-permute-start(f32[64,128]{1,0:T(8,128)S(1)} %get-tuple-element.77), channel_id=1, source_target_pairs={{0,8},{8,0},{16,24},{24,16},{1,9},{9,1},{17,25},{25,17},{2,10},{10... | collective-permute-start | bytes 98312 | tf_op jit(solution)/shard_map/mid_lower/ppermute | solution.py:120
  33.5 1.7 %collective-permute-start.17 = (f32[64,128]{1,0:T(8,128)S(1)}, f32[64,128]{1,0:T(8,128)S(1)}, u32[]{:S(2)}, u32[]{:S(2)}) collective-permute-start(f32[64,128]{1,0:T(8,128)S(1)} %mid_lower.15.mine), channel_id=1, source_target_pairs={{0,4},{1,5},{2,6},{3,7},{4,0},{5,1},{6,2},{7,3},{8,12},{9,13},{10,... | collective-permute-start | bytes 98312 | tf_op jit(solution)/shard_map/mid_lower/ppermute | solution.py:120
  37.4 1.7 %collective-permute-done.16.refs_0_ = f32[64,128]{1,0:T(8,128)S(1)} collective-permute-done((f32[64,128]{1,0:T(8,128)S(1)}, f32[64,128]{1,0:T(8,128)S(1)}, u32[]{:S(2)}, u32[]{:S(2)}) %collective-permute-start.16) | collective-permute-done | bytes 32800 | tf_op jit(solution)/shard_map/mid_lower/ppermute | solution.py:120
  39.2 1.8 %mid_lower.18.matrix = bf16[512,2048]{1,0:T(8,128)(2,1)S(1)} custom-call(f32[2,2,256,1024]{3,2,1,0:T(8,128)} %refs_0_.2), custom_call_target="tpu_custom_call" | custom-call | flops 262144000 | bytes 374491 | tf_op jit(solution)/shard_map/mid_lower/pallas_call | solution.py:155
  44.3 2.1 %collective-permute-start.26 = (f32[64,128]{1,0:T(8,128)S(1)}, f32[64,128]{1,0:T(8,128)S(1)}, u32[]{:S(2)}, u32[]{:S(2)}) collective-permute-start(f32[64,128]{1,0:T(8,128)S(1)} %mid_lower.19.mine.refs_0_), channel_id=1, source_target_pairs={{0,6},{1,7},{2,4},{3,5},{4,2},{5,3},{6,0},{7,1},{8,14},{9,15},{10,... | collective-permute-start | bytes 98312 | tf_op jit(solution)/shard_map/root_cut/ppermute | solution.py:120
  51.0 2.7 %collective-permute-start.28 = (f32[64,128]{1,0:T(8,128)S(1)}, f32[64,128]{1,0:T(8,128)S(1)}, u32[]{:S(2)}, u32[]{:S(2)}) collective-permute-start(f32[64,128]{1,0:T(8,128)S(1)} %get-tuple-element.88), channel_id=1, source_target_pairs={{0,16},{8,24},{16,0},{24,8},{1,17},{9,25},{17,1},{25,9},{2,18},{10... | collective-permute-start | bytes 98312 | tf_op jit(solution)/shard_map/root_cut/ppermute | solution.py:120
  54.3 1.5 %collective-permute-done.28.refs_1_ = f32[64,128]{1,0:T(8,128)S(1)} collective-permute-done((f32[64,128]{1,0:T(8,128)S(1)}, f32[64,128]{1,0:T(8,128)S(1)}, u32[]{:S(2)}, u32[]{:S(2)}) %collective-permute-start.28) | collective-permute-done | bytes 32800 | tf_op jit(solution)/shard_map/root_cut/ppermute | solution.py:120
  55.9 1.6 %collective-permute-start.31 = (f32[64,128]{1,0:T(8,128)S(1)}, f32[64,128]{1,0:T(8,128)S(1)}, u32[]{:S(2)}, u32[]{:S(2)}) collective-permute-start(f32[64,128]{1,0:T(8,128)S(1)} %root_cut.13.mine), channel_id=1, source_target_pairs={{0,4},{1,5},{2,6},{3,7},{4,0},{5,1},{6,2},{7,3},{8,12},{9,13},{10,... | collective-permute-start | bytes 98312 | tf_op jit(solution)/shard_map/root_solve/ppermute | solution.py:120
  57.5 1.4 %collective-permute-start.30 = (f32[64,128]{1,0:T(8,128)S(1)}, f32[64,128]{1,0:T(8,128)S(1)}, u32[]{:S(2)}, u32[]{:S(2)}) collective-permute-start(f32[64,128]{1,0:T(8,128)S(1)} %root_cut.13.mine), channel_id=1, source_target_pairs={{0,2},{1,3},{2,0},{3,1},{4,6},{5,7},{6,4},{7,5},{8,10},{9,11},{10,... | collective-permute-start | bytes 98312 | tf_op jit(solution)/shard_map/root_solve/ppermute | solution.py:120
  59.8 1.6 %collective-permute-done.30.refs_0_ = f32[64,128]{1,0:T(8,128)S(1)} collective-permute-done((f32[64,128]{1,0:T(8,128)S(1)}, f32[64,128]{1,0:T(8,128)S(1)}, u32[]{:S(2)}, u32[]{:S(2)}) %collective-permute-start.30) | collective-permute-done | bytes 32800 | tf_op jit(solution)/shard_map/root_solve/ppermute | solution.py:120
  67.0 2.2 %collective-permute-start.39 = (f32[64,128]{1,0:T(8,128)S(1)}, f32[64,128]{1,0:T(8,128)S(1)}, u32[]{:S(2)}, u32[]{:S(2)}) collective-permute-start(f32[64,128]{1,0:T(8,128)S(1)} %root_solve.11.mine), channel_id=1, source_target_pairs={{0,6},{1,7},{2,4},{3,5},{4,2},{5,3},{6,0},{7,1},{8,14},{9,15},{10,... | collective-permute-start | bytes 98312 | tf_op jit(solution)/shard_map/root_solve/ppermute | solution.py:120
  69.9 1.5 %root_solve.13 = (bf16[2048,512]{1,0:T(8,128)(2,1)S(1)}, bf16[1024,256]{1,0:T(8,128)(2,1)S(1)}, bf16[128,1024]{1,0:T(8,128)(2,1)S(1)}) custom-call(f32[2,2,1024,256]{3,2,1,0:T(8,128)S(1)} %copy-done, f32[2,1,512,128]{3,2,1,0:T(8,128)S(1)} %copy-done.5, f32[2,1,64,512]{3,2,1,0:T(8,128)S(1)} %copy-done.6), custom_call_target="tpu_custom_call" | custom-call | flops 360448000 | bytes 514925 | tf_op jit(solution)/shard_map/root_solve/pallas_call | solution.py:155
  73.8 2.5 %collective-permute-start.41 = (f32[64,128]{1,0:T(8,128)S(1)}, f32[64,128]{1,0:T(8,128)S(1)}, u32[]{:S(2)}, u32[]{:S(2)}) collective-permute-start(f32[64,128]{1,0:T(8,128)S(1)} %root_solve.15.mine), channel_id=1, source_target_pairs={{0,16},{8,24},{16,0},{24,8},{1,17},{9,25},{17,1},{25,9},{2,18},{10... | collective-permute-start | bytes 98312 | tf_op jit(solution)/shard_map/mid_upper/ppermute | solution.py:120
  76.4 2.3 %collective-permute-done.41.other = f32[64,128]{1,0:T(8,128)S(1)} collective-permute-done((f32[64,128]{1,0:T(8,128)S(1)}, f32[64,128]{1,0:T(8,128)S(1)}, u32[]{:S(2)}, u32[]{:S(2)}) %collective-permute-start.41) | collective-permute-done | bytes 32800 | tf_op jit(solution)/shard_map/mid_upper/ppermute | solution.py:120
  79.9 1.3 %collective-permute-done.43.refs_1_ = f32[256,128]{1,0:T(8,128)S(1)} collective-permute-done((f32[256,128]{1,0:T(8,128)S(1)}, f32[256,128]{1,0:T(8,128)S(1)}, u32[]{:S(2)}, u32[]{:S(2)}) %collective-permute-start.43) | collective-permute-done | bytes 131104 | tf_op jit(solution)/shard_map/mid_upper/ppermute | solution.py:120
  82.5 3.8 %collective-permute-done.44.refs_1_ = f32[256,128]{1,0:T(8,128)S(1)} collective-permute-done((f32[256,128]{1,0:T(8,128)S(1)}, f32[256,128]{1,0:T(8,128)S(1)}, u32[]{:S(2)}, u32[]{:S(2)}) %collective-permute-start.44) | collective-permute-done | bytes 131104 | tf_op jit(solution)/shard_map/mid_upper/ppermute | solution.py:478
  86.3 2.8 %collective-permute-start.45 = (f32[256,128]{1,0:T(8,128)S(1)}, f32[256,128]{1,0:T(8,128)S(1)}, u32[]{:S(2)}, u32[]{:S(2)}) collective-permute-start(f32[256,128]{1,0:T(8,128)S(1)} %mid_upper.10.refs_0_), channel_id=1, source_target_pairs={{0,4},{1,3},{2,6},{3,1},{4,0},{5,7},{6,2},{7,5},{8,12},{9,11},{10,... | collective-permute-start | bytes 393224 | tf_op jit(solution)/shard_map/mid_upper/ppermute | solution.py:478
  89.1 2.9 %collective-permute-done.45.refs_1_ = f32[256,128]{1,0:T(8,128)S(1)} collective-permute-done((f32[256,128]{1,0:T(8,128)S(1)}, f32[256,128]{1,0:T(8,128)S(1)}, u32[]{:S(2)}, u32[]{:S(2)}) %collective-permute-start.45) | collective-permute-done | bytes 131104 | tf_op jit(solution)/shard_map/mid_upper/ppermute | solution.py:478
  98.9 1.3 %collective-permute-done.48.refs_1_ = f32[256,128]{1,0:T(8,128)S(1)} collective-permute-done((f32[256,128]{1,0:T(8,128)S(1)}, f32[256,128]{1,0:T(8,128)S(1)}, u32[]{:S(2)}, u32[]{:S(2)}) %collective-permute-start.48) | collective-permute-done | bytes 131104 | tf_op jit(solution)/shard_map/leaf_upper/ppermute | solution.py:120
  101.4 3.9 %collective-permute-done.49.refs_1_ = f32[256,128]{1,0:T(8,128)S(1)} collective-permute-done((f32[256,128]{1,0:T(8,128)S(1)}, f32[256,128]{1,0:T(8,128)S(1)}, u32[]{:S(2)}, u32[]{:S(2)}) %collective-permute-start.49) | collective-permute-done | bytes 131104 | tf_op jit(solution)/shard_map/leaf_upper/ppermute | solution.py:478
  105.3 1.9 %collective-permute-start.50 = (f32[256,128]{1,0:T(8,128)S(1)}, f32[256,128]{1,0:T(8,128)S(1)}, u32[]{:S(2)}, u32[]{:S(2)}) collective-permute-start(f32[256,128]{1,0:T(8,128)S(1)} %leaf_upper.9.refs_0_), channel_id=1, source_target_pairs={{0,4},{1,3},{2,6},{3,1},{4,0},{5,7},{6,2},{7,5},{8,12},{9,11},{10,... | collective-permute-start | bytes 393224 | tf_op jit(solution)/shard_map/leaf_upper/ppermute | solution.py:478
  107.2 2.5 %collective-permute-start.51 = (f32[128,128]{1,0:T(8,128)S(1)}, f32[128,128]{1,0:T(8,128)S(1)}, u32[]{:S(2)}, u32[]{:S(2)}) collective-permute-start(f32[128,128]{1,0:T(8,128)S(1)} %get-tuple-element.109.mine), channel_id=1, source_target_pairs={{0,16},{8,24},{16,0},{24,8},{1,17},{9,25},{17,1},{25,9},{2,18},{10... | collective-permute-start | bytes 196616 | tf_op jit(solution)/shard_map/leaf_upper/ppermute | solution.py:120
  110.4 2.0 %collective-permute-done.51.other = f32[128,128]{1,0:T(8,128)S(1)} collective-permute-done((f32[128,128]{1,0:T(8,128)S(1)}, f32[128,128]{1,0:T(8,128)S(1)}, u32[]{:S(2)}, u32[]{:S(2)}) %collective-permute-start.51) | collective-permute-done | bytes 65568 | tf_op jit(solution)/shard_map/leaf_upper/ppermute | solution.py:120
  (134 shorter events, 46.5 us)
Async XLA Ops:
  1.7 4.8 %collective-permute-start = (f32[32,128]{1,0:T(8,128)S(1)}, f32[32,128]{1,0:T(8,128)S(1)}, u32[]{:S(2)}, u32[]{:S(2)}) collective-permute-start(f32[32,128]{1,0:T(8,128)S(1)} %get-tuple-element.64), channel_id=1, source_target_pairs={{0,8},{8,0},{16,24},{24,16},{1,9},{9,1},{17,25},{25,17},{2,10},{10... | collective-permute-start | bytes 49160 | tf_op jit(solution)/shard_map/right_hand_sides/ppermute | solution.py:120
  6.5 4.7 %collective-permute-start.1 = (f32[32,128]{1,0:T(8,128)S(1)}, f32[32,128]{1,0:T(8,128)S(1)}, u32[]{:S(2)}, u32[]{:S(2)}) collective-permute-start(f32[32,128]{1,0:T(8,128)S(1)} %right_hand_sides.6), channel_id=1, source_target_pairs={{0,16},{8,24},{16,0},{24,8},{1,17},{9,25},{17,1},{25,9},{2,18},{10... | collective-permute-start | bytes 49160 | tf_op jit(solution)/shard_map/right_hand_sides/ppermute | solution.py:120
  11.3 4.0 %collective-permute-start.3 = (f32[72,128]{1,0:T(8,128)S(1)}, f32[72,128]{1,0:T(8,128)S(1)}, u32[]{:S(2)}, u32[]{:S(2)}) collective-permute-start(f32[72,128]{1,0:T(8,128)S(1)} %right_hand_sides.7.refs_0_), channel_id=1, source_target_pairs={{0,4},{1,5},{2,6},{3,7},{4,0},{5,1},{6,2},{7,3},{8,12},{9,13},{10,... | collective-permute-start | bytes 110600 | tf_op jit(solution)/shard_map/leaf_lower/ppermute | solution.py:120
  13.3 4.0 %collective-permute-start.2 = (f32[72,128]{1,0:T(8,128)S(1)}, f32[72,128]{1,0:T(8,128)S(1)}, u32[]{:S(2)}, u32[]{:S(2)}) collective-permute-start(f32[72,128]{1,0:T(8,128)S(1)} %right_hand_sides.7.refs_0_), channel_id=1, source_target_pairs={{0,2},{1,3},{2,0},{3,1},{4,6},{5,7},{6,4},{7,5},{8,10},{9,11},{10,... | collective-permute-start | bytes 110600 | tf_op jit(solution)/shard_map/leaf_lower/ppermute | solution.py:120
  14.7 4.9 %collective-permute-start.5 = (f32[72,128]{1,0:T(8,128)S(1)}, f32[72,128]{1,0:T(8,128)S(1)}, u32[]{:S(2)}, u32[]{:S(2)}) collective-permute-start(f32[72,128]{1,0:T(8,128)S(1)} %right_hand_sides.7.refs_0_), channel_id=1, source_target_pairs={{0,6},{1,7},{2,4},{3,5},{4,2},{5,3},{6,0},{7,1},{8,14},{9,15},{10,... | collective-permute-start | bytes 110600 | tf_op jit(solution)/shard_map/leaf_lower/ppermute | solution.py:120
  17.2 3.6 %collective-permute-start.7 = (f32[144,128]{1,0:T(8,128)S(1)}, f32[144,128]{1,0:T(8,128)S(1)}, u32[]{:S(2)}, u32[]{:S(2)}) collective-permute-start(f32[144,128]{1,0:T(8,128)S(1)} %leaf_lower.3), channel_id=1, source_target_pairs={{0,1},{1,0},{2,3},{3,2},{4,5},{5,4},{6,7},{7,6},{8,9},{9,8},{10,11... | collective-permute-start | bytes 221192 | tf_op jit(solution)/shard_map/leaf_lower/ppermute | solution.py:120
  21.5 4.0 %collective-permute-start.9 = (f32[64,128]{1,0:T(8,128)S(1)}, f32[64,128]{1,0:T(8,128)S(1)}, u32[]{:S(2)}, u32[]{:S(2)}) collective-permute-start(f32[64,128]{1,0:T(8,128)S(1)} %leaf_lower.5.mine.refs_0_), channel_id=1, source_target_pairs={{0,4},{1,5},{2,6},{3,7},{4,0},{5,1},{6,2},{7,3},{8,12},{9,13},{10,... | collective-permute-start | bytes 98312 | tf_op jit(solution)/shard_map/mid_lower/ppermute | solution.py:120
  22.1 3.9 %collective-permute-start.8 = (f32[64,128]{1,0:T(8,128)S(1)}, f32[64,128]{1,0:T(8,128)S(1)}, u32[]{:S(2)}, u32[]{:S(2)}) collective-permute-start(f32[64,128]{1,0:T(8,128)S(1)} %leaf_lower.5.mine.refs_0_), channel_id=1, source_target_pairs={{0,2},{1,3},{2,0},{3,1},{4,6},{5,7},{6,4},{7,5},{8,10},{9,11},{10,... | collective-permute-start | bytes 98312 | tf_op jit(solution)/shard_map/mid_lower/ppermute | solution.py:120
  22.8 4.9 %collective-permute-start.12 = (f32[64,128]{1,0:T(8,128)S(1)}, f32[64,128]{1,0:T(8,128)S(1)}, u32[]{:S(2)}, u32[]{:S(2)}) collective-permute-start(f32[64,128]{1,0:T(8,128)S(1)} %leaf_lower.5.mine.refs_0_), channel_id=1, source_target_pairs={{0,6},{1,7},{2,4},{3,5},{4,2},{5,3},{6,0},{7,1},{8,14},{9,15},{10,... | collective-permute-start | bytes 98312 | tf_op jit(solution)/shard_map/mid_lower/ppermute | solution.py:120
  29.5 4.0 %collective-permute-start.14 = (f32[64,128]{1,0:T(8,128)S(1)}, f32[64,128]{1,0:T(8,128)S(1)}, u32[]{:S(2)}, u32[]{:S(2)}) collective-permute-start(f32[64,128]{1,0:T(8,128)S(1)} %get-tuple-element.77), channel_id=1, source_target_pairs={{0,8},{8,0},{16,24},{24,16},{1,9},{9,1},{17,25},{25,17},{2,10},{10... | collective-permute-start | bytes 98312 | tf_op jit(solution)/shard_map/mid_lower/ppermute | solution.py:120
  31.8 9.2 %collective-permute-start.20 = (f32[128,128]{1,0:T(8,128)S(1)}, f32[128,128]{1,0:T(8,128)S(1)}, u32[]{:S(2)}, u32[]{:S(2)}) collective-permute-start(f32[128,128]{1,0:T(8,128)S(1)} %get-tuple-element.82), channel_id=1, source_target_pairs={{0,8},{8,0},{16,24},{24,16},{1,9},{9,1},{17,25},{25,17},{2,10},{10... | collective-permute-start | bytes 196616 | tf_op jit(solution)/shard_map/mid_lower/ppermute | solution.py:120
  33.5 3.9 %collective-permute-start.17 = (f32[64,128]{1,0:T(8,128)S(1)}, f32[64,128]{1,0:T(8,128)S(1)}, u32[]{:S(2)}, u32[]{:S(2)}) collective-permute-start(f32[64,128]{1,0:T(8,128)S(1)} %mid_lower.15.mine), channel_id=1, source_target_pairs={{0,4},{1,5},{2,6},{3,7},{4,0},{5,1},{6,2},{7,3},{8,12},{9,13},{10,... | collective-permute-start | bytes 98312 | tf_op jit(solution)/shard_map/mid_lower/ppermute | solution.py:120
  35.2 3.9 %collective-permute-start.16 = (f32[64,128]{1,0:T(8,128)S(1)}, f32[64,128]{1,0:T(8,128)S(1)}, u32[]{:S(2)}, u32[]{:S(2)}) collective-permute-start(f32[64,128]{1,0:T(8,128)S(1)} %mid_lower.15.mine), channel_id=1, source_target_pairs={{0,2},{1,3},{2,0},{3,1},{4,6},{5,7},{6,4},{7,5},{8,10},{9,11},{10,... | collective-permute-start | bytes 98312 | tf_op jit(solution)/shard_map/mid_lower/ppermute | solution.py:120
  36.1 4.9 %collective-permute-start.19 = (f32[64,128]{1,0:T(8,128)S(1)}, f32[64,128]{1,0:T(8,128)S(1)}, u32[]{:S(2)}, u32[]{:S(2)}) collective-permute-start(f32[64,128]{1,0:T(8,128)S(1)} %mid_lower.15.mine), channel_id=1, source_target_pairs={{0,6},{1,7},{2,4},{3,5},{4,2},{5,3},{6,0},{7,1},{8,14},{9,15},{10,... | collective-permute-start | bytes 98312 | tf_op jit(solution)/shard_map/mid_lower/ppermute | solution.py:120
  42.8 4.0 %collective-permute-start.23 = (f32[64,128]{1,0:T(8,128)S(1)}, f32[64,128]{1,0:T(8,128)S(1)}, u32[]{:S(2)}, u32[]{:S(2)}) collective-permute-start(f32[64,128]{1,0:T(8,128)S(1)} %mid_lower.19.mine.refs_0_), channel_id=1, source_target_pairs={{0,4},{1,5},{2,6},{3,7},{4,0},{5,1},{6,2},{7,3},{8,12},{9,13},{10,... | collective-permute-start | bytes 98312 | tf_op jit(solution)/shard_map/root_cut/ppermute | solution.py:120
  43.3 3.9 %collective-permute-start.22 = (f32[64,128]{1,0:T(8,128)S(1)}, f32[64,128]{1,0:T(8,128)S(1)}, u32[]{:S(2)}, u32[]{:S(2)}) collective-permute-start(f32[64,128]{1,0:T(8,128)S(1)} %mid_lower.19.mine.refs_0_), channel_id=1, source_target_pairs={{0,2},{1,3},{2,0},{3,1},{4,6},{5,7},{6,4},{7,5},{8,10},{9,11},{10,... | collective-permute-start | bytes 98312 | tf_op jit(solution)/shard_map/root_cut/ppermute | solution.py:120
  44.3 4.8 %collective-permute-start.26 = (f32[64,128]{1,0:T(8,128)S(1)}, f32[64,128]{1,0:T(8,128)S(1)}, u32[]{:S(2)}, u32[]{:S(2)}) collective-permute-start(f32[64,128]{1,0:T(8,128)S(1)} %mid_lower.19.mine.refs_0_), channel_id=1, source_target_pairs={{0,6},{1,7},{2,4},{3,5},{4,2},{5,3},{6,0},{7,1},{8,14},{9,15},{10,... | collective-permute-start | bytes 98312 | tf_op jit(solution)/shard_map/root_cut/ppermute | solution.py:120
  51.0 4.9 %collective-permute-start.28 = (f32[64,128]{1,0:T(8,128)S(1)}, f32[64,128]{1,0:T(8,128)S(1)}, u32[]{:S(2)}, u32[]{:S(2)}) collective-permute-start(f32[64,128]{1,0:T(8,128)S(1)} %get-tuple-element.88), channel_id=1, source_target_pairs={{0,16},{8,24},{16,0},{24,8},{1,17},{9,25},{17,1},{25,9},{2,18},{10... | collective-permute-start | bytes 98312 | tf_op jit(solution)/shard_map/root_cut/ppermute | solution.py:120
  55.9 3.9 %collective-permute-start.31 = (f32[64,128]{1,0:T(8,128)S(1)}, f32[64,128]{1,0:T(8,128)S(1)}, u32[]{:S(2)}, u32[]{:S(2)}) collective-permute-start(f32[64,128]{1,0:T(8,128)S(1)} %root_cut.13.mine), channel_id=1, source_target_pairs={{0,4},{1,5},{2,6},{3,7},{4,0},{5,1},{6,2},{7,3},{8,12},{9,13},{10,... | collective-permute-start | bytes 98312 | tf_op jit(solution)/shard_map/root_solve/ppermute | solution.py:120
  57.5 3.9 %collective-permute-start.30 = (f32[64,128]{1,0:T(8,128)S(1)}, f32[64,128]{1,0:T(8,128)S(1)}, u32[]{:S(2)}, u32[]{:S(2)}) collective-permute-start(f32[64,128]{1,0:T(8,128)S(1)} %root_cut.13.mine), channel_id=1, source_target_pairs={{0,2},{1,3},{2,0},{3,1},{4,6},{5,7},{6,4},{7,5},{8,10},{9,11},{10,... | collective-permute-start | bytes 98312 | tf_op jit(solution)/shard_map/root_solve/ppermute | solution.py:120
  58.9 4.8 %collective-permute-start.33 = (f32[64,128]{1,0:T(8,128)S(1)}, f32[64,128]{1,0:T(8,128)S(1)}, u32[]{:S(2)}, u32[]{:S(2)}) collective-permute-start(f32[64,128]{1,0:T(8,128)S(1)} %root_cut.13.mine), channel_id=1, source_target_pairs={{0,6},{1,7},{2,4},{3,5},{4,2},{5,3},{6,0},{7,1},{8,14},{9,15},{10,... | collective-permute-start | bytes 98312 | tf_op jit(solution)/shard_map/root_solve/ppermute | solution.py:120
  65.7 4.0 %collective-permute-start.36 = (f32[64,128]{1,0:T(8,128)S(1)}, f32[64,128]{1,0:T(8,128)S(1)}, u32[]{:S(2)}, u32[]{:S(2)}) collective-permute-start(f32[64,128]{1,0:T(8,128)S(1)} %root_solve.11.mine), channel_id=1, source_target_pairs={{0,4},{1,5},{2,6},{3,7},{4,0},{5,1},{6,2},{7,3},{8,12},{9,13},{10,... | collective-permute-start | bytes 98312 | tf_op jit(solution)/shard_map/root_solve/ppermute | solution.py:120
  65.9 3.9 %collective-permute-start.35 = (f32[64,128]{1,0:T(8,128)S(1)}, f32[64,128]{1,0:T(8,128)S(1)}, u32[]{:S(2)}, u32[]{:S(2)}) collective-permute-start(f32[64,128]{1,0:T(8,128)S(1)} %root_solve.11.mine), channel_id=1, source_target_pairs={{0,2},{1,3},{2,0},{3,1},{4,6},{5,7},{6,4},{7,5},{8,10},{9,11},{10,... | collective-permute-start | bytes 98312 | tf_op jit(solution)/shard_map/root_solve/ppermute | solution.py:120
  67.0 4.8 %collective-permute-start.39 = (f32[64,128]{1,0:T(8,128)S(1)}, f32[64,128]{1,0:T(8,128)S(1)}, u32[]{:S(2)}, u32[]{:S(2)}) collective-permute-start(f32[64,128]{1,0:T(8,128)S(1)} %root_solve.11.mine), channel_id=1, source_target_pairs={{0,6},{1,7},{2,4},{3,5},{4,2},{5,3},{6,0},{7,1},{8,14},{9,15},{10,... | collective-permute-start | bytes 98312 | tf_op jit(solution)/shard_map/root_solve/ppermute | solution.py:120
  73.8 4.9 %collective-permute-start.41 = (f32[64,128]{1,0:T(8,128)S(1)}, f32[64,128]{1,0:T(8,128)S(1)}, u32[]{:S(2)}, u32[]{:S(2)}) collective-permute-start(f32[64,128]{1,0:T(8,128)S(1)} %root_solve.15.mine), channel_id=1, source_target_pairs={{0,16},{8,24},{16,0},{24,8},{1,17},{9,25},{17,1},{25,9},{2,18},{10... | collective-permute-start | bytes 98312 | tf_op jit(solution)/shard_map/mid_upper/ppermute | solution.py:120
  81.3 5.0 %collective-permute-start.44 = (f32[256,128]{1,0:T(8,128)S(1)}, f32[256,128]{1,0:T(8,128)S(1)}, u32[]{:S(2)}, u32[]{:S(2)}) collective-permute-start(f32[256,128]{1,0:T(8,128)S(1)} %mid_upper.9.refs_0_), channel_id=1, source_target_pairs={{0,2},{1,5},{2,0},{3,7},{4,6},{5,1},{6,4},{7,3},{8,10},{9,13},{10,... | collective-permute-start | bytes 393224 | tf_op jit(solution)/shard_map/mid_upper/ppermute | solution.py:478
  86.3 5.7 %collective-permute-start.45 = (f32[256,128]{1,0:T(8,128)S(1)}, f32[256,128]{1,0:T(8,128)S(1)}, u32[]{:S(2)}, u32[]{:S(2)}) collective-permute-start(f32[256,128]{1,0:T(8,128)S(1)} %mid_upper.10.refs_0_), channel_id=1, source_target_pairs={{0,4},{1,3},{2,6},{3,1},{4,0},{5,7},{6,2},{7,5},{8,12},{9,11},{10,... | collective-permute-start | bytes 393224 | tf_op jit(solution)/shard_map/mid_upper/ppermute | solution.py:478
  92.1 4.5 %collective-permute-start.42 = (f32[128,128]{1,0:T(8,128)S(1)}, f32[128,128]{1,0:T(8,128)S(1)}, u32[]{:S(2)}, u32[]{:S(2)}) collective-permute-start(f32[128,128]{1,0:T(8,128)S(1)} %get-tuple-element.104.mine), channel_id=1, source_target_pairs={{0,8},{8,0},{16,24},{24,16},{1,9},{9,1},{17,25},{25,17},{2,10},{10... | collective-permute-start | bytes 196616 | tf_op jit(solution)/shard_map/mid_upper/ppermute | solution.py:120
  94.3 4.0 %collective-permute-start.47 = (f32[64,128]{1,0:T(8,128)S(1)}, f32[64,128]{1,0:T(8,128)S(1)}, u32[]{:S(2)}, u32[]{:S(2)}) collective-permute-start(f32[64,128]{1,0:T(8,128)S(1)} %mid_upper.13.mine), channel_id=1, source_target_pairs={{0,8},{8,0},{16,24},{24,16},{1,9},{9,1},{17,25},{25,17},{2,10},{10... | collective-permute-start | bytes 98312 | tf_op jit(solution)/shard_map/leaf_upper/ppermute | solution.py:120
  100.3 5.0 %collective-permute-start.49 = (f32[256,128]{1,0:T(8,128)S(1)}, f32[256,128]{1,0:T(8,128)S(1)}, u32[]{:S(2)}, u32[]{:S(2)}) collective-permute-start(f32[256,128]{1,0:T(8,128)S(1)} %leaf_upper.8.refs_0_), channel_id=1, source_target_pairs={{0,2},{1,5},{2,0},{3,7},{4,6},{5,1},{6,4},{7,3},{8,10},{9,13},{10,... | collective-permute-start | bytes 393224 | tf_op jit(solution)/shard_map/leaf_upper/ppermute | solution.py:478
  105.3 5.0 %collective-permute-start.50 = (f32[256,128]{1,0:T(8,128)S(1)}, f32[256,128]{1,0:T(8,128)S(1)}, u32[]{:S(2)}, u32[]{:S(2)}) collective-permute-start(f32[256,128]{1,0:T(8,128)S(1)} %leaf_upper.9.refs_0_), channel_id=1, source_target_pairs={{0,4},{1,3},{2,6},{3,1},{4,0},{5,7},{6,2},{7,5},{8,12},{9,11},{10,... | collective-permute-start | bytes 393224 | tf_op jit(solution)/shard_map/leaf_upper/ppermute | solution.py:478
  107.2 5.2 %collective-permute-start.51 = (f32[128,128]{1,0:T(8,128)S(1)}, f32[128,128]{1,0:T(8,128)S(1)}, u32[]{:S(2)}, u32[]{:S(2)}) collective-permute-start(f32[128,128]{1,0:T(8,128)S(1)} %get-tuple-element.109.mine), channel_id=1, source_target_pairs={{0,16},{8,24},{16,0},{24,8},{1,17},{9,25},{17,1},{25,9},{2,18},{10... | collective-permute-start | bytes 196616 | tf_op jit(solution)/shard_map/leaf_upper/ppermute | solution.py:120
  (28 other events, 96.1 us)

commit v12 on v11

--- a/solution.py
+++ b/solution.py
@@ -127,10 +127,17 @@
         at += ref.shape[0]
 
 
+def hop(fronts, step, odd):
+    return 2 << (step ^ odd) if fronts == 8 else 2 * step + 2
+
+
 def gather_front(x, meanwhile=None, others=()):
     fronts = lax.axis_size("front")
-    mine = [swap("front", x, k) for k in range(2, fronts, 2)]
-    near, last = mine[:-1], mine[-1]
+    last = swap("front", x, fronts - 2)
+    near = [
+        lax.ppermute(x, "front", [(i, i ^ hop(fronts, step, i & 1)) for i in range(fronts)])
+        for step in range(fronts // 2 - 2)
+    ]
     own = swap("front", x, 1)
     (both,) = kernel(stack, [(len(near) * x.shape[0], LANES)], *near)
     extra = tuple(meanwhile((both, own))) if meanwhile else ()
@@ -140,14 +147,14 @@
 
 def blocks_of(parts):
     rows, fronts = parts[0].shape[0], 2 * len(parts) - 6
-    evens = list(range(2, fronts, 2))
+    odd = lax.axis_index("front") & 1
     yield 0, parts[0]
     yield 1, parts[1]
-    for k, part in zip(evens[::-1], parts[2:-2]):
-        yield k, part
-    yield evens[-1] + 1, parts[-2]
-    for i, k in enumerate(evens[:-1]):
-        yield k + 1, parts[-1].at[rows * i : rows * i + rows, :]
+    yield fronts - 2, parts[2]
+    yield fronts - 1, parts[-2]
+    for step, part in enumerate(parts[-3:2:-1]):
+        yield hop(fronts, step, odd), part
+        yield hop(fronts, step, odd ^ 1) + 1, parts[-1].at[rows * step : rows * step + rows, :]
 
 
 def kernel(fn, outs, *args, scratch=(), vmem=8, work=0, hbm=(), pinned=()):
@@ -172,11 +179,14 @@
 
 def first_products(width, matrix, mine, other, *refs):
     near, both, out = refs[:-2], refs[-2], refs[-1]
-    rows = mine.shape[0]
+    rows, fronts = mine.shape[0], lax.axis_size("front")
+    odd = lax.axis_index("front") & 1
     total = chip_product(matrix, 0, mine[...], other[...], width)
-    for i, block in enumerate(near):
-        second = both[rows * i : rows * i + rows, :]
-        total += chip_product(matrix, 2 * i + 2, block[...], second, width)
+    for step, block in enumerate(near):
+        at = rows * (len(near) - 1 - step if fronts == 8 else step)
+        total += chip_product(
+            matrix, hop(fronts, step, odd), block[...], both[at : at + rows, :], width
+        )
     out[...] = total
 
 
@@ -445,22 +455,33 @@
     send[...] = jnp.where(first, high, low)
 
 
-def halved(value, keep, send):
-    rows = keep.shape[0]
-    odd = (lax.axis_index("front") & 1) == 1
-    low, high = value[:rows], value[rows:]
-    keep[...] = jnp.where(odd, high, low)
-    send[...] = jnp.where(odd, low, high)
-
-
-def root_to_mid(matrix, mine, other, keep, send, x_root):
+def column_half(matrix, x, theirs):
+    core = (lax.axis_index("front") & 1) ^ theirs
+    half, n = x.shape[1] // 2, x.shape[1]
+    turned = jnp.concatenate([-x[:, half:], x[:, :half]], axis=1)
+    columns = jnp.concatenate(split(jnp.concatenate([x, turned], axis=0)), axis=1)
+    height, chunks = matrix.shape[0] // 2, LANES // n
+    rows, pieces = height // chunks // 2, []
+    for chunk in range(chunks):
+        at = pl.multiple_of((2 * chunk + core) * rows, 16)
+        high = dot(matrix[pl.ds(at, rows), :], columns)
+        low = dot(matrix[pl.ds(height + at, rows), :], columns[:, :n])
+        pieces.append((high[:, n:] + low) + high[:, :n])
+    return jnp.concatenate(pieces, axis=1)
+
+
+def root_to_mid(matrix, mine, other, send, x_root):
     first = lax.axis_index("leaf") < 2
     mine, other = unpack(mine[...], COLS), unpack(other[...], COLS)
     low, high = jnp.where(first, mine, other), jnp.where(first, other, mine)
     width = COLS // 2
     x = jnp.concatenate([low[:, :width], high[:, :width], low[:, width:], high[:, width:]], axis=1)
     x_root[...] = pack(x)
-    halved(pack(complex_dot(matrix[...], x)), keep, send)
+    send[...] = column_half(matrix, x, 1)
+
+
+def root_to_mid_kept(matrix, x_root, keep):
+    keep[...] = column_half(matrix, unpack(x_root[...], 2 * COLS), 0)
 
 
 def root_to_leaf(matrix, mine, other, out, forward, adjoint):
@@ -483,10 +504,20 @@
     out[...] = pack(combined(known[...] + half_product(1, 2 * COLS, matrix, y, piece)))
 
 
-def mid_to_leaf(matrix, from_root, mine, other, keep, send, x_mid):
+def core_rows(ref, theirs):
+    rows = ref.shape[0] // 2
+    core = (lax.axis_index("front") & 1) ^ theirs
+    return ref[pl.ds(pl.multiple_of(core * rows, 8), rows), :]
+
+
+def mid_to_leaf(matrix, from_root, mine, other, send, x_mid):
     x = by_solve(lax.axis_index("leaf"), unpack(mine[...], 2 * COLS), unpack(other[...], 2 * COLS))
     x_mid[...] = x
-    halved(complex_dot(matrix[...], x) + from_root[...], keep, send)
+    send[...] = column_half(matrix, x, 1) + core_rows(from_root, 1)
+
+
+def mid_to_leaf_kept(matrix, from_root, x_mid, keep):
+    keep[...] = column_half(matrix, x_mid[...], 0) + core_rows(from_root, 0)
 
 
 def leaf_upper(matrix, y, piece, known, forward, adjoint):
@@ -617,13 +648,14 @@
         )
         (x_root,) = gathered(packed_to, COLS, [(n2 // 4, LANES)], ru, parts)
     with jax.named_scope("mid_upper"):
-        keep, send, x_root = kernel(
+        send, x_root = kernel(
             root_to_mid,
-            [(s1 // 4, LANES)] * 2 + [(n2 // 2, LANES)],
+            [(s1 // 4, LANES), (n2 // 2, LANES)],
             m2r_up,
             x_root,
             swap("leaf", x_root, 2),
         )
+        (keep,) = kernel(root_to_mid_kept, [(s1 // 4, LANES)], m2r_up, x_root)
         mine, theirs = sum_front(keep, send)
         (known,) = kernel(functools.partial(own_half, 2 * COLS), [(2 * n1, 4 * COLS)], mu, y_mid_full, mine)
         (x_mid,) = kernel(mid_upper, [(n1 // 2, LANES)], mu, y_mid_full, theirs, known)
@@ -635,14 +667,15 @@
             swap("leaf", after(x_root, send), 1),
         )
     with jax.named_scope("leaf_upper"):
-        keep, send, x_mid = kernel(
+        send, x_mid = kernel(
             mid_to_leaf,
-            [(s0 // 2, LANES)] * 2 + [(n1, LANES)],
+            [(s0 // 2, LANES), (n1, LANES)],
             l2m_up,
             from_root,
             x_mid,
             swap("leaf", x_mid, 1),
         )
+        (keep,) = kernel(mid_to_leaf_kept, [(s0 // 2, LANES)], l2m_up, from_root, x_mid)
         x_other = swap("leaf", x_mid, 2)
         mid_field, mid_adjoint = kernel(mid_outputs, [(2, 2, COLS, n1)] * 2, x_mid, x_other)
         mine, theirs = sum_front(keep, send, x_other)

time: 115 us -> 115 us (level)
  waiting for transfers between devices: 39.7 us -> 38.5 us
    ppermute x0 -> x12, starting transfers between devices: none -> 13 us  [gather_front(): lax.ppermute(x, 'front', [(i, i ^ hop(fronts, step, i & 1)) for i in rang...]
    ppermute x49 -> x37, starting transfers between devices: 40.7 us -> 27.7 us  [swap(): return lax.ppermute(x, axis, [(i, i ^ k) for i in range(size)])]
    ppermute x49 -> x37, waiting for transfers between devices: 28.3 us -> 18.4 us  [swap(): return lax.ppermute(x, axis, [(i, i ^ k) for i in range(size)])]
    ppermute x0 -> x12, waiting for transfers between devices: none -> 8.97 us  [gather_front(): lax.ppermute(x, 'front', [(i, i ^ hop(fronts, step, i & 1)) for i in rang...]
    pallas_call x46 -> x48, Pallas kernels: 26.2 us -> 26.8 us  [kernel(): pl.pallas_call(fn, out_shape=[jax.ShapeDtypeStruct(*o) for o in outs], in...]
  transfers between devices with their start and end apart: 53 -> 53, of which waited for: 36 -> 35; matrix products, arithmetic and copies ran while one was open for 0% -> 0% of each run, Pallas kernels for 16% -> 17%
where the time goes in v12:
time: 115 us; the launch traced here: 114 us
  starting transfers between devices  47.8 us (42%)
  waiting for transfers between devices  38.5 us (33%)
  Pallas kernels  26.8 us (23%)
    ppermute x37, starting transfers between devices, swap(): return lax.ppermute(x, axis, [(i, i ^ k) for i in range(size)])  27.7 us
    pallas_call x48, Pallas kernels, kernel(): pl.pallas_call(fn, out_shape=[jax.ShapeDtypeStruct(*o) for o in outs], in...  26.8 us
    ppermute x37, waiting for transfers between devices, swap(): return lax.ppermute(x, axis, [(i, i ^ k) for i in range(size)])  18.4 us
    ppermute x12, starting transfers between devices, gather_front(): lax.ppermute(x, 'front', [(i, i ^ hop(fronts, step, i & 1)) for i in rang...  13 us
    ppermute x4, waiting for transfers between devices, sum_front(): lax.ppermute(total, 'front', pairs)  11.1 us
    ppermute x12, waiting for transfers between devices, gather_front(): lax.ppermute(x, 'front', [(i, i ^ hop(fronts, step, i & 1)) for i in rang...  8.97 us
    ppermute x4, starting transfers between devices, sum_front(): lax.ppermute(total, 'front', pairs)  7.09 us
  transfers between devices with their start and end apart: 53, of which 35 were waited for; matrix products, arithmetic and copies ran while one was open for 0% of the time, Pallas kernels for 17%

profile of v12, /device:TPU:0, one launch (start us, length us, event | category | flops | bytes accessed | tf_op | source)
XLA Modules:
  0.0 114.3 jit_solution(2129323974484540260)
XLA Ops:
  1.7 3.1 %collective-permute-start = (f32[32,128]{1,0:T(8,128)S(1)}, f32[32,128]{1,0:T(8,128)S(1)}, u32[]{:S(2)}, u32[]{:S(2)}) collective-permute-start(f32[32,128]{1,0:T(8,128)S(1)} %get-tuple-element.62), channel_id=1, source_target_pairs={{0,8},{8,0},{16,24},{24,16},{1,9},{9,1},{17,25},{25,17},{2,10},{10... | collective-permute-start | bytes 49160 | tf_op jit(solution)/shard_map/right_hand_sides/ppermute | solution.py:120
  4.8 1.7 %collective-permute-done.came.near = f32[32,128]{1,0:T(8,128)S(1)} collective-permute-done((f32[32,128]{1,0:T(8,128)S(1)}, f32[32,128]{1,0:T(8,128)S(1)}, u32[]{:S(2)}, u32[]{:S(2)}) %collective-permute-start) | collective-permute-done | bytes 16416 | tf_op jit(solution)/shard_map/right_hand_sides/ppermute | solution.py:120
  6.5 3.0 %collective-permute-start.1 = (f32[32,128]{1,0:T(8,128)S(1)}, f32[32,128]{1,0:T(8,128)S(1)}, u32[]{:S(2)}, u32[]{:S(2)}) collective-permute-start(f32[32,128]{1,0:T(8,128)S(1)} %right_hand_sides.6), channel_id=1, source_target_pairs={{0,16},{8,24},{16,0},{24,8},{1,17},{9,25},{17,1},{25,9},{2,18},{10... | collective-permute-start | bytes 49160 | tf_op jit(solution)/shard_map/right_hand_sides/ppermute | solution.py:120
  11.3 1.9 %collective-permute-start.3 = (f32[72,128]{1,0:T(8,128)S(1)}, f32[72,128]{1,0:T(8,128)S(1)}, u32[]{:S(2)}, u32[]{:S(2)}) collective-permute-start(f32[72,128]{1,0:T(8,128)S(1)} %right_hand_sides.7.refs_0_), channel_id=1, source_target_pairs={{0,4},{1,3},{2,6},{3,1},{4,0},{5,7},{6,2},{7,5},{8,12},{9,11},{10,... | collective-permute-start | bytes 110600 | tf_op jit(solution)/shard_map/leaf_lower/ppermute | solution.py:138
  13.3 1.5 %collective-permute-start.2 = (f32[72,128]{1,0:T(8,128)S(1)}, f32[72,128]{1,0:T(8,128)S(1)}, u32[]{:S(2)}, u32[]{:S(2)}) collective-permute-start(f32[72,128]{1,0:T(8,128)S(1)} %right_hand_sides.7.refs_0_), channel_id=1, source_target_pairs={{0,2},{1,5},{2,0},{3,7},{4,6},{5,1},{6,4},{7,3},{8,10},{9,13},{10,... | collective-permute-start | bytes 110600 | tf_op jit(solution)/shard_map/leaf_lower/ppermute | solution.py:138
  15.4 1.9 %collective-permute-done.2.refs_0_.refs_4_ = f32[72,128]{1,0:T(8,128)S(1)} collective-permute-done((f32[72,128]{1,0:T(8,128)S(1)}, f32[72,128]{1,0:T(8,128)S(1)}, u32[]{:S(2)}, u32[]{:S(2)}) %collective-permute-start.2) | collective-permute-done | bytes 36896 | tf_op jit(solution)/shard_map/leaf_lower/ppermute | solution.py:138
  17.2 1.3 %leaf_lower.4 = (bf16[128,1024]{1,0:T(8,128)(2,1)S(1)}, bf16[256,1024]{1,0:T(8,128)(2,1)S(1)}) custom-call(f32[2,1,64,512]{3,2,1,0:T(8,128)} %refs_0_, f32[2,1,128,512]{3,2,1,0:T(8,128)} %refs_1_.4), custom_call_target="tpu_custom_call" | custom-call | flops 98304000 | bytes 140434 | tf_op jit(solution)/shard_map/leaf_lower/pallas_call | solution.py:162
  22.8 2.3 %collective-permute-start.12 = (f32[64,128]{1,0:T(8,128)S(1)}, f32[64,128]{1,0:T(8,128)S(1)}, u32[]{:S(2)}, u32[]{:S(2)}) collective-permute-start(f32[64,128]{1,0:T(8,128)S(1)} %leaf_lower.5.mine.refs_0_), channel_id=1, source_target_pairs={{0,6},{1,7},{2,4},{3,5},{4,2},{5,3},{6,0},{7,1},{8,14},{9,15},{10,... | collective-permute-start | bytes 98312 | tf_op jit(solution)/shard_map/mid_lower/ppermute | solution.py:120
  26.0 1.6 %mid_lower.11 = (bf16[512,1024]{1,0:T(8,128)(2,1)S(1)}, bf16[256,2048]{1,0:T(8,128)(2,1)S(1)}) custom-call(f32[2,1,256,512]{3,2,1,0:T(8,128)} %refs_0_.1, f32[2,2,128,1024]{3,2,1,0:T(8,128)} %refs_1_.5), custom_call_target="tpu_custom_call" | custom-call | flops 262144000 | bytes 374491 | tf_op jit(solution)/shard_map/mid_lower/pallas_call | solution.py:162
  29.5 1.6 %collective-permute-start.14 = (f32[64,128]{1,0:T(8,128)S(1)}, f32[64,128]{1,0:T(8,128)S(1)}, u32[]{:S(2)}, u32[]{:S(2)}) collective-permute-start(f32[64,128]{1,0:T(8,128)S(1)} %get-tuple-element.75), channel_id=1, source_target_pairs={{0,8},{8,0},{16,24},{24,16},{1,9},{9,1},{17,25},{25,17},{2,10},{10... | collective-permute-start | bytes 98312 | tf_op jit(solution)/shard_map/mid_lower/ppermute | solution.py:120
  33.5 1.7 %collective-permute-start.17 = (f32[64,128]{1,0:T(8,128)S(1)}, f32[64,128]{1,0:T(8,128)S(1)}, u32[]{:S(2)}, u32[]{:S(2)}) collective-permute-start(f32[64,128]{1,0:T(8,128)S(1)} %mid_lower.15.mine), channel_id=1, source_target_pairs={{0,4},{1,3},{2,6},{3,1},{4,0},{5,7},{6,2},{7,5},{8,12},{9,11},{10,... | collective-permute-start | bytes 98312 | tf_op jit(solution)/shard_map/mid_lower/ppermute | solution.py:138
  37.4 1.7 %collective-permute-done.16.refs_0_ = f32[64,128]{1,0:T(8,128)S(1)} collective-permute-done((f32[64,128]{1,0:T(8,128)S(1)}, f32[64,128]{1,0:T(8,128)S(1)}, u32[]{:S(2)}, u32[]{:S(2)}) %collective-permute-start.16) | collective-permute-done | bytes 32800 | tf_op jit(solution)/shard_map/mid_lower/ppermute | solution.py:138
  39.2 1.8 %mid_lower.18.matrix = bf16[512,2048]{1,0:T(8,128)(2,1)S(1)} custom-call(f32[2,2,256,1024]{3,2,1,0:T(8,128)} %refs_0_.2), custom_call_target="tpu_custom_call" | custom-call | flops 262144000 | bytes 374491 | tf_op jit(solution)/shard_map/mid_lower/pallas_call | solution.py:162
  44.3 2.1 %collective-permute-start.26 = (f32[64,128]{1,0:T(8,128)S(1)}, f32[64,128]{1,0:T(8,128)S(1)}, u32[]{:S(2)}, u32[]{:S(2)}) collective-permute-start(f32[64,128]{1,0:T(8,128)S(1)} %mid_lower.19.mine.refs_0_), channel_id=1, source_target_pairs={{0,6},{1,7},{2,4},{3,5},{4,2},{5,3},{6,0},{7,1},{8,14},{9,15},{10,... | collective-permute-start | bytes 98312 | tf_op jit(solution)/shard_map/root_cut/ppermute | solution.py:120
  47.3 1.3 %root_cut.8.matrix = bf16[512,4096]{1,0:T(8,128)(2,1)S(1)} custom-call(f32[2,256,2048]{2,1,0:T(8,128)S(1)} %copy-done.1), custom_call_target="tpu_custom_call" | custom-call | flops 524288000 | bytes 748982 | tf_op jit(solution)/shard_map/root_cut/pallas_call | solution.py:162
  51.0 2.7 %collective-permute-start.28 = (f32[64,128]{1,0:T(8,128)S(1)}, f32[64,128]{1,0:T(8,128)S(1)}, u32[]{:S(2)}, u32[]{:S(2)}) collective-permute-start(f32[64,128]{1,0:T(8,128)S(1)} %get-tuple-element.86), channel_id=1, source_target_pairs={{0,16},{8,24},{16,0},{24,8},{1,17},{9,25},{17,1},{25,9},{2,18},{10... | collective-permute-start | bytes 98312 | tf_op jit(solution)/shard_map/root_cut/ppermute | solution.py:120
  54.3 1.5 %collective-permute-done.28.refs_1_ = f32[64,128]{1,0:T(8,128)S(1)} collective-permute-done((f32[64,128]{1,0:T(8,128)S(1)}, f32[64,128]{1,0:T(8,128)S(1)}, u32[]{:S(2)}, u32[]{:S(2)}) %collective-permute-start.28) | collective-permute-done | bytes 32800 | tf_op jit(solution)/shard_map/root_cut/ppermute | solution.py:120
  55.9 1.6 %collective-permute-start.31 = (f32[64,128]{1,0:T(8,128)S(1)}, f32[64,128]{1,0:T(8,128)S(1)}, u32[]{:S(2)}, u32[]{:S(2)}) collective-permute-start(f32[64,128]{1,0:T(8,128)S(1)} %root_cut.13.mine), channel_id=1, source_target_pairs={{0,4},{1,3},{2,6},{3,1},{4,0},{5,7},{6,2},{7,5},{8,12},{9,11},{10,... | collective-permute-start | bytes 98312 | tf_op jit(solution)/shard_map/root_solve/ppermute | solution.py:138
  57.5 1.4 %collective-permute-start.30 = (f32[64,128]{1,0:T(8,128)S(1)}, f32[64,128]{1,0:T(8,128)S(1)}, u32[]{:S(2)}, u32[]{:S(2)}) collective-permute-start(f32[64,128]{1,0:T(8,128)S(1)} %root_cut.13.mine), channel_id=1, source_target_pairs={{0,2},{1,5},{2,0},{3,7},{4,6},{5,1},{6,4},{7,3},{8,10},{9,13},{10,... | collective-permute-start | bytes 98312 | tf_op jit(solution)/shard_map/root_solve/ppermute | solution.py:138
  59.8 1.6 %collective-permute-done.30.refs_0_ = f32[64,128]{1,0:T(8,128)S(1)} collective-permute-done((f32[64,128]{1,0:T(8,128)S(1)}, f32[64,128]{1,0:T(8,128)S(1)}, u32[]{:S(2)}, u32[]{:S(2)}) %collective-permute-start.30) | collective-permute-done | bytes 32800 | tf_op jit(solution)/shard_map/root_solve/ppermute | solution.py:138
  67.0 2.2 %collective-permute-start.39 = (f32[64,128]{1,0:T(8,128)S(1)}, f32[64,128]{1,0:T(8,128)S(1)}, u32[]{:S(2)}, u32[]{:S(2)}) collective-permute-start(f32[64,128]{1,0:T(8,128)S(1)} %root_solve.11.mine), channel_id=1, source_target_pairs={{0,6},{1,7},{2,4},{3,5},{4,2},{5,3},{6,0},{7,1},{8,14},{9,15},{10,... | collective-permute-start | bytes 98312 | tf_op jit(solution)/shard_map/root_solve/ppermute | solution.py:120
  70.1 1.5 %root_solve.13 = (bf16[2048,512]{1,0:T(8,128)(2,1)S(1)}, bf16[1024,256]{1,0:T(8,128)(2,1)S(1)}, bf16[128,1024]{1,0:T(8,128)(2,1)S(1)}) custom-call(f32[2,2,1024,256]{3,2,1,0:T(8,128)S(1)} %copy-done, f32[2,1,512,128]{3,2,1,0:T(8,128)S(1)} %copy-done.5, f32[2,1,64,512]{3,2,1,0:T(8,128)S(1)} %copy-done.6), custom_call_target="tpu_custom_call" | custom-call | flops 360448000 | bytes 514925 | tf_op jit(solution)/shard_map/root_solve/pallas_call | solution.py:162
  74.0 2.3 %collective-permute-start.41 = (f32[64,128]{1,0:T(8,128)S(1)}, f32[64,128]{1,0:T(8,128)S(1)}, u32[]{:S(2)}, u32[]{:S(2)}) collective-permute-start(f32[64,128]{1,0:T(8,128)S(1)} %root_solve.15.mine), channel_id=1, source_target_pairs={{0,16},{8,24},{16,0},{24,8},{1,17},{9,25},{17,1},{25,9},{2,18},{10... | collective-permute-start | bytes 98312 | tf_op jit(solution)/shard_map/mid_upper/ppermute | solution.py:120
  76.4 2.5 %collective-permute-done.41.other = f32[64,128]{1,0:T(8,128)S(1)} collective-permute-done((f32[64,128]{1,0:T(8,128)S(1)}, f32[64,128]{1,0:T(8,128)S(1)}, u32[]{:S(2)}, u32[]{:S(2)}) %collective-permute-start.41) | collective-permute-done | bytes 32800 | tf_op jit(solution)/shard_map/mid_upper/ppermute | solution.py:120
  81.2 1.5 %collective-permute-start.44 = (f32[256,128]{1,0:T(8,128)S(1)}, f32[256,128]{1,0:T(8,128)S(1)}, u32[]{:S(2)}, u32[]{:S(2)}) collective-permute-start(f32[256,128]{1,0:T(8,128)S(1)} %mid_upper.11.refs_0_), channel_id=1, source_target_pairs={{0,2},{1,5},{2,0},{3,7},{4,6},{5,1},{6,4},{7,3},{8,10},{9,13},{10,... | collective-permute-start | bytes 393224 | tf_op jit(solution)/shard_map/mid_upper/ppermute | solution.py:499
  82.7 3.5 %collective-permute-done.44.refs_1_ = f32[256,128]{1,0:T(8,128)S(1)} collective-permute-done((f32[256,128]{1,0:T(8,128)S(1)}, f32[256,128]{1,0:T(8,128)S(1)}, u32[]{:S(2)}, u32[]{:S(2)}) %collective-permute-start.44) | collective-permute-done | bytes 131104 | tf_op jit(solution)/shard_map/mid_upper/ppermute | solution.py:499
  86.2 2.6 %collective-permute-start.45 = (f32[256,128]{1,0:T(8,128)S(1)}, f32[256,128]{1,0:T(8,128)S(1)}, u32[]{:S(2)}, u32[]{:S(2)}) collective-permute-start(f32[256,128]{1,0:T(8,128)S(1)} %mid_upper.12.refs_0_), channel_id=1, source_target_pairs={{0,4},{1,3},{2,6},{3,1},{4,0},{5,7},{6,2},{7,5},{8,12},{9,11},{10,... | collective-permute-start | bytes 393224 | tf_op jit(solution)/shard_map/mid_upper/ppermute | solution.py:499
  88.8 2.9 %collective-permute-done.45.refs_1_ = f32[256,128]{1,0:T(8,128)S(1)} collective-permute-done((f32[256,128]{1,0:T(8,128)S(1)}, f32[256,128]{1,0:T(8,128)S(1)}, u32[]{:S(2)}, u32[]{:S(2)}) %collective-permute-start.45) | collective-permute-done | bytes 131104 | tf_op jit(solution)/shard_map/mid_upper/ppermute | solution.py:499
  101.1 3.9 %collective-permute-done.49.refs_1_ = f32[256,128]{1,0:T(8,128)S(1)} collective-permute-done((f32[256,128]{1,0:T(8,128)S(1)}, f32[256,128]{1,0:T(8,128)S(1)}, u32[]{:S(2)}, u32[]{:S(2)}) %collective-permute-start.49) | collective-permute-done | bytes 131104 | tf_op jit(solution)/shard_map/leaf_upper/ppermute | solution.py:499
  105.0 1.9 %collective-permute-start.50 = (f32[256,128]{1,0:T(8,128)S(1)}, f32[256,128]{1,0:T(8,128)S(1)}, u32[]{:S(2)}, u32[]{:S(2)}) collective-permute-start(f32[256,128]{1,0:T(8,128)S(1)} %leaf_upper.11.refs_0_), channel_id=1, source_target_pairs={{0,4},{1,3},{2,6},{3,1},{4,0},{5,7},{6,2},{7,5},{8,12},{9,11},{10,... | collective-permute-start | bytes 393224 | tf_op jit(solution)/shard_map/leaf_upper/ppermute | solution.py:499
  106.8 2.5 %collective-permute-start.51 = (f32[128,128]{1,0:T(8,128)S(1)}, f32[128,128]{1,0:T(8,128)S(1)}, u32[]{:S(2)}, u32[]{:S(2)}) collective-permute-start(f32[128,128]{1,0:T(8,128)S(1)} %get-tuple-element.104.x_mid.mine), channel_id=1, source_target_pairs={{0,16},{8,24},{16,0},{24,8},{1,17},{9,25},{17,1},{25,9},{2,18},{10... | collective-permute-start | bytes 196616 | tf_op jit(solution)/shard_map/leaf_upper/ppermute | solution.py:120
  110.0 2.0 %collective-permute-done.51.other = f32[128,128]{1,0:T(8,128)S(1)} collective-permute-done((f32[128,128]{1,0:T(8,128)S(1)}, f32[128,128]{1,0:T(8,128)S(1)}, u32[]{:S(2)}, u32[]{:S(2)}) %collective-permute-start.51) | collective-permute-done | bytes 65568 | tf_op jit(solution)/shard_map/leaf_upper/ppermute | solution.py:120
  (136 shorter events, 46.5 us)
Async XLA Ops:
  1.7 4.8 %collective-permute-start = (f32[32,128]{1,0:T(8,128)S(1)}, f32[32,128]{1,0:T(8,128)S(1)}, u32[]{:S(2)}, u32[]{:S(2)}) collective-permute-start(f32[32,128]{1,0:T(8,128)S(1)} %get-tuple-element.62), channel_id=1, source_target_pairs={{0,8},{8,0},{16,24},{24,16},{1,9},{9,1},{17,25},{25,17},{2,10},{10... | collective-permute-start | bytes 49160 | tf_op jit(solution)/shard_map/right_hand_sides/ppermute | solution.py:120
  6.5 4.7 %collective-permute-start.1 = (f32[32,128]{1,0:T(8,128)S(1)}, f32[32,128]{1,0:T(8,128)S(1)}, u32[]{:S(2)}, u32[]{:S(2)}) collective-permute-start(f32[32,128]{1,0:T(8,128)S(1)} %right_hand_sides.6), channel_id=1, source_target_pairs={{0,16},{8,24},{16,0},{24,8},{1,17},{9,25},{17,1},{25,9},{2,18},{10... | collective-permute-start | bytes 49160 | tf_op jit(solution)/shard_map/right_hand_sides/ppermute | solution.py:120
  11.3 4.0 %collective-permute-start.3 = (f32[72,128]{1,0:T(8,128)S(1)}, f32[72,128]{1,0:T(8,128)S(1)}, u32[]{:S(2)}, u32[]{:S(2)}) collective-permute-start(f32[72,128]{1,0:T(8,128)S(1)} %right_hand_sides.7.refs_0_), channel_id=1, source_target_pairs={{0,4},{1,3},{2,6},{3,1},{4,0},{5,7},{6,2},{7,5},{8,12},{9,11},{10,... | collective-permute-start | bytes 110600 | tf_op jit(solution)/shard_map/leaf_lower/ppermute | solution.py:138
  13.3 4.0 %collective-permute-start.2 = (f32[72,128]{1,0:T(8,128)S(1)}, f32[72,128]{1,0:T(8,128)S(1)}, u32[]{:S(2)}, u32[]{:S(2)}) collective-permute-start(f32[72,128]{1,0:T(8,128)S(1)} %right_hand_sides.7.refs_0_), channel_id=1, source_target_pairs={{0,2},{1,5},{2,0},{3,7},{4,6},{5,1},{6,4},{7,3},{8,10},{9,13},{10,... | collective-permute-start | bytes 110600 | tf_op jit(solution)/shard_map/leaf_lower/ppermute | solution.py:138
  14.7 4.9 %collective-permute-start.5 = (f32[72,128]{1,0:T(8,128)S(1)}, f32[72,128]{1,0:T(8,128)S(1)}, u32[]{:S(2)}, u32[]{:S(2)}) collective-permute-start(f32[72,128]{1,0:T(8,128)S(1)} %right_hand_sides.7.refs_0_), channel_id=1, source_target_pairs={{0,6},{1,7},{2,4},{3,5},{4,2},{5,3},{6,0},{7,1},{8,14},{9,15},{10,... | collective-permute-start | bytes 110600 | tf_op jit(solution)/shard_map/leaf_lower/ppermute | solution.py:120
  17.2 3.6 %collective-permute-start.7 = (f32[144,128]{1,0:T(8,128)S(1)}, f32[144,128]{1,0:T(8,128)S(1)}, u32[]{:S(2)}, u32[]{:S(2)}) collective-permute-start(f32[144,128]{1,0:T(8,128)S(1)} %leaf_lower.3), channel_id=1, source_target_pairs={{0,1},{1,0},{2,3},{3,2},{4,5},{5,4},{6,7},{7,6},{8,9},{9,8},{10,11... | collective-permute-start | bytes 221192 | tf_op jit(solution)/shard_map/leaf_lower/ppermute | solution.py:120
  21.5 4.3 %collective-permute-start.9 = (f32[64,128]{1,0:T(8,128)S(1)}, f32[64,128]{1,0:T(8,128)S(1)}, u32[]{:S(2)}, u32[]{:S(2)}) collective-permute-start(f32[64,128]{1,0:T(8,128)S(1)} %leaf_lower.5.mine.refs_0_), channel_id=1, source_target_pairs={{0,4},{1,3},{2,6},{3,1},{4,0},{5,7},{6,2},{7,5},{8,12},{9,11},{10,... | collective-permute-start | bytes 98312 | tf_op jit(solution)/shard_map/mid_lower/ppermute | solution.py:138
  22.1 3.9 %collective-permute-start.8 = (f32[64,128]{1,0:T(8,128)S(1)}, f32[64,128]{1,0:T(8,128)S(1)}, u32[]{:S(2)}, u32[]{:S(2)}) collective-permute-start(f32[64,128]{1,0:T(8,128)S(1)} %leaf_lower.5.mine.refs_0_), channel_id=1, source_target_pairs={{0,2},{1,5},{2,0},{3,7},{4,6},{5,1},{6,4},{7,3},{8,10},{9,13},{10,... | collective-permute-start | bytes 98312 | tf_op jit(solution)/shard_map/mid_lower/ppermute | solution.py:138
  22.8 4.9 %collective-permute-start.12 = (f32[64,128]{1,0:T(8,128)S(1)}, f32[64,128]{1,0:T(8,128)S(1)}, u32[]{:S(2)}, u32[]{:S(2)}) collective-permute-start(f32[64,128]{1,0:T(8,128)S(1)} %leaf_lower.5.mine.refs_0_), channel_id=1, source_target_pairs={{0,6},{1,7},{2,4},{3,5},{4,2},{5,3},{6,0},{7,1},{8,14},{9,15},{10,... | collective-permute-start | bytes 98312 | tf_op jit(solution)/shard_map/mid_lower/ppermute | solution.py:120
  29.5 4.0 %collective-permute-start.14 = (f32[64,128]{1,0:T(8,128)S(1)}, f32[64,128]{1,0:T(8,128)S(1)}, u32[]{:S(2)}, u32[]{:S(2)}) collective-permute-start(f32[64,128]{1,0:T(8,128)S(1)} %get-tuple-element.75), channel_id=1, source_target_pairs={{0,8},{8,0},{16,24},{24,16},{1,9},{9,1},{17,25},{25,17},{2,10},{10... | collective-permute-start | bytes 98312 | tf_op jit(solution)/shard_map/mid_lower/ppermute | solution.py:120
  31.8 9.2 %collective-permute-start.20 = (f32[128,128]{1,0:T(8,128)S(1)}, f32[128,128]{1,0:T(8,128)S(1)}, u32[]{:S(2)}, u32[]{:S(2)}) collective-permute-start(f32[128,128]{1,0:T(8,128)S(1)} %get-tuple-element.80), channel_id=1, source_target_pairs={{0,8},{8,0},{16,24},{24,16},{1,9},{9,1},{17,25},{25,17},{2,10},{10... | collective-permute-start | bytes 196616 | tf_op jit(solution)/shard_map/mid_lower/ppermute | solution.py:120
  33.5 3.9 %collective-permute-start.17 = (f32[64,128]{1,0:T(8,128)S(1)}, f32[64,128]{1,0:T(8,128)S(1)}, u32[]{:S(2)}, u32[]{:S(2)}) collective-permute-start(f32[64,128]{1,0:T(8,128)S(1)} %mid_lower.15.mine), channel_id=1, source_target_pairs={{0,4},{1,3},{2,6},{3,1},{4,0},{5,7},{6,2},{7,5},{8,12},{9,11},{10,... | collective-permute-start | bytes 98312 | tf_op jit(solution)/shard_map/mid_lower/ppermute | solution.py:138
  35.2 3.9 %collective-permute-start.16 = (f32[64,128]{1,0:T(8,128)S(1)}, f32[64,128]{1,0:T(8,128)S(1)}, u32[]{:S(2)}, u32[]{:S(2)}) collective-permute-start(f32[64,128]{1,0:T(8,128)S(1)} %mid_lower.15.mine), channel_id=1, source_target_pairs={{0,2},{1,5},{2,0},{3,7},{4,6},{5,1},{6,4},{7,3},{8,10},{9,13},{10,... | collective-permute-start | bytes 98312 | tf_op jit(solution)/shard_map/mid_lower/ppermute | solution.py:138
  36.1 4.9 %collective-permute-start.19 = (f32[64,128]{1,0:T(8,128)S(1)}, f32[64,128]{1,0:T(8,128)S(1)}, u32[]{:S(2)}, u32[]{:S(2)}) collective-permute-start(f32[64,128]{1,0:T(8,128)S(1)} %mid_lower.15.mine), channel_id=1, source_target_pairs={{0,6},{1,7},{2,4},{3,5},{4,2},{5,3},{6,0},{7,1},{8,14},{9,15},{10,... | collective-permute-start | bytes 98312 | tf_op jit(solution)/shard_map/mid_lower/ppermute | solution.py:120
  42.8 4.3 %collective-permute-start.23 = (f32[64,128]{1,0:T(8,128)S(1)}, f32[64,128]{1,0:T(8,128)S(1)}, u32[]{:S(2)}, u32[]{:S(2)}) collective-permute-start(f32[64,128]{1,0:T(8,128)S(1)} %mid_lower.19.mine.refs_0_), channel_id=1, source_target_pairs={{0,4},{1,3},{2,6},{3,1},{4,0},{5,7},{6,2},{7,5},{8,12},{9,11},{10,... | collective-permute-start | bytes 98312 | tf_op jit(solution)/shard_map/root_cut/ppermute | solution.py:138
  43.3 3.9 %collective-permute-start.22 = (f32[64,128]{1,0:T(8,128)S(1)}, f32[64,128]{1,0:T(8,128)S(1)}, u32[]{:S(2)}, u32[]{:S(2)}) collective-permute-start(f32[64,128]{1,0:T(8,128)S(1)} %mid_lower.19.mine.refs_0_), channel_id=1, source_target_pairs={{0,2},{1,5},{2,0},{3,7},{4,6},{5,1},{6,4},{7,3},{8,10},{9,13},{10,... | collective-permute-start | bytes 98312 | tf_op jit(solution)/shard_map/root_cut/ppermute | solution.py:138
  44.3 4.8 %collective-permute-start.26 = (f32[64,128]{1,0:T(8,128)S(1)}, f32[64,128]{1,0:T(8,128)S(1)}, u32[]{:S(2)}, u32[]{:S(2)}) collective-permute-start(f32[64,128]{1,0:T(8,128)S(1)} %mid_lower.19.mine.refs_0_), channel_id=1, source_target_pairs={{0,6},{1,7},{2,4},{3,5},{4,2},{5,3},{6,0},{7,1},{8,14},{9,15},{10,... | collective-permute-start | bytes 98312 | tf_op jit(solution)/shard_map/root_cut/ppermute | solution.py:120
  51.0 4.9 %collective-permute-start.28 = (f32[64,128]{1,0:T(8,128)S(1)}, f32[64,128]{1,0:T(8,128)S(1)}, u32[]{:S(2)}, u32[]{:S(2)}) collective-permute-start(f32[64,128]{1,0:T(8,128)S(1)} %get-tuple-element.86), channel_id=1, source_target_pairs={{0,16},{8,24},{16,0},{24,8},{1,17},{9,25},{17,1},{25,9},{2,18},{10... | collective-permute-start | bytes 98312 | tf_op jit(solution)/shard_map/root_cut/ppermute | solution.py:120
  55.9 3.9 %collective-permute-start.31 = (f32[64,128]{1,0:T(8,128)S(1)}, f32[64,128]{1,0:T(8,128)S(1)}, u32[]{:S(2)}, u32[]{:S(2)}) collective-permute-start(f32[64,128]{1,0:T(8,128)S(1)} %root_cut.13.mine), channel_id=1, source_target_pairs={{0,4},{1,3},{2,6},{3,1},{4,0},{5,7},{6,2},{7,5},{8,12},{9,11},{10,... | collective-permute-start | bytes 98312 | tf_op jit(solution)/shard_map/root_solve/ppermute | solution.py:138
  57.5 3.9 %collective-permute-start.30 = (f32[64,128]{1,0:T(8,128)S(1)}, f32[64,128]{1,0:T(8,128)S(1)}, u32[]{:S(2)}, u32[]{:S(2)}) collective-permute-start(f32[64,128]{1,0:T(8,128)S(1)} %root_cut.13.mine), channel_id=1, source_target_pairs={{0,2},{1,5},{2,0},{3,7},{4,6},{5,1},{6,4},{7,3},{8,10},{9,13},{10,... | collective-permute-start | bytes 98312 | tf_op jit(solution)/shard_map/root_solve/ppermute | solution.py:138
  58.9 4.8 %collective-permute-start.33 = (f32[64,128]{1,0:T(8,128)S(1)}, f32[64,128]{1,0:T(8,128)S(1)}, u32[]{:S(2)}, u32[]{:S(2)}) collective-permute-start(f32[64,128]{1,0:T(8,128)S(1)} %root_cut.13.mine), channel_id=1, source_target_pairs={{0,6},{1,7},{2,4},{3,5},{4,2},{5,3},{6,0},{7,1},{8,14},{9,15},{10,... | collective-permute-start | bytes 98312 | tf_op jit(solution)/shard_map/root_solve/ppermute | solution.py:120
  65.7 4.2 %collective-permute-start.36 = (f32[64,128]{1,0:T(8,128)S(1)}, f32[64,128]{1,0:T(8,128)S(1)}, u32[]{:S(2)}, u32[]{:S(2)}) collective-permute-start(f32[64,128]{1,0:T(8,128)S(1)} %root_solve.11.mine), channel_id=1, source_target_pairs={{0,4},{1,3},{2,6},{3,1},{4,0},{5,7},{6,2},{7,5},{8,12},{9,11},{10,... | collective-permute-start | bytes 98312 | tf_op jit(solution)/shard_map/root_solve/ppermute | solution.py:138
  65.9 4.0 %collective-permute-start.35 = (f32[64,128]{1,0:T(8,128)S(1)}, f32[64,128]{1,0:T(8,128)S(1)}, u32[]{:S(2)}, u32[]{:S(2)}) collective-permute-start(f32[64,128]{1,0:T(8,128)S(1)} %root_solve.11.mine), channel_id=1, source_target_pairs={{0,2},{1,5},{2,0},{3,7},{4,6},{5,1},{6,4},{7,3},{8,10},{9,13},{10,... | collective-permute-start | bytes 98312 | tf_op jit(solution)/shard_map/root_solve/ppermute | solution.py:138
  67.0 4.8 %collective-permute-start.39 = (f32[64,128]{1,0:T(8,128)S(1)}, f32[64,128]{1,0:T(8,128)S(1)}, u32[]{:S(2)}, u32[]{:S(2)}) collective-permute-start(f32[64,128]{1,0:T(8,128)S(1)} %root_solve.11.mine), channel_id=1, source_target_pairs={{0,6},{1,7},{2,4},{3,5},{4,2},{5,3},{6,0},{7,1},{8,14},{9,15},{10,... | collective-permute-start | bytes 98312 | tf_op jit(solution)/shard_map/root_solve/ppermute | solution.py:120
  74.0 4.9 %collective-permute-start.41 = (f32[64,128]{1,0:T(8,128)S(1)}, f32[64,128]{1,0:T(8,128)S(1)}, u32[]{:S(2)}, u32[]{:S(2)}) collective-permute-start(f32[64,128]{1,0:T(8,128)S(1)} %root_solve.15.mine), channel_id=1, source_target_pairs={{0,16},{8,24},{16,0},{24,8},{1,17},{9,25},{17,1},{25,9},{2,18},{10... | collective-permute-start | bytes 98312 | tf_op jit(solution)/shard_map/mid_upper/ppermute | solution.py:120
  81.2 5.0 %collective-permute-start.44 = (f32[256,128]{1,0:T(8,128)S(1)}, f32[256,128]{1,0:T(8,128)S(1)}, u32[]{:S(2)}, u32[]{:S(2)}) collective-permute-start(f32[256,128]{1,0:T(8,128)S(1)} %mid_upper.11.refs_0_), channel_id=1, source_target_pairs={{0,2},{1,5},{2,0},{3,7},{4,6},{5,1},{6,4},{7,3},{8,10},{9,13},{10,... | collective-permute-start | bytes 393224 | tf_op jit(solution)/shard_map/mid_upper/ppermute | solution.py:499
  86.2 5.5 %collective-permute-start.45 = (f32[256,128]{1,0:T(8,128)S(1)}, f32[256,128]{1,0:T(8,128)S(1)}, u32[]{:S(2)}, u32[]{:S(2)}) collective-permute-start(f32[256,128]{1,0:T(8,128)S(1)} %mid_upper.12.refs_0_), channel_id=1, source_target_pairs={{0,4},{1,3},{2,6},{3,1},{4,0},{5,7},{6,2},{7,5},{8,12},{9,11},{10,... | collective-permute-start | bytes 393224 | tf_op jit(solution)/shard_map/mid_upper/ppermute | solution.py:499
  91.9 4.5 %collective-permute-start.42 = (f32[128,128]{1,0:T(8,128)S(1)}, f32[128,128]{1,0:T(8,128)S(1)}, u32[]{:S(2)}, u32[]{:S(2)}) collective-permute-start(f32[128,128]{1,0:T(8,128)S(1)} %get-tuple-element.102.mine.x_root), channel_id=1, source_target_pairs={{0,8},{8,0},{16,24},{24,16},{1,9},{9,1},{17,25},{25,17},{2,10},{10... | collective-permute-start | bytes 196616 | tf_op jit(solution)/shard_map/mid_upper/ppermute | solution.py:120
  94.1 4.0 %collective-permute-start.47 = (f32[64,128]{1,0:T(8,128)S(1)}, f32[64,128]{1,0:T(8,128)S(1)}, u32[]{:S(2)}, u32[]{:S(2)}) collective-permute-start(f32[64,128]{1,0:T(8,128)S(1)} %mid_upper.15.mine), channel_id=1, source_target_pairs={{0,8},{8,0},{16,24},{24,16},{1,9},{9,1},{17,25},{25,17},{2,10},{10... | collective-permute-start | bytes 98312 | tf_op jit(solution)/shard_map/leaf_upper/ppermute | solution.py:120
  99.9 5.0 %collective-permute-start.49 = (f32[256,128]{1,0:T(8,128)S(1)}, f32[256,128]{1,0:T(8,128)S(1)}, u32[]{:S(2)}, u32[]{:S(2)}) collective-permute-start(f32[256,128]{1,0:T(8,128)S(1)} %leaf_upper.10.refs_0_), channel_id=1, source_target_pairs={{0,2},{1,5},{2,0},{3,7},{4,6},{5,1},{6,4},{7,3},{8,10},{9,13},{10,... | collective-permute-start | bytes 393224 | tf_op jit(solution)/shard_map/leaf_upper/ppermute | solution.py:499
  105.0 5.0 %collective-permute-start.50 = (f32[256,128]{1,0:T(8,128)S(1)}, f32[256,128]{1,0:T(8,128)S(1)}, u32[]{:S(2)}, u32[]{:S(2)}) collective-permute-start(f32[256,128]{1,0:T(8,128)S(1)} %leaf_upper.11.refs_0_), channel_id=1, source_target_pairs={{0,4},{1,3},{2,6},{3,1},{4,0},{5,7},{6,2},{7,5},{8,12},{9,11},{10,... | collective-permute-start | bytes 393224 | tf_op jit(solution)/shard_map/leaf_upper/ppermute | solution.py:499
  106.8 5.2 %collective-permute-start.51 = (f32[128,128]{1,0:T(8,128)S(1)}, f32[128,128]{1,0:T(8,128)S(1)}, u32[]{:S(2)}, u32[]{:S(2)}) collective-permute-start(f32[128,128]{1,0:T(8,128)S(1)} %get-tuple-element.104.x_mid.mine), channel_id=1, source_target_pairs={{0,16},{8,24},{16,0},{24,8},{1,17},{9,25},{17,1},{25,9},{2,18},{10... | collective-permute-start | bytes 196616 | tf_op jit(solution)/shard_map/leaf_upper/ppermute | solution.py:120
  (28 other events, 97.1 us)

commit v13 on v12

--- a/solution.py
+++ b/solution.py
@@ -470,34 +470,42 @@
     return jnp.concatenate(pieces, axis=1)
 
 
-def root_to_mid(matrix, mine, other, send, x_root):
+def root_to_mid(matrix, mine, other, send, top, low_rows):
     first = lax.axis_index("leaf") < 2
     mine, other = unpack(mine[...], COLS), unpack(other[...], COLS)
     low, high = jnp.where(first, mine, other), jnp.where(first, other, mine)
     width = COLS // 2
     x = jnp.concatenate([low[:, :width], high[:, :width], low[:, width:], high[:, width:]], axis=1)
-    x_root[...] = pack(x)
+    packed, rows = pack(x), top.shape[0]
+    top[...] = packed[:rows]
+    low_rows[...] = packed[rows:]
     send[...] = column_half(matrix, x, 1)
 
 
-def root_to_mid_kept(matrix, x_root, keep):
-    keep[...] = column_half(matrix, unpack(x_root[...], 2 * COLS), 0)
-
-
-def root_to_leaf(matrix, mine, other, out, forward, adjoint):
-    x = by_solve(lax.axis_index("leaf"), unpack(mine[...], 2 * COLS), unpack(other[...], 2 * COLS))
+def stacked(top, low):
+    return unpack(jnp.concatenate([top[...], low[...]], axis=0), 2 * COLS)
+
+
+def root_to_mid_kept(matrix, top, low, keep):
+    keep[...] = column_half(matrix, stacked(top, low), 0)
+
+
+def root_to_leaf(matrix, top, low, other_top, other_low, out, forward, adjoint):
+    x = by_solve(lax.axis_index("leaf"), stacked(top, low), stacked(other_top, other_low))
     out[...] = complex_dot(matrix[...], x)
     fields_of(x, forward, adjoint, ())
 
 
-def sum_front(kept, sent, *others):
+def sum_front(kept, sent, before_last=(), at_end=()):
     fronts = lax.axis_size("front")
     (total,) = kernel(add, [kept.shape], kept, swap("front", sent, 1))
     hops = [1 << i for i in range(1, fronts.bit_length() - 1)]
     for hop, back in zip(hops, hops[::-1]):
         pairs = [(i, i ^ (back if i & 1 else hop)) for i in range(fronts)]
+        if hop == hops[-1]:
+            total = after(total, *before_last)
         (total,) = kernel(add, [kept.shape], total, lax.ppermute(total, "front", pairs))
-    return [total, swap("front", after(total, *others), 1)]
+    return [total, swap("front", after(total, *at_end), 1)]
 
 
 def mid_upper(matrix, y, piece, known, out):
@@ -524,10 +532,11 @@
     fields_of(combined(known[...] + half_product(1, LANES, matrix, y, piece)), forward, adjoint, ())
 
 
-def mid_outputs(mine, other, forward, adjoint):
+def mid_outputs(mine, far, other, forward, adjoint):
     parent = lax.axis_index("leaf") // 2
+    x = by_solve(lax.axis_index("leaf"), unpack(far[...], 2 * COLS), unpack(other[...], 2 * COLS))
     fields_of(mine[...], forward, adjoint, (parent,))
-    fields_of(other[...], forward, adjoint, (1 - parent,))
+    fields_of(x, forward, adjoint, (1 - parent,))
 
 
 def after(x, *others):
@@ -648,25 +657,27 @@
         )
         (x_root,) = gathered(packed_to, COLS, [(n2 // 4, LANES)], ru, parts)
     with jax.named_scope("mid_upper"):
-        send, x_root = kernel(
+        send, *x_halves = kernel(
             root_to_mid,
-            [(s1 // 4, LANES), (n2 // 2, LANES)],
+            [(s1 // 4, LANES), (n2 // 4, LANES), (n2 // 4, LANES)],
             m2r_up,
             x_root,
             swap("leaf", x_root, 2),
         )
-        (keep,) = kernel(root_to_mid_kept, [(s1 // 4, LANES)], m2r_up, x_root)
-        mine, theirs = sum_front(keep, send)
+        (keep,) = kernel(root_to_mid_kept, [(s1 // 4, LANES)], m2r_up, *x_halves)
+        came = [swap("leaf", after(half, send), 1) for half in x_halves]
+        mine, theirs = sum_front(keep, send, (came[0],), (came[1],))
         (known,) = kernel(functools.partial(own_half, 2 * COLS), [(2 * n1, 4 * COLS)], mu, y_mid_full, mine)
         (x_mid,) = kernel(mid_upper, [(n1 // 2, LANES)], mu, y_mid_full, theirs, known)
         from_root, root_field, root_adjoint = kernel(
             root_to_leaf,
             [(s0, LANES), (2, COLS, n2), (2, COLS, n2)],
             l2r_up,
-            x_root,
-            swap("leaf", after(x_root, send), 1),
+            *x_halves,
+            *came,
         )
     with jax.named_scope("leaf_upper"):
+        x_far = swap("leaf", x_mid, 2)
         send, x_mid = kernel(
             mid_to_leaf,
             [(s0 // 2, LANES), (n1, LANES)],
@@ -676,9 +687,11 @@
             swap("leaf", x_mid, 1),
         )
         (keep,) = kernel(mid_to_leaf_kept, [(s0 // 2, LANES)], l2m_up, from_root, x_mid)
-        x_other = swap("leaf", x_mid, 2)
-        mid_field, mid_adjoint = kernel(mid_outputs, [(2, 2, COLS, n1)] * 2, x_mid, x_other)
-        mine, theirs = sum_front(keep, send, x_other)
+        x_other = swap("leaf", x_far, 1)
+        mid_field, mid_adjoint = kernel(
+            mid_outputs, [(2, 2, COLS, n1)] * 2, x_mid, x_far, x_other
+        )
+        mine, theirs = sum_front(keep, send, (x_far,), (x_other,))
         (known,) = kernel(functools.partial(own_half, LANES), [(2 * n0, 2 * LANES)], lu, y_full, mine)
         leaf_field, leaf_adjoint = kernel(
             leaf_upper, [(2, COLS, n0)] * 2, lu, y_full, theirs, after(known, mid_field)

time: 115 us -> 114 us (level)
  starting transfers between devices: 47.8 us -> 45.7 us
  waiting for transfers between devices: 38.5 us -> 40.3 us
    ppermute x37 -> x39, waiting for transfers between devices: 18.4 us -> 20.4 us  [swap(): return lax.ppermute(x, axis, [(i, i ^ k) for i in range(size)])]
    ppermute x4, starting transfers between devices: 7.09 us -> 5.49 us  [sum_front(): lax.ppermute(total, 'front', pairs)]
    ppermute x37 -> x39, starting transfers between devices: 27.7 us -> 27.1 us  [swap(): return lax.ppermute(x, axis, [(i, i ^ k) for i in range(size)])]
  transfers between devices with their start and end apart: 53 -> 55, of which waited for: 35 -> 38; matrix products, arithmetic and copies ran while one was open for 0% -> 0% of each run, Pallas kernels for 17% -> 17%
where the time goes in v13:
time: 114 us
  starting transfers between devices  45.7 us (40%)
  waiting for transfers between devices  40.3 us (35%)
  Pallas kernels  27 us (24%)
    ppermute x39, starting transfers between devices, swap(): return lax.ppermute(x, axis, [(i, i ^ k) for i in range(size)])  27.1 us
    pallas_call x48, Pallas kernels, kernel(): pl.pallas_call(fn, out_shape=[jax.ShapeDtypeStruct(*o) for o in outs], in...  27 us
    ppermute x39, waiting for transfers between devices, swap(): return lax.ppermute(x, axis, [(i, i ^ k) for i in range(size)])  20.4 us
    ppermute x12, starting transfers between devices, gather_front(): lax.ppermute(x, 'front', [(i, i ^ hop(fronts, step, i & 1)) for i in rang...  13 us
    ppermute x4, waiting for transfers between devices, sum_front(): lax.ppermute(total, 'front', pairs)  10.9 us
    ppermute x12, waiting for transfers between devices, gather_front(): lax.ppermute(x, 'front', [(i, i ^ hop(fronts, step, i & 1)) for i in rang...  8.97 us
    ppermute x4, starting transfers between devices, sum_front(): lax.ppermute(total, 'front', pairs)  5.49 us
  transfers between devices with their start and end apart: 55, of which 38 were waited for; matrix products, arithmetic and copies ran while one was open for 0% of the time, Pallas kernels for 17%

profile of v13, /device:TPU:0, one launch (start us, length us, event | category | flops | bytes accessed | tf_op | source)
XLA Modules:
  0.0 114.1 jit_solution(12558754361566079824)
XLA Ops:
  1.7 3.1 %collective-permute-start = (f32[32,128]{1,0:T(8,128)S(1)}, f32[32,128]{1,0:T(8,128)S(1)}, u32[]{:S(2)}, u32[]{:S(2)}) collective-permute-start(f32[32,128]{1,0:T(8,128)S(1)} %get-tuple-element.67), channel_id=1, source_target_pairs={{0,8},{8,0},{16,24},{24,16},{1,9},{9,1},{17,25},{25,17},{2,10},{10... | collective-permute-start | bytes 49160 | tf_op jit(solution)/shard_map/right_hand_sides/ppermute | solution.py:120
  4.8 1.7 %collective-permute-done.came.near = f32[32,128]{1,0:T(8,128)S(1)} collective-permute-done((f32[32,128]{1,0:T(8,128)S(1)}, f32[32,128]{1,0:T(8,128)S(1)}, u32[]{:S(2)}, u32[]{:S(2)}) %collective-permute-start) | collective-permute-done | bytes 16416 | tf_op jit(solution)/shard_map/right_hand_sides/ppermute | solution.py:120
  6.5 3.0 %collective-permute-start.1 = (f32[32,128]{1,0:T(8,128)S(1)}, f32[32,128]{1,0:T(8,128)S(1)}, u32[]{:S(2)}, u32[]{:S(2)}) collective-permute-start(f32[32,128]{1,0:T(8,128)S(1)} %right_hand_sides.6), channel_id=1, source_target_pairs={{0,16},{8,24},{16,0},{24,8},{1,17},{9,25},{17,1},{25,9},{2,18},{10... | collective-permute-start | bytes 49160 | tf_op jit(solution)/shard_map/right_hand_sides/ppermute | solution.py:120
  11.3 1.9 %collective-permute-start.3 = (f32[72,128]{1,0:T(8,128)S(1)}, f32[72,128]{1,0:T(8,128)S(1)}, u32[]{:S(2)}, u32[]{:S(2)}) collective-permute-start(f32[72,128]{1,0:T(8,128)S(1)} %right_hand_sides.7.refs_0_), channel_id=1, source_target_pairs={{0,4},{1,3},{2,6},{3,1},{4,0},{5,7},{6,2},{7,5},{8,12},{9,11},{10,... | collective-permute-start | bytes 110600 | tf_op jit(solution)/shard_map/leaf_lower/ppermute | solution.py:138
  13.3 1.5 %collective-permute-start.2 = (f32[72,128]{1,0:T(8,128)S(1)}, f32[72,128]{1,0:T(8,128)S(1)}, u32[]{:S(2)}, u32[]{:S(2)}) collective-permute-start(f32[72,128]{1,0:T(8,128)S(1)} %right_hand_sides.7.refs_0_), channel_id=1, source_target_pairs={{0,2},{1,5},{2,0},{3,7},{4,6},{5,1},{6,4},{7,3},{8,10},{9,13},{10,... | collective-permute-start | bytes 110600 | tf_op jit(solution)/shard_map/leaf_lower/ppermute | solution.py:138
  15.4 1.9 %collective-permute-done.2.refs_0_.refs_4_ = f32[72,128]{1,0:T(8,128)S(1)} collective-permute-done((f32[72,128]{1,0:T(8,128)S(1)}, f32[72,128]{1,0:T(8,128)S(1)}, u32[]{:S(2)}, u32[]{:S(2)}) %collective-permute-start.2) | collective-permute-done | bytes 36896 | tf_op jit(solution)/shard_map/leaf_lower/ppermute | solution.py:138
  17.2 1.3 %leaf_lower.4 = (bf16[128,1024]{1,0:T(8,128)(2,1)S(1)}, bf16[256,1024]{1,0:T(8,128)(2,1)S(1)}) custom-call(f32[2,1,64,512]{3,2,1,0:T(8,128)} %refs_0_, f32[2,1,128,512]{3,2,1,0:T(8,128)} %refs_1_.4), custom_call_target="tpu_custom_call" | custom-call | flops 98304000 | bytes 140434 | tf_op jit(solution)/shard_map/leaf_lower/pallas_call | solution.py:162
  22.8 2.3 %collective-permute-start.12 = (f32[64,128]{1,0:T(8,128)S(1)}, f32[64,128]{1,0:T(8,128)S(1)}, u32[]{:S(2)}, u32[]{:S(2)}) collective-permute-start(f32[64,128]{1,0:T(8,128)S(1)} %leaf_lower.5.mine.refs_0_), channel_id=1, source_target_pairs={{0,6},{1,7},{2,4},{3,5},{4,2},{5,3},{6,0},{7,1},{8,14},{9,15},{10,... | collective-permute-start | bytes 98312 | tf_op jit(solution)/shard_map/mid_lower/ppermute | solution.py:120
  26.0 1.6 %mid_lower.11 = (bf16[512,1024]{1,0:T(8,128)(2,1)S(1)}, bf16[256,2048]{1,0:T(8,128)(2,1)S(1)}) custom-call(f32[2,1,256,512]{3,2,1,0:T(8,128)} %refs_0_.1, f32[2,2,128,1024]{3,2,1,0:T(8,128)} %refs_1_.5), custom_call_target="tpu_custom_call" | custom-call | flops 262144000 | bytes 374491 | tf_op jit(solution)/shard_map/mid_lower/pallas_call | solution.py:162
  29.5 1.6 %collective-permute-start.14 = (f32[64,128]{1,0:T(8,128)S(1)}, f32[64,128]{1,0:T(8,128)S(1)}, u32[]{:S(2)}, u32[]{:S(2)}) collective-permute-start(f32[64,128]{1,0:T(8,128)S(1)} %get-tuple-element.80), channel_id=1, source_target_pairs={{0,8},{8,0},{16,24},{24,16},{1,9},{9,1},{17,25},{25,17},{2,10},{10... | collective-permute-start | bytes 98312 | tf_op jit(solution)/shard_map/mid_lower/ppermute | solution.py:120
  33.5 1.7 %collective-permute-start.17 = (f32[64,128]{1,0:T(8,128)S(1)}, f32[64,128]{1,0:T(8,128)S(1)}, u32[]{:S(2)}, u32[]{:S(2)}) collective-permute-start(f32[64,128]{1,0:T(8,128)S(1)} %mid_lower.15.mine), channel_id=1, source_target_pairs={{0,4},{1,3},{2,6},{3,1},{4,0},{5,7},{6,2},{7,5},{8,12},{9,11},{10,... | collective-permute-start | bytes 98312 | tf_op jit(solution)/shard_map/mid_lower/ppermute | solution.py:138
  37.4 1.7 %collective-permute-done.16.refs_0_ = f32[64,128]{1,0:T(8,128)S(1)} collective-permute-done((f32[64,128]{1,0:T(8,128)S(1)}, f32[64,128]{1,0:T(8,128)S(1)}, u32[]{:S(2)}, u32[]{:S(2)}) %collective-permute-start.16) | collective-permute-done | bytes 32800 | tf_op jit(solution)/shard_map/mid_lower/ppermute | solution.py:138
  39.2 1.8 %mid_lower.18.matrix = bf16[512,2048]{1,0:T(8,128)(2,1)S(1)} custom-call(f32[2,2,256,1024]{3,2,1,0:T(8,128)} %refs_0_.2), custom_call_target="tpu_custom_call" | custom-call | flops 262144000 | bytes 374491 | tf_op jit(solution)/shard_map/mid_lower/pallas_call | solution.py:162
  44.3 2.1 %collective-permute-start.26 = (f32[64,128]{1,0:T(8,128)S(1)}, f32[64,128]{1,0:T(8,128)S(1)}, u32[]{:S(2)}, u32[]{:S(2)}) collective-permute-start(f32[64,128]{1,0:T(8,128)S(1)} %mid_lower.19.mine.refs_0_), channel_id=1, source_target_pairs={{0,6},{1,7},{2,4},{3,5},{4,2},{5,3},{6,0},{7,1},{8,14},{9,15},{10,... | collective-permute-start | bytes 98312 | tf_op jit(solution)/shard_map/root_cut/ppermute | solution.py:120
  47.3 1.3 %root_cut.8.matrix = bf16[512,4096]{1,0:T(8,128)(2,1)S(1)} custom-call(f32[2,256,2048]{2,1,0:T(8,128)S(1)} %copy-done.1), custom_call_target="tpu_custom_call" | custom-call | flops 524288000 | bytes 748982 | tf_op jit(solution)/shard_map/root_cut/pallas_call | solution.py:162
  51.0 2.7 %collective-permute-start.28 = (f32[64,128]{1,0:T(8,128)S(1)}, f32[64,128]{1,0:T(8,128)S(1)}, u32[]{:S(2)}, u32[]{:S(2)}) collective-permute-start(f32[64,128]{1,0:T(8,128)S(1)} %get-tuple-element.91), channel_id=1, source_target_pairs={{0,16},{8,24},{16,0},{24,8},{1,17},{9,25},{17,1},{25,9},{2,18},{10... | collective-permute-start | bytes 98312 | tf_op jit(solution)/shard_map/root_cut/ppermute | solution.py:120
  54.3 1.5 %collective-permute-done.28.refs_1_ = f32[64,128]{1,0:T(8,128)S(1)} collective-permute-done((f32[64,128]{1,0:T(8,128)S(1)}, f32[64,128]{1,0:T(8,128)S(1)}, u32[]{:S(2)}, u32[]{:S(2)}) %collective-permute-start.28) | collective-permute-done | bytes 32800 | tf_op jit(solution)/shard_map/root_cut/ppermute | solution.py:120
  55.9 1.6 %collective-permute-start.31 = (f32[64,128]{1,0:T(8,128)S(1)}, f32[64,128]{1,0:T(8,128)S(1)}, u32[]{:S(2)}, u32[]{:S(2)}) collective-permute-start(f32[64,128]{1,0:T(8,128)S(1)} %root_cut.13.mine), channel_id=1, source_target_pairs={{0,4},{1,3},{2,6},{3,1},{4,0},{5,7},{6,2},{7,5},{8,12},{9,11},{10,... | collective-permute-start | bytes 98312 | tf_op jit(solution)/shard_map/root_solve/ppermute | solution.py:138
  57.5 1.4 %collective-permute-start.30 = (f32[64,128]{1,0:T(8,128)S(1)}, f32[64,128]{1,0:T(8,128)S(1)}, u32[]{:S(2)}, u32[]{:S(2)}) collective-permute-start(f32[64,128]{1,0:T(8,128)S(1)} %root_cut.13.mine), channel_id=1, source_target_pairs={{0,2},{1,5},{2,0},{3,7},{4,6},{5,1},{6,4},{7,3},{8,10},{9,13},{10,... | collective-permute-start | bytes 98312 | tf_op jit(solution)/shard_map/root_solve/ppermute | solution.py:138
  59.8 1.6 %collective-permute-done.30.refs_0_ = f32[64,128]{1,0:T(8,128)S(1)} collective-permute-done((f32[64,128]{1,0:T(8,128)S(1)}, f32[64,128]{1,0:T(8,128)S(1)}, u32[]{:S(2)}, u32[]{:S(2)}) %collective-permute-start.30) | collective-permute-done | bytes 32800 | tf_op jit(solution)/shard_map/root_solve/ppermute | solution.py:138
  67.0 2.2 %collective-permute-start.39 = (f32[64,128]{1,0:T(8,128)S(1)}, f32[64,128]{1,0:T(8,128)S(1)}, u32[]{:S(2)}, u32[]{:S(2)}) collective-permute-start(f32[64,128]{1,0:T(8,128)S(1)} %root_solve.11.mine), channel_id=1, source_target_pairs={{0,6},{1,7},{2,4},{3,5},{4,2},{5,3},{6,0},{7,1},{8,14},{9,15},{10,... | collective-permute-start | bytes 98312 | tf_op jit(solution)/shard_map/root_solve/ppermute | solution.py:120
  70.1 1.5 %root_solve.13 = (bf16[2048,512]{1,0:T(8,128)(2,1)S(1)}, bf16[1024,256]{1,0:T(8,128)(2,1)S(1)}, bf16[128,1024]{1,0:T(8,128)(2,1)S(1)}) custom-call(f32[2,2,1024,256]{3,2,1,0:T(8,128)S(1)} %copy-done, f32[2,1,512,128]{3,2,1,0:T(8,128)S(1)} %copy-done.5, f32[2,1,64,512]{3,2,1,0:T(8,128)S(1)} %copy-done.6), custom_call_target="tpu_custom_call" | custom-call | flops 360448000 | bytes 514925 | tf_op jit(solution)/shard_map/root_solve/pallas_call | solution.py:162
  74.0 2.3 %collective-permute-start.41 = (f32[64,128]{1,0:T(8,128)S(1)}, f32[64,128]{1,0:T(8,128)S(1)}, u32[]{:S(2)}, u32[]{:S(2)}) collective-permute-start(f32[64,128]{1,0:T(8,128)S(1)} %root_solve.15.mine), channel_id=1, source_target_pairs={{0,16},{8,24},{16,0},{24,8},{1,17},{9,25},{17,1},{25,9},{2,18},{10... | collective-permute-start | bytes 98312 | tf_op jit(solution)/shard_map/mid_upper/ppermute | solution.py:120
  76.4 2.5 %collective-permute-done.41.other = f32[64,128]{1,0:T(8,128)S(1)} collective-permute-done((f32[64,128]{1,0:T(8,128)S(1)}, f32[64,128]{1,0:T(8,128)S(1)}, u32[]{:S(2)}, u32[]{:S(2)}) %collective-permute-start.41) | collective-permute-done | bytes 32800 | tf_op jit(solution)/shard_map/mid_upper/ppermute | solution.py:120
  81.2 1.5 %collective-permute-start.45 = (f32[256,128]{1,0:T(8,128)S(1)}, f32[256,128]{1,0:T(8,128)S(1)}, u32[]{:S(2)}, u32[]{:S(2)}) collective-permute-start(f32[256,128]{1,0:T(8,128)S(1)} %mid_upper.11.refs_0_), channel_id=1, source_target_pairs={{0,2},{1,5},{2,0},{3,7},{4,6},{5,1},{6,4},{7,3},{8,10},{9,13},{10,... | collective-permute-start | bytes 393224 | tf_op jit(solution)/shard_map/mid_upper/ppermute | solution.py:507
  83.8 2.5 %collective-permute-done.45.refs_1_ = f32[256,128]{1,0:T(8,128)S(1)} collective-permute-done((f32[256,128]{1,0:T(8,128)S(1)}, f32[256,128]{1,0:T(8,128)S(1)}, u32[]{:S(2)}, u32[]{:S(2)}) %collective-permute-start.45) | collective-permute-done | bytes 131104 | tf_op jit(solution)/shard_map/mid_upper/ppermute | solution.py:507
  86.9 1.9 %collective-permute-start.46 = (f32[256,128]{1,0:T(8,128)S(1)}, f32[256,128]{1,0:T(8,128)S(1)}, u32[]{:S(2)}, u32[]{:S(2)}) collective-permute-start(f32[256,128]{1,0:T(8,128)S(1)} %mid_upper.12.refs_0_), channel_id=1, source_target_pairs={{0,4},{1,3},{2,6},{3,1},{4,0},{5,7},{6,2},{7,5},{8,12},{9,11},{10,... | collective-permute-start | bytes 393224 | tf_op jit(solution)/shard_map/mid_upper/ppermute | solution.py:507
  89.3 2.6 %collective-permute-done.46.refs_1_ = f32[256,128]{1,0:T(8,128)S(1)} collective-permute-done((f32[256,128]{1,0:T(8,128)S(1)}, f32[256,128]{1,0:T(8,128)S(1)}, u32[]{:S(2)}, u32[]{:S(2)}) %collective-permute-start.46) | collective-permute-done | bytes 131104 | tf_op jit(solution)/shard_map/mid_upper/ppermute | solution.py:507
  96.5 2.2 %collective-permute-done.48.other = f32[64,128]{1,0:T(8,128)S(1)} collective-permute-done((f32[64,128]{1,0:T(8,128)S(1)}, f32[64,128]{1,0:T(8,128)S(1)}, u32[]{:S(2)}, u32[]{:S(2)}) %collective-permute-start.48) | collective-permute-done | bytes 32800 | tf_op jit(solution)/shard_map/leaf_upper/ppermute | solution.py:120
  101.6 1.5 %collective-permute-start.51 = (f32[64,128]{1,0:T(8,128)S(1)}, f32[64,128]{1,0:T(8,128)S(1)}, u32[]{:S(2)}, u32[]{:S(2)}) collective-permute-start(f32[64,128]{1,0:T(8,128)S(1)} %mid_upper.15.mine), channel_id=1, source_target_pairs={{0,16},{8,24},{16,0},{24,8},{1,17},{9,25},{17,1},{25,9},{2,18},{10... | collective-permute-start | bytes 98312 | tf_op jit(solution)/shard_map/leaf_upper/ppermute | solution.py:120
  103.1 2.6 %collective-permute-done.50.refs_1_ = f32[256,128]{1,0:T(8,128)S(1)} collective-permute-done((f32[256,128]{1,0:T(8,128)S(1)}, f32[256,128]{1,0:T(8,128)S(1)}, u32[]{:S(2)}, u32[]{:S(2)}) %collective-permute-start.50) | collective-permute-done | bytes 131104 | tf_op jit(solution)/shard_map/leaf_upper/ppermute | solution.py:507
  108.4 3.3 %collective-permute-done.52.refs_1_ = f32[256,128]{1,0:T(8,128)S(1)} collective-permute-done((f32[256,128]{1,0:T(8,128)S(1)}, f32[256,128]{1,0:T(8,128)S(1)}, u32[]{:S(2)}, u32[]{:S(2)}) %collective-permute-start.52) | collective-permute-done | bytes 131104 | tf_op jit(solution)/shard_map/leaf_upper/ppermute | solution.py:507
  (140 shorter events, 49.0 us)
Async XLA Ops:
  1.7 4.8 %collective-permute-start = (f32[32,128]{1,0:T(8,128)S(1)}, f32[32,128]{1,0:T(8,128)S(1)}, u32[]{:S(2)}, u32[]{:S(2)}) collective-permute-start(f32[32,128]{1,0:T(8,128)S(1)} %get-tuple-element.67), channel_id=1, source_target_pairs={{0,8},{8,0},{16,24},{24,16},{1,9},{9,1},{17,25},{25,17},{2,10},{10... | collective-permute-start | bytes 49160 | tf_op jit(solution)/shard_map/right_hand_sides/ppermute | solution.py:120
  6.5 4.7 %collective-permute-start.1 = (f32[32,128]{1,0:T(8,128)S(1)}, f32[32,128]{1,0:T(8,128)S(1)}, u32[]{:S(2)}, u32[]{:S(2)}) collective-permute-start(f32[32,128]{1,0:T(8,128)S(1)} %right_hand_sides.6), channel_id=1, source_target_pairs={{0,16},{8,24},{16,0},{24,8},{1,17},{9,25},{17,1},{25,9},{2,18},{10... | collective-permute-start | bytes 49160 | tf_op jit(solution)/shard_map/right_hand_sides/ppermute | solution.py:120
  11.3 4.0 %collective-permute-start.3 = (f32[72,128]{1,0:T(8,128)S(1)}, f32[72,128]{1,0:T(8,128)S(1)}, u32[]{:S(2)}, u32[]{:S(2)}) collective-permute-start(f32[72,128]{1,0:T(8,128)S(1)} %right_hand_sides.7.refs_0_), channel_id=1, source_target_pairs={{0,4},{1,3},{2,6},{3,1},{4,0},{5,7},{6,2},{7,5},{8,12},{9,11},{10,... | collective-permute-start | bytes 110600 | tf_op jit(solution)/shard_map/leaf_lower/ppermute | solution.py:138
  13.3 4.0 %collective-permute-start.2 = (f32[72,128]{1,0:T(8,128)S(1)}, f32[72,128]{1,0:T(8,128)S(1)}, u32[]{:S(2)}, u32[]{:S(2)}) collective-permute-start(f32[72,128]{1,0:T(8,128)S(1)} %right_hand_sides.7.refs_0_), channel_id=1, source_target_pairs={{0,2},{1,5},{2,0},{3,7},{4,6},{5,1},{6,4},{7,3},{8,10},{9,13},{10,... | collective-permute-start | bytes 110600 | tf_op jit(solution)/shard_map/leaf_lower/ppermute | solution.py:138
  14.7 4.9 %collective-permute-start.5 = (f32[72,128]{1,0:T(8,128)S(1)}, f32[72,128]{1,0:T(8,128)S(1)}, u32[]{:S(2)}, u32[]{:S(2)}) collective-permute-start(f32[72,128]{1,0:T(8,128)S(1)} %right_hand_sides.7.refs_0_), channel_id=1, source_target_pairs={{0,6},{1,7},{2,4},{3,5},{4,2},{5,3},{6,0},{7,1},{8,14},{9,15},{10,... | collective-permute-start | bytes 110600 | tf_op jit(solution)/shard_map/leaf_lower/ppermute | solution.py:120
  21.5 4.3 %collective-permute-start.9 = (f32[64,128]{1,0:T(8,128)S(1)}, f32[64,128]{1,0:T(8,128)S(1)}, u32[]{:S(2)}, u32[]{:S(2)}) collective-permute-start(f32[64,128]{1,0:T(8,128)S(1)} %leaf_lower.5.mine.refs_0_), channel_id=1, source_target_pairs={{0,4},{1,3},{2,6},{3,1},{4,0},{5,7},{6,2},{7,5},{8,12},{9,11},{10,... | collective-permute-start | bytes 98312 | tf_op jit(solution)/shard_map/mid_lower/ppermute | solution.py:138
  22.1 3.9 %collective-permute-start.8 = (f32[64,128]{1,0:T(8,128)S(1)}, f32[64,128]{1,0:T(8,128)S(1)}, u32[]{:S(2)}, u32[]{:S(2)}) collective-permute-start(f32[64,128]{1,0:T(8,128)S(1)} %leaf_lower.5.mine.refs_0_), channel_id=1, source_target_pairs={{0,2},{1,5},{2,0},{3,7},{4,6},{5,1},{6,4},{7,3},{8,10},{9,13},{10,... | collective-permute-start | bytes 98312 | tf_op jit(solution)/shard_map/mid_lower/ppermute | solution.py:138
  22.8 4.9 %collective-permute-start.12 = (f32[64,128]{1,0:T(8,128)S(1)}, f32[64,128]{1,0:T(8,128)S(1)}, u32[]{:S(2)}, u32[]{:S(2)}) collective-permute-start(f32[64,128]{1,0:T(8,128)S(1)} %leaf_lower.5.mine.refs_0_), channel_id=1, source_target_pairs={{0,6},{1,7},{2,4},{3,5},{4,2},{5,3},{6,0},{7,1},{8,14},{9,15},{10,... | collective-permute-start | bytes 98312 | tf_op jit(solution)/shard_map/mid_lower/ppermute | solution.py:120
  29.5 4.0 %collective-permute-start.14 = (f32[64,128]{1,0:T(8,128)S(1)}, f32[64,128]{1,0:T(8,128)S(1)}, u32[]{:S(2)}, u32[]{:S(2)}) collective-permute-start(f32[64,128]{1,0:T(8,128)S(1)} %get-tuple-element.80), channel_id=1, source_target_pairs={{0,8},{8,0},{16,24},{24,16},{1,9},{9,1},{17,25},{25,17},{2,10},{10... | collective-permute-start | bytes 98312 | tf_op jit(solution)/shard_map/mid_lower/ppermute | solution.py:120
  31.8 9.2 %collective-permute-start.20 = (f32[128,128]{1,0:T(8,128)S(1)}, f32[128,128]{1,0:T(8,128)S(1)}, u32[]{:S(2)}, u32[]{:S(2)}) collective-permute-start(f32[128,128]{1,0:T(8,128)S(1)} %get-tuple-element.85), channel_id=1, source_target_pairs={{0,8},{8,0},{16,24},{24,16},{1,9},{9,1},{17,25},{25,17},{2,10},{10... | collective-permute-start | bytes 196616 | tf_op jit(solution)/shard_map/mid_lower/ppermute | solution.py:120
  33.5 3.9 %collective-permute-start.17 = (f32[64,128]{1,0:T(8,128)S(1)}, f32[64,128]{1,0:T(8,128)S(1)}, u32[]{:S(2)}, u32[]{:S(2)}) collective-permute-start(f32[64,128]{1,0:T(8,128)S(1)} %mid_lower.15.mine), channel_id=1, source_target_pairs={{0,4},{1,3},{2,6},{3,1},{4,0},{5,7},{6,2},{7,5},{8,12},{9,11},{10,... | collective-permute-start | bytes 98312 | tf_op jit(solution)/shard_map/mid_lower/ppermute | solution.py:138
  35.2 3.9 %collective-permute-start.16 = (f32[64,128]{1,0:T(8,128)S(1)}, f32[64,128]{1,0:T(8,128)S(1)}, u32[]{:S(2)}, u32[]{:S(2)}) collective-permute-start(f32[64,128]{1,0:T(8,128)S(1)} %mid_lower.15.mine), channel_id=1, source_target_pairs={{0,2},{1,5},{2,0},{3,7},{4,6},{5,1},{6,4},{7,3},{8,10},{9,13},{10,... | collective-permute-start | bytes 98312 | tf_op jit(solution)/shard_map/mid_lower/ppermute | solution.py:138
  36.1 4.9 %collective-permute-start.19 = (f32[64,128]{1,0:T(8,128)S(1)}, f32[64,128]{1,0:T(8,128)S(1)}, u32[]{:S(2)}, u32[]{:S(2)}) collective-permute-start(f32[64,128]{1,0:T(8,128)S(1)} %mid_lower.15.mine), channel_id=1, source_target_pairs={{0,6},{1,7},{2,4},{3,5},{4,2},{5,3},{6,0},{7,1},{8,14},{9,15},{10,... | collective-permute-start | bytes 98312 | tf_op jit(solution)/shard_map/mid_lower/ppermute | solution.py:120
  42.8 4.3 %collective-permute-start.23 = (f32[64,128]{1,0:T(8,128)S(1)}, f32[64,128]{1,0:T(8,128)S(1)}, u32[]{:S(2)}, u32[]{:S(2)}) collective-permute-start(f32[64,128]{1,0:T(8,128)S(1)} %mid_lower.19.mine.refs_0_), channel_id=1, source_target_pairs={{0,4},{1,3},{2,6},{3,1},{4,0},{5,7},{6,2},{7,5},{8,12},{9,11},{10,... | collective-permute-start | bytes 98312 | tf_op jit(solution)/shard_map/root_cut/ppermute | solution.py:138
  43.3 3.9 %collective-permute-start.22 = (f32[64,128]{1,0:T(8,128)S(1)}, f32[64,128]{1,0:T(8,128)S(1)}, u32[]{:S(2)}, u32[]{:S(2)}) collective-permute-start(f32[64,128]{1,0:T(8,128)S(1)} %mid_lower.19.mine.refs_0_), channel_id=1, source_target_pairs={{0,2},{1,5},{2,0},{3,7},{4,6},{5,1},{6,4},{7,3},{8,10},{9,13},{10,... | collective-permute-start | bytes 98312 | tf_op jit(solution)/shard_map/root_cut/ppermute | solution.py:138
  44.3 4.8 %collective-permute-start.26 = (f32[64,128]{1,0:T(8,128)S(1)}, f32[64,128]{1,0:T(8,128)S(1)}, u32[]{:S(2)}, u32[]{:S(2)}) collective-permute-start(f32[64,128]{1,0:T(8,128)S(1)} %mid_lower.19.mine.refs_0_), channel_id=1, source_target_pairs={{0,6},{1,7},{2,4},{3,5},{4,2},{5,3},{6,0},{7,1},{8,14},{9,15},{10,... | collective-permute-start | bytes 98312 | tf_op jit(solution)/shard_map/root_cut/ppermute | solution.py:120
  51.0 4.9 %collective-permute-start.28 = (f32[64,128]{1,0:T(8,128)S(1)}, f32[64,128]{1,0:T(8,128)S(1)}, u32[]{:S(2)}, u32[]{:S(2)}) collective-permute-start(f32[64,128]{1,0:T(8,128)S(1)} %get-tuple-element.91), channel_id=1, source_target_pairs={{0,16},{8,24},{16,0},{24,8},{1,17},{9,25},{17,1},{25,9},{2,18},{10... | collective-permute-start | bytes 98312 | tf_op jit(solution)/shard_map/root_cut/ppermute | solution.py:120
  55.9 3.9 %collective-permute-start.31 = (f32[64,128]{1,0:T(8,128)S(1)}, f32[64,128]{1,0:T(8,128)S(1)}, u32[]{:S(2)}, u32[]{:S(2)}) collective-permute-start(f32[64,128]{1,0:T(8,128)S(1)} %root_cut.13.mine), channel_id=1, source_target_pairs={{0,4},{1,3},{2,6},{3,1},{4,0},{5,7},{6,2},{7,5},{8,12},{9,11},{10,... | collective-permute-start | bytes 98312 | tf_op jit(solution)/shard_map/root_solve/ppermute | solution.py:138
  57.5 3.9 %collective-permute-start.30 = (f32[64,128]{1,0:T(8,128)S(1)}, f32[64,128]{1,0:T(8,128)S(1)}, u32[]{:S(2)}, u32[]{:S(2)}) collective-permute-start(f32[64,128]{1,0:T(8,128)S(1)} %root_cut.13.mine), channel_id=1, source_target_pairs={{0,2},{1,5},{2,0},{3,7},{4,6},{5,1},{6,4},{7,3},{8,10},{9,13},{10,... | collective-permute-start | bytes 98312 | tf_op jit(solution)/shard_map/root_solve/ppermute | solution.py:138
  58.9 4.8 %collective-permute-start.33 = (f32[64,128]{1,0:T(8,128)S(1)}, f32[64,128]{1,0:T(8,128)S(1)}, u32[]{:S(2)}, u32[]{:S(2)}) collective-permute-start(f32[64,128]{1,0:T(8,128)S(1)} %root_cut.13.mine), channel_id=1, source_target_pairs={{0,6},{1,7},{2,4},{3,5},{4,2},{5,3},{6,0},{7,1},{8,14},{9,15},{10,... | collective-permute-start | bytes 98312 | tf_op jit(solution)/shard_map/root_solve/ppermute | solution.py:120
  65.7 4.2 %collective-permute-start.36 = (f32[64,128]{1,0:T(8,128)S(1)}, f32[64,128]{1,0:T(8,128)S(1)}, u32[]{:S(2)}, u32[]{:S(2)}) collective-permute-start(f32[64,128]{1,0:T(8,128)S(1)} %root_solve.11.mine), channel_id=1, source_target_pairs={{0,4},{1,3},{2,6},{3,1},{4,0},{5,7},{6,2},{7,5},{8,12},{9,11},{10,... | collective-permute-start | bytes 98312 | tf_op jit(solution)/shard_map/root_solve/ppermute | solution.py:138
  65.9 4.0 %collective-permute-start.35 = (f32[64,128]{1,0:T(8,128)S(1)}, f32[64,128]{1,0:T(8,128)S(1)}, u32[]{:S(2)}, u32[]{:S(2)}) collective-permute-start(f32[64,128]{1,0:T(8,128)S(1)} %root_solve.11.mine), channel_id=1, source_target_pairs={{0,2},{1,5},{2,0},{3,7},{4,6},{5,1},{6,4},{7,3},{8,10},{9,13},{10,... | collective-permute-start | bytes 98312 | tf_op jit(solution)/shard_map/root_solve/ppermute | solution.py:138
  67.0 4.8 %collective-permute-start.39 = (f32[64,128]{1,0:T(8,128)S(1)}, f32[64,128]{1,0:T(8,128)S(1)}, u32[]{:S(2)}, u32[]{:S(2)}) collective-permute-start(f32[64,128]{1,0:T(8,128)S(1)} %root_solve.11.mine), channel_id=1, source_target_pairs={{0,6},{1,7},{2,4},{3,5},{4,2},{5,3},{6,0},{7,1},{8,14},{9,15},{10,... | collective-permute-start | bytes 98312 | tf_op jit(solution)/shard_map/root_solve/ppermute | solution.py:120
  74.0 4.9 %collective-permute-start.41 = (f32[64,128]{1,0:T(8,128)S(1)}, f32[64,128]{1,0:T(8,128)S(1)}, u32[]{:S(2)}, u32[]{:S(2)}) collective-permute-start(f32[64,128]{1,0:T(8,128)S(1)} %root_solve.15.mine), channel_id=1, source_target_pairs={{0,16},{8,24},{16,0},{24,8},{1,17},{9,25},{17,1},{25,9},{2,18},{10... | collective-permute-start | bytes 98312 | tf_op jit(solution)/shard_map/mid_upper/ppermute | solution.py:120
  81.2 5.0 %collective-permute-start.45 = (f32[256,128]{1,0:T(8,128)S(1)}, f32[256,128]{1,0:T(8,128)S(1)}, u32[]{:S(2)}, u32[]{:S(2)}) collective-permute-start(f32[256,128]{1,0:T(8,128)S(1)} %mid_upper.11.refs_0_), channel_id=1, source_target_pairs={{0,2},{1,5},{2,0},{3,7},{4,6},{5,1},{6,4},{7,3},{8,10},{9,13},{10,... | collective-permute-start | bytes 393224 | tf_op jit(solution)/shard_map/mid_upper/ppermute | solution.py:507
  82.7 4.2 %collective-permute-start.42 = (f32[64,128]{1,0:T(8,128)S(1)}, f32[64,128]{1,0:T(8,128)S(1)}, u32[]{:S(2)}, u32[]{:S(2)}) collective-permute-start(f32[64,128]{1,0:T(8,128)S(1)} %get-tuple-element.108.top), channel_id=1, source_target_pairs={{0,8},{8,0},{16,24},{24,16},{1,9},{9,1},{17,25},{25,17},{2,10},{10... | collective-permute-start | bytes 98312 | tf_op jit(solution)/shard_map/mid_upper/ppermute | solution.py:120
  86.9 5.0 %collective-permute-start.46 = (f32[256,128]{1,0:T(8,128)S(1)}, f32[256,128]{1,0:T(8,128)S(1)}, u32[]{:S(2)}, u32[]{:S(2)}) collective-permute-start(f32[256,128]{1,0:T(8,128)S(1)} %mid_upper.12.refs_0_), channel_id=1, source_target_pairs={{0,4},{1,3},{2,6},{3,1},{4,0},{5,7},{6,2},{7,5},{8,12},{9,11},{10,... | collective-permute-start | bytes 393224 | tf_op jit(solution)/shard_map/mid_upper/ppermute | solution.py:507
  88.8 3.9 %collective-permute-start.43 = (f32[64,128]{1,0:T(8,128)S(1)}, f32[64,128]{1,0:T(8,128)S(1)}, u32[]{:S(2)}, u32[]{:S(2)}) collective-permute-start(f32[64,128]{1,0:T(8,128)S(1)} %get-tuple-element.109.low), channel_id=1, source_target_pairs={{0,8},{8,0},{16,24},{24,16},{1,9},{9,1},{17,25},{25,17},{2,10},{10... | collective-permute-start | bytes 98312 | tf_op jit(solution)/shard_map/mid_upper/ppermute | solution.py:120
  94.8 4.0 %collective-permute-start.48 = (f32[64,128]{1,0:T(8,128)S(1)}, f32[64,128]{1,0:T(8,128)S(1)}, u32[]{:S(2)}, u32[]{:S(2)}) collective-permute-start(f32[64,128]{1,0:T(8,128)S(1)} %mid_upper.15.mine), channel_id=1, source_target_pairs={{0,8},{8,0},{16,24},{24,16},{1,9},{9,1},{17,25},{25,17},{2,10},{10... | collective-permute-start | bytes 98312 | tf_op jit(solution)/shard_map/leaf_upper/ppermute | solution.py:120
  100.6 5.0 %collective-permute-start.50 = (f32[256,128]{1,0:T(8,128)S(1)}, f32[256,128]{1,0:T(8,128)S(1)}, u32[]{:S(2)}, u32[]{:S(2)}) collective-permute-start(f32[256,128]{1,0:T(8,128)S(1)} %leaf_upper.10.refs_0_), channel_id=1, source_target_pairs={{0,2},{1,5},{2,0},{3,7},{4,6},{5,1},{6,4},{7,3},{8,10},{9,13},{10,... | collective-permute-start | bytes 393224 | tf_op jit(solution)/shard_map/leaf_upper/ppermute | solution.py:507
  101.6 5.2 %collective-permute-start.51 = (f32[64,128]{1,0:T(8,128)S(1)}, f32[64,128]{1,0:T(8,128)S(1)}, u32[]{:S(2)}, u32[]{:S(2)}) collective-permute-start(f32[64,128]{1,0:T(8,128)S(1)} %mid_upper.15.mine), channel_id=1, source_target_pairs={{0,16},{8,24},{16,0},{24,8},{1,17},{9,25},{17,1},{25,9},{2,18},{10... | collective-permute-start | bytes 98312 | tf_op jit(solution)/shard_map/leaf_upper/ppermute | solution.py:120
  106.7 5.0 %collective-permute-start.52 = (f32[256,128]{1,0:T(8,128)S(1)}, f32[256,128]{1,0:T(8,128)S(1)}, u32[]{:S(2)}, u32[]{:S(2)}) collective-permute-start(f32[256,128]{1,0:T(8,128)S(1)} %leaf_upper.11.refs_0_), channel_id=1, source_target_pairs={{0,4},{1,3},{2,6},{3,1},{4,0},{5,7},{6,2},{7,5},{8,12},{9,11},{10,... | collective-permute-start | bytes 393224 | tf_op jit(solution)/shard_map/leaf_upper/ppermute | solution.py:507
  (30 other events, 104.4 us)

commit v14 on v12

--- a/solution.py
+++ b/solution.py
@@ -127,17 +127,13 @@
         at += ref.shape[0]
 
 
-def hop(fronts, step, odd):
-    return 2 << (step ^ odd) if fronts == 8 else 2 * step + 2
+def hops(fronts):
+    return [2, 6, 4] if fronts == 8 else list(range(2, fronts, 2))
 
 
 def gather_front(x, meanwhile=None, others=()):
     fronts = lax.axis_size("front")
-    last = swap("front", x, fronts - 2)
-    near = [
-        lax.ppermute(x, "front", [(i, i ^ hop(fronts, step, i & 1)) for i in range(fronts)])
-        for step in range(fronts // 2 - 2)
-    ]
+    *near, last = [swap("front", x, k) for k in hops(fronts)]
     own = swap("front", x, 1)
     (both,) = kernel(stack, [(len(near) * x.shape[0], LANES)], *near)
     extra = tuple(meanwhile((both, own))) if meanwhile else ()
@@ -146,15 +142,15 @@
 
 
 def blocks_of(parts):
-    rows, fronts = parts[0].shape[0], 2 * len(parts) - 6
-    odd = lax.axis_index("front") & 1
+    rows = parts[0].shape[0]
+    *near, last = hops(2 * len(parts) - 6)
     yield 0, parts[0]
     yield 1, parts[1]
-    yield fronts - 2, parts[2]
-    yield fronts - 1, parts[-2]
-    for step, part in enumerate(parts[-3:2:-1]):
-        yield hop(fronts, step, odd), part
-        yield hop(fronts, step, odd ^ 1) + 1, parts[-1].at[rows * step : rows * step + rows, :]
+    yield last, parts[2]
+    yield last + 1, parts[-2]
+    for step, (k, part) in enumerate(zip(near, parts[-3:2:-1])):
+        yield k, part
+        yield k + 1, parts[-1].at[rows * step : rows * step + rows, :]
 
 
 def kernel(fn, outs, *args, scratch=(), vmem=8, work=0, hbm=(), pinned=()):
@@ -179,14 +175,11 @@
 
 def first_products(width, matrix, mine, other, *refs):
     near, both, out = refs[:-2], refs[-2], refs[-1]
-    rows, fronts = mine.shape[0], lax.axis_size("front")
-    odd = lax.axis_index("front") & 1
+    rows = mine.shape[0]
     total = chip_product(matrix, 0, mine[...], other[...], width)
-    for step, block in enumerate(near):
-        at = rows * (len(near) - 1 - step if fronts == 8 else step)
-        total += chip_product(
-            matrix, hop(fronts, step, odd), block[...], both[at : at + rows, :], width
-        )
+    for step, (k, block) in enumerate(zip(hops(lax.axis_size("front")), near)):
+        second = both[rows * step : rows * step + rows, :]
+        total += chip_product(matrix, k, block[...], second, width)
     out[...] = total
 
 
@@ -194,7 +187,7 @@
     parts, rest = refs[:count], refs[count:]
     if count == 3:
         known, mine, other = parts
-        k = lax.axis_size("front") - 2
+        k = hops(lax.axis_size("front"))[-1]
         finish(combined(known[...] + chip_product(matrix, k, mine[...], other[...], width)), *rest)
     else:
         assemble(rest[-1], parts, lax.axis_index("front"), width)
@@ -490,14 +483,16 @@
     fields_of(x, forward, adjoint, ())
 
 
-def sum_front(kept, sent, *others):
+def sum_front(kept, sent, before_last=(), at_end=()):
     fronts = lax.axis_size("front")
     (total,) = kernel(add, [kept.shape], kept, swap("front", sent, 1))
     hops = [1 << i for i in range(1, fronts.bit_length() - 1)]
     for hop, back in zip(hops, hops[::-1]):
         pairs = [(i, i ^ (back if i & 1 else hop)) for i in range(fronts)]
+        if hop == hops[-1]:
+            total = after(total, *before_last)
         (total,) = kernel(add, [kept.shape], total, lax.ppermute(total, "front", pairs))
-    return [total, swap("front", after(total, *others), 1)]
+    return [total, swap("front", after(total, *at_end), 1)]
 
 
 def mid_upper(matrix, y, piece, known, out):
@@ -524,10 +519,11 @@
     fields_of(combined(known[...] + half_product(1, LANES, matrix, y, piece)), forward, adjoint, ())
 
 
-def mid_outputs(mine, other, forward, adjoint):
+def mid_outputs(mine, far, other, forward, adjoint):
     parent = lax.axis_index("leaf") // 2
+    x = by_solve(lax.axis_index("leaf"), unpack(far[...], 2 * COLS), unpack(other[...], 2 * COLS))
     fields_of(mine[...], forward, adjoint, (parent,))
-    fields_of(other[...], forward, adjoint, (1 - parent,))
+    fields_of(x, forward, adjoint, (1 - parent,))
 
 
 def after(x, *others):
@@ -667,6 +663,7 @@
             swap("leaf", after(x_root, send), 1),
         )
     with jax.named_scope("leaf_upper"):
+        x_far = swap("leaf", x_mid, 2)
         send, x_mid = kernel(
             mid_to_leaf,
             [(s0 // 2, LANES), (n1, LANES)],
@@ -676,9 +673,11 @@
             swap("leaf", x_mid, 1),
         )
         (keep,) = kernel(mid_to_leaf_kept, [(s0 // 2, LANES)], l2m_up, from_root, x_mid)
-        x_other = swap("leaf", x_mid, 2)
-        mid_field, mid_adjoint = kernel(mid_outputs, [(2, 2, COLS, n1)] * 2, x_mid, x_other)
-        mine, theirs = sum_front(keep, send, x_other)
+        x_other = swap("leaf", x_far, 1)
+        mid_field, mid_adjoint = kernel(
+            mid_outputs, [(2, 2, COLS, n1)] * 2, x_mid, x_far, x_other
+        )
+        mine, theirs = sum_front(keep, send, (x_far,), (x_other,))
         (known,) = kernel(functools.partial(own_half, LANES), [(2 * n0, 2 * LANES)], lu, y_full, mine)
         leaf_field, leaf_adjoint = kernel(
             leaf_upper, [(2, COLS, n0)] * 2, lu, y_full, theirs, after(known, mid_field)

time: 115 us -> 116 us (level)
    ppermute x37 -> x50, starting transfers between devices: 27.7 us -> 44.1 us  [swap(): return lax.ppermute(x, axis, [(i, i ^ k) for i in range(size)])]
    ppermute x12 -> x0, starting transfers between devices: 13 us -> none  [gather_front(): lax.ppermute(x, 'front', [(i, i ^ hop(fronts, step, i & 1)) for i in rang...]
    ppermute x12 -> x0, waiting for transfers between devices: 8.97 us -> none  [gather_front(): lax.ppermute(x, 'front', [(i, i ^ hop(fronts, step, i & 1)) for i in rang...]
    ppermute x37 -> x50, waiting for transfers between devices: 18.4 us -> 26.5 us  [swap(): return lax.ppermute(x, axis, [(i, i ^ k) for i in range(size)])]
    ppermute x4, starting transfers between devices: 7.09 us -> 4.53 us  [sum_front(): lax.ppermute(total, 'front', pairs)]
  transfers between devices with their start and end apart: 53 -> 54, of which waited for: 35 -> 31; matrix products, arithmetic and copies ran while one was open for 0% -> 0% of each run, Pallas kernels for 17% -> 17%
where the time goes in v14:
time: 116 us; the launch traced here: 115 us
  starting transfers between devices  48.6 us (42%)
  waiting for transfers between devices  38.7 us (33%)
  Pallas kernels  27 us (23%)
  between operations  1.19 us (1%)
    ppermute x50, starting transfers between devices, swap(): return lax.ppermute(x, axis, [(i, i ^ k) for i in range(size)])  44.1 us
    pallas_call x48, Pallas kernels, kernel(): pl.pallas_call(fn, out_shape=[jax.ShapeDtypeStruct(*o) for o in outs], in...  27 us
    ppermute x50, waiting for transfers between devices, swap(): return lax.ppermute(x, axis, [(i, i ^ k) for i in range(size)])  26.5 us
    ppermute x4, waiting for transfers between devices, sum_front(): lax.ppermute(total, 'front', pairs)  12.2 us
    ppermute x4, starting transfers between devices, sum_front(): lax.ppermute(total, 'front', pairs)  4.53 us
  transfers between devices with their start and end apart: 54, of which 31 were waited for; matrix products, arithmetic and copies ran while one was open for 0% of the time, Pallas kernels for 17%

profile of v14, /device:TPU:0, one launch (start us, length us, event | category | flops | bytes accessed | tf_op | source)
XLA Modules:
  0.0 115.5 jit_solution(13050108390360231686)
XLA Ops:
  1.7 3.1 %collective-permute-start = (f32[32,128]{1,0:T(8,128)S(1)}, f32[32,128]{1,0:T(8,128)S(1)}, u32[]{:S(2)}, u32[]{:S(2)}) collective-permute-start(f32[32,128]{1,0:T(8,128)S(1)} %get-tuple-element.63), channel_id=1, source_target_pairs={{0,8},{8,0},{16,24},{24,16},{1,9},{9,1},{17,25},{25,17},{2,10},{10... | collective-permute-start | bytes 49160 | tf_op jit(solution)/shard_map/right_hand_sides/ppermute | solution.py:120
  4.8 1.7 %collective-permute-done.came.near = f32[32,128]{1,0:T(8,128)S(1)} collective-permute-done((f32[32,128]{1,0:T(8,128)S(1)}, f32[32,128]{1,0:T(8,128)S(1)}, u32[]{:S(2)}, u32[]{:S(2)}) %collective-permute-start) | collective-permute-done | bytes 16416 | tf_op jit(solution)/shard_map/right_hand_sides/ppermute | solution.py:120
  6.5 3.0 %collective-permute-start.1 = (f32[32,128]{1,0:T(8,128)S(1)}, f32[32,128]{1,0:T(8,128)S(1)}, u32[]{:S(2)}, u32[]{:S(2)}) collective-permute-start(f32[32,128]{1,0:T(8,128)S(1)} %right_hand_sides.6), channel_id=1, source_target_pairs={{0,16},{8,24},{16,0},{24,8},{1,17},{9,25},{17,1},{25,9},{2,18},{10... | collective-permute-start | bytes 49160 | tf_op jit(solution)/shard_map/right_hand_sides/ppermute | solution.py:120
  11.3 2.8 %collective-permute-start.3 = (f32[72,128]{1,0:T(8,128)S(1)}, f32[72,128]{1,0:T(8,128)S(1)}, u32[]{:S(2)}, u32[]{:S(2)}) collective-permute-start(f32[72,128]{1,0:T(8,128)S(1)} %right_hand_sides.7.refs_0_), channel_id=1, source_target_pairs={{0,6},{1,7},{2,4},{3,5},{4,2},{5,3},{6,0},{7,1},{8,14},{9,15},{10,... | collective-permute-start | bytes 110600 | tf_op jit(solution)/shard_map/leaf_lower/ppermute | solution.py:120
  14.9 1.4 %collective-permute-done.3.refs_1_.refs_3_ = f32[72,128]{1,0:T(8,128)S(1)} collective-permute-done((f32[72,128]{1,0:T(8,128)S(1)}, f32[72,128]{1,0:T(8,128)S(1)}, u32[]{:S(2)}, u32[]{:S(2)}) %collective-permute-start.3) | collective-permute-done | bytes 36896 | tf_op jit(solution)/shard_map/leaf_lower/ppermute | solution.py:120
  16.3 1.9 %collective-permute-done.2.refs_0_.refs_4_ = f32[72,128]{1,0:T(8,128)S(1)} collective-permute-done((f32[72,128]{1,0:T(8,128)S(1)}, f32[72,128]{1,0:T(8,128)S(1)}, u32[]{:S(2)}, u32[]{:S(2)}) %collective-permute-start.2) | collective-permute-done | bytes 36896 | tf_op jit(solution)/shard_map/leaf_lower/ppermute | solution.py:120
  18.2 1.3 %leaf_lower.4 = (bf16[128,1024]{1,0:T(8,128)(2,1)S(1)}, bf16[256,1024]{1,0:T(8,128)(2,1)S(1)}) custom-call(f32[2,1,64,512]{3,2,1,0:T(8,128)} %refs_0_, f32[2,1,128,512]{3,2,1,0:T(8,128)} %refs_1_.4), custom_call_target="tpu_custom_call" | custom-call | flops 98304000 | bytes 140434 | tf_op jit(solution)/shard_map/leaf_lower/pallas_call | solution.py:158
  23.6 1.5 %collective-permute-start.12 = (f32[64,128]{1,0:T(8,128)S(1)}, f32[64,128]{1,0:T(8,128)S(1)}, u32[]{:S(2)}, u32[]{:S(2)}) collective-permute-start(f32[64,128]{1,0:T(8,128)S(1)} %leaf_lower.5.mine.refs_0_), channel_id=1, source_target_pairs={{0,4},{1,5},{2,6},{3,7},{4,0},{5,1},{6,2},{7,3},{8,12},{9,13},{10,... | collective-permute-start | bytes 98312 | tf_op jit(solution)/shard_map/mid_lower/ppermute | solution.py:120
  25.2 1.4 %collective-permute-done.9.refs_1_.refs_3_ = f32[64,128]{1,0:T(8,128)S(1)} collective-permute-done((f32[64,128]{1,0:T(8,128)S(1)}, f32[64,128]{1,0:T(8,128)S(1)}, u32[]{:S(2)}, u32[]{:S(2)}) %collective-permute-start.9) | collective-permute-done | bytes 32800 | tf_op jit(solution)/shard_map/mid_lower/ppermute | solution.py:120
  26.7 1.6 %mid_lower.11 = (bf16[512,1024]{1,0:T(8,128)(2,1)S(1)}, bf16[256,2048]{1,0:T(8,128)(2,1)S(1)}) custom-call(f32[2,1,256,512]{3,2,1,0:T(8,128)} %refs_0_.1, f32[2,2,128,1024]{3,2,1,0:T(8,128)} %refs_1_.5), custom_call_target="tpu_custom_call" | custom-call | flops 262144000 | bytes 374491 | tf_op jit(solution)/shard_map/mid_lower/pallas_call | solution.py:158
  30.1 1.6 %collective-permute-start.14 = (f32[64,128]{1,0:T(8,128)S(1)}, f32[64,128]{1,0:T(8,128)S(1)}, u32[]{:S(2)}, u32[]{:S(2)}) collective-permute-start(f32[64,128]{1,0:T(8,128)S(1)} %get-tuple-element.76), channel_id=1, source_target_pairs={{0,8},{8,0},{16,24},{24,16},{1,9},{9,1},{17,25},{25,17},{2,10},{10... | collective-permute-start | bytes 98312 | tf_op jit(solution)/shard_map/mid_lower/ppermute | solution.py:120
  34.1 1.9 %collective-permute-start.17 = (f32[64,128]{1,0:T(8,128)S(1)}, f32[64,128]{1,0:T(8,128)S(1)}, u32[]{:S(2)}, u32[]{:S(2)}) collective-permute-start(f32[64,128]{1,0:T(8,128)S(1)} %mid_lower.15.mine), channel_id=1, source_target_pairs={{0,6},{1,7},{2,4},{3,5},{4,2},{5,3},{6,0},{7,1},{8,14},{9,15},{10,... | collective-permute-start | bytes 98312 | tf_op jit(solution)/shard_map/mid_lower/ppermute | solution.py:120
  37.6 1.3 %collective-permute-done.17.refs_1_ = f32[64,128]{1,0:T(8,128)S(1)} collective-permute-done((f32[64,128]{1,0:T(8,128)S(1)}, f32[64,128]{1,0:T(8,128)S(1)}, u32[]{:S(2)}, u32[]{:S(2)}) %collective-permute-start.17) | collective-permute-done | bytes 32800 | tf_op jit(solution)/shard_map/mid_lower/ppermute | solution.py:120
  40.0 1.8 %mid_lower.18.matrix = bf16[512,2048]{1,0:T(8,128)(2,1)S(1)} custom-call(f32[2,2,256,1024]{3,2,1,0:T(8,128)} %refs_0_.2), custom_call_target="tpu_custom_call" | custom-call | flops 262144000 | bytes 374491 | tf_op jit(solution)/shard_map/mid_lower/pallas_call | solution.py:158
  45.6 1.5 %collective-permute-start.26 = (f32[64,128]{1,0:T(8,128)S(1)}, f32[64,128]{1,0:T(8,128)S(1)}, u32[]{:S(2)}, u32[]{:S(2)}) collective-permute-start(f32[64,128]{1,0:T(8,128)S(1)} %mid_lower.19.mine.refs_0_), channel_id=1, source_target_pairs={{0,4},{1,5},{2,6},{3,7},{4,0},{5,1},{6,2},{7,3},{8,12},{9,13},{10,... | collective-permute-start | bytes 98312 | tf_op jit(solution)/shard_map/root_cut/ppermute | solution.py:120
  47.2 1.4 %collective-permute-done.23.refs_1_.refs_3_ = f32[64,128]{1,0:T(8,128)S(1)} collective-permute-done((f32[64,128]{1,0:T(8,128)S(1)}, f32[64,128]{1,0:T(8,128)S(1)}, u32[]{:S(2)}, u32[]{:S(2)}) %collective-permute-start.23) | collective-permute-done | bytes 32800 | tf_op jit(solution)/shard_map/root_cut/ppermute | solution.py:120
  48.7 1.3 %root_cut.8.matrix = bf16[512,4096]{1,0:T(8,128)(2,1)S(1)} custom-call(f32[2,256,2048]{2,1,0:T(8,128)S(1)} %copy-done.1), custom_call_target="tpu_custom_call" | custom-call | flops 524288000 | bytes 748982 | tf_op jit(solution)/shard_map/root_cut/pallas_call | solution.py:158
  52.1 2.7 %collective-permute-start.28 = (f32[64,128]{1,0:T(8,128)S(1)}, f32[64,128]{1,0:T(8,128)S(1)}, u32[]{:S(2)}, u32[]{:S(2)}) collective-permute-start(f32[64,128]{1,0:T(8,128)S(1)} %get-tuple-element.87), channel_id=1, source_target_pairs={{0,16},{8,24},{16,0},{24,8},{1,17},{9,25},{17,1},{25,9},{2,18},{10... | collective-permute-start | bytes 98312 | tf_op jit(solution)/shard_map/root_cut/ppermute | solution.py:120
  55.4 1.5 %collective-permute-done.28.refs_1_ = f32[64,128]{1,0:T(8,128)S(1)} collective-permute-done((f32[64,128]{1,0:T(8,128)S(1)}, f32[64,128]{1,0:T(8,128)S(1)}, u32[]{:S(2)}, u32[]{:S(2)}) %collective-permute-start.28) | collective-permute-done | bytes 32800 | tf_op jit(solution)/shard_map/root_cut/ppermute | solution.py:120
  57.0 1.9 %collective-permute-start.31 = (f32[64,128]{1,0:T(8,128)S(1)}, f32[64,128]{1,0:T(8,128)S(1)}, u32[]{:S(2)}, u32[]{:S(2)}) collective-permute-start(f32[64,128]{1,0:T(8,128)S(1)} %root_cut.13.mine), channel_id=1, source_target_pairs={{0,6},{1,7},{2,4},{3,5},{4,2},{5,3},{6,0},{7,1},{8,14},{9,15},{10,... | collective-permute-start | bytes 98312 | tf_op jit(solution)/shard_map/root_solve/ppermute | solution.py:120
  60.5 1.3 %collective-permute-done.31.refs_1_ = f32[64,128]{1,0:T(8,128)S(1)} collective-permute-done((f32[64,128]{1,0:T(8,128)S(1)}, f32[64,128]{1,0:T(8,128)S(1)}, u32[]{:S(2)}, u32[]{:S(2)}) %collective-permute-start.31) | collective-permute-done | bytes 32800 | tf_op jit(solution)/shard_map/root_solve/ppermute | solution.py:120
  68.5 1.5 %collective-permute-start.39 = (f32[64,128]{1,0:T(8,128)S(1)}, f32[64,128]{1,0:T(8,128)S(1)}, u32[]{:S(2)}, u32[]{:S(2)}) collective-permute-start(f32[64,128]{1,0:T(8,128)S(1)} %root_solve.11.mine), channel_id=1, source_target_pairs={{0,4},{1,5},{2,6},{3,7},{4,0},{5,1},{6,2},{7,3},{8,12},{9,13},{10,... | collective-permute-start | bytes 98312 | tf_op jit(solution)/shard_map/root_solve/ppermute | solution.py:120
  70.0 1.3 %collective-permute-done.36.refs_1_ = f32[64,128]{1,0:T(8,128)S(1)} collective-permute-done((f32[64,128]{1,0:T(8,128)S(1)}, f32[64,128]{1,0:T(8,128)S(1)}, u32[]{:S(2)}, u32[]{:S(2)}) %collective-permute-start.36) | collective-permute-done | bytes 32800 | tf_op jit(solution)/shard_map/root_solve/ppermute | solution.py:120
  71.5 1.5 %root_solve.13 = (bf16[2048,512]{1,0:T(8,128)(2,1)S(1)}, bf16[1024,256]{1,0:T(8,128)(2,1)S(1)}, bf16[128,1024]{1,0:T(8,128)(2,1)S(1)}) custom-call(f32[2,2,1024,256]{3,2,1,0:T(8,128)S(1)} %copy-done, f32[2,1,512,128]{3,2,1,0:T(8,128)S(1)} %copy-done.5, f32[2,1,64,512]{3,2,1,0:T(8,128)S(1)} %copy-done.6), custom_call_target="tpu_custom_call" | custom-call | flops 360448000 | bytes 514925 | tf_op jit(solution)/shard_map/root_solve/pallas_call | solution.py:158
  75.5 2.7 %collective-permute-start.41 = (f32[64,128]{1,0:T(8,128)S(1)}, f32[64,128]{1,0:T(8,128)S(1)}, u32[]{:S(2)}, u32[]{:S(2)}) collective-permute-start(f32[64,128]{1,0:T(8,128)S(1)} %root_solve.15.mine), channel_id=1, source_target_pairs={{0,16},{8,24},{16,0},{24,8},{1,17},{9,25},{17,1},{25,9},{2,18},{10... | collective-permute-start | bytes 98312 | tf_op jit(solution)/shard_map/mid_upper/ppermute | solution.py:120
  78.1 2.2 %collective-permute-done.41.other = f32[64,128]{1,0:T(8,128)S(1)} collective-permute-done((f32[64,128]{1,0:T(8,128)S(1)}, f32[64,128]{1,0:T(8,128)S(1)}, u32[]{:S(2)}, u32[]{:S(2)}) %collective-permute-start.41) | collective-permute-done | bytes 32800 | tf_op jit(solution)/shard_map/mid_upper/ppermute | solution.py:120
  83.6 4.0 %collective-permute-done.44.refs_1_ = f32[256,128]{1,0:T(8,128)S(1)} collective-permute-done((f32[256,128]{1,0:T(8,128)S(1)}, f32[256,128]{1,0:T(8,128)S(1)}, u32[]{:S(2)}, u32[]{:S(2)}) %collective-permute-start.44) | collective-permute-done | bytes 131104 | tf_op jit(solution)/shard_map/mid_upper/ppermute | solution.py:494
  88.7 4.0 %collective-permute-done.45.refs_1_ = f32[256,128]{1,0:T(8,128)S(1)} collective-permute-done((f32[256,128]{1,0:T(8,128)S(1)}, f32[256,128]{1,0:T(8,128)S(1)}, u32[]{:S(2)}, u32[]{:S(2)}) %collective-permute-start.45) | collective-permute-done | bytes 131104 | tf_op jit(solution)/shard_map/mid_upper/ppermute | solution.py:494
  92.8 1.7 %collective-permute-start.42 = (f32[128,128]{1,0:T(8,128)S(1)}, f32[128,128]{1,0:T(8,128)S(1)}, u32[]{:S(2)}, u32[]{:S(2)}) collective-permute-start(f32[128,128]{1,0:T(8,128)S(1)} %get-tuple-element.103.mine.x_root), channel_id=1, source_target_pairs={{0,8},{8,0},{16,24},{24,16},{1,9},{9,1},{17,25},{25,17},{2,10},{10... | collective-permute-start | bytes 196616 | tf_op jit(solution)/shard_map/mid_upper/ppermute | solution.py:120
  102.6 2.9 %collective-permute-start.50 = (f32[64,128]{1,0:T(8,128)S(1)}, f32[64,128]{1,0:T(8,128)S(1)}, u32[]{:S(2)}, u32[]{:S(2)}) collective-permute-start(f32[64,128]{1,0:T(8,128)S(1)} %mid_upper.15.mine), channel_id=1, source_target_pairs={{0,16},{8,24},{16,0},{24,8},{1,17},{9,25},{17,1},{25,9},{2,18},{10... | collective-permute-start | bytes 98312 | tf_op jit(solution)/shard_map/leaf_upper/ppermute | solution.py:120
  107.7 1.5 %collective-permute-start.51 = (f32[256,128]{1,0:T(8,128)S(1)}, f32[256,128]{1,0:T(8,128)S(1)}, u32[]{:S(2)}, u32[]{:S(2)}) collective-permute-start(f32[256,128]{1,0:T(8,128)S(1)} %leaf_upper.11.refs_0_), channel_id=1, source_target_pairs={{0,4},{1,3},{2,6},{3,1},{4,0},{5,7},{6,2},{7,5},{8,12},{9,11},{10,... | collective-permute-start | bytes 393224 | tf_op jit(solution)/shard_map/leaf_upper/ppermute | solution.py:494
  109.7 3.0 %collective-permute-done.51.refs_1_ = f32[256,128]{1,0:T(8,128)S(1)} collective-permute-done((f32[256,128]{1,0:T(8,128)S(1)}, f32[256,128]{1,0:T(8,128)S(1)}, u32[]{:S(2)}, u32[]{:S(2)}) %collective-permute-start.51) | collective-permute-done | bytes 131104 | tf_op jit(solution)/shard_map/leaf_upper/ppermute | solution.py:494
  (138 shorter events, 50.0 us)
Async XLA Ops:
  1.7 4.8 %collective-permute-start = (f32[32,128]{1,0:T(8,128)S(1)}, f32[32,128]{1,0:T(8,128)S(1)}, u32[]{:S(2)}, u32[]{:S(2)}) collective-permute-start(f32[32,128]{1,0:T(8,128)S(1)} %get-tuple-element.63), channel_id=1, source_target_pairs={{0,8},{8,0},{16,24},{24,16},{1,9},{9,1},{17,25},{25,17},{2,10},{10... | collective-permute-start | bytes 49160 | tf_op jit(solution)/shard_map/right_hand_sides/ppermute | solution.py:120
  6.5 4.7 %collective-permute-start.1 = (f32[32,128]{1,0:T(8,128)S(1)}, f32[32,128]{1,0:T(8,128)S(1)}, u32[]{:S(2)}, u32[]{:S(2)}) collective-permute-start(f32[32,128]{1,0:T(8,128)S(1)} %right_hand_sides.6), channel_id=1, source_target_pairs={{0,16},{8,24},{16,0},{24,8},{1,17},{9,25},{17,1},{25,9},{2,18},{10... | collective-permute-start | bytes 49160 | tf_op jit(solution)/shard_map/right_hand_sides/ppermute | solution.py:120
  11.3 4.9 %collective-permute-start.3 = (f32[72,128]{1,0:T(8,128)S(1)}, f32[72,128]{1,0:T(8,128)S(1)}, u32[]{:S(2)}, u32[]{:S(2)}) collective-permute-start(f32[72,128]{1,0:T(8,128)S(1)} %right_hand_sides.7.refs_0_), channel_id=1, source_target_pairs={{0,6},{1,7},{2,4},{3,5},{4,2},{5,3},{6,0},{7,1},{8,14},{9,15},{10,... | collective-permute-start | bytes 110600 | tf_op jit(solution)/shard_map/leaf_lower/ppermute | solution.py:120
  14.2 4.0 %collective-permute-start.2 = (f32[72,128]{1,0:T(8,128)S(1)}, f32[72,128]{1,0:T(8,128)S(1)}, u32[]{:S(2)}, u32[]{:S(2)}) collective-permute-start(f32[72,128]{1,0:T(8,128)S(1)} %right_hand_sides.7.refs_0_), channel_id=1, source_target_pairs={{0,2},{1,3},{2,0},{3,1},{4,6},{5,7},{6,4},{7,5},{8,10},{9,11},{10,... | collective-permute-start | bytes 110600 | tf_op jit(solution)/shard_map/leaf_lower/ppermute | solution.py:120
  14.7 4.8 %collective-permute-start.5 = (f32[72,128]{1,0:T(8,128)S(1)}, f32[72,128]{1,0:T(8,128)S(1)}, u32[]{:S(2)}, u32[]{:S(2)}) collective-permute-start(f32[72,128]{1,0:T(8,128)S(1)} %right_hand_sides.7.refs_0_), channel_id=1, source_target_pairs={{0,4},{1,5},{2,6},{3,7},{4,0},{5,1},{6,2},{7,3},{8,12},{9,13},{10,... | collective-permute-start | bytes 110600 | tf_op jit(solution)/shard_map/leaf_lower/ppermute | solution.py:120
  21.6 5.0 %collective-permute-start.9 = (f32[64,128]{1,0:T(8,128)S(1)}, f32[64,128]{1,0:T(8,128)S(1)}, u32[]{:S(2)}, u32[]{:S(2)}) collective-permute-start(f32[64,128]{1,0:T(8,128)S(1)} %leaf_lower.5.mine.refs_0_), channel_id=1, source_target_pairs={{0,6},{1,7},{2,4},{3,5},{4,2},{5,3},{6,0},{7,1},{8,14},{9,15},{10,... | collective-permute-start | bytes 98312 | tf_op jit(solution)/shard_map/mid_lower/ppermute | solution.py:120
  22.6 3.9 %collective-permute-start.8 = (f32[64,128]{1,0:T(8,128)S(1)}, f32[64,128]{1,0:T(8,128)S(1)}, u32[]{:S(2)}, u32[]{:S(2)}) collective-permute-start(f32[64,128]{1,0:T(8,128)S(1)} %leaf_lower.5.mine.refs_0_), channel_id=1, source_target_pairs={{0,2},{1,3},{2,0},{3,1},{4,6},{5,7},{6,4},{7,5},{8,10},{9,11},{10,... | collective-permute-start | bytes 98312 | tf_op jit(solution)/shard_map/mid_lower/ppermute | solution.py:120
  23.6 4.6 %collective-permute-start.12 = (f32[64,128]{1,0:T(8,128)S(1)}, f32[64,128]{1,0:T(8,128)S(1)}, u32[]{:S(2)}, u32[]{:S(2)}) collective-permute-start(f32[64,128]{1,0:T(8,128)S(1)} %leaf_lower.5.mine.refs_0_), channel_id=1, source_target_pairs={{0,4},{1,5},{2,6},{3,7},{4,0},{5,1},{6,2},{7,3},{8,12},{9,13},{10,... | collective-permute-start | bytes 98312 | tf_op jit(solution)/shard_map/mid_lower/ppermute | solution.py:120
  30.1 4.0 %collective-permute-start.14 = (f32[64,128]{1,0:T(8,128)S(1)}, f32[64,128]{1,0:T(8,128)S(1)}, u32[]{:S(2)}, u32[]{:S(2)}) collective-permute-start(f32[64,128]{1,0:T(8,128)S(1)} %get-tuple-element.76), channel_id=1, source_target_pairs={{0,8},{8,0},{16,24},{24,16},{1,9},{9,1},{17,25},{25,17},{2,10},{10... | collective-permute-start | bytes 98312 | tf_op jit(solution)/shard_map/mid_lower/ppermute | solution.py:120
  32.5 9.4 %collective-permute-start.20 = (f32[128,128]{1,0:T(8,128)S(1)}, f32[128,128]{1,0:T(8,128)S(1)}, u32[]{:S(2)}, u32[]{:S(2)}) collective-permute-start(f32[128,128]{1,0:T(8,128)S(1)} %get-tuple-element.81), channel_id=1, source_target_pairs={{0,8},{8,0},{16,24},{24,16},{1,9},{9,1},{17,25},{25,17},{2,10},{10... | collective-permute-start | bytes 196616 | tf_op jit(solution)/shard_map/mid_lower/ppermute | solution.py:120
  34.1 4.8 %collective-permute-start.17 = (f32[64,128]{1,0:T(8,128)S(1)}, f32[64,128]{1,0:T(8,128)S(1)}, u32[]{:S(2)}, u32[]{:S(2)}) collective-permute-start(f32[64,128]{1,0:T(8,128)S(1)} %mid_lower.15.mine), channel_id=1, source_target_pairs={{0,6},{1,7},{2,4},{3,5},{4,2},{5,3},{6,0},{7,1},{8,14},{9,15},{10,... | collective-permute-start | bytes 98312 | tf_op jit(solution)/shard_map/mid_lower/ppermute | solution.py:120
  36.0 3.9 %collective-permute-start.16 = (f32[64,128]{1,0:T(8,128)S(1)}, f32[64,128]{1,0:T(8,128)S(1)}, u32[]{:S(2)}, u32[]{:S(2)}) collective-permute-start(f32[64,128]{1,0:T(8,128)S(1)} %mid_lower.15.mine), channel_id=1, source_target_pairs={{0,2},{1,3},{2,0},{3,1},{4,6},{5,7},{6,4},{7,5},{8,10},{9,11},{10,... | collective-permute-start | bytes 98312 | tf_op jit(solution)/shard_map/mid_lower/ppermute | solution.py:120
  36.5 5.3 %collective-permute-start.19 = (f32[64,128]{1,0:T(8,128)S(1)}, f32[64,128]{1,0:T(8,128)S(1)}, u32[]{:S(2)}, u32[]{:S(2)}) collective-permute-start(f32[64,128]{1,0:T(8,128)S(1)} %mid_lower.15.mine), channel_id=1, source_target_pairs={{0,4},{1,5},{2,6},{3,7},{4,0},{5,1},{6,2},{7,3},{8,12},{9,13},{10,... | collective-permute-start | bytes 98312 | tf_op jit(solution)/shard_map/mid_lower/ppermute | solution.py:120
  43.6 4.9 %collective-permute-start.23 = (f32[64,128]{1,0:T(8,128)S(1)}, f32[64,128]{1,0:T(8,128)S(1)}, u32[]{:S(2)}, u32[]{:S(2)}) collective-permute-start(f32[64,128]{1,0:T(8,128)S(1)} %mid_lower.19.mine.refs_0_), channel_id=1, source_target_pairs={{0,6},{1,7},{2,4},{3,5},{4,2},{5,3},{6,0},{7,1},{8,14},{9,15},{10,... | collective-permute-start | bytes 98312 | tf_op jit(solution)/shard_map/root_cut/ppermute | solution.py:120
  44.7 3.9 %collective-permute-start.22 = (f32[64,128]{1,0:T(8,128)S(1)}, f32[64,128]{1,0:T(8,128)S(1)}, u32[]{:S(2)}, u32[]{:S(2)}) collective-permute-start(f32[64,128]{1,0:T(8,128)S(1)} %mid_lower.19.mine.refs_0_), channel_id=1, source_target_pairs={{0,2},{1,3},{2,0},{3,1},{4,6},{5,7},{6,4},{7,5},{8,10},{9,11},{10,... | collective-permute-start | bytes 98312 | tf_op jit(solution)/shard_map/root_cut/ppermute | solution.py:120
  45.6 4.3 %collective-permute-start.26 = (f32[64,128]{1,0:T(8,128)S(1)}, f32[64,128]{1,0:T(8,128)S(1)}, u32[]{:S(2)}, u32[]{:S(2)}) collective-permute-start(f32[64,128]{1,0:T(8,128)S(1)} %mid_lower.19.mine.refs_0_), channel_id=1, source_target_pairs={{0,4},{1,5},{2,6},{3,7},{4,0},{5,1},{6,2},{7,3},{8,12},{9,13},{10,... | collective-permute-start | bytes 98312 | tf_op jit(solution)/shard_map/root_cut/ppermute | solution.py:120
  52.1 4.9 %collective-permute-start.28 = (f32[64,128]{1,0:T(8,128)S(1)}, f32[64,128]{1,0:T(8,128)S(1)}, u32[]{:S(2)}, u32[]{:S(2)}) collective-permute-start(f32[64,128]{1,0:T(8,128)S(1)} %get-tuple-element.87), channel_id=1, source_target_pairs={{0,16},{8,24},{16,0},{24,8},{1,17},{9,25},{17,1},{25,9},{2,18},{10... | collective-permute-start | bytes 98312 | tf_op jit(solution)/shard_map/root_cut/ppermute | solution.py:120
  57.0 4.8 %collective-permute-start.31 = (f32[64,128]{1,0:T(8,128)S(1)}, f32[64,128]{1,0:T(8,128)S(1)}, u32[]{:S(2)}, u32[]{:S(2)}) collective-permute-start(f32[64,128]{1,0:T(8,128)S(1)} %root_cut.13.mine), channel_id=1, source_target_pairs={{0,6},{1,7},{2,4},{3,5},{4,2},{5,3},{6,0},{7,1},{8,14},{9,15},{10,... | collective-permute-start | bytes 98312 | tf_op jit(solution)/shard_map/root_solve/ppermute | solution.py:120
  58.9 3.9 %collective-permute-start.30 = (f32[64,128]{1,0:T(8,128)S(1)}, f32[64,128]{1,0:T(8,128)S(1)}, u32[]{:S(2)}, u32[]{:S(2)}) collective-permute-start(f32[64,128]{1,0:T(8,128)S(1)} %root_cut.13.mine), channel_id=1, source_target_pairs={{0,2},{1,3},{2,0},{3,1},{4,6},{5,7},{6,4},{7,5},{8,10},{9,11},{10,... | collective-permute-start | bytes 98312 | tf_op jit(solution)/shard_map/root_solve/ppermute | solution.py:120
  59.4 4.5 %collective-permute-start.33 = (f32[64,128]{1,0:T(8,128)S(1)}, f32[64,128]{1,0:T(8,128)S(1)}, u32[]{:S(2)}, u32[]{:S(2)}) collective-permute-start(f32[64,128]{1,0:T(8,128)S(1)} %root_cut.13.mine), channel_id=1, source_target_pairs={{0,4},{1,5},{2,6},{3,7},{4,0},{5,1},{6,2},{7,3},{8,12},{9,13},{10,... | collective-permute-start | bytes 98312 | tf_op jit(solution)/shard_map/root_solve/ppermute | solution.py:120
  66.4 4.9 %collective-permute-start.36 = (f32[64,128]{1,0:T(8,128)S(1)}, f32[64,128]{1,0:T(8,128)S(1)}, u32[]{:S(2)}, u32[]{:S(2)}) collective-permute-start(f32[64,128]{1,0:T(8,128)S(1)} %root_solve.11.mine), channel_id=1, source_target_pairs={{0,6},{1,7},{2,4},{3,5},{4,2},{5,3},{6,0},{7,1},{8,14},{9,15},{10,... | collective-permute-start | bytes 98312 | tf_op jit(solution)/shard_map/root_solve/ppermute | solution.py:120
  67.5 3.9 %collective-permute-start.35 = (f32[64,128]{1,0:T(8,128)S(1)}, f32[64,128]{1,0:T(8,128)S(1)}, u32[]{:S(2)}, u32[]{:S(2)}) collective-permute-start(f32[64,128]{1,0:T(8,128)S(1)} %root_solve.11.mine), channel_id=1, source_target_pairs={{0,2},{1,3},{2,0},{3,1},{4,6},{5,7},{6,4},{7,5},{8,10},{9,11},{10,... | collective-permute-start | bytes 98312 | tf_op jit(solution)/shard_map/root_solve/ppermute | solution.py:120
  68.5 4.5 %collective-permute-start.39 = (f32[64,128]{1,0:T(8,128)S(1)}, f32[64,128]{1,0:T(8,128)S(1)}, u32[]{:S(2)}, u32[]{:S(2)}) collective-permute-start(f32[64,128]{1,0:T(8,128)S(1)} %root_solve.11.mine), channel_id=1, source_target_pairs={{0,4},{1,5},{2,6},{3,7},{4,0},{5,1},{6,2},{7,3},{8,12},{9,13},{10,... | collective-permute-start | bytes 98312 | tf_op jit(solution)/shard_map/root_solve/ppermute | solution.py:120
  75.5 4.9 %collective-permute-start.41 = (f32[64,128]{1,0:T(8,128)S(1)}, f32[64,128]{1,0:T(8,128)S(1)}, u32[]{:S(2)}, u32[]{:S(2)}) collective-permute-start(f32[64,128]{1,0:T(8,128)S(1)} %root_solve.15.mine), channel_id=1, source_target_pairs={{0,16},{8,24},{16,0},{24,8},{1,17},{9,25},{17,1},{25,9},{2,18},{10... | collective-permute-start | bytes 98312 | tf_op jit(solution)/shard_map/mid_upper/ppermute | solution.py:120
  82.6 5.0 %collective-permute-start.44 = (f32[256,128]{1,0:T(8,128)S(1)}, f32[256,128]{1,0:T(8,128)S(1)}, u32[]{:S(2)}, u32[]{:S(2)}) collective-permute-start(f32[256,128]{1,0:T(8,128)S(1)} %mid_upper.11.refs_0_), channel_id=1, source_target_pairs={{0,2},{1,5},{2,0},{3,7},{4,6},{5,1},{6,4},{7,3},{8,10},{9,13},{10,... | collective-permute-start | bytes 393224 | tf_op jit(solution)/shard_map/mid_upper/ppermute | solution.py:494
  87.7 5.0 %collective-permute-start.45 = (f32[256,128]{1,0:T(8,128)S(1)}, f32[256,128]{1,0:T(8,128)S(1)}, u32[]{:S(2)}, u32[]{:S(2)}) collective-permute-start(f32[256,128]{1,0:T(8,128)S(1)} %mid_upper.12.refs_0_), channel_id=1, source_target_pairs={{0,4},{1,3},{2,6},{3,1},{4,0},{5,7},{6,2},{7,5},{8,12},{9,11},{10,... | collective-permute-start | bytes 393224 | tf_op jit(solution)/shard_map/mid_upper/ppermute | solution.py:494
  92.8 4.5 %collective-permute-start.42 = (f32[128,128]{1,0:T(8,128)S(1)}, f32[128,128]{1,0:T(8,128)S(1)}, u32[]{:S(2)}, u32[]{:S(2)}) collective-permute-start(f32[128,128]{1,0:T(8,128)S(1)} %get-tuple-element.103.mine.x_root), channel_id=1, source_target_pairs={{0,8},{8,0},{16,24},{24,16},{1,9},{9,1},{17,25},{25,17},{2,10},{10... | collective-permute-start | bytes 196616 | tf_op jit(solution)/shard_map/mid_upper/ppermute | solution.py:120
  95.7 4.0 %collective-permute-start.47 = (f32[64,128]{1,0:T(8,128)S(1)}, f32[64,128]{1,0:T(8,128)S(1)}, u32[]{:S(2)}, u32[]{:S(2)}) collective-permute-start(f32[64,128]{1,0:T(8,128)S(1)} %mid_upper.15.mine), channel_id=1, source_target_pairs={{0,8},{8,0},{16,24},{24,16},{1,9},{9,1},{17,25},{25,17},{2,10},{10... | collective-permute-start | bytes 98312 | tf_op jit(solution)/shard_map/leaf_upper/ppermute | solution.py:120
  101.6 5.0 %collective-permute-start.49 = (f32[256,128]{1,0:T(8,128)S(1)}, f32[256,128]{1,0:T(8,128)S(1)}, u32[]{:S(2)}, u32[]{:S(2)}) collective-permute-start(f32[256,128]{1,0:T(8,128)S(1)} %leaf_upper.10.refs_0_), channel_id=1, source_target_pairs={{0,2},{1,5},{2,0},{3,7},{4,6},{5,1},{6,4},{7,3},{8,10},{9,13},{10,... | collective-permute-start | bytes 393224 | tf_op jit(solution)/shard_map/leaf_upper/ppermute | solution.py:494
  102.6 5.2 %collective-permute-start.50 = (f32[64,128]{1,0:T(8,128)S(1)}, f32[64,128]{1,0:T(8,128)S(1)}, u32[]{:S(2)}, u32[]{:S(2)}) collective-permute-start(f32[64,128]{1,0:T(8,128)S(1)} %mid_upper.15.mine), channel_id=1, source_target_pairs={{0,16},{8,24},{16,0},{24,8},{1,17},{9,25},{17,1},{25,9},{2,18},{10... | collective-permute-start | bytes 98312 | tf_op jit(solution)/shard_map/leaf_upper/ppermute | solution.py:120
  107.7 5.0 %collective-permute-start.51 = (f32[256,128]{1,0:T(8,128)S(1)}, f32[256,128]{1,0:T(8,128)S(1)}, u32[]{:S(2)}, u32[]{:S(2)}) collective-permute-start(f32[256,128]{1,0:T(8,128)S(1)} %leaf_upper.11.refs_0_), channel_id=1, source_target_pairs={{0,4},{1,3},{2,6},{3,1},{4,0},{5,7},{6,2},{7,5},{8,12},{9,11},{10,... | collective-permute-start | bytes 393224 | tf_op jit(solution)/shard_map/leaf_upper/ppermute | solution.py:494
  109.2 3.9 %collective-permute-start.52 = (f32[64,128]{1,0:T(8,128)S(1)}, f32[64,128]{1,0:T(8,128)S(1)}, u32[]{:S(2)}, u32[]{:S(2)}) collective-permute-start(f32[64,128]{1,0:T(8,128)S(1)} %collective-permute-done.50.far), channel_id=1, source_target_pairs={{0,8},{8,0},{16,24},{24,16},{1,9},{9,1},{17,25},{25,17},{2,10},{10... | collective-permute-start | bytes 98312 | tf_op jit(solution)/shard_map/leaf_upper/ppermute | solution.py:120
  (29 other events, 103.3 us)

commit v15 on v14

--- a/solution.py
+++ b/solution.py
@@ -135,8 +135,8 @@
     fronts = lax.axis_size("front")
     *near, last = [swap("front", x, k) for k in hops(fronts)]
     own = swap("front", x, 1)
-    (both,) = kernel(stack, [(len(near) * x.shape[0], LANES)], *near)
-    extra = tuple(meanwhile((both, own))) if meanwhile else ()
+    extra = tuple(meanwhile((own,))) if meanwhile else ()
+    (both,) = kernel(stack, [(len(near) * x.shape[0], LANES)], *near[:-1], after(near[-1], *extra))
     last = after(last, *extra, *others)
     return [x, own, last, *near[::-1], swap("front", last, 1), swap("front", both, 1)], extra
 

time: 116 us -> 114 us (0.983)
  starting transfers between devices: 48.6 us -> 46.4 us
    ppermute x4, starting transfers between devices: 4.53 us -> 3.29 us  [sum_front(): lax.ppermute(total, 'front', pairs)]
  transfers between devices with their start and end apart: 54 -> 54, of which waited for: 31 -> 34; matrix products, arithmetic and copies ran while one was open for 0% -> 0% of each run, Pallas kernels for 17% -> 17%
where the time goes in v15:
time: 114 us
  starting transfers between devices  46.4 us (41%)
  waiting for transfers between devices  39.8 us (35%)
  Pallas kernels  26.6 us (23%)
    ppermute x50, starting transfers between devices, swap(): return lax.ppermute(x, axis, [(i, i ^ k) for i in range(size)])  43.1 us
    pallas_call x48, Pallas kernels, kernel(): pl.pallas_call(fn, out_shape=[jax.ShapeDtypeStruct(*o) for o in outs], in...  26.6 us
    ppermute x50, waiting for transfers between devices, swap(): return lax.ppermute(x, axis, [(i, i ^ k) for i in range(size)])  26.5 us
    ppermute x4, waiting for transfers between devices, sum_front(): lax.ppermute(total, 'front', pairs)  13.3 us
    ppermute x4, starting transfers between devices, sum_front(): lax.ppermute(total, 'front', pairs)  3.29 us
  transfers between devices with their start and end apart: 54, of which 34 were waited for; matrix products, arithmetic and copies ran while one was open for 0% of the time, Pallas kernels for 17%

profile of v15, /device:TPU:0, one launch (start us, length us, event | category | flops | bytes accessed | tf_op | source)
XLA Modules:
  0.0 114.0 jit_solution(10717989067937603814)
XLA Ops:
  1.7 3.1 %collective-permute-start = (f32[32,128]{1,0:T(8,128)S(1)}, f32[32,128]{1,0:T(8,128)S(1)}, u32[]{:S(2)}, u32[]{:S(2)}) collective-permute-start(f32[32,128]{1,0:T(8,128)S(1)} %get-tuple-element.69), channel_id=1, source_target_pairs={{0,8},{8,0},{16,24},{24,16},{1,9},{9,1},{17,25},{25,17},{2,10},{10... | collective-permute-start | bytes 49160 | tf_op jit(solution)/shard_map/right_hand_sides/ppermute | solution.py:120
  4.8 1.7 %collective-permute-done.came.near = f32[32,128]{1,0:T(8,128)S(1)} collective-permute-done((f32[32,128]{1,0:T(8,128)S(1)}, f32[32,128]{1,0:T(8,128)S(1)}, u32[]{:S(2)}, u32[]{:S(2)}) %collective-permute-start) | collective-permute-done | bytes 16416 | tf_op jit(solution)/shard_map/right_hand_sides/ppermute | solution.py:120
  6.5 3.0 %collective-permute-start.1 = (f32[32,128]{1,0:T(8,128)S(1)}, f32[32,128]{1,0:T(8,128)S(1)}, u32[]{:S(2)}, u32[]{:S(2)}) collective-permute-start(f32[32,128]{1,0:T(8,128)S(1)} %right_hand_sides.6), channel_id=1, source_target_pairs={{0,16},{8,24},{16,0},{24,8},{1,17},{9,25},{17,1},{25,9},{2,18},{10... | collective-permute-start | bytes 49160 | tf_op jit(solution)/shard_map/right_hand_sides/ppermute | solution.py:120
  11.4 2.8 %collective-permute-start.4 = (f32[72,128]{1,0:T(8,128)S(1)}, f32[72,128]{1,0:T(8,128)S(1)}, u32[]{:S(2)}, u32[]{:S(2)}) collective-permute-start(f32[72,128]{1,0:T(8,128)S(1)} %right_hand_sides.7.refs_0_), channel_id=1, source_target_pairs={{0,6},{1,7},{2,4},{3,5},{4,2},{5,3},{6,0},{7,1},{8,14},{9,15},{10,... | collective-permute-start | bytes 110600 | tf_op jit(solution)/shard_map/leaf_lower/ppermute | solution.py:120
  16.3 1.9 %collective-permute-done.5.refs_0_.refs_4_ = f32[72,128]{1,0:T(8,128)S(1)} collective-permute-done((f32[72,128]{1,0:T(8,128)S(1)}, f32[72,128]{1,0:T(8,128)S(1)}, u32[]{:S(2)}, u32[]{:S(2)}) %collective-permute-start.5) | collective-permute-done | bytes 36896 | tf_op jit(solution)/shard_map/leaf_lower/ppermute | solution.py:120
  20.9 1.4 %collective-permute-start.10 = (f32[64,128]{1,0:T(8,128)S(1)}, f32[64,128]{1,0:T(8,128)S(1)}, u32[]{:S(2)}, u32[]{:S(2)}) collective-permute-start(f32[64,128]{1,0:T(8,128)S(1)} %leaf_lower.5.mine.refs_0_), channel_id=1, source_target_pairs={{0,6},{1,7},{2,4},{3,5},{4,2},{5,3},{6,0},{7,1},{8,14},{9,15},{10,... | collective-permute-start | bytes 98312 | tf_op jit(solution)/shard_map/mid_lower/ppermute | solution.py:120
  22.7 1.7 %collective-permute-start.12 = (f32[64,128]{1,0:T(8,128)S(1)}, f32[64,128]{1,0:T(8,128)S(1)}, u32[]{:S(2)}, u32[]{:S(2)}) collective-permute-start(f32[64,128]{1,0:T(8,128)S(1)} %leaf_lower.5.mine.refs_0_), channel_id=1, source_target_pairs={{0,4},{1,5},{2,6},{3,7},{4,0},{5,1},{6,2},{7,3},{8,12},{9,13},{10,... | collective-permute-start | bytes 98312 | tf_op jit(solution)/shard_map/mid_lower/ppermute | solution.py:120
  24.4 1.6 %mid_lower.10 = (bf16[512,1024]{1,0:T(8,128)(2,1)S(1)}, bf16[256,2048]{1,0:T(8,128)(2,1)S(1)}) custom-call(f32[2,1,256,512]{3,2,1,0:T(8,128)} %refs_0_.1, f32[2,2,128,1024]{3,2,1,0:T(8,128)} %refs_1_.5), custom_call_target="tpu_custom_call" | custom-call | flops 262144000 | bytes 374491 | tf_op jit(solution)/shard_map/mid_lower/pallas_call | solution.py:158
  28.4 1.7 %collective-permute-start.14 = (f32[64,128]{1,0:T(8,128)S(1)}, f32[64,128]{1,0:T(8,128)S(1)}, u32[]{:S(2)}, u32[]{:S(2)}) collective-permute-start(f32[64,128]{1,0:T(8,128)S(1)} %get-tuple-element.84), channel_id=1, source_target_pairs={{0,8},{8,0},{16,24},{24,16},{1,9},{9,1},{17,25},{25,17},{2,10},{10... | collective-permute-start | bytes 98312 | tf_op jit(solution)/shard_map/mid_lower/ppermute | solution.py:120
  30.8 1.6 %collective-permute-done.14.refs_1_ = f32[64,128]{1,0:T(8,128)S(1)} collective-permute-done((f32[64,128]{1,0:T(8,128)S(1)}, f32[64,128]{1,0:T(8,128)S(1)}, u32[]{:S(2)}, u32[]{:S(2)}) %collective-permute-start.14) | collective-permute-done | bytes 32800 | tf_op jit(solution)/shard_map/mid_lower/ppermute | solution.py:120
  32.4 2.6 %collective-permute-start.17 = (f32[64,128]{1,0:T(8,128)S(1)}, f32[64,128]{1,0:T(8,128)S(1)}, u32[]{:S(2)}, u32[]{:S(2)}) collective-permute-start(f32[64,128]{1,0:T(8,128)S(1)} %mid_lower.15.mine), channel_id=1, source_target_pairs={{0,6},{1,7},{2,4},{3,5},{4,2},{5,3},{6,0},{7,1},{8,14},{9,15},{10,... | collective-permute-start | bytes 98312 | tf_op jit(solution)/shard_map/mid_lower/ppermute | solution.py:120
  35.5 1.6 %collective-permute-start.20 = (f32[128,128]{1,0:T(8,128)S(1)}, f32[128,128]{1,0:T(8,128)S(1)}, u32[]{:S(2)}, u32[]{:S(2)}) collective-permute-start(f32[128,128]{1,0:T(8,128)S(1)} %get-tuple-element.90), channel_id=1, source_target_pairs={{0,8},{8,0},{16,24},{24,16},{1,9},{9,1},{17,25},{25,17},{2,10},{10... | collective-permute-start | bytes 196616 | tf_op jit(solution)/shard_map/mid_lower/ppermute | solution.py:120
  37.5 1.6 %mid_lower.16.matrix = bf16[512,2048]{1,0:T(8,128)(2,1)S(1)} custom-call(f32[2,2,256,1024]{3,2,1,0:T(8,128)} %refs_0_.2), custom_call_target="tpu_custom_call" | custom-call | flops 262144000 | bytes 374491 | tf_op jit(solution)/shard_map/mid_lower/pallas_call | solution.py:158
  39.3 1.7 %collective-permute-done.19.refs_1_ = f32[64,128]{1,0:T(8,128)S(1)} collective-permute-done((f32[64,128]{1,0:T(8,128)S(1)}, f32[64,128]{1,0:T(8,128)S(1)}, u32[]{:S(2)}, u32[]{:S(2)}) %collective-permute-start.19) | collective-permute-done | bytes 32800 | tf_op jit(solution)/shard_map/mid_lower/ppermute | solution.py:120
  42.9 1.5 %collective-permute-start.23 = (f32[64,128]{1,0:T(8,128)S(1)}, f32[64,128]{1,0:T(8,128)S(1)}, u32[]{:S(2)}, u32[]{:S(2)}) collective-permute-start(f32[64,128]{1,0:T(8,128)S(1)} %mid_lower.19.mine.refs_0_), channel_id=1, source_target_pairs={{0,2},{1,3},{2,0},{3,1},{4,6},{5,7},{6,4},{7,5},{8,10},{9,11},{10,... | collective-permute-start | bytes 98312 | tf_op jit(solution)/shard_map/root_cut/ppermute | solution.py:120
  44.9 1.5 %collective-permute-start.26 = (f32[64,128]{1,0:T(8,128)S(1)}, f32[64,128]{1,0:T(8,128)S(1)}, u32[]{:S(2)}, u32[]{:S(2)}) collective-permute-start(f32[64,128]{1,0:T(8,128)S(1)} %mid_lower.19.mine.refs_0_), channel_id=1, source_target_pairs={{0,4},{1,5},{2,6},{3,7},{4,0},{5,1},{6,2},{7,3},{8,12},{9,13},{10,... | collective-permute-start | bytes 98312 | tf_op jit(solution)/shard_map/root_cut/ppermute | solution.py:120
  47.5 1.7 %collective-permute-done.24.refs_1_.refs_3_ = f32[64,128]{1,0:T(8,128)S(1)} collective-permute-done((f32[64,128]{1,0:T(8,128)S(1)}, f32[64,128]{1,0:T(8,128)S(1)}, u32[]{:S(2)}, u32[]{:S(2)}) %collective-permute-start.24) | collective-permute-done | bytes 32800 | tf_op jit(solution)/shard_map/root_cut/ppermute | solution.py:120
  52.0 2.7 %collective-permute-start.28 = (f32[64,128]{1,0:T(8,128)S(1)}, f32[64,128]{1,0:T(8,128)S(1)}, u32[]{:S(2)}, u32[]{:S(2)}) collective-permute-start(f32[64,128]{1,0:T(8,128)S(1)} %get-tuple-element.97), channel_id=1, source_target_pairs={{0,16},{8,24},{16,0},{24,8},{1,17},{9,25},{17,1},{25,9},{2,18},{10... | collective-permute-start | bytes 98312 | tf_op jit(solution)/shard_map/root_cut/ppermute | solution.py:120
  55.4 1.7 %collective-permute-done.28.refs_1_ = f32[64,128]{1,0:T(8,128)S(1)} collective-permute-done((f32[64,128]{1,0:T(8,128)S(1)}, f32[64,128]{1,0:T(8,128)S(1)}, u32[]{:S(2)}, u32[]{:S(2)}) %collective-permute-start.28) | collective-permute-done | bytes 32800 | tf_op jit(solution)/shard_map/root_cut/ppermute | solution.py:120
  57.7 1.5 %collective-permute-start.31 = (f32[64,128]{1,0:T(8,128)S(1)}, f32[64,128]{1,0:T(8,128)S(1)}, u32[]{:S(2)}, u32[]{:S(2)}) collective-permute-start(f32[64,128]{1,0:T(8,128)S(1)} %root_cut.13.mine), channel_id=1, source_target_pairs={{0,6},{1,7},{2,4},{3,5},{4,2},{5,3},{6,0},{7,1},{8,14},{9,15},{10,... | collective-permute-start | bytes 98312 | tf_op jit(solution)/shard_map/root_solve/ppermute | solution.py:120
  59.2 1.5 %collective-permute-start.33 = (f32[64,128]{1,0:T(8,128)S(1)}, f32[64,128]{1,0:T(8,128)S(1)}, u32[]{:S(2)}, u32[]{:S(2)}) collective-permute-start(f32[64,128]{1,0:T(8,128)S(1)} %root_cut.13.mine), channel_id=1, source_target_pairs={{0,4},{1,5},{2,6},{3,7},{4,0},{5,1},{6,2},{7,3},{8,12},{9,13},{10,... | collective-permute-start | bytes 98312 | tf_op jit(solution)/shard_map/root_solve/ppermute | solution.py:120
  66.1 1.5 %collective-permute-start.36 = (f32[64,128]{1,0:T(8,128)S(1)}, f32[64,128]{1,0:T(8,128)S(1)}, u32[]{:S(2)}, u32[]{:S(2)}) collective-permute-start(f32[64,128]{1,0:T(8,128)S(1)} %root_solve.11.mine), channel_id=1, source_target_pairs={{0,2},{1,3},{2,0},{3,1},{4,6},{5,7},{6,4},{7,5},{8,10},{9,11},{10,... | collective-permute-start | bytes 98312 | tf_op jit(solution)/shard_map/root_solve/ppermute | solution.py:120
  69.6 1.4 %root_solve.12 = (bf16[2048,512]{1,0:T(8,128)(2,1)S(1)}, bf16[1024,256]{1,0:T(8,128)(2,1)S(1)}, bf16[128,1024]{1,0:T(8,128)(2,1)S(1)}) custom-call(f32[2,2,1024,256]{3,2,1,0:T(8,128)S(1)} %copy-done, f32[2,1,512,128]{3,2,1,0:T(8,128)S(1)} %copy-done.5, f32[2,1,64,512]{3,2,1,0:T(8,128)S(1)} %copy-done.6), custom_call_target="tpu_custom_call" | custom-call | flops 360448000 | bytes 514925 | tf_op jit(solution)/shard_map/root_solve/pallas_call | solution.py:158
  75.6 2.5 %collective-permute-start.41 = (f32[64,128]{1,0:T(8,128)S(1)}, f32[64,128]{1,0:T(8,128)S(1)}, u32[]{:S(2)}, u32[]{:S(2)}) collective-permute-start(f32[64,128]{1,0:T(8,128)S(1)} %root_solve.15.mine), channel_id=1, source_target_pairs={{0,16},{8,24},{16,0},{24,8},{1,17},{9,25},{17,1},{25,9},{2,18},{10... | collective-permute-start | bytes 98312 | tf_op jit(solution)/shard_map/mid_upper/ppermute | solution.py:120
  78.1 2.4 %collective-permute-done.41.other = f32[64,128]{1,0:T(8,128)S(1)} collective-permute-done((f32[64,128]{1,0:T(8,128)S(1)}, f32[64,128]{1,0:T(8,128)S(1)}, u32[]{:S(2)}, u32[]{:S(2)}) %collective-permute-start.41) | collective-permute-done | bytes 32800 | tf_op jit(solution)/shard_map/mid_upper/ppermute | solution.py:120
  83.4 4.4 %collective-permute-done.44.refs_1_ = f32[256,128]{1,0:T(8,128)S(1)} collective-permute-done((f32[256,128]{1,0:T(8,128)S(1)}, f32[256,128]{1,0:T(8,128)S(1)}, u32[]{:S(2)}, u32[]{:S(2)}) %collective-permute-start.44) | collective-permute-done | bytes 131104 | tf_op jit(solution)/shard_map/mid_upper/ppermute | solution.py:494
  88.5 4.4 %collective-permute-done.45.refs_1_ = f32[256,128]{1,0:T(8,128)S(1)} collective-permute-done((f32[256,128]{1,0:T(8,128)S(1)}, f32[256,128]{1,0:T(8,128)S(1)}, u32[]{:S(2)}, u32[]{:S(2)}) %collective-permute-start.45) | collective-permute-done | bytes 131104 | tf_op jit(solution)/shard_map/mid_upper/ppermute | solution.py:494
  95.0 1.4 %collective-permute-start.47 = (f32[64,128]{1,0:T(8,128)S(1)}, f32[64,128]{1,0:T(8,128)S(1)}, u32[]{:S(2)}, u32[]{:S(2)}) collective-permute-start(f32[64,128]{1,0:T(8,128)S(1)} %mid_upper.15.mine), channel_id=1, source_target_pairs={{0,8},{8,0},{16,24},{24,16},{1,9},{9,1},{17,25},{25,17},{2,10},{10... | collective-permute-start | bytes 98312 | tf_op jit(solution)/shard_map/leaf_upper/ppermute | solution.py:120
  101.4 2.4 %collective-permute-start.50 = (f32[64,128]{1,0:T(8,128)S(1)}, f32[64,128]{1,0:T(8,128)S(1)}, u32[]{:S(2)}, u32[]{:S(2)}) collective-permute-start(f32[64,128]{1,0:T(8,128)S(1)} %mid_upper.15.mine), channel_id=1, source_target_pairs={{0,16},{8,24},{16,0},{24,8},{1,17},{9,25},{17,1},{25,9},{2,18},{10... | collective-permute-start | bytes 98312 | tf_op jit(solution)/shard_map/leaf_upper/ppermute | solution.py:120
  103.8 2.0 %collective-permute-done.49.refs_1_ = f32[256,128]{1,0:T(8,128)S(1)} collective-permute-done((f32[256,128]{1,0:T(8,128)S(1)}, f32[256,128]{1,0:T(8,128)S(1)}, u32[]{:S(2)}, u32[]{:S(2)}) %collective-permute-start.49) | collective-permute-done | bytes 131104 | tf_op jit(solution)/shard_map/leaf_upper/ppermute | solution.py:494
  106.2 1.5 %collective-permute-start.51 = (f32[256,128]{1,0:T(8,128)S(1)}, f32[256,128]{1,0:T(8,128)S(1)}, u32[]{:S(2)}, u32[]{:S(2)}) collective-permute-start(f32[256,128]{1,0:T(8,128)S(1)} %leaf_upper.11.refs_0_), channel_id=1, source_target_pairs={{0,4},{1,3},{2,6},{3,1},{4,0},{5,7},{6,2},{7,5},{8,12},{9,11},{10,... | collective-permute-start | bytes 393224 | tf_op jit(solution)/shard_map/leaf_upper/ppermute | solution.py:494
  108.8 2.4 %collective-permute-done.51.refs_1_ = f32[256,128]{1,0:T(8,128)S(1)} collective-permute-done((f32[256,128]{1,0:T(8,128)S(1)}, f32[256,128]{1,0:T(8,128)S(1)}, u32[]{:S(2)}, u32[]{:S(2)}) %collective-permute-start.51) | collective-permute-done | bytes 131104 | tf_op jit(solution)/shard_map/leaf_upper/ppermute | solution.py:494
  (138 shorter events, 46.4 us)
Async XLA Ops:
  1.7 4.8 %collective-permute-start = (f32[32,128]{1,0:T(8,128)S(1)}, f32[32,128]{1,0:T(8,128)S(1)}, u32[]{:S(2)}, u32[]{:S(2)}) collective-permute-start(f32[32,128]{1,0:T(8,128)S(1)} %get-tuple-element.69), channel_id=1, source_target_pairs={{0,8},{8,0},{16,24},{24,16},{1,9},{9,1},{17,25},{25,17},{2,10},{10... | collective-permute-start | bytes 49160 | tf_op jit(solution)/shard_map/right_hand_sides/ppermute | solution.py:120
  6.5 4.7 %collective-permute-start.1 = (f32[32,128]{1,0:T(8,128)S(1)}, f32[32,128]{1,0:T(8,128)S(1)}, u32[]{:S(2)}, u32[]{:S(2)}) collective-permute-start(f32[32,128]{1,0:T(8,128)S(1)} %right_hand_sides.6), channel_id=1, source_target_pairs={{0,16},{8,24},{16,0},{24,8},{1,17},{9,25},{17,1},{25,9},{2,18},{10... | collective-permute-start | bytes 49160 | tf_op jit(solution)/shard_map/right_hand_sides/ppermute | solution.py:120
  11.4 4.9 %collective-permute-start.4 = (f32[72,128]{1,0:T(8,128)S(1)}, f32[72,128]{1,0:T(8,128)S(1)}, u32[]{:S(2)}, u32[]{:S(2)}) collective-permute-start(f32[72,128]{1,0:T(8,128)S(1)} %right_hand_sides.7.refs_0_), channel_id=1, source_target_pairs={{0,6},{1,7},{2,4},{3,5},{4,2},{5,3},{6,0},{7,1},{8,14},{9,15},{10,... | collective-permute-start | bytes 110600 | tf_op jit(solution)/shard_map/leaf_lower/ppermute | solution.py:120
  14.3 4.0 %collective-permute-start.5 = (f32[72,128]{1,0:T(8,128)S(1)}, f32[72,128]{1,0:T(8,128)S(1)}, u32[]{:S(2)}, u32[]{:S(2)}) collective-permute-start(f32[72,128]{1,0:T(8,128)S(1)} %right_hand_sides.7.refs_0_), channel_id=1, source_target_pairs={{0,2},{1,3},{2,0},{3,1},{4,6},{5,7},{6,4},{7,5},{8,10},{9,11},{10,... | collective-permute-start | bytes 110600 | tf_op jit(solution)/shard_map/leaf_lower/ppermute | solution.py:120
  14.8 4.0 %collective-permute-start.3 = (f32[72,128]{1,0:T(8,128)S(1)}, f32[72,128]{1,0:T(8,128)S(1)}, u32[]{:S(2)}, u32[]{:S(2)}) collective-permute-start(f32[72,128]{1,0:T(8,128)S(1)} %right_hand_sides.7.refs_0_), channel_id=1, source_target_pairs={{0,4},{1,5},{2,6},{3,7},{4,0},{5,1},{6,2},{7,3},{8,12},{9,13},{10,... | collective-permute-start | bytes 110600 | tf_op jit(solution)/shard_map/leaf_lower/ppermute | solution.py:120
  20.9 5.1 %collective-permute-start.10 = (f32[64,128]{1,0:T(8,128)S(1)}, f32[64,128]{1,0:T(8,128)S(1)}, u32[]{:S(2)}, u32[]{:S(2)}) collective-permute-start(f32[64,128]{1,0:T(8,128)S(1)} %leaf_lower.5.mine.refs_0_), channel_id=1, source_target_pairs={{0,6},{1,7},{2,4},{3,5},{4,2},{5,3},{6,0},{7,1},{8,14},{9,15},{10,... | collective-permute-start | bytes 98312 | tf_op jit(solution)/shard_map/mid_lower/ppermute | solution.py:120
  22.3 3.9 %collective-permute-start.9 = (f32[64,128]{1,0:T(8,128)S(1)}, f32[64,128]{1,0:T(8,128)S(1)}, u32[]{:S(2)}, u32[]{:S(2)}) collective-permute-start(f32[64,128]{1,0:T(8,128)S(1)} %leaf_lower.5.mine.refs_0_), channel_id=1, source_target_pairs={{0,2},{1,3},{2,0},{3,1},{4,6},{5,7},{6,4},{7,5},{8,10},{9,11},{10,... | collective-permute-start | bytes 98312 | tf_op jit(solution)/shard_map/mid_lower/ppermute | solution.py:120
  22.7 3.9 %collective-permute-start.12 = (f32[64,128]{1,0:T(8,128)S(1)}, f32[64,128]{1,0:T(8,128)S(1)}, u32[]{:S(2)}, u32[]{:S(2)}) collective-permute-start(f32[64,128]{1,0:T(8,128)S(1)} %leaf_lower.5.mine.refs_0_), channel_id=1, source_target_pairs={{0,4},{1,5},{2,6},{3,7},{4,0},{5,1},{6,2},{7,3},{8,12},{9,13},{10,... | collective-permute-start | bytes 98312 | tf_op jit(solution)/shard_map/mid_lower/ppermute | solution.py:120
  28.4 4.0 %collective-permute-start.14 = (f32[64,128]{1,0:T(8,128)S(1)}, f32[64,128]{1,0:T(8,128)S(1)}, u32[]{:S(2)}, u32[]{:S(2)}) collective-permute-start(f32[64,128]{1,0:T(8,128)S(1)} %get-tuple-element.84), channel_id=1, source_target_pairs={{0,8},{8,0},{16,24},{24,16},{1,9},{9,1},{17,25},{25,17},{2,10},{10... | collective-permute-start | bytes 98312 | tf_op jit(solution)/shard_map/mid_lower/ppermute | solution.py:120
  32.4 5.2 %collective-permute-start.15 = (f32[64,128]{1,0:T(8,128)S(1)}, f32[64,128]{1,0:T(8,128)S(1)}, u32[]{:S(2)}, u32[]{:S(2)}) collective-permute-start(f32[64,128]{1,0:T(8,128)S(1)} %mid_lower.15.mine), channel_id=1, source_target_pairs={{0,1},{1,0},{2,3},{3,2},{4,5},{5,4},{6,7},{7,6},{8,9},{9,8},{10,11... | collective-permute-start | bytes 98312 | tf_op jit(solution)/shard_map/mid_lower/ppermute | solution.py:120
  32.4 6.8 %collective-permute-start.17 = (f32[64,128]{1,0:T(8,128)S(1)}, f32[64,128]{1,0:T(8,128)S(1)}, u32[]{:S(2)}, u32[]{:S(2)}) collective-permute-start(f32[64,128]{1,0:T(8,128)S(1)} %mid_lower.15.mine), channel_id=1, source_target_pairs={{0,6},{1,7},{2,4},{3,5},{4,2},{5,3},{6,0},{7,1},{8,14},{9,15},{10,... | collective-permute-start | bytes 98312 | tf_op jit(solution)/shard_map/mid_lower/ppermute | solution.py:120
  34.9 4.3 %collective-permute-start.16 = (f32[64,128]{1,0:T(8,128)S(1)}, f32[64,128]{1,0:T(8,128)S(1)}, u32[]{:S(2)}, u32[]{:S(2)}) collective-permute-start(f32[64,128]{1,0:T(8,128)S(1)} %mid_lower.15.mine), channel_id=1, source_target_pairs={{0,2},{1,3},{2,0},{3,1},{4,6},{5,7},{6,4},{7,5},{8,10},{9,11},{10,... | collective-permute-start | bytes 98312 | tf_op jit(solution)/shard_map/mid_lower/ppermute | solution.py:120
  35.5 5.5 %collective-permute-start.20 = (f32[128,128]{1,0:T(8,128)S(1)}, f32[128,128]{1,0:T(8,128)S(1)}, u32[]{:S(2)}, u32[]{:S(2)}) collective-permute-start(f32[128,128]{1,0:T(8,128)S(1)} %get-tuple-element.90), channel_id=1, source_target_pairs={{0,8},{8,0},{16,24},{24,16},{1,9},{9,1},{17,25},{25,17},{2,10},{10... | collective-permute-start | bytes 196616 | tf_op jit(solution)/shard_map/mid_lower/ppermute | solution.py:120
  37.0 3.9 %collective-permute-start.19 = (f32[64,128]{1,0:T(8,128)S(1)}, f32[64,128]{1,0:T(8,128)S(1)}, u32[]{:S(2)}, u32[]{:S(2)}) collective-permute-start(f32[64,128]{1,0:T(8,128)S(1)} %mid_lower.15.mine), channel_id=1, source_target_pairs={{0,4},{1,5},{2,6},{3,7},{4,0},{5,1},{6,2},{7,3},{8,12},{9,13},{10,... | collective-permute-start | bytes 98312 | tf_op jit(solution)/shard_map/mid_lower/ppermute | solution.py:120
  42.9 6.3 %collective-permute-start.23 = (f32[64,128]{1,0:T(8,128)S(1)}, f32[64,128]{1,0:T(8,128)S(1)}, u32[]{:S(2)}, u32[]{:S(2)}) collective-permute-start(f32[64,128]{1,0:T(8,128)S(1)} %mid_lower.19.mine.refs_0_), channel_id=1, source_target_pairs={{0,2},{1,3},{2,0},{3,1},{4,6},{5,7},{6,4},{7,5},{8,10},{9,11},{10,... | collective-permute-start | bytes 98312 | tf_op jit(solution)/shard_map/root_cut/ppermute | solution.py:120
  44.4 4.8 %collective-permute-start.24 = (f32[64,128]{1,0:T(8,128)S(1)}, f32[64,128]{1,0:T(8,128)S(1)}, u32[]{:S(2)}, u32[]{:S(2)}) collective-permute-start(f32[64,128]{1,0:T(8,128)S(1)} %mid_lower.19.mine.refs_0_), channel_id=1, source_target_pairs={{0,6},{1,7},{2,4},{3,5},{4,2},{5,3},{6,0},{7,1},{8,14},{9,15},{10,... | collective-permute-start | bytes 98312 | tf_op jit(solution)/shard_map/root_cut/ppermute | solution.py:120
  44.9 4.4 %collective-permute-start.26 = (f32[64,128]{1,0:T(8,128)S(1)}, f32[64,128]{1,0:T(8,128)S(1)}, u32[]{:S(2)}, u32[]{:S(2)}) collective-permute-start(f32[64,128]{1,0:T(8,128)S(1)} %mid_lower.19.mine.refs_0_), channel_id=1, source_target_pairs={{0,4},{1,5},{2,6},{3,7},{4,0},{5,1},{6,2},{7,3},{8,12},{9,13},{10,... | collective-permute-start | bytes 98312 | tf_op jit(solution)/shard_map/root_cut/ppermute | solution.py:120
  52.0 5.1 %collective-permute-start.28 = (f32[64,128]{1,0:T(8,128)S(1)}, f32[64,128]{1,0:T(8,128)S(1)}, u32[]{:S(2)}, u32[]{:S(2)}) collective-permute-start(f32[64,128]{1,0:T(8,128)S(1)} %get-tuple-element.97), channel_id=1, source_target_pairs={{0,16},{8,24},{16,0},{24,8},{1,17},{9,25},{17,1},{25,9},{2,18},{10... | collective-permute-start | bytes 98312 | tf_op jit(solution)/shard_map/root_cut/ppermute | solution.py:120
  57.1 5.4 %collective-permute-start.30 = (f32[64,128]{1,0:T(8,128)S(1)}, f32[64,128]{1,0:T(8,128)S(1)}, u32[]{:S(2)}, u32[]{:S(2)}) collective-permute-start(f32[64,128]{1,0:T(8,128)S(1)} %root_cut.13.mine), channel_id=1, source_target_pairs={{0,2},{1,3},{2,0},{3,1},{4,6},{5,7},{6,4},{7,5},{8,10},{9,11},{10,... | collective-permute-start | bytes 98312 | tf_op jit(solution)/shard_map/root_solve/ppermute | solution.py:120
  57.7 4.8 %collective-permute-start.31 = (f32[64,128]{1,0:T(8,128)S(1)}, f32[64,128]{1,0:T(8,128)S(1)}, u32[]{:S(2)}, u32[]{:S(2)}) collective-permute-start(f32[64,128]{1,0:T(8,128)S(1)} %root_cut.13.mine), channel_id=1, source_target_pairs={{0,6},{1,7},{2,4},{3,5},{4,2},{5,3},{6,0},{7,1},{8,14},{9,15},{10,... | collective-permute-start | bytes 98312 | tf_op jit(solution)/shard_map/root_solve/ppermute | solution.py:120
  66.1 6.3 %collective-permute-start.36 = (f32[64,128]{1,0:T(8,128)S(1)}, f32[64,128]{1,0:T(8,128)S(1)}, u32[]{:S(2)}, u32[]{:S(2)}) collective-permute-start(f32[64,128]{1,0:T(8,128)S(1)} %root_solve.11.mine), channel_id=1, source_target_pairs={{0,2},{1,3},{2,0},{3,1},{4,6},{5,7},{6,4},{7,5},{8,10},{9,11},{10,... | collective-permute-start | bytes 98312 | tf_op jit(solution)/shard_map/root_solve/ppermute | solution.py:120
  67.6 4.8 %collective-permute-start.37 = (f32[64,128]{1,0:T(8,128)S(1)}, f32[64,128]{1,0:T(8,128)S(1)}, u32[]{:S(2)}, u32[]{:S(2)}) collective-permute-start(f32[64,128]{1,0:T(8,128)S(1)} %root_solve.11.mine), channel_id=1, source_target_pairs={{0,6},{1,7},{2,4},{3,5},{4,2},{5,3},{6,0},{7,1},{8,14},{9,15},{10,... | collective-permute-start | bytes 98312 | tf_op jit(solution)/shard_map/root_solve/ppermute | solution.py:120
  68.8 3.9 %collective-permute-start.39 = (f32[64,128]{1,0:T(8,128)S(1)}, f32[64,128]{1,0:T(8,128)S(1)}, u32[]{:S(2)}, u32[]{:S(2)}) collective-permute-start(f32[64,128]{1,0:T(8,128)S(1)} %root_solve.11.mine), channel_id=1, source_target_pairs={{0,4},{1,5},{2,6},{3,7},{4,0},{5,1},{6,2},{7,3},{8,12},{9,13},{10,... | collective-permute-start | bytes 98312 | tf_op jit(solution)/shard_map/root_solve/ppermute | solution.py:120
  75.6 4.9 %collective-permute-start.41 = (f32[64,128]{1,0:T(8,128)S(1)}, f32[64,128]{1,0:T(8,128)S(1)}, u32[]{:S(2)}, u32[]{:S(2)}) collective-permute-start(f32[64,128]{1,0:T(8,128)S(1)} %root_solve.15.mine), channel_id=1, source_target_pairs={{0,16},{8,24},{16,0},{24,8},{1,17},{9,25},{17,1},{25,9},{2,18},{10... | collective-permute-start | bytes 98312 | tf_op jit(solution)/shard_map/mid_upper/ppermute | solution.py:120
  82.8 5.0 %collective-permute-start.44 = (f32[256,128]{1,0:T(8,128)S(1)}, f32[256,128]{1,0:T(8,128)S(1)}, u32[]{:S(2)}, u32[]{:S(2)}) collective-permute-start(f32[256,128]{1,0:T(8,128)S(1)} %mid_upper.11.refs_0_), channel_id=1, source_target_pairs={{0,2},{1,5},{2,0},{3,7},{4,6},{5,1},{6,4},{7,3},{8,10},{9,13},{10,... | collective-permute-start | bytes 393224 | tf_op jit(solution)/shard_map/mid_upper/ppermute | solution.py:494
  87.8 5.0 %collective-permute-start.45 = (f32[256,128]{1,0:T(8,128)S(1)}, f32[256,128]{1,0:T(8,128)S(1)}, u32[]{:S(2)}, u32[]{:S(2)}) collective-permute-start(f32[256,128]{1,0:T(8,128)S(1)} %mid_upper.12.refs_0_), channel_id=1, source_target_pairs={{0,4},{1,3},{2,6},{3,1},{4,0},{5,7},{6,2},{7,5},{8,12},{9,11},{10,... | collective-permute-start | bytes 393224 | tf_op jit(solution)/shard_map/mid_upper/ppermute | solution.py:494
  93.0 4.5 %collective-permute-start.42 = (f32[128,128]{1,0:T(8,128)S(1)}, f32[128,128]{1,0:T(8,128)S(1)}, u32[]{:S(2)}, u32[]{:S(2)}) collective-permute-start(f32[128,128]{1,0:T(8,128)S(1)} %get-tuple-element.115.mine.x_root), channel_id=1, source_target_pairs={{0,8},{8,0},{16,24},{24,16},{1,9},{9,1},{17,25},{25,17},{2,10},{10... | collective-permute-start | bytes 196616 | tf_op jit(solution)/shard_map/mid_upper/ppermute | solution.py:120
  95.0 4.0 %collective-permute-start.47 = (f32[64,128]{1,0:T(8,128)S(1)}, f32[64,128]{1,0:T(8,128)S(1)}, u32[]{:S(2)}, u32[]{:S(2)}) collective-permute-start(f32[64,128]{1,0:T(8,128)S(1)} %mid_upper.15.mine), channel_id=1, source_target_pairs={{0,8},{8,0},{16,24},{24,16},{1,9},{9,1},{17,25},{25,17},{2,10},{10... | collective-permute-start | bytes 98312 | tf_op jit(solution)/shard_map/leaf_upper/ppermute | solution.py:120
  100.8 5.0 %collective-permute-start.49 = (f32[256,128]{1,0:T(8,128)S(1)}, f32[256,128]{1,0:T(8,128)S(1)}, u32[]{:S(2)}, u32[]{:S(2)}) collective-permute-start(f32[256,128]{1,0:T(8,128)S(1)} %leaf_upper.10.refs_0_), channel_id=1, source_target_pairs={{0,2},{1,5},{2,0},{3,7},{4,6},{5,1},{6,4},{7,3},{8,10},{9,13},{10,... | collective-permute-start | bytes 393224 | tf_op jit(solution)/shard_map/leaf_upper/ppermute | solution.py:494
  101.4 4.8 %collective-permute-start.50 = (f32[64,128]{1,0:T(8,128)S(1)}, f32[64,128]{1,0:T(8,128)S(1)}, u32[]{:S(2)}, u32[]{:S(2)}) collective-permute-start(f32[64,128]{1,0:T(8,128)S(1)} %mid_upper.15.mine), channel_id=1, source_target_pairs={{0,16},{8,24},{16,0},{24,8},{1,17},{9,25},{17,1},{25,9},{2,18},{10... | collective-permute-start | bytes 98312 | tf_op jit(solution)/shard_map/leaf_upper/ppermute | solution.py:120
  106.2 5.0 %collective-permute-start.51 = (f32[256,128]{1,0:T(8,128)S(1)}, f32[256,128]{1,0:T(8,128)S(1)}, u32[]{:S(2)}, u32[]{:S(2)}) collective-permute-start(f32[256,128]{1,0:T(8,128)S(1)} %leaf_upper.11.refs_0_), channel_id=1, source_target_pairs={{0,4},{1,3},{2,6},{3,1},{4,0},{5,7},{6,2},{7,5},{8,12},{9,11},{10,... | collective-permute-start | bytes 393224 | tf_op jit(solution)/shard_map/leaf_upper/ppermute | solution.py:494
  107.7 3.9 %collective-permute-start.52 = (f32[64,128]{1,0:T(8,128)S(1)}, f32[64,128]{1,0:T(8,128)S(1)}, u32[]{:S(2)}, u32[]{:S(2)}) collective-permute-start(f32[64,128]{1,0:T(8,128)S(1)} %collective-permute-done.50.far), channel_id=1, source_target_pairs={{0,8},{8,0},{16,24},{24,16},{1,9},{9,1},{17,25},{25,17},{2,10},{10... | collective-permute-start | bytes 98312 | tf_op jit(solution)/shard_map/leaf_upper/ppermute | solution.py:120
  (29 other events, 104.5 us)

commit v16 on v15

--- a/solution.py
+++ b/solution.py
@@ -128,7 +128,7 @@
 
 
 def hops(fronts):
-    return [2, 6, 4] if fronts == 8 else list(range(2, fronts, 2))
+    return [6, 2, 4] if fronts == 8 else list(range(2, fronts, 2))
 
 
 def gather_front(x, meanwhile=None, others=()):
@@ -136,7 +136,7 @@
     *near, last = [swap("front", x, k) for k in hops(fronts)]
     own = swap("front", x, 1)
     extra = tuple(meanwhile((own,))) if meanwhile else ()
-    (both,) = kernel(stack, [(len(near) * x.shape[0], LANES)], *near[:-1], after(near[-1], *extra))
+    (both,) = kernel(stack, [(len(near) * x.shape[0], LANES)], after(near[0], *extra, *others), *near[1:])
     last = after(last, *extra, *others)
     return [x, own, last, *near[::-1], swap("front", last, 1), swap("front", both, 1)], extra
 

time: 114 us -> 113 us (level)
  waiting for transfers between devices: 39.8 us -> 38.1 us
    ppermute x4, starting transfers between devices: 3.29 us -> 4.61 us  [sum_front(): lax.ppermute(total, 'front', pairs)]
    ppermute x50, starting transfers between devices: 43.1 us -> 41.9 us  [swap(): return lax.ppermute(x, axis, [(i, i ^ k) for i in range(size)])]
  transfers between devices with their start and end apart: 54 -> 54, of which waited for: 34 -> 37; matrix products, arithmetic and copies ran while one was open for 0% -> 0% of each run, Pallas kernels for 17% -> 17%
where the time goes in v16:
time: 113 us; the launch traced here: 112 us
  starting transfers between devices  46.6 us (41%)
  waiting for transfers between devices  38.1 us (34%)
  Pallas kernels  26.6 us (24%)
    ppermute x50, starting transfers between devices, swap(): return lax.ppermute(x, axis, [(i, i ^ k) for i in range(size)])  41.9 us
    pallas_call x48, Pallas kernels, kernel(): pl.pallas_call(fn, out_shape=[jax.ShapeDtypeStruct(*o) for o in outs], in...  26.6 us
    ppermute x50, waiting for transfers between devices, swap(): return lax.ppermute(x, axis, [(i, i ^ k) for i in range(size)])  25.8 us
    ppermute x4, waiting for transfers between devices, sum_front(): lax.ppermute(total, 'front', pairs)  12.3 us
    ppermute x4, starting transfers between devices, sum_front(): lax.ppermute(total, 'front', pairs)  4.61 us
  transfers between devices with their start and end apart: 54, of which 37 were waited for; matrix products, arithmetic and copies ran while one was open for 0% of the time, Pallas kernels for 17%

profile of v16, /device:TPU:0, one launch (start us, length us, event | category | flops | bytes accessed | tf_op | source)
XLA Modules:
  0.0 112.3 jit_solution(9248831280037544188)
XLA Ops:
  1.7 3.1 %collective-permute-start = (f32[32,128]{1,0:T(8,128)S(1)}, f32[32,128]{1,0:T(8,128)S(1)}, u32[]{:S(2)}, u32[]{:S(2)}) collective-permute-start(f32[32,128]{1,0:T(8,128)S(1)} %get-tuple-element.69), channel_id=1, source_target_pairs={{0,8},{8,0},{16,24},{24,16},{1,9},{9,1},{17,25},{25,17},{2,10},{10... | collective-permute-start | bytes 49160 | tf_op jit(solution)/shard_map/right_hand_sides/ppermute | solution.py:120
  4.8 1.7 %collective-permute-done.came.near = f32[32,128]{1,0:T(8,128)S(1)} collective-permute-done((f32[32,128]{1,0:T(8,128)S(1)}, f32[32,128]{1,0:T(8,128)S(1)}, u32[]{:S(2)}, u32[]{:S(2)}) %collective-permute-start) | collective-permute-done | bytes 16416 | tf_op jit(solution)/shard_map/right_hand_sides/ppermute | solution.py:120
  6.5 3.0 %collective-permute-start.1 = (f32[32,128]{1,0:T(8,128)S(1)}, f32[32,128]{1,0:T(8,128)S(1)}, u32[]{:S(2)}, u32[]{:S(2)}) collective-permute-start(f32[32,128]{1,0:T(8,128)S(1)} %right_hand_sides.6), channel_id=1, source_target_pairs={{0,16},{8,24},{16,0},{24,8},{1,17},{9,25},{17,1},{25,9},{2,18},{10... | collective-permute-start | bytes 49160 | tf_op jit(solution)/shard_map/right_hand_sides/ppermute | solution.py:120
  11.4 2.8 %collective-permute-start.5 = (f32[72,128]{1,0:T(8,128)S(1)}, f32[72,128]{1,0:T(8,128)S(1)}, u32[]{:S(2)}, u32[]{:S(2)}) collective-permute-start(f32[72,128]{1,0:T(8,128)S(1)} %right_hand_sides.7.refs_0_), channel_id=1, source_target_pairs={{0,6},{1,7},{2,4},{3,5},{4,2},{5,3},{6,0},{7,1},{8,14},{9,15},{10,... | collective-permute-start | bytes 110600 | tf_op jit(solution)/shard_map/leaf_lower/ppermute | solution.py:120
  15.0 1.3 %leaf_lower.3 = (bf16[128,1024]{1,0:T(8,128)(2,1)S(1)}, bf16[256,1024]{1,0:T(8,128)(2,1)S(1)}) custom-call(f32[2,1,64,512]{3,2,1,0:T(8,128)} %refs_0_, f32[2,1,128,512]{3,2,1,0:T(8,128)} %refs_1_.4), custom_call_target="tpu_custom_call" | custom-call | flops 98304000 | bytes 140434 | tf_op jit(solution)/shard_map/leaf_lower/pallas_call | solution.py:158
  16.3 1.9 %collective-permute-done.4.refs_1_.refs_3_ = f32[72,128]{1,0:T(8,128)S(1)} collective-permute-done((f32[72,128]{1,0:T(8,128)S(1)}, f32[72,128]{1,0:T(8,128)S(1)}, u32[]{:S(2)}, u32[]{:S(2)}) %collective-permute-start.4) | collective-permute-done | bytes 36896 | tf_op jit(solution)/shard_map/leaf_lower/ppermute | solution.py:120
  20.9 1.4 %collective-permute-start.9 = (f32[64,128]{1,0:T(8,128)S(1)}, f32[64,128]{1,0:T(8,128)S(1)}, u32[]{:S(2)}, u32[]{:S(2)}) collective-permute-start(f32[64,128]{1,0:T(8,128)S(1)} %leaf_lower.5.mine.refs_0_), channel_id=1, source_target_pairs={{0,6},{1,7},{2,4},{3,5},{4,2},{5,3},{6,0},{7,1},{8,14},{9,15},{10,... | collective-permute-start | bytes 98312 | tf_op jit(solution)/shard_map/mid_lower/ppermute | solution.py:120
  22.7 1.7 %collective-permute-start.12 = (f32[64,128]{1,0:T(8,128)S(1)}, f32[64,128]{1,0:T(8,128)S(1)}, u32[]{:S(2)}, u32[]{:S(2)}) collective-permute-start(f32[64,128]{1,0:T(8,128)S(1)} %leaf_lower.5.mine.refs_0_), channel_id=1, source_target_pairs={{0,4},{1,5},{2,6},{3,7},{4,0},{5,1},{6,2},{7,3},{8,12},{9,13},{10,... | collective-permute-start | bytes 98312 | tf_op jit(solution)/shard_map/mid_lower/ppermute | solution.py:120
  24.4 1.6 %mid_lower.10 = (bf16[512,1024]{1,0:T(8,128)(2,1)S(1)}, bf16[256,2048]{1,0:T(8,128)(2,1)S(1)}) custom-call(f32[2,1,256,512]{3,2,1,0:T(8,128)} %refs_0_.1, f32[2,2,128,1024]{3,2,1,0:T(8,128)} %refs_1_.5), custom_call_target="tpu_custom_call" | custom-call | flops 262144000 | bytes 374491 | tf_op jit(solution)/shard_map/mid_lower/pallas_call | solution.py:158
  28.4 1.7 %collective-permute-start.14 = (f32[64,128]{1,0:T(8,128)S(1)}, f32[64,128]{1,0:T(8,128)S(1)}, u32[]{:S(2)}, u32[]{:S(2)}) collective-permute-start(f32[64,128]{1,0:T(8,128)S(1)} %get-tuple-element.84), channel_id=1, source_target_pairs={{0,8},{8,0},{16,24},{24,16},{1,9},{9,1},{17,25},{25,17},{2,10},{10... | collective-permute-start | bytes 98312 | tf_op jit(solution)/shard_map/mid_lower/ppermute | solution.py:120
  32.4 2.6 %collective-permute-start.16 = (f32[64,128]{1,0:T(8,128)S(1)}, f32[64,128]{1,0:T(8,128)S(1)}, u32[]{:S(2)}, u32[]{:S(2)}) collective-permute-start(f32[64,128]{1,0:T(8,128)S(1)} %mid_lower.15.mine), channel_id=1, source_target_pairs={{0,6},{1,7},{2,4},{3,5},{4,2},{5,3},{6,0},{7,1},{8,14},{9,15},{10,... | collective-permute-start | bytes 98312 | tf_op jit(solution)/shard_map/mid_lower/ppermute | solution.py:120
  36.0 1.6 %mid_lower.16.matrix = bf16[512,2048]{1,0:T(8,128)(2,1)S(1)} custom-call(f32[2,2,256,1024]{3,2,1,0:T(8,128)} %refs_0_.2), custom_call_target="tpu_custom_call" | custom-call | flops 262144000 | bytes 374491 | tf_op jit(solution)/shard_map/mid_lower/pallas_call | solution.py:158
  37.7 1.3 %collective-permute-done.17.refs_1_ = f32[64,128]{1,0:T(8,128)S(1)} collective-permute-done((f32[64,128]{1,0:T(8,128)S(1)}, f32[64,128]{1,0:T(8,128)S(1)}, u32[]{:S(2)}, u32[]{:S(2)}) %collective-permute-start.17) | collective-permute-done | bytes 32800 | tf_op jit(solution)/shard_map/mid_lower/ppermute | solution.py:120
  41.5 1.3 %collective-permute-start.23 = (f32[64,128]{1,0:T(8,128)S(1)}, f32[64,128]{1,0:T(8,128)S(1)}, u32[]{:S(2)}, u32[]{:S(2)}) collective-permute-start(f32[64,128]{1,0:T(8,128)S(1)} %mid_lower.19.mine.refs_0_), channel_id=1, source_target_pairs={{0,6},{1,7},{2,4},{3,5},{4,2},{5,3},{6,0},{7,1},{8,14},{9,15},{10,... | collective-permute-start | bytes 98312 | tf_op jit(solution)/shard_map/root_cut/ppermute | solution.py:120
  43.5 1.5 %collective-permute-start.26 = (f32[64,128]{1,0:T(8,128)S(1)}, f32[64,128]{1,0:T(8,128)S(1)}, u32[]{:S(2)}, u32[]{:S(2)}) collective-permute-start(f32[64,128]{1,0:T(8,128)S(1)} %mid_lower.19.mine.refs_0_), channel_id=1, source_target_pairs={{0,4},{1,5},{2,6},{3,7},{4,0},{5,1},{6,2},{7,3},{8,12},{9,13},{10,... | collective-permute-start | bytes 98312 | tf_op jit(solution)/shard_map/root_cut/ppermute | solution.py:120
  49.6 2.7 %collective-permute-start.28 = (f32[64,128]{1,0:T(8,128)S(1)}, f32[64,128]{1,0:T(8,128)S(1)}, u32[]{:S(2)}, u32[]{:S(2)}) collective-permute-start(f32[64,128]{1,0:T(8,128)S(1)} %get-tuple-element.97), channel_id=1, source_target_pairs={{0,16},{8,24},{16,0},{24,8},{1,17},{9,25},{17,1},{25,9},{2,18},{10... | collective-permute-start | bytes 98312 | tf_op jit(solution)/shard_map/root_cut/ppermute | solution.py:120
  52.9 1.5 %collective-permute-done.28.refs_1_ = f32[64,128]{1,0:T(8,128)S(1)} collective-permute-done((f32[64,128]{1,0:T(8,128)S(1)}, f32[64,128]{1,0:T(8,128)S(1)}, u32[]{:S(2)}, u32[]{:S(2)}) %collective-permute-start.28) | collective-permute-done | bytes 32800 | tf_op jit(solution)/shard_map/root_cut/ppermute | solution.py:120
  54.5 2.1 %collective-permute-start.30 = (f32[64,128]{1,0:T(8,128)S(1)}, f32[64,128]{1,0:T(8,128)S(1)}, u32[]{:S(2)}, u32[]{:S(2)}) collective-permute-start(f32[64,128]{1,0:T(8,128)S(1)} %root_cut.13.mine), channel_id=1, source_target_pairs={{0,6},{1,7},{2,4},{3,5},{4,2},{5,3},{6,0},{7,1},{8,14},{9,15},{10,... | collective-permute-start | bytes 98312 | tf_op jit(solution)/shard_map/root_solve/ppermute | solution.py:120
  66.1 1.5 %collective-permute-start.39 = (f32[64,128]{1,0:T(8,128)S(1)}, f32[64,128]{1,0:T(8,128)S(1)}, u32[]{:S(2)}, u32[]{:S(2)}) collective-permute-start(f32[64,128]{1,0:T(8,128)S(1)} %root_solve.11.mine), channel_id=1, source_target_pairs={{0,4},{1,5},{2,6},{3,7},{4,0},{5,1},{6,2},{7,3},{8,12},{9,13},{10,... | collective-permute-start | bytes 98312 | tf_op jit(solution)/shard_map/root_solve/ppermute | solution.py:120
  67.5 1.4 %root_solve.12 = (bf16[2048,512]{1,0:T(8,128)(2,1)S(1)}, bf16[1024,256]{1,0:T(8,128)(2,1)S(1)}, bf16[128,1024]{1,0:T(8,128)(2,1)S(1)}) custom-call(f32[2,2,1024,256]{3,2,1,0:T(8,128)S(1)} %copy-done, f32[2,1,512,128]{3,2,1,0:T(8,128)S(1)} %copy-done.5, f32[2,1,64,512]{3,2,1,0:T(8,128)S(1)} %copy-done.6), custom_call_target="tpu_custom_call" | custom-call | flops 360448000 | bytes 514925 | tf_op jit(solution)/shard_map/root_solve/pallas_call | solution.py:158
  72.4 2.7 %collective-permute-start.41 = (f32[64,128]{1,0:T(8,128)S(1)}, f32[64,128]{1,0:T(8,128)S(1)}, u32[]{:S(2)}, u32[]{:S(2)}) collective-permute-start(f32[64,128]{1,0:T(8,128)S(1)} %root_solve.15.mine), channel_id=1, source_target_pairs={{0,16},{8,24},{16,0},{24,8},{1,17},{9,25},{17,1},{25,9},{2,18},{10... | collective-permute-start | bytes 98312 | tf_op jit(solution)/shard_map/mid_upper/ppermute | solution.py:120
  75.1 2.2 %collective-permute-done.41.other = f32[64,128]{1,0:T(8,128)S(1)} collective-permute-done((f32[64,128]{1,0:T(8,128)S(1)}, f32[64,128]{1,0:T(8,128)S(1)}, u32[]{:S(2)}, u32[]{:S(2)}) %collective-permute-start.41) | collective-permute-done | bytes 32800 | tf_op jit(solution)/shard_map/mid_upper/ppermute | solution.py:120
  80.6 4.0 %collective-permute-done.44.refs_1_ = f32[256,128]{1,0:T(8,128)S(1)} collective-permute-done((f32[256,128]{1,0:T(8,128)S(1)}, f32[256,128]{1,0:T(8,128)S(1)}, u32[]{:S(2)}, u32[]{:S(2)}) %collective-permute-start.44) | collective-permute-done | bytes 131104 | tf_op jit(solution)/shard_map/mid_upper/ppermute | solution.py:494
  84.6 1.3 %collective-permute-start.45 = (f32[256,128]{1,0:T(8,128)S(1)}, f32[256,128]{1,0:T(8,128)S(1)}, u32[]{:S(2)}, u32[]{:S(2)}) collective-permute-start(f32[256,128]{1,0:T(8,128)S(1)} %mid_upper.12.refs_0_), channel_id=1, source_target_pairs={{0,4},{1,3},{2,6},{3,1},{4,0},{5,7},{6,2},{7,5},{8,12},{9,11},{10,... | collective-permute-start | bytes 393224 | tf_op jit(solution)/shard_map/mid_upper/ppermute | solution.py:494
  85.9 3.8 %collective-permute-done.45.refs_1_ = f32[256,128]{1,0:T(8,128)S(1)} collective-permute-done((f32[256,128]{1,0:T(8,128)S(1)}, f32[256,128]{1,0:T(8,128)S(1)}, u32[]{:S(2)}, u32[]{:S(2)}) %collective-permute-start.45) | collective-permute-done | bytes 131104 | tf_op jit(solution)/shard_map/mid_upper/ppermute | solution.py:494
  89.7 1.9 %collective-permute-start.42 = (f32[128,128]{1,0:T(8,128)S(1)}, f32[128,128]{1,0:T(8,128)S(1)}, u32[]{:S(2)}, u32[]{:S(2)}) collective-permute-start(f32[128,128]{1,0:T(8,128)S(1)} %get-tuple-element.115.mine.x_root), channel_id=1, source_target_pairs={{0,8},{8,0},{16,24},{24,16},{1,9},{9,1},{17,25},{25,17},{2,10},{10... | collective-permute-start | bytes 196616 | tf_op jit(solution)/shard_map/mid_upper/ppermute | solution.py:120
  94.3 1.2 %mid_upper.9 = (f32[512,128]{1,0:T(8,128)S(1)}, f32[2,32,256]{2,1,0:T(8,128)}, f32[2,32,256]{2,1,0:T(8,128)}) custom-call(bf16[1024,512]{1,0:T(8,128)(2,1)S(1)} %get-tuple-element.109.matrix, f32[128,128]{1,0:T(8,128)S(1)} %get-tuple-element.115.mine.x_root, f32[128,128]{1,0:T(8,128)S(1)} %collective-permute-done.42.other), custom_call_target="tpu_custom_call" | custom-call | tf_op jit(solution)/shard_map/mid_upper/pallas_call | solution.py:158
  95.5 1.3 %collective-permute-done.47.other = f32[64,128]{1,0:T(8,128)S(1)} collective-permute-done((f32[64,128]{1,0:T(8,128)S(1)}, f32[64,128]{1,0:T(8,128)S(1)}, u32[]{:S(2)}, u32[]{:S(2)}) %collective-permute-start.47) | collective-permute-done | bytes 32800 | tf_op jit(solution)/shard_map/leaf_upper/ppermute | solution.py:120
  99.7 2.7 %collective-permute-start.50 = (f32[64,128]{1,0:T(8,128)S(1)}, f32[64,128]{1,0:T(8,128)S(1)}, u32[]{:S(2)}, u32[]{:S(2)}) collective-permute-start(f32[64,128]{1,0:T(8,128)S(1)} %mid_upper.15.mine), channel_id=1, source_target_pairs={{0,16},{8,24},{16,0},{24,8},{1,17},{9,25},{17,1},{25,9},{2,18},{10... | collective-permute-start | bytes 98312 | tf_op jit(solution)/shard_map/leaf_upper/ppermute | solution.py:120
  102.4 1.3 %collective-permute-done.49.refs_1_ = f32[256,128]{1,0:T(8,128)S(1)} collective-permute-done((f32[256,128]{1,0:T(8,128)S(1)}, f32[256,128]{1,0:T(8,128)S(1)}, u32[]{:S(2)}, u32[]{:S(2)}) %collective-permute-start.49) | collective-permute-done | bytes 131104 | tf_op jit(solution)/shard_map/leaf_upper/ppermute | solution.py:494
  104.9 1.2 %collective-permute-start.51 = (f32[256,128]{1,0:T(8,128)S(1)}, f32[256,128]{1,0:T(8,128)S(1)}, u32[]{:S(2)}, u32[]{:S(2)}) collective-permute-start(f32[256,128]{1,0:T(8,128)S(1)} %leaf_upper.11.refs_0_), channel_id=1, source_target_pairs={{0,4},{1,3},{2,6},{3,1},{4,0},{5,7},{6,2},{7,5},{8,12},{9,11},{10,... | collective-permute-start | bytes 393224 | tf_op jit(solution)/shard_map/leaf_upper/ppermute | solution.py:494
  106.6 3.3 %collective-permute-done.51.refs_1_ = f32[256,128]{1,0:T(8,128)S(1)} collective-permute-done((f32[256,128]{1,0:T(8,128)S(1)}, f32[256,128]{1,0:T(8,128)S(1)}, u32[]{:S(2)}, u32[]{:S(2)}) %collective-permute-start.51) | collective-permute-done | bytes 131104 | tf_op jit(solution)/shard_map/leaf_upper/ppermute | solution.py:494
  (138 shorter events, 46.7 us)
Async XLA Ops:
  1.7 4.8 %collective-permute-start = (f32[32,128]{1,0:T(8,128)S(1)}, f32[32,128]{1,0:T(8,128)S(1)}, u32[]{:S(2)}, u32[]{:S(2)}) collective-permute-start(f32[32,128]{1,0:T(8,128)S(1)} %get-tuple-element.69), channel_id=1, source_target_pairs={{0,8},{8,0},{16,24},{24,16},{1,9},{9,1},{17,25},{25,17},{2,10},{10... | collective-permute-start | bytes 49160 | tf_op jit(solution)/shard_map/right_hand_sides/ppermute | solution.py:120
  6.5 4.7 %collective-permute-start.1 = (f32[32,128]{1,0:T(8,128)S(1)}, f32[32,128]{1,0:T(8,128)S(1)}, u32[]{:S(2)}, u32[]{:S(2)}) collective-permute-start(f32[32,128]{1,0:T(8,128)S(1)} %right_hand_sides.6), channel_id=1, source_target_pairs={{0,16},{8,24},{16,0},{24,8},{1,17},{9,25},{17,1},{25,9},{2,18},{10... | collective-permute-start | bytes 49160 | tf_op jit(solution)/shard_map/right_hand_sides/ppermute | solution.py:120
  11.4 4.9 %collective-permute-start.5 = (f32[72,128]{1,0:T(8,128)S(1)}, f32[72,128]{1,0:T(8,128)S(1)}, u32[]{:S(2)}, u32[]{:S(2)}) collective-permute-start(f32[72,128]{1,0:T(8,128)S(1)} %right_hand_sides.7.refs_0_), channel_id=1, source_target_pairs={{0,6},{1,7},{2,4},{3,5},{4,2},{5,3},{6,0},{7,1},{8,14},{9,15},{10,... | collective-permute-start | bytes 110600 | tf_op jit(solution)/shard_map/leaf_lower/ppermute | solution.py:120
  14.3 4.0 %collective-permute-start.4 = (f32[72,128]{1,0:T(8,128)S(1)}, f32[72,128]{1,0:T(8,128)S(1)}, u32[]{:S(2)}, u32[]{:S(2)}) collective-permute-start(f32[72,128]{1,0:T(8,128)S(1)} %right_hand_sides.7.refs_0_), channel_id=1, source_target_pairs={{0,2},{1,3},{2,0},{3,1},{4,6},{5,7},{6,4},{7,5},{8,10},{9,11},{10,... | collective-permute-start | bytes 110600 | tf_op jit(solution)/shard_map/leaf_lower/ppermute | solution.py:120
  14.8 4.0 %collective-permute-start.3 = (f32[72,128]{1,0:T(8,128)S(1)}, f32[72,128]{1,0:T(8,128)S(1)}, u32[]{:S(2)}, u32[]{:S(2)}) collective-permute-start(f32[72,128]{1,0:T(8,128)S(1)} %right_hand_sides.7.refs_0_), channel_id=1, source_target_pairs={{0,4},{1,5},{2,6},{3,7},{4,0},{5,1},{6,2},{7,3},{8,12},{9,13},{10,... | collective-permute-start | bytes 110600 | tf_op jit(solution)/shard_map/leaf_lower/ppermute | solution.py:120
  20.9 5.1 %collective-permute-start.9 = (f32[64,128]{1,0:T(8,128)S(1)}, f32[64,128]{1,0:T(8,128)S(1)}, u32[]{:S(2)}, u32[]{:S(2)}) collective-permute-start(f32[64,128]{1,0:T(8,128)S(1)} %leaf_lower.5.mine.refs_0_), channel_id=1, source_target_pairs={{0,6},{1,7},{2,4},{3,5},{4,2},{5,3},{6,0},{7,1},{8,14},{9,15},{10,... | collective-permute-start | bytes 98312 | tf_op jit(solution)/shard_map/mid_lower/ppermute | solution.py:120
  22.3 3.9 %collective-permute-start.10 = (f32[64,128]{1,0:T(8,128)S(1)}, f32[64,128]{1,0:T(8,128)S(1)}, u32[]{:S(2)}, u32[]{:S(2)}) collective-permute-start(f32[64,128]{1,0:T(8,128)S(1)} %leaf_lower.5.mine.refs_0_), channel_id=1, source_target_pairs={{0,2},{1,3},{2,0},{3,1},{4,6},{5,7},{6,4},{7,5},{8,10},{9,11},{10,... | collective-permute-start | bytes 98312 | tf_op jit(solution)/shard_map/mid_lower/ppermute | solution.py:120
  22.7 3.9 %collective-permute-start.12 = (f32[64,128]{1,0:T(8,128)S(1)}, f32[64,128]{1,0:T(8,128)S(1)}, u32[]{:S(2)}, u32[]{:S(2)}) collective-permute-start(f32[64,128]{1,0:T(8,128)S(1)} %leaf_lower.5.mine.refs_0_), channel_id=1, source_target_pairs={{0,4},{1,5},{2,6},{3,7},{4,0},{5,1},{6,2},{7,3},{8,12},{9,13},{10,... | collective-permute-start | bytes 98312 | tf_op jit(solution)/shard_map/mid_lower/ppermute | solution.py:120
  28.4 4.0 %collective-permute-start.14 = (f32[64,128]{1,0:T(8,128)S(1)}, f32[64,128]{1,0:T(8,128)S(1)}, u32[]{:S(2)}, u32[]{:S(2)}) collective-permute-start(f32[64,128]{1,0:T(8,128)S(1)} %get-tuple-element.84), channel_id=1, source_target_pairs={{0,8},{8,0},{16,24},{24,16},{1,9},{9,1},{17,25},{25,17},{2,10},{10... | collective-permute-start | bytes 98312 | tf_op jit(solution)/shard_map/mid_lower/ppermute | solution.py:120
  30.8 6.9 %collective-permute-start.18 = (f32[128,128]{1,0:T(8,128)S(1)}, f32[128,128]{1,0:T(8,128)S(1)}, u32[]{:S(2)}, u32[]{:S(2)}) collective-permute-start(f32[128,128]{1,0:T(8,128)S(1)} %get-tuple-element.89), channel_id=1, source_target_pairs={{0,8},{8,0},{16,24},{24,16},{1,9},{9,1},{17,25},{25,17},{2,10},{10... | collective-permute-start | bytes 196616 | tf_op jit(solution)/shard_map/mid_lower/ppermute | solution.py:120
  32.4 5.2 %collective-permute-start.16 = (f32[64,128]{1,0:T(8,128)S(1)}, f32[64,128]{1,0:T(8,128)S(1)}, u32[]{:S(2)}, u32[]{:S(2)}) collective-permute-start(f32[64,128]{1,0:T(8,128)S(1)} %mid_lower.15.mine), channel_id=1, source_target_pairs={{0,6},{1,7},{2,4},{3,5},{4,2},{5,3},{6,0},{7,1},{8,14},{9,15},{10,... | collective-permute-start | bytes 98312 | tf_op jit(solution)/shard_map/mid_lower/ppermute | solution.py:120
  35.0 3.9 %collective-permute-start.17 = (f32[64,128]{1,0:T(8,128)S(1)}, f32[64,128]{1,0:T(8,128)S(1)}, u32[]{:S(2)}, u32[]{:S(2)}) collective-permute-start(f32[64,128]{1,0:T(8,128)S(1)} %mid_lower.15.mine), channel_id=1, source_target_pairs={{0,2},{1,3},{2,0},{3,1},{4,6},{5,7},{6,4},{7,5},{8,10},{9,11},{10,... | collective-permute-start | bytes 98312 | tf_op jit(solution)/shard_map/mid_lower/ppermute | solution.py:120
  35.5 3.9 %collective-permute-start.20 = (f32[64,128]{1,0:T(8,128)S(1)}, f32[64,128]{1,0:T(8,128)S(1)}, u32[]{:S(2)}, u32[]{:S(2)}) collective-permute-start(f32[64,128]{1,0:T(8,128)S(1)} %mid_lower.15.mine), channel_id=1, source_target_pairs={{0,4},{1,5},{2,6},{3,7},{4,0},{5,1},{6,2},{7,3},{8,12},{9,13},{10,... | collective-permute-start | bytes 98312 | tf_op jit(solution)/shard_map/mid_lower/ppermute | solution.py:120
  41.5 4.9 %collective-permute-start.23 = (f32[64,128]{1,0:T(8,128)S(1)}, f32[64,128]{1,0:T(8,128)S(1)}, u32[]{:S(2)}, u32[]{:S(2)}) collective-permute-start(f32[64,128]{1,0:T(8,128)S(1)} %mid_lower.19.mine.refs_0_), channel_id=1, source_target_pairs={{0,6},{1,7},{2,4},{3,5},{4,2},{5,3},{6,0},{7,1},{8,14},{9,15},{10,... | collective-permute-start | bytes 98312 | tf_op jit(solution)/shard_map/root_cut/ppermute | solution.py:120
  42.9 3.9 %collective-permute-start.24 = (f32[64,128]{1,0:T(8,128)S(1)}, f32[64,128]{1,0:T(8,128)S(1)}, u32[]{:S(2)}, u32[]{:S(2)}) collective-permute-start(f32[64,128]{1,0:T(8,128)S(1)} %mid_lower.19.mine.refs_0_), channel_id=1, source_target_pairs={{0,2},{1,3},{2,0},{3,1},{4,6},{5,7},{6,4},{7,5},{8,10},{9,11},{10,... | collective-permute-start | bytes 98312 | tf_op jit(solution)/shard_map/root_cut/ppermute | solution.py:120
  43.5 3.9 %collective-permute-start.26 = (f32[64,128]{1,0:T(8,128)S(1)}, f32[64,128]{1,0:T(8,128)S(1)}, u32[]{:S(2)}, u32[]{:S(2)}) collective-permute-start(f32[64,128]{1,0:T(8,128)S(1)} %mid_lower.19.mine.refs_0_), channel_id=1, source_target_pairs={{0,4},{1,5},{2,6},{3,7},{4,0},{5,1},{6,2},{7,3},{8,12},{9,13},{10,... | collective-permute-start | bytes 98312 | tf_op jit(solution)/shard_map/root_cut/ppermute | solution.py:120
  49.6 4.9 %collective-permute-start.28 = (f32[64,128]{1,0:T(8,128)S(1)}, f32[64,128]{1,0:T(8,128)S(1)}, u32[]{:S(2)}, u32[]{:S(2)}) collective-permute-start(f32[64,128]{1,0:T(8,128)S(1)} %get-tuple-element.97), channel_id=1, source_target_pairs={{0,16},{8,24},{16,0},{24,8},{1,17},{9,25},{17,1},{25,9},{2,18},{10... | collective-permute-start | bytes 98312 | tf_op jit(solution)/shard_map/root_cut/ppermute | solution.py:120
  54.5 4.9 %collective-permute-start.30 = (f32[64,128]{1,0:T(8,128)S(1)}, f32[64,128]{1,0:T(8,128)S(1)}, u32[]{:S(2)}, u32[]{:S(2)}) collective-permute-start(f32[64,128]{1,0:T(8,128)S(1)} %root_cut.13.mine), channel_id=1, source_target_pairs={{0,6},{1,7},{2,4},{3,5},{4,2},{5,3},{6,0},{7,1},{8,14},{9,15},{10,... | collective-permute-start | bytes 98312 | tf_op jit(solution)/shard_map/root_solve/ppermute | solution.py:120
  56.6 3.9 %collective-permute-start.31 = (f32[64,128]{1,0:T(8,128)S(1)}, f32[64,128]{1,0:T(8,128)S(1)}, u32[]{:S(2)}, u32[]{:S(2)}) collective-permute-start(f32[64,128]{1,0:T(8,128)S(1)} %root_cut.13.mine), channel_id=1, source_target_pairs={{0,2},{1,3},{2,0},{3,1},{4,6},{5,7},{6,4},{7,5},{8,10},{9,11},{10,... | collective-permute-start | bytes 98312 | tf_op jit(solution)/shard_map/root_solve/ppermute | solution.py:120
  57.5 3.9 %collective-permute-start.33 = (f32[64,128]{1,0:T(8,128)S(1)}, f32[64,128]{1,0:T(8,128)S(1)}, u32[]{:S(2)}, u32[]{:S(2)}) collective-permute-start(f32[64,128]{1,0:T(8,128)S(1)} %root_cut.13.mine), channel_id=1, source_target_pairs={{0,4},{1,5},{2,6},{3,7},{4,0},{5,1},{6,2},{7,3},{8,12},{9,13},{10,... | collective-permute-start | bytes 98312 | tf_op jit(solution)/shard_map/root_solve/ppermute | solution.py:120
  64.0 5.1 %collective-permute-start.36 = (f32[64,128]{1,0:T(8,128)S(1)}, f32[64,128]{1,0:T(8,128)S(1)}, u32[]{:S(2)}, u32[]{:S(2)}) collective-permute-start(f32[64,128]{1,0:T(8,128)S(1)} %root_solve.11.mine), channel_id=1, source_target_pairs={{0,6},{1,7},{2,4},{3,5},{4,2},{5,3},{6,0},{7,1},{8,14},{9,15},{10,... | collective-permute-start | bytes 98312 | tf_op jit(solution)/shard_map/root_solve/ppermute | solution.py:120
  65.2 3.9 %collective-permute-start.37 = (f32[64,128]{1,0:T(8,128)S(1)}, f32[64,128]{1,0:T(8,128)S(1)}, u32[]{:S(2)}, u32[]{:S(2)}) collective-permute-start(f32[64,128]{1,0:T(8,128)S(1)} %root_solve.11.mine), channel_id=1, source_target_pairs={{0,2},{1,3},{2,0},{3,1},{4,6},{5,7},{6,4},{7,5},{8,10},{9,11},{10,... | collective-permute-start | bytes 98312 | tf_op jit(solution)/shard_map/root_solve/ppermute | solution.py:120
  66.1 3.9 %collective-permute-start.39 = (f32[64,128]{1,0:T(8,128)S(1)}, f32[64,128]{1,0:T(8,128)S(1)}, u32[]{:S(2)}, u32[]{:S(2)}) collective-permute-start(f32[64,128]{1,0:T(8,128)S(1)} %root_solve.11.mine), channel_id=1, source_target_pairs={{0,4},{1,5},{2,6},{3,7},{4,0},{5,1},{6,2},{7,3},{8,12},{9,13},{10,... | collective-permute-start | bytes 98312 | tf_op jit(solution)/shard_map/root_solve/ppermute | solution.py:120
  72.4 4.9 %collective-permute-start.41 = (f32[64,128]{1,0:T(8,128)S(1)}, f32[64,128]{1,0:T(8,128)S(1)}, u32[]{:S(2)}, u32[]{:S(2)}) collective-permute-start(f32[64,128]{1,0:T(8,128)S(1)} %root_solve.15.mine), channel_id=1, source_target_pairs={{0,16},{8,24},{16,0},{24,8},{1,17},{9,25},{17,1},{25,9},{2,18},{10... | collective-permute-start | bytes 98312 | tf_op jit(solution)/shard_map/mid_upper/ppermute | solution.py:120
  79.6 5.0 %collective-permute-start.44 = (f32[256,128]{1,0:T(8,128)S(1)}, f32[256,128]{1,0:T(8,128)S(1)}, u32[]{:S(2)}, u32[]{:S(2)}) collective-permute-start(f32[256,128]{1,0:T(8,128)S(1)} %mid_upper.11.refs_0_), channel_id=1, source_target_pairs={{0,2},{1,5},{2,0},{3,7},{4,6},{5,1},{6,4},{7,3},{8,10},{9,13},{10,... | collective-permute-start | bytes 393224 | tf_op jit(solution)/shard_map/mid_upper/ppermute | solution.py:494
  84.6 5.0 %collective-permute-start.45 = (f32[256,128]{1,0:T(8,128)S(1)}, f32[256,128]{1,0:T(8,128)S(1)}, u32[]{:S(2)}, u32[]{:S(2)}) collective-permute-start(f32[256,128]{1,0:T(8,128)S(1)} %mid_upper.12.refs_0_), channel_id=1, source_target_pairs={{0,4},{1,3},{2,6},{3,1},{4,0},{5,7},{6,2},{7,5},{8,12},{9,11},{10,... | collective-permute-start | bytes 393224 | tf_op jit(solution)/shard_map/mid_upper/ppermute | solution.py:494
  89.7 4.5 %collective-permute-start.42 = (f32[128,128]{1,0:T(8,128)S(1)}, f32[128,128]{1,0:T(8,128)S(1)}, u32[]{:S(2)}, u32[]{:S(2)}) collective-permute-start(f32[128,128]{1,0:T(8,128)S(1)} %get-tuple-element.115.mine.x_root), channel_id=1, source_target_pairs={{0,8},{8,0},{16,24},{24,16},{1,9},{9,1},{17,25},{25,17},{2,10},{10... | collective-permute-start | bytes 196616 | tf_op jit(solution)/shard_map/mid_upper/ppermute | solution.py:120
  92.8 4.0 %collective-permute-start.47 = (f32[64,128]{1,0:T(8,128)S(1)}, f32[64,128]{1,0:T(8,128)S(1)}, u32[]{:S(2)}, u32[]{:S(2)}) collective-permute-start(f32[64,128]{1,0:T(8,128)S(1)} %mid_upper.15.mine), channel_id=1, source_target_pairs={{0,8},{8,0},{16,24},{24,16},{1,9},{9,1},{17,25},{25,17},{2,10},{10... | collective-permute-start | bytes 98312 | tf_op jit(solution)/shard_map/leaf_upper/ppermute | solution.py:120
  98.7 5.0 %collective-permute-start.49 = (f32[256,128]{1,0:T(8,128)S(1)}, f32[256,128]{1,0:T(8,128)S(1)}, u32[]{:S(2)}, u32[]{:S(2)}) collective-permute-start(f32[256,128]{1,0:T(8,128)S(1)} %leaf_upper.10.refs_0_), channel_id=1, source_target_pairs={{0,2},{1,5},{2,0},{3,7},{4,6},{5,1},{6,4},{7,3},{8,10},{9,13},{10,... | collective-permute-start | bytes 393224 | tf_op jit(solution)/shard_map/leaf_upper/ppermute | solution.py:494
  99.7 5.2 %collective-permute-start.50 = (f32[64,128]{1,0:T(8,128)S(1)}, f32[64,128]{1,0:T(8,128)S(1)}, u32[]{:S(2)}, u32[]{:S(2)}) collective-permute-start(f32[64,128]{1,0:T(8,128)S(1)} %mid_upper.15.mine), channel_id=1, source_target_pairs={{0,16},{8,24},{16,0},{24,8},{1,17},{9,25},{17,1},{25,9},{2,18},{10... | collective-permute-start | bytes 98312 | tf_op jit(solution)/shard_map/leaf_upper/ppermute | solution.py:120
  104.9 5.0 %collective-permute-start.51 = (f32[256,128]{1,0:T(8,128)S(1)}, f32[256,128]{1,0:T(8,128)S(1)}, u32[]{:S(2)}, u32[]{:S(2)}) collective-permute-start(f32[256,128]{1,0:T(8,128)S(1)} %leaf_upper.11.refs_0_), channel_id=1, source_target_pairs={{0,4},{1,3},{2,6},{3,1},{4,0},{5,7},{6,2},{7,5},{8,12},{9,11},{10,... | collective-permute-start | bytes 393224 | tf_op jit(solution)/shard_map/leaf_upper/ppermute | solution.py:494
  106.1 3.9 %collective-permute-start.52 = (f32[64,128]{1,0:T(8,128)S(1)}, f32[64,128]{1,0:T(8,128)S(1)}, u32[]{:S(2)}, u32[]{:S(2)}) collective-permute-start(f32[64,128]{1,0:T(8,128)S(1)} %collective-permute-done.50.far), channel_id=1, source_target_pairs={{0,8},{8,0},{16,24},{24,16},{1,9},{9,1},{17,25},{25,17},{2,10},{10... | collective-permute-start | bytes 98312 | tf_op jit(solution)/shard_map/leaf_upper/ppermute | solution.py:120
  (29 other events, 102.8 us)

commit v17 on v16

--- a/solution.py
+++ b/solution.py
@@ -607,16 +607,16 @@
             scratch=[pltpu.VMEM((s0, LANES), F32), pltpu.VMEM((fronts, *message.shape), F32)],
         )
     with jax.named_scope("mid_lower"):
-        parts, (l2r, ml) = gather_front(
-            y_leaf,
-            lambda x: load((after(leaf_to_root_lower, *x), "leaf"), (mid_lower_inv, "own"), pinned=True),
+        parts, (l2r,) = gather_front(
+            y_leaf, lambda x: load((after(leaf_to_root_lower, *x), "leaf"), pinned=True)
         )
         keep, send = gathered(leaf_to_mid, LANES, [(n1 // 2, LANES)] * 2, l2m, parts, mid_own)
         came = swap("leaf", send, 1)
         root_kept, root_sent, y_full = kernel(
             leaf_to_root, [(n2 // 2, LANES)] * 2 + [(s0, LANES)], l2r, after(parts[0], send), *parts[1:]
         )
-        (cut_mid,) = kernel(add, [(n1 // 2, LANES)], after(keep, root_kept), came)
+        (ml,) = load((after(mid_lower_inv, root_kept), "own"), pinned=True)
+        (cut_mid,) = kernel(add, [(n1 // 2, LANES)], after(keep, root_kept, ml), came)
         root_came = swap("leaf", root_sent, 1)
         parts, (m2r,) = gather_front(
             cut_mid, lambda x: load((after(mid_to_root_lower, *x), "own"), pinned=True), (root_came,)

time: 113 us -> 113 us (level)
    pallas_call x48 -> x49, Pallas kernels: 26.6 us -> 27.5 us  [kernel(): pl.pallas_call(fn, out_shape=[jax.ShapeDtypeStruct(*o) for o in outs], in...]
  transfers between devices with their start and end apart: 54 -> 54, of which waited for: 37 -> 37; matrix products, arithmetic and copies ran while one was open for 0% -> 0% of each run, Pallas kernels for 17% -> 18%
where the time goes in v17:
time: 113 us; the launch traced here: 112 us
  starting transfers between devices  46.4 us (41%)
  waiting for transfers between devices  37.3 us (33%)
  Pallas kernels  27.5 us (24%)
  between operations  1.14 us (1%)
    ppermute x50, starting transfers between devices, swap(): return lax.ppermute(x, axis, [(i, i ^ k) for i in range(size)])  41.8 us
    pallas_call x49, Pallas kernels, kernel(): pl.pallas_call(fn, out_shape=[jax.ShapeDtypeStruct(*o) for o in outs], in...  27.5 us
    ppermute x50, waiting for transfers between devices, swap(): return lax.ppermute(x, axis, [(i, i ^ k) for i in range(size)])  25 us
    ppermute x4, waiting for transfers between devices, sum_front(): lax.ppermute(total, 'front', pairs)  12.3 us
    ppermute x4, starting transfers between devices, sum_front(): lax.ppermute(total, 'front', pairs)  4.56 us
  transfers between devices with their start and end apart: 54, of which 37 were waited for; matrix products, arithmetic and copies ran while one was open for 0% of the time, Pallas kernels for 18%

profile of v17, /device:TPU:0, one launch (start us, length us, event | category | flops | bytes accessed | tf_op | source)
XLA Modules:
  0.0 112.3 jit_solution(11497146792921230861)
XLA Ops:
  1.7 3.1 %collective-permute-start = (f32[32,128]{1,0:T(8,128)S(1)}, f32[32,128]{1,0:T(8,128)S(1)}, u32[]{:S(2)}, u32[]{:S(2)}) collective-permute-start(f32[32,128]{1,0:T(8,128)S(1)} %get-tuple-element.68), channel_id=1, source_target_pairs={{0,8},{8,0},{16,24},{24,16},{1,9},{9,1},{17,25},{25,17},{2,10},{10... | collective-permute-start | bytes 49160 | tf_op jit(solution)/shard_map/right_hand_sides/ppermute | solution.py:120
  4.8 1.7 %collective-permute-done.came.near = f32[32,128]{1,0:T(8,128)S(1)} collective-permute-done((f32[32,128]{1,0:T(8,128)S(1)}, f32[32,128]{1,0:T(8,128)S(1)}, u32[]{:S(2)}, u32[]{:S(2)}) %collective-permute-start) | collective-permute-done | bytes 16416 | tf_op jit(solution)/shard_map/right_hand_sides/ppermute | solution.py:120
  6.5 3.0 %collective-permute-start.1 = (f32[32,128]{1,0:T(8,128)S(1)}, f32[32,128]{1,0:T(8,128)S(1)}, u32[]{:S(2)}, u32[]{:S(2)}) collective-permute-start(f32[32,128]{1,0:T(8,128)S(1)} %right_hand_sides.6), channel_id=1, source_target_pairs={{0,16},{8,24},{16,0},{24,8},{1,17},{9,25},{17,1},{25,9},{2,18},{10... | collective-permute-start | bytes 49160 | tf_op jit(solution)/shard_map/right_hand_sides/ppermute | solution.py:120
  11.4 2.8 %collective-permute-start.5 = (f32[72,128]{1,0:T(8,128)S(1)}, f32[72,128]{1,0:T(8,128)S(1)}, u32[]{:S(2)}, u32[]{:S(2)}) collective-permute-start(f32[72,128]{1,0:T(8,128)S(1)} %right_hand_sides.7.refs_0_), channel_id=1, source_target_pairs={{0,6},{1,7},{2,4},{3,5},{4,2},{5,3},{6,0},{7,1},{8,14},{9,15},{10,... | collective-permute-start | bytes 110600 | tf_op jit(solution)/shard_map/leaf_lower/ppermute | solution.py:120
  15.0 1.3 %leaf_lower.3 = (bf16[128,1024]{1,0:T(8,128)(2,1)S(1)}, bf16[256,1024]{1,0:T(8,128)(2,1)S(1)}) custom-call(f32[2,1,64,512]{3,2,1,0:T(8,128)} %refs_0_, f32[2,1,128,512]{3,2,1,0:T(8,128)} %refs_1_.3), custom_call_target="tpu_custom_call" | custom-call | flops 98304000 | bytes 140434 | tf_op jit(solution)/shard_map/leaf_lower/pallas_call | solution.py:158
  16.3 1.9 %collective-permute-done.4.refs_1_.refs_3_ = f32[72,128]{1,0:T(8,128)S(1)} collective-permute-done((f32[72,128]{1,0:T(8,128)S(1)}, f32[72,128]{1,0:T(8,128)S(1)}, u32[]{:S(2)}, u32[]{:S(2)}) %collective-permute-start.4) | collective-permute-done | bytes 36896 | tf_op jit(solution)/shard_map/leaf_lower/ppermute | solution.py:120
  20.9 1.4 %collective-permute-start.9 = (f32[64,128]{1,0:T(8,128)S(1)}, f32[64,128]{1,0:T(8,128)S(1)}, u32[]{:S(2)}, u32[]{:S(2)}) collective-permute-start(f32[64,128]{1,0:T(8,128)S(1)} %leaf_lower.5.mine.refs_0_), channel_id=1, source_target_pairs={{0,6},{1,7},{2,4},{3,5},{4,2},{5,3},{6,0},{7,1},{8,14},{9,15},{10,... | collective-permute-start | bytes 98312 | tf_op jit(solution)/shard_map/mid_lower/ppermute | solution.py:120
  22.7 1.7 %collective-permute-start.12 = (f32[64,128]{1,0:T(8,128)S(1)}, f32[64,128]{1,0:T(8,128)S(1)}, u32[]{:S(2)}, u32[]{:S(2)}) collective-permute-start(f32[64,128]{1,0:T(8,128)S(1)} %leaf_lower.5.mine.refs_0_), channel_id=1, source_target_pairs={{0,4},{1,5},{2,6},{3,7},{4,0},{5,1},{6,2},{7,3},{8,12},{9,13},{10,... | collective-permute-start | bytes 98312 | tf_op jit(solution)/shard_map/mid_lower/ppermute | solution.py:120
  24.4 1.3 %mid_lower.11.matrix = bf16[512,1024]{1,0:T(8,128)(2,1)S(1)} custom-call(f32[2,1,256,512]{3,2,1,0:T(8,128)} %refs_0_.1), custom_call_target="tpu_custom_call" | custom-call | flops 131072000 | bytes 187245 | tf_op jit(solution)/shard_map/mid_lower/pallas_call | solution.py:158
  28.4 1.7 %collective-permute-start.14 = (f32[64,128]{1,0:T(8,128)S(1)}, f32[64,128]{1,0:T(8,128)S(1)}, u32[]{:S(2)}, u32[]{:S(2)}) collective-permute-start(f32[64,128]{1,0:T(8,128)S(1)} %get-tuple-element.80), channel_id=1, source_target_pairs={{0,8},{8,0},{16,24},{24,16},{1,9},{9,1},{17,25},{25,17},{2,10},{10... | collective-permute-start | bytes 98312 | tf_op jit(solution)/shard_map/mid_lower/ppermute | solution.py:120
  31.2 1.3 %mid_lower.16.matrix = bf16[256,2048]{1,0:T(8,128)(2,1)S(1)} custom-call(f32[2,2,128,1024]{3,2,1,0:T(8,128)} %refs_0_.2), custom_call_target="tpu_custom_call" | custom-call | flops 131072000 | bytes 187245 | tf_op jit(solution)/shard_map/mid_lower/pallas_call | solution.py:158
  32.6 2.6 %collective-permute-start.16 = (f32[64,128]{1,0:T(8,128)S(1)}, f32[64,128]{1,0:T(8,128)S(1)}, u32[]{:S(2)}, u32[]{:S(2)}) collective-permute-start(f32[64,128]{1,0:T(8,128)S(1)} %mid_lower.17.mine), channel_id=1, source_target_pairs={{0,6},{1,7},{2,4},{3,5},{4,2},{5,3},{6,0},{7,1},{8,14},{9,15},{10,... | collective-permute-start | bytes 98312 | tf_op jit(solution)/shard_map/mid_lower/ppermute | solution.py:120
  36.2 1.6 %mid_lower.18.matrix = bf16[512,2048]{1,0:T(8,128)(2,1)S(1)} custom-call(f32[2,2,256,1024]{3,2,1,0:T(8,128)} %refs_0_.3), custom_call_target="tpu_custom_call" | custom-call | flops 262144000 | bytes 374491 | tf_op jit(solution)/shard_map/mid_lower/pallas_call | solution.py:158
  37.8 1.3 %collective-permute-done.17.refs_1_ = f32[64,128]{1,0:T(8,128)S(1)} collective-permute-done((f32[64,128]{1,0:T(8,128)S(1)}, f32[64,128]{1,0:T(8,128)S(1)}, u32[]{:S(2)}, u32[]{:S(2)}) %collective-permute-start.17) | collective-permute-done | bytes 32800 | tf_op jit(solution)/shard_map/mid_lower/ppermute | solution.py:120
  41.7 1.3 %collective-permute-start.23 = (f32[64,128]{1,0:T(8,128)S(1)}, f32[64,128]{1,0:T(8,128)S(1)}, u32[]{:S(2)}, u32[]{:S(2)}) collective-permute-start(f32[64,128]{1,0:T(8,128)S(1)} %mid_lower.21.mine.refs_0_), channel_id=1, source_target_pairs={{0,6},{1,7},{2,4},{3,5},{4,2},{5,3},{6,0},{7,1},{8,14},{9,15},{10,... | collective-permute-start | bytes 98312 | tf_op jit(solution)/shard_map/root_cut/ppermute | solution.py:120
  43.7 1.5 %collective-permute-start.26 = (f32[64,128]{1,0:T(8,128)S(1)}, f32[64,128]{1,0:T(8,128)S(1)}, u32[]{:S(2)}, u32[]{:S(2)}) collective-permute-start(f32[64,128]{1,0:T(8,128)S(1)} %mid_lower.21.mine.refs_0_), channel_id=1, source_target_pairs={{0,4},{1,5},{2,6},{3,7},{4,0},{5,1},{6,2},{7,3},{8,12},{9,13},{10,... | collective-permute-start | bytes 98312 | tf_op jit(solution)/shard_map/root_cut/ppermute | solution.py:120
  49.7 2.7 %collective-permute-start.28 = (f32[64,128]{1,0:T(8,128)S(1)}, f32[64,128]{1,0:T(8,128)S(1)}, u32[]{:S(2)}, u32[]{:S(2)}) collective-permute-start(f32[64,128]{1,0:T(8,128)S(1)} %get-tuple-element.95), channel_id=1, source_target_pairs={{0,16},{8,24},{16,0},{24,8},{1,17},{9,25},{17,1},{25,9},{2,18},{10... | collective-permute-start | bytes 98312 | tf_op jit(solution)/shard_map/root_cut/ppermute | solution.py:120
  53.1 1.6 %collective-permute-done.28.refs_1_ = f32[64,128]{1,0:T(8,128)S(1)} collective-permute-done((f32[64,128]{1,0:T(8,128)S(1)}, f32[64,128]{1,0:T(8,128)S(1)}, u32[]{:S(2)}, u32[]{:S(2)}) %collective-permute-start.28) | collective-permute-done | bytes 32800 | tf_op jit(solution)/shard_map/root_cut/ppermute | solution.py:120
  54.6 2.1 %collective-permute-start.30 = (f32[64,128]{1,0:T(8,128)S(1)}, f32[64,128]{1,0:T(8,128)S(1)}, u32[]{:S(2)}, u32[]{:S(2)}) collective-permute-start(f32[64,128]{1,0:T(8,128)S(1)} %root_cut.13.mine), channel_id=1, source_target_pairs={{0,6},{1,7},{2,4},{3,5},{4,2},{5,3},{6,0},{7,1},{8,14},{9,15},{10,... | collective-permute-start | bytes 98312 | tf_op jit(solution)/shard_map/root_solve/ppermute | solution.py:120
  64.2 1.2 %collective-permute-start.36 = (f32[64,128]{1,0:T(8,128)S(1)}, f32[64,128]{1,0:T(8,128)S(1)}, u32[]{:S(2)}, u32[]{:S(2)}) collective-permute-start(f32[64,128]{1,0:T(8,128)S(1)} %root_solve.11.mine), channel_id=1, source_target_pairs={{0,6},{1,7},{2,4},{3,5},{4,2},{5,3},{6,0},{7,1},{8,14},{9,15},{10,... | collective-permute-start | bytes 98312 | tf_op jit(solution)/shard_map/root_solve/ppermute | solution.py:120
  66.2 1.5 %collective-permute-start.39 = (f32[64,128]{1,0:T(8,128)S(1)}, f32[64,128]{1,0:T(8,128)S(1)}, u32[]{:S(2)}, u32[]{:S(2)}) collective-permute-start(f32[64,128]{1,0:T(8,128)S(1)} %root_solve.11.mine), channel_id=1, source_target_pairs={{0,4},{1,5},{2,6},{3,7},{4,0},{5,1},{6,2},{7,3},{8,12},{9,13},{10,... | collective-permute-start | bytes 98312 | tf_op jit(solution)/shard_map/root_solve/ppermute | solution.py:120
  67.7 1.4 %root_solve.12 = (bf16[2048,512]{1,0:T(8,128)(2,1)S(1)}, bf16[1024,256]{1,0:T(8,128)(2,1)S(1)}, bf16[128,1024]{1,0:T(8,128)(2,1)S(1)}) custom-call(f32[2,2,1024,256]{3,2,1,0:T(8,128)S(1)} %copy-done, f32[2,1,512,128]{3,2,1,0:T(8,128)S(1)} %copy-done.5, f32[2,1,64,512]{3,2,1,0:T(8,128)S(1)} %copy-done.6), custom_call_target="tpu_custom_call" | custom-call | flops 360448000 | bytes 514925 | tf_op jit(solution)/shard_map/root_solve/pallas_call | solution.py:158
  72.6 2.7 %collective-permute-start.41 = (f32[64,128]{1,0:T(8,128)S(1)}, f32[64,128]{1,0:T(8,128)S(1)}, u32[]{:S(2)}, u32[]{:S(2)}) collective-permute-start(f32[64,128]{1,0:T(8,128)S(1)} %root_solve.15.mine), channel_id=1, source_target_pairs={{0,16},{8,24},{16,0},{24,8},{1,17},{9,25},{17,1},{25,9},{2,18},{10... | collective-permute-start | bytes 98312 | tf_op jit(solution)/shard_map/mid_upper/ppermute | solution.py:120
  75.2 2.2 %collective-permute-done.41.other = f32[64,128]{1,0:T(8,128)S(1)} collective-permute-done((f32[64,128]{1,0:T(8,128)S(1)}, f32[64,128]{1,0:T(8,128)S(1)}, u32[]{:S(2)}, u32[]{:S(2)}) %collective-permute-start.41) | collective-permute-done | bytes 32800 | tf_op jit(solution)/shard_map/mid_upper/ppermute | solution.py:120
  80.8 4.0 %collective-permute-done.44.refs_1_ = f32[256,128]{1,0:T(8,128)S(1)} collective-permute-done((f32[256,128]{1,0:T(8,128)S(1)}, f32[256,128]{1,0:T(8,128)S(1)}, u32[]{:S(2)}, u32[]{:S(2)}) %collective-permute-start.44) | collective-permute-done | bytes 131104 | tf_op jit(solution)/shard_map/mid_upper/ppermute | solution.py:494
  84.8 1.3 %collective-permute-start.45 = (f32[256,128]{1,0:T(8,128)S(1)}, f32[256,128]{1,0:T(8,128)S(1)}, u32[]{:S(2)}, u32[]{:S(2)}) collective-permute-start(f32[256,128]{1,0:T(8,128)S(1)} %mid_upper.12.refs_0_), channel_id=1, source_target_pairs={{0,4},{1,3},{2,6},{3,1},{4,0},{5,7},{6,2},{7,5},{8,12},{9,11},{10,... | collective-permute-start | bytes 393224 | tf_op jit(solution)/shard_map/mid_upper/ppermute | solution.py:494
  86.1 3.8 %collective-permute-done.45.refs_1_ = f32[256,128]{1,0:T(8,128)S(1)} collective-permute-done((f32[256,128]{1,0:T(8,128)S(1)}, f32[256,128]{1,0:T(8,128)S(1)}, u32[]{:S(2)}, u32[]{:S(2)}) %collective-permute-start.45) | collective-permute-done | bytes 131104 | tf_op jit(solution)/shard_map/mid_upper/ppermute | solution.py:494
  89.9 1.7 %collective-permute-start.42 = (f32[128,128]{1,0:T(8,128)S(1)}, f32[128,128]{1,0:T(8,128)S(1)}, u32[]{:S(2)}, u32[]{:S(2)}) collective-permute-start(f32[128,128]{1,0:T(8,128)S(1)} %get-tuple-element.113.mine.x_root), channel_id=1, source_target_pairs={{0,8},{8,0},{16,24},{24,16},{1,9},{9,1},{17,25},{25,17},{2,10},{10... | collective-permute-start | bytes 196616 | tf_op jit(solution)/shard_map/mid_upper/ppermute | solution.py:120
  94.4 1.2 %mid_upper.9 = (f32[512,128]{1,0:T(8,128)S(1)}, f32[2,32,256]{2,1,0:T(8,128)}, f32[2,32,256]{2,1,0:T(8,128)}) custom-call(bf16[1024,512]{1,0:T(8,128)(2,1)S(1)} %get-tuple-element.107.matrix, f32[128,128]{1,0:T(8,128)S(1)} %get-tuple-element.113.mine.x_root, f32[128,128]{1,0:T(8,128)S(1)} %collective-permute-done.42.other), custom_call_target="tpu_custom_call" | custom-call | tf_op jit(solution)/shard_map/mid_upper/pallas_call | solution.py:158
  99.7 2.8 %collective-permute-start.50 = (f32[64,128]{1,0:T(8,128)S(1)}, f32[64,128]{1,0:T(8,128)S(1)}, u32[]{:S(2)}, u32[]{:S(2)}) collective-permute-start(f32[64,128]{1,0:T(8,128)S(1)} %mid_upper.15.mine), channel_id=1, source_target_pairs={{0,16},{8,24},{16,0},{24,8},{1,17},{9,25},{17,1},{25,9},{2,18},{10... | collective-permute-start | bytes 98312 | tf_op jit(solution)/shard_map/leaf_upper/ppermute | solution.py:120
  104.9 1.2 %collective-permute-start.51 = (f32[256,128]{1,0:T(8,128)S(1)}, f32[256,128]{1,0:T(8,128)S(1)}, u32[]{:S(2)}, u32[]{:S(2)}) collective-permute-start(f32[256,128]{1,0:T(8,128)S(1)} %leaf_upper.11.refs_0_), channel_id=1, source_target_pairs={{0,4},{1,3},{2,6},{3,1},{4,0},{5,7},{6,2},{7,5},{8,12},{9,11},{10,... | collective-permute-start | bytes 393224 | tf_op jit(solution)/shard_map/leaf_upper/ppermute | solution.py:494
  106.6 3.3 %collective-permute-done.51.refs_1_ = f32[256,128]{1,0:T(8,128)S(1)} collective-permute-done((f32[256,128]{1,0:T(8,128)S(1)}, f32[256,128]{1,0:T(8,128)S(1)}, u32[]{:S(2)}, u32[]{:S(2)}) %collective-permute-start.51) | collective-permute-done | bytes 131104 | tf_op jit(solution)/shard_map/leaf_upper/ppermute | solution.py:494
  (139 shorter events, 47.1 us)
Async XLA Ops:
  1.7 4.8 %collective-permute-start = (f32[32,128]{1,0:T(8,128)S(1)}, f32[32,128]{1,0:T(8,128)S(1)}, u32[]{:S(2)}, u32[]{:S(2)}) collective-permute-start(f32[32,128]{1,0:T(8,128)S(1)} %get-tuple-element.68), channel_id=1, source_target_pairs={{0,8},{8,0},{16,24},{24,16},{1,9},{9,1},{17,25},{25,17},{2,10},{10... | collective-permute-start | bytes 49160 | tf_op jit(solution)/shard_map/right_hand_sides/ppermute | solution.py:120
  6.5 4.7 %collective-permute-start.1 = (f32[32,128]{1,0:T(8,128)S(1)}, f32[32,128]{1,0:T(8,128)S(1)}, u32[]{:S(2)}, u32[]{:S(2)}) collective-permute-start(f32[32,128]{1,0:T(8,128)S(1)} %right_hand_sides.6), channel_id=1, source_target_pairs={{0,16},{8,24},{16,0},{24,8},{1,17},{9,25},{17,1},{25,9},{2,18},{10... | collective-permute-start | bytes 49160 | tf_op jit(solution)/shard_map/right_hand_sides/ppermute | solution.py:120
  11.4 4.9 %collective-permute-start.5 = (f32[72,128]{1,0:T(8,128)S(1)}, f32[72,128]{1,0:T(8,128)S(1)}, u32[]{:S(2)}, u32[]{:S(2)}) collective-permute-start(f32[72,128]{1,0:T(8,128)S(1)} %right_hand_sides.7.refs_0_), channel_id=1, source_target_pairs={{0,6},{1,7},{2,4},{3,5},{4,2},{5,3},{6,0},{7,1},{8,14},{9,15},{10,... | collective-permute-start | bytes 110600 | tf_op jit(solution)/shard_map/leaf_lower/ppermute | solution.py:120
  14.3 4.0 %collective-permute-start.4 = (f32[72,128]{1,0:T(8,128)S(1)}, f32[72,128]{1,0:T(8,128)S(1)}, u32[]{:S(2)}, u32[]{:S(2)}) collective-permute-start(f32[72,128]{1,0:T(8,128)S(1)} %right_hand_sides.7.refs_0_), channel_id=1, source_target_pairs={{0,2},{1,3},{2,0},{3,1},{4,6},{5,7},{6,4},{7,5},{8,10},{9,11},{10,... | collective-permute-start | bytes 110600 | tf_op jit(solution)/shard_map/leaf_lower/ppermute | solution.py:120
  14.8 4.0 %collective-permute-start.3 = (f32[72,128]{1,0:T(8,128)S(1)}, f32[72,128]{1,0:T(8,128)S(1)}, u32[]{:S(2)}, u32[]{:S(2)}) collective-permute-start(f32[72,128]{1,0:T(8,128)S(1)} %right_hand_sides.7.refs_0_), channel_id=1, source_target_pairs={{0,4},{1,5},{2,6},{3,7},{4,0},{5,1},{6,2},{7,3},{8,12},{9,13},{10,... | collective-permute-start | bytes 110600 | tf_op jit(solution)/shard_map/leaf_lower/ppermute | solution.py:120
  20.9 4.9 %collective-permute-start.9 = (f32[64,128]{1,0:T(8,128)S(1)}, f32[64,128]{1,0:T(8,128)S(1)}, u32[]{:S(2)}, u32[]{:S(2)}) collective-permute-start(f32[64,128]{1,0:T(8,128)S(1)} %leaf_lower.5.mine.refs_0_), channel_id=1, source_target_pairs={{0,6},{1,7},{2,4},{3,5},{4,2},{5,3},{6,0},{7,1},{8,14},{9,15},{10,... | collective-permute-start | bytes 98312 | tf_op jit(solution)/shard_map/mid_lower/ppermute | solution.py:120
  22.3 3.9 %collective-permute-start.10 = (f32[64,128]{1,0:T(8,128)S(1)}, f32[64,128]{1,0:T(8,128)S(1)}, u32[]{:S(2)}, u32[]{:S(2)}) collective-permute-start(f32[64,128]{1,0:T(8,128)S(1)} %leaf_lower.5.mine.refs_0_), channel_id=1, source_target_pairs={{0,2},{1,3},{2,0},{3,1},{4,6},{5,7},{6,4},{7,5},{8,10},{9,11},{10,... | collective-permute-start | bytes 98312 | tf_op jit(solution)/shard_map/mid_lower/ppermute | solution.py:120
  22.7 3.9 %collective-permute-start.12 = (f32[64,128]{1,0:T(8,128)S(1)}, f32[64,128]{1,0:T(8,128)S(1)}, u32[]{:S(2)}, u32[]{:S(2)}) collective-permute-start(f32[64,128]{1,0:T(8,128)S(1)} %leaf_lower.5.mine.refs_0_), channel_id=1, source_target_pairs={{0,4},{1,5},{2,6},{3,7},{4,0},{5,1},{6,2},{7,3},{8,12},{9,13},{10,... | collective-permute-start | bytes 98312 | tf_op jit(solution)/shard_map/mid_lower/ppermute | solution.py:120
  28.4 4.1 %collective-permute-start.14 = (f32[64,128]{1,0:T(8,128)S(1)}, f32[64,128]{1,0:T(8,128)S(1)}, u32[]{:S(2)}, u32[]{:S(2)}) collective-permute-start(f32[64,128]{1,0:T(8,128)S(1)} %get-tuple-element.80), channel_id=1, source_target_pairs={{0,8},{8,0},{16,24},{24,16},{1,9},{9,1},{17,25},{25,17},{2,10},{10... | collective-permute-start | bytes 98312 | tf_op jit(solution)/shard_map/mid_lower/ppermute | solution.py:120
  30.8 7.1 %collective-permute-start.18 = (f32[128,128]{1,0:T(8,128)S(1)}, f32[128,128]{1,0:T(8,128)S(1)}, u32[]{:S(2)}, u32[]{:S(2)}) collective-permute-start(f32[128,128]{1,0:T(8,128)S(1)} %get-tuple-element.87), channel_id=1, source_target_pairs={{0,8},{8,0},{16,24},{24,16},{1,9},{9,1},{17,25},{25,17},{2,10},{10... | collective-permute-start | bytes 196616 | tf_op jit(solution)/shard_map/mid_lower/ppermute | solution.py:120
  32.6 5.2 %collective-permute-start.16 = (f32[64,128]{1,0:T(8,128)S(1)}, f32[64,128]{1,0:T(8,128)S(1)}, u32[]{:S(2)}, u32[]{:S(2)}) collective-permute-start(f32[64,128]{1,0:T(8,128)S(1)} %mid_lower.17.mine), channel_id=1, source_target_pairs={{0,6},{1,7},{2,4},{3,5},{4,2},{5,3},{6,0},{7,1},{8,14},{9,15},{10,... | collective-permute-start | bytes 98312 | tf_op jit(solution)/shard_map/mid_lower/ppermute | solution.py:120
  35.2 3.9 %collective-permute-start.17 = (f32[64,128]{1,0:T(8,128)S(1)}, f32[64,128]{1,0:T(8,128)S(1)}, u32[]{:S(2)}, u32[]{:S(2)}) collective-permute-start(f32[64,128]{1,0:T(8,128)S(1)} %mid_lower.17.mine), channel_id=1, source_target_pairs={{0,2},{1,3},{2,0},{3,1},{4,6},{5,7},{6,4},{7,5},{8,10},{9,11},{10,... | collective-permute-start | bytes 98312 | tf_op jit(solution)/shard_map/mid_lower/ppermute | solution.py:120
  35.7 3.9 %collective-permute-start.20 = (f32[64,128]{1,0:T(8,128)S(1)}, f32[64,128]{1,0:T(8,128)S(1)}, u32[]{:S(2)}, u32[]{:S(2)}) collective-permute-start(f32[64,128]{1,0:T(8,128)S(1)} %mid_lower.17.mine), channel_id=1, source_target_pairs={{0,4},{1,5},{2,6},{3,7},{4,0},{5,1},{6,2},{7,3},{8,12},{9,13},{10,... | collective-permute-start | bytes 98312 | tf_op jit(solution)/shard_map/mid_lower/ppermute | solution.py:120
  41.7 4.9 %collective-permute-start.23 = (f32[64,128]{1,0:T(8,128)S(1)}, f32[64,128]{1,0:T(8,128)S(1)}, u32[]{:S(2)}, u32[]{:S(2)}) collective-permute-start(f32[64,128]{1,0:T(8,128)S(1)} %mid_lower.21.mine.refs_0_), channel_id=1, source_target_pairs={{0,6},{1,7},{2,4},{3,5},{4,2},{5,3},{6,0},{7,1},{8,14},{9,15},{10,... | collective-permute-start | bytes 98312 | tf_op jit(solution)/shard_map/root_cut/ppermute | solution.py:120
  43.0 3.9 %collective-permute-start.24 = (f32[64,128]{1,0:T(8,128)S(1)}, f32[64,128]{1,0:T(8,128)S(1)}, u32[]{:S(2)}, u32[]{:S(2)}) collective-permute-start(f32[64,128]{1,0:T(8,128)S(1)} %mid_lower.21.mine.refs_0_), channel_id=1, source_target_pairs={{0,2},{1,3},{2,0},{3,1},{4,6},{5,7},{6,4},{7,5},{8,10},{9,11},{10,... | collective-permute-start | bytes 98312 | tf_op jit(solution)/shard_map/root_cut/ppermute | solution.py:120
  43.7 3.9 %collective-permute-start.26 = (f32[64,128]{1,0:T(8,128)S(1)}, f32[64,128]{1,0:T(8,128)S(1)}, u32[]{:S(2)}, u32[]{:S(2)}) collective-permute-start(f32[64,128]{1,0:T(8,128)S(1)} %mid_lower.21.mine.refs_0_), channel_id=1, source_target_pairs={{0,4},{1,5},{2,6},{3,7},{4,0},{5,1},{6,2},{7,3},{8,12},{9,13},{10,... | collective-permute-start | bytes 98312 | tf_op jit(solution)/shard_map/root_cut/ppermute | solution.py:120
  49.7 4.9 %collective-permute-start.28 = (f32[64,128]{1,0:T(8,128)S(1)}, f32[64,128]{1,0:T(8,128)S(1)}, u32[]{:S(2)}, u32[]{:S(2)}) collective-permute-start(f32[64,128]{1,0:T(8,128)S(1)} %get-tuple-element.95), channel_id=1, source_target_pairs={{0,16},{8,24},{16,0},{24,8},{1,17},{9,25},{17,1},{25,9},{2,18},{10... | collective-permute-start | bytes 98312 | tf_op jit(solution)/shard_map/root_cut/ppermute | solution.py:120
  54.6 4.9 %collective-permute-start.30 = (f32[64,128]{1,0:T(8,128)S(1)}, f32[64,128]{1,0:T(8,128)S(1)}, u32[]{:S(2)}, u32[]{:S(2)}) collective-permute-start(f32[64,128]{1,0:T(8,128)S(1)} %root_cut.13.mine), channel_id=1, source_target_pairs={{0,6},{1,7},{2,4},{3,5},{4,2},{5,3},{6,0},{7,1},{8,14},{9,15},{10,... | collective-permute-start | bytes 98312 | tf_op jit(solution)/shard_map/root_solve/ppermute | solution.py:120
  56.8 3.9 %collective-permute-start.31 = (f32[64,128]{1,0:T(8,128)S(1)}, f32[64,128]{1,0:T(8,128)S(1)}, u32[]{:S(2)}, u32[]{:S(2)}) collective-permute-start(f32[64,128]{1,0:T(8,128)S(1)} %root_cut.13.mine), channel_id=1, source_target_pairs={{0,2},{1,3},{2,0},{3,1},{4,6},{5,7},{6,4},{7,5},{8,10},{9,11},{10,... | collective-permute-start | bytes 98312 | tf_op jit(solution)/shard_map/root_solve/ppermute | solution.py:120
  57.6 3.9 %collective-permute-start.33 = (f32[64,128]{1,0:T(8,128)S(1)}, f32[64,128]{1,0:T(8,128)S(1)}, u32[]{:S(2)}, u32[]{:S(2)}) collective-permute-start(f32[64,128]{1,0:T(8,128)S(1)} %root_cut.13.mine), channel_id=1, source_target_pairs={{0,4},{1,5},{2,6},{3,7},{4,0},{5,1},{6,2},{7,3},{8,12},{9,13},{10,... | collective-permute-start | bytes 98312 | tf_op jit(solution)/shard_map/root_solve/ppermute | solution.py:120
  64.2 5.1 %collective-permute-start.36 = (f32[64,128]{1,0:T(8,128)S(1)}, f32[64,128]{1,0:T(8,128)S(1)}, u32[]{:S(2)}, u32[]{:S(2)}) collective-permute-start(f32[64,128]{1,0:T(8,128)S(1)} %root_solve.11.mine), channel_id=1, source_target_pairs={{0,6},{1,7},{2,4},{3,5},{4,2},{5,3},{6,0},{7,1},{8,14},{9,15},{10,... | collective-permute-start | bytes 98312 | tf_op jit(solution)/shard_map/root_solve/ppermute | solution.py:120
  65.4 3.9 %collective-permute-start.37 = (f32[64,128]{1,0:T(8,128)S(1)}, f32[64,128]{1,0:T(8,128)S(1)}, u32[]{:S(2)}, u32[]{:S(2)}) collective-permute-start(f32[64,128]{1,0:T(8,128)S(1)} %root_solve.11.mine), channel_id=1, source_target_pairs={{0,2},{1,3},{2,0},{3,1},{4,6},{5,7},{6,4},{7,5},{8,10},{9,11},{10,... | collective-permute-start | bytes 98312 | tf_op jit(solution)/shard_map/root_solve/ppermute | solution.py:120
  66.2 3.9 %collective-permute-start.39 = (f32[64,128]{1,0:T(8,128)S(1)}, f32[64,128]{1,0:T(8,128)S(1)}, u32[]{:S(2)}, u32[]{:S(2)}) collective-permute-start(f32[64,128]{1,0:T(8,128)S(1)} %root_solve.11.mine), channel_id=1, source_target_pairs={{0,4},{1,5},{2,6},{3,7},{4,0},{5,1},{6,2},{7,3},{8,12},{9,13},{10,... | collective-permute-start | bytes 98312 | tf_op jit(solution)/shard_map/root_solve/ppermute | solution.py:120
  72.6 4.9 %collective-permute-start.41 = (f32[64,128]{1,0:T(8,128)S(1)}, f32[64,128]{1,0:T(8,128)S(1)}, u32[]{:S(2)}, u32[]{:S(2)}) collective-permute-start(f32[64,128]{1,0:T(8,128)S(1)} %root_solve.15.mine), channel_id=1, source_target_pairs={{0,16},{8,24},{16,0},{24,8},{1,17},{9,25},{17,1},{25,9},{2,18},{10... | collective-permute-start | bytes 98312 | tf_op jit(solution)/shard_map/mid_upper/ppermute | solution.py:120
  79.7 5.0 %collective-permute-start.44 = (f32[256,128]{1,0:T(8,128)S(1)}, f32[256,128]{1,0:T(8,128)S(1)}, u32[]{:S(2)}, u32[]{:S(2)}) collective-permute-start(f32[256,128]{1,0:T(8,128)S(1)} %mid_upper.11.refs_0_), channel_id=1, source_target_pairs={{0,2},{1,5},{2,0},{3,7},{4,6},{5,1},{6,4},{7,3},{8,10},{9,13},{10,... | collective-permute-start | bytes 393224 | tf_op jit(solution)/shard_map/mid_upper/ppermute | solution.py:494
  84.8 5.0 %collective-permute-start.45 = (f32[256,128]{1,0:T(8,128)S(1)}, f32[256,128]{1,0:T(8,128)S(1)}, u32[]{:S(2)}, u32[]{:S(2)}) collective-permute-start(f32[256,128]{1,0:T(8,128)S(1)} %mid_upper.12.refs_0_), channel_id=1, source_target_pairs={{0,4},{1,3},{2,6},{3,1},{4,0},{5,7},{6,2},{7,5},{8,12},{9,11},{10,... | collective-permute-start | bytes 393224 | tf_op jit(solution)/shard_map/mid_upper/ppermute | solution.py:494
  89.9 4.5 %collective-permute-start.42 = (f32[128,128]{1,0:T(8,128)S(1)}, f32[128,128]{1,0:T(8,128)S(1)}, u32[]{:S(2)}, u32[]{:S(2)}) collective-permute-start(f32[128,128]{1,0:T(8,128)S(1)} %get-tuple-element.113.mine.x_root), channel_id=1, source_target_pairs={{0,8},{8,0},{16,24},{24,16},{1,9},{9,1},{17,25},{25,17},{2,10},{10... | collective-permute-start | bytes 196616 | tf_op jit(solution)/shard_map/mid_upper/ppermute | solution.py:120
  92.8 4.0 %collective-permute-start.47 = (f32[64,128]{1,0:T(8,128)S(1)}, f32[64,128]{1,0:T(8,128)S(1)}, u32[]{:S(2)}, u32[]{:S(2)}) collective-permute-start(f32[64,128]{1,0:T(8,128)S(1)} %mid_upper.15.mine), channel_id=1, source_target_pairs={{0,8},{8,0},{16,24},{24,16},{1,9},{9,1},{17,25},{25,17},{2,10},{10... | collective-permute-start | bytes 98312 | tf_op jit(solution)/shard_map/leaf_upper/ppermute | solution.py:120
  98.7 5.0 %collective-permute-start.49 = (f32[256,128]{1,0:T(8,128)S(1)}, f32[256,128]{1,0:T(8,128)S(1)}, u32[]{:S(2)}, u32[]{:S(2)}) collective-permute-start(f32[256,128]{1,0:T(8,128)S(1)} %leaf_upper.10.refs_0_), channel_id=1, source_target_pairs={{0,2},{1,5},{2,0},{3,7},{4,6},{5,1},{6,4},{7,3},{8,10},{9,13},{10,... | collective-permute-start | bytes 393224 | tf_op jit(solution)/shard_map/leaf_upper/ppermute | solution.py:494
  99.7 5.2 %collective-permute-start.50 = (f32[64,128]{1,0:T(8,128)S(1)}, f32[64,128]{1,0:T(8,128)S(1)}, u32[]{:S(2)}, u32[]{:S(2)}) collective-permute-start(f32[64,128]{1,0:T(8,128)S(1)} %mid_upper.15.mine), channel_id=1, source_target_pairs={{0,16},{8,24},{16,0},{24,8},{1,17},{9,25},{17,1},{25,9},{2,18},{10... | collective-permute-start | bytes 98312 | tf_op jit(solution)/shard_map/leaf_upper/ppermute | solution.py:120
  104.9 5.0 %collective-permute-start.51 = (f32[256,128]{1,0:T(8,128)S(1)}, f32[256,128]{1,0:T(8,128)S(1)}, u32[]{:S(2)}, u32[]{:S(2)}) collective-permute-start(f32[256,128]{1,0:T(8,128)S(1)} %leaf_upper.11.refs_0_), channel_id=1, source_target_pairs={{0,4},{1,3},{2,6},{3,1},{4,0},{5,7},{6,2},{7,5},{8,12},{9,11},{10,... | collective-permute-start | bytes 393224 | tf_op jit(solution)/shard_map/leaf_upper/ppermute | solution.py:494
  106.1 3.9 %collective-permute-start.52 = (f32[64,128]{1,0:T(8,128)S(1)}, f32[64,128]{1,0:T(8,128)S(1)}, u32[]{:S(2)}, u32[]{:S(2)}) collective-permute-start(f32[64,128]{1,0:T(8,128)S(1)} %collective-permute-done.50.far), channel_id=1, source_target_pairs={{0,8},{8,0},{16,24},{24,16},{1,9},{9,1},{17,25},{25,17},{2,10},{10... | collective-permute-start | bytes 98312 | tf_op jit(solution)/shard_map/leaf_upper/ppermute | solution.py:120
  (29 other events, 102.7 us)
